TPU v7x, 32 devices: a whole 2x2x4 slice. The times are simulated.
32 devices in a mesh: pts: 8 (over y, x, core), cells: 4 (over z).
Axes of the slice: x: 2, y: 2, z: 4, core: 2. Of those that a mesh axis runs over, the one named last changes fastest.
Arguments:
- codes: int32 [4096, 512], P(('pts', 'cells')), may hold values from -127 to 127
- exponents: int32 [4096], P(('pts', 'cells')), may hold values from 6 to 9
- centroids: bfloat16 [24576, 512], P('cells'), as said below
- counters: int32 [24576], P('cells'), may hold values from 0 to 4095
Outputs:
- cell_sums: float32 [4, 6144, 512], P('cells', 'pts')
- cell_mass: float32 [4, 6144], P('cells', 'pts')
Inputs may be any that keep to these rules, and one draw needn't show every extreme that they name: `centroids`: centroids are real-valued with row scales that differ from row to row.
All inputs are finite; a program needn't handle non-finite values.
Results may differ from a plain program's by a relative error of at most 0.013.
Values may be sent and summed in bfloat16 or wider, within the bound.
No kernel may reach another device: no remote copies, remote signals or barrier semaphores. Data moves between devices by JAX's collectives and lax.ppermute only.
A program may use at most 64 MiB of HBM per device.

v0:
```python
import math

import jax
import jax.numpy as jnp
from jax import lax
from jax.sharding import PartitionSpec as P


def body(codes, exponents, centroids, counters):
    scaled = codes.astype(jnp.float32) * jnp.exp2(-exponents.astype(jnp.float32))[:, None]
    local_rows = scaled.astype(jnp.bfloat16)
    points = lax.all_gather(local_rows, "cells", axis=0, tiled=True)
    width = points.shape[1]
    beta = 4.0 / math.sqrt(width)
    logits = (
        lax.dot_general(
            points, centroids, (((1,), (1,)), ((), ())), preferred_element_type=jnp.float32
        )
        * beta
    )
    inverse = lax.rsqrt(counters.astype(jnp.float32) + 1.0)
    local_top = jnp.max(logits, axis=1)
    top = lax.pmax(local_top, "cells")
    expo = jnp.exp(logits - top[:, None])
    total, novel = lax.psum(
        (jnp.sum(expo, axis=1), jnp.dot(expo, inverse, preferred_element_type=jnp.float32)), "cells"
    )
    weight = novel / total
    share = (expo * (weight / total)[:, None]).astype(jnp.bfloat16)
    mass_local = jnp.sum(share.astype(jnp.float32), axis=0)
    sums_local = lax.dot_general(
        share, points, (((0,), (0,)), ((), ())), preferred_element_type=jnp.float32
    )
    sums, mass = (
        lax.psum_scatter(sums_local, "pts", scatter_dimension=0, tiled=True),
        lax.psum_scatter(mass_local, "pts", scatter_dimension=0, tiled=True),
    )
    return (sums[None], mass[None])


def solution(mesh):
    in_specs = (P(("pts", "cells"), None), P(("pts", "cells")), P("cells", None), P("cells"))
    out_specs = (P("cells", "pts", None), P("cells", "pts"))
    return jax.shard_map(body, mesh=mesh, in_specs=in_specs, out_specs=out_specs, check_vma=False)
```

profile of v0, /device:TPU:0, one launch (start us, length us, event | category | flops | bytes accessed | tf_op | source)
XLA Modules:
  0.0 178.8 jit_solution(13451430943544630812)
XLA Ops:
  7.2 0.0 copy-start.1
  7.2 0.0 reduce-scatter.2.cloned.1.call-start
  7.2 0.7 multiply_exponential_fusion
  7.9 1.0 multiply_convert_fusion.1
  8.9 17.4 %all_gather.3 = bf16[512,512]{1,0:T(8,128)(2,1)S(1)} all-gather(bf16[128,512]{1,0:T(8,128)(2,1)S(1)} %multiply_convert_fusion.1), channel_id=1, replica_groups=mesh['pts'=8,'cells'=4] {'cells'}, dimensions={0}, use_global_device_ids=true | all-gather | bytes 655360 | tf_op jit(solution)/shard_map/all_gather | solution.py:12
  26.3 9.2 %multiply_reduce_fusion = (f32[512]{0:T(512)S(1)}, f32[512,6144]{1,0:T(8,128)}) fusion(bf16[512,512]{1,0:T(8,128)(2,1)S(1)} %all_gather.3, bf16[6144,512]{1,0:T(8,128)(2,1)} %param.6), kind=kOutput, calls=%fused_computation.3 | convolution fusion | flops 3227516416 | bytes 19400704 | tf_op jit(solution)/shard_map/dot_general | solution.py:16
  35.5 12.4 %pmax.7 = f32[512]{0:T(512)S(1)} all-reduce(f32[512]{0:T(512)S(1)} %get-tuple-element.6), channel_id=1, replica_groups=mesh['pts'=8,'cells'=4] {'cells'}, use_global_device_ids=true, to_apply=%region_1.0 | all-reduce | flops 512 | bytes 4096 | tf_op jit(solution)/shard_map/pmax | solution.py:23
  47.9 0.0 copy-done.1
  47.9 0.0 copy-start
  47.9 6.9 %fusion = f32[512]{0:T(512)S(1)} fusion(f32[512,6144]{1,0:T(8,128)} %get-tuple-element.7, f32[512]{0:T(512)S(1)} %pmax.7), kind=kLoop, calls=%fused_computation.4 | loop fusion | flops 9436672 | bytes 12587008 | tf_op jit(solution)/shard_map/reduce_sum | solution.py:26
  54.8 1.2 copy-done
  56.1 2.2 %fusion.1 = f32[1,512]{1,0:T(1,128)S(1)} fusion(f32[6144,1]{0,1:T(1,128)S(1)} %bitcast.9, f32[512,6144]{1,0:T(8,128)S(1)} %copy-done, f32[512]{0:T(512)S(1)} %pmax.7), kind=kOutput, calls=%fused_computation.5 | convolution fusion | flops 12582912 | bytes 12611584 | tf_op jit(solution)/shard_map/dot_general | solution.py:26
  58.3 8.3 %all-reduce.1 = (f32[512]{0:T(512)S(1)}, f32[512]{0:T(512)S(1)}) all-reduce(f32[512]{0:T(512)S(1)} %bitcast.10, f32[512]{0:T(512)S(1)} %fusion), channel_id=1, replica_groups=mesh['pts'=8,'cells'=4] {'cells'}, use_global_device_ids=true, to_apply=%region_2.0 | all-reduce | flops 1024 | bytes 8192 | tf_op jit(solution)/shard_map/psum | solution.py:25
  66.7 6.6 %convert_reduce_fusion = (f32[6144]{0:T(1024)S(1)}, bf16[512,6144]{1,0:T(8,128)(2,1)S(1)}) fusion(f32[512]{0:T(512)S(1)} %multiply_divide_fusion, f32[512]{0:T(512)S(1)} %pmax.7, f32[512,6144]{1,0:T(8,128)} %get-tuple-element.7), kind=kLoop, calls=%fused_computation | loop fusion | flops 18868224 | bytes 18903040 | tf_op jit(solution)/shard_map/reduce_sum | solution.py:30
  73.3 6.5 %fusion.5 = f32[6144,512]{1,0:T(8,128)} fusion(bf16[512,6144]{1,0:T(8,128)(2,1)S(1)} %get-tuple-element.5, bf16[512,512]{1,0:T(8,128)(2,1)S(1)} %all_gather.3), kind=kOutput, calls=%fused_computation.13 | convolution fusion | flops 3221225472 | bytes 19398656 | tf_op jit(solution)/shard_map/dot_general | solution.py:31
  79.7 0.0 copy-start.2
  79.7 0.0 reduce-scatter.2.cloned.1.call-update
  79.8 0.6 copy-done.2
  80.4 0.6 dynamic-slice
  81.6 22.4 %all-reduce = f32[6144]{0:T(1024)S(1)} all-reduce(f32[6144]{0:T(1024)S(1)} %get-tuple-element.4), channel_id=3, replica_groups=mesh['pts'=8,'cells'=4] {'pts'}, use_global_device_ids=true, to_apply=%region_7.0.clone | all-reduce | flops 6144 | bytes 49152
  104.0 0.1 dynamic-slice.1
  104.1 0.6 broadcast_in_dim.10
  104.7 67.3 %reduce-scatter.2.cloned.1.call-done = f32[768,512]{1,0:T(8,128)} async-done(((f32[6144,512]{1,0:T(8,128)}), f32[768,512]{1,0:T(8,128)}) %reduce-scatter.2.cloned.1.call-update) | async-done | bytes 1572880 | tf_op jit(solution)/shard_map/reduce_scatter | solution.py:35
  (2 shorter events, 0.0 us)
Async XLA Ops:
  7.2 40.8 %copy-start.1 = (s32[6144]{0:T(1024)S(1)}, s32[6144]{0:T(1024)}, u32[]{:S(2)}) copy-start(s32[6144]{0:T(1024)} %param.7) | copy-start | bytes 73732
  7.2 164.8 %reduce-scatter.2.cloned.1.call-start = ((), (), s32[]{:S(2)}) async-start(), calls=%async_computation.1 | async-start | bytes 14155776 | tf_op jit(solution)/shard_map/reduce_scatter | solution.py:35
  47.9 8.2 %copy-start = (f32[512,6144]{1,0:T(8,128)S(1)}, f32[512,6144]{1,0:T(8,128)}, u32[]{:S(2)}) copy-start(f32[512,6144]{1,0:T(8,128)} %get-tuple-element.7) | copy-start | bytes 37748740
  79.7 0.7 copy-start.2
Sparse Core Ops, SparseCore 0:
  79.9 92.0 reduce-scatter.1
where the time goes:
time: 179 us
  waiting for transfers between devices  67.3 us (38%)
  blocking collectives  60.5 us (34%)
  matrix products  17.9 us (10%)
  other arithmetic  15.2 us (8%)
  between operations  14.7 us (8%)
  local copies, waits for them, and re-layouts  3.12 us (2%)
    reduce_scatter x1, waiting for transfers between devices, body(): lax.psum_scatter(sums_local, 'pts', scatter_dimension=0, tiled=True)  67.3 us
    unnamed x1, blocking collectives  22.4 us
    all_gather x1, blocking collectives, body(): points = lax.all_gather(local_rows, 'cells', axis=0, tiled=True)  17.4 us
    pmax x1, blocking collectives, body(): top = lax.pmax(local_top, 'cells')  12.4 us
    dot_general x1, matrix products, body(): lax.dot_general(points, centroids, (((1,), (1,)), ((), ())), preferred_el...  9.19 us
    psum x1, blocking collectives, body(): lax.psum((jnp.sum(expo, axis=1), jnp.dot(expo, inverse, preferred_element...  8.35 us
    reduce_sum x1, other arithmetic, body(): jnp.sum(expo, axis=1)  6.9 us
    reduce_sum x1, other arithmetic, body(): mass_local = jnp.sum(share.astype(jnp.float32), axis=0)  6.56 us
  transfers between devices with their start and end apart: 1, of which 1 were waited for; matrix products, arithmetic and copies ran while one was open for 1% of the time, Pallas kernels for 0%

commit v1 on v0

v1 whole, which is shorter than its diff:
```python
import math

import jax
import jax.numpy as jnp
from jax import lax
from jax.sharding import Mesh, PartitionSpec as P

GATHER_BYTES = 8 << 20


def to_points(codes, exponents):
    scaled = codes.astype(jnp.float32) * jnp.exp2(-exponents.astype(jnp.float32))[:, None]
    return scaled.astype(jnp.bfloat16)


def split_points(codes, exponents, centroids, counters):
    local_rows = to_points(codes, exponents)
    points = lax.all_gather(local_rows, "cells", axis=0, tiled=True)
    beta = 4.0 / math.sqrt(points.shape[1])
    logits = (
        lax.dot_general(
            points, centroids, (((1,), (1,)), ((), ())), preferred_element_type=jnp.float32
        )
        * beta
    )
    inverse = lax.rsqrt(counters.astype(jnp.float32) + 1.0)
    top = lax.pmax(jnp.max(logits, axis=1), "cells")
    expo = jnp.exp(logits - top[:, None])
    total, novel = lax.psum(
        (jnp.sum(expo, axis=1), jnp.dot(expo, inverse, preferred_element_type=jnp.float32)), "cells"
    )
    weight = novel / total
    share = (expo * (weight / total)[:, None]).astype(jnp.bfloat16)
    mass_local = jnp.sum(share.astype(jnp.float32), axis=0)
    sums_local = lax.dot_general(
        share, points, (((0,), (0,)), ((), ())), preferred_element_type=jnp.float32
    )
    pts = ("hi", "lo")
    sums = lax.psum_scatter(sums_local, pts, scatter_dimension=0, tiled=True)
    mass = lax.psum_scatter(mass_local, pts, scatter_dimension=0, tiled=True)
    return (sums[None], mass[None])


def split_cells(codes, exponents, centroids, counters):
    n_hi, n_lo = lax.axis_size("hi"), lax.axis_size("lo")
    hi, lo = lax.axis_index("hi"), lax.axis_index("lo")
    group = ("hi", "cells")
    local_rows = to_points(codes, exponents)
    points = lax.all_gather(local_rows, group, axis=0, tiled=True)
    beta = 4.0 / math.sqrt(points.shape[1])
    per_pair = centroids.shape[0] // n_hi
    mine = lax.dynamic_slice_in_dim(centroids, hi * per_pair, per_pair)
    inverse = lax.rsqrt(
        lax.dynamic_slice_in_dim(counters, hi * per_pair, per_pair).astype(jnp.float32) + 1.0
    )
    logits = (
        lax.dot_general(
            points, mine, (((1,), (1,)), ((), ())), preferred_element_type=jnp.float32
        )
        * beta
    )
    top = jnp.max(logits, axis=1)
    expo = jnp.exp(logits - top[:, None])
    stats = jnp.stack(
        [top, jnp.sum(expo, axis=1), jnp.dot(expo, inverse, preferred_element_type=jnp.float32)]
    )
    every = lax.all_gather(stats, group, axis=0)
    tops = every[:, 0]
    highest = jnp.max(tops, axis=0)
    scale = jnp.exp(tops - highest)
    total = jnp.sum(every[:, 1] * scale, axis=0)
    novel = jnp.sum(every[:, 2] * scale, axis=0)
    factor = jnp.exp(top - highest) * (novel / total / total)
    share = (expo * factor[:, None]).astype(jnp.bfloat16)
    per_device = per_pair // n_lo
    sums = mass = None
    for step in range(n_lo):
        away = (n_lo - 1 - step)
        block = lax.dynamic_slice_in_dim(share, (lo + away) % n_lo * per_device, per_device, axis=1)
        part = lax.dot_general(block, points, (((0,), (0,)), ((), ())), preferred_element_type=jnp.float32)
        part_mass = jnp.sum(block.astype(jnp.float32), axis=0)
        if away:
            hops = [(at, (at + away) % n_lo) for at in range(n_lo)]
            part, part_mass = (lax.ppermute(a, "lo", hops) for a in (part, part_mass))
        sums = part if sums is None else sums + part
        mass = part_mass if mass is None else mass + part_mass
    return (sums[None], mass[None])


def solution(mesh):
    pts, cells = (mesh.shape[name] for name in ("pts", "cells"))
    fine = Mesh(mesh.devices.reshape(pts // 2, 2, cells), ("hi", "lo", "cells"))
    in_specs = (P(("hi", "lo", "cells"), None), P(("hi", "lo", "cells")), P("cells", None), P("cells"))
    out_specs = (P("cells", ("hi", "lo"), None), P("cells", ("hi", "lo")))

    def run(codes, exponents, centroids, counters):
        small = codes.size * 2 <= GATHER_BYTES
        body = split_cells if small else split_points
        mapped = jax.shard_map(body, mesh=fine, in_specs=in_specs, out_specs=out_specs, check_vma=False)
        return mapped(codes, exponents, centroids, counters)

    return run
```

time: 179 us -> 154 us (0.86)
  blocking collectives: 60.5 us -> 43.1 us
  other arithmetic: 15.2 us -> 12.5 us
  matrix products: 17.9 us -> 15.3 us
  waiting for transfers between devices: 67.3 us -> 65.3 us
    reduce_scatter x1 -> x0, waiting for transfers between devices: 67.3 us -> none  [body(): lax.psum_scatter(sums_local, 'pts', scatter_dimension=0, tiled=True)]
    all_gather x0 -> x1, waiting for transfers between devices: none -> 64.4 us  [split_cells(): points = lax.all_gather(local_rows, group, axis=0, tiled=True)]
    all_gather x1, blocking collectives: 17.4 us -> 43.1 us  [split_cells(): every = lax.all_gather(stats, group, axis=0)]
    unnamed x1 -> x0, blocking collectives: 22.4 us -> none
    pmax x1 -> x0, blocking collectives: 12.4 us -> none  [body(): top = lax.pmax(local_top, 'cells')]
    psum x1 -> x0, blocking collectives: 8.35 us -> none  [body(): lax.psum((jnp.sum(expo, axis=1), jnp.dot(expo, inverse, preferred_element...]
    reduce_sum x2 -> x3, other arithmetic: 13.5 us -> 6.22 us  [the longest x1 3.88 us: split_cells(): part_mass = jnp.sum(block.astype(jnp.float32), axis=0)]
    convert_element_type x1 -> x2, other arithmetic: 1.04 us -> 4.46 us  [the longest x1 2.76 us: split_cells(): share = (expo * factor[:, None]).astype(jnp.bfloat16)]
  transfers between devices with their start and end apart: 1 -> 3, of which waited for: 1 -> 2; matrix products, arithmetic and copies ran while one was open for 1% -> 3% of each run, Pallas kernels for 0% -> 0%
where the time goes in v1:
time: 154 us
  waiting for transfers between devices  65.3 us (42%)
  blocking collectives  43.1 us (28%)
  matrix products  15.3 us (10%)
  between operations  14.1 us (9%)
  other arithmetic  12.5 us (8%)
  local copies, waits for them, and re-layouts  3.25 us (2%)
    all_gather x1, waiting for transfers between devices, split_cells(): points = lax.all_gather(local_rows, group, axis=0, tiled=True)  64.4 us
    all_gather x1, blocking collectives, split_cells(): every = lax.all_gather(stats, group, axis=0)  43.1 us
    dot_general x2, matrix products, split_cells(): lax.dot_general(block, points, (((0,), (0,)), ((), ())), preferred_elemen...  7.36 us
    dot_general x1, matrix products, split_cells(): lax.dot_general(points, mine, (((1,), (1,)), ((), ())), preferred_element...  5.67 us
    reduce_sum x1, other arithmetic, split_cells(): part_mass = jnp.sum(block.astype(jnp.float32), axis=0)  3.88 us
  transfers between devices with their start and end apart: 3, of which 2 were waited for; matrix products, arithmetic and copies ran while one was open for 3% of the time, Pallas kernels for 0%

profile of v1, /device:TPU:0, one launch (start us, length us, event | category | flops | bytes accessed | tf_op | source)
XLA Modules:
  0.0 154.2 jit_solution(13967223652524089053)
XLA Ops:
  7.2 0.0 all-gather.4.cloned.1.call-start
  7.2 0.7 multiply_exponential_fusion
  7.9 1.7 %multiply_convert_fusion.1 = bf16[128,512]{1,0:T(8,128)(2,1)} fusion(s32[128,512]{1,0:T(8,128)} %param.4, f32[128]{0:T(128)S(1)} %multiply_exponential_fusion), kind=kLoop, calls=%fused_computation.16 | loop fusion | flops 196608 | bytes 393728 | tf_op jit(solution)/shard_map/convert_element_type | solution.py:13
  9.6 0.0 all-gather.4.cloned.1.call-update
  9.6 0.8 add_rsqrt_fusion
  10.4 64.4 %all-gather.4.cloned.1.call-done = bf16[2048,512]{1,0:T(8,128)(2,1)} async-done(((bf16[128,512]{1,0:T(8,128)(2,1)}), bf16[2048,512]{1,0:T(8,128)(2,1)}) %all-gather.4.cloned.1.call-update) | async-done | bytes 2097168 | tf_op jit(solution)/shard_map/all_gather | solution.py:49
  74.8 5.7 %multiply_reduce_fusion = (f32[2048]{0:T(1024)S(1)}, f32[2048,1536]{1,0:T(8,128)S(1)}) fusion(bf16[2048,512]{1,0:T(8,128)(2,1)} %all-gather.4.cloned.1.call-done, bf16[6144,512]{1,0:T(8,128)(2,1)} %param.6, s32[]{:T(128)S(6)} %select_n.21), kind=kOutput, calls=%fused_computation.2 | convolution fusion | flops 3227514880 | bytes 16261124 | tf_op jit(solution)/shard_map/dot_general | solution.py:57
  80.5 2.2 %fusion.1 = f32[2048]{0:T(1024)S(1)} fusion(f32[2048,1536]{1,0:T(8,128)S(1)} %get-tuple-element.11, f32[2048]{0:T(1024)S(1)} %get-tuple-element.10), kind=kLoop, calls=%fused_computation.4 | loop fusion | flops 9435136 | bytes 12599296 | tf_op jit(solution)/shard_map/reduce_sum | solution.py:65
  82.7 2.3 %fusion = f32[1,2048]{1,0:T(1,128)S(1)} fusion(bf16[1536,1]{0,1:T(2,128)(2,1)S(1)} %reshape.24, f32[2048,1536]{1,0:T(8,128)S(1)} %get-tuple-element.11, f32[2048]{0:T(1024)S(1)} %get-tuple-element.10), kind=kOutput, calls=%fused_computation.3 | convolution fusion | flops 12582912 | bytes 12602368 | tf_op jit(solution)/shard_map/dot_general | solution.py:65
  85.1 43.1 %all-gather.1 = f32[16,3,2048]{2,1,0:T(4,128)S(1)} all-gather(f32[1,3,2048]{2,1,0:T(4,128)S(1)} %maximum_bitcast_fusion), channel_id=2, replica_groups=mesh['hi'=4,'lo'=2,'cells'=4] {'hi','cells'}, dimensions={0}, use_global_device_ids=true | all-gather | bytes 417792 | tf_op jit(solution)/shard_map/all_gather | solution.py:67
  128.2 0.3 fusion.21
  128.5 0.1 fusion.13
  128.7 0.0 copy-start.2
  128.7 2.8 %multiply_convert_fusion = bf16[2048,1536]{1,0:T(8,128)(2,1)S(1)} fusion(f32[2048,1536]{1,0:T(8,128)S(1)} %get-tuple-element.11, f32[2048]{0:T(1024)S(1)} %divide_multiply_fusion, f32[2048]{0:T(1024)S(1)} %get-tuple-element.10), kind=kLoop, calls=%fused_computation | loop fusion | flops 12582912 | bytes 18890752 | tf_op jit(solution)/shard_map/convert_element_type | solution.py:74
  131.5 0.0 copy-start
  131.5 2.7 %copy-done = bf16[2048,1536]{1,0:T(8,128)(2,1)} copy-done((bf16[2048,1536]{1,0:T(8,128)(2,1)}, bf16[2048,1536]{1,0:T(8,128)(2,1)S(1)}, u32[]{:S(2)}) %copy-start) | copy-done | bytes 6291480
  134.1 0.0 copy-done.2
  134.1 3.0 %fusion.6 = f32[768,512]{1,0:T(8,128)} fusion(bf16[2048,512]{1,0:T(8,128)(2,1)S(1)} %copy-done.2, bf16[2048,1536]{1,0:T(8,128)(2,1)S(1)} %multiply_convert_fusion, s32[]{:T(128)S(6)} %select_n.23), kind=kOutput, calls=%fused_computation.11 | convolution fusion | flops 1610612736 | bytes 6815748 | tf_op jit(solution)/shard_map/dot_general | solution.py:80
  137.1 0.0 collective-permute-start
  137.1 0.0 copy-start.1
  137.1 3.9 %convert_reduce_fusion = (f32[768]{0:T(1024)S(1)}, f32[768]{0:T(1024)S(1)}) fusion(bf16[2048,1536]{1,0:T(8,128)(2,1)} %copy-done, s32[]{:T(128)S(6)} %select_n.25, s32[]{:T(128)S(6)} %select_n.23), kind=kLoop, calls=%fused_computation.5 | loop fusion | flops 6289920 | bytes 6297608 | tf_op jit(solution)/shard_map/reduce_sum | solution.py:81
  141.0 0.6 collective-permute-start.1
  141.6 0.8 collective-permute-done.1
  142.4 0.6 broadcast_in_dim.5
  143.0 0.0 collective-permute-done
  143.0 0.0 copy-done.1
  143.0 4.4 %add_bitcast_fusion = f32[1,768,512]{2,1,0:T(8,128)} fusion(f32[768,512]{1,0:T(8,128)} %collective-permute-done, bf16[2048,512]{1,0:T(8,128)(2,1)S(1)} %copy-done.2, bf16[2048,1536]{1,0:T(8,128)(2,1)S(1)} %copy-done.1, s32[]{:T(128)S(6)} %select_n.25), kind=kOutput, calls=%fused_computation.13 | convolution fusion | flops 1611005952 | bytes 8388612 | tf_op jit(solution)/shard_map/dot_general | solution.py:80
  (4 shorter events, 0.1 us)
Async XLA Ops:
  7.2 67.7 %all-gather.4.cloned.1.call-start = ((), (), s32[]{:S(2)}) async-start(), calls=%async_computation | async-start | bytes 2228224 | tf_op jit(solution)/shard_map/all_gather | solution.py:49
  128.7 5.4 %copy-start.2 = (bf16[2048,512]{1,0:T(8,128)(2,1)S(1)}, bf16[2048,512]{1,0:T(8,128)(2,1)}, u32[]{:S(2)}) copy-start(bf16[2048,512]{1,0:T(8,128)(2,1)} %all-gather.4.cloned.1.call-done) | copy-start | bytes 6291460
  131.5 2.7 %copy-start = (bf16[2048,1536]{1,0:T(8,128)(2,1)}, bf16[2048,1536]{1,0:T(8,128)(2,1)S(1)}, u32[]{:S(2)}) copy-start(bf16[2048,1536]{1,0:T(8,128)(2,1)S(1)} %multiply_convert_fusion) | copy-start | bytes 18874372
  137.1 5.9 %collective-permute-start = (f32[768,512]{1,0:T(8,128)}, f32[768,512]{1,0:T(8,128)}, u32[]{:S(2)}, u32[]{:S(2)}) collective-permute-start(f32[768,512]{1,0:T(8,128)} %fusion.6), channel_id=1, source_target_pairs={{0,4},{4,0},{1,5},{5,1},{2,6},{6,2},{3,7},{7,3},{8,12},{12,8},{9,1... | collective-permute-start | bytes 4718600 | tf_op jit(solution)/shard_map/ppermute | solution.py:84
  137.1 5.9 %copy-start.1 = (bf16[2048,1536]{1,0:T(8,128)(2,1)S(1)}, bf16[2048,1536]{1,0:T(8,128)(2,1)}, u32[]{:S(2)}) copy-start(bf16[2048,1536]{1,0:T(8,128)(2,1)} %copy-done) | copy-start | bytes 18874372
  141.0 1.4 collective-permute-start.1
Sparse Core Ops, SparseCore 0:
  11.4 63.4 all-gather.3

commit v2 on v0

v2 whole, which is shorter than its diff:
```python
import functools
import math

import jax
import jax.numpy as jnp
from jax import lax
from jax.experimental import pallas as pl
from jax.experimental.pallas import tpu as pltpu
from jax.sharding import Mesh, PartitionSpec as P

GATHER_BYTES = 8 << 20
VMEM_BYTES = 40 << 20


def to_points(codes, exponents):
    scaled = codes.astype(jnp.float32) * jnp.exp2(-exponents.astype(jnp.float32))[:, None]
    return scaled.astype(jnp.bfloat16)


def split_points(codes, exponents, centroids, counters):
    local_rows = to_points(codes, exponents)
    points = lax.all_gather(local_rows, "cells", axis=0, tiled=True)
    beta = 4.0 / math.sqrt(points.shape[1])
    logits = (
        lax.dot_general(
            points, centroids, (((1,), (1,)), ((), ())), preferred_element_type=jnp.float32
        )
        * beta
    )
    inverse = lax.rsqrt(counters.astype(jnp.float32) + 1.0)
    top = lax.pmax(jnp.max(logits, axis=1), "cells")
    expo = jnp.exp(logits - top[:, None])
    total, novel = lax.psum(
        (jnp.sum(expo, axis=1), jnp.dot(expo, inverse, preferred_element_type=jnp.float32)), "cells"
    )
    weight = novel / total
    share = (expo * (weight / total)[:, None]).astype(jnp.bfloat16)
    mass_local = jnp.sum(share.astype(jnp.float32), axis=0)
    sums_local = lax.dot_general(
        share, points, (((0,), (0,)), ((), ())), preferred_element_type=jnp.float32
    )
    sums = lax.psum_scatter(sums_local, "pts", scatter_dimension=0, tiled=True)
    mass = lax.psum_scatter(mass_local, "pts", scatter_dimension=0, tiled=True)
    return (sums[None], mass[None])


def swap(a, axis):
    return lax.ppermute(a, axis, [(0, 1), (1, 0)])


def rotate(a, axis, by):
    size = lax.axis_size(axis)
    return lax.ppermute(a, axis, [((at + by) % size, at) for at in range(size)])


def expo_kernel(rate, near, along_x, along_y, across, cells, inverse, expo, block_top, stats, points):
    step = pl.program_id(0)
    rows = near.shape[0]

    @pl.when(step == 0)
    def _():
        for at, piece in enumerate((near, along_x, along_y, across)):
            points[at * rows : (at + 1) * rows, :] = piece[...]

    logits = lax.dot_general(
        cells[...], points[...], (((1,), (1,)), ((), ())), preferred_element_type=jnp.float32
    )
    top = jnp.max(logits, axis=0, keepdims=True)
    value = jnp.exp2((logits - top) * rate)
    expo[...] = value.astype(jnp.bfloat16)
    total = jnp.sum(value, axis=0, keepdims=True)
    novel = jnp.sum(value * inverse[...], axis=0, keepdims=True)
    block_top[pl.ds(step, 1), :] = top

    @pl.when(step == 0)
    def _():
        stats[...] = jnp.concatenate([top, total, novel], axis=0)

    @pl.when(step > 0)
    def _():
        so_far = stats[...]
        highest = jnp.maximum(so_far[:1], top)
        old, new = jnp.exp2((so_far[:1] - highest) * rate), jnp.exp2((top - highest) * rate)
        stats[...] = jnp.concatenate(
            [highest, so_far[1:2] * old + total * new, so_far[2:] * old + novel * new], axis=0
        )


def expo_call(rate, block, pieces, cells, inverse):
    rows, width = pieces[0].shape
    count, n_points = cells.shape[0], rows * len(pieces)
    steps = count // block
    whole = lambda *shape: pl.BlockSpec(shape, lambda i: (0,) * len(shape))
    return pl.pallas_call(
        functools.partial(expo_kernel, rate),
        grid=(steps,),
        in_specs=[whole(rows, width)] * 4
        + [pl.BlockSpec((block, width), lambda i: (i, 0)), pl.BlockSpec((block, 1), lambda i: (i, 0))],
        out_specs=[
            pl.BlockSpec((block, n_points), lambda i: (i, 0)),
            whole(steps, n_points),
            whole(3, n_points),
            whole(n_points, width),
        ],
        out_shape=[
            jax.ShapeDtypeStruct((count, n_points), jnp.bfloat16),
            jax.ShapeDtypeStruct((steps, n_points), jnp.float32),
            jax.ShapeDtypeStruct((3, n_points), jnp.float32),
            jax.ShapeDtypeStruct((n_points, width), jnp.bfloat16),
        ],
        compiler_params=pltpu.CompilerParams(vmem_limit_bytes=VMEM_BYTES),
        cost_estimate=pl.CostEstimate(
            flops=2 * count * n_points * width,
            bytes_accessed=2 * (count * width + n_points * width + count * n_points),
            transcendentals=count * n_points,
        ),
    )(*pieces, cells, inverse)


def sums_kernel(n, *refs):
    expos, points, (factor, sums, mass) = refs[:n], refs[n : 2 * n], refs[2 * n :]
    total, weight = None, None
    for at in range(n):
        share = (expos[at][...].astype(jnp.float32) * factor[0, at : at + 1, :]).astype(jnp.bfloat16)
        part = jnp.dot(share, points[at][...], preferred_element_type=jnp.float32)
        wide = share.astype(jnp.float32)
        lanes = sum(wide[:, i : i + 128] for i in range(0, wide.shape[1], 128))
        total = part if total is None else total + part
        weight = lanes if weight is None else weight + lanes
    sums[...] = total.astype(sums.dtype)
    mass[0] = jnp.sum(weight.T, axis=0, keepdims=True)


def sums_call(block, first, count, expos, points, factor, dtype):
    n = len(expos)
    n_points, width = points[0].shape
    return pl.pallas_call(
        functools.partial(sums_kernel, n),
        grid=(count,),
        in_specs=[pl.BlockSpec((block, n_points), lambda i: (i + first, 0))] * n
        + [pl.BlockSpec((n_points, width), lambda i: (0, 0))] * n
        + [pl.BlockSpec((1, n, n_points), lambda i: (i + first, 0, 0))],
        out_specs=[
            pl.BlockSpec((block, width), lambda i: (i, 0)),
            pl.BlockSpec((1, 1, block), lambda i: (i, 0, 0)),
        ],
        out_shape=[
            jax.ShapeDtypeStruct((count * block, width), dtype),
            jax.ShapeDtypeStruct((count, 1, block), jnp.float32),
        ],
        compiler_params=pltpu.CompilerParams(vmem_limit_bytes=VMEM_BYTES),
        cost_estimate=pl.CostEstimate(
            flops=2 * count * block * n * n_points * width,
            bytes_accessed=2 * n * n_points * (count * block + width) + 4 * count * block * width,
            transcendentals=0,
        ),
    )(*expos, *points, factor)


def merge(rate, stats):
    highest = functools.reduce(jnp.maximum, [s[0] for s in stats])
    scales = [jnp.exp2((s[0] - highest) * rate) for s in stats]
    total = sum(s[1] * scale for s, scale in zip(stats, scales))
    novel = sum(s[2] * scale for s, scale in zip(stats, scales))
    return jnp.stack([highest, total, novel])


def split_cells(codes, exponents, centroids, counters):
    n = lax.axis_size("cells")
    chip = lax.axis_index("y") * lax.axis_size("x") + lax.axis_index("x")
    lo = lax.axis_index("lo")
    own = to_points(codes, exponents)
    rate = 4.0 / math.sqrt(own.shape[1]) * math.log2(math.e)

    per_device = centroids.shape[0] // (4 * 2)
    block = per_device // 2

    def halves(a):
        start = chip * 2 * per_device
        other = lax.dynamic_slice_in_dim(a, start + (1 - lo) * per_device, per_device)
        return jnp.concatenate([other, lax.dynamic_slice_in_dim(a, start + lo * per_device, per_device)])

    cells = halves(centroids)
    inverse = lax.rsqrt(halves(counters).astype(jnp.float32) + 1.0)[:, None]

    expos, tops, stats, points = [], [], [], []
    for shift in range(n):
        near = rotate(own, "cells", shift) if shift else own
        along_x, along_y = swap(near, "x"), swap(near, "y")
        across = swap(along_x, "y") if shift % 2 else swap(along_y, "x")
        expo, top, stat, chunk = expo_call(rate, block, (near, along_x, along_y, across), cells, inverse)
        from_x, from_y = swap(stat, "x"), swap(stat, "y")
        from_xy = lax.ppermute(stat, ("y", "x"), [(0, 3), (1, 2), (2, 1), (3, 0)])
        place = lambda a, order: a.reshape(3, 4, -1)[:, list(order)].reshape(a.shape)
        stat = merge(
            rate,
            [stat, place(from_x, (1, 0, 3, 2)), place(from_y, (2, 3, 0, 1)), place(from_xy, (3, 2, 1, 0))],
        )
        expos.append(expo), tops.append(top), stats.append(stat), points.append(chunk)

    mine = jnp.stack(stats)
    others = [rotate(mine, "cells", shift) for shift in range(1, n)]
    factors = []
    for shift in range(n):
        top, total, novel = merge(
            rate, [mine[shift]] + [a[(shift - by) % n] for by, a in zip(range(1, n), others)]
        )
        factors.append(jnp.exp2((tops[shift] - top) * rate) * (novel / total / total))
    factor = jnp.stack(factors, axis=1)

    there, mass_there = sums_call(block, 0, 2, expos, points, factor, jnp.bfloat16)
    there, mass_there = swap(there, "lo"), swap(mass_there, "lo")
    here, mass_here = sums_call(block, 2, 2, expos, points, factor, jnp.float32)
    return ((here + there.astype(jnp.float32))[None], (mass_here + mass_there).reshape(1, -1))


def solution(mesh):
    pts, cells = (mesh.shape[name] for name in ("pts", "cells"))
    square = pts == 8
    shape, names = ((2, 2, 2, cells), ("y", "x", "lo", "cells")) if square else ((pts, cells), ("pts", "cells"))
    fine = Mesh(mesh.devices.reshape(shape), names)
    spread = names[:-1]
    in_specs = (P(names, None), P(names), P("cells", None), P("cells"))
    out_specs = (P("cells", spread, None), P("cells", spread))

    def run(codes, exponents, centroids, counters):
        small = codes.size * 2 <= GATHER_BYTES
        body = split_cells if square and small else split_points
        mapped = jax.shard_map(body, mesh=fine, in_specs=in_specs, out_specs=out_specs, check_vma=False)
        return mapped(codes, exponents, centroids, counters)

    return run
```

time: 179 us -> 107 us (0.60)
  blocking collectives: 60.5 us -> 0 us
  waiting for transfers between devices: 67.3 us -> 11.4 us
  starting transfers between devices: 0.04 us -> 37.6 us
  local copies, waits for them, and re-layouts: 3.12 us -> 33.1 us
  matrix products: 17.9 us -> 0 us
  Pallas kernels: 0 us -> 17.7 us
  between operations: 14.7 us -> 1.1 us
  other arithmetic: 15.2 us -> 4.89 us
    reduce_scatter x1 -> x0, waiting for transfers between devices: 67.3 us -> none  [body(): lax.psum_scatter(sums_local, 'pts', scatter_dimension=0, tiled=True)]
    ppermute x0 -> x32, starting transfers between devices: none -> 37.6 us  [the longest x22 21.6 us: swap(): return lax.ppermute(a, axis, [(0, 1), (1, 0)])]
    unnamed x1 -> x0, blocking collectives: 22.4 us -> none
    unnamed x8 -> x62, local copies, waits for them, and re-layouts: 2.53 us -> 22.2 us
    dot_general x3 -> x0, matrix products: 17.9 us -> none  [the longest x1 9.19 us: body(): lax.dot_general(points, centroids, (((1,), (1,)), ((), ())), preferred_el...]
    pallas_call x0 -> x6, Pallas kernels: none -> 17.7 us  [the longest x4 13.5 us: expo_call(): pl.pallas_call(functools.partial(expo_kernel, rate), grid=(steps,), in_sp...]
    all_gather x1 -> x0, blocking collectives: 17.4 us -> none  [body(): points = lax.all_gather(local_rows, 'cells', axis=0, tiled=True)]
    reduce_sum x2 -> x0, other arithmetic: 13.5 us -> none  [the longest x1 6.9 us: body(): jnp.sum(expo, axis=1)]
  transfers between devices with their start and end apart: 1 -> 32, of which waited for: 1 -> 5; matrix products, arithmetic and copies ran while one was open for 1% -> 11% of each run, Pallas kernels for 0% -> 15%
where the time goes in v2:
time: 107 us; the launch traced here: 106 us
  starting transfers between devices  37.6 us (35%)
  local copies, waits for them, and re-layouts  33.1 us (31%)
  Pallas kernels  17.7 us (17%)
  waiting for transfers between devices  11.4 us (11%)
  other arithmetic  4.89 us (5%)
  between operations  1.1 us (1%)
    unnamed x62, local copies, waits for them, and re-layouts  22.2 us
    ppermute x22, starting transfers between devices, swap(): return lax.ppermute(a, axis, [(0, 1), (1, 0)])  21.6 us
    pallas_call x4, Pallas kernels, expo_call(): pl.pallas_call(functools.partial(expo_kernel, rate), grid=(steps,), in_sp...  13.5 us
    ppermute x6, starting transfers between devices, rotate(): return lax.ppermute(a, axis, [((at + by) % size, at) for at in range(size)])  8.95 us
    gather x12, local copies, waits for them, and re-layouts, split_cells(): a.reshape(3, 4, -1)[:, list(order)].reshape(a.shape)  8.06 us
    ppermute x6, waiting for transfers between devices, rotate(): return lax.ppermute(a, axis, [((at + by) % size, at) for at in range(size)])  7.65 us
    ppermute x4, starting transfers between devices, split_cells(): from_xy = lax.ppermute(stat, ('y', 'x'), [(0, 3), (1, 2), (2, 1), (3, 0)])  7 us
    pallas_call x2, Pallas kernels, sums_call(): pl.pallas_call(functools.partial(sums_kernel, n), grid=(count,), in_specs...  4.19 us
  transfers between devices with their start and end apart: 32, of which 5 were waited for; matrix products, arithmetic and copies ran while one was open for 11% of the time, Pallas kernels for 15%

profile of v2, /device:TPU:0, one launch (start us, length us, event | category | flops | bytes accessed | tf_op | source)
XLA Modules:
  0.0 105.7 jit_solution(3242751719732978299)
XLA Ops:
  0.6 0.7 multiply_exponential_fusion.16
  1.3 1.0 multiply_convert_fusion.near
  2.3 3.0 %collective-permute-start = (bf16[128,512]{1,0:T(8,128)(2,1)S(1)}, bf16[128,512]{1,0:T(8,128)(2,1)S(1)}, u32[]{:S(2)}, u32[]{:S(2)}) collective-permute-start(bf16[128,512]{1,0:T(8,128)(2,1)S(1)} %multiply_convert_fusion.near), channel_id=1, source_target_pairs={{0,8},{8,0},{1,9},{9,1},{2,10},{10,2},{3,11},{11,3},{4,12},{12,4},... | collective-permute-start | bytes 393224 | tf_op jit(solution)/shard_map/ppermute | solution.py:48
  5.3 1.5 %collective-permute-start.1 = (bf16[128,512]{1,0:T(8,128)(2,1)S(1)}, bf16[128,512]{1,0:T(8,128)(2,1)S(1)}, u32[]{:S(2)}, u32[]{:S(2)}) collective-permute-start(bf16[128,512]{1,0:T(8,128)(2,1)S(1)} %multiply_convert_fusion.near), channel_id=1, source_target_pairs={{0,16},{16,0},{1,17},{17,1},{2,18},{18,2},{3,19},{19,3},{4,20},{20... | collective-permute-start | bytes 393224 | tf_op jit(solution)/shard_map/ppermute | solution.py:48
  6.9 3.6 %collective-permute-start.3 = (bf16[128,512]{1,0:T(8,128)(2,1)S(1)}, bf16[128,512]{1,0:T(8,128)(2,1)S(1)}, u32[]{:S(2)}, u32[]{:S(2)}) collective-permute-start(bf16[128,512]{1,0:T(8,128)(2,1)S(1)} %multiply_convert_fusion.near), channel_id=1, source_target_pairs={{1,0},{2,1},{3,2},{0,3},{5,4},{6,5},{7,6},{4,7},{9,8},{10,9},{11,1... | collective-permute-start | bytes 393224 | tf_op jit(solution)/shard_map/ppermute | solution.py:53
  10.5 1.0 collective-permute-start.11
  11.5 1.5 %constant_dynamic-slice_fusion.1 = (bf16[768,512]{1,0:T(8,128)(2,1)S(1)}, bf16[768,512]{1,0:T(8,128)(2,1)S(1)}) fusion(bf16[6144,512]{1,0:T(8,128)(2,1)} %param.18, s32[]{:T(128)S(6)} %select_n.44, s32[]{:T(128)S(6)} %select_n.45), kind=kLoop, calls=%fused_computation.231 | loop fusion | bytes 3145736 | tf_op jit(solution)/shard_map/dynamic_slice | solution.py:180
  13.1 0.9 fusion.105
  15.7 5.7 %collective-permute-done.7.near = bf16[128,512]{1,0:T(8,128)(2,1)} collective-permute-done((bf16[128,512]{1,0:T(8,128)(2,1)S(1)}, bf16[128,512]{1,0:T(8,128)(2,1)}, u32[]{:S(2)}, u32[]{:S(2)}) %collective-permute-start.7) | collective-permute-done | bytes 131104 | tf_op jit(solution)/shard_map/ppermute | solution.py:53
  22.4 0.6 copy-done.16
  23.7 0.9 copy-done.17
  24.6 0.9 copy-done.19
  25.5 0.9 copy-done.25
  26.4 2.6 %shard_map.167 = (bf16[1536,512]{1,0:T(8,128)(2,1)S(1)}, f32[4,512]{1,0:T(4,128)S(1)}, f32[3,512]{1,0:T(4,128)S(1)}, bf16[512,512]{1,0:T(8,128)(2,1)S(1)}) custom-call(bf16[128,512]{1,0:T(8,128)(2,1)S(1)} %multiply_convert_fusion.near, bf16[128,512]{1,0:T(8,128)(2,1)S(1)} %copy-done.17, bf16[128,512]{1,0:T(8,128)(2,1)S(1)} %copy-done.19, ...), custom_call_target="tpu_custom_call" | custom-call | flops 805306368 | bytes 3670016 | tf_op jit(solution)/shard_map/pallas_call | solution.py:94
  29.1 0.8 copy-done.4
  29.9 2.4 %collective-permute-start.17 = (f32[3,512]{1,0:T(4,128)S(1)}, f32[3,512]{1,0:T(4,128)S(1)}, u32[]{:S(2)}, u32[]{:S(2)}) collective-permute-start(f32[3,512]{1,0:T(4,128)S(1)} %get-tuple-element.31), channel_id=1, source_target_pairs={{0,24},{8,16},{16,8},{24,0},{1,25},{9,17},{17,9},{25,1},{2,26},{10... | collective-permute-start | bytes 18440 | tf_op jit(solution)/shard_map/ppermute | solution.py:193
  33.0 1.5 %collective-permute-done.17 = f32[3,512]{1,0:T(4,128)S(1)} collective-permute-done((f32[3,512]{1,0:T(4,128)S(1)}, f32[3,512]{1,0:T(4,128)S(1)}, u32[]{:S(2)}, u32[]{:S(2)}) %collective-permute-start.17) | collective-permute-done | bytes 6176 | tf_op jit(solution)/shard_map/ppermute | solution.py:193
  34.5 1.5 %collective-permute-start.15 = (f32[3,512]{1,0:T(4,128)S(1)}, f32[3,512]{1,0:T(4,128)S(1)}, u32[]{:S(2)}, u32[]{:S(2)}) collective-permute-start(f32[3,512]{1,0:T(4,128)S(1)} %get-tuple-element.31), channel_id=1, source_target_pairs={{0,8},{8,0},{1,9},{9,1},{2,10},{10,2},{3,11},{11,3},{4,12},{12,4},... | collective-permute-start | bytes 18440 | tf_op jit(solution)/shard_map/ppermute | solution.py:48
  36.0 0.7 gather_fusion.2
  37.9 1.6 %collective-permute-start.13 = (bf16[128,512]{1,0:T(8,128)(2,1)S(1)}, bf16[128,512]{1,0:T(8,128)(2,1)}, u32[]{:S(2)}, u32[]{:S(2)}) collective-permute-start(bf16[128,512]{1,0:T(8,128)(2,1)S(1)} %collective-permute-done.11.near), channel_id=1, source_target_pairs={{0,16},{16,0},{1,17},{17,1},{2,18},{18,2},{3,19},{19,3},{4,20},{20... | collective-permute-start | bytes 393224 | tf_op jit(solution)/shard_map/ppermute | solution.py:48
  39.4 1.5 %collective-permute-start.4 = (bf16[128,512]{1,0:T(8,128)(2,1)S(1)}, bf16[128,512]{1,0:T(8,128)(2,1)}, u32[]{:S(2)}, u32[]{:S(2)}) collective-permute-start(bf16[128,512]{1,0:T(8,128)(2,1)S(1)} %collective-permute-done.3.near), channel_id=1, source_target_pairs={{0,8},{8,0},{1,9},{9,1},{2,10},{10,2},{3,11},{11,3},{4,12},{12,4},... | collective-permute-start | bytes 393224 | tf_op jit(solution)/shard_map/ppermute | solution.py:48
  42.6 2.1 %collective-permute-done.4.along_x = bf16[128,512]{1,0:T(8,128)(2,1)} collective-permute-done((bf16[128,512]{1,0:T(8,128)(2,1)S(1)}, bf16[128,512]{1,0:T(8,128)(2,1)}, u32[]{:S(2)}, u32[]{:S(2)}) %collective-permute-start.4) | collective-permute-done | bytes 131104 | tf_op jit(solution)/shard_map/ppermute | solution.py:48
  44.8 1.1 %collective-permute-start.5 = (bf16[128,512]{1,0:T(8,128)(2,1)S(1)}, bf16[128,512]{1,0:T(8,128)(2,1)S(1)}, u32[]{:S(2)}, u32[]{:S(2)}) collective-permute-start(bf16[128,512]{1,0:T(8,128)(2,1)S(1)} %collective-permute-done.3.near), channel_id=1, source_target_pairs={{0,16},{16,0},{1,17},{17,1},{2,18},{18,2},{3,19},{19,3},{4,20},{20... | collective-permute-start | bytes 393224 | tf_op jit(solution)/shard_map/ppermute | solution.py:48
  46.5 1.0 collective-permute-start.6
  47.4 0.7 copy-done.22
  48.1 1.4 %copy-done.13 = bf16[1536,512]{1,0:T(8,128)(2,1)S(1)} copy-done((bf16[1536,512]{1,0:T(8,128)(2,1)S(1)}, bf16[1536,512]{1,0:T(8,128)(2,1)}, u32[]{:S(2)}) %copy-start.13) | copy-done | bytes 1572888
  49.5 1.1 %copy-done.15 = f32[1536,1]{1,0:T(8,128)S(1)} copy-done((f32[1536,1]{1,0:T(8,128)S(1)}, f32[1536,1]{1,0:T(8,128)}, u32[]{:S(2)}) %copy-start.15) | copy-done | bytes 6168
  50.7 0.9 copy-done.21
  51.6 0.9 copy-done.23
  52.5 3.6 %shard_map.169 = (bf16[1536,512]{1,0:T(8,128)(2,1)S(1)}, f32[4,512]{1,0:T(4,128)S(1)}, f32[3,512]{1,0:T(4,128)S(1)}, bf16[512,512]{1,0:T(8,128)(2,1)S(1)}) custom-call(bf16[128,512]{1,0:T(8,128)(2,1)} %collective-permute-done.7.near, bf16[128,512]{1,0:T(8,128)(2,1)S(1)} %copy-done.21, bf16[128,512]{1,0:T(8,128)(2,1)} %collective-permute-done.9.along_y, ...), custom_call_target="tpu_custom_call" | custom-call | flops 805306368 | bytes 3670016 | tf_op jit(solution)/shard_map/pallas_call | solution.py:94
  56.1 0.8 copy-done.6
  56.9 1.5 %collective-permute-start.23 = (f32[3,512]{1,0:T(4,128)S(1)}, f32[3,512]{1,0:T(4,128)S(1)}, u32[]{:S(2)}, u32[]{:S(2)}) collective-permute-start(f32[3,512]{1,0:T(4,128)S(1)} %get-tuple-element.33), channel_id=1, source_target_pairs={{0,24},{8,16},{16,8},{24,0},{1,25},{9,17},{17,9},{25,1},{2,26},{10... | collective-permute-start | bytes 18440 | tf_op jit(solution)/shard_map/ppermute | solution.py:193
  58.4 1.4 %collective-permute-start.22 = (f32[3,512]{1,0:T(4,128)S(1)}, f32[3,512]{1,0:T(4,128)S(1)}, u32[]{:S(2)}, u32[]{:S(2)}) collective-permute-start(f32[3,512]{1,0:T(4,128)S(1)} %get-tuple-element.33), channel_id=1, source_target_pairs={{0,16},{16,0},{1,17},{17,1},{2,18},{18,2},{3,19},{19,3},{4,20},{20... | collective-permute-start | bytes 18440 | tf_op jit(solution)/shard_map/ppermute | solution.py:48
  60.4 3.7 %shard_map.170 = (bf16[1536,512]{1,0:T(8,128)(2,1)S(1)}, f32[4,512]{1,0:T(4,128)S(1)}, f32[3,512]{1,0:T(4,128)S(1)}, bf16[512,512]{1,0:T(8,128)(2,1)S(1)}) custom-call(bf16[128,512]{1,0:T(8,128)(2,1)S(1)} %collective-permute-done.11.near, bf16[128,512]{1,0:T(8,128)(2,1)} %collective-permute-done.12.along_x, ...), custom_call_target="tpu_custom_call" | custom-call | flops 805306368 | bytes 3670016 | tf_op jit(solution)/shard_map/pallas_call | solution.py:94
  64.1 1.2 %copy-done = bf16[1536,512]{1,0:T(8,128)(2,1)} copy-done((bf16[1536,512]{1,0:T(8,128)(2,1)}, bf16[1536,512]{1,0:T(8,128)(2,1)S(1)}, u32[]{:S(2)}) %copy-start) | copy-done | bytes 1572888
  65.2 0.8 copy-done.8
  66.1 1.5 %collective-permute-start.26 = (f32[3,512]{1,0:T(4,128)S(1)}, f32[3,512]{1,0:T(4,128)S(1)}, u32[]{:S(2)}, u32[]{:S(2)}) collective-permute-start(f32[3,512]{1,0:T(4,128)S(1)} %get-tuple-element.34), channel_id=1, source_target_pairs={{0,24},{8,16},{16,8},{24,0},{1,25},{9,17},{17,9},{25,1},{2,26},{10... | collective-permute-start | bytes 18440 | tf_op jit(solution)/shard_map/ppermute | solution.py:193
  67.6 1.4 %collective-permute-start.25 = (f32[3,512]{1,0:T(4,128)S(1)}, f32[3,512]{1,0:T(4,128)S(1)}, u32[]{:S(2)}, u32[]{:S(2)}) collective-permute-start(f32[3,512]{1,0:T(4,128)S(1)} %get-tuple-element.34), channel_id=1, source_target_pairs={{0,16},{16,0},{1,17},{17,1},{2,18},{18,2},{3,19},{19,3},{4,20},{20... | collective-permute-start | bytes 18440 | tf_op jit(solution)/shard_map/ppermute | solution.py:48
  69.0 3.6 %shard_map.168 = (bf16[1536,512]{1,0:T(8,128)(2,1)S(1)}, f32[4,512]{1,0:T(4,128)S(1)}, f32[3,512]{1,0:T(4,128)S(1)}, bf16[512,512]{1,0:T(8,128)(2,1)S(1)}) custom-call(bf16[128,512]{1,0:T(8,128)(2,1)S(1)} %collective-permute-done.3.near, bf16[128,512]{1,0:T(8,128)(2,1)} %collective-permute-done.4.along_x, ...), custom_call_target="tpu_custom_call" | custom-call | flops 805306368 | bytes 3670016 | tf_op jit(solution)/shard_map/pallas_call | solution.py:94
  72.6 1.1 %copy-done.2 = bf16[1536,512]{1,0:T(8,128)(2,1)} copy-done((bf16[1536,512]{1,0:T(8,128)(2,1)}, bf16[1536,512]{1,0:T(8,128)(2,1)S(1)}, u32[]{:S(2)}) %copy-start.2) | copy-done | bytes 1572888
  73.7 0.8 copy-done.10
  75.1 0.7 gather_fusion.8
  75.8 1.6 %collective-permute-start.20 = (f32[3,512]{1,0:T(4,128)S(1)}, f32[3,512]{1,0:T(4,128)S(1)}, u32[]{:S(2)}, u32[]{:S(2)}) collective-permute-start(f32[3,512]{1,0:T(4,128)S(1)} %get-tuple-element.32), channel_id=1, source_target_pairs={{0,24},{8,16},{16,8},{24,0},{1,25},{9,17},{17,9},{25,1},{2,26},{10... | collective-permute-start | bytes 18440 | tf_op jit(solution)/shard_map/ppermute | solution.py:193
  77.3 0.7 gather_fusion.7
  78.0 1.5 %collective-permute-start.19 = (f32[3,512]{1,0:T(4,128)S(1)}, f32[3,512]{1,0:T(4,128)S(1)}, u32[]{:S(2)}, u32[]{:S(2)}) collective-permute-start(f32[3,512]{1,0:T(4,128)S(1)} %get-tuple-element.32), channel_id=1, source_target_pairs={{0,16},{16,0},{1,17},{17,1},{2,18},{18,2},{3,19},{19,3},{4,20},{20... | collective-permute-start | bytes 18440 | tf_op jit(solution)/shard_map/ppermute | solution.py:48
  79.5 0.7 gather_fusion.6
  80.9 0.7 gather_fusion.11
  81.6 0.7 gather_fusion.10
  82.3 0.7 gather_fusion.9
  83.1 0.7 gather_fusion.5
  83.8 0.7 gather_fusion.4
  84.5 0.7 gather_fusion.3
  85.4 1.8 %collective-permute-start.28 = (f32[4,3,512]{2,1,0:T(4,128)S(1)}, f32[4,3,512]{2,1,0:T(4,128)S(1)}, u32[]{:S(2)}, u32[]{:S(2)}) collective-permute-start(f32[4,3,512]{2,1,0:T(4,128)S(1)} %pad_maximum_fusion.1), channel_id=1, source_target_pairs={{2,0},{3,1},{0,2},{1,3},{6,4},{7,5},{4,6},{5,7},{10,8},{11,9},{8,1... | collective-permute-start | bytes 73736 | tf_op jit(solution)/shard_map/ppermute | solution.py:53
  87.1 2.5 %collective-permute-start.27 = (f32[4,3,512]{2,1,0:T(4,128)S(1)}, f32[4,3,512]{2,1,0:T(4,128)S(1)}, u32[]{:S(2)}, u32[]{:S(2)}) collective-permute-start(f32[4,3,512]{2,1,0:T(4,128)S(1)} %pad_maximum_fusion.1), channel_id=1, source_target_pairs={{1,0},{2,1},{3,2},{0,3},{5,4},{6,5},{7,6},{4,7},{9,8},{10,9},{11,1... | collective-permute-start | bytes 73736 | tf_op jit(solution)/shard_map/ppermute | solution.py:53
  89.7 1.4 %collective-permute-done.29 = f32[4,3,512]{2,1,0:T(4,128)S(1)} collective-permute-done((f32[4,3,512]{2,1,0:T(4,128)S(1)}, f32[4,3,512]{2,1,0:T(4,128)S(1)}, u32[]{:S(2)}, u32[]{:S(2)}) %collective-permute-start.29) | collective-permute-done | bytes 24608 | tf_op jit(solution)/shard_map/ppermute | solution.py:53
  92.0 1.4 %copy-done.1 = bf16[1536,512]{1,0:T(8,128)(2,1)S(1)} copy-done((bf16[1536,512]{1,0:T(8,128)(2,1)S(1)}, bf16[1536,512]{1,0:T(8,128)(2,1)}, u32[]{:S(2)}) %copy-start.1) | copy-done | bytes 1572888
  93.4 1.4 %copy-done.3 = bf16[1536,512]{1,0:T(8,128)(2,1)S(1)} copy-done((bf16[1536,512]{1,0:T(8,128)(2,1)S(1)}, bf16[1536,512]{1,0:T(8,128)(2,1)}, u32[]{:S(2)}) %copy-start.3) | copy-done | bytes 1572888
  94.8 1.0 copy-done.5
  95.9 1.0 copy-done.7
  96.9 1.0 copy-done.9
  97.9 1.0 copy-done.11
  99.0 2.1 %shard_map.172 = (bf16[768,512]{1,0:T(8,128)(2,1)S(1)}, f32[2,1,384]{2,1,0:T(1,128)S(1)}) custom-call(bf16[1536,512]{1,0:T(8,128)(2,1)S(1)} %get-tuple-element.22.refs_0_, bf16[1536,512]{1,0:T(8,128)(2,1)S(1)} %copy-done.3, bf16[1536,512]{1,0:T(8,128)(2,1)S(1)} %get-tuple-element.24.refs_2_, bf16[1536,512]{1,0:T(8,128)(2,1)S(1)} %copy-done.1, ...), custom_call_target="tpu_custom_call" | custom-call | flops 1610612736 | bytes 6815744 | tf_op jit(solution)/shard_map/pallas_call | solution.py:137
  101.7 2.1 %shard_map.171 = (f32[768,512]{1,0:T(8,128)S(1)}, f32[2,1,384]{2,1,0:T(1,128)S(1)}) custom-call(bf16[1536,512]{1,0:T(8,128)(2,1)S(1)} %get-tuple-element.22.refs_0_, bf16[1536,512]{1,0:T(8,128)(2,1)S(1)} %copy-done.3, bf16[1536,512]{1,0:T(8,128)(2,1)S(1)} %get-tuple-element.24.refs_2_, bf16[1536,512]{1,0:T(8,128)(2,1)S(1)} %copy-done.1, ...), custom_call_target="tpu_custom_call" | custom-call | flops 1610612736 | bytes 6815744 | tf_op jit(solution)/shard_map/pallas_call | solution.py:137
  104.4 1.4 %add_bitcast_fusion = f32[1,768,512]{2,1,0:T(8,128)} fusion(f32[768,512]{1,0:T(8,128)S(1)} %get-tuple-element.38, bf16[768,512]{1,0:T(8,128)(2,1)S(1)} %collective-permute-done.30), kind=kLoop, calls=%fused_computation.13 | loop fusion | flops 786432 | bytes 3932160 | tf_op jit(solution)/shard_map/broadcast_in_dim | solution.py:214
  (119 shorter events, 11.6 us)
Async XLA Ops:
  2.3 20.1 %collective-permute-start = (bf16[128,512]{1,0:T(8,128)(2,1)S(1)}, bf16[128,512]{1,0:T(8,128)(2,1)S(1)}, u32[]{:S(2)}, u32[]{:S(2)}) collective-permute-start(bf16[128,512]{1,0:T(8,128)(2,1)S(1)} %multiply_convert_fusion.near), channel_id=1, source_target_pairs={{0,8},{8,0},{1,9},{9,1},{2,10},{10,2},{3,11},{11,3},{4,12},{12,4},... | collective-permute-start | bytes 393224 | tf_op jit(solution)/shard_map/ppermute | solution.py:48
  5.3 8.7 %collective-permute-start.1 = (bf16[128,512]{1,0:T(8,128)(2,1)S(1)}, bf16[128,512]{1,0:T(8,128)(2,1)S(1)}, u32[]{:S(2)}, u32[]{:S(2)}) collective-permute-start(bf16[128,512]{1,0:T(8,128)(2,1)S(1)} %multiply_convert_fusion.near), channel_id=1, source_target_pairs={{0,16},{16,0},{1,17},{17,1},{2,18},{18,2},{3,19},{19,3},{4,20},{20... | collective-permute-start | bytes 393224 | tf_op jit(solution)/shard_map/ppermute | solution.py:48
  6.9 31.0 %collective-permute-start.3 = (bf16[128,512]{1,0:T(8,128)(2,1)S(1)}, bf16[128,512]{1,0:T(8,128)(2,1)S(1)}, u32[]{:S(2)}, u32[]{:S(2)}) collective-permute-start(bf16[128,512]{1,0:T(8,128)(2,1)S(1)} %multiply_convert_fusion.near), channel_id=1, source_target_pairs={{1,0},{2,1},{3,2},{0,3},{5,4},{6,5},{7,6},{4,7},{9,8},{10,9},{11,1... | collective-permute-start | bytes 393224 | tf_op jit(solution)/shard_map/ppermute | solution.py:53
  10.5 10.9 %collective-permute-start.7 = (bf16[128,512]{1,0:T(8,128)(2,1)S(1)}, bf16[128,512]{1,0:T(8,128)(2,1)}, u32[]{:S(2)}, u32[]{:S(2)}) collective-permute-start(bf16[128,512]{1,0:T(8,128)(2,1)S(1)} %multiply_convert_fusion.near), channel_id=1, source_target_pairs={{2,0},{3,1},{0,2},{1,3},{6,4},{7,5},{4,6},{5,7},{10,8},{11,9},{8,1... | collective-permute-start | bytes 393224 | tf_op jit(solution)/shard_map/ppermute | solution.py:53
  10.5 11.4 %collective-permute-start.11 = (bf16[128,512]{1,0:T(8,128)(2,1)S(1)}, bf16[128,512]{1,0:T(8,128)(2,1)S(1)}, u32[]{:S(2)}, u32[]{:S(2)}) collective-permute-start(bf16[128,512]{1,0:T(8,128)(2,1)S(1)} %multiply_convert_fusion.near), channel_id=1, source_target_pairs={{3,0},{0,1},{1,2},{2,3},{7,4},{4,5},{5,6},{6,7},{11,8},{8,9},{9,10... | collective-permute-start | bytes 393224 | tf_op jit(solution)/shard_map/ppermute | solution.py:53
  13.1 16.0 %copy-start.12 = (bf16[1536,512]{1,0:T(8,128)(2,1)}, bf16[1536,512]{1,0:T(8,128)(2,1)S(1)}, u32[]{:S(2)}) copy-start(bf16[1536,512]{1,0:T(8,128)(2,1)S(1)} %pad_maximum_fusion.cells) | copy-start | bytes 4718596
  13.1 2.0 %copy-start.30 = (s32[4]{0:T(128)S(1)}, s32[4]{0:T(128)}, u32[]{:S(2)}) copy-start(s32[4]{0:T(128)} %constant.97) | copy-start | bytes 52
  14.0 8.4 %copy-start.18 = (bf16[128,512]{1,0:T(8,128)(2,1)}, bf16[128,512]{1,0:T(8,128)(2,1)S(1)}, u32[]{:S(2)}) copy-start(bf16[128,512]{1,0:T(8,128)(2,1)S(1)} %collective-permute-done.1.along_y) | copy-start | bytes 393220
  14.0 9.0 %collective-permute-start.2 = (bf16[128,512]{1,0:T(8,128)(2,1)S(1)}, bf16[128,512]{1,0:T(8,128)(2,1)S(1)}, u32[]{:S(2)}, u32[]{:S(2)}) collective-permute-start(bf16[128,512]{1,0:T(8,128)(2,1)S(1)} %collective-permute-done.1.along_y), channel_id=1, source_target_pairs={{0,8},{8,0},{1,9},{9,1},{2,10},{10,2},{3,11},{11,3},{4,12},{12,4},... | collective-permute-start | bytes 393224 | tf_op jit(solution)/shard_map/ppermute | solution.py:48
  15.1 14.8 %copy-start.14 = (f32[1536,1]{1,0:T(8,128)}, f32[1536,1]{1,0:T(8,128)S(1)}, u32[]{:S(2)}) copy-start(f32[1536,1]{1,0:T(8,128)S(1)} %rsqrt.10.inverse) | copy-start | bytes 18436
  15.1 17.3 %copy-start.29 = (s32[4]{0:T(128)S(1)}, s32[4]{0:T(128)}, u32[]{:S(2)}) copy-start(s32[4]{0:T(128)} %constant.96) | copy-start | bytes 52
  15.1 20.9 %copy-start.28 = (s32[4]{0:T(128)S(1)}, s32[4]{0:T(128)}, u32[]{:S(2)}) copy-start(s32[4]{0:T(128)} %constant.95) | copy-start | bytes 52
  21.4 18.1 %collective-permute-start.9 = (bf16[128,512]{1,0:T(8,128)(2,1)}, bf16[128,512]{1,0:T(8,128)(2,1)}, u32[]{:S(2)}, u32[]{:S(2)}) collective-permute-start(bf16[128,512]{1,0:T(8,128)(2,1)} %collective-permute-done.7.near), channel_id=1, source_target_pairs={{0,16},{16,0},{1,17},{17,1},{2,18},{18,2},{3,19},{19,3},{4,20},{20... | collective-permute-start | bytes 393224 | tf_op jit(solution)/shard_map/ppermute | solution.py:48
  21.9 19.0 %collective-permute-start.12 = (bf16[128,512]{1,0:T(8,128)(2,1)S(1)}, bf16[128,512]{1,0:T(8,128)(2,1)}, u32[]{:S(2)}, u32[]{:S(2)}) collective-permute-start(bf16[128,512]{1,0:T(8,128)(2,1)S(1)} %collective-permute-done.11.near), channel_id=1, source_target_pairs={{0,8},{8,0},{1,9},{9,1},{2,10},{10,2},{3,11},{11,3},{4,12},{12,4},... | collective-permute-start | bytes 393224 | tf_op jit(solution)/shard_map/ppermute | solution.py:48
  22.4 0.6 copy-start.16
  23.1 0.6 copy-start.24
  23.7 0.9 copy-start.17
  24.6 0.9 copy-start.19
  25.5 0.9 copy-start.25
  29.1 0.8 copy-start.4
  29.9 4.5 %collective-permute-start.17 = (f32[3,512]{1,0:T(4,128)S(1)}, f32[3,512]{1,0:T(4,128)S(1)}, u32[]{:S(2)}, u32[]{:S(2)}) collective-permute-start(f32[3,512]{1,0:T(4,128)S(1)} %get-tuple-element.31), channel_id=1, source_target_pairs={{0,24},{8,16},{16,8},{24,0},{1,25},{9,17},{17,9},{25,1},{2,26},{10... | collective-permute-start | bytes 18440 | tf_op jit(solution)/shard_map/ppermute | solution.py:193
  32.4 8.6 %copy-start.26 = (s32[1024]{0:T(1024)}, s32[1024]{0:T(1024)S(1)}, u32[]{:S(2)}) copy-start(s32[1024]{0:T(1024)S(1)} %pad_clamp_fusion.1) | copy-start | bytes 12292
  32.4 4.3 %collective-permute-start.16 = (f32[3,512]{1,0:T(4,128)S(1)}, f32[3,512]{1,0:T(4,128)S(1)}, u32[]{:S(2)}, u32[]{:S(2)}) collective-permute-start(f32[3,512]{1,0:T(4,128)S(1)} %get-tuple-element.31), channel_id=1, source_target_pairs={{0,16},{16,0},{1,17},{17,1},{2,18},{18,2},{3,19},{19,3},{4,20},{20... | collective-permute-start | bytes 18440 | tf_op jit(solution)/shard_map/ppermute | solution.py:48
  34.5 7.0 %collective-permute-start.15 = (f32[3,512]{1,0:T(4,128)S(1)}, f32[3,512]{1,0:T(4,128)S(1)}, u32[]{:S(2)}, u32[]{:S(2)}) collective-permute-start(f32[3,512]{1,0:T(4,128)S(1)} %get-tuple-element.31), channel_id=1, source_target_pairs={{0,8},{8,0},{1,9},{9,1},{2,10},{10,2},{3,11},{11,3},{4,12},{12,4},... | collective-permute-start | bytes 18440 | tf_op jit(solution)/shard_map/ppermute | solution.py:48
  36.0 11.5 %copy-start.27 = (s32[1024]{0:T(1024)}, s32[1024]{0:T(1024)S(1)}, u32[]{:S(2)}) copy-start(s32[1024]{0:T(1024)S(1)} %pad_clamp_fusion.2) | copy-start | bytes 12292
  36.7 9.1 %collective-permute-start.8 = (bf16[128,512]{1,0:T(8,128)(2,1)}, bf16[128,512]{1,0:T(8,128)(2,1)S(1)}, u32[]{:S(2)}, u32[]{:S(2)}) collective-permute-start(bf16[128,512]{1,0:T(8,128)(2,1)} %collective-permute-done.7.near), channel_id=1, source_target_pairs={{0,8},{8,0},{1,9},{9,1},{2,10},{10,2},{3,11},{11,3},{4,12},{12,4},... | collective-permute-start | bytes 393224 | tf_op jit(solution)/shard_map/ppermute | solution.py:48
  37.9 20.5 %collective-permute-start.13 = (bf16[128,512]{1,0:T(8,128)(2,1)S(1)}, bf16[128,512]{1,0:T(8,128)(2,1)}, u32[]{:S(2)}, u32[]{:S(2)}) collective-permute-start(bf16[128,512]{1,0:T(8,128)(2,1)S(1)} %collective-permute-done.11.near), channel_id=1, source_target_pairs={{0,16},{16,0},{1,17},{17,1},{2,18},{18,2},{3,19},{19,3},{4,20},{20... | collective-permute-start | bytes 393224 | tf_op jit(solution)/shard_map/ppermute | solution.py:48
  39.4 5.3 %collective-permute-start.4 = (bf16[128,512]{1,0:T(8,128)(2,1)S(1)}, bf16[128,512]{1,0:T(8,128)(2,1)}, u32[]{:S(2)}, u32[]{:S(2)}) collective-permute-start(bf16[128,512]{1,0:T(8,128)(2,1)S(1)} %collective-permute-done.3.near), channel_id=1, source_target_pairs={{0,8},{8,0},{1,9},{9,1},{2,10},{10,2},{3,11},{11,3},{4,12},{12,4},... | collective-permute-start | bytes 393224 | tf_op jit(solution)/shard_map/ppermute | solution.py:48
  40.9 6.5 %collective-permute-start.10 = (bf16[128,512]{1,0:T(8,128)(2,1)}, bf16[128,512]{1,0:T(8,128)(2,1)S(1)}, u32[]{:S(2)}, u32[]{:S(2)}) collective-permute-start(bf16[128,512]{1,0:T(8,128)(2,1)} %collective-permute-done.9.along_y), channel_id=1, source_target_pairs={{0,8},{8,0},{1,9},{9,1},{2,10},{10,2},{3,11},{11,3},{4,12},{12,4},... | collective-permute-start | bytes 393224 | tf_op jit(solution)/shard_map/ppermute | solution.py:48
  41.5 18.4 %collective-permute-start.14 = (bf16[128,512]{1,0:T(8,128)(2,1)}, bf16[128,512]{1,0:T(8,128)(2,1)}, u32[]{:S(2)}, u32[]{:S(2)}) collective-permute-start(bf16[128,512]{1,0:T(8,128)(2,1)} %collective-permute-done.12.along_x), channel_id=1, source_target_pairs={{0,16},{16,0},{1,17},{17,1},{2,18},{18,2},{3,19},{19,3},{4,20},{20... | collective-permute-start | bytes 393224 | tf_op jit(solution)/shard_map/ppermute | solution.py:48
  44.8 21.3 %collective-permute-start.5 = (bf16[128,512]{1,0:T(8,128)(2,1)S(1)}, bf16[128,512]{1,0:T(8,128)(2,1)S(1)}, u32[]{:S(2)}, u32[]{:S(2)}) collective-permute-start(bf16[128,512]{1,0:T(8,128)(2,1)S(1)} %collective-permute-done.3.near), channel_id=1, source_target_pairs={{0,16},{16,0},{1,17},{17,1},{2,18},{18,2},{3,19},{19,3},{4,20},{20... | collective-permute-start | bytes 393224 | tf_op jit(solution)/shard_map/ppermute | solution.py:48
  45.8 0.6 copy-start.20
  46.5 21.1 %collective-permute-start.6 = (bf16[128,512]{1,0:T(8,128)(2,1)}, bf16[128,512]{1,0:T(8,128)(2,1)S(1)}, u32[]{:S(2)}, u32[]{:S(2)}) collective-permute-start(bf16[128,512]{1,0:T(8,128)(2,1)} %collective-permute-done.4.along_x), channel_id=1, source_target_pairs={{0,16},{16,0},{1,17},{17,1},{2,18},{18,2},{3,19},{19,3},{4,20},{20... | collective-permute-start | bytes 393224 | tf_op jit(solution)/shard_map/ppermute | solution.py:48
  47.4 0.7 copy-start.22
  48.1 1.4 %copy-start.13 = (bf16[1536,512]{1,0:T(8,128)(2,1)S(1)}, bf16[1536,512]{1,0:T(8,128)(2,1)}, u32[]{:S(2)}) copy-start(bf16[1536,512]{1,0:T(8,128)(2,1)} %copy-done.12) | copy-start | bytes 4718596
  49.5 1.1 %copy-start.15 = (f32[1536,1]{1,0:T(8,128)S(1)}, f32[1536,1]{1,0:T(8,128)}, u32[]{:S(2)}) copy-start(f32[1536,1]{1,0:T(8,128)} %copy-done.14) | copy-start | bytes 18436
  50.7 0.9 copy-start.21
  51.6 0.9 copy-start.23
  56.1 0.8 copy-start.6
  56.9 17.6 %collective-permute-start.23 = (f32[3,512]{1,0:T(4,128)S(1)}, f32[3,512]{1,0:T(4,128)S(1)}, u32[]{:S(2)}, u32[]{:S(2)}) collective-permute-start(f32[3,512]{1,0:T(4,128)S(1)} %get-tuple-element.33), channel_id=1, source_target_pairs={{0,24},{8,16},{16,8},{24,0},{1,25},{9,17},{17,9},{25,1},{2,26},{10... | collective-permute-start | bytes 18440 | tf_op jit(solution)/shard_map/ppermute | solution.py:193
  58.4 17.4 %collective-permute-start.22 = (f32[3,512]{1,0:T(4,128)S(1)}, f32[3,512]{1,0:T(4,128)S(1)}, u32[]{:S(2)}, u32[]{:S(2)}) collective-permute-start(f32[3,512]{1,0:T(4,128)S(1)} %get-tuple-element.33), channel_id=1, source_target_pairs={{0,16},{16,0},{1,17},{17,1},{2,18},{18,2},{3,19},{19,3},{4,20},{20... | collective-permute-start | bytes 18440 | tf_op jit(solution)/shard_map/ppermute | solution.py:48
  59.8 18.2 %collective-permute-start.21 = (f32[3,512]{1,0:T(4,128)S(1)}, f32[3,512]{1,0:T(4,128)S(1)}, u32[]{:S(2)}, u32[]{:S(2)}) collective-permute-start(f32[3,512]{1,0:T(4,128)S(1)} %get-tuple-element.33), channel_id=1, source_target_pairs={{0,8},{8,0},{1,9},{9,1},{2,10},{10,2},{3,11},{11,3},{4,12},{12,4},... | collective-permute-start | bytes 18440 | tf_op jit(solution)/shard_map/ppermute | solution.py:48
  64.1 1.2 %copy-start = (bf16[1536,512]{1,0:T(8,128)(2,1)}, bf16[1536,512]{1,0:T(8,128)(2,1)S(1)}, u32[]{:S(2)}) copy-start(bf16[1536,512]{1,0:T(8,128)(2,1)S(1)} %get-tuple-element.25.refs_3_) | copy-start | bytes 4718596
  65.2 0.8 copy-start.8
  66.1 14.2 %collective-permute-start.26 = (f32[3,512]{1,0:T(4,128)S(1)}, f32[3,512]{1,0:T(4,128)S(1)}, u32[]{:S(2)}, u32[]{:S(2)}) collective-permute-start(f32[3,512]{1,0:T(4,128)S(1)} %get-tuple-element.34), channel_id=1, source_target_pairs={{0,24},{8,16},{16,8},{24,0},{1,25},{9,17},{17,9},{25,1},{2,26},{10... | collective-permute-start | bytes 18440 | tf_op jit(solution)/shard_map/ppermute | solution.py:193
  67.6 14.1 %collective-permute-start.25 = (f32[3,512]{1,0:T(4,128)S(1)}, f32[3,512]{1,0:T(4,128)S(1)}, u32[]{:S(2)}, u32[]{:S(2)}) collective-permute-start(f32[3,512]{1,0:T(4,128)S(1)} %get-tuple-element.34), channel_id=1, source_target_pairs={{0,16},{16,0},{1,17},{17,1},{2,18},{18,2},{3,19},{19,3},{4,20},{20... | collective-permute-start | bytes 18440 | tf_op jit(solution)/shard_map/ppermute | solution.py:48
  72.6 1.1 %copy-start.2 = (bf16[1536,512]{1,0:T(8,128)(2,1)}, bf16[1536,512]{1,0:T(8,128)(2,1)S(1)}, u32[]{:S(2)}) copy-start(bf16[1536,512]{1,0:T(8,128)(2,1)S(1)} %get-tuple-element.23.refs_1_) | copy-start | bytes 4718596
  73.7 0.8 copy-start.10
  74.5 7.8 %collective-permute-start.24 = (f32[3,512]{1,0:T(4,128)S(1)}, f32[3,512]{1,0:T(4,128)S(1)}, u32[]{:S(2)}, u32[]{:S(2)}) collective-permute-start(f32[3,512]{1,0:T(4,128)S(1)} %get-tuple-element.34), channel_id=1, source_target_pairs={{0,8},{8,0},{1,9},{9,1},{2,10},{10,2},{3,11},{11,3},{4,12},{12,4},... | collective-permute-start | bytes 18440 | tf_op jit(solution)/shard_map/ppermute | solution.py:48
  75.8 7.3 %collective-permute-start.20 = (f32[3,512]{1,0:T(4,128)S(1)}, f32[3,512]{1,0:T(4,128)S(1)}, u32[]{:S(2)}, u32[]{:S(2)}) collective-permute-start(f32[3,512]{1,0:T(4,128)S(1)} %get-tuple-element.32), channel_id=1, source_target_pairs={{0,24},{8,16},{16,8},{24,0},{1,25},{9,17},{17,9},{25,1},{2,26},{10... | collective-permute-start | bytes 18440 | tf_op jit(solution)/shard_map/ppermute | solution.py:193
  78.0 5.7 %collective-permute-start.19 = (f32[3,512]{1,0:T(4,128)S(1)}, f32[3,512]{1,0:T(4,128)S(1)}, u32[]{:S(2)}, u32[]{:S(2)}) collective-permute-start(f32[3,512]{1,0:T(4,128)S(1)} %get-tuple-element.32), channel_id=1, source_target_pairs={{0,16},{16,0},{1,17},{17,1},{2,18},{18,2},{3,19},{19,3},{4,20},{20... | collective-permute-start | bytes 18440 | tf_op jit(solution)/shard_map/ppermute | solution.py:48
  80.3 4.2 %collective-permute-start.18 = (f32[3,512]{1,0:T(4,128)S(1)}, f32[3,512]{1,0:T(4,128)S(1)}, u32[]{:S(2)}, u32[]{:S(2)}) collective-permute-start(f32[3,512]{1,0:T(4,128)S(1)} %get-tuple-element.32), channel_id=1, source_target_pairs={{0,8},{8,0},{1,9},{9,1},{2,10},{10,2},{3,11},{11,3},{4,12},{12,4},... | collective-permute-start | bytes 18440 | tf_op jit(solution)/shard_map/ppermute | solution.py:48
  85.3 5.8 %collective-permute-start.29 = (f32[4,3,512]{2,1,0:T(4,128)S(1)}, f32[4,3,512]{2,1,0:T(4,128)S(1)}, u32[]{:S(2)}, u32[]{:S(2)}) collective-permute-start(f32[4,3,512]{2,1,0:T(4,128)S(1)} %pad_maximum_fusion.1), channel_id=1, source_target_pairs={{3,0},{0,1},{1,2},{2,3},{7,4},{4,5},{5,6},{6,7},{11,8},{8,9},{9,10... | collective-permute-start | bytes 73736 | tf_op jit(solution)/shard_map/ppermute | solution.py:53
  85.4 5.7 %collective-permute-start.28 = (f32[4,3,512]{2,1,0:T(4,128)S(1)}, f32[4,3,512]{2,1,0:T(4,128)S(1)}, u32[]{:S(2)}, u32[]{:S(2)}) collective-permute-start(f32[4,3,512]{2,1,0:T(4,128)S(1)} %pad_maximum_fusion.1), channel_id=1, source_target_pairs={{2,0},{3,1},{0,2},{1,3},{6,4},{7,5},{4,6},{5,7},{10,8},{11,9},{8,1... | collective-permute-start | bytes 73736 | tf_op jit(solution)/shard_map/ppermute | solution.py:53
  87.1 4.5 %collective-permute-start.27 = (f32[4,3,512]{2,1,0:T(4,128)S(1)}, f32[4,3,512]{2,1,0:T(4,128)S(1)}, u32[]{:S(2)}, u32[]{:S(2)}) collective-permute-start(f32[4,3,512]{2,1,0:T(4,128)S(1)} %pad_maximum_fusion.1), channel_id=1, source_target_pairs={{1,0},{2,1},{3,2},{0,3},{5,4},{6,5},{7,6},{4,7},{9,8},{10,9},{11,1... | collective-permute-start | bytes 73736 | tf_op jit(solution)/shard_map/ppermute | solution.py:53
  92.0 1.4 %copy-start.1 = (bf16[1536,512]{1,0:T(8,128)(2,1)S(1)}, bf16[1536,512]{1,0:T(8,128)(2,1)}, u32[]{:S(2)}) copy-start(bf16[1536,512]{1,0:T(8,128)(2,1)} %copy-done) | copy-start | bytes 4718596
  93.4 1.4 %copy-start.3 = (bf16[1536,512]{1,0:T(8,128)(2,1)S(1)}, bf16[1536,512]{1,0:T(8,128)(2,1)}, u32[]{:S(2)}) copy-start(bf16[1536,512]{1,0:T(8,128)(2,1)} %copy-done.2) | copy-start | bytes 4718596
  94.8 1.0 copy-start.5
  95.9 1.0 copy-start.7
  96.9 1.0 copy-start.9
  97.9 1.0 copy-start.11
  101.1 3.3 %collective-permute-start.30 = (bf16[768,512]{1,0:T(8,128)(2,1)S(1)}, bf16[768,512]{1,0:T(8,128)(2,1)S(1)}, u32[]{:S(2)}, u32[]{:S(2)}) collective-permute-start(bf16[768,512]{1,0:T(8,128)(2,1)S(1)} %get-tuple-element.39), channel_id=1, source_target_pairs={{0,4},{4,0},{1,5},{5,1},{2,6},{6,2},{3,7},{7,3},{8,12},{12,8},{9,1... | collective-permute-start | bytes 2359304 | tf_op jit(solution)/shard_map/ppermute | solution.py:48
  101.2 2.6 %collective-permute-start.31 = (f32[2,1,384]{2,1,0:T(1,128)S(1)}, f32[2,1,384]{2,1,0:T(1,128)S(1)}, u32[]{:S(2)}, u32[]{:S(2)}) collective-permute-start(f32[2,1,384]{2,1,0:T(1,128)S(1)} %get-tuple-element.41), channel_id=1, source_target_pairs={{0,4},{4,0},{1,5},{5,1},{2,6},{6,2},{3,7},{7,3},{8,12},{12,8},{9,1... | collective-permute-start | bytes 9224 | tf_op jit(solution)/shard_map/ppermute | solution.py:48

commit v3 on v0

v3 whole, which is shorter than its diff:
```python
import functools
import math

import jax
import jax.numpy as jnp
from jax import lax
from jax.experimental import pallas as pl
from jax.experimental.pallas import tpu as pltpu
from jax.sharding import Mesh, PartitionSpec as P

GATHER_BYTES = 8 << 20
VMEM_BYTES = 16 << 20


def to_points(codes, exponents):
    scaled = codes.astype(jnp.float32) * jnp.exp2(-exponents.astype(jnp.float32))[:, None]
    return scaled.astype(jnp.bfloat16)


def split_points(codes, exponents, centroids, counters):
    local_rows = to_points(codes, exponents)
    points = lax.all_gather(local_rows, "cells", axis=0, tiled=True)
    beta = 4.0 / math.sqrt(points.shape[1])
    logits = (
        lax.dot_general(
            points, centroids, (((1,), (1,)), ((), ())), preferred_element_type=jnp.float32
        )
        * beta
    )
    inverse = lax.rsqrt(counters.astype(jnp.float32) + 1.0)
    top = lax.pmax(jnp.max(logits, axis=1), "cells")
    expo = jnp.exp(logits - top[:, None])
    total, novel = lax.psum(
        (jnp.sum(expo, axis=1), jnp.dot(expo, inverse, preferred_element_type=jnp.float32)), "cells"
    )
    weight = novel / total
    share = (expo * (weight / total)[:, None]).astype(jnp.bfloat16)
    mass_local = jnp.sum(share.astype(jnp.float32), axis=0)
    sums_local = lax.dot_general(
        share, points, (((0,), (0,)), ((), ())), preferred_element_type=jnp.float32
    )
    sums = lax.psum_scatter(sums_local, "pts", scatter_dimension=0, tiled=True)
    mass = lax.psum_scatter(mass_local, "pts", scatter_dimension=0, tiled=True)
    return (sums[None], mass[None])


def exchange(a, axes, partner):
    count = math.prod(lax.axis_size(axis) for axis in axes)
    return lax.ppermute(a, axes, [(partner(at), at) for at in range(count)])


def in_vmem(n):
    return [pl.BlockSpec(memory_space=pltpu.VMEM)] * n


def points_kernel(codes, exponents, points):
    rows, width = codes.shape
    scale = jnp.exp2(-exponents[...].astype(jnp.float32))
    scale = jnp.broadcast_to(scale, (128, rows)).T
    for at in range(0, width, 128):
        points[:, at : at + 128] = (codes[:, at : at + 128].astype(jnp.float32) * scale).astype(jnp.bfloat16)


def points_call(codes, exponents):
    return pl.pallas_call(
        points_kernel,
        in_specs=in_vmem(2),
        out_specs=in_vmem(1)[0],
        out_shape=jax.ShapeDtypeStruct(codes.shape, jnp.bfloat16),
        compiler_params=pltpu.CompilerParams(vmem_limit_bytes=VMEM_BYTES),
    )(codes, exponents[None])


def expo_kernel(rate, block, place, near, first, second, cells, inverse, expo, tops, stats, points):
    rows = near.shape[0]
    pieces = (near[...], first[...], second[:rows, :], second[rows:, :])
    for at, piece in enumerate(pieces):
        points[pl.ds(pl.multiple_of(place[at] * rows, rows), rows), :] = piece
    every = points[...]
    highest = total = novel = None
    for at in range(cells.shape[0] // block):
        here = slice(at * block, (at + 1) * block)
        logits = lax.dot_general(
            cells[here, :], every, (((1,), (1,)), ((), ())), preferred_element_type=jnp.float32
        )
        top = jnp.max(logits, axis=0, keepdims=True)
        value = jnp.exp2((logits - top) * rate)
        expo[here, :] = value.astype(jnp.bfloat16)
        tops[at : at + 1, :] = top
        part = jnp.sum(value, axis=0, keepdims=True)
        weighed = jnp.concatenate(
            [
                jnp.sum(value[:, i : i + 128] * inverse[here, :], axis=0, keepdims=True)
                for i in range(0, value.shape[1], 128)
            ],
            axis=1,
        )
        if at:
            higher = jnp.maximum(highest, top)
            old, new = jnp.exp2((highest - higher) * rate), jnp.exp2((top - higher) * rate)
            highest, total, novel = higher, total * old + part * new, novel * old + weighed * new
        else:
            highest, total, novel = top, part, weighed
    stats[...] = jnp.concatenate([highest, total, novel], axis=0)


def expo_call(rate, block, place, pieces, cells, inverse):
    count, width = cells.shape
    n_points = sum(piece.shape[0] for piece in pieces)
    return pl.pallas_call(
        functools.partial(expo_kernel, rate, block),
        in_specs=[pl.BlockSpec(memory_space=pltpu.SMEM)] + in_vmem(5),
        out_specs=in_vmem(4),
        out_shape=[
            jax.ShapeDtypeStruct((count, n_points), jnp.bfloat16),
            jax.ShapeDtypeStruct((count // block, n_points), jnp.float32),
            jax.ShapeDtypeStruct((3, n_points), jnp.float32),
            jax.ShapeDtypeStruct((n_points, width), jnp.bfloat16),
        ],
        compiler_params=pltpu.CompilerParams(vmem_limit_bytes=VMEM_BYTES),
        cost_estimate=pl.CostEstimate(
            flops=2 * count * n_points * width,
            bytes_accessed=2 * (count * width + n_points * width + count * n_points),
            transcendentals=count * n_points,
        ),
    )(place, *pieces, cells, inverse)


def weighed_sums(first, count, expos, points, factor):
    total = weight = None
    for at, (expo, chunk) in enumerate(zip(expos, points)):
        scale = factor[at, first // count : first // count + 1, :]
        share = (expo[first : first + count, :].astype(jnp.float32) * scale).astype(jnp.bfloat16)
        part = jnp.dot(share, chunk[...], preferred_element_type=jnp.float32)
        wide = share.astype(jnp.float32)
        lanes = sum(wide[:, i : i + 128] for i in range(0, wide.shape[1], 128))
        total = part if total is None else total + part
        weight = lanes if weight is None else weight + lanes
    return total, jnp.sum(weight.T, axis=0, keepdims=True)


def sums_kernel(n, block, first, *refs):
    expos, points, (factor, sums, mass) = refs[:n], refs[n : 2 * n], refs[2 * n :]
    for at in range(sums.shape[0] // block):
        here = slice(at * block, (at + 1) * block)
        total, weight = weighed_sums((first + at) * block, block, expos, points, factor)
        sums[here, :] = total.astype(sums.dtype)
        mass[:, here] = weight


def last_kernel(n, block, first, *refs):
    expos, points, (factor, early, early_mass, there, there_mass, sums, mass) = refs[:n], refs[n : 2 * n], refs[2 * n :]
    done = early.shape[0]
    sums[:done, :] = early[...] + there[:done, :].astype(jnp.float32)
    mass[:, :done] = early_mass[...] + there_mass[:, :done]
    for at in range(sums.shape[0] // block - done // block):
        here = slice(done + at * block, done + (at + 1) * block)
        total, weight = weighed_sums((first + at) * block, block, expos, points, factor)
        sums[here, :] = total + there[here, :].astype(jnp.float32)
        mass[:, here] = weight + there_mass[:, here]


def sums_call(kernel, block, first, count, expos, points, factor, *more, rows, dtype):
    n = len(expos)
    n_points, width = points[0].shape
    return pl.pallas_call(
        functools.partial(kernel, n, block, first),
        in_specs=in_vmem(2 * n + 1 + len(more)),
        out_specs=in_vmem(2),
        out_shape=[jax.ShapeDtypeStruct((rows, width), dtype), jax.ShapeDtypeStruct((1, rows), jnp.float32)],
        compiler_params=pltpu.CompilerParams(vmem_limit_bytes=VMEM_BYTES),
        cost_estimate=pl.CostEstimate(
            flops=2 * count * block * n * n_points * width,
            bytes_accessed=2 * n * n_points * (count * block + width) + 4 * rows * width,
            transcendentals=0,
        ),
    )(*expos, *points, factor, *more)


def merge(rate, mine, theirs):
    top = jnp.maximum(mine[0], theirs[0])
    old, new = jnp.exp2((mine[0] - top) * rate), jnp.exp2((theirs[0] - top) * rate)
    return jnp.stack([top, mine[1] * old + theirs[1] * new, mine[2] * old + theirs[2] * new])


def split_cells(codes, exponents, centroids, counters):
    chip = lax.axis_index("y") * 2 + lax.axis_index("x")
    lo = lax.axis_index("lo")
    own = points_call(codes, exponents)
    rate = 4.0 / math.sqrt(own.shape[1]) * math.log2(math.e)
    plane = ("y", "x", "lo")

    turn = lambda a: exchange(a, plane, lambda at: at ^ (4 if at % 2 else 2))
    turn_back = lambda a: exchange(a, plane, lambda at: at ^ (2 if at % 2 else 4))
    along_z = lambda a, by: exchange(a, ("cells",), lambda at: at ^ by)
    place = jnp.stack([chip, chip ^ (1 + lo), chip ^ (2 - lo), chip ^ 3]).astype(jnp.int32)

    per_device = centroids.shape[0] // 8
    block = per_device // 2

    def halves(a):
        start = chip * 2 * per_device
        other = lax.dynamic_slice_in_dim(a, start + (1 - lo) * per_device, per_device)
        return jnp.concatenate([other, lax.dynamic_slice_in_dim(a, start + lo * per_device, per_device)])

    cells = halves(centroids)
    inverse = lax.rsqrt(halves(counters).astype(jnp.float32) + 1.0)
    inverse = jnp.broadcast_to(inverse[:, None], (inverse.shape[0], 128))

    expos, tops, stats, points = [], [], [], []
    for step in range(4):
        near = along_z(own, step) if step else own
        first = turn(near)
        second = turn_back(jnp.concatenate([near, first]))
        expo, top, stat, chunk = expo_call(rate, block, place, (near, first, second), cells, inverse)
        expos.append(expo), tops.append(top), stats.append(stat), points.append(chunk)

    stat = jnp.stack(stats, axis=1)
    for axis in ("x", "y"):
        stat = merge(rate, stat, exchange(stat, (axis,), lambda at: at ^ 1))
    for by in (1, 2):
        theirs = along_z(stat, by)
        theirs = jnp.stack([theirs[:, step ^ by] for step in range(4)], axis=1)
        stat = merge(rate, stat, theirs)
    factor = jnp.exp2((jnp.stack(tops) - stat[0][:, None]) * rate) * (stat[2] / stat[1] / stat[1])[:, None]

    sums = functools.partial(sums_call, expos=expos, points=points, factor=factor)
    there, there_mass = sums(sums_kernel, block, 0, 2, rows=per_device, dtype=jnp.bfloat16)
    there, there_mass = (exchange(a, ("lo",), lambda at: at ^ 1) for a in (there, there_mass))
    early, early_mass = sums(sums_kernel, block, 2, 1, rows=block, dtype=jnp.float32)
    out, mass = sums_call(
        last_kernel, block, 3, 1, expos, points, factor, early, early_mass, there, there_mass,
        rows=per_device, dtype=jnp.float32,
    )
    return (out[None], mass)


def solution(mesh):
    pts, cells = (mesh.shape[name] for name in ("pts", "cells"))
    square = (pts, cells) == (8, 4)
    shape, names = ((2, 2, 2, cells), ("y", "x", "lo", "cells")) if square else ((pts, cells), ("pts", "cells"))
    fine = Mesh(mesh.devices.reshape(shape), names)
    spread = names[:-1]
    in_specs = (P(names, None), P(names), P("cells", None), P("cells"))
    out_specs = (P("cells", spread, None), P("cells", spread))

    def run(codes, exponents, centroids, counters):
        small = codes.size * 2 <= GATHER_BYTES
        body = split_cells if square and small else split_points
        mapped = jax.shard_map(body, mesh=fine, in_specs=in_specs, out_specs=out_specs, check_vma=False)
        return mapped(codes, exponents, centroids, counters)

    return run
```

time: 179 us -> 62.8 us (0.35)
  blocking collectives: 60.5 us -> 0 us
  waiting for transfers between devices: 67.3 us -> 18.9 us
  starting transfers between devices: 0.04 us -> 23.3 us
  matrix products: 17.9 us -> 0 us
  Pallas kernels: 0 us -> 14.7 us
  other arithmetic: 15.2 us -> 0.5 us
  between operations: 14.7 us -> 0.83 us
    reduce_scatter x1 -> x0, waiting for transfers between devices: 67.3 us -> none  [body(): lax.psum_scatter(sums_local, 'pts', scatter_dimension=0, tiled=True)]
    ppermute x0 -> x17, starting transfers between devices: none -> 23.3 us  [exchange(): return lax.ppermute(a, axes, [(partner(at), at) for at in range(count)])]
    unnamed x1 -> x0, blocking collectives: 22.4 us -> none
    ppermute x0 -> x17, waiting for transfers between devices: none -> 18.9 us  [exchange(): return lax.ppermute(a, axes, [(partner(at), at) for at in range(count)])]
    dot_general x3 -> x0, matrix products: 17.9 us -> none  [the longest x1 9.19 us: body(): lax.dot_general(points, centroids, (((1,), (1,)), ((), ())), preferred_el...]
    all_gather x1 -> x0, blocking collectives: 17.4 us -> none  [body(): points = lax.all_gather(local_rows, 'cells', axis=0, tiled=True)]
    pallas_call x0 -> x8, Pallas kernels: none -> 14.7 us  [the longest x4 9.22 us: expo_call(): pl.pallas_call(functools.partial(expo_kernel, rate, block), in_specs=[pl....]
    reduce_sum x2 -> x0, other arithmetic: 13.5 us -> none  [the longest x1 6.9 us: body(): jnp.sum(expo, axis=1)]
  transfers between devices with their start and end apart: 1 -> 17, of which waited for: 1 -> 8; matrix products, arithmetic and copies ran while one was open for 1% -> 5% of each run, Pallas kernels for 0% -> 13%
where the time goes in v3:
time: 62.8 us; the launch traced here: 62.5 us
  starting transfers between devices  23.3 us (37%)
  waiting for transfers between devices  18.9 us (30%)
  Pallas kernels  14.7 us (23%)
  local copies, waits for them, and re-layouts  4.24 us (7%)
  between operations  0.83 us (1%)
    ppermute x17, starting transfers between devices, exchange(): return lax.ppermute(a, axes, [(partner(at), at) for at in range(count)])  23.3 us
    ppermute x17, waiting for transfers between devices, exchange(): return lax.ppermute(a, axes, [(partner(at), at) for at in range(count)])  18.9 us
    pallas_call x4, Pallas kernels, expo_call(): pl.pallas_call(functools.partial(expo_kernel, rate, block), in_specs=[pl....  9.22 us
    pallas_call x3, Pallas kernels, sums_call(): pl.pallas_call(functools.partial(kernel, n, block, first), in_specs=in_vm...  5.41 us
    dynamic_slice x2, local copies, waits for them, and re-layouts, halves(): lax.dynamic_slice_in_dim(a, start + (1 - lo) * per_device, per_device)  2.33 us
    unnamed x4, local copies, waits for them, and re-layouts  1.6 us
  transfers between devices with their start and end apart: 17, of which 8 were waited for; matrix products, arithmetic and copies ran while one was open for 5% of the time, Pallas kernels for 13%

profile of v3, /device:TPU:0, one launch (start us, length us, event | category | flops | bytes accessed | tf_op | source)
XLA Modules:
  0.0 62.5 jit_solution(5519193616892504937)
XLA Ops:
  0.6 0.0 copy-start
  0.6 0.9 %copy-done = s32[128,512]{1,0:T(8,128)S(1)} copy-done((s32[128,512]{1,0:T(8,128)S(1)}, s32[128,512]{1,0:T(8,128)}, u32[]{:S(2)}) %copy-start) | copy-done | bytes 262168
  1.6 0.0 copy-start.1
  1.6 0.7 %copy-done.1 = s32[128]{0:T(128)S(1)} copy-done((s32[128]{0:T(128)S(1)}, s32[128]{0:T(128)}, u32[]{:S(2)}) %copy-start.1) | copy-done | bytes 536
  2.2 0.1 shard_map.59.near
  2.4 5.1 %collective-permute-start.8 = (bf16[128,512]{1,0:T(8,128)(2,1)S(1)}, bf16[128,512]{1,0:T(8,128)(2,1)S(1)}, u32[]{:S(2)}, u32[]{:S(2)}) collective-permute-start(bf16[128,512]{1,0:T(8,128)(2,1)S(1)} %shard_map.59.near), channel_id=1, source_target_pairs={{3,0},{2,1},{1,2},{0,3},{7,4},{6,5},{5,6},{4,7},{11,8},{10,9},{9,1... | collective-permute-start | bytes 393224 | tf_op jit(solution)/shard_map/ppermute | solution.py:49
  7.5 0.0 collective-permute-start.5
  7.5 0.6 %collective-permute-start.2 = (bf16[128,512]{1,0:T(8,128)(2,1)S(1)}, bf16[128,512]{1,0:T(8,128)(2,1)S(1)}, u32[]{:S(2)}, u32[]{:S(2)}) collective-permute-start(bf16[128,512]{1,0:T(8,128)(2,1)S(1)} %shard_map.59.near), channel_id=1, source_target_pairs={{1,0},{0,1},{3,2},{2,3},{5,4},{4,5},{7,6},{6,7},{9,8},{8,9},{11,10... | collective-permute-start | bytes 393224 | tf_op jit(solution)/shard_map/ppermute | solution.py:49
  8.1 1.6 %collective-permute-start = (bf16[128,512]{1,0:T(8,128)(2,1)S(1)}, bf16[128,512]{1,0:T(8,128)(2,1)S(1)}, u32[]{:S(2)}, u32[]{:S(2)}) collective-permute-start(bf16[128,512]{1,0:T(8,128)(2,1)S(1)} %shard_map.59.near), channel_id=1, source_target_pairs={{8,0},{20,4},{0,8},{28,12},{24,16},{4,20},{16,24},{12,28},{9,1},{2... | collective-permute-start | bytes 393224 | tf_op jit(solution)/shard_map/ppermute | solution.py:49
  9.7 1.5 %constant_dynamic-slice_fusion.1 = (bf16[768,512]{1,0:T(8,128)(2,1)S(1)}, bf16[768,512]{1,0:T(8,128)(2,1)S(1)}) fusion(bf16[6144,512]{1,0:T(8,128)(2,1)} %param.6, s32[]{:T(128)S(6)} %select_n.8, s32[]{:T(128)S(6)} %select_n.9), kind=kLoop, calls=%fused_computation.92 | loop fusion | bytes 3145736 | tf_op jit(solution)/shard_map/dynamic_slice | solution.py:203
  11.2 0.1 pad_maximum_fusion.cells
  11.3 0.9 %fusion.46 = (s32[768]{0:T(1024)S(1)}, s32[768]{0:T(1024)S(1)}) fusion(s32[6144]{0:T(1024)} %param.7, s32[]{:T(128)S(6)} %select_n.8, s32[]{:T(128)S(6)} %select_n.9), kind=kLoop, calls=%fused_computation.95 | loop fusion | bytes 12296 | tf_op jit(solution)/shard_map/dynamic_slice | solution.py:203
  12.2 0.0 collective-permute-done.8.near
  12.2 1.4 %collective-permute-start.9 = (bf16[128,512]{1,0:T(8,128)(2,1)S(1)}, bf16[128,512]{1,0:T(8,128)(2,1)S(1)}, u32[]{:S(2)}, u32[]{:S(2)}) collective-permute-start(bf16[128,512]{1,0:T(8,128)(2,1)S(1)} %collective-permute-done.8.near), channel_id=1, source_target_pairs={{8,0},{20,4},{0,8},{28,12},{24,16},{4,20},{16,24},{12,28},{9,1},{2... | collective-permute-start | bytes 393224 | tf_op jit(solution)/shard_map/ppermute | solution.py:49
  13.6 4.9 %collective-permute-done.5.near = bf16[128,512]{1,0:T(8,128)(2,1)S(1)} collective-permute-done((bf16[128,512]{1,0:T(8,128)(2,1)S(1)}, bf16[128,512]{1,0:T(8,128)(2,1)S(1)}, u32[]{:S(2)}, u32[]{:S(2)}) %collective-permute-start.5) | collective-permute-done | bytes 131104 | tf_op jit(solution)/shard_map/ppermute | solution.py:49
  18.5 1.5 %collective-permute-start.6 = (bf16[128,512]{1,0:T(8,128)(2,1)S(1)}, bf16[128,512]{1,0:T(8,128)(2,1)S(1)}, u32[]{:S(2)}, u32[]{:S(2)}) collective-permute-start(bf16[128,512]{1,0:T(8,128)(2,1)S(1)} %collective-permute-done.5.near), channel_id=1, source_target_pairs={{8,0},{20,4},{0,8},{28,12},{24,16},{4,20},{16,24},{12,28},{9,1},{2... | collective-permute-start | bytes 393224 | tf_op jit(solution)/shard_map/ppermute | solution.py:49
  20.0 0.0 collective-permute-done.first
  20.1 1.6 %collective-permute-start.1 = (bf16[256,512]{1,0:T(8,128)(2,1)S(1)}, bf16[256,512]{1,0:T(8,128)(2,1)S(1)}, u32[]{:S(2)}, u32[]{:S(2)}) collective-permute-start(bf16[256,512]{1,0:T(8,128)(2,1)S(1)} %pad_maximum_fusion.1), channel_id=1, source_target_pairs={{16,0},{12,4},{24,8},{4,12},{0,16},{28,20},{8,24},{20,28},{17,1},{... | collective-permute-start | bytes 786440 | tf_op jit(solution)/shard_map/ppermute | solution.py:49
  21.6 0.0 collective-permute-done.2.near
  21.6 0.5 collective-permute-start.3
  22.2 0.0 collective-permute-done.9.first
  22.2 0.6 collective-permute-start.10
  22.8 2.1 %collective-permute-done.6.first = bf16[128,512]{1,0:T(8,128)(2,1)S(1)} collective-permute-done((bf16[128,512]{1,0:T(8,128)(2,1)S(1)}, bf16[128,512]{1,0:T(8,128)(2,1)S(1)}, u32[]{:S(2)}, u32[]{:S(2)}) %collective-permute-start.6) | collective-permute-done | bytes 131104 | tf_op jit(solution)/shard_map/ppermute | solution.py:49
  24.9 1.7 %collective-permute-start.7 = (bf16[256,512]{1,0:T(8,128)(2,1)S(1)}, bf16[256,512]{1,0:T(8,128)(2,1)S(1)}, u32[]{:S(2)}, u32[]{:S(2)}) collective-permute-start(bf16[256,512]{1,0:T(8,128)(2,1)S(1)} %pad_maximum_fusion.3), channel_id=1, source_target_pairs={{16,0},{12,4},{24,8},{4,12},{0,16},{28,20},{8,24},{20,28},{17,1},{... | collective-permute-start | bytes 786440 | tf_op jit(solution)/shard_map/ppermute | solution.py:49
  26.6 1.5 %collective-permute-done.3.first = bf16[128,512]{1,0:T(8,128)(2,1)S(1)} collective-permute-done((bf16[128,512]{1,0:T(8,128)(2,1)S(1)}, bf16[128,512]{1,0:T(8,128)(2,1)S(1)}, u32[]{:S(2)}, u32[]{:S(2)}) %collective-permute-start.3) | collective-permute-done | bytes 131104 | tf_op jit(solution)/shard_map/ppermute | solution.py:49
  28.1 1.3 %collective-permute-start.4 = (bf16[256,512]{1,0:T(8,128)(2,1)S(1)}, bf16[256,512]{1,0:T(8,128)(2,1)S(1)}, u32[]{:S(2)}, u32[]{:S(2)}) collective-permute-start(bf16[256,512]{1,0:T(8,128)(2,1)S(1)} %pad_maximum_fusion.2), channel_id=1, source_target_pairs={{16,0},{12,4},{24,8},{4,12},{0,16},{28,20},{8,24},{20,28},{17,1},{... | collective-permute-start | bytes 786440 | tf_op jit(solution)/shard_map/ppermute | solution.py:49
  29.4 0.1 pad_add_fusion.place
  29.5 0.0 collective-permute-done.1.second
  29.5 0.3 broadcast_in_dim.14.inverse
  29.7 2.3 %shard_map.60 = (bf16[1536,512]{1,0:T(8,128)(2,1)S(1)}, f32[4,512]{1,0:T(4,128)S(1)}, f32[3,512]{1,0:T(4,128)S(1)}, bf16[512,512]{1,0:T(8,128)(2,1)S(1)}) custom-call(s32[4]{0:T(128)S(1)} %pad_add_fusion.place, bf16[128,512]{1,0:T(8,128)(2,1)S(1)} %shard_map.59.near, bf16[128,512]{1,0:T(8,128)(2,1)S(1)} %collective-permute-done.first, ...), custom_call_target="tpu_custom_call" | custom-call | flops 805306368 | bytes 3670016 | tf_op jit(solution)/shard_map/pallas_call | solution.py:110
  32.0 0.0 collective-permute-done.10.second
  32.0 2.3 %shard_map.63 = (bf16[1536,512]{1,0:T(8,128)(2,1)S(1)}, f32[4,512]{1,0:T(4,128)S(1)}, f32[3,512]{1,0:T(4,128)S(1)}, bf16[512,512]{1,0:T(8,128)(2,1)S(1)}) custom-call(s32[4]{0:T(128)S(1)} %pad_add_fusion.place, bf16[128,512]{1,0:T(8,128)(2,1)S(1)} %collective-permute-done.8.near, bf16[128,512]{1,0:T(8,128)(2,1)S(1)} %collective-permute-done.9.first, ...), custom_call_target="tpu_custom_call" | custom-call | flops 805306368 | bytes 3670016 | tf_op jit(solution)/shard_map/pallas_call | solution.py:110
  34.3 0.0 collective-permute-done.7.second
  34.4 2.3 %shard_map.62 = (bf16[1536,512]{1,0:T(8,128)(2,1)S(1)}, f32[4,512]{1,0:T(4,128)S(1)}, f32[3,512]{1,0:T(4,128)S(1)}, bf16[512,512]{1,0:T(8,128)(2,1)S(1)}) custom-call(s32[4]{0:T(128)S(1)} %pad_add_fusion.place, bf16[128,512]{1,0:T(8,128)(2,1)S(1)} %collective-permute-done.5.near, bf16[128,512]{1,0:T(8,128)(2,1)S(1)} %collective-permute-done.6.first, ...), custom_call_target="tpu_custom_call" | custom-call | flops 805306368 | bytes 3670016 | tf_op jit(solution)/shard_map/pallas_call | solution.py:110
  36.7 0.0 collective-permute-done.4.second
  36.7 2.3 %shard_map.61 = (bf16[1536,512]{1,0:T(8,128)(2,1)S(1)}, f32[4,512]{1,0:T(4,128)S(1)}, f32[3,512]{1,0:T(4,128)S(1)}, bf16[512,512]{1,0:T(8,128)(2,1)S(1)}) custom-call(s32[4]{0:T(128)S(1)} %pad_add_fusion.place, bf16[128,512]{1,0:T(8,128)(2,1)S(1)} %collective-permute-done.2.near, bf16[128,512]{1,0:T(8,128)(2,1)S(1)} %collective-permute-done.3.first, ...), custom_call_target="tpu_custom_call" | custom-call | flops 805306368 | bytes 3670016 | tf_op jit(solution)/shard_map/pallas_call | solution.py:110
  39.0 1.6 %collective-permute-start.11 = (f32[3,4,512]{2,1,0:T(4,128)S(1)}, f32[3,4,512]{2,1,0:T(4,128)S(1)}, u32[]{:S(2)}, u32[]{:S(2)}) collective-permute-start(f32[3,4,512]{2,1,0:T(4,128)S(1)} %copy.6), channel_id=1, source_target_pairs={{8,0},{0,8},{9,1},{1,9},{10,2},{2,10},{11,3},{3,11},{12,4},{4,12},... | collective-permute-start | bytes 73736 | tf_op jit(solution)/shard_map/ppermute | solution.py:49
  40.6 2.3 %collective-permute-done.11 = f32[3,4,512]{2,1,0:T(4,128)S(1)} collective-permute-done((f32[3,4,512]{2,1,0:T(4,128)S(1)}, f32[3,4,512]{2,1,0:T(4,128)S(1)}, u32[]{:S(2)}, u32[]{:S(2)}) %collective-permute-start.11) | collective-permute-done | bytes 24608 | tf_op jit(solution)/shard_map/ppermute | solution.py:49
  43.0 0.9 %collective-permute-start.12 = (f32[3,4,512]{2,1,0:T(4,128)S(1)}, f32[3,4,512]{2,1,0:T(4,128)S(1)}, u32[]{:S(2)}, u32[]{:S(2)}) collective-permute-start(f32[3,4,512]{2,1,0:T(4,128)S(1)} %pad_maximum_fusion.6), channel_id=1, source_target_pairs={{16,0},{0,16},{17,1},{1,17},{18,2},{2,18},{19,3},{3,19},{20,4},{4,... | collective-permute-start | bytes 73736 | tf_op jit(solution)/shard_map/ppermute | solution.py:49
  43.9 3.0 %collective-permute-done.12 = f32[3,4,512]{2,1,0:T(4,128)S(1)} collective-permute-done((f32[3,4,512]{2,1,0:T(4,128)S(1)}, f32[3,4,512]{2,1,0:T(4,128)S(1)}, u32[]{:S(2)}, u32[]{:S(2)}) %collective-permute-start.12) | collective-permute-done | bytes 24608 | tf_op jit(solution)/shard_map/ppermute | solution.py:49
  46.9 1.5 %collective-permute-start.13 = (f32[3,4,512]{2,1,0:T(4,128)S(1)}, f32[3,4,512]{2,1,0:T(4,128)S(1)}, u32[]{:S(2)}, u32[]{:S(2)}) collective-permute-start(f32[3,4,512]{2,1,0:T(4,128)S(1)} %pad_maximum_fusion.7), channel_id=1, source_target_pairs={{1,0},{0,1},{3,2},{2,3},{5,4},{4,5},{7,6},{6,7},{9,8},{8,9},{11,10... | collective-permute-start | bytes 73736 | tf_op jit(solution)/shard_map/ppermute | solution.py:49
  48.4 2.4 %collective-permute-done.13 = f32[3,4,512]{2,1,0:T(4,128)S(1)} collective-permute-done((f32[3,4,512]{2,1,0:T(4,128)S(1)}, f32[3,4,512]{2,1,0:T(4,128)S(1)}, u32[]{:S(2)}, u32[]{:S(2)}) %collective-permute-start.13) | collective-permute-done | bytes 24608 | tf_op jit(solution)/shard_map/ppermute | solution.py:49
  50.9 2.8 %collective-permute-start.14 = (f32[3,4,512]{2,1,0:T(4,128)S(1)}, f32[3,4,512]{2,1,0:T(4,128)S(1)}, u32[]{:S(2)}, u32[]{:S(2)}) collective-permute-start(f32[3,4,512]{2,1,0:T(4,128)S(1)} %pad_maximum_fusion.9), channel_id=1, source_target_pairs={{2,0},{3,1},{0,2},{1,3},{6,4},{7,5},{4,6},{5,7},{10,8},{11,9},{8,1... | collective-permute-start | bytes 73736 | tf_op jit(solution)/shard_map/ppermute | solution.py:49
  53.7 2.0 %collective-permute-done.14 = f32[3,4,512]{2,1,0:T(4,128)S(1)} collective-permute-done((f32[3,4,512]{2,1,0:T(4,128)S(1)}, f32[3,4,512]{2,1,0:T(4,128)S(1)}, u32[]{:S(2)}, u32[]{:S(2)}) %collective-permute-start.14) | collective-permute-done | bytes 24608 | tf_op jit(solution)/shard_map/ppermute | solution.py:49
  55.7 0.1 fusion.7
  55.8 2.1 %shard_map.65 = (bf16[768,512]{1,0:T(8,128)(2,1)S(1)}, f32[1,768]{1,0:T(1,128)S(1)}) custom-call(bf16[1536,512]{1,0:T(8,128)(2,1)S(1)} %get-tuple-element.24.refs_0_, bf16[1536,512]{1,0:T(8,128)(2,1)S(1)} %get-tuple-element.25.refs_1_, bf16[1536,512]{1,0:T(8,128)(2,1)S(1)} %get-tuple-element.26.refs_2_, bf16[1536,512]{1,0:T(8,128)(2,1)S(1)} %get-tuple-element.27.refs_3_, ...), custom_call_target="tpu_custom_call" | custom-call | flops 1610612736 | bytes 6815744 | tf_op jit(solution)/shard_map/pallas_call | solution.py:166
  57.9 0.1 collective-permute-start.15
  58.0 0.5 collective-permute-start.16
  58.5 1.1 %shard_map.64 = (f32[384,512]{1,0:T(8,128)S(1)}, f32[1,384]{1,0:T(1,128)S(1)}) custom-call(bf16[1536,512]{1,0:T(8,128)(2,1)S(1)} %get-tuple-element.24.refs_0_, bf16[1536,512]{1,0:T(8,128)(2,1)S(1)} %get-tuple-element.25.refs_1_, bf16[1536,512]{1,0:T(8,128)(2,1)S(1)} %get-tuple-element.26.refs_2_, bf16[1536,512]{1,0:T(8,128)(2,1)S(1)} %get-tuple-element.27.refs_3_, ...), custom_call_target="tpu_custom_call" | custom-call | flops 805306368 | bytes 4456448 | tf_op jit(solution)/shard_map/pallas_call | solution.py:166
  59.5 0.7 %collective-permute-done.16.refs_12_ = f32[1,768]{1,0:T(1,128)S(1)} collective-permute-done((f32[1,768]{1,0:T(1,128)S(1)}, f32[1,768]{1,0:T(1,128)S(1)}, u32[]{:S(2)}, u32[]{:S(2)}) %collective-permute-start.16) | collective-permute-done | bytes 3104 | tf_op jit(solution)/shard_map/ppermute | solution.py:49
  60.2 0.0 collective-permute-done.15.refs_11_
  60.2 2.3 %shard_map.66 = (f32[768,512]{1,0:T(8,128)}, f32[1,768]{1,0:T(1,128)}) custom-call(bf16[1536,512]{1,0:T(8,128)(2,1)S(1)} %get-tuple-element.24.refs_0_, bf16[1536,512]{1,0:T(8,128)(2,1)S(1)} %get-tuple-element.25.refs_1_, bf16[1536,512]{1,0:T(8,128)(2,1)S(1)} %get-tuple-element.26.refs_2_, bf16[1536,512]{1,0:T(8,128)(2,1)S(1)} %get-tuple-element.27.refs_3_, ...), custom_call_target="tpu_custom_call" | custom-call | flops 805306368 | bytes 5242880 | tf_op jit(solution)/shard_map/pallas_call | solution.py:166
  (20 shorter events, 0.3 us)
Async XLA Ops:
  0.6 1.0 %copy-start = (s32[128,512]{1,0:T(8,128)S(1)}, s32[128,512]{1,0:T(8,128)}, u32[]{:S(2)}) copy-start(s32[128,512]{1,0:T(8,128)} %codes.1) | copy-start | bytes 786436
  1.6 0.7 %copy-start.1 = (s32[128]{0:T(128)S(1)}, s32[128]{0:T(128)}, u32[]{:S(2)}) copy-start(s32[128]{0:T(128)} %param.5) | copy-start | bytes 1540
  2.4 9.8 %collective-permute-start.8 = (bf16[128,512]{1,0:T(8,128)(2,1)S(1)}, bf16[128,512]{1,0:T(8,128)(2,1)S(1)}, u32[]{:S(2)}, u32[]{:S(2)}) collective-permute-start(bf16[128,512]{1,0:T(8,128)(2,1)S(1)} %shard_map.59.near), channel_id=1, source_target_pairs={{3,0},{2,1},{1,2},{0,3},{7,4},{6,5},{5,6},{4,7},{11,8},{10,9},{9,1... | collective-permute-start | bytes 393224 | tf_op jit(solution)/shard_map/ppermute | solution.py:49
  7.5 11.1 %collective-permute-start.5 = (bf16[128,512]{1,0:T(8,128)(2,1)S(1)}, bf16[128,512]{1,0:T(8,128)(2,1)S(1)}, u32[]{:S(2)}, u32[]{:S(2)}) collective-permute-start(bf16[128,512]{1,0:T(8,128)(2,1)S(1)} %shard_map.59.near), channel_id=1, source_target_pairs={{2,0},{3,1},{0,2},{1,3},{6,4},{7,5},{4,6},{5,7},{10,8},{11,9},{8,1... | collective-permute-start | bytes 393224 | tf_op jit(solution)/shard_map/ppermute | solution.py:49
  7.5 14.2 %collective-permute-start.2 = (bf16[128,512]{1,0:T(8,128)(2,1)S(1)}, bf16[128,512]{1,0:T(8,128)(2,1)S(1)}, u32[]{:S(2)}, u32[]{:S(2)}) collective-permute-start(bf16[128,512]{1,0:T(8,128)(2,1)S(1)} %shard_map.59.near), channel_id=1, source_target_pairs={{1,0},{0,1},{3,2},{2,3},{5,4},{4,5},{7,6},{6,7},{9,8},{8,9},{11,10... | collective-permute-start | bytes 393224 | tf_op jit(solution)/shard_map/ppermute | solution.py:49
  8.1 11.9 %collective-permute-start = (bf16[128,512]{1,0:T(8,128)(2,1)S(1)}, bf16[128,512]{1,0:T(8,128)(2,1)S(1)}, u32[]{:S(2)}, u32[]{:S(2)}) collective-permute-start(bf16[128,512]{1,0:T(8,128)(2,1)S(1)} %shard_map.59.near), channel_id=1, source_target_pairs={{8,0},{20,4},{0,8},{28,12},{24,16},{4,20},{16,24},{12,28},{9,1},{2... | collective-permute-start | bytes 393224 | tf_op jit(solution)/shard_map/ppermute | solution.py:49
  12.2 10.0 %collective-permute-start.9 = (bf16[128,512]{1,0:T(8,128)(2,1)S(1)}, bf16[128,512]{1,0:T(8,128)(2,1)S(1)}, u32[]{:S(2)}, u32[]{:S(2)}) collective-permute-start(bf16[128,512]{1,0:T(8,128)(2,1)S(1)} %collective-permute-done.8.near), channel_id=1, source_target_pairs={{8,0},{20,4},{0,8},{28,12},{24,16},{4,20},{16,24},{12,28},{9,1},{2... | collective-permute-start | bytes 393224 | tf_op jit(solution)/shard_map/ppermute | solution.py:49
  18.5 6.3 %collective-permute-start.6 = (bf16[128,512]{1,0:T(8,128)(2,1)S(1)}, bf16[128,512]{1,0:T(8,128)(2,1)S(1)}, u32[]{:S(2)}, u32[]{:S(2)}) collective-permute-start(bf16[128,512]{1,0:T(8,128)(2,1)S(1)} %collective-permute-done.5.near), channel_id=1, source_target_pairs={{8,0},{20,4},{0,8},{28,12},{24,16},{4,20},{16,24},{12,28},{9,1},{2... | collective-permute-start | bytes 393224 | tf_op jit(solution)/shard_map/ppermute | solution.py:49
  20.1 9.4 %collective-permute-start.1 = (bf16[256,512]{1,0:T(8,128)(2,1)S(1)}, bf16[256,512]{1,0:T(8,128)(2,1)S(1)}, u32[]{:S(2)}, u32[]{:S(2)}) collective-permute-start(bf16[256,512]{1,0:T(8,128)(2,1)S(1)} %pad_maximum_fusion.1), channel_id=1, source_target_pairs={{16,0},{12,4},{24,8},{4,12},{0,16},{28,20},{8,24},{20,28},{17,1},{... | collective-permute-start | bytes 786440 | tf_op jit(solution)/shard_map/ppermute | solution.py:49
  21.6 6.4 %collective-permute-start.3 = (bf16[128,512]{1,0:T(8,128)(2,1)S(1)}, bf16[128,512]{1,0:T(8,128)(2,1)S(1)}, u32[]{:S(2)}, u32[]{:S(2)}) collective-permute-start(bf16[128,512]{1,0:T(8,128)(2,1)S(1)} %collective-permute-done.2.near), channel_id=1, source_target_pairs={{8,0},{20,4},{0,8},{28,12},{24,16},{4,20},{16,24},{12,28},{9,1},{2... | collective-permute-start | bytes 393224 | tf_op jit(solution)/shard_map/ppermute | solution.py:49
  22.2 9.8 %collective-permute-start.10 = (bf16[256,512]{1,0:T(8,128)(2,1)S(1)}, bf16[256,512]{1,0:T(8,128)(2,1)S(1)}, u32[]{:S(2)}, u32[]{:S(2)}) collective-permute-start(bf16[256,512]{1,0:T(8,128)(2,1)S(1)} %pad_maximum_fusion.4), channel_id=1, source_target_pairs={{16,0},{12,4},{24,8},{4,12},{0,16},{28,20},{8,24},{20,28},{17,1},{... | collective-permute-start | bytes 786440 | tf_op jit(solution)/shard_map/ppermute | solution.py:49
  24.9 9.5 %collective-permute-start.7 = (bf16[256,512]{1,0:T(8,128)(2,1)S(1)}, bf16[256,512]{1,0:T(8,128)(2,1)S(1)}, u32[]{:S(2)}, u32[]{:S(2)}) collective-permute-start(bf16[256,512]{1,0:T(8,128)(2,1)S(1)} %pad_maximum_fusion.3), channel_id=1, source_target_pairs={{16,0},{12,4},{24,8},{4,12},{0,16},{28,20},{8,24},{20,28},{17,1},{... | collective-permute-start | bytes 786440 | tf_op jit(solution)/shard_map/ppermute | solution.py:49
  28.1 8.6 %collective-permute-start.4 = (bf16[256,512]{1,0:T(8,128)(2,1)S(1)}, bf16[256,512]{1,0:T(8,128)(2,1)S(1)}, u32[]{:S(2)}, u32[]{:S(2)}) collective-permute-start(bf16[256,512]{1,0:T(8,128)(2,1)S(1)} %pad_maximum_fusion.2), channel_id=1, source_target_pairs={{16,0},{12,4},{24,8},{4,12},{0,16},{28,20},{8,24},{20,28},{17,1},{... | collective-permute-start | bytes 786440 | tf_op jit(solution)/shard_map/ppermute | solution.py:49
  39.0 3.9 %collective-permute-start.11 = (f32[3,4,512]{2,1,0:T(4,128)S(1)}, f32[3,4,512]{2,1,0:T(4,128)S(1)}, u32[]{:S(2)}, u32[]{:S(2)}) collective-permute-start(f32[3,4,512]{2,1,0:T(4,128)S(1)} %copy.6), channel_id=1, source_target_pairs={{8,0},{0,8},{9,1},{1,9},{10,2},{2,10},{11,3},{3,11},{12,4},{4,12},... | collective-permute-start | bytes 73736 | tf_op jit(solution)/shard_map/ppermute | solution.py:49
  43.0 3.9 %collective-permute-start.12 = (f32[3,4,512]{2,1,0:T(4,128)S(1)}, f32[3,4,512]{2,1,0:T(4,128)S(1)}, u32[]{:S(2)}, u32[]{:S(2)}) collective-permute-start(f32[3,4,512]{2,1,0:T(4,128)S(1)} %pad_maximum_fusion.6), channel_id=1, source_target_pairs={{16,0},{0,16},{17,1},{1,17},{18,2},{2,18},{19,3},{3,19},{20,4},{4,... | collective-permute-start | bytes 73736 | tf_op jit(solution)/shard_map/ppermute | solution.py:49
  46.9 3.9 %collective-permute-start.13 = (f32[3,4,512]{2,1,0:T(4,128)S(1)}, f32[3,4,512]{2,1,0:T(4,128)S(1)}, u32[]{:S(2)}, u32[]{:S(2)}) collective-permute-start(f32[3,4,512]{2,1,0:T(4,128)S(1)} %pad_maximum_fusion.7), channel_id=1, source_target_pairs={{1,0},{0,1},{3,2},{2,3},{5,4},{4,5},{7,6},{6,7},{9,8},{8,9},{11,10... | collective-permute-start | bytes 73736 | tf_op jit(solution)/shard_map/ppermute | solution.py:49
  50.9 4.8 %collective-permute-start.14 = (f32[3,4,512]{2,1,0:T(4,128)S(1)}, f32[3,4,512]{2,1,0:T(4,128)S(1)}, u32[]{:S(2)}, u32[]{:S(2)}) collective-permute-start(f32[3,4,512]{2,1,0:T(4,128)S(1)} %pad_maximum_fusion.9), channel_id=1, source_target_pairs={{2,0},{3,1},{0,2},{1,3},{6,4},{7,5},{4,6},{5,7},{10,8},{11,9},{8,1... | collective-permute-start | bytes 73736 | tf_op jit(solution)/shard_map/ppermute | solution.py:49
  57.9 2.3 %collective-permute-start.15 = (bf16[768,512]{1,0:T(8,128)(2,1)S(1)}, bf16[768,512]{1,0:T(8,128)(2,1)S(1)}, u32[]{:S(2)}, u32[]{:S(2)}) collective-permute-start(bf16[768,512]{1,0:T(8,128)(2,1)S(1)} %get-tuple-element.42), channel_id=1, source_target_pairs={{4,0},{0,4},{5,1},{1,5},{6,2},{2,6},{7,3},{3,7},{12,8},{8,12},{13,... | collective-permute-start | bytes 2359304 | tf_op jit(solution)/shard_map/ppermute | solution.py:49
  58.0 2.3 %collective-permute-start.16 = (f32[1,768]{1,0:T(1,128)S(1)}, f32[1,768]{1,0:T(1,128)S(1)}, u32[]{:S(2)}, u32[]{:S(2)}) collective-permute-start(f32[1,768]{1,0:T(1,128)S(1)} %get-tuple-element.43), channel_id=1, source_target_pairs={{4,0},{0,4},{5,1},{1,5},{6,2},{2,6},{7,3},{3,7},{12,8},{8,12},{13,... | collective-permute-start | bytes 9224 | tf_op jit(solution)/shard_map/ppermute | solution.py:49

commit v4 on v3

--- a/solution.py
+++ b/solution.py
@@ -13,8 +13,8 @@
 
 
 def to_points(codes, exponents):
-    scaled = codes.astype(jnp.float32) * jnp.exp2(-exponents.astype(jnp.float32))[:, None]
-    return scaled.astype(jnp.bfloat16)
+    scale = lax.shift_left(jnp.ones_like(exponents), 16 - exponents).astype(jnp.float32) * 2.0**-16
+    return (codes.astype(jnp.float32) * scale[:, None]).astype(jnp.bfloat16)
 
 
 def split_points(codes, exponents, centroids, counters):
@@ -53,22 +53,20 @@
     return [pl.BlockSpec(memory_space=pltpu.VMEM)] * n
 
 
-def points_kernel(codes, exponents, points):
-    rows, width = codes.shape
-    scale = jnp.exp2(-exponents[...].astype(jnp.float32))
-    scale = jnp.broadcast_to(scale, (128, rows)).T
-    for at in range(0, width, 128):
-        points[:, at : at + 128] = (codes[:, at : at + 128].astype(jnp.float32) * scale).astype(jnp.bfloat16)
-
-
-def points_call(codes, exponents):
+def join_kernel(above, below, *refs):
+    out, rows = refs[-1], above.shape[0]
+    out[:rows, :] = above[...]
+    out[rows:, :] = below[...]
+
+
+def join(above, below, *after):
     return pl.pallas_call(
-        points_kernel,
-        in_specs=in_vmem(2),
+        join_kernel,
+        in_specs=in_vmem(2 + len(after)),
         out_specs=in_vmem(1)[0],
-        out_shape=jax.ShapeDtypeStruct(codes.shape, jnp.bfloat16),
+        out_shape=jax.ShapeDtypeStruct((above.shape[0] + below.shape[0], above.shape[1]), above.dtype),
         compiler_params=pltpu.CompilerParams(vmem_limit_bytes=VMEM_BYTES),
-    )(codes, exponents[None])
+    )(above, below, *after)
 
 
 def expo_kernel(rate, block, place, near, first, second, cells, inverse, expo, tops, stats, points):
@@ -126,11 +124,11 @@
     )(place, *pieces, cells, inverse)
 
 
-def weighed_sums(first, count, expos, points, factor):
+def weighed_sums(at, count, expos, points, factor):
     total = weight = None
-    for at, (expo, chunk) in enumerate(zip(expos, points)):
-        scale = factor[at, first // count : first // count + 1, :]
-        share = (expo[first : first + count, :].astype(jnp.float32) * scale).astype(jnp.bfloat16)
+    here = pl.ds(pl.multiple_of(at * count, count), count)
+    for expo, chunk, scales in zip(expos, points, factor):
+        share = (expo[here, :].astype(jnp.float32) * scales[pl.ds(at, 1), :]).astype(jnp.bfloat16)
         part = jnp.dot(share, chunk[...], preferred_element_type=jnp.float32)
         wide = share.astype(jnp.float32)
         lanes = sum(wide[:, i : i + 128] for i in range(0, wide.shape[1], 128))
@@ -139,54 +137,70 @@
     return total, jnp.sum(weight.T, axis=0, keepdims=True)
 
 
-def sums_kernel(n, block, first, *refs):
-    expos, points, (factor, sums, mass) = refs[:n], refs[n : 2 * n], refs[2 * n :]
+def sums_kernel(n, block, skip, half, *refs):
+    expos, points, factor, (sums, mass) = refs[:n], refs[n : 2 * n], refs[2 * n], refs[2 * n + 1 :]
+    factor = [factor.at[at] for at in range(n)]
     for at in range(sums.shape[0] // block):
         here = slice(at * block, (at + 1) * block)
-        total, weight = weighed_sums((first + at) * block, block, expos, points, factor)
+        total, weight = weighed_sums(half[0] * 2 + skip + at, block, expos, points, factor)
         sums[here, :] = total.astype(sums.dtype)
         mass[:, here] = weight
 
 
-def last_kernel(n, block, first, *refs):
-    expos, points, (factor, early, early_mass, there, there_mass, sums, mass) = refs[:n], refs[n : 2 * n], refs[2 * n :]
-    done = early.shape[0]
-    sums[:done, :] = early[...] + there[:done, :].astype(jnp.float32)
-    mass[:, :done] = early_mass[...] + there_mass[:, :done]
-    for at in range(sums.shape[0] // block - done // block):
-        here = slice(done + at * block, done + (at + 1) * block)
-        total, weight = weighed_sums((first + at) * block, block, expos, points, factor)
-        sums[here, :] = total + there[here, :].astype(jnp.float32)
-        mass[:, here] = weight + there_mass[:, here]
-
-
-def sums_call(kernel, block, first, count, expos, points, factor, *more, rows, dtype):
+def last_kernel(n, block, skip, half, *refs):
+    expos, points, factor = refs[:n], refs[n : 2 * n], refs[2 * n]
+    early, early_mass, there, there_mass, sums, mass, out, left = refs[2 * n + 1 :]
+    factor = [factor.at[at] for at in range(n)]
+    copies = []
+
+    def store(start, stop, value):
+        out[start:stop, :] = value + there[start:stop, :].astype(jnp.float32)
+        here = pl.ds(start, stop - start)
+        copies.append(pltpu.make_async_copy(out.at[here, :], sums.at[here, :], left.at[len(copies)]))
+        copies[-1].start()
+
+    store(0, skip * block, early[...])
+    mass[:, : skip * block] = early_mass[...] + there_mass[:, : skip * block]
+    for at in range(skip, out.shape[0] // block):
+        start, stop = at * block, (at + 1) * block
+        total, weight = weighed_sums(half[0] * 2 + at, block, expos, points, factor)
+        store(start, stop, total)
+        mass[:, start:stop] = weight + there_mass[:, start:stop]
+    for copy in copies:
+        copy.wait()
+
+
+def sums_call(kernel, block, skip, rows, dtype, half, expos, points, factor, *more, last=False):
     n = len(expos)
     n_points, width = points[0].shape
+    work = rows // block - skip if last else rows // block
     return pl.pallas_call(
-        functools.partial(kernel, n, block, first),
-        in_specs=in_vmem(2 * n + 1 + len(more)),
-        out_specs=in_vmem(2),
+        functools.partial(kernel, n, block, skip),
+        in_specs=[pl.BlockSpec(memory_space=pltpu.SMEM)] + in_vmem(2 * n + 1 + len(more)),
+        out_specs=[pl.BlockSpec(memory_space=pltpu.HBM if last else pltpu.VMEM)] + in_vmem(1),
         out_shape=[jax.ShapeDtypeStruct((rows, width), dtype), jax.ShapeDtypeStruct((1, rows), jnp.float32)],
+        scratch_shapes=[pltpu.VMEM((rows, width), dtype), pltpu.SemaphoreType.DMA((1 + work,))] if last else [],
         compiler_params=pltpu.CompilerParams(vmem_limit_bytes=VMEM_BYTES),
         cost_estimate=pl.CostEstimate(
-            flops=2 * count * block * n * n_points * width,
-            bytes_accessed=2 * n * n_points * (count * block + width) + 4 * rows * width,
+            flops=2 * work * block * n * n_points * width,
+            bytes_accessed=2 * n * n_points * (work * block + width) + 4 * rows * width,
             transcendentals=0,
         ),
-    )(*expos, *points, factor, *more)
-
-
-def merge(rate, mine, theirs):
-    top = jnp.maximum(mine[0], theirs[0])
-    old, new = jnp.exp2((mine[0] - top) * rate), jnp.exp2((theirs[0] - top) * rate)
-    return jnp.stack([top, mine[1] * old + theirs[1] * new, mine[2] * old + theirs[2] * new])
+    )(half, *expos, *points, factor, *more)
+
+
+def merge(rate, stats):
+    top = functools.reduce(jnp.maximum, [s[0] for s in stats])
+    scales = [jnp.exp2((s[0] - top) * rate) for s in stats]
+    total = sum(s[1] * scale for s, scale in zip(stats, scales))
+    novel = sum(s[2] * scale for s, scale in zip(stats, scales))
+    return jnp.stack([top, total, novel])
 
 
 def split_cells(codes, exponents, centroids, counters):
     chip = lax.axis_index("y") * 2 + lax.axis_index("x")
     lo = lax.axis_index("lo")
-    own = points_call(codes, exponents)
+    own = to_points(codes, exponents)
     rate = 4.0 / math.sqrt(own.shape[1]) * math.log2(math.e)
     plane = ("y", "x", "lo")
 
@@ -198,39 +212,34 @@
     per_device = centroids.shape[0] // 8
     block = per_device // 2
 
-    def halves(a):
-        start = chip * 2 * per_device
-        other = lax.dynamic_slice_in_dim(a, start + (1 - lo) * per_device, per_device)
-        return jnp.concatenate([other, lax.dynamic_slice_in_dim(a, start + lo * per_device, per_device)])
-
-    cells = halves(centroids)
-    inverse = lax.rsqrt(halves(counters).astype(jnp.float32) + 1.0)
+    cells, counts = (lax.dynamic_slice_in_dim(a, chip * 2 * per_device, 2 * per_device) for a in (centroids, counters))
+    inverse = lax.rsqrt(counts.astype(jnp.float32) + 1.0)
     inverse = jnp.broadcast_to(inverse[:, None], (inverse.shape[0], 128))
 
+    nears = [own] + [along_z(own, by) for by in (1, 2, 3)]
+    firsts = [turn(near) for near in nears]
     expos, tops, stats, points = [], [], [], []
-    for step in range(4):
-        near = along_z(own, step) if step else own
-        first = turn(near)
-        second = turn_back(jnp.concatenate([near, first]))
+    for step, (near, first) in enumerate(zip(nears, firsts)):
+        second = turn_back(join(near, first, *stats[step - 2 : step - 1] if step > 1 else ()))
         expo, top, stat, chunk = expo_call(rate, block, place, (near, first, second), cells, inverse)
         expos.append(expo), tops.append(top), stats.append(stat), points.append(chunk)
 
     stat = jnp.stack(stats, axis=1)
-    for axis in ("x", "y"):
-        stat = merge(rate, stat, exchange(stat, (axis,), lambda at: at ^ 1))
-    for by in (1, 2):
+    stat = merge(rate, [stat] + [exchange(stat, ("y", "x"), lambda at: at ^ by) for by in (1, 2, 3)])
+    every = [stat]
+    for by in (1, 2, 3):
         theirs = along_z(stat, by)
-        theirs = jnp.stack([theirs[:, step ^ by] for step in range(4)], axis=1)
-        stat = merge(rate, stat, theirs)
+        every.append(jnp.stack([theirs[:, step ^ by] for step in range(4)], axis=1))
+    stat = merge(rate, every)
     factor = jnp.exp2((jnp.stack(tops) - stat[0][:, None]) * rate) * (stat[2] / stat[1] / stat[1])[:, None]
 
-    sums = functools.partial(sums_call, expos=expos, points=points, factor=factor)
-    there, there_mass = sums(sums_kernel, block, 0, 2, rows=per_device, dtype=jnp.bfloat16)
+    other, mine = ((a * jnp.ones((1,), jnp.int32)).astype(jnp.int32) for a in (1 - lo, lo))
+    parts = (expos, points, factor)
+    there, there_mass = sums_call(sums_kernel, block, 0, per_device, jnp.bfloat16, other, *parts)
     there, there_mass = (exchange(a, ("lo",), lambda at: at ^ 1) for a in (there, there_mass))
-    early, early_mass = sums(sums_kernel, block, 2, 1, rows=block, dtype=jnp.float32)
+    early, early_mass = sums_call(sums_kernel, block, 0, block, jnp.float32, mine, *parts)
     out, mass = sums_call(
-        last_kernel, block, 3, 1, expos, points, factor, early, early_mass, there, there_mass,
-        rows=per_device, dtype=jnp.float32,
+        last_kernel, block, 1, per_device, jnp.float32, mine, *parts, early, early_mass, there, there_mass, last=True
     )
     return (out[None], mass)
 

time: 62.8 us -> 76.6 us (1.22)
  local copies, waits for them, and re-layouts: 4.24 us -> 17.3 us
  waiting for transfers between devices: 18.9 us -> 11.8 us
  Pallas kernels: 14.7 us -> 18.6 us
  other arithmetic: 0.5 us -> 2.77 us
  starting transfers between devices: 23.3 us -> 24.6 us
    unnamed x4 -> x46, local copies, waits for them, and re-layouts: 1.6 us -> 15.5 us
    ppermute x17 -> x19, waiting for transfers between devices: 18.9 us -> 11.8 us  [exchange(): return lax.ppermute(a, axes, [(partner(at), at) for at in range(count)])]
    pallas_call x4 -> x7, Pallas kernels: 5.51 us -> 8.08 us  [the longest x3 5.87 us: sums_call(): pl.pallas_call(functools.partial(kernel, n, block, skip), in_specs=[pl.Bl...]
    pallas_call x4, Pallas kernels: 9.22 us -> 10.5 us  [expo_call(): pl.pallas_call(functools.partial(expo_kernel, rate, block), in_specs=[pl....]
    ppermute x17 -> x19, starting transfers between devices: 23.3 us -> 24.6 us  [exchange(): return lax.ppermute(a, axes, [(partner(at), at) for at in range(count)])]
    convert_element_type x0 -> x1, other arithmetic: none -> 1.03 us  [to_points(): return (codes.astype(jnp.float32) * scale[:, None]).astype(jnp.bfloat16)]
    dynamic_slice x2 -> x1, local copies, waits for them, and re-layouts: 2.33 us -> 1.51 us  [split_cells(): lax.dynamic_slice_in_dim(a, chip * 2 * per_device, 2 * per_device)]
    rsqrt x1, other arithmetic: 0.01 us -> 0.78 us  [split_cells(): inverse = lax.rsqrt(counts.astype(jnp.float32) + 1.0)]
  transfers between devices with their start and end apart: 17 -> 19, of which waited for: 8 -> 10; matrix products, arithmetic and copies ran while one was open for 5% -> 4% of each run, Pallas kernels for 13% -> 15%
where the time goes in v4:
time: 76.6 us; the launch traced here: 76 us
  starting transfers between devices  24.6 us (32%)
  Pallas kernels  18.6 us (24%)
  local copies, waits for them, and re-layouts  17.3 us (23%)
  waiting for transfers between devices  11.8 us (15%)
  other arithmetic  2.77 us (4%)
  between operations  0.89 us (1%)
    ppermute x19, starting transfers between devices, exchange(): return lax.ppermute(a, axes, [(partner(at), at) for at in range(count)])  24.6 us
    unnamed x46, local copies, waits for them, and re-layouts  15.5 us
    ppermute x19, waiting for transfers between devices, exchange(): return lax.ppermute(a, axes, [(partner(at), at) for at in range(count)])  11.8 us
    pallas_call x4, Pallas kernels, expo_call(): pl.pallas_call(functools.partial(expo_kernel, rate, block), in_specs=[pl....  10.5 us
    pallas_call x3, Pallas kernels, sums_call(): pl.pallas_call(functools.partial(kernel, n, block, skip), in_specs=[pl.Bl...  5.87 us
    pallas_call x4, Pallas kernels, join(): pl.pallas_call(join_kernel, in_specs=in_vmem(2 + len(after)), out_specs=i...  2.21 us
  transfers between devices with their start and end apart: 19, of which 10 were waited for; matrix products, arithmetic and copies ran while one was open for 4% of the time, Pallas kernels for 15%

profile of v4, /device:TPU:0, one launch (start us, length us, event | category | flops | bytes accessed | tf_op | source)
XLA Modules:
  0.0 76.0 jit_solution(14342819551852965309)
XLA Ops:
  0.6 0.7 convert_multiply_fusion
  1.3 1.0 %multiply_convert_fusion.above.near = bf16[128,512]{1,0:T(8,128)(2,1)S(1)} fusion(s32[128,512]{1,0:T(8,128)} %param.4, f32[128]{0:T(128)S(1)} %convert_multiply_fusion), kind=kLoop, calls=%fused_computation | loop fusion | flops 196608 | bytes 393728 | tf_op jit(solution)/shard_map/convert_element_type | solution.py:17
  2.3 3.0 %collective-permute-start = (bf16[128,512]{1,0:T(8,128)(2,1)S(1)}, bf16[128,512]{1,0:T(8,128)(2,1)S(1)}, u32[]{:S(2)}, u32[]{:S(2)}) collective-permute-start(bf16[128,512]{1,0:T(8,128)(2,1)S(1)} %multiply_convert_fusion.above.near), channel_id=1, source_target_pairs={{8,0},{20,4},{0,8},{28,12},{24,16},{4,20},{16,24},{12,28},{9,1},{2... | collective-permute-start | bytes 393224 | tf_op jit(solution)/shard_map/ppermute | solution.py:49
  5.3 1.6 %collective-permute-start.2 = (bf16[128,512]{1,0:T(8,128)(2,1)S(1)}, bf16[128,512]{1,0:T(8,128)(2,1)S(1)}, u32[]{:S(2)}, u32[]{:S(2)}) collective-permute-start(bf16[128,512]{1,0:T(8,128)(2,1)S(1)} %multiply_convert_fusion.above.near), channel_id=1, source_target_pairs={{1,0},{0,1},{3,2},{2,3},{5,4},{4,5},{7,6},{6,7},{9,8},{8,9},{11,10... | collective-permute-start | bytes 393224 | tf_op jit(solution)/shard_map/ppermute | solution.py:49
  6.9 2.5 %collective-permute-start.8 = (bf16[128,512]{1,0:T(8,128)(2,1)S(1)}, bf16[128,512]{1,0:T(8,128)(2,1)}, u32[]{:S(2)}, u32[]{:S(2)}) collective-permute-start(bf16[128,512]{1,0:T(8,128)(2,1)S(1)} %multiply_convert_fusion.above.near), channel_id=1, source_target_pairs={{3,0},{2,1},{1,2},{0,3},{7,4},{6,5},{5,6},{4,7},{11,8},{10,9},{9,1... | collective-permute-start | bytes 393224 | tf_op jit(solution)/shard_map/ppermute | solution.py:49
  9.4 0.1 collective-permute-start.5
  9.5 1.6 %collective-permute-start.1 = (bf16[256,512]{1,0:T(8,128)(2,1)S(1)}, bf16[256,512]{1,0:T(8,128)(2,1)S(1)}, u32[]{:S(2)}, u32[]{:S(2)}) collective-permute-start(bf16[256,512]{1,0:T(8,128)(2,1)S(1)} %shard_map.59), channel_id=1, source_target_pairs={{16,0},{12,4},{24,8},{4,12},{0,16},{28,20},{8,24},{20,28},{17,1},{... | collective-permute-start | bytes 786440 | tf_op jit(solution)/shard_map/ppermute | solution.py:49
  11.1 0.8 %collective-permute-start.3 = (bf16[128,512]{1,0:T(8,128)(2,1)S(1)}, bf16[128,512]{1,0:T(8,128)(2,1)S(1)}, u32[]{:S(2)}, u32[]{:S(2)}) collective-permute-start(bf16[128,512]{1,0:T(8,128)(2,1)S(1)} %collective-permute-done.2.above.near), channel_id=1, source_target_pairs={{8,0},{20,4},{0,8},{28,12},{24,16},{4,20},{16,24},{12,28},{9,1},{2... | collective-permute-start | bytes 393224 | tf_op jit(solution)/shard_map/ppermute | solution.py:49
  11.9 1.5 %constant_dynamic-slice_fusion.cells = bf16[1536,512]{1,0:T(8,128)(2,1)S(1)} fusion(bf16[6144,512]{1,0:T(8,128)(2,1)} %param.6, s32[]{:T(128)S(6)} %select_n.4), kind=kLoop, calls=%fused_computation.83 | loop fusion | bytes 3145732 | tf_op jit(solution)/shard_map/dynamic_slice | solution.py:215
  13.4 0.0 copy-start.12
  13.5 2.6 %collective-permute-done.3.below.first = bf16[128,512]{1,0:T(8,128)(2,1)S(1)} collective-permute-done((bf16[128,512]{1,0:T(8,128)(2,1)S(1)}, bf16[128,512]{1,0:T(8,128)(2,1)S(1)}, u32[]{:S(2)}, u32[]{:S(2)}) %collective-permute-start.3) | collective-permute-done | bytes 131104 | tf_op jit(solution)/shard_map/ppermute | solution.py:49
  16.1 0.6 copy-done.19
  16.8 2.3 %collective-permute-start.4 = (bf16[256,512]{1,0:T(8,128)(2,1)S(1)}, bf16[256,512]{1,0:T(8,128)(2,1)}, u32[]{:S(2)}, u32[]{:S(2)}) collective-permute-start(bf16[256,512]{1,0:T(8,128)(2,1)S(1)} %shard_map.61), channel_id=1, source_target_pairs={{16,0},{12,4},{24,8},{4,12},{0,16},{28,20},{8,24},{20,28},{17,1},{... | collective-permute-start | bytes 786440 | tf_op jit(solution)/shard_map/ppermute | solution.py:49
  19.1 0.8 %add_rsqrt_fusion = f32[1536]{0:T(1024)S(1)} fusion(s32[6144]{0:T(1024)} %param.7, s32[]{:T(128)S(6)} %select_n.4), kind=kLoop, calls=%fused_computation.80 | loop fusion | flops 3072 | bytes 12292 | tf_op jit(solution)/shard_map/rsqrt | solution.py:216
  19.9 1.1 %collective-permute-done.5.above.near = bf16[128,512]{1,0:T(8,128)(2,1)} collective-permute-done((bf16[128,512]{1,0:T(8,128)(2,1)S(1)}, bf16[128,512]{1,0:T(8,128)(2,1)}, u32[]{:S(2)}, u32[]{:S(2)}) %collective-permute-start.5) | collective-permute-done | bytes 131104 | tf_op jit(solution)/shard_map/ppermute | solution.py:49
  21.0 1.5 %collective-permute-start.6 = (bf16[128,512]{1,0:T(8,128)(2,1)}, bf16[128,512]{1,0:T(8,128)(2,1)S(1)}, u32[]{:S(2)}, u32[]{:S(2)}) collective-permute-start(bf16[128,512]{1,0:T(8,128)(2,1)} %collective-permute-done.5.above.near), channel_id=1, source_target_pairs={{8,0},{20,4},{0,8},{28,12},{24,16},{4,20},{16,24},{12,28},{9,1},{2... | collective-permute-start | bytes 393224 | tf_op jit(solution)/shard_map/ppermute | solution.py:49
  22.5 0.1 pad_add_fusion.place
  22.6 0.5 collective-permute-start.9
  23.1 0.7 copy-done.21
  23.8 0.3 broadcast_in_dim.7.inverse
  24.1 0.9 %copy-done.18 = bf16[128,512]{1,0:T(8,128)(2,1)S(1)} copy-done((bf16[128,512]{1,0:T(8,128)(2,1)S(1)}, bf16[128,512]{1,0:T(8,128)(2,1)}, u32[]{:S(2)}) %copy-start.18) | copy-done | bytes 131096
  25.0 0.9 %copy-done.22 = bf16[256,512]{1,0:T(8,128)(2,1)S(1)} copy-done((bf16[256,512]{1,0:T(8,128)(2,1)S(1)}, bf16[256,512]{1,0:T(8,128)(2,1)}, u32[]{:S(2)}) %copy-start.22) | copy-done | bytes 262168
  26.0 2.3 %shard_map.60 = (bf16[1536,512]{1,0:T(8,128)(2,1)S(1)}, f32[4,512]{1,0:T(4,128)S(1)}, f32[3,512]{1,0:T(4,128)S(1)}, bf16[512,512]{1,0:T(8,128)(2,1)S(1)}) custom-call(s32[4]{0:T(128)S(1)} %pad_add_fusion.place, bf16[128,512]{1,0:T(8,128)(2,1)S(1)} %multiply_convert_fusion.above.near, bf16[128,512]{1,0:T(8,128)(2,1)S(1)} %copy-done.18, ...), custom_call_target="tpu_custom_call" | custom-call | flops 805306368 | bytes 3670016 | tf_op jit(solution)/shard_map/pallas_call | solution.py:108
  28.3 1.1 %shard_map.63 = bf16[256,512]{1,0:T(8,128)(2,1)S(1)} custom-call(bf16[128,512]{1,0:T(8,128)(2,1)} %collective-permute-done.5.above.near, bf16[128,512]{1,0:T(8,128)(2,1)S(1)} %collective-permute-done.6.below.first, f32[3,512]{1,0:T(4,128)S(1)} %get-tuple-element.26.refs_0_), custom_call_target="tpu_custom_call" | custom-call | tf_op jit(solution)/shard_map/pallas_call | solution.py:63
  29.4 0.6 collective-permute-start.7
  30.0 0.0 copy-start.13
  30.0 1.4 %copy-done.13 = bf16[1536,512]{1,0:T(8,128)(2,1)S(1)} copy-done((bf16[1536,512]{1,0:T(8,128)(2,1)S(1)}, bf16[1536,512]{1,0:T(8,128)(2,1)}, u32[]{:S(2)}) %copy-start.13) | copy-done | bytes 1572888
  31.4 2.9 %shard_map.62 = (bf16[1536,512]{1,0:T(8,128)(2,1)S(1)}, f32[4,512]{1,0:T(4,128)S(1)}, f32[3,512]{1,0:T(4,128)S(1)}, bf16[512,512]{1,0:T(8,128)(2,1)S(1)}) custom-call(s32[4]{0:T(128)S(1)} %pad_add_fusion.place, bf16[128,512]{1,0:T(8,128)(2,1)S(1)} %copy-done.16, bf16[128,512]{1,0:T(8,128)(2,1)S(1)} %copy-done.20, ...), custom_call_target="tpu_custom_call" | custom-call | flops 805306368 | bytes 3670016 | tf_op jit(solution)/shard_map/pallas_call | solution.py:108
  34.3 1.1 %shard_map.65 = bf16[256,512]{1,0:T(8,128)(2,1)S(1)} custom-call(bf16[128,512]{1,0:T(8,128)(2,1)} %collective-permute-done.8.above.near, bf16[128,512]{1,0:T(8,128)(2,1)S(1)} %collective-permute-done.9.below.first, f32[3,512]{1,0:T(4,128)S(1)} %get-tuple-element.28.refs_0_), custom_call_target="tpu_custom_call" | custom-call | tf_op jit(solution)/shard_map/pallas_call | solution.py:63
  35.3 1.6 %collective-permute-start.10 = (bf16[256,512]{1,0:T(8,128)(2,1)S(1)}, bf16[256,512]{1,0:T(8,128)(2,1)S(1)}, u32[]{:S(2)}, u32[]{:S(2)}) collective-permute-start(bf16[256,512]{1,0:T(8,128)(2,1)S(1)} %shard_map.65), channel_id=1, source_target_pairs={{16,0},{12,4},{24,8},{4,12},{0,16},{28,20},{8,24},{20,28},{17,1},{... | collective-permute-start | bytes 786440 | tf_op jit(solution)/shard_map/ppermute | solution.py:49
  36.9 2.7 %shard_map.64 = (bf16[1536,512]{1,0:T(8,128)(2,1)S(1)}, f32[4,512]{1,0:T(4,128)S(1)}, f32[3,512]{1,0:T(4,128)S(1)}, bf16[512,512]{1,0:T(8,128)(2,1)S(1)}) custom-call(s32[4]{0:T(128)S(1)} %pad_add_fusion.place, bf16[128,512]{1,0:T(8,128)(2,1)} %collective-permute-done.5.above.near, bf16[128,512]{1,0:T(8,128)(2,1)S(1)} %collective-permute-done.6.below.first, ...), custom_call_target="tpu_custom_call" | custom-call | flops 805306368 | bytes 3670016 | tf_op jit(solution)/shard_map/pallas_call | solution.py:108
  39.6 0.0 copy-start
  39.6 1.1 %copy-done = bf16[1536,512]{1,0:T(8,128)(2,1)} copy-done((bf16[1536,512]{1,0:T(8,128)(2,1)}, bf16[1536,512]{1,0:T(8,128)(2,1)S(1)}, u32[]{:S(2)}) %copy-start) | copy-done | bytes 1572888
  40.8 0.8 %copy-done.8 = bf16[512,512]{1,0:T(8,128)(2,1)} copy-done((bf16[512,512]{1,0:T(8,128)(2,1)}, bf16[512,512]{1,0:T(8,128)(2,1)S(1)}, u32[]{:S(2)}) %copy-start.8) | copy-done | bytes 524312
  41.6 0.2 collective-permute-done.10.second
  41.8 2.7 %shard_map.66 = (bf16[1536,512]{1,0:T(8,128)(2,1)S(1)}, f32[4,512]{1,0:T(4,128)S(1)}, f32[3,512]{1,0:T(4,128)S(1)}, bf16[512,512]{1,0:T(8,128)(2,1)S(1)}) custom-call(s32[4]{0:T(128)S(1)} %pad_add_fusion.place, bf16[128,512]{1,0:T(8,128)(2,1)} %collective-permute-done.8.above.near, bf16[128,512]{1,0:T(8,128)(2,1)S(1)} %collective-permute-done.9.below.first, ...), custom_call_target="tpu_custom_call" | custom-call | flops 805306368 | bytes 3670016 | tf_op jit(solution)/shard_map/pallas_call | solution.py:108
  44.5 1.2 %copy-done.2 = bf16[1536,512]{1,0:T(8,128)(2,1)} copy-done((bf16[1536,512]{1,0:T(8,128)(2,1)}, bf16[1536,512]{1,0:T(8,128)(2,1)S(1)}, u32[]{:S(2)}) %copy-start.2) | copy-done | bytes 1572888
  45.6 0.8 %copy-done.10 = bf16[512,512]{1,0:T(8,128)(2,1)} copy-done((bf16[512,512]{1,0:T(8,128)(2,1)}, bf16[512,512]{1,0:T(8,128)(2,1)S(1)}, u32[]{:S(2)}) %copy-start.10) | copy-done | bytes 524312
  46.5 2.5 %collective-permute-start.13 = (f32[3,4,512]{2,1,0:T(4,128)S(1)}, f32[3,4,512]{2,1,0:T(4,128)S(1)}, u32[]{:S(2)}, u32[]{:S(2)}) collective-permute-start(f32[3,4,512]{2,1,0:T(4,128)S(1)} %copy.6), channel_id=1, source_target_pairs={{24,0},{16,8},{8,16},{0,24},{25,1},{17,9},{9,17},{1,25},{26,2},{18... | collective-permute-start | bytes 73736 | tf_op jit(solution)/shard_map/ppermute | solution.py:49
  49.0 0.5 collective-permute-start.12
  49.5 0.5 collective-permute-start.11
  50.0 1.2 %collective-permute-done.13 = f32[3,4,512]{2,1,0:T(4,128)S(1)} collective-permute-done((f32[3,4,512]{2,1,0:T(4,128)S(1)}, f32[3,4,512]{2,1,0:T(4,128)S(1)}, u32[]{:S(2)}, u32[]{:S(2)}) %collective-permute-start.13) | collective-permute-done | bytes 24608 | tf_op jit(solution)/shard_map/ppermute | solution.py:49
  51.2 1.6 %collective-permute-done.12 = f32[3,4,512]{2,1,0:T(4,128)S(1)} collective-permute-done((f32[3,4,512]{2,1,0:T(4,128)S(1)}, f32[3,4,512]{2,1,0:T(4,128)S(1)}, u32[]{:S(2)}, u32[]{:S(2)}) %collective-permute-start.12) | collective-permute-done | bytes 24608 | tf_op jit(solution)/shard_map/ppermute | solution.py:49
  52.8 0.5 collective-permute-done.11
  53.4 3.6 %collective-permute-start.16 = (f32[3,4,512]{2,1,0:T(4,128)S(1)}, f32[3,4,512]{2,1,0:T(4,128)S(1)}, u32[]{:S(2)}, u32[]{:S(2)}) collective-permute-start(f32[3,4,512]{2,1,0:T(4,128)S(1)} %pad_maximum_fusion.1), channel_id=1, source_target_pairs={{3,0},{2,1},{1,2},{0,3},{7,4},{6,5},{5,6},{4,7},{11,8},{10,9},{9,1... | collective-permute-start | bytes 73736 | tf_op jit(solution)/shard_map/ppermute | solution.py:49
  57.0 0.9 %collective-permute-start.14 = (f32[3,4,512]{2,1,0:T(4,128)S(1)}, f32[3,4,512]{2,1,0:T(4,128)S(1)}, u32[]{:S(2)}, u32[]{:S(2)}) collective-permute-start(f32[3,4,512]{2,1,0:T(4,128)S(1)} %pad_maximum_fusion.1), channel_id=1, source_target_pairs={{1,0},{0,1},{3,2},{2,3},{5,4},{4,5},{7,6},{6,7},{9,8},{8,9},{11,10... | collective-permute-start | bytes 73736 | tf_op jit(solution)/shard_map/ppermute | solution.py:49
  57.9 1.2 %collective-permute-done.16 = f32[3,4,512]{2,1,0:T(4,128)S(1)} collective-permute-done((f32[3,4,512]{2,1,0:T(4,128)S(1)}, f32[3,4,512]{2,1,0:T(4,128)S(1)}, u32[]{:S(2)}, u32[]{:S(2)}) %collective-permute-start.16) | collective-permute-done | bytes 24608 | tf_op jit(solution)/shard_map/ppermute | solution.py:49
  59.1 1.7 %collective-permute-done.14 = f32[3,4,512]{2,1,0:T(4,128)S(1)} collective-permute-done((f32[3,4,512]{2,1,0:T(4,128)S(1)}, f32[3,4,512]{2,1,0:T(4,128)S(1)}, u32[]{:S(2)}, u32[]{:S(2)}) %collective-permute-start.14) | collective-permute-done | bytes 24608 | tf_op jit(solution)/shard_map/ppermute | solution.py:49
  60.8 0.1 pad_maximum_fusion.2
  60.9 0.8 %collective-permute-done.15 = f32[3,4,512]{2,1,0:T(4,128)S(1)} collective-permute-done((f32[3,4,512]{2,1,0:T(4,128)S(1)}, f32[3,4,512]{2,1,0:T(4,128)S(1)}, u32[]{:S(2)}, u32[]{:S(2)}) %collective-permute-start.15) | collective-permute-done | bytes 24608 | tf_op jit(solution)/shard_map/ppermute | solution.py:49
  61.7 0.1 fusion.8
  61.8 0.0 copy-start.1
  61.8 1.4 %copy-done.1 = bf16[1536,512]{1,0:T(8,128)(2,1)S(1)} copy-done((bf16[1536,512]{1,0:T(8,128)(2,1)S(1)}, bf16[1536,512]{1,0:T(8,128)(2,1)}, u32[]{:S(2)}) %copy-start.1) | copy-done | bytes 1572888
  63.2 1.4 %copy-done.3 = bf16[1536,512]{1,0:T(8,128)(2,1)S(1)} copy-done((bf16[1536,512]{1,0:T(8,128)(2,1)S(1)}, bf16[1536,512]{1,0:T(8,128)(2,1)}, u32[]{:S(2)}) %copy-start.3) | copy-done | bytes 1572888
  64.6 1.0 %copy-done.5 = bf16[512,512]{1,0:T(8,128)(2,1)S(1)} copy-done((bf16[512,512]{1,0:T(8,128)(2,1)S(1)}, bf16[512,512]{1,0:T(8,128)(2,1)}, u32[]{:S(2)}) %copy-start.5) | copy-done | bytes 524312
  65.7 1.0 %copy-done.7 = bf16[512,512]{1,0:T(8,128)(2,1)S(1)} copy-done((bf16[512,512]{1,0:T(8,128)(2,1)S(1)}, bf16[512,512]{1,0:T(8,128)(2,1)}, u32[]{:S(2)}) %copy-start.7) | copy-done | bytes 524312
  66.7 1.0 %copy-done.9 = bf16[512,512]{1,0:T(8,128)(2,1)S(1)} copy-done((bf16[512,512]{1,0:T(8,128)(2,1)S(1)}, bf16[512,512]{1,0:T(8,128)(2,1)}, u32[]{:S(2)}) %copy-start.9) | copy-done | bytes 524312
  67.8 1.0 %copy-done.11 = bf16[512,512]{1,0:T(8,128)(2,1)S(1)} copy-done((bf16[512,512]{1,0:T(8,128)(2,1)S(1)}, bf16[512,512]{1,0:T(8,128)(2,1)}, u32[]{:S(2)}) %copy-start.11) | copy-done | bytes 524312
  68.8 2.0 %shard_map.68 = (bf16[768,512]{1,0:T(8,128)(2,1)S(1)}, f32[1,768]{1,0:T(1,128)S(1)}) custom-call(s32[1]{0:T(128)} %bitcast.33.half, bf16[1536,512]{1,0:T(8,128)(2,1)S(1)} %get-tuple-element.24.refs_0_, bf16[1536,512]{1,0:T(8,128)(2,1)S(1)} %get-tuple-element.25.refs_1_, bf16[1536,512]{1,0:T(8,128)(2,1)S(1)} %copy-done.1, bf16[1536,512]{1,0:T(8,128)(2,1)S(1)} %copy-done.3, ...), custom_call_target="tpu_custom_call" | custom-call | flops 1610612736 | bytes 6815744 | tf_op jit(solution)/shard_map/pallas_call | solution.py:177
  70.8 0.1 collective-permute-start.17
  70.9 0.5 collective-permute-start.18
  71.4 1.0 %shard_map.67 = (f32[384,512]{1,0:T(8,128)S(1)}, f32[1,384]{1,0:T(1,128)S(1)}) custom-call(s32[1]{0:T(128)} %bitcast.half, bf16[1536,512]{1,0:T(8,128)(2,1)S(1)} %get-tuple-element.24.refs_0_, bf16[1536,512]{1,0:T(8,128)(2,1)S(1)} %get-tuple-element.25.refs_1_, bf16[1536,512]{1,0:T(8,128)(2,1)S(1)} %copy-done.1, bf16[1536,512]{1,0:T(8,128)(2,1)S(1)} %copy-done.3, ...), custom_call_target="tpu_custom_call" | custom-call | flops 805306368 | bytes 4456448 | tf_op jit(solution)/shard_map/pallas_call | solution.py:177
  72.4 0.7 collective-permute-done.18.refs_12_
  73.2 2.8 %shard_map.69 = (f32[768,512]{1,0:T(8,128)}, f32[1,768]{1,0:T(1,128)}) custom-call(s32[1]{0:T(128)} %bitcast.half, bf16[1536,512]{1,0:T(8,128)(2,1)S(1)} %get-tuple-element.24.refs_0_, bf16[1536,512]{1,0:T(8,128)(2,1)S(1)} %get-tuple-element.25.refs_1_, bf16[1536,512]{1,0:T(8,128)(2,1)S(1)} %copy-done.1, bf16[1536,512]{1,0:T(8,128)(2,1)S(1)} %copy-done.3, ...), custom_call_target="tpu_custom_call" | custom-call | flops 805306368 | bytes 5242880 | tf_op jit(solution)/shard_map/pallas_call | solution.py:177
  (49 shorter events, 0.3 us)
Async XLA Ops:
  2.3 7.2 %collective-permute-start = (bf16[128,512]{1,0:T(8,128)(2,1)S(1)}, bf16[128,512]{1,0:T(8,128)(2,1)S(1)}, u32[]{:S(2)}, u32[]{:S(2)}) collective-permute-start(bf16[128,512]{1,0:T(8,128)(2,1)S(1)} %multiply_convert_fusion.above.near), channel_id=1, source_target_pairs={{8,0},{20,4},{0,8},{28,12},{24,16},{4,20},{16,24},{12,28},{9,1},{2... | collective-permute-start | bytes 393224 | tf_op jit(solution)/shard_map/ppermute | solution.py:49
  5.3 5.8 %collective-permute-start.2 = (bf16[128,512]{1,0:T(8,128)(2,1)S(1)}, bf16[128,512]{1,0:T(8,128)(2,1)S(1)}, u32[]{:S(2)}, u32[]{:S(2)}) collective-permute-start(bf16[128,512]{1,0:T(8,128)(2,1)S(1)} %multiply_convert_fusion.above.near), channel_id=1, source_target_pairs={{1,0},{0,1},{3,2},{2,3},{5,4},{4,5},{7,6},{6,7},{9,8},{8,9},{11,10... | collective-permute-start | bytes 393224 | tf_op jit(solution)/shard_map/ppermute | solution.py:49
  6.9 15.7 %collective-permute-start.8 = (bf16[128,512]{1,0:T(8,128)(2,1)S(1)}, bf16[128,512]{1,0:T(8,128)(2,1)}, u32[]{:S(2)}, u32[]{:S(2)}) collective-permute-start(bf16[128,512]{1,0:T(8,128)(2,1)S(1)} %multiply_convert_fusion.above.near), channel_id=1, source_target_pairs={{3,0},{2,1},{1,2},{0,3},{7,4},{6,5},{5,6},{4,7},{11,8},{10,9},{9,1... | collective-permute-start | bytes 393224 | tf_op jit(solution)/shard_map/ppermute | solution.py:49
  9.4 11.6 %collective-permute-start.5 = (bf16[128,512]{1,0:T(8,128)(2,1)S(1)}, bf16[128,512]{1,0:T(8,128)(2,1)}, u32[]{:S(2)}, u32[]{:S(2)}) collective-permute-start(bf16[128,512]{1,0:T(8,128)(2,1)S(1)} %multiply_convert_fusion.above.near), channel_id=1, source_target_pairs={{2,0},{3,1},{0,2},{1,3},{6,4},{7,5},{4,6},{5,7},{10,8},{11,9},{8,1... | collective-permute-start | bytes 393224 | tf_op jit(solution)/shard_map/ppermute | solution.py:49
  9.5 3.9 %copy-start.17 = (bf16[128,512]{1,0:T(8,128)(2,1)}, bf16[128,512]{1,0:T(8,128)(2,1)S(1)}, u32[]{:S(2)}) copy-start(bf16[128,512]{1,0:T(8,128)(2,1)S(1)} %collective-permute-done.below.first) | copy-start | bytes 393220
  9.5 13.6 %collective-permute-start.1 = (bf16[256,512]{1,0:T(8,128)(2,1)S(1)}, bf16[256,512]{1,0:T(8,128)(2,1)S(1)}, u32[]{:S(2)}, u32[]{:S(2)}) collective-permute-start(bf16[256,512]{1,0:T(8,128)(2,1)S(1)} %shard_map.59), channel_id=1, source_target_pairs={{16,0},{12,4},{24,8},{4,12},{0,16},{28,20},{8,24},{20,28},{17,1},{... | collective-permute-start | bytes 786440 | tf_op jit(solution)/shard_map/ppermute | solution.py:49
  11.1 5.0 %copy-start.15 = (bf16[128,512]{1,0:T(8,128)(2,1)}, bf16[128,512]{1,0:T(8,128)(2,1)S(1)}, u32[]{:S(2)}) copy-start(bf16[128,512]{1,0:T(8,128)(2,1)S(1)} %collective-permute-done.2.above.near) | copy-start | bytes 393220
  11.1 5.0 %collective-permute-start.3 = (bf16[128,512]{1,0:T(8,128)(2,1)S(1)}, bf16[128,512]{1,0:T(8,128)(2,1)S(1)}, u32[]{:S(2)}, u32[]{:S(2)}) collective-permute-start(bf16[128,512]{1,0:T(8,128)(2,1)S(1)} %collective-permute-done.2.above.near), channel_id=1, source_target_pairs={{8,0},{20,4},{0,8},{28,12},{24,16},{4,20},{16,24},{12,28},{9,1},{2... | collective-permute-start | bytes 393224 | tf_op jit(solution)/shard_map/ppermute | solution.py:49
  13.4 14.8 %copy-start.12 = (bf16[1536,512]{1,0:T(8,128)(2,1)}, bf16[1536,512]{1,0:T(8,128)(2,1)S(1)}, u32[]{:S(2)}) copy-start(bf16[1536,512]{1,0:T(8,128)(2,1)S(1)} %constant_dynamic-slice_fusion.cells) | copy-start | bytes 4718596
  16.1 0.6 copy-start.19
  16.8 13.2 %collective-permute-start.4 = (bf16[256,512]{1,0:T(8,128)(2,1)S(1)}, bf16[256,512]{1,0:T(8,128)(2,1)}, u32[]{:S(2)}, u32[]{:S(2)}) collective-permute-start(bf16[256,512]{1,0:T(8,128)(2,1)S(1)} %shard_map.61), channel_id=1, source_target_pairs={{16,0},{12,4},{24,8},{4,12},{0,16},{28,20},{8,24},{20,28},{17,1},{... | collective-permute-start | bytes 786440 | tf_op jit(solution)/shard_map/ppermute | solution.py:49
  21.0 7.3 %collective-permute-start.6 = (bf16[128,512]{1,0:T(8,128)(2,1)}, bf16[128,512]{1,0:T(8,128)(2,1)S(1)}, u32[]{:S(2)}, u32[]{:S(2)}) collective-permute-start(bf16[128,512]{1,0:T(8,128)(2,1)} %collective-permute-done.5.above.near), channel_id=1, source_target_pairs={{8,0},{20,4},{0,8},{28,12},{24,16},{4,20},{16,24},{12,28},{9,1},{2... | collective-permute-start | bytes 393224 | tf_op jit(solution)/shard_map/ppermute | solution.py:49
  22.6 11.7 %collective-permute-start.9 = (bf16[128,512]{1,0:T(8,128)(2,1)}, bf16[128,512]{1,0:T(8,128)(2,1)S(1)}, u32[]{:S(2)}, u32[]{:S(2)}) collective-permute-start(bf16[128,512]{1,0:T(8,128)(2,1)} %collective-permute-done.8.above.near), channel_id=1, source_target_pairs={{8,0},{20,4},{0,8},{28,12},{24,16},{4,20},{16,24},{12,28},{9,1},{2... | collective-permute-start | bytes 393224 | tf_op jit(solution)/shard_map/ppermute | solution.py:49
  23.1 0.7 copy-start.21
  24.1 0.9 %copy-start.18 = (bf16[128,512]{1,0:T(8,128)(2,1)S(1)}, bf16[128,512]{1,0:T(8,128)(2,1)}, u32[]{:S(2)}) copy-start(bf16[128,512]{1,0:T(8,128)(2,1)} %copy-done.17) | copy-start | bytes 393220
  25.0 0.9 %copy-start.22 = (bf16[256,512]{1,0:T(8,128)(2,1)S(1)}, bf16[256,512]{1,0:T(8,128)(2,1)}, u32[]{:S(2)}) copy-start(bf16[256,512]{1,0:T(8,128)(2,1)} %copy-done.21) | copy-start | bytes 786436
  25.9 4.0 %copy-start.16 = (bf16[128,512]{1,0:T(8,128)(2,1)S(1)}, bf16[128,512]{1,0:T(8,128)(2,1)}, u32[]{:S(2)}) copy-start(bf16[128,512]{1,0:T(8,128)(2,1)} %copy-done.15) | copy-start | bytes 393220
  25.9 4.0 %copy-start.20 = (bf16[128,512]{1,0:T(8,128)(2,1)S(1)}, bf16[128,512]{1,0:T(8,128)(2,1)}, u32[]{:S(2)}) copy-start(bf16[128,512]{1,0:T(8,128)(2,1)} %copy-done.19) | copy-start | bytes 393220
  28.3 6.0 %copy-start.4 = (bf16[512,512]{1,0:T(8,128)(2,1)}, bf16[512,512]{1,0:T(8,128)(2,1)S(1)}, u32[]{:S(2)}) copy-start(bf16[512,512]{1,0:T(8,128)(2,1)S(1)} %get-tuple-element.30.refs_4_) | copy-start | bytes 1572868
  29.4 7.5 %collective-permute-start.7 = (bf16[256,512]{1,0:T(8,128)(2,1)S(1)}, bf16[256,512]{1,0:T(8,128)(2,1)S(1)}, u32[]{:S(2)}, u32[]{:S(2)}) collective-permute-start(bf16[256,512]{1,0:T(8,128)(2,1)S(1)} %shard_map.63), channel_id=1, source_target_pairs={{16,0},{12,4},{24,8},{4,12},{0,16},{28,20},{8,24},{20,28},{17,1},{... | collective-permute-start | bytes 786440 | tf_op jit(solution)/shard_map/ppermute | solution.py:49
  30.0 1.4 %copy-start.13 = (bf16[1536,512]{1,0:T(8,128)(2,1)S(1)}, bf16[1536,512]{1,0:T(8,128)(2,1)}, u32[]{:S(2)}) copy-start(bf16[1536,512]{1,0:T(8,128)(2,1)} %copy-done.12) | copy-start | bytes 4718596
  31.4 5.6 %copy-start.14 = (bf16[1536,512]{1,0:T(8,128)(2,1)S(1)}, bf16[1536,512]{1,0:T(8,128)(2,1)}, u32[]{:S(2)}) copy-start(bf16[1536,512]{1,0:T(8,128)(2,1)} %copy-done.12) | copy-start | bytes 4718596
  34.2 2.7 %copy-start.6 = (bf16[512,512]{1,0:T(8,128)(2,1)}, bf16[512,512]{1,0:T(8,128)(2,1)S(1)}, u32[]{:S(2)}) copy-start(bf16[512,512]{1,0:T(8,128)(2,1)S(1)} %get-tuple-element.31.refs_5_) | copy-start | bytes 1572868
  35.3 6.4 %collective-permute-start.10 = (bf16[256,512]{1,0:T(8,128)(2,1)S(1)}, bf16[256,512]{1,0:T(8,128)(2,1)S(1)}, u32[]{:S(2)}, u32[]{:S(2)}) collective-permute-start(bf16[256,512]{1,0:T(8,128)(2,1)S(1)} %shard_map.65), channel_id=1, source_target_pairs={{16,0},{12,4},{24,8},{4,12},{0,16},{28,20},{8,24},{20,28},{17,1},{... | collective-permute-start | bytes 786440 | tf_op jit(solution)/shard_map/ppermute | solution.py:49
  39.6 1.1 %copy-start = (bf16[1536,512]{1,0:T(8,128)(2,1)}, bf16[1536,512]{1,0:T(8,128)(2,1)S(1)}, u32[]{:S(2)}) copy-start(bf16[1536,512]{1,0:T(8,128)(2,1)S(1)} %get-tuple-element.27.refs_2_) | copy-start | bytes 4718596
  40.8 0.8 %copy-start.8 = (bf16[512,512]{1,0:T(8,128)(2,1)}, bf16[512,512]{1,0:T(8,128)(2,1)S(1)}, u32[]{:S(2)}) copy-start(bf16[512,512]{1,0:T(8,128)(2,1)S(1)} %get-tuple-element.32.refs_6_) | copy-start | bytes 1572868
  44.5 1.2 %copy-start.2 = (bf16[1536,512]{1,0:T(8,128)(2,1)}, bf16[1536,512]{1,0:T(8,128)(2,1)S(1)}, u32[]{:S(2)}) copy-start(bf16[1536,512]{1,0:T(8,128)(2,1)S(1)} %get-tuple-element.29.refs_3_) | copy-start | bytes 4718596
  45.6 0.8 %copy-start.10 = (bf16[512,512]{1,0:T(8,128)(2,1)}, bf16[512,512]{1,0:T(8,128)(2,1)S(1)}, u32[]{:S(2)}) copy-start(bf16[512,512]{1,0:T(8,128)(2,1)S(1)} %get-tuple-element.33.refs_7_) | copy-start | bytes 1572868
  46.5 4.8 %collective-permute-start.13 = (f32[3,4,512]{2,1,0:T(4,128)S(1)}, f32[3,4,512]{2,1,0:T(4,128)S(1)}, u32[]{:S(2)}, u32[]{:S(2)}) collective-permute-start(f32[3,4,512]{2,1,0:T(4,128)S(1)} %copy.6), channel_id=1, source_target_pairs={{24,0},{16,8},{8,16},{0,24},{25,1},{17,9},{9,17},{1,25},{26,2},{18... | collective-permute-start | bytes 73736 | tf_op jit(solution)/shard_map/ppermute | solution.py:49
  49.0 3.8 %collective-permute-start.12 = (f32[3,4,512]{2,1,0:T(4,128)S(1)}, f32[3,4,512]{2,1,0:T(4,128)S(1)}, u32[]{:S(2)}, u32[]{:S(2)}) collective-permute-start(f32[3,4,512]{2,1,0:T(4,128)S(1)} %copy.6), channel_id=1, source_target_pairs={{16,0},{24,8},{0,16},{8,24},{17,1},{25,9},{1,17},{9,25},{18,2},{26... | collective-permute-start | bytes 73736 | tf_op jit(solution)/shard_map/ppermute | solution.py:49
  49.5 3.8 %collective-permute-start.11 = (f32[3,4,512]{2,1,0:T(4,128)S(1)}, f32[3,4,512]{2,1,0:T(4,128)S(1)}, u32[]{:S(2)}, u32[]{:S(2)}) collective-permute-start(f32[3,4,512]{2,1,0:T(4,128)S(1)} %copy.6), channel_id=1, source_target_pairs={{8,0},{0,8},{24,16},{16,24},{9,1},{1,9},{25,17},{17,25},{10,2},{2,... | collective-permute-start | bytes 73736 | tf_op jit(solution)/shard_map/ppermute | solution.py:49
  53.4 5.7 %collective-permute-start.16 = (f32[3,4,512]{2,1,0:T(4,128)S(1)}, f32[3,4,512]{2,1,0:T(4,128)S(1)}, u32[]{:S(2)}, u32[]{:S(2)}) collective-permute-start(f32[3,4,512]{2,1,0:T(4,128)S(1)} %pad_maximum_fusion.1), channel_id=1, source_target_pairs={{3,0},{2,1},{1,2},{0,3},{7,4},{6,5},{5,6},{4,7},{11,8},{10,9},{9,1... | collective-permute-start | bytes 73736 | tf_op jit(solution)/shard_map/ppermute | solution.py:49
  57.0 4.7 %collective-permute-start.15 = (f32[3,4,512]{2,1,0:T(4,128)S(1)}, f32[3,4,512]{2,1,0:T(4,128)S(1)}, u32[]{:S(2)}, u32[]{:S(2)}) collective-permute-start(f32[3,4,512]{2,1,0:T(4,128)S(1)} %pad_maximum_fusion.1), channel_id=1, source_target_pairs={{2,0},{3,1},{0,2},{1,3},{6,4},{7,5},{4,6},{5,7},{10,8},{11,9},{8,1... | collective-permute-start | bytes 73736 | tf_op jit(solution)/shard_map/ppermute | solution.py:49
  57.0 3.8 %collective-permute-start.14 = (f32[3,4,512]{2,1,0:T(4,128)S(1)}, f32[3,4,512]{2,1,0:T(4,128)S(1)}, u32[]{:S(2)}, u32[]{:S(2)}) collective-permute-start(f32[3,4,512]{2,1,0:T(4,128)S(1)} %pad_maximum_fusion.1), channel_id=1, source_target_pairs={{1,0},{0,1},{3,2},{2,3},{5,4},{4,5},{7,6},{6,7},{9,8},{8,9},{11,10... | collective-permute-start | bytes 73736 | tf_op jit(solution)/shard_map/ppermute | solution.py:49
  61.8 1.4 %copy-start.1 = (bf16[1536,512]{1,0:T(8,128)(2,1)S(1)}, bf16[1536,512]{1,0:T(8,128)(2,1)}, u32[]{:S(2)}) copy-start(bf16[1536,512]{1,0:T(8,128)(2,1)} %copy-done) | copy-start | bytes 4718596
  63.2 1.4 %copy-start.3 = (bf16[1536,512]{1,0:T(8,128)(2,1)S(1)}, bf16[1536,512]{1,0:T(8,128)(2,1)}, u32[]{:S(2)}) copy-start(bf16[1536,512]{1,0:T(8,128)(2,1)} %copy-done.2) | copy-start | bytes 4718596
  64.6 1.0 %copy-start.5 = (bf16[512,512]{1,0:T(8,128)(2,1)S(1)}, bf16[512,512]{1,0:T(8,128)(2,1)}, u32[]{:S(2)}) copy-start(bf16[512,512]{1,0:T(8,128)(2,1)} %copy-done.4) | copy-start | bytes 1572868
  65.7 1.0 %copy-start.7 = (bf16[512,512]{1,0:T(8,128)(2,1)S(1)}, bf16[512,512]{1,0:T(8,128)(2,1)}, u32[]{:S(2)}) copy-start(bf16[512,512]{1,0:T(8,128)(2,1)} %copy-done.6) | copy-start | bytes 1572868
  66.7 1.0 %copy-start.9 = (bf16[512,512]{1,0:T(8,128)(2,1)S(1)}, bf16[512,512]{1,0:T(8,128)(2,1)}, u32[]{:S(2)}) copy-start(bf16[512,512]{1,0:T(8,128)(2,1)} %copy-done.8) | copy-start | bytes 1572868
  67.8 1.0 %copy-start.11 = (bf16[512,512]{1,0:T(8,128)(2,1)S(1)}, bf16[512,512]{1,0:T(8,128)(2,1)}, u32[]{:S(2)}) copy-start(bf16[512,512]{1,0:T(8,128)(2,1)} %copy-done.10) | copy-start | bytes 1572868
  70.8 2.3 %collective-permute-start.17 = (bf16[768,512]{1,0:T(8,128)(2,1)S(1)}, bf16[768,512]{1,0:T(8,128)(2,1)S(1)}, u32[]{:S(2)}, u32[]{:S(2)}) collective-permute-start(bf16[768,512]{1,0:T(8,128)(2,1)S(1)} %get-tuple-element.42), channel_id=1, source_target_pairs={{4,0},{0,4},{5,1},{1,5},{6,2},{2,6},{7,3},{3,7},{12,8},{8,12},{13,... | collective-permute-start | bytes 2359304 | tf_op jit(solution)/shard_map/ppermute | solution.py:49
  70.9 2.3 %collective-permute-start.18 = (f32[1,768]{1,0:T(1,128)S(1)}, f32[1,768]{1,0:T(1,128)S(1)}, u32[]{:S(2)}, u32[]{:S(2)}) collective-permute-start(f32[1,768]{1,0:T(1,128)S(1)} %get-tuple-element.43), channel_id=1, source_target_pairs={{4,0},{0,4},{5,1},{1,5},{6,2},{2,6},{7,3},{3,7},{12,8},{8,12},{13,... | collective-permute-start | bytes 9224 | tf_op jit(solution)/shard_map/ppermute | solution.py:49

commit v5 on v4

--- a/solution.py
+++ b/solution.py
@@ -9,7 +9,8 @@
 from jax.sharding import Mesh, PartitionSpec as P
 
 GATHER_BYTES = 8 << 20
-VMEM_BYTES = 16 << 20
+VMEM_BYTES = 4 << 20
+SUMS_VMEM_BYTES = 16 << 20
 
 
 def to_points(codes, exponents):
@@ -53,27 +54,24 @@
     return [pl.BlockSpec(memory_space=pltpu.VMEM)] * n
 
 
-def join_kernel(above, below, *refs):
-    out, rows = refs[-1], above.shape[0]
-    out[:rows, :] = above[...]
-    out[rows:, :] = below[...]
-
-
-def join(above, below, *after):
+def hold(a, after):
+    def kernel(a, after, out):
+        out[...] = a[...]
+
     return pl.pallas_call(
-        join_kernel,
-        in_specs=in_vmem(2 + len(after)),
+        kernel,
+        in_specs=in_vmem(2),
         out_specs=in_vmem(1)[0],
-        out_shape=jax.ShapeDtypeStruct((above.shape[0] + below.shape[0], above.shape[1]), above.dtype),
+        out_shape=jax.ShapeDtypeStruct(a.shape, a.dtype),
         compiler_params=pltpu.CompilerParams(vmem_limit_bytes=VMEM_BYTES),
-    )(above, below, *after)
-
-
-def expo_kernel(rate, block, place, near, first, second, cells, inverse, expo, tops, stats, points):
-    rows = near.shape[0]
-    pieces = (near[...], first[...], second[:rows, :], second[rows:, :])
+    )(a, after)
+
+
+def expo_kernel(rate, block, place, *refs):
+    pieces, (cells, inverse, expo, tops, stats, points) = refs[:4], refs[4:]
+    rows = pieces[0].shape[0]
     for at, piece in enumerate(pieces):
-        points[pl.ds(pl.multiple_of(place[at] * rows, rows), rows), :] = piece
+        points[pl.ds(pl.multiple_of(place[at] * rows, rows), rows), :] = piece[...]
     every = points[...]
     highest = total = novel = None
     for at in range(cells.shape[0] // block):
@@ -107,7 +105,7 @@
     n_points = sum(piece.shape[0] for piece in pieces)
     return pl.pallas_call(
         functools.partial(expo_kernel, rate, block),
-        in_specs=[pl.BlockSpec(memory_space=pltpu.SMEM)] + in_vmem(5),
+        in_specs=[pl.BlockSpec(memory_space=pltpu.SMEM)] + in_vmem(6),
         out_specs=in_vmem(4),
         out_shape=[
             jax.ShapeDtypeStruct((count, n_points), jnp.bfloat16),
@@ -137,64 +135,77 @@
     return total, jnp.sum(weight.T, axis=0, keepdims=True)
 
 
-def sums_kernel(n, block, skip, half, *refs):
+def sums_kernel(n, block, half, *refs):
     expos, points, factor, (sums, mass) = refs[:n], refs[n : 2 * n], refs[2 * n], refs[2 * n + 1 :]
     factor = [factor.at[at] for at in range(n)]
-    for at in range(sums.shape[0] // block):
-        here = slice(at * block, (at + 1) * block)
-        total, weight = weighed_sums(half[0] * 2 + skip + at, block, expos, points, factor)
+
+    @pl.loop(0, sums.shape[0] // block)
+    def _(at):
+        here = pl.ds(pl.multiple_of(at * block, block), block)
+        total, weight = weighed_sums(half[0] + at, block, expos, points, factor)
         sums[here, :] = total.astype(sums.dtype)
         mass[:, here] = weight
 
 
-def last_kernel(n, block, skip, half, *refs):
+def last_kernel(n, block, half, *refs):
     expos, points, factor = refs[:n], refs[n : 2 * n], refs[2 * n]
     early, early_mass, there, there_mass, sums, mass, out, left = refs[2 * n + 1 :]
     factor = [factor.at[at] for at in range(n)]
-    copies = []
-
-    def store(start, stop, value):
-        out[start:stop, :] = value + there[start:stop, :].astype(jnp.float32)
-        here = pl.ds(start, stop - start)
-        copies.append(pltpu.make_async_copy(out.at[here, :], sums.at[here, :], left.at[len(copies)]))
-        copies[-1].start()
-
-    store(0, skip * block, early[...])
-    mass[:, : skip * block] = early_mass[...] + there_mass[:, : skip * block]
-    for at in range(skip, out.shape[0] // block):
-        start, stop = at * block, (at + 1) * block
-        total, weight = weighed_sums(half[0] * 2 + at, block, expos, points, factor)
-        store(start, stop, total)
-        mass[:, start:stop] = weight + there_mass[:, start:stop]
-    for copy in copies:
-        copy.wait()
-
-
-def sums_call(kernel, block, skip, rows, dtype, half, expos, points, factor, *more, last=False):
-    n = len(expos)
+    rows, skip = there.shape[0], early.shape[0]
+
+    def copy(at):
+        here = pl.ds(at * block, block)
+        return pltpu.make_async_copy(out.at[at % 2], sums.at[here, :], left.at[at % 2])
+
+    mass[:, :skip] = early_mass[...] + there_mass[:, :skip]
+    for at in range(rows // block):
+        here = slice(at * block, (at + 1) * block)
+        if at >= 2:
+            copy(at - 2).wait()
+        if at * block < skip:
+            total = early[here, :]
+        else:
+            total, weight = weighed_sums(half[0] + at, block, expos, points, factor)
+            mass[:, here] = weight + there_mass[:, here]
+        out[at % 2] = total + there[here, :].astype(jnp.float32)
+        copy(at).start()
+    for at in range(max(rows // block - 2, 0), rows // block):
+        copy(at).wait()
+
+
+def sums_call(kernel, block, rows, dtype, half, expos, points, factor, *more):
+    n, last = len(expos), kernel is last_kernel
     n_points, width = points[0].shape
-    work = rows // block - skip if last else rows // block
+    work = rows - more[0].shape[0] if last else rows
     return pl.pallas_call(
-        functools.partial(kernel, n, block, skip),
+        functools.partial(kernel, n, block),
         in_specs=[pl.BlockSpec(memory_space=pltpu.SMEM)] + in_vmem(2 * n + 1 + len(more)),
         out_specs=[pl.BlockSpec(memory_space=pltpu.HBM if last else pltpu.VMEM)] + in_vmem(1),
         out_shape=[jax.ShapeDtypeStruct((rows, width), dtype), jax.ShapeDtypeStruct((1, rows), jnp.float32)],
-        scratch_shapes=[pltpu.VMEM((rows, width), dtype), pltpu.SemaphoreType.DMA((1 + work,))] if last else [],
-        compiler_params=pltpu.CompilerParams(vmem_limit_bytes=VMEM_BYTES),
+        scratch_shapes=[pltpu.VMEM((2, block, width), dtype), pltpu.SemaphoreType.DMA((2,))] if last else [],
+        compiler_params=pltpu.CompilerParams(vmem_limit_bytes=SUMS_VMEM_BYTES),
         cost_estimate=pl.CostEstimate(
-            flops=2 * work * block * n * n_points * width,
-            bytes_accessed=2 * n * n_points * (work * block + width) + 4 * rows * width,
+            flops=2 * work * n * n_points * width,
+            bytes_accessed=2 * n * n_points * (work + width) + 4 * rows * width,
             transcendentals=0,
         ),
     )(half, *expos, *points, factor, *more)
 
 
 def merge(rate, stats):
-    top = functools.reduce(jnp.maximum, [s[0] for s in stats])
-    scales = [jnp.exp2((s[0] - top) * rate) for s in stats]
-    total = sum(s[1] * scale for s, scale in zip(stats, scales))
-    novel = sum(s[2] * scale for s, scale in zip(stats, scales))
-    return jnp.stack([top, total, novel])
+    top = jnp.max(stats[:, 0], axis=0)
+    scale = jnp.exp2((stats[:, 0] - top) * rate)
+    return jnp.stack([top, jnp.sum(stats[:, 1] * scale, axis=0), jnp.sum(stats[:, 2] * scale, axis=0)])
+
+
+def everyone(a, axes):
+    count = math.prod(lax.axis_size(axis) for axis in axes)
+    return lax.all_to_all(jnp.broadcast_to(a, (count, *a.shape)), axes, 0, 0)
+
+
+def shuffle(a, by):
+    a = jnp.where(by & 1, jnp.stack([a[:, d ^ 1] for d in range(4)], axis=1), a)
+    return jnp.where(by & 2, jnp.stack([a[:, d ^ 2] for d in range(4)], axis=1), a)
 
 
 def split_cells(codes, exponents, centroids, counters):
@@ -210,36 +221,34 @@
     place = jnp.stack([chip, chip ^ (1 + lo), chip ^ (2 - lo), chip ^ 3]).astype(jnp.int32)
 
     per_device = centroids.shape[0] // 8
-    block = per_device // 2
+    block = per_device // 3
 
     cells, counts = (lax.dynamic_slice_in_dim(a, chip * 2 * per_device, 2 * per_device) for a in (centroids, counters))
     inverse = lax.rsqrt(counts.astype(jnp.float32) + 1.0)
     inverse = jnp.broadcast_to(inverse[:, None], (inverse.shape[0], 128))
 
     nears = [own] + [along_z(own, by) for by in (1, 2, 3)]
-    firsts = [turn(near) for near in nears]
     expos, tops, stats, points = [], [], [], []
-    for step, (near, first) in enumerate(zip(nears, firsts)):
-        second = turn_back(join(near, first, *stats[step - 2 : step - 1] if step > 1 else ()))
-        expo, top, stat, chunk = expo_call(rate, block, place, (near, first, second), cells, inverse)
+    for step, near in enumerate(nears):
+        first, second = turn(near), turn_back(near)
+        across = turn_back(hold(first, stats[step // 2]) if step % 2 else first)
+        expo, top, stat, chunk = expo_call(rate, block, place, (near, first, second, across), cells, inverse)
         expos.append(expo), tops.append(top), stats.append(stat), points.append(chunk)
 
-    stat = jnp.stack(stats, axis=1)
-    stat = merge(rate, [stat] + [exchange(stat, ("y", "x"), lambda at: at ^ by) for by in (1, 2, 3)])
-    every = [stat]
-    for by in (1, 2, 3):
-        theirs = along_z(stat, by)
-        every.append(jnp.stack([theirs[:, step ^ by] for step in range(4)], axis=1))
-    stat = merge(rate, every)
+    z = lax.axis_index("cells")
+    stat = shuffle(jnp.stack(stats, axis=1), z)
+    for axes in (("y", "x"), ("cells",)):
+        stat = merge(rate, everyone(stat, axes))
+    stat = shuffle(stat, z)
     factor = jnp.exp2((jnp.stack(tops) - stat[0][:, None]) * rate) * (stat[2] / stat[1] / stat[1])[:, None]
 
-    other, mine = ((a * jnp.ones((1,), jnp.int32)).astype(jnp.int32) for a in (1 - lo, lo))
+    other, mine = ((a * jnp.full((1,), per_device // block)).astype(jnp.int32) for a in (1 - lo, lo))
     parts = (expos, points, factor)
-    there, there_mass = sums_call(sums_kernel, block, 0, per_device, jnp.bfloat16, other, *parts)
+    there, there_mass = sums_call(sums_kernel, block, per_device, jnp.bfloat16, other, *parts)
     there, there_mass = (exchange(a, ("lo",), lambda at: at ^ 1) for a in (there, there_mass))
-    early, early_mass = sums_call(sums_kernel, block, 0, block, jnp.float32, mine, *parts)
+    early, early_mass = sums_call(sums_kernel, block, 2 * block, jnp.float32, mine, *parts)
     out, mass = sums_call(
-        last_kernel, block, 1, per_device, jnp.float32, mine, *parts, early, early_mass, there, there_mass, last=True
+        last_kernel, block, per_device, jnp.float32, mine, *parts, early, early_mass, there, there_mass
     )
     return (out[None], mass)
 

time: 76.6 us -> 94 us (1.23)
  local copies, waits for them, and re-layouts: 17.3 us -> 29.8 us
  blocking collectives: 0 us -> 8.08 us
  waiting for transfers between devices: 11.8 us -> 8.51 us
    unnamed x46 -> x59, local copies, waits for them, and re-layouts: 15.5 us -> 27.3 us
    ppermute x19 -> x17, waiting for transfers between devices: 11.8 us -> 2.68 us  [exchange(): return lax.ppermute(a, axes, [(partner(at), at) for at in range(count)])]
    all_to_all x0 -> x1, blocking collectives: none -> 8.08 us  [everyone(): return lax.all_to_all(jnp.broadcast_to(a, (count, *a.shape)), axes, 0, 0)]
    all_to_all x0 -> x1, waiting for transfers between devices: none -> 5.83 us  [everyone(): return lax.all_to_all(jnp.broadcast_to(a, (count, *a.shape)), axes, 0, 0)]
    ppermute x19 -> x17, starting transfers between devices: 24.6 us -> 19.7 us  [exchange(): return lax.ppermute(a, axes, [(partner(at), at) for at in range(count)])]
    all_to_all x0 -> x1, starting transfers between devices: none -> 4.02 us  [everyone(): return lax.all_to_all(jnp.broadcast_to(a, (count, *a.shape)), axes, 0, 0)]
    pallas_call x7 -> x5, Pallas kernels: 8.08 us -> 8.59 us  [the longest x3 8.57 us: sums_call(): pl.pallas_call(functools.partial(kernel, n, block), in_specs=[pl.BlockSpe...]
  transfers between devices with their start and end apart: 19 -> 18, of which waited for: 10 -> 4; matrix products, arithmetic and copies ran while one was open for 4% -> 3% of each run, Pallas kernels for 15% -> 10%
where the time goes in v5:
time: 94 us; the launch traced here: 92.9 us
  local copies, waits for them, and re-layouts  29.8 us (32%)
  starting transfers between devices  23.7 us (25%)
  Pallas kernels  18.9 us (20%)
  waiting for transfers between devices  8.51 us (9%)
  blocking collectives  8.08 us (9%)
  other arithmetic  2.86 us (3%)
    unnamed x59, local copies, waits for them, and re-layouts  27.3 us
    ppermute x17, starting transfers between devices, exchange(): return lax.ppermute(a, axes, [(partner(at), at) for at in range(count)])  19.7 us
    pallas_call x4, Pallas kernels, expo_call(): pl.pallas_call(functools.partial(expo_kernel, rate, block), in_specs=[pl....  10.3 us
    pallas_call x3, Pallas kernels, sums_call(): pl.pallas_call(functools.partial(kernel, n, block), in_specs=[pl.BlockSpe...  8.57 us
    all_to_all x1, blocking collectives, everyone(): return lax.all_to_all(jnp.broadcast_to(a, (count, *a.shape)), axes, 0, 0)  8.08 us
    all_to_all x1, waiting for transfers between devices, everyone(): return lax.all_to_all(jnp.broadcast_to(a, (count, *a.shape)), axes, 0, 0)  5.83 us
    all_to_all x1, starting transfers between devices, everyone(): return lax.all_to_all(jnp.broadcast_to(a, (count, *a.shape)), axes, 0, 0)  4.02 us
    ppermute x17, waiting for transfers between devices, exchange(): return lax.ppermute(a, axes, [(partner(at), at) for at in range(count)])  2.68 us
  transfers between devices with their start and end apart: 18, of which 4 were waited for; matrix products, arithmetic and copies ran while one was open for 3% of the time, Pallas kernels for 10%

profile of v5, /device:TPU:0, one launch (start us, length us, event | category | flops | bytes accessed | tf_op | source)
XLA Modules:
  0.0 92.9 jit_solution(6554322793941796460)
XLA Ops:
  0.6 0.7 convert_multiply_fusion
  1.3 1.0 %multiply_convert_fusion.refs_0_ = bf16[128,512]{1,0:T(8,128)(2,1)S(1)} fusion(s32[128,512]{1,0:T(8,128)} %param.4, f32[128]{0:T(128)S(1)} %convert_multiply_fusion), kind=kLoop, calls=%fused_computation | loop fusion | flops 196608 | bytes 393728 | tf_op jit(solution)/shard_map/convert_element_type | solution.py:18
  2.3 5.1 %collective-permute-start.11 = (bf16[128,512]{1,0:T(8,128)(2,1)S(1)}, bf16[128,512]{1,0:T(8,128)(2,1)}, u32[]{:S(2)}, u32[]{:S(2)}) collective-permute-start(bf16[128,512]{1,0:T(8,128)(2,1)S(1)} %multiply_convert_fusion.refs_0_), channel_id=1, source_target_pairs={{3,0},{2,1},{1,2},{0,3},{7,4},{6,5},{5,6},{4,7},{11,8},{10,9},{9,1... | collective-permute-start | bytes 393224 | tf_op jit(solution)/shard_map/ppermute | solution.py:50
  7.4 0.6 collective-permute-start.3
  8.1 1.7 %collective-permute-start.1 = (bf16[128,512]{1,0:T(8,128)(2,1)S(1)}, bf16[128,512]{1,0:T(8,128)(2,1)S(1)}, u32[]{:S(2)}, u32[]{:S(2)}) collective-permute-start(bf16[128,512]{1,0:T(8,128)(2,1)S(1)} %multiply_convert_fusion.refs_0_), channel_id=1, source_target_pairs={{16,0},{12,4},{24,8},{4,12},{0,16},{28,20},{8,24},{20,28},{17,1},{... | collective-permute-start | bytes 393224 | tf_op jit(solution)/shard_map/ppermute | solution.py:50
  9.8 1.5 %collective-permute-start = (bf16[128,512]{1,0:T(8,128)(2,1)S(1)}, bf16[128,512]{1,0:T(8,128)(2,1)S(1)}, u32[]{:S(2)}, u32[]{:S(2)}) collective-permute-start(bf16[128,512]{1,0:T(8,128)(2,1)S(1)} %multiply_convert_fusion.refs_0_), channel_id=1, source_target_pairs={{8,0},{20,4},{0,8},{28,12},{24,16},{4,20},{16,24},{12,28},{9,1},{2... | collective-permute-start | bytes 393224 | tf_op jit(solution)/shard_map/ppermute | solution.py:50
  11.2 1.5 %constant_dynamic-slice_fusion.refs_4_ = bf16[1536,512]{1,0:T(8,128)(2,1)S(1)} fusion(bf16[6144,512]{1,0:T(8,128)(2,1)} %param.6, s32[]{:T(128)S(6)} %select_n.26), kind=kLoop, calls=%fused_computation.38 | loop fusion | bytes 3145732 | tf_op jit(solution)/shard_map/dynamic_slice | solution.py:226
  12.8 0.0 copy-start.18
  12.8 2.0 %collective-permute-done.refs_1_ = bf16[128,512]{1,0:T(8,128)(2,1)S(1)} collective-permute-done((bf16[128,512]{1,0:T(8,128)(2,1)S(1)}, bf16[128,512]{1,0:T(8,128)(2,1)S(1)}, u32[]{:S(2)}, u32[]{:S(2)}) %collective-permute-start) | collective-permute-done | bytes 131104 | tf_op jit(solution)/shard_map/ppermute | solution.py:50
  14.7 0.4 collective-permute-start.2
  15.1 0.6 copy-done.25
  15.7 0.8 add_rsqrt_fusion
  16.5 1.7 %collective-permute-start.4 = (bf16[128,512]{1,0:T(8,128)(2,1)S(1)}, bf16[128,512]{1,0:T(8,128)(2,1)S(1)}, u32[]{:S(2)}, u32[]{:S(2)}) collective-permute-start(bf16[128,512]{1,0:T(8,128)(2,1)S(1)} %collective-permute-done.3.refs_0_), channel_id=1, source_target_pairs={{8,0},{20,4},{0,8},{28,12},{24,16},{4,20},{16,24},{12,28},{9,1},{2... | collective-permute-start | bytes 393224 | tf_op jit(solution)/shard_map/ppermute | solution.py:50
  18.2 0.1 pad_add_fusion.place
  18.3 0.3 collective-permute-done.7.refs_0_
  18.6 1.5 %collective-permute-start.5 = (bf16[128,512]{1,0:T(8,128)(2,1)S(1)}, bf16[128,512]{1,0:T(8,128)(2,1)S(1)}, u32[]{:S(2)}, u32[]{:S(2)}) collective-permute-start(bf16[128,512]{1,0:T(8,128)(2,1)S(1)} %collective-permute-done.3.refs_0_), channel_id=1, source_target_pairs={{16,0},{12,4},{24,8},{4,12},{0,16},{28,20},{8,24},{20,28},{17,1},{... | collective-permute-start | bytes 393224 | tf_op jit(solution)/shard_map/ppermute | solution.py:50
  20.2 0.6 copy-done.23
  20.8 1.5 %collective-permute-start.8 = (bf16[128,512]{1,0:T(8,128)(2,1)}, bf16[128,512]{1,0:T(8,128)(2,1)}, u32[]{:S(2)}, u32[]{:S(2)}) collective-permute-start(bf16[128,512]{1,0:T(8,128)(2,1)} %collective-permute-done.7.refs_0_), channel_id=1, source_target_pairs={{8,0},{20,4},{0,8},{28,12},{24,16},{4,20},{16,24},{12,28},{9,1},{2... | collective-permute-start | bytes 393224 | tf_op jit(solution)/shard_map/ppermute | solution.py:50
  22.3 0.7 copy-done.27
  23.0 0.3 broadcast_in_dim.11.refs_5_
  23.2 0.9 copy-done.24
  24.1 0.9 copy-done.26
  25.0 0.9 copy-done.28
  25.9 2.3 %shard_map.59 = (bf16[1536,512]{1,0:T(8,128)(2,1)S(1)}, f32[6,512]{1,0:T(8,128)S(1)}, f32[3,512]{1,0:T(4,128)S(1)}, bf16[512,512]{1,0:T(8,128)(2,1)S(1)}) custom-call(s32[4]{0:T(128)S(1)} %pad_add_fusion.place, bf16[128,512]{1,0:T(8,128)(2,1)S(1)} %multiply_convert_fusion.refs_0_, bf16[128,512]{1,0:T(8,128)(2,1)S(1)} %copy-done.26, ...), custom_call_target="tpu_custom_call" | custom-call | flops 805306368 | bytes 3670016 | tf_op jit(solution)/shard_map/pallas_call | solution.py:106
  28.3 0.6 collective-permute-start.6
  28.9 0.5 collective-permute-start.12
  29.4 1.5 %collective-permute-start.13 = (bf16[128,512]{1,0:T(8,128)(2,1)}, bf16[128,512]{1,0:T(8,128)(2,1)}, u32[]{:S(2)}, u32[]{:S(2)}) collective-permute-start(bf16[128,512]{1,0:T(8,128)(2,1)} %collective-permute-done.11.refs_0_), channel_id=1, source_target_pairs={{16,0},{12,4},{24,8},{4,12},{0,16},{28,20},{8,24},{20,28},{17,1},{... | collective-permute-start | bytes 393224 | tf_op jit(solution)/shard_map/ppermute | solution.py:50
  30.9 0.5 collective-permute-start.9
  31.4 1.5 %collective-permute-start.10 = (bf16[128,512]{1,0:T(8,128)(2,1)}, bf16[128,512]{1,0:T(8,128)(2,1)}, u32[]{:S(2)}, u32[]{:S(2)}) collective-permute-start(bf16[128,512]{1,0:T(8,128)(2,1)} %collective-permute-done.8.refs_1_), channel_id=1, source_target_pairs={{16,0},{12,4},{24,8},{4,12},{0,16},{28,20},{8,24},{20,28},{17,1},{... | collective-permute-start | bytes 393224 | tf_op jit(solution)/shard_map/ppermute | solution.py:50
  33.0 0.4 collective-permute-done.6.refs_3_
  33.3 1.4 %copy-done.19 = bf16[1536,512]{1,0:T(8,128)(2,1)S(1)} copy-done((bf16[1536,512]{1,0:T(8,128)(2,1)S(1)}, bf16[1536,512]{1,0:T(8,128)(2,1)}, u32[]{:S(2)}) %copy-start.19) | copy-done | bytes 1572888
  34.7 2.3 %shard_map.61 = (bf16[1536,512]{1,0:T(8,128)(2,1)S(1)}, f32[6,512]{1,0:T(8,128)S(1)}, f32[3,512]{1,0:T(4,128)S(1)}, bf16[512,512]{1,0:T(8,128)(2,1)S(1)}) custom-call(s32[4]{0:T(128)S(1)} %pad_add_fusion.place, bf16[128,512]{1,0:T(8,128)(2,1)S(1)} %collective-permute-done.3.refs_0_, bf16[128,512]{1,0:T(8,128)(2,1)S(1)} %collective-permute-done.4.a.refs_1_, ...), custom_call_target="tpu_custom_call" | custom-call | flops 805306368 | bytes 3670016 | tf_op jit(solution)/shard_map/pallas_call | solution.py:106
  37.1 0.8 copy-done.9
  37.9 0.6 collective-permute-start.14
  38.5 1.4 %copy-done.20 = bf16[1536,512]{1,0:T(8,128)(2,1)S(1)} copy-done((bf16[1536,512]{1,0:T(8,128)(2,1)S(1)}, bf16[1536,512]{1,0:T(8,128)(2,1)}, u32[]{:S(2)}) %copy-start.20) | copy-done | bytes 1572888
  39.9 1.1 %copy-done.22 = f32[1536,128]{1,0:T(8,128)S(1)} copy-done((f32[1536,128]{1,0:T(8,128)S(1)}, f32[1536,128]{1,0:T(8,128)}, u32[]{:S(2)}) %copy-start.22) | copy-done | bytes 786456
  41.0 2.9 %shard_map.62 = (bf16[1536,512]{1,0:T(8,128)(2,1)S(1)}, f32[6,512]{1,0:T(8,128)S(1)}, f32[3,512]{1,0:T(4,128)S(1)}, bf16[512,512]{1,0:T(8,128)(2,1)S(1)}) custom-call(s32[4]{0:T(128)S(1)} %pad_add_fusion.place, bf16[128,512]{1,0:T(8,128)(2,1)} %collective-permute-done.7.refs_0_, bf16[128,512]{1,0:T(8,128)(2,1)} %collective-permute-done.8.refs_1_, ...), custom_call_target="tpu_custom_call" | custom-call | flops 805306368 | bytes 3670016 | tf_op jit(solution)/shard_map/pallas_call | solution.py:106
  43.9 0.0 copy-start
  43.9 1.1 %copy-done = bf16[1536,512]{1,0:T(8,128)(2,1)} copy-done((bf16[1536,512]{1,0:T(8,128)(2,1)}, bf16[1536,512]{1,0:T(8,128)(2,1)S(1)}, u32[]{:S(2)}) %copy-start) | copy-done | bytes 1572888
  45.0 0.8 copy-done.12
  45.8 2.8 %shard_map.64 = (bf16[1536,512]{1,0:T(8,128)(2,1)S(1)}, f32[6,512]{1,0:T(8,128)S(1)}, f32[3,512]{1,0:T(4,128)S(1)}, bf16[512,512]{1,0:T(8,128)(2,1)S(1)}) custom-call(s32[4]{0:T(128)S(1)} %pad_add_fusion.place, bf16[128,512]{1,0:T(8,128)(2,1)} %collective-permute-done.11.refs_0_, bf16[128,512]{1,0:T(8,128)(2,1)S(1)} %collective-permute-done.12.a.refs_1_, ...), custom_call_target="tpu_custom_call" | custom-call | flops 805306368 | bytes 3670016 | tf_op jit(solution)/shard_map/pallas_call | solution.py:106
  48.7 1.2 %copy-done.3 = bf16[1536,512]{1,0:T(8,128)(2,1)} copy-done((bf16[1536,512]{1,0:T(8,128)(2,1)}, bf16[1536,512]{1,0:T(8,128)(2,1)S(1)}, u32[]{:S(2)}) %copy-start.3) | copy-done | bytes 1572888
  49.9 0.8 copy-done.15
  50.8 8.1 %all_to_all.10 = f32[4,3,4,512]{3,2,1,0:T(4,128)S(1)} all-to-all(f32[4,3,4,512]{3,2,1,0:T(4,128)S(1)} %broadcast_in_dim.24), channel_id=1, replica_groups=mesh['y'=2,'x'=2,'lo'=2,'cells'=4] {'y','x'}, dimensions={0} | all-to-all | bytes 196608 | tf_op jit(solution)/shard_map/all_to_all | solution.py:203
  58.9 0.7 broadcast_in_dim.25
  59.6 4.0 %all-to-all-start.1 = ((f32[4,3,4,512]{3,2,1,0:T(4,128)}), f32[4,3,4,512]{3,2,1,0:T(4,128)S(1)}, u32[]{:S(2)}, u32[]{:S(2)}) async-start(f32[4,3,4,512]{3,2,1,0:T(4,128)} %broadcast_in_dim.25), calls=%async_computation.1 | async-start | bytes 196608 | tf_op jit(solution)/shard_map/all_to_all | solution.py:203
  63.6 5.8 %all-to-all-done.1 = f32[4,3,4,512]{3,2,1,0:T(4,128)S(1)} async-done(((f32[4,3,4,512]{3,2,1,0:T(4,128)}), f32[4,3,4,512]{3,2,1,0:T(4,128)S(1)}, u32[]{:S(2)}, u32[]{:S(2)}) %all-to-all-start.1) | async-done | bytes 98336 | tf_op jit(solution)/shard_map/all_to_all | solution.py:203
  69.8 0.0 copy-start.1
  69.8 1.4 %copy-done.1 = bf16[1536,512]{1,0:T(8,128)(2,1)S(1)} copy-done((bf16[1536,512]{1,0:T(8,128)(2,1)S(1)}, bf16[1536,512]{1,0:T(8,128)(2,1)}, u32[]{:S(2)}) %copy-start.1) | copy-done | bytes 1572888
  71.2 1.4 %copy-done.4 = bf16[1536,512]{1,0:T(8,128)(2,1)S(1)} copy-done((bf16[1536,512]{1,0:T(8,128)(2,1)S(1)}, bf16[1536,512]{1,0:T(8,128)(2,1)}, u32[]{:S(2)}) %copy-start.4) | copy-done | bytes 1572888
  72.6 1.0 %copy-done.7 = bf16[512,512]{1,0:T(8,128)(2,1)S(1)} copy-done((bf16[512,512]{1,0:T(8,128)(2,1)S(1)}, bf16[512,512]{1,0:T(8,128)(2,1)}, u32[]{:S(2)}) %copy-start.7) | copy-done | bytes 524312
  73.7 1.0 %copy-done.10 = bf16[512,512]{1,0:T(8,128)(2,1)S(1)} copy-done((bf16[512,512]{1,0:T(8,128)(2,1)S(1)}, bf16[512,512]{1,0:T(8,128)(2,1)}, u32[]{:S(2)}) %copy-start.10) | copy-done | bytes 524312
  74.7 1.0 %copy-done.13 = bf16[512,512]{1,0:T(8,128)(2,1)S(1)} copy-done((bf16[512,512]{1,0:T(8,128)(2,1)S(1)}, bf16[512,512]{1,0:T(8,128)(2,1)}, u32[]{:S(2)}) %copy-start.13) | copy-done | bytes 524312
  75.7 1.0 %copy-done.16 = bf16[512,512]{1,0:T(8,128)(2,1)S(1)} copy-done((bf16[512,512]{1,0:T(8,128)(2,1)S(1)}, bf16[512,512]{1,0:T(8,128)(2,1)}, u32[]{:S(2)}) %copy-start.16) | copy-done | bytes 524312
  76.8 3.0 %shard_map.66 = (bf16[768,512]{1,0:T(8,128)(2,1)}, f32[1,768]{1,0:T(1,128)S(1)}) custom-call(s32[1]{0:T(128)} %bitcast.22.half, bf16[1536,512]{1,0:T(8,128)(2,1)S(1)} %get-tuple-element.24.refs_0_, bf16[1536,512]{1,0:T(8,128)(2,1)S(1)} %get-tuple-element.26.refs_1_, bf16[1536,512]{1,0:T(8,128)(2,1)S(1)} %copy-done.1, bf16[1536,512]{1,0:T(8,128)(2,1)S(1)} %copy-done.4, ...), custom_call_target="tpu_custom_call" | custom-call | flops 1610612736 | bytes 6815744 | tf_op jit(solution)/shard_map/pallas_call | solution.py:180
  79.8 0.5 collective-permute-start.16
  80.3 1.4 %copy-done.2 = bf16[1536,512]{1,0:T(8,128)(2,1)S(1)} copy-done((bf16[1536,512]{1,0:T(8,128)(2,1)S(1)}, bf16[1536,512]{1,0:T(8,128)(2,1)}, u32[]{:S(2)}) %copy-start.2) | copy-done | bytes 1572888
  81.7 1.4 %copy-done.5 = bf16[1536,512]{1,0:T(8,128)(2,1)S(1)} copy-done((bf16[1536,512]{1,0:T(8,128)(2,1)S(1)}, bf16[1536,512]{1,0:T(8,128)(2,1)}, u32[]{:S(2)}) %copy-start.5) | copy-done | bytes 1572888
  83.2 1.0 %copy-done.8 = bf16[512,512]{1,0:T(8,128)(2,1)S(1)} copy-done((bf16[512,512]{1,0:T(8,128)(2,1)S(1)}, bf16[512,512]{1,0:T(8,128)(2,1)}, u32[]{:S(2)}) %copy-start.8) | copy-done | bytes 524312
  84.2 1.0 %copy-done.11 = bf16[512,512]{1,0:T(8,128)(2,1)S(1)} copy-done((bf16[512,512]{1,0:T(8,128)(2,1)S(1)}, bf16[512,512]{1,0:T(8,128)(2,1)}, u32[]{:S(2)}) %copy-start.11) | copy-done | bytes 524312
  85.2 1.0 %copy-done.14 = bf16[512,512]{1,0:T(8,128)(2,1)S(1)} copy-done((bf16[512,512]{1,0:T(8,128)(2,1)S(1)}, bf16[512,512]{1,0:T(8,128)(2,1)}, u32[]{:S(2)}) %copy-start.14) | copy-done | bytes 524312
  86.3 1.0 %copy-done.17 = bf16[512,512]{1,0:T(8,128)(2,1)S(1)} copy-done((bf16[512,512]{1,0:T(8,128)(2,1)S(1)}, bf16[512,512]{1,0:T(8,128)(2,1)}, u32[]{:S(2)}) %copy-start.17) | copy-done | bytes 524312
  87.3 1.4 %shard_map.65 = (f32[512,512]{1,0:T(8,128)S(1)}, f32[1,512]{1,0:T(1,128)S(1)}) custom-call(s32[1]{0:T(128)} %bitcast.half, bf16[1536,512]{1,0:T(8,128)(2,1)S(1)} %get-tuple-element.24.refs_0_, bf16[1536,512]{1,0:T(8,128)(2,1)S(1)} %get-tuple-element.26.refs_1_, bf16[1536,512]{1,0:T(8,128)(2,1)S(1)} %copy-done.2, bf16[1536,512]{1,0:T(8,128)(2,1)S(1)} %copy-done.5, ...), custom_call_target="tpu_custom_call" | custom-call | flops 1073741824 | bytes 5242880 | tf_op jit(solution)/shard_map/pallas_call | solution.py:180
  88.8 4.1 %shard_map.67 = (f32[768,512]{1,0:T(8,128)}, f32[1,768]{1,0:T(1,128)}) custom-call(s32[1]{0:T(128)} %bitcast.half, bf16[1536,512]{1,0:T(8,128)(2,1)S(1)} %get-tuple-element.24.refs_0_, bf16[1536,512]{1,0:T(8,128)(2,1)S(1)} %get-tuple-element.26.refs_1_, bf16[1536,512]{1,0:T(8,128)(2,1)S(1)} %copy-done.2, bf16[1536,512]{1,0:T(8,128)(2,1)S(1)} %copy-done.5, ...), custom_call_target="tpu_custom_call" | custom-call | flops 536870912 | bytes 4718592 | tf_op jit(solution)/shard_map/pallas_call | solution.py:180
  (68 shorter events, 0.5 us)
Async XLA Ops:
  2.3 26.5 %collective-permute-start.11 = (bf16[128,512]{1,0:T(8,128)(2,1)S(1)}, bf16[128,512]{1,0:T(8,128)(2,1)}, u32[]{:S(2)}, u32[]{:S(2)}) collective-permute-start(bf16[128,512]{1,0:T(8,128)(2,1)S(1)} %multiply_convert_fusion.refs_0_), channel_id=1, source_target_pairs={{3,0},{2,1},{1,2},{0,3},{7,4},{6,5},{5,6},{4,7},{11,8},{10,9},{9,1... | collective-permute-start | bytes 393224 | tf_op jit(solution)/shard_map/ppermute | solution.py:50
  7.4 11.2 %collective-permute-start.7 = (bf16[128,512]{1,0:T(8,128)(2,1)S(1)}, bf16[128,512]{1,0:T(8,128)(2,1)}, u32[]{:S(2)}, u32[]{:S(2)}) collective-permute-start(bf16[128,512]{1,0:T(8,128)(2,1)S(1)} %multiply_convert_fusion.refs_0_), channel_id=1, source_target_pairs={{2,0},{3,1},{0,2},{1,3},{6,4},{7,5},{4,6},{5,7},{10,8},{11,9},{8,1... | collective-permute-start | bytes 393224 | tf_op jit(solution)/shard_map/ppermute | solution.py:50
  7.4 9.1 %collective-permute-start.3 = (bf16[128,512]{1,0:T(8,128)(2,1)S(1)}, bf16[128,512]{1,0:T(8,128)(2,1)S(1)}, u32[]{:S(2)}, u32[]{:S(2)}) collective-permute-start(bf16[128,512]{1,0:T(8,128)(2,1)S(1)} %multiply_convert_fusion.refs_0_), channel_id=1, source_target_pairs={{1,0},{0,1},{3,2},{2,3},{5,4},{4,5},{7,6},{6,7},{9,8},{8,9},{11,10... | collective-permute-start | bytes 393224 | tf_op jit(solution)/shard_map/ppermute | solution.py:50
  8.1 12.1 %collective-permute-start.1 = (bf16[128,512]{1,0:T(8,128)(2,1)S(1)}, bf16[128,512]{1,0:T(8,128)(2,1)S(1)}, u32[]{:S(2)}, u32[]{:S(2)}) collective-permute-start(bf16[128,512]{1,0:T(8,128)(2,1)S(1)} %multiply_convert_fusion.refs_0_), channel_id=1, source_target_pairs={{16,0},{12,4},{24,8},{4,12},{0,16},{28,20},{8,24},{20,28},{17,1},{... | collective-permute-start | bytes 393224 | tf_op jit(solution)/shard_map/ppermute | solution.py:50
  9.8 5.0 %collective-permute-start = (bf16[128,512]{1,0:T(8,128)(2,1)S(1)}, bf16[128,512]{1,0:T(8,128)(2,1)S(1)}, u32[]{:S(2)}, u32[]{:S(2)}) collective-permute-start(bf16[128,512]{1,0:T(8,128)(2,1)S(1)} %multiply_convert_fusion.refs_0_), channel_id=1, source_target_pairs={{8,0},{20,4},{0,8},{28,12},{24,16},{4,20},{16,24},{12,28},{9,1},{2... | collective-permute-start | bytes 393224 | tf_op jit(solution)/shard_map/ppermute | solution.py:50
  12.8 15.5 %copy-start.18 = (bf16[1536,512]{1,0:T(8,128)(2,1)}, bf16[1536,512]{1,0:T(8,128)(2,1)S(1)}, u32[]{:S(2)}) copy-start(bf16[1536,512]{1,0:T(8,128)(2,1)S(1)} %constant_dynamic-slice_fusion.refs_4_) | copy-start | bytes 4718596
  14.7 7.6 %collective-permute-start.2 = (bf16[128,512]{1,0:T(8,128)(2,1)S(1)}, bf16[128,512]{1,0:T(8,128)(2,1)S(1)}, u32[]{:S(2)}, u32[]{:S(2)}) collective-permute-start(bf16[128,512]{1,0:T(8,128)(2,1)S(1)} %collective-permute-done.refs_1_), channel_id=1, source_target_pairs={{16,0},{12,4},{24,8},{4,12},{0,16},{28,20},{8,24},{20,28},{17,1},{... | collective-permute-start | bytes 393224 | tf_op jit(solution)/shard_map/ppermute | solution.py:50
  15.1 0.7 copy-start.25
  16.5 11.7 %collective-permute-start.4 = (bf16[128,512]{1,0:T(8,128)(2,1)S(1)}, bf16[128,512]{1,0:T(8,128)(2,1)S(1)}, u32[]{:S(2)}, u32[]{:S(2)}) collective-permute-start(bf16[128,512]{1,0:T(8,128)(2,1)S(1)} %collective-permute-done.3.refs_0_), channel_id=1, source_target_pairs={{8,0},{20,4},{0,8},{28,12},{24,16},{4,20},{16,24},{12,28},{9,1},{2... | collective-permute-start | bytes 393224 | tf_op jit(solution)/shard_map/ppermute | solution.py:50
  18.6 12.8 %collective-permute-start.5 = (bf16[128,512]{1,0:T(8,128)(2,1)S(1)}, bf16[128,512]{1,0:T(8,128)(2,1)S(1)}, u32[]{:S(2)}, u32[]{:S(2)}) collective-permute-start(bf16[128,512]{1,0:T(8,128)(2,1)S(1)} %collective-permute-done.3.refs_0_), channel_id=1, source_target_pairs={{16,0},{12,4},{24,8},{4,12},{0,16},{28,20},{8,24},{20,28},{17,1},{... | collective-permute-start | bytes 393224 | tf_op jit(solution)/shard_map/ppermute | solution.py:50
  20.1 0.7 copy-start.23
  20.8 10.1 %collective-permute-start.8 = (bf16[128,512]{1,0:T(8,128)(2,1)}, bf16[128,512]{1,0:T(8,128)(2,1)}, u32[]{:S(2)}, u32[]{:S(2)}) collective-permute-start(bf16[128,512]{1,0:T(8,128)(2,1)} %collective-permute-done.7.refs_0_), channel_id=1, source_target_pairs={{8,0},{20,4},{0,8},{28,12},{24,16},{4,20},{16,24},{12,28},{9,1},{2... | collective-permute-start | bytes 393224 | tf_op jit(solution)/shard_map/ppermute | solution.py:50
  22.3 0.7 copy-start.27
  23.2 0.9 copy-start.24
  24.1 0.9 copy-start.26
  25.0 0.9 copy-start.28
  25.9 7.4 %copy-start.21 = (f32[1536,128]{1,0:T(8,128)}, f32[1536,128]{1,0:T(8,128)S(1)}, u32[]{:S(2)}) copy-start(f32[1536,128]{1,0:T(8,128)S(1)} %broadcast_in_dim.11.refs_5_) | copy-start | bytes 2359300
  28.3 8.8 %copy-start.6 = (bf16[512,512]{1,0:T(8,128)(2,1)}, bf16[512,512]{1,0:T(8,128)(2,1)S(1)}, u32[]{:S(2)}) copy-start(bf16[512,512]{1,0:T(8,128)(2,1)S(1)} %get-tuple-element.30.refs_4_) | copy-start | bytes 1572868
  28.3 5.0 %collective-permute-start.6 = (bf16[128,512]{1,0:T(8,128)(2,1)S(1)}, bf16[128,512]{1,0:T(8,128)(2,1)S(1)}, u32[]{:S(2)}, u32[]{:S(2)}) collective-permute-start(bf16[128,512]{1,0:T(8,128)(2,1)S(1)} %shard_map.60), channel_id=1, source_target_pairs={{16,0},{12,4},{24,8},{4,12},{0,16},{28,20},{8,24},{20,28},{17,1},{... | collective-permute-start | bytes 393224 | tf_op jit(solution)/shard_map/ppermute | solution.py:50
  28.9 9.0 %collective-permute-start.12 = (bf16[128,512]{1,0:T(8,128)(2,1)}, bf16[128,512]{1,0:T(8,128)(2,1)S(1)}, u32[]{:S(2)}, u32[]{:S(2)}) collective-permute-start(bf16[128,512]{1,0:T(8,128)(2,1)} %collective-permute-done.11.refs_0_), channel_id=1, source_target_pairs={{8,0},{20,4},{0,8},{28,12},{24,16},{4,20},{16,24},{12,28},{9,1},{2... | collective-permute-start | bytes 393224 | tf_op jit(solution)/shard_map/ppermute | solution.py:50
  29.4 16.4 %collective-permute-start.13 = (bf16[128,512]{1,0:T(8,128)(2,1)}, bf16[128,512]{1,0:T(8,128)(2,1)}, u32[]{:S(2)}, u32[]{:S(2)}) collective-permute-start(bf16[128,512]{1,0:T(8,128)(2,1)} %collective-permute-done.11.refs_0_), channel_id=1, source_target_pairs={{16,0},{12,4},{24,8},{4,12},{0,16},{28,20},{8,24},{20,28},{17,1},{... | collective-permute-start | bytes 393224 | tf_op jit(solution)/shard_map/ppermute | solution.py:50
  30.9 7.5 %collective-permute-start.9 = (bf16[128,512]{1,0:T(8,128)(2,1)}, bf16[128,512]{1,0:T(8,128)(2,1)}, u32[]{:S(2)}, u32[]{:S(2)}) collective-permute-start(bf16[128,512]{1,0:T(8,128)(2,1)} %collective-permute-done.7.refs_0_), channel_id=1, source_target_pairs={{16,0},{12,4},{24,8},{4,12},{0,16},{28,20},{8,24},{20,28},{17,1},{... | collective-permute-start | bytes 393224 | tf_op jit(solution)/shard_map/ppermute | solution.py:50
  31.4 7.0 %collective-permute-start.10 = (bf16[128,512]{1,0:T(8,128)(2,1)}, bf16[128,512]{1,0:T(8,128)(2,1)}, u32[]{:S(2)}, u32[]{:S(2)}) collective-permute-start(bf16[128,512]{1,0:T(8,128)(2,1)} %collective-permute-done.8.refs_1_), channel_id=1, source_target_pairs={{16,0},{12,4},{24,8},{4,12},{0,16},{28,20},{8,24},{20,28},{17,1},{... | collective-permute-start | bytes 393224 | tf_op jit(solution)/shard_map/ppermute | solution.py:50
  33.3 1.4 %copy-start.19 = (bf16[1536,512]{1,0:T(8,128)(2,1)S(1)}, bf16[1536,512]{1,0:T(8,128)(2,1)}, u32[]{:S(2)}) copy-start(bf16[1536,512]{1,0:T(8,128)(2,1)} %copy-done.18) | copy-start | bytes 4718596
  37.1 0.8 copy-start.9
  37.9 8.0 %collective-permute-start.14 = (bf16[128,512]{1,0:T(8,128)(2,1)S(1)}, bf16[128,512]{1,0:T(8,128)(2,1)}, u32[]{:S(2)}, u32[]{:S(2)}) collective-permute-start(bf16[128,512]{1,0:T(8,128)(2,1)S(1)} %shard_map.63), channel_id=1, source_target_pairs={{16,0},{12,4},{24,8},{4,12},{0,16},{28,20},{8,24},{20,28},{17,1},{... | collective-permute-start | bytes 393224 | tf_op jit(solution)/shard_map/ppermute | solution.py:50
  38.5 1.4 %copy-start.20 = (bf16[1536,512]{1,0:T(8,128)(2,1)S(1)}, bf16[1536,512]{1,0:T(8,128)(2,1)}, u32[]{:S(2)}) copy-start(bf16[1536,512]{1,0:T(8,128)(2,1)} %copy-done.18) | copy-start | bytes 4718596
  39.9 1.1 %copy-start.22 = (f32[1536,128]{1,0:T(8,128)S(1)}, f32[1536,128]{1,0:T(8,128)}, u32[]{:S(2)}) copy-start(f32[1536,128]{1,0:T(8,128)} %copy-done.21) | copy-start | bytes 2359300
  43.9 1.1 %copy-start = (bf16[1536,512]{1,0:T(8,128)(2,1)}, bf16[1536,512]{1,0:T(8,128)(2,1)S(1)}, u32[]{:S(2)}) copy-start(bf16[1536,512]{1,0:T(8,128)(2,1)S(1)} %get-tuple-element.27.refs_2_) | copy-start | bytes 4718596
  45.0 0.8 copy-start.12
  48.7 1.2 %copy-start.3 = (bf16[1536,512]{1,0:T(8,128)(2,1)}, bf16[1536,512]{1,0:T(8,128)(2,1)S(1)}, u32[]{:S(2)}) copy-start(bf16[1536,512]{1,0:T(8,128)(2,1)S(1)} %get-tuple-element.29.refs_3_) | copy-start | bytes 4718596
  49.9 0.8 copy-start.15
  59.6 9.9 %all-to-all-start.1 = ((f32[4,3,4,512]{3,2,1,0:T(4,128)}), f32[4,3,4,512]{3,2,1,0:T(4,128)S(1)}, u32[]{:S(2)}, u32[]{:S(2)}) async-start(f32[4,3,4,512]{3,2,1,0:T(4,128)} %broadcast_in_dim.25), calls=%async_computation.1 | async-start | bytes 196608 | tf_op jit(solution)/shard_map/all_to_all | solution.py:203
  69.8 1.4 %copy-start.1 = (bf16[1536,512]{1,0:T(8,128)(2,1)S(1)}, bf16[1536,512]{1,0:T(8,128)(2,1)}, u32[]{:S(2)}) copy-start(bf16[1536,512]{1,0:T(8,128)(2,1)} %copy-done) | copy-start | bytes 4718596
  71.2 1.4 %copy-start.4 = (bf16[1536,512]{1,0:T(8,128)(2,1)S(1)}, bf16[1536,512]{1,0:T(8,128)(2,1)}, u32[]{:S(2)}) copy-start(bf16[1536,512]{1,0:T(8,128)(2,1)} %copy-done.3) | copy-start | bytes 4718596
  72.6 1.0 %copy-start.7 = (bf16[512,512]{1,0:T(8,128)(2,1)S(1)}, bf16[512,512]{1,0:T(8,128)(2,1)}, u32[]{:S(2)}) copy-start(bf16[512,512]{1,0:T(8,128)(2,1)} %copy-done.6) | copy-start | bytes 1572868
  73.7 1.0 %copy-start.10 = (bf16[512,512]{1,0:T(8,128)(2,1)S(1)}, bf16[512,512]{1,0:T(8,128)(2,1)}, u32[]{:S(2)}) copy-start(bf16[512,512]{1,0:T(8,128)(2,1)} %copy-done.9) | copy-start | bytes 1572868
  74.7 1.0 %copy-start.13 = (bf16[512,512]{1,0:T(8,128)(2,1)S(1)}, bf16[512,512]{1,0:T(8,128)(2,1)}, u32[]{:S(2)}) copy-start(bf16[512,512]{1,0:T(8,128)(2,1)} %copy-done.12) | copy-start | bytes 1572868
  75.7 1.0 %copy-start.16 = (bf16[512,512]{1,0:T(8,128)(2,1)S(1)}, bf16[512,512]{1,0:T(8,128)(2,1)}, u32[]{:S(2)}) copy-start(bf16[512,512]{1,0:T(8,128)(2,1)} %copy-done.15) | copy-start | bytes 1572868
  79.8 9.0 %collective-permute-start.15 = (bf16[768,512]{1,0:T(8,128)(2,1)}, bf16[768,512]{1,0:T(8,128)(2,1)}, u32[]{:S(2)}, u32[]{:S(2)}) collective-permute-start(bf16[768,512]{1,0:T(8,128)(2,1)} %get-tuple-element.42), channel_id=1, source_target_pairs={{4,0},{0,4},{5,1},{1,5},{6,2},{2,6},{7,3},{3,7},{12,8},{8,12},{13,... | collective-permute-start | bytes 2359304 | tf_op jit(solution)/shard_map/ppermute | solution.py:50
  79.8 8.9 %collective-permute-start.16 = (f32[1,768]{1,0:T(1,128)S(1)}, f32[1,768]{1,0:T(1,128)S(1)}, u32[]{:S(2)}, u32[]{:S(2)}) collective-permute-start(f32[1,768]{1,0:T(1,128)S(1)} %get-tuple-element.43), channel_id=1, source_target_pairs={{4,0},{0,4},{5,1},{1,5},{6,2},{2,6},{7,3},{3,7},{12,8},{8,12},{13,... | collective-permute-start | bytes 9224 | tf_op jit(solution)/shard_map/ppermute | solution.py:50
  80.3 1.4 %copy-start.2 = (bf16[1536,512]{1,0:T(8,128)(2,1)S(1)}, bf16[1536,512]{1,0:T(8,128)(2,1)}, u32[]{:S(2)}) copy-start(bf16[1536,512]{1,0:T(8,128)(2,1)} %copy-done) | copy-start | bytes 4718596
  81.7 1.4 %copy-start.5 = (bf16[1536,512]{1,0:T(8,128)(2,1)S(1)}, bf16[1536,512]{1,0:T(8,128)(2,1)}, u32[]{:S(2)}) copy-start(bf16[1536,512]{1,0:T(8,128)(2,1)} %copy-done.3) | copy-start | bytes 4718596
  83.2 1.0 %copy-start.8 = (bf16[512,512]{1,0:T(8,128)(2,1)S(1)}, bf16[512,512]{1,0:T(8,128)(2,1)}, u32[]{:S(2)}) copy-start(bf16[512,512]{1,0:T(8,128)(2,1)} %copy-done.6) | copy-start | bytes 1572868
  84.2 1.0 %copy-start.11 = (bf16[512,512]{1,0:T(8,128)(2,1)S(1)}, bf16[512,512]{1,0:T(8,128)(2,1)}, u32[]{:S(2)}) copy-start(bf16[512,512]{1,0:T(8,128)(2,1)} %copy-done.9) | copy-start | bytes 1572868
  85.2 1.0 %copy-start.14 = (bf16[512,512]{1,0:T(8,128)(2,1)S(1)}, bf16[512,512]{1,0:T(8,128)(2,1)}, u32[]{:S(2)}) copy-start(bf16[512,512]{1,0:T(8,128)(2,1)} %copy-done.12) | copy-start | bytes 1572868
  86.3 1.0 %copy-start.17 = (bf16[512,512]{1,0:T(8,128)(2,1)S(1)}, bf16[512,512]{1,0:T(8,128)(2,1)}, u32[]{:S(2)}) copy-start(bf16[512,512]{1,0:T(8,128)(2,1)} %copy-done.15) | copy-start | bytes 1572868

commit v6 on v5

--- a/solution.py
+++ b/solution.py
@@ -54,6 +54,39 @@
     return [pl.BlockSpec(memory_space=pltpu.VMEM)] * n
 
 
+def cells_kernel(centroids, counters, cells, inverse, counters_here, arrived):
+    rows = cells.shape[0]
+    lines = rows // 128
+    chip = lax.axis_index("y") * 2 + lax.axis_index("x")
+    copies = [
+        pltpu.make_async_copy(counters, counters_here, arrived.at[0]),
+        pltpu.make_async_copy(centroids.at[pl.ds(pl.multiple_of(chip * rows, rows), rows), :], cells, arrived.at[1]),
+    ]
+    for copy in copies:
+        copy.start()
+    copies[0].wait()
+    for line in range(lines):
+        row = counters_here[pl.ds(chip * lines + line, 1), :]
+        row = lax.rsqrt(row.astype(jnp.float32) + 1.0)
+        inverse[line * 128 : (line + 1) * 128, :] = jnp.broadcast_to(row, (128, 128)).T
+    copies[1].wait()
+
+
+def cells_call(centroids, counters, rows):
+    counters = counters.reshape(-1, 128)
+    return pl.pallas_call(
+        cells_kernel,
+        in_specs=[pl.BlockSpec(memory_space=pltpu.HBM)] * 2,
+        out_specs=in_vmem(2),
+        out_shape=[
+            jax.ShapeDtypeStruct((rows, centroids.shape[1]), jnp.bfloat16),
+            jax.ShapeDtypeStruct((rows, 128), jnp.float32),
+        ],
+        scratch_shapes=[pltpu.VMEM(counters.shape, counters.dtype), pltpu.SemaphoreType.DMA((2,))],
+        compiler_params=pltpu.CompilerParams(vmem_limit_bytes=VMEM_BYTES),
+    )(centroids, counters)
+
+
 def hold(a, after):
     def kernel(a, after, out):
         out[...] = a[...]
@@ -67,11 +100,13 @@
     )(a, after)
 
 
-def expo_kernel(rate, block, place, *refs):
+def expo_kernel(rate, block, *refs):
     pieces, (cells, inverse, expo, tops, stats, points) = refs[:4], refs[4:]
     rows = pieces[0].shape[0]
-    for at, piece in enumerate(pieces):
-        points[pl.ds(pl.multiple_of(place[at] * rows, rows), rows), :] = piece[...]
+    chip = lax.axis_index("y") * 2 + lax.axis_index("x")
+    lo = lax.axis_index("lo")
+    for away, piece in zip((0, 1 + lo, 2 - lo, 3), pieces):
+        points[pl.ds(pl.multiple_of((chip ^ away) * rows, rows), rows), :] = piece[...]
     every = points[...]
     highest = total = novel = None
     for at in range(cells.shape[0] // block):
@@ -100,12 +135,12 @@
     stats[...] = jnp.concatenate([highest, total, novel], axis=0)
 
 
-def expo_call(rate, block, place, pieces, cells, inverse):
+def expo_call(rate, block, pieces, cells, inverse):
     count, width = cells.shape
     n_points = sum(piece.shape[0] for piece in pieces)
     return pl.pallas_call(
         functools.partial(expo_kernel, rate, block),
-        in_specs=[pl.BlockSpec(memory_space=pltpu.SMEM)] + in_vmem(6),
+        in_specs=in_vmem(6),
         out_specs=in_vmem(4),
         out_shape=[
             jax.ShapeDtypeStruct((count, n_points), jnp.bfloat16),
@@ -119,7 +154,7 @@
             bytes_accessed=2 * (count * width + n_points * width + count * n_points),
             transcendentals=count * n_points,
         ),
-    )(place, *pieces, cells, inverse)
+    )(*pieces, cells, inverse)
 
 
 def weighed_sums(at, count, expos, points, factor):
@@ -135,19 +170,23 @@
     return total, jnp.sum(weight.T, axis=0, keepdims=True)
 
 
-def sums_kernel(n, block, half, *refs):
+def first_block(side, blocks):
+    return (lax.axis_index("lo") ^ side) * blocks
+
+
+def sums_kernel(n, block, first, *refs):
     expos, points, factor, (sums, mass) = refs[:n], refs[n : 2 * n], refs[2 * n], refs[2 * n + 1 :]
     factor = [factor.at[at] for at in range(n)]
 
     @pl.loop(0, sums.shape[0] // block)
     def _(at):
         here = pl.ds(pl.multiple_of(at * block, block), block)
-        total, weight = weighed_sums(half[0] + at, block, expos, points, factor)
+        total, weight = weighed_sums(first() + at, block, expos, points, factor)
         sums[here, :] = total.astype(sums.dtype)
         mass[:, here] = weight
 
 
-def last_kernel(n, block, half, *refs):
+def last_kernel(n, block, first, *refs):
     expos, points, factor = refs[:n], refs[n : 2 * n], refs[2 * n]
     early, early_mass, there, there_mass, sums, mass, out, left = refs[2 * n + 1 :]
     factor = [factor.at[at] for at in range(n)]
@@ -165,7 +204,7 @@
         if at * block < skip:
             total = early[here, :]
         else:
-            total, weight = weighed_sums(half[0] + at, block, expos, points, factor)
+            total, weight = weighed_sums(first() + at, block, expos, points, factor)
             mass[:, here] = weight + there_mass[:, here]
         out[at % 2] = total + there[here, :].astype(jnp.float32)
         copy(at).start()
@@ -173,13 +212,13 @@
         copy(at).wait()
 
 
-def sums_call(kernel, block, rows, dtype, half, expos, points, factor, *more):
+def sums_call(kernel, block, side, rows, dtype, expos, points, factor, *more):
     n, last = len(expos), kernel is last_kernel
     n_points, width = points[0].shape
     work = rows - more[0].shape[0] if last else rows
     return pl.pallas_call(
-        functools.partial(kernel, n, block),
-        in_specs=[pl.BlockSpec(memory_space=pltpu.SMEM)] + in_vmem(2 * n + 1 + len(more)),
+        functools.partial(kernel, n, block, functools.partial(first_block, side, expos[0].shape[0] // 2 // block)),
+        in_specs=in_vmem(2 * n + 1 + len(more)),
         out_specs=[pl.BlockSpec(memory_space=pltpu.HBM if last else pltpu.VMEM)] + in_vmem(1),
         out_shape=[jax.ShapeDtypeStruct((rows, width), dtype), jax.ShapeDtypeStruct((1, rows), jnp.float32)],
         scratch_shapes=[pltpu.VMEM((2, block, width), dtype), pltpu.SemaphoreType.DMA((2,))] if last else [],
@@ -189,28 +228,18 @@
             bytes_accessed=2 * n * n_points * (work + width) + 4 * rows * width,
             transcendentals=0,
         ),
-    )(half, *expos, *points, factor, *more)
+    )(*expos, *points, factor, *more)
 
 
 def merge(rate, stats):
-    top = jnp.max(stats[:, 0], axis=0)
-    scale = jnp.exp2((stats[:, 0] - top) * rate)
-    return jnp.stack([top, jnp.sum(stats[:, 1] * scale, axis=0), jnp.sum(stats[:, 2] * scale, axis=0)])
-
-
-def everyone(a, axes):
-    count = math.prod(lax.axis_size(axis) for axis in axes)
-    return lax.all_to_all(jnp.broadcast_to(a, (count, *a.shape)), axes, 0, 0)
-
-
-def shuffle(a, by):
-    a = jnp.where(by & 1, jnp.stack([a[:, d ^ 1] for d in range(4)], axis=1), a)
-    return jnp.where(by & 2, jnp.stack([a[:, d ^ 2] for d in range(4)], axis=1), a)
+    top = functools.reduce(jnp.maximum, [s[0] for s in stats])
+    scales = [jnp.exp2((s[0] - top) * rate) for s in stats]
+    total = sum(s[1] * scale for s, scale in zip(stats, scales))
+    novel = sum(s[2] * scale for s, scale in zip(stats, scales))
+    return jnp.stack([top, total, novel])
 
 
 def split_cells(codes, exponents, centroids, counters):
-    chip = lax.axis_index("y") * 2 + lax.axis_index("x")
-    lo = lax.axis_index("lo")
     own = to_points(codes, exponents)
     rate = 4.0 / math.sqrt(own.shape[1]) * math.log2(math.e)
     plane = ("y", "x", "lo")
@@ -218,37 +247,34 @@
     turn = lambda a: exchange(a, plane, lambda at: at ^ (4 if at % 2 else 2))
     turn_back = lambda a: exchange(a, plane, lambda at: at ^ (2 if at % 2 else 4))
     along_z = lambda a, by: exchange(a, ("cells",), lambda at: at ^ by)
-    place = jnp.stack([chip, chip ^ (1 + lo), chip ^ (2 - lo), chip ^ 3]).astype(jnp.int32)
 
     per_device = centroids.shape[0] // 8
     block = per_device // 3
 
-    cells, counts = (lax.dynamic_slice_in_dim(a, chip * 2 * per_device, 2 * per_device) for a in (centroids, counters))
-    inverse = lax.rsqrt(counts.astype(jnp.float32) + 1.0)
-    inverse = jnp.broadcast_to(inverse[:, None], (inverse.shape[0], 128))
-
+    cells, inverse = cells_call(centroids, counters, 2 * per_device)
     nears = [own] + [along_z(own, by) for by in (1, 2, 3)]
     expos, tops, stats, points = [], [], [], []
     for step, near in enumerate(nears):
         first, second = turn(near), turn_back(near)
         across = turn_back(hold(first, stats[step // 2]) if step % 2 else first)
-        expo, top, stat, chunk = expo_call(rate, block, place, (near, first, second, across), cells, inverse)
+        expo, top, stat, chunk = expo_call(rate, block, (near, first, second, across), cells, inverse)
         expos.append(expo), tops.append(top), stats.append(stat), points.append(chunk)
 
-    z = lax.axis_index("cells")
-    stat = shuffle(jnp.stack(stats, axis=1), z)
-    for axes in (("y", "x"), ("cells",)):
-        stat = merge(rate, everyone(stat, axes))
-    stat = shuffle(stat, z)
+    stat = jnp.stack(stats, axis=1)
+    stat = merge(rate, [stat] + [exchange(stat, ("y", "x"), lambda at: at ^ by) for by in (1, 2, 3)])
+    every = [stat]
+    for by in (1, 2, 3):
+        theirs = along_z(stat, by)
+        every.append(jnp.stack([theirs[:, step ^ by] for step in range(4)], axis=1))
+    stat = merge(rate, every)
     factor = jnp.exp2((jnp.stack(tops) - stat[0][:, None]) * rate) * (stat[2] / stat[1] / stat[1])[:, None]
 
-    other, mine = ((a * jnp.full((1,), per_device // block)).astype(jnp.int32) for a in (1 - lo, lo))
     parts = (expos, points, factor)
-    there, there_mass = sums_call(sums_kernel, block, per_device, jnp.bfloat16, other, *parts)
+    there, there_mass = sums_call(sums_kernel, block, 1, per_device, jnp.bfloat16, *parts)
     there, there_mass = (exchange(a, ("lo",), lambda at: at ^ 1) for a in (there, there_mass))
-    early, early_mass = sums_call(sums_kernel, block, 2 * block, jnp.float32, mine, *parts)
+    early, early_mass = sums_call(sums_kernel, block, 0, 2 * block, jnp.float32, *parts)
     out, mass = sums_call(
-        last_kernel, block, per_device, jnp.float32, mine, *parts, early, early_mass, there, there_mass
+        last_kernel, block, 0, per_device, jnp.float32, *parts, early, early_mass, there, there_mass
     )
     return (out[None], mass)
 

time: 94 us -> 59.9 us (0.64)
  local copies, waits for them, and re-layouts: 29.8 us -> 3.59 us
  blocking collectives: 8.08 us -> 0 us
  starting transfers between devices: 23.7 us -> 31 us
  Pallas kernels: 18.9 us -> 13.8 us
  other arithmetic: 2.86 us -> 1.91 us
    unnamed x59 -> x4, local copies, waits for them, and re-layouts: 27.3 us -> 3.52 us
    ppermute x17 -> x23, starting transfers between devices: 19.7 us -> 31 us  [exchange(): return lax.ppermute(a, axes, [(partner(at), at) for at in range(count)])]
    all_to_all x1 -> x0, blocking collectives: 8.08 us -> none  [everyone(): return lax.all_to_all(jnp.broadcast_to(a, (count, *a.shape)), axes, 0, 0)]
    ppermute x17 -> x23, waiting for transfers between devices: 2.68 us -> 8.63 us  [exchange(): return lax.ppermute(a, axes, [(partner(at), at) for at in range(count)])]
    all_to_all x1 -> x0, waiting for transfers between devices: 5.83 us -> none  [everyone(): return lax.all_to_all(jnp.broadcast_to(a, (count, *a.shape)), axes, 0, 0)]
    pallas_call x7 -> x8, Pallas kernels: 18.9 us -> 13.7 us  [the longest x4 6.78 us: expo_call(): pl.pallas_call(functools.partial(expo_kernel, rate, block), in_specs=in_v...]
    all_to_all x1 -> x0, starting transfers between devices: 4.02 us -> none  [everyone(): return lax.all_to_all(jnp.broadcast_to(a, (count, *a.shape)), axes, 0, 0)]
    dynamic_slice x1 -> x0, local copies, waits for them, and re-layouts: 1.51 us -> none  [split_cells(): lax.dynamic_slice_in_dim(a, chip * 2 * per_device, 2 * per_device)]
  transfers between devices with their start and end apart: 18 -> 23, of which waited for: 4 -> 10; matrix products, arithmetic and copies ran while one was open for 3% -> 0% of each run, Pallas kernels for 10% -> 12%
where the time goes in v6:
time: 59.9 us; the launch traced here: 59.7 us
  starting transfers between devices  31 us (52%)
  Pallas kernels  13.8 us (23%)
  waiting for transfers between devices  8.63 us (14%)
  local copies, waits for them, and re-layouts  3.59 us (6%)
  other arithmetic  1.91 us (3%)
  between operations  0.8 us (1%)
    ppermute x23, starting transfers between devices, exchange(): return lax.ppermute(a, axes, [(partner(at), at) for at in range(count)])  31 us
    ppermute x23, waiting for transfers between devices, exchange(): return lax.ppermute(a, axes, [(partner(at), at) for at in range(count)])  8.63 us
    pallas_call x4, Pallas kernels, expo_call(): pl.pallas_call(functools.partial(expo_kernel, rate, block), in_specs=in_v...  6.78 us
    pallas_call x3, Pallas kernels, sums_call(): pl.pallas_call(functools.partial(kernel, n, block, functools.partial(firs...  6.54 us
    unnamed x4, local copies, waits for them, and re-layouts  3.52 us
  transfers between devices with their start and end apart: 23, of which 10 were waited for; matrix products, arithmetic and copies ran while one was open for 0% of the time, Pallas kernels for 12%

profile of v6, /device:TPU:0, one launch (start us, length us, event | category | flops | bytes accessed | tf_op | source)
XLA Modules:
  0.0 59.7 jit_solution(7090142480424205895)
XLA Ops:
  0.6 0.7 %convert_multiply_fusion = f32[128]{0:T(128)S(1)} fusion(s32[128]{0:T(128)} %param.5), kind=kLoop, calls=%fused_computation.80 | loop fusion | flops 512 | bytes 1024 | tf_op jit(solution)/shard_map/mul | solution.py:17
  1.3 1.0 %multiply_convert_fusion.refs_0_ = bf16[128,512]{1,0:T(8,128)(2,1)S(1)} fusion(s32[128,512]{1,0:T(8,128)} %param.4, f32[128]{0:T(128)S(1)} %convert_multiply_fusion), kind=kLoop, calls=%fused_computation | loop fusion | flops 196608 | bytes 393728 | tf_op jit(solution)/shard_map/convert_element_type | solution.py:18
  2.3 3.0 %collective-permute-start = (bf16[128,512]{1,0:T(8,128)(2,1)S(1)}, bf16[128,512]{1,0:T(8,128)(2,1)S(1)}, u32[]{:S(2)}, u32[]{:S(2)}) collective-permute-start(bf16[128,512]{1,0:T(8,128)(2,1)S(1)} %multiply_convert_fusion.refs_0_), channel_id=1, source_target_pairs={{8,0},{20,4},{0,8},{28,12},{24,16},{4,20},{16,24},{12,28},{9,1},{2... | collective-permute-start | bytes 393224 | tf_op jit(solution)/shard_map/ppermute | solution.py:50
  5.3 1.6 %collective-permute-start.3 = (bf16[128,512]{1,0:T(8,128)(2,1)S(1)}, bf16[128,512]{1,0:T(8,128)(2,1)S(1)}, u32[]{:S(2)}, u32[]{:S(2)}) collective-permute-start(bf16[128,512]{1,0:T(8,128)(2,1)S(1)} %multiply_convert_fusion.refs_0_), channel_id=1, source_target_pairs={{1,0},{0,1},{3,2},{2,3},{5,4},{4,5},{7,6},{6,7},{9,8},{8,9},{11,10... | collective-permute-start | bytes 393224 | tf_op jit(solution)/shard_map/ppermute | solution.py:50
  6.9 2.6 %collective-permute-start.7 = (bf16[128,512]{1,0:T(8,128)(2,1)S(1)}, bf16[128,512]{1,0:T(8,128)(2,1)S(1)}, u32[]{:S(2)}, u32[]{:S(2)}) collective-permute-start(bf16[128,512]{1,0:T(8,128)(2,1)S(1)} %multiply_convert_fusion.refs_0_), channel_id=1, source_target_pairs={{2,0},{3,1},{0,2},{1,3},{6,4},{7,5},{4,6},{5,7},{10,8},{11,9},{8,1... | collective-permute-start | bytes 393224 | tf_op jit(solution)/shard_map/ppermute | solution.py:50
  9.5 1.5 %collective-permute-start.1 = (bf16[128,512]{1,0:T(8,128)(2,1)S(1)}, bf16[128,512]{1,0:T(8,128)(2,1)S(1)}, u32[]{:S(2)}, u32[]{:S(2)}) collective-permute-start(bf16[128,512]{1,0:T(8,128)(2,1)S(1)} %multiply_convert_fusion.refs_0_), channel_id=1, source_target_pairs={{16,0},{12,4},{24,8},{4,12},{0,16},{28,20},{8,24},{20,28},{17,1},{... | collective-permute-start | bytes 393224 | tf_op jit(solution)/shard_map/ppermute | solution.py:50
  11.0 0.0 collective-permute-done.refs_1_
  11.0 0.5 collective-permute-start.2
  11.5 0.5 collective-permute-done.3.refs_0_
  12.0 2.4 %collective-permute-start.4 = (bf16[128,512]{1,0:T(8,128)(2,1)S(1)}, bf16[128,512]{1,0:T(8,128)(2,1)S(1)}, u32[]{:S(2)}, u32[]{:S(2)}) collective-permute-start(bf16[128,512]{1,0:T(8,128)(2,1)S(1)} %collective-permute-done.3.refs_0_), channel_id=1, source_target_pairs={{8,0},{20,4},{0,8},{28,12},{24,16},{4,20},{16,24},{12,28},{9,1},{2... | collective-permute-start | bytes 393224 | tf_op jit(solution)/shard_map/ppermute | solution.py:50
  14.5 2.5 %collective-permute-start.11 = (bf16[128,512]{1,0:T(8,128)(2,1)S(1)}, bf16[128,512]{1,0:T(8,128)(2,1)S(1)}, u32[]{:S(2)}, u32[]{:S(2)}) collective-permute-start(bf16[128,512]{1,0:T(8,128)(2,1)S(1)} %multiply_convert_fusion.refs_0_), channel_id=1, source_target_pairs={{3,0},{2,1},{1,2},{0,3},{7,4},{6,5},{5,6},{4,7},{11,8},{10,9},{9,1... | collective-permute-start | bytes 393224 | tf_op jit(solution)/shard_map/ppermute | solution.py:50
  17.0 0.0 copy-start
  17.0 2.8 %copy-done = bf16[6144,512]{1,0:T(8,128)(2,1)S(1)} copy-done((bf16[6144,512]{1,0:T(8,128)(2,1)S(1)}, bf16[6144,512]{1,0:T(8,128)(2,1)}, u32[]{:S(2)}) %copy-start) | copy-done | bytes 6291480
  19.8 0.0 copy-start.1
  19.8 0.7 %copy-done.1 = s32[6144]{0:T(1024)S(1)} copy-done((s32[6144]{0:T(1024)S(1)}, s32[6144]{0:T(1024)}, u32[]{:S(2)}) %copy-start.1) | copy-done | bytes 24600
  20.5 0.4 shard_map.59
  20.9 0.0 collective-permute-done.7.refs_0_
  20.9 0.5 collective-permute-start.5
  21.4 0.0 collective-permute-done.1.refs_2_
  21.5 0.9 %collective-permute-start.8 = (bf16[128,512]{1,0:T(8,128)(2,1)S(1)}, bf16[128,512]{1,0:T(8,128)(2,1)S(1)}, u32[]{:S(2)}, u32[]{:S(2)}) collective-permute-start(bf16[128,512]{1,0:T(8,128)(2,1)S(1)} %collective-permute-done.7.refs_0_), channel_id=1, source_target_pairs={{8,0},{20,4},{0,8},{28,12},{24,16},{4,20},{16,24},{12,28},{9,1},{2... | collective-permute-start | bytes 393224 | tf_op jit(solution)/shard_map/ppermute | solution.py:50
  22.3 0.0 collective-permute-done.2.refs_3_
  22.3 1.7 %shard_map.60 = (bf16[1536,512]{1,0:T(8,128)(2,1)S(1)}, f32[6,512]{1,0:T(8,128)S(1)}, f32[3,512]{1,0:T(4,128)S(1)}, bf16[512,512]{1,0:T(8,128)(2,1)S(1)}) custom-call(bf16[128,512]{1,0:T(8,128)(2,1)S(1)} %multiply_convert_fusion.refs_0_, bf16[128,512]{1,0:T(8,128)(2,1)S(1)} %collective-permute-done.refs_1_, ...), custom_call_target="tpu_custom_call" | custom-call | flops 805306368 | bytes 3670016 | tf_op jit(solution)/shard_map/pallas_call | solution.py:141
  24.0 0.0 collective-permute-done.4.a.refs_1_
  24.1 1.2 %collective-permute-start.6 = (bf16[128,512]{1,0:T(8,128)(2,1)S(1)}, bf16[128,512]{1,0:T(8,128)(2,1)S(1)}, u32[]{:S(2)}, u32[]{:S(2)}) collective-permute-start(bf16[128,512]{1,0:T(8,128)(2,1)S(1)} %shard_map.61), channel_id=1, source_target_pairs={{16,0},{12,4},{24,8},{4,12},{0,16},{28,20},{8,24},{20,28},{17,1},{... | collective-permute-start | bytes 393224 | tf_op jit(solution)/shard_map/ppermute | solution.py:50
  25.3 0.0 collective-permute-done.11.refs_0_
  25.3 1.6 %collective-permute-start.12 = (bf16[128,512]{1,0:T(8,128)(2,1)S(1)}, bf16[128,512]{1,0:T(8,128)(2,1)S(1)}, u32[]{:S(2)}, u32[]{:S(2)}) collective-permute-start(bf16[128,512]{1,0:T(8,128)(2,1)S(1)} %collective-permute-done.11.refs_0_), channel_id=1, source_target_pairs={{8,0},{20,4},{0,8},{28,12},{24,16},{4,20},{16,24},{12,28},{9,1},{2... | collective-permute-start | bytes 393224 | tf_op jit(solution)/shard_map/ppermute | solution.py:50
  26.9 0.4 collective-permute-start.13
  27.3 0.0 collective-permute-done.8.refs_1_
  27.3 2.1 %collective-permute-start.9 = (bf16[128,512]{1,0:T(8,128)(2,1)S(1)}, bf16[128,512]{1,0:T(8,128)(2,1)S(1)}, u32[]{:S(2)}, u32[]{:S(2)}) collective-permute-start(bf16[128,512]{1,0:T(8,128)(2,1)S(1)} %collective-permute-done.7.refs_0_), channel_id=1, source_target_pairs={{16,0},{12,4},{24,8},{4,12},{0,16},{28,20},{8,24},{20,28},{17,1},{... | collective-permute-start | bytes 393224 | tf_op jit(solution)/shard_map/ppermute | solution.py:50
  29.4 0.0 collective-permute-done.5.refs_2_
  29.4 0.0 collective-permute-start.10
  29.4 0.0 collective-permute-done.6.refs_3_
  29.4 1.7 %shard_map.62 = (bf16[1536,512]{1,0:T(8,128)(2,1)S(1)}, f32[6,512]{1,0:T(8,128)S(1)}, f32[3,512]{1,0:T(4,128)S(1)}, bf16[512,512]{1,0:T(8,128)(2,1)S(1)}) custom-call(bf16[128,512]{1,0:T(8,128)(2,1)S(1)} %collective-permute-done.3.refs_0_, bf16[128,512]{1,0:T(8,128)(2,1)S(1)} %collective-permute-done.4.a.refs_1_, ...), custom_call_target="tpu_custom_call" | custom-call | flops 805306368 | bytes 3670016 | tf_op jit(solution)/shard_map/pallas_call | solution.py:141
  31.1 0.6 collective-permute-done.12.a.refs_1_
  31.7 1.5 %collective-permute-start.14 = (bf16[128,512]{1,0:T(8,128)(2,1)S(1)}, bf16[128,512]{1,0:T(8,128)(2,1)S(1)}, u32[]{:S(2)}, u32[]{:S(2)}) collective-permute-start(bf16[128,512]{1,0:T(8,128)(2,1)S(1)} %shard_map.64), channel_id=1, source_target_pairs={{16,0},{12,4},{24,8},{4,12},{0,16},{28,20},{8,24},{20,28},{17,1},{... | collective-permute-start | bytes 393224 | tf_op jit(solution)/shard_map/ppermute | solution.py:50
  33.2 0.0 collective-permute-done.9.refs_2_
  33.2 1.4 %collective-permute-done.10.refs_3_ = bf16[128,512]{1,0:T(8,128)(2,1)S(1)} collective-permute-done((bf16[128,512]{1,0:T(8,128)(2,1)S(1)}, bf16[128,512]{1,0:T(8,128)(2,1)S(1)}, u32[]{:S(2)}, u32[]{:S(2)}) %collective-permute-start.10) | collective-permute-done | bytes 131104 | tf_op jit(solution)/shard_map/ppermute | solution.py:50
  34.6 1.7 %shard_map.63 = (bf16[1536,512]{1,0:T(8,128)(2,1)S(1)}, f32[6,512]{1,0:T(8,128)S(1)}, f32[3,512]{1,0:T(4,128)S(1)}, bf16[512,512]{1,0:T(8,128)(2,1)S(1)}) custom-call(bf16[128,512]{1,0:T(8,128)(2,1)S(1)} %collective-permute-done.7.refs_0_, bf16[128,512]{1,0:T(8,128)(2,1)S(1)} %collective-permute-done.8.refs_1_, ...), custom_call_target="tpu_custom_call" | custom-call | flops 805306368 | bytes 3670016 | tf_op jit(solution)/shard_map/pallas_call | solution.py:141
  36.3 0.0 collective-permute-done.13.refs_2_
  36.3 0.4 collective-permute-done.14.refs_3_
  36.8 1.7 %shard_map.65 = (bf16[1536,512]{1,0:T(8,128)(2,1)S(1)}, f32[6,512]{1,0:T(8,128)S(1)}, f32[3,512]{1,0:T(4,128)S(1)}, bf16[512,512]{1,0:T(8,128)(2,1)S(1)}) custom-call(bf16[128,512]{1,0:T(8,128)(2,1)S(1)} %collective-permute-done.11.refs_0_, bf16[128,512]{1,0:T(8,128)(2,1)S(1)} %collective-permute-done.12.a.refs_1_, ...), custom_call_target="tpu_custom_call" | custom-call | flops 805306368 | bytes 3670016 | tf_op jit(solution)/shard_map/pallas_call | solution.py:141
  38.5 1.5 %collective-permute-start.17 = (f32[3,4,512]{2,1,0:T(4,128)S(1)}, f32[3,4,512]{2,1,0:T(4,128)S(1)}, u32[]{:S(2)}, u32[]{:S(2)}) collective-permute-start(f32[3,4,512]{2,1,0:T(4,128)S(1)} %copy.6), channel_id=1, source_target_pairs={{24,0},{16,8},{8,16},{0,24},{25,1},{17,9},{9,17},{1,25},{26,2},{18... | collective-permute-start | bytes 73736 | tf_op jit(solution)/shard_map/ppermute | solution.py:50
  40.0 1.6 %collective-permute-start.16 = (f32[3,4,512]{2,1,0:T(4,128)S(1)}, f32[3,4,512]{2,1,0:T(4,128)S(1)}, u32[]{:S(2)}, u32[]{:S(2)}) collective-permute-start(f32[3,4,512]{2,1,0:T(4,128)S(1)} %copy.6), channel_id=1, source_target_pairs={{16,0},{24,8},{0,16},{8,24},{17,1},{25,9},{1,17},{9,25},{18,2},{26... | collective-permute-start | bytes 73736 | tf_op jit(solution)/shard_map/ppermute | solution.py:50
  41.6 0.4 collective-permute-start.15
  42.1 1.2 %collective-permute-done.17 = f32[3,4,512]{2,1,0:T(4,128)S(1)} collective-permute-done((f32[3,4,512]{2,1,0:T(4,128)S(1)}, f32[3,4,512]{2,1,0:T(4,128)S(1)}, u32[]{:S(2)}, u32[]{:S(2)}) %collective-permute-start.17) | collective-permute-done | bytes 24608 | tf_op jit(solution)/shard_map/ppermute | solution.py:50
  43.3 0.5 collective-permute-done.16
  43.8 1.6 %collective-permute-done.15 = f32[3,4,512]{2,1,0:T(4,128)S(1)} collective-permute-done((f32[3,4,512]{2,1,0:T(4,128)S(1)}, f32[3,4,512]{2,1,0:T(4,128)S(1)}, u32[]{:S(2)}, u32[]{:S(2)}) %collective-permute-start.15) | collective-permute-done | bytes 24608 | tf_op jit(solution)/shard_map/ppermute | solution.py:50
  45.5 1.4 %collective-permute-start.20 = (f32[3,4,512]{2,1,0:T(4,128)S(1)}, f32[3,4,512]{2,1,0:T(4,128)S(1)}, u32[]{:S(2)}, u32[]{:S(2)}) collective-permute-start(f32[3,4,512]{2,1,0:T(4,128)S(1)} %pad_maximum_fusion.1), channel_id=1, source_target_pairs={{3,0},{2,1},{1,2},{0,3},{7,4},{6,5},{5,6},{4,7},{11,8},{10,9},{9,1... | collective-permute-start | bytes 73736 | tf_op jit(solution)/shard_map/ppermute | solution.py:50
  46.9 0.0 collective-permute-start.19
  46.9 3.1 %collective-permute-start.18 = (f32[3,4,512]{2,1,0:T(4,128)S(1)}, f32[3,4,512]{2,1,0:T(4,128)S(1)}, u32[]{:S(2)}, u32[]{:S(2)}) collective-permute-start(f32[3,4,512]{2,1,0:T(4,128)S(1)} %pad_maximum_fusion.1), channel_id=1, source_target_pairs={{1,0},{0,1},{3,2},{2,3},{5,4},{4,5},{7,6},{6,7},{9,8},{8,9},{11,10... | collective-permute-start | bytes 73736 | tf_op jit(solution)/shard_map/ppermute | solution.py:50
  50.0 1.2 %collective-permute-done.20 = f32[3,4,512]{2,1,0:T(4,128)S(1)} collective-permute-done((f32[3,4,512]{2,1,0:T(4,128)S(1)}, f32[3,4,512]{2,1,0:T(4,128)S(1)}, u32[]{:S(2)}, u32[]{:S(2)}) %collective-permute-start.20) | collective-permute-done | bytes 24608 | tf_op jit(solution)/shard_map/ppermute | solution.py:50
  51.2 0.8 %collective-permute-done.18 = f32[3,4,512]{2,1,0:T(4,128)S(1)} collective-permute-done((f32[3,4,512]{2,1,0:T(4,128)S(1)}, f32[3,4,512]{2,1,0:T(4,128)S(1)}, u32[]{:S(2)}, u32[]{:S(2)}) %collective-permute-start.18) | collective-permute-done | bytes 24608 | tf_op jit(solution)/shard_map/ppermute | solution.py:50
  52.0 0.1 pad_maximum_fusion.2
  52.1 0.0 collective-permute-done.19
  52.1 0.1 fusion.8
  52.2 2.2 %shard_map.67 = (bf16[768,512]{1,0:T(8,128)(2,1)S(1)}, f32[1,768]{1,0:T(1,128)S(1)}) custom-call(bf16[1536,512]{1,0:T(8,128)(2,1)S(1)} %get-tuple-element.28.refs_0_, bf16[1536,512]{1,0:T(8,128)(2,1)S(1)} %get-tuple-element.30.refs_1_, bf16[1536,512]{1,0:T(8,128)(2,1)S(1)} %get-tuple-element.31.refs_2_, bf16[1536,512]{1,0:T(8,128)(2,1)S(1)} %get-tuple-element.33.refs_3_, ...), custom_call_target="tpu_custom_call" | custom-call | flops 1610612736 | bytes 6815744 | tf_op jit(solution)/shard_map/pallas_call | solution.py:219
  54.4 0.1 collective-permute-start.21
  54.4 0.5 collective-permute-start.22
  54.9 1.4 %shard_map.66 = (f32[512,512]{1,0:T(8,128)S(1)}, f32[1,512]{1,0:T(1,128)S(1)}) custom-call(bf16[1536,512]{1,0:T(8,128)(2,1)S(1)} %get-tuple-element.28.refs_0_, bf16[1536,512]{1,0:T(8,128)(2,1)S(1)} %get-tuple-element.30.refs_1_, bf16[1536,512]{1,0:T(8,128)(2,1)S(1)} %get-tuple-element.31.refs_2_, bf16[1536,512]{1,0:T(8,128)(2,1)S(1)} %get-tuple-element.33.refs_3_, ...), custom_call_target="tpu_custom_call" | custom-call | flops 1073741824 | bytes 5242880 | tf_op jit(solution)/shard_map/pallas_call | solution.py:219
  56.4 0.3 collective-permute-done.22.refs_12_
  56.7 0.0 collective-permute-done.21.refs_11_
  56.7 2.9 %shard_map.68 = (f32[768,512]{1,0:T(8,128)}, f32[1,768]{1,0:T(1,128)}) custom-call(bf16[1536,512]{1,0:T(8,128)(2,1)S(1)} %get-tuple-element.28.refs_0_, bf16[1536,512]{1,0:T(8,128)(2,1)S(1)} %get-tuple-element.30.refs_1_, bf16[1536,512]{1,0:T(8,128)(2,1)S(1)} %get-tuple-element.31.refs_2_, bf16[1536,512]{1,0:T(8,128)(2,1)S(1)} %get-tuple-element.33.refs_3_, ...), custom_call_target="tpu_custom_call" | custom-call | flops 536870912 | bytes 4718592 | tf_op jit(solution)/shard_map/pallas_call | solution.py:219
  (12 shorter events, 0.2 us)
Async XLA Ops:
  2.3 8.7 %collective-permute-start = (bf16[128,512]{1,0:T(8,128)(2,1)S(1)}, bf16[128,512]{1,0:T(8,128)(2,1)S(1)}, u32[]{:S(2)}, u32[]{:S(2)}) collective-permute-start(bf16[128,512]{1,0:T(8,128)(2,1)S(1)} %multiply_convert_fusion.refs_0_), channel_id=1, source_target_pairs={{8,0},{20,4},{0,8},{28,12},{24,16},{4,20},{16,24},{12,28},{9,1},{2... | collective-permute-start | bytes 393224 | tf_op jit(solution)/shard_map/ppermute | solution.py:50
  5.3 6.7 %collective-permute-start.3 = (bf16[128,512]{1,0:T(8,128)(2,1)S(1)}, bf16[128,512]{1,0:T(8,128)(2,1)S(1)}, u32[]{:S(2)}, u32[]{:S(2)}) collective-permute-start(bf16[128,512]{1,0:T(8,128)(2,1)S(1)} %multiply_convert_fusion.refs_0_), channel_id=1, source_target_pairs={{1,0},{0,1},{3,2},{2,3},{5,4},{4,5},{7,6},{6,7},{9,8},{8,9},{11,10... | collective-permute-start | bytes 393224 | tf_op jit(solution)/shard_map/ppermute | solution.py:50
  6.9 14.0 %collective-permute-start.7 = (bf16[128,512]{1,0:T(8,128)(2,1)S(1)}, bf16[128,512]{1,0:T(8,128)(2,1)S(1)}, u32[]{:S(2)}, u32[]{:S(2)}) collective-permute-start(bf16[128,512]{1,0:T(8,128)(2,1)S(1)} %multiply_convert_fusion.refs_0_), channel_id=1, source_target_pairs={{2,0},{3,1},{0,2},{1,3},{6,4},{7,5},{4,6},{5,7},{10,8},{11,9},{8,1... | collective-permute-start | bytes 393224 | tf_op jit(solution)/shard_map/ppermute | solution.py:50
  9.5 11.9 %collective-permute-start.1 = (bf16[128,512]{1,0:T(8,128)(2,1)S(1)}, bf16[128,512]{1,0:T(8,128)(2,1)S(1)}, u32[]{:S(2)}, u32[]{:S(2)}) collective-permute-start(bf16[128,512]{1,0:T(8,128)(2,1)S(1)} %multiply_convert_fusion.refs_0_), channel_id=1, source_target_pairs={{16,0},{12,4},{24,8},{4,12},{0,16},{28,20},{8,24},{20,28},{17,1},{... | collective-permute-start | bytes 393224 | tf_op jit(solution)/shard_map/ppermute | solution.py:50
  11.0 11.3 %collective-permute-start.2 = (bf16[128,512]{1,0:T(8,128)(2,1)S(1)}, bf16[128,512]{1,0:T(8,128)(2,1)S(1)}, u32[]{:S(2)}, u32[]{:S(2)}) collective-permute-start(bf16[128,512]{1,0:T(8,128)(2,1)S(1)} %collective-permute-done.refs_1_), channel_id=1, source_target_pairs={{16,0},{12,4},{24,8},{4,12},{0,16},{28,20},{8,24},{20,28},{17,1},{... | collective-permute-start | bytes 393224 | tf_op jit(solution)/shard_map/ppermute | solution.py:50
  12.0 12.0 %collective-permute-start.4 = (bf16[128,512]{1,0:T(8,128)(2,1)S(1)}, bf16[128,512]{1,0:T(8,128)(2,1)S(1)}, u32[]{:S(2)}, u32[]{:S(2)}) collective-permute-start(bf16[128,512]{1,0:T(8,128)(2,1)S(1)} %collective-permute-done.3.refs_0_), channel_id=1, source_target_pairs={{8,0},{20,4},{0,8},{28,12},{24,16},{4,20},{16,24},{12,28},{9,1},{2... | collective-permute-start | bytes 393224 | tf_op jit(solution)/shard_map/ppermute | solution.py:50
  14.5 10.8 %collective-permute-start.11 = (bf16[128,512]{1,0:T(8,128)(2,1)S(1)}, bf16[128,512]{1,0:T(8,128)(2,1)S(1)}, u32[]{:S(2)}, u32[]{:S(2)}) collective-permute-start(bf16[128,512]{1,0:T(8,128)(2,1)S(1)} %multiply_convert_fusion.refs_0_), channel_id=1, source_target_pairs={{3,0},{2,1},{1,2},{0,3},{7,4},{6,5},{5,6},{4,7},{11,8},{10,9},{9,1... | collective-permute-start | bytes 393224 | tf_op jit(solution)/shard_map/ppermute | solution.py:50
  17.0 2.8 %copy-start = (bf16[6144,512]{1,0:T(8,128)(2,1)S(1)}, bf16[6144,512]{1,0:T(8,128)(2,1)}, u32[]{:S(2)}) copy-start(bf16[6144,512]{1,0:T(8,128)(2,1)} %centroids.1) | copy-start | bytes 18874372
  19.8 0.7 %copy-start.1 = (s32[6144]{0:T(1024)S(1)}, s32[6144]{0:T(1024)}, u32[]{:S(2)}) copy-start(s32[6144]{0:T(1024)} %param.7) | copy-start | bytes 73732
  20.9 8.5 %collective-permute-start.5 = (bf16[128,512]{1,0:T(8,128)(2,1)S(1)}, bf16[128,512]{1,0:T(8,128)(2,1)S(1)}, u32[]{:S(2)}, u32[]{:S(2)}) collective-permute-start(bf16[128,512]{1,0:T(8,128)(2,1)S(1)} %collective-permute-done.3.refs_0_), channel_id=1, source_target_pairs={{16,0},{12,4},{24,8},{4,12},{0,16},{28,20},{8,24},{20,28},{17,1},{... | collective-permute-start | bytes 393224 | tf_op jit(solution)/shard_map/ppermute | solution.py:50
  21.5 5.9 %collective-permute-start.8 = (bf16[128,512]{1,0:T(8,128)(2,1)S(1)}, bf16[128,512]{1,0:T(8,128)(2,1)S(1)}, u32[]{:S(2)}, u32[]{:S(2)}) collective-permute-start(bf16[128,512]{1,0:T(8,128)(2,1)S(1)} %collective-permute-done.7.refs_0_), channel_id=1, source_target_pairs={{8,0},{20,4},{0,8},{28,12},{24,16},{4,20},{16,24},{12,28},{9,1},{2... | collective-permute-start | bytes 393224 | tf_op jit(solution)/shard_map/ppermute | solution.py:50
  24.1 5.4 %collective-permute-start.6 = (bf16[128,512]{1,0:T(8,128)(2,1)S(1)}, bf16[128,512]{1,0:T(8,128)(2,1)S(1)}, u32[]{:S(2)}, u32[]{:S(2)}) collective-permute-start(bf16[128,512]{1,0:T(8,128)(2,1)S(1)} %shard_map.61), channel_id=1, source_target_pairs={{16,0},{12,4},{24,8},{4,12},{0,16},{28,20},{8,24},{20,28},{17,1},{... | collective-permute-start | bytes 393224 | tf_op jit(solution)/shard_map/ppermute | solution.py:50
  25.3 6.4 %collective-permute-start.12 = (bf16[128,512]{1,0:T(8,128)(2,1)S(1)}, bf16[128,512]{1,0:T(8,128)(2,1)S(1)}, u32[]{:S(2)}, u32[]{:S(2)}) collective-permute-start(bf16[128,512]{1,0:T(8,128)(2,1)S(1)} %collective-permute-done.11.refs_0_), channel_id=1, source_target_pairs={{8,0},{20,4},{0,8},{28,12},{24,16},{4,20},{16,24},{12,28},{9,1},{2... | collective-permute-start | bytes 393224 | tf_op jit(solution)/shard_map/ppermute | solution.py:50
  26.9 9.5 %collective-permute-start.13 = (bf16[128,512]{1,0:T(8,128)(2,1)S(1)}, bf16[128,512]{1,0:T(8,128)(2,1)S(1)}, u32[]{:S(2)}, u32[]{:S(2)}) collective-permute-start(bf16[128,512]{1,0:T(8,128)(2,1)S(1)} %collective-permute-done.11.refs_0_), channel_id=1, source_target_pairs={{16,0},{12,4},{24,8},{4,12},{0,16},{28,20},{8,24},{20,28},{17,1},{... | collective-permute-start | bytes 393224 | tf_op jit(solution)/shard_map/ppermute | solution.py:50
  27.3 5.9 %collective-permute-start.9 = (bf16[128,512]{1,0:T(8,128)(2,1)S(1)}, bf16[128,512]{1,0:T(8,128)(2,1)S(1)}, u32[]{:S(2)}, u32[]{:S(2)}) collective-permute-start(bf16[128,512]{1,0:T(8,128)(2,1)S(1)} %collective-permute-done.7.refs_0_), channel_id=1, source_target_pairs={{16,0},{12,4},{24,8},{4,12},{0,16},{28,20},{8,24},{20,28},{17,1},{... | collective-permute-start | bytes 393224 | tf_op jit(solution)/shard_map/ppermute | solution.py:50
  29.4 5.2 %collective-permute-start.10 = (bf16[128,512]{1,0:T(8,128)(2,1)S(1)}, bf16[128,512]{1,0:T(8,128)(2,1)S(1)}, u32[]{:S(2)}, u32[]{:S(2)}) collective-permute-start(bf16[128,512]{1,0:T(8,128)(2,1)S(1)} %collective-permute-done.8.refs_1_), channel_id=1, source_target_pairs={{16,0},{12,4},{24,8},{4,12},{0,16},{28,20},{8,24},{20,28},{17,1},{... | collective-permute-start | bytes 393224 | tf_op jit(solution)/shard_map/ppermute | solution.py:50
  31.7 5.0 %collective-permute-start.14 = (bf16[128,512]{1,0:T(8,128)(2,1)S(1)}, bf16[128,512]{1,0:T(8,128)(2,1)S(1)}, u32[]{:S(2)}, u32[]{:S(2)}) collective-permute-start(bf16[128,512]{1,0:T(8,128)(2,1)S(1)} %shard_map.64), channel_id=1, source_target_pairs={{16,0},{12,4},{24,8},{4,12},{0,16},{28,20},{8,24},{20,28},{17,1},{... | collective-permute-start | bytes 393224 | tf_op jit(solution)/shard_map/ppermute | solution.py:50
  38.5 4.8 %collective-permute-start.17 = (f32[3,4,512]{2,1,0:T(4,128)S(1)}, f32[3,4,512]{2,1,0:T(4,128)S(1)}, u32[]{:S(2)}, u32[]{:S(2)}) collective-permute-start(f32[3,4,512]{2,1,0:T(4,128)S(1)} %copy.6), channel_id=1, source_target_pairs={{24,0},{16,8},{8,16},{0,24},{25,1},{17,9},{9,17},{1,25},{26,2},{18... | collective-permute-start | bytes 73736 | tf_op jit(solution)/shard_map/ppermute | solution.py:50
  40.0 3.8 %collective-permute-start.16 = (f32[3,4,512]{2,1,0:T(4,128)S(1)}, f32[3,4,512]{2,1,0:T(4,128)S(1)}, u32[]{:S(2)}, u32[]{:S(2)}) collective-permute-start(f32[3,4,512]{2,1,0:T(4,128)S(1)} %copy.6), channel_id=1, source_target_pairs={{16,0},{24,8},{0,16},{8,24},{17,1},{25,9},{1,17},{9,25},{18,2},{26... | collective-permute-start | bytes 73736 | tf_op jit(solution)/shard_map/ppermute | solution.py:50
  41.6 3.8 %collective-permute-start.15 = (f32[3,4,512]{2,1,0:T(4,128)S(1)}, f32[3,4,512]{2,1,0:T(4,128)S(1)}, u32[]{:S(2)}, u32[]{:S(2)}) collective-permute-start(f32[3,4,512]{2,1,0:T(4,128)S(1)} %copy.6), channel_id=1, source_target_pairs={{8,0},{0,8},{24,16},{16,24},{9,1},{1,9},{25,17},{17,25},{10,2},{2,... | collective-permute-start | bytes 73736 | tf_op jit(solution)/shard_map/ppermute | solution.py:50
  45.5 5.7 %collective-permute-start.20 = (f32[3,4,512]{2,1,0:T(4,128)S(1)}, f32[3,4,512]{2,1,0:T(4,128)S(1)}, u32[]{:S(2)}, u32[]{:S(2)}) collective-permute-start(f32[3,4,512]{2,1,0:T(4,128)S(1)} %pad_maximum_fusion.1), channel_id=1, source_target_pairs={{3,0},{2,1},{1,2},{0,3},{7,4},{6,5},{5,6},{4,7},{11,8},{10,9},{9,1... | collective-permute-start | bytes 73736 | tf_op jit(solution)/shard_map/ppermute | solution.py:50
  46.9 5.2 %collective-permute-start.19 = (f32[3,4,512]{2,1,0:T(4,128)S(1)}, f32[3,4,512]{2,1,0:T(4,128)S(1)}, u32[]{:S(2)}, u32[]{:S(2)}) collective-permute-start(f32[3,4,512]{2,1,0:T(4,128)S(1)} %pad_maximum_fusion.1), channel_id=1, source_target_pairs={{2,0},{3,1},{0,2},{1,3},{6,4},{7,5},{4,6},{5,7},{10,8},{11,9},{8,1... | collective-permute-start | bytes 73736 | tf_op jit(solution)/shard_map/ppermute | solution.py:50
  46.9 5.1 %collective-permute-start.18 = (f32[3,4,512]{2,1,0:T(4,128)S(1)}, f32[3,4,512]{2,1,0:T(4,128)S(1)}, u32[]{:S(2)}, u32[]{:S(2)}) collective-permute-start(f32[3,4,512]{2,1,0:T(4,128)S(1)} %pad_maximum_fusion.1), channel_id=1, source_target_pairs={{1,0},{0,1},{3,2},{2,3},{5,4},{4,5},{7,6},{6,7},{9,8},{8,9},{11,10... | collective-permute-start | bytes 73736 | tf_op jit(solution)/shard_map/ppermute | solution.py:50
  54.4 2.4 %collective-permute-start.21 = (bf16[768,512]{1,0:T(8,128)(2,1)S(1)}, bf16[768,512]{1,0:T(8,128)(2,1)S(1)}, u32[]{:S(2)}, u32[]{:S(2)}) collective-permute-start(bf16[768,512]{1,0:T(8,128)(2,1)S(1)} %get-tuple-element.46), channel_id=1, source_target_pairs={{4,0},{0,4},{5,1},{1,5},{6,2},{2,6},{7,3},{3,7},{12,8},{8,12},{13,... | collective-permute-start | bytes 2359304 | tf_op jit(solution)/shard_map/ppermute | solution.py:50
  54.4 2.3 %collective-permute-start.22 = (f32[1,768]{1,0:T(1,128)S(1)}, f32[1,768]{1,0:T(1,128)S(1)}, u32[]{:S(2)}, u32[]{:S(2)}) collective-permute-start(f32[1,768]{1,0:T(1,128)S(1)} %get-tuple-element.47), channel_id=1, source_target_pairs={{4,0},{0,4},{5,1},{1,5},{6,2},{2,6},{7,3},{3,7},{12,8},{8,12},{13,... | collective-permute-start | bytes 9224 | tf_op jit(solution)/shard_map/ppermute | solution.py:50

commit v7 on v5

v7 whole, which is shorter than its diff:
```python
import functools
import math

import jax
import jax.numpy as jnp
from jax import lax
from jax.experimental import pallas as pl
from jax.experimental.pallas import tpu as pltpu
from jax.sharding import Mesh, PartitionSpec as P

GATHER_BYTES = 8 << 20
VMEM_BYTES = 16 << 20
FETCH_VMEM_BYTES = 43 << 20


def to_points(codes, exponents):
    scale = lax.shift_left(jnp.ones_like(exponents), 16 - exponents).astype(jnp.float32) * 2.0**-16
    return (codes.astype(jnp.float32) * scale[:, None]).astype(jnp.bfloat16)


def split_points(codes, exponents, centroids, counters):
    local_rows = to_points(codes, exponents)
    points = lax.all_gather(local_rows, "cells", axis=0, tiled=True)
    beta = 4.0 / math.sqrt(points.shape[1])
    logits = (
        lax.dot_general(
            points, centroids, (((1,), (1,)), ((), ())), preferred_element_type=jnp.float32
        )
        * beta
    )
    inverse = lax.rsqrt(counters.astype(jnp.float32) + 1.0)
    top = lax.pmax(jnp.max(logits, axis=1), "cells")
    expo = jnp.exp(logits - top[:, None])
    total, novel = lax.psum(
        (jnp.sum(expo, axis=1), jnp.dot(expo, inverse, preferred_element_type=jnp.float32)), "cells"
    )
    weight = novel / total
    share = (expo * (weight / total)[:, None]).astype(jnp.bfloat16)
    mass_local = jnp.sum(share.astype(jnp.float32), axis=0)
    sums_local = lax.dot_general(
        share, points, (((0,), (0,)), ((), ())), preferred_element_type=jnp.float32
    )
    sums = lax.psum_scatter(sums_local, "pts", scatter_dimension=0, tiled=True)
    mass = lax.psum_scatter(mass_local, "pts", scatter_dimension=0, tiled=True)
    return (sums[None], mass[None])


def exchange(a, axes, partner):
    count = math.prod(lax.axis_size(axis) for axis in axes)
    return lax.ppermute(a, axes, [(partner(at), at) for at in range(count)])


def in_vmem(n):
    return [pl.BlockSpec(memory_space=pltpu.VMEM)] * n


def join(above, below, after):
    def kernel(above, below, after, out):
        out[: above.shape[0], :] = above[...]
        out[above.shape[0] :, :] = below[...]

    return pl.pallas_call(
        kernel,
        in_specs=in_vmem(3),
        out_specs=in_vmem(1)[0],
        out_shape=jax.ShapeDtypeStruct((above.shape[0] + below.shape[0], above.shape[1]), above.dtype),
        compiler_params=pltpu.CompilerParams(vmem_limit_bytes=VMEM_BYTES),
    )(above, below, after)


def scores(cells, points):
    return lax.dot_general(cells, points, (((1,), (1,)), ((), ())), preferred_element_type=jnp.float32)


def chip_index():
    return lax.axis_index("y") * 2 + lax.axis_index("x")


def totals_kernel(rate, block, fetch, points, cells_from, inverse_from, *refs):
    every = points[...]
    if fetch:
        cells, inverse, stats, counters, arrived = refs
    else:
        cells, inverse, (stats,) = cells_from, inverse_from, refs
    count = cells.shape[0] // block

    def copy(at):
        if at == count:
            return pltpu.make_async_copy(inverse_from, counters, arrived.at[at])
        here = pl.ds(at * block, block)
        return pltpu.make_async_copy(cells_from.at[here, :], cells.at[here, :], arrived.at[at])

    if fetch:
        for at in (count, *range(count)):
            copy(at).start()
        copy(count).wait()
    highest = total = novel = None
    for at in range(count):
        here = slice(at * block, (at + 1) * block)
        if fetch:
            for line in range(at * block // 128, (at + 1) * block // 128):
                row = lax.rsqrt(counters[line : line + 1, :].astype(jnp.float32) + 1.0)
                inverse[line * 128 : (line + 1) * 128, :] = jnp.broadcast_to(row, (128, 128)).T
            copy(at).wait()
        logits = scores(cells[here, :], every)
        top = jnp.max(logits, axis=0, keepdims=True)
        value = jnp.exp2((logits - top) * rate)
        part = jnp.sum(value, axis=0, keepdims=True)
        scale = inverse[here, :]
        weighed = jnp.concatenate(
            [
                jnp.sum(value[:, i : i + 128] * scale, axis=0, keepdims=True)
                for i in range(0, value.shape[1], 128)
            ],
            axis=1,
        )
        if at:
            higher = jnp.maximum(highest, top)
            old, new = jnp.exp2((highest - higher) * rate), jnp.exp2((top - higher) * rate)
            highest, total, novel = higher, total * old + part * new, novel * old + weighed * new
        else:
            highest, total, novel = top, part, weighed
    stats[...] = jnp.concatenate([highest, total, novel], axis=0)


def totals_call(rate, block, points, cells, inverse=None, counters=None):
    fetch = inverse is None
    n_points, width = points.shape
    n_cells = cells.shape[0]
    out_shape = [jax.ShapeDtypeStruct((3, n_points), jnp.float32)]
    scratch = []
    if fetch:
        inverse = counters.reshape(-1, 128)
        out_shape = [
            jax.ShapeDtypeStruct(cells.shape, cells.dtype),
            jax.ShapeDtypeStruct((n_cells, 128), jnp.float32),
        ] + out_shape
        scratch = [pltpu.VMEM(inverse.shape, inverse.dtype), pltpu.SemaphoreType.DMA((n_cells // block + 1,))]
    return pl.pallas_call(
        functools.partial(totals_kernel, rate, block, fetch),
        in_specs=in_vmem(1) + [pl.BlockSpec(memory_space=pltpu.HBM if fetch else pltpu.VMEM)] * 2,
        out_specs=in_vmem(len(out_shape)),
        out_shape=out_shape,
        scratch_shapes=scratch,
        compiler_params=pltpu.CompilerParams(vmem_limit_bytes=FETCH_VMEM_BYTES if fetch else VMEM_BYTES),
        cost_estimate=pl.CostEstimate(
            flops=2 * n_cells * n_points * width,
            bytes_accessed=2 * n_cells * width,
            transcendentals=n_cells * n_points,
        ),
    )(points, cells, inverse)


def goal_kernel(rate, *refs):
    *stats, goal = refs
    for at in range(4):
        here = [stat[:, (at ^ by) * 128 : ((at ^ by) + 1) * 128] for by, stat in enumerate(stats)]
        top = functools.reduce(jnp.maximum, [s[:1] for s in here])
        scales = [jnp.exp2((s[:1] - top) * rate) for s in here]
        total = sum(s[1:2] * scale for s, scale in zip(here, scales))
        novel = sum(s[2:] * scale for s, scale in zip(here, scales))
        goal[:, at * 128 : (at + 1) * 128] = jnp.concatenate([top, novel / total / total], axis=0)


def goal_call(rate, *stats):
    return pl.pallas_call(
        functools.partial(goal_kernel, rate),
        in_specs=in_vmem(len(stats)),
        out_specs=in_vmem(1)[0],
        out_shape=jax.ShapeDtypeStruct((2, stats[0].shape[1]), jnp.float32),
        compiler_params=pltpu.CompilerParams(vmem_limit_bytes=VMEM_BYTES),
    )(*stats)


def factor_kernel(rate, *refs):
    goals, tops, (factor, top, weight) = refs[:4], refs[4:6], refs[6:]
    chip = chip_index()
    for by, goal in enumerate(goals):
        for at in range(4):
            spot = pl.ds(pl.multiple_of((at % 2 * 4 + (chip ^ by)) * 128, 128), 128)
            piece = goal[:, at * 128 : (at + 1) * 128]
            top[at // 2, :, spot] = piece[:1]
            weight[at // 2, :, spot] = piece[1:]
    for group in range(2):
        factor[group] = jnp.exp2((tops[group][...] - top[group]) * rate) * weight[group]


def factor_call(rate, goals, tops):
    blocks, n_points = tops[0].shape
    return pl.pallas_call(
        functools.partial(factor_kernel, rate),
        in_specs=in_vmem(6),
        out_specs=in_vmem(1)[0],
        out_shape=jax.ShapeDtypeStruct((2, blocks, n_points), jnp.float32),
        scratch_shapes=[pltpu.VMEM((2, 1, n_points), jnp.float32)] * 2,
        compiler_params=pltpu.CompilerParams(vmem_limit_bytes=VMEM_BYTES),
    )(*goals, *tops)


def expo_kernel(rate, block, *refs):
    pieces, (cells, expo, tops, points) = refs[:4], refs[4:]
    rows = pieces[0].shape[0] // 2
    chip, lo = chip_index(), lax.axis_index("lo")
    for away, piece in zip((0, 1 + lo, 2 - lo, 3), pieces):
        for at in range(2):
            spot = pl.ds(pl.multiple_of((at * 4 + (chip ^ away)) * rows, rows), rows)
            points[spot, :] = piece[at * rows : (at + 1) * rows, :]
    count = expo.shape[0] // block
    for part in range(2):
        some = slice(part * 4 * rows, (part + 1) * 4 * rows)
        for at in range(count):
            mine = pl.ds(pl.multiple_of((chip * count + at) * block, block), block)
            logits = scores(cells[mine, :], points[some, :])
            top = jnp.max(logits, axis=0, keepdims=True)
            expo[at * block : (at + 1) * block, some] = jnp.exp2((logits - top) * rate).astype(jnp.bfloat16)
            tops[at : at + 1, some] = top


def expo_call(rate, block, count, pieces, cells):
    width = cells.shape[1]
    n_points = sum(piece.shape[0] for piece in pieces)
    return pl.pallas_call(
        functools.partial(expo_kernel, rate, block),
        in_specs=in_vmem(5),
        out_specs=in_vmem(3),
        out_shape=[
            jax.ShapeDtypeStruct((count, n_points), jnp.bfloat16),
            jax.ShapeDtypeStruct((count // block, n_points), jnp.float32),
            jax.ShapeDtypeStruct((n_points, width), jnp.bfloat16),
        ],
        compiler_params=pltpu.CompilerParams(vmem_limit_bytes=VMEM_BYTES),
        cost_estimate=pl.CostEstimate(
            flops=2 * count * n_points * width,
            bytes_accessed=2 * (count * width + n_points * width + count * n_points),
            transcendentals=count * n_points,
        ),
    )(*pieces, cells)


def weighed_sums(at, count, expos, points, factor):
    total = weight = None
    here = pl.ds(pl.multiple_of(at * count, count), count)
    for expo, chunk, scales in zip(expos, points, factor):
        share = (expo[here, :].astype(jnp.float32) * scales[pl.ds(at, 1), :]).astype(jnp.bfloat16)
        part = jnp.dot(share, chunk[...], preferred_element_type=jnp.float32)
        wide = share.astype(jnp.float32)
        lanes = sum(wide[:, i : i + 128] for i in range(0, wide.shape[1], 128))
        total = part if total is None else total + part
        weight = lanes if weight is None else weight + lanes
    return total, jnp.sum(weight.T, axis=0, keepdims=True)


def sums_kernel(n, block, side, *refs):
    expos, points, factor, (sums, mass) = refs[:n], refs[n : 2 * n], refs[2 * n], refs[2 * n + 1 :]
    factor = [factor.at[at] for at in range(n)]
    count = sums.shape[0] // block
    first = (lax.axis_index("lo") ^ side) * count
    for at in range(count):
        here = slice(at * block, (at + 1) * block)
        total, weight = weighed_sums(first + at, block, expos, points, factor)
        sums[here, :] = total.astype(sums.dtype)
        mass[:, here] = weight


def sums_call(block, side, rows, dtype, expos, points, factor):
    n = len(expos)
    n_points, width = points[0].shape
    return pl.pallas_call(
        functools.partial(sums_kernel, n, block, side),
        in_specs=in_vmem(2 * n + 1),
        out_specs=in_vmem(2),
        out_shape=[jax.ShapeDtypeStruct((rows, width), dtype), jax.ShapeDtypeStruct((1, rows), jnp.float32)],
        compiler_params=pltpu.CompilerParams(vmem_limit_bytes=VMEM_BYTES),
        cost_estimate=pl.CostEstimate(
            flops=2 * rows * n * n_points * width,
            bytes_accessed=2 * n * n_points * (rows + width) + 4 * rows * width,
            transcendentals=0,
        ),
    )(*expos, *points, factor)


def add_kernel(block, here, here_mass, there, there_mass, sums, mass, out, left):
    def copy(at):
        rows = pl.ds(at * block, block)
        return pltpu.make_async_copy(out.at[rows, :], sums.at[rows, :], left.at[at])

    count = here.shape[0] // block
    for at in range(count):
        rows = slice(at * block, (at + 1) * block)
        out[rows, :] = here[rows, :] + there[rows, :].astype(jnp.float32)
        copy(at).start()
    mass[...] = here_mass[...] + there_mass[...]
    for at in range(count):
        copy(at).wait()


def add_call(block, here, here_mass, there, there_mass):
    return pl.pallas_call(
        functools.partial(add_kernel, block),
        in_specs=in_vmem(4),
        out_specs=[pl.BlockSpec(memory_space=pltpu.HBM)] + in_vmem(1),
        out_shape=[
            jax.ShapeDtypeStruct(here.shape, jnp.float32),
            jax.ShapeDtypeStruct(here_mass.shape, jnp.float32),
        ],
        scratch_shapes=[
            pltpu.VMEM(here.shape, jnp.float32),
            pltpu.SemaphoreType.DMA((here.shape[0] // block,)),
        ],
        compiler_params=pltpu.CompilerParams(vmem_limit_bytes=VMEM_BYTES),
    )(here, here_mass, there, there_mass)


def split_cells(codes, exponents, centroids, counters):
    own = to_points(codes, exponents)
    rate = 4.0 / math.sqrt(own.shape[1]) * math.log2(math.e)
    plane = ("y", "x", "lo")

    turn = lambda a: exchange(a, plane, lambda at: at ^ (4 if at % 2 else 2))
    turn_back = lambda a: exchange(a, plane, lambda at: at ^ (2 if at % 2 else 4))
    along_z = lambda a, by: exchange(a, ("cells",), lambda at: at ^ by)
    around = lambda a, by: exchange(a, ("y", "x"), lambda at: at ^ by)

    per_device = centroids.shape[0] // 8
    block = per_device // 3

    near_1, near_2, near_3 = (along_z(own, by) for by in (1, 2, 3))
    near = jnp.concatenate([own, near_1])
    cells, inverse, stat = totals_call(rate, 2 * block, near, centroids, counters=counters)
    nears, stats = [near], [stat]
    near = join(near_2, near_3, stat)
    nears.append(near)
    stats += totals_call(rate, 2 * block, near, cells, inverse)

    stat = jnp.concatenate(stats, axis=1)
    goal = goal_call(rate, stat, *(along_z(stat, by) for by in (1, 2, 3)))
    goals = [goal] + [around(goal, by) for by in (1, 2, 3)]

    expos, tops, points = [], [], []
    for near in nears:
        first, second = turn(near), turn_back(near)
        pieces = (near, first, second, turn_back(first))
        expo, top, chunks = expo_call(rate, block, 2 * per_device, pieces, cells)
        expos.append(expo), tops.append(top), points.append(chunks)
    factor = factor_call(rate, goals, tops)

    there = sums_call(block, 1, per_device, jnp.bfloat16, expos, points, factor)
    there = [exchange(a, ("lo",), lambda at: at ^ 1) for a in there]
    here = sums_call(block, 0, per_device, jnp.float32, expos, points, factor)
    out, mass = add_call(block, *here, *there)
    return (out[None], mass)


def solution(mesh):
    pts, cells = (mesh.shape[name] for name in ("pts", "cells"))
    square = (pts, cells) == (8, 4)
    shape, names = ((2, 2, 2, cells), ("y", "x", "lo", "cells")) if square else ((pts, cells), ("pts", "cells"))
    fine = Mesh(mesh.devices.reshape(shape), names)
    spread = names[:-1]
    in_specs = (P(names, None), P(names), P("cells", None), P("cells"))
    out_specs = (P("cells", spread, None), P("cells", spread))

    def run(codes, exponents, centroids, counters):
        small = codes.size * 2 <= GATHER_BYTES and codes.shape[0] == 128 * pts * cells
        body = split_cells if square and small else split_points
        mapped = jax.shard_map(body, mesh=fine, in_specs=in_specs, out_specs=out_specs, check_vma=False)
        return mapped(codes, exponents, centroids, counters)

    return run
```

time: 94 us -> 65.3 us (0.69)
  local copies, waits for them, and re-layouts: 29.8 us -> 0.73 us
  waiting for transfers between devices: 8.51 us -> 16.8 us
  blocking collectives: 8.08 us -> 0 us
  Pallas kernels: 18.9 us -> 21.8 us
  other arithmetic: 2.86 us -> 1.72 us
    unnamed x59 -> x2, local copies, waits for them, and re-layouts: 27.3 us -> 0.73 us
    ppermute x17, waiting for transfers between devices: 2.68 us -> 16.8 us  [exchange(): return lax.ppermute(a, axes, [(partner(at), at) for at in range(count)])]
    all_to_all x1 -> x0, blocking collectives: 8.08 us -> none  [everyone(): return lax.all_to_all(jnp.broadcast_to(a, (count, *a.shape)), axes, 0, 0)]
    all_to_all x1 -> x0, waiting for transfers between devices: 5.83 us -> none  [everyone(): return lax.all_to_all(jnp.broadcast_to(a, (count, *a.shape)), axes, 0, 0)]
    all_to_all x1 -> x0, starting transfers between devices: 4.02 us -> none  [everyone(): return lax.all_to_all(jnp.broadcast_to(a, (count, *a.shape)), axes, 0, 0)]
    ppermute x17, starting transfers between devices: 19.7 us -> 23.1 us  [exchange(): return lax.ppermute(a, axes, [(partner(at), at) for at in range(count)])]
    pallas_call x9 -> x10, Pallas kernels: 18.9 us -> 21.8 us  [the longest x2 11.6 us: totals_call(): pl.pallas_call(functools.partial(totals_kernel, rate, block, fetch), in_s...]
    dynamic_slice x1 -> x0, local copies, waits for them, and re-layouts: 1.51 us -> none  [split_cells(): lax.dynamic_slice_in_dim(a, chip * 2 * per_device, 2 * per_device)]
  transfers between devices with their start and end apart: 18 -> 17, of which waited for: 4 -> 7; matrix products, arithmetic and copies ran while one was open for 3% -> 0% of each run, Pallas kernels for 10% -> 28%
where the time goes in v7:
time: 65.3 us; the launch traced here: 65.1 us
  starting transfers between devices  23.1 us (35%)
  Pallas kernels  21.8 us (33%)
  waiting for transfers between devices  16.8 us (26%)
  other arithmetic  1.72 us (3%)
  between operations  0.94 us (1%)
  local copies, waits for them, and re-layouts  0.73 us (1%)
    ppermute x17, starting transfers between devices, exchange(): return lax.ppermute(a, axes, [(partner(at), at) for at in range(count)])  23.1 us
    ppermute x17, waiting for transfers between devices, exchange(): return lax.ppermute(a, axes, [(partner(at), at) for at in range(count)])  16.8 us
    pallas_call x2, Pallas kernels, totals_call(): pl.pallas_call(functools.partial(totals_kernel, rate, block, fetch), in_s...  11.6 us
    pallas_call x2, Pallas kernels, expo_call(): pl.pallas_call(functools.partial(expo_kernel, rate, block), in_specs=in_v...  4.37 us
    pallas_call x2, Pallas kernels, sums_call(): pl.pallas_call(functools.partial(sums_kernel, n, block, side), in_specs=i...  3.96 us
    pallas_call x1, Pallas kernels, add_call(): pl.pallas_call(functools.partial(add_kernel, block), in_specs=in_vmem(4),...  1.79 us
  transfers between devices with their start and end apart: 17, of which 7 were waited for; matrix products, arithmetic and copies ran while one was open for 0% of the time, Pallas kernels for 28%

profile of v7, /device:TPU:0, one launch (start us, length us, event | category | flops | bytes accessed | tf_op | source)
XLA Modules:
  0.0 65.1 jit_solution(12327884627688780051)
XLA Ops:
  0.6 0.7 %convert_multiply_fusion = f32[128]{0:T(128)S(1)} fusion(s32[128]{0:T(128)} %param.5), kind=kLoop, calls=%fused_computation.3 | loop fusion | flops 512 | bytes 1024 | tf_op jit(solution)/shard_map/mul | solution.py:17
  1.3 1.0 %multiply_convert_fusion = bf16[128,512]{1,0:T(8,128)(2,1)S(1)} fusion(s32[128,512]{1,0:T(8,128)} %param.4, f32[128]{0:T(128)S(1)} %convert_multiply_fusion), kind=kLoop, calls=%fused_computation.1 | loop fusion | flops 196608 | bytes 393728 | tf_op jit(solution)/shard_map/convert_element_type | solution.py:18
  2.3 3.1 %collective-permute-start = (bf16[128,512]{1,0:T(8,128)(2,1)S(1)}, bf16[128,512]{1,0:T(8,128)(2,1)S(1)}, u32[]{:S(2)}, u32[]{:S(2)}) collective-permute-start(bf16[128,512]{1,0:T(8,128)(2,1)S(1)} %multiply_convert_fusion), channel_id=1, source_target_pairs={{1,0},{0,1},{3,2},{2,3},{5,4},{4,5},{7,6},{6,7},{9,8},{8,9},{11,10... | collective-permute-start | bytes 393224 | tf_op jit(solution)/shard_map/ppermute | solution.py:50
  5.4 2.5 %collective-permute-start.5 = (bf16[128,512]{1,0:T(8,128)(2,1)S(1)}, bf16[128,512]{1,0:T(8,128)(2,1)S(1)}, u32[]{:S(2)}, u32[]{:S(2)}) collective-permute-start(bf16[128,512]{1,0:T(8,128)(2,1)S(1)} %multiply_convert_fusion), channel_id=1, source_target_pairs={{3,0},{2,1},{1,2},{0,3},{7,4},{6,5},{5,6},{4,7},{11,8},{10,9},{9,1... | collective-permute-start | bytes 393224 | tf_op jit(solution)/shard_map/ppermute | solution.py:50
  7.9 0.1 collective-permute-start.4
  8.0 0.9 %collective-permute-done = bf16[128,512]{1,0:T(8,128)(2,1)S(1)} collective-permute-done((bf16[128,512]{1,0:T(8,128)(2,1)S(1)}, bf16[128,512]{1,0:T(8,128)(2,1)S(1)}, u32[]{:S(2)}, u32[]{:S(2)}) %collective-permute-start) | collective-permute-done | bytes 131104 | tf_op jit(solution)/shard_map/ppermute | solution.py:50
  8.9 0.0 copy-start
  9.0 0.7 %copy-done = s32[6144]{0:T(1024)S(1)} copy-done((s32[6144]{0:T(1024)S(1)}, s32[6144]{0:T(1024)}, u32[]{:S(2)}) %copy-start) | copy-done | bytes 24600
  9.7 8.6 %shard_map.59 = (bf16[6144,512]{1,0:T(8,128)(2,1)S(1)}, f32[6144,128]{1,0:T(8,128)S(1)}, f32[3,256]{1,0:T(4,128)S(1)}) custom-call(bf16[256,512]{1,0:T(8,128)(2,1)S(1)} %pad_maximum_fusion.points.refs_0_, bf16[6144,512]{1,0:T(8,128)(2,1)} %cells_from.1, s32[48,128]{1,0:T(8,128)S(1)} %bitcast.2), custom_call_target="tpu_custom_call" | custom-call | flops 1610612736 | bytes 6291456 | tf_op jit(solution)/shard_map/pallas_call | solution.py:139
  18.3 0.0 collective-permute-done.5.below
  18.3 1.4 %collective-permute-done.4.above = bf16[128,512]{1,0:T(8,128)(2,1)S(1)} collective-permute-done((bf16[128,512]{1,0:T(8,128)(2,1)S(1)}, bf16[128,512]{1,0:T(8,128)(2,1)S(1)}, u32[]{:S(2)}, u32[]{:S(2)}) %collective-permute-start.4) | collective-permute-done | bytes 131104 | tf_op jit(solution)/shard_map/ppermute | solution.py:50
  19.7 1.6 %collective-permute-start.6 = (bf16[256,512]{1,0:T(8,128)(2,1)S(1)}, bf16[256,512]{1,0:T(8,128)(2,1)S(1)}, u32[]{:S(2)}, u32[]{:S(2)}) collective-permute-start(bf16[256,512]{1,0:T(8,128)(2,1)S(1)} %shard_map.61.refs_0_.points), channel_id=1, source_target_pairs={{8,0},{20,4},{0,8},{28,12},{24,16},{4,20},{16,24},{12,28},{9,1},{2... | collective-permute-start | bytes 786440 | tf_op jit(solution)/shard_map/ppermute | solution.py:50
  21.2 0.5 collective-permute-start.1
  21.8 1.5 %collective-permute-start.2 = (bf16[256,512]{1,0:T(8,128)(2,1)S(1)}, bf16[256,512]{1,0:T(8,128)(2,1)S(1)}, u32[]{:S(2)}, u32[]{:S(2)}) collective-permute-start(bf16[256,512]{1,0:T(8,128)(2,1)S(1)} %pad_maximum_fusion.points.refs_0_), channel_id=1, source_target_pairs={{16,0},{12,4},{24,8},{4,12},{0,16},{28,20},{8,24},{20,28},{17,1},{... | collective-permute-start | bytes 786440 | tf_op jit(solution)/shard_map/ppermute | solution.py:50
  23.3 0.5 collective-permute-start.7
  23.8 5.1 %collective-permute-done.6.refs_1_ = bf16[256,512]{1,0:T(8,128)(2,1)S(1)} collective-permute-done((bf16[256,512]{1,0:T(8,128)(2,1)S(1)}, bf16[256,512]{1,0:T(8,128)(2,1)S(1)}, u32[]{:S(2)}, u32[]{:S(2)}) %collective-permute-start.6) | collective-permute-done | bytes 262176 | tf_op jit(solution)/shard_map/ppermute | solution.py:50
  28.9 1.5 %collective-permute-start.8 = (bf16[256,512]{1,0:T(8,128)(2,1)S(1)}, bf16[256,512]{1,0:T(8,128)(2,1)S(1)}, u32[]{:S(2)}, u32[]{:S(2)}) collective-permute-start(bf16[256,512]{1,0:T(8,128)(2,1)S(1)} %collective-permute-done.6.refs_1_), channel_id=1, source_target_pairs={{16,0},{12,4},{24,8},{4,12},{0,16},{28,20},{8,24},{20,28},{17,1},{... | collective-permute-start | bytes 786440 | tf_op jit(solution)/shard_map/ppermute | solution.py:50
  30.4 3.0 %shard_map.63 = f32[3,256]{1,0:T(4,128)S(1)} custom-call(bf16[256,512]{1,0:T(8,128)(2,1)S(1)} %shard_map.61.refs_0_.points, bf16[6144,512]{1,0:T(8,128)(2,1)S(1)} %get-tuple-element.17.refs_4_.cells_from, f32[6144,128]{1,0:T(8,128)S(1)} %get-tuple-element.23.inverse_from), custom_call_target="tpu_custom_call" | custom-call | flops 1610612736 | bytes 6291456 | tf_op jit(solution)/shard_map/pallas_call | solution.py:139
  33.5 1.1 %collective-permute-done.1.refs_1_ = bf16[256,512]{1,0:T(8,128)(2,1)S(1)} collective-permute-done((bf16[256,512]{1,0:T(8,128)(2,1)S(1)}, bf16[256,512]{1,0:T(8,128)(2,1)S(1)}, u32[]{:S(2)}, u32[]{:S(2)}) %collective-permute-start.1) | collective-permute-done | bytes 262176 | tf_op jit(solution)/shard_map/ppermute | solution.py:50
  34.5 1.5 %collective-permute-start.3 = (bf16[256,512]{1,0:T(8,128)(2,1)S(1)}, bf16[256,512]{1,0:T(8,128)(2,1)S(1)}, u32[]{:S(2)}, u32[]{:S(2)}) collective-permute-start(bf16[256,512]{1,0:T(8,128)(2,1)S(1)} %collective-permute-done.1.refs_1_), channel_id=1, source_target_pairs={{16,0},{12,4},{24,8},{4,12},{0,16},{28,20},{8,24},{20,28},{17,1},{... | collective-permute-start | bytes 786440 | tf_op jit(solution)/shard_map/ppermute | solution.py:50
  36.1 4.6 %collective-permute-start.11 = (f32[3,512]{1,0:T(4,128)S(1)}, f32[3,512]{1,0:T(4,128)S(1)}, u32[]{:S(2)}, u32[]{:S(2)}) collective-permute-start(f32[3,512]{1,0:T(4,128)S(1)} %pad_maximum_fusion.1.refs_0_), channel_id=1, source_target_pairs={{3,0},{2,1},{1,2},{0,3},{7,4},{6,5},{5,6},{4,7},{11,8},{10,9},{9,1... | collective-permute-start | bytes 18440 | tf_op jit(solution)/shard_map/ppermute | solution.py:50
  40.6 1.6 %collective-permute-done.11.refs_3_ = f32[3,512]{1,0:T(4,128)S(1)} collective-permute-done((f32[3,512]{1,0:T(4,128)S(1)}, f32[3,512]{1,0:T(4,128)S(1)}, u32[]{:S(2)}, u32[]{:S(2)}) %collective-permute-start.11) | collective-permute-done | bytes 6176 | tf_op jit(solution)/shard_map/ppermute | solution.py:50
  42.3 0.1 collective-permute-start.10
  42.3 4.5 %collective-permute-done.10.refs_2_ = f32[3,512]{1,0:T(4,128)S(1)} collective-permute-done((f32[3,512]{1,0:T(4,128)S(1)}, f32[3,512]{1,0:T(4,128)S(1)}, u32[]{:S(2)}, u32[]{:S(2)}) %collective-permute-start.10) | collective-permute-done | bytes 6176 | tf_op jit(solution)/shard_map/ppermute | solution.py:50
  46.8 1.5 %collective-permute-start.9 = (f32[3,512]{1,0:T(4,128)S(1)}, f32[3,512]{1,0:T(4,128)S(1)}, u32[]{:S(2)}, u32[]{:S(2)}) collective-permute-start(f32[3,512]{1,0:T(4,128)S(1)} %pad_maximum_fusion.1.refs_0_), channel_id=1, source_target_pairs={{1,0},{0,1},{3,2},{2,3},{5,4},{4,5},{7,6},{6,7},{9,8},{8,9},{11,10... | collective-permute-start | bytes 18440 | tf_op jit(solution)/shard_map/ppermute | solution.py:50
  48.3 2.2 %collective-permute-done.9.refs_1_ = f32[3,512]{1,0:T(4,128)S(1)} collective-permute-done((f32[3,512]{1,0:T(4,128)S(1)}, f32[3,512]{1,0:T(4,128)S(1)}, u32[]{:S(2)}, u32[]{:S(2)}) %collective-permute-start.9) | collective-permute-done | bytes 6176 | tf_op jit(solution)/shard_map/ppermute | solution.py:50
  50.5 1.5 %collective-permute-start.14 = (f32[2,512]{1,0:T(2,128)S(1)}, f32[2,512]{1,0:T(2,128)S(1)}, u32[]{:S(2)}, u32[]{:S(2)}) collective-permute-start(f32[2,512]{1,0:T(2,128)S(1)} %shard_map.64.refs_0_), channel_id=1, source_target_pairs={{24,0},{16,8},{8,16},{0,24},{25,1},{17,9},{9,17},{1,25},{26,2},{18... | collective-permute-start | bytes 12296 | tf_op jit(solution)/shard_map/ppermute | solution.py:50
  52.0 0.0 collective-permute-done.7.refs_2_
  52.0 1.5 %collective-permute-start.13 = (f32[2,512]{1,0:T(2,128)S(1)}, f32[2,512]{1,0:T(2,128)S(1)}, u32[]{:S(2)}, u32[]{:S(2)}) collective-permute-start(f32[2,512]{1,0:T(2,128)S(1)} %shard_map.64.refs_0_), channel_id=1, source_target_pairs={{16,0},{24,8},{0,16},{8,24},{17,1},{25,9},{1,17},{9,25},{18,2},{26... | collective-permute-start | bytes 12296 | tf_op jit(solution)/shard_map/ppermute | solution.py:50
  53.5 0.0 collective-permute-done.8.refs_3_
  53.5 0.5 collective-permute-start.12
  54.1 2.1 %shard_map.62 = (bf16[1536,1024]{1,0:T(8,128)(2,1)S(1)}, f32[6,1024]{1,0:T(8,128)S(1)}, bf16[1024,512]{1,0:T(8,128)(2,1)S(1)}) custom-call(bf16[256,512]{1,0:T(8,128)(2,1)S(1)} %shard_map.61.refs_0_.points, bf16[256,512]{1,0:T(8,128)(2,1)S(1)} %collective-permute-done.6.refs_1_, bf16[256,512]{1,0:T(8,128)(2,1)S(1)} %collective-permute-done.7.refs_2_, ...), custom_call_target="tpu_custom_call" | custom-call | flops 1610612736 | bytes 5767168 | tf_op jit(solution)/shard_map/pallas_call | solution.py:222
  56.2 0.0 collective-permute-done.2.refs_2_
  56.2 0.0 collective-permute-done.3.refs_3_
  56.2 2.3 %shard_map.60 = (bf16[1536,1024]{1,0:T(8,128)(2,1)S(1)}, f32[6,1024]{1,0:T(8,128)S(1)}, bf16[1024,512]{1,0:T(8,128)(2,1)S(1)}) custom-call(bf16[256,512]{1,0:T(8,128)(2,1)S(1)} %pad_maximum_fusion.points.refs_0_, bf16[256,512]{1,0:T(8,128)(2,1)S(1)} %collective-permute-done.1.refs_1_, bf16[256,512]{1,0:T(8,128)(2,1)S(1)} %collective-permute-done.2.refs_2_, ...), custom_call_target="tpu_custom_call" | custom-call | flops 1610612736 | bytes 5767168 | tf_op jit(solution)/shard_map/pallas_call | solution.py:222
  58.5 0.0 collective-permute-done.14.refs_3_
  58.5 0.0 collective-permute-done.13.refs_2_
  58.5 0.0 collective-permute-done.12.refs_1_
  58.5 2.0 %shard_map.67 = (bf16[768,512]{1,0:T(8,128)(2,1)S(1)}, f32[1,768]{1,0:T(1,128)S(1)}) custom-call(bf16[1536,1024]{1,0:T(8,128)(2,1)S(1)} %get-tuple-element.18.refs_0_, bf16[1536,1024]{1,0:T(8,128)(2,1)S(1)} %get-tuple-element.20.refs_1_, bf16[1024,512]{1,0:T(8,128)(2,1)S(1)} %get-tuple-element.21.refs_2_, bf16[1024,512]{1,0:T(8,128)(2,1)S(1)} %get-tuple-element.22.refs_3_, ...), custom_call_target="tpu_custom_call" | custom-call | flops 1610612736 | bytes 6815744 | tf_op jit(solution)/shard_map/pallas_call | solution.py:268
  60.5 0.1 collective-permute-start.15
  60.6 0.5 collective-permute-start.16
  61.1 2.0 %shard_map.66 = (f32[768,512]{1,0:T(8,128)S(1)}, f32[1,768]{1,0:T(1,128)S(1)}) custom-call(bf16[1536,1024]{1,0:T(8,128)(2,1)S(1)} %get-tuple-element.18.refs_0_, bf16[1536,1024]{1,0:T(8,128)(2,1)S(1)} %get-tuple-element.20.refs_1_, bf16[1024,512]{1,0:T(8,128)(2,1)S(1)} %get-tuple-element.21.refs_2_, bf16[1024,512]{1,0:T(8,128)(2,1)S(1)} %get-tuple-element.22.refs_3_, ...), custom_call_target="tpu_custom_call" | custom-call | flops 1610612736 | bytes 6815744 | tf_op jit(solution)/shard_map/pallas_call | solution.py:268
  63.1 0.0 collective-permute-done.16.there_mass
  63.1 0.0 collective-permute-done.15.there
  63.1 1.8 %shard_map.68 = (f32[768,512]{1,0:T(8,128)}, f32[1,768]{1,0:T(1,128)}) custom-call(f32[768,512]{1,0:T(8,128)S(1)} %get-tuple-element.26.here, f32[1,768]{1,0:T(1,128)S(1)} %get-tuple-element.27.here_mass, bf16[768,512]{1,0:T(8,128)(2,1)S(1)} %collective-permute-done.15.there, f32[1,768]{1,0:T(1,128)S(1)} %collective-permute-done.16.there_mass), custom_call_target="tpu_custom_call" | custom-call | tf_op jit(solution)/shard_map/pallas_call | solution.py:298
  (5 shorter events, 0.1 us)
Async XLA Ops:
  2.3 6.6 %collective-permute-start = (bf16[128,512]{1,0:T(8,128)(2,1)S(1)}, bf16[128,512]{1,0:T(8,128)(2,1)S(1)}, u32[]{:S(2)}, u32[]{:S(2)}) collective-permute-start(bf16[128,512]{1,0:T(8,128)(2,1)S(1)} %multiply_convert_fusion), channel_id=1, source_target_pairs={{1,0},{0,1},{3,2},{2,3},{5,4},{4,5},{7,6},{6,7},{9,8},{8,9},{11,10... | collective-permute-start | bytes 393224 | tf_op jit(solution)/shard_map/ppermute | solution.py:50
  5.4 12.9 %collective-permute-start.5 = (bf16[128,512]{1,0:T(8,128)(2,1)S(1)}, bf16[128,512]{1,0:T(8,128)(2,1)S(1)}, u32[]{:S(2)}, u32[]{:S(2)}) collective-permute-start(bf16[128,512]{1,0:T(8,128)(2,1)S(1)} %multiply_convert_fusion), channel_id=1, source_target_pairs={{3,0},{2,1},{1,2},{0,3},{7,4},{6,5},{5,6},{4,7},{11,8},{10,9},{9,1... | collective-permute-start | bytes 393224 | tf_op jit(solution)/shard_map/ppermute | solution.py:50
  7.9 11.8 %collective-permute-start.4 = (bf16[128,512]{1,0:T(8,128)(2,1)S(1)}, bf16[128,512]{1,0:T(8,128)(2,1)S(1)}, u32[]{:S(2)}, u32[]{:S(2)}) collective-permute-start(bf16[128,512]{1,0:T(8,128)(2,1)S(1)} %multiply_convert_fusion), channel_id=1, source_target_pairs={{2,0},{3,1},{0,2},{1,3},{6,4},{7,5},{4,6},{5,7},{10,8},{11,9},{8,1... | collective-permute-start | bytes 393224 | tf_op jit(solution)/shard_map/ppermute | solution.py:50
  8.9 0.7 %copy-start = (s32[6144]{0:T(1024)S(1)}, s32[6144]{0:T(1024)}, u32[]{:S(2)}) copy-start(s32[6144]{0:T(1024)} %param.7) | copy-start | bytes 73732
  19.7 9.2 %collective-permute-start.6 = (bf16[256,512]{1,0:T(8,128)(2,1)S(1)}, bf16[256,512]{1,0:T(8,128)(2,1)S(1)}, u32[]{:S(2)}, u32[]{:S(2)}) collective-permute-start(bf16[256,512]{1,0:T(8,128)(2,1)S(1)} %shard_map.61.refs_0_.points), channel_id=1, source_target_pairs={{8,0},{20,4},{0,8},{28,12},{24,16},{4,20},{16,24},{12,28},{9,1},{2... | collective-permute-start | bytes 786440 | tf_op jit(solution)/shard_map/ppermute | solution.py:50
  21.2 13.3 %collective-permute-start.1 = (bf16[256,512]{1,0:T(8,128)(2,1)S(1)}, bf16[256,512]{1,0:T(8,128)(2,1)S(1)}, u32[]{:S(2)}, u32[]{:S(2)}) collective-permute-start(bf16[256,512]{1,0:T(8,128)(2,1)S(1)} %pad_maximum_fusion.points.refs_0_), channel_id=1, source_target_pairs={{8,0},{20,4},{0,8},{28,12},{24,16},{4,20},{16,24},{12,28},{9,1},{2... | collective-permute-start | bytes 786440 | tf_op jit(solution)/shard_map/ppermute | solution.py:50
  21.8 34.4 %collective-permute-start.2 = (bf16[256,512]{1,0:T(8,128)(2,1)S(1)}, bf16[256,512]{1,0:T(8,128)(2,1)S(1)}, u32[]{:S(2)}, u32[]{:S(2)}) collective-permute-start(bf16[256,512]{1,0:T(8,128)(2,1)S(1)} %pad_maximum_fusion.points.refs_0_), channel_id=1, source_target_pairs={{16,0},{12,4},{24,8},{4,12},{0,16},{28,20},{8,24},{20,28},{17,1},{... | collective-permute-start | bytes 786440 | tf_op jit(solution)/shard_map/ppermute | solution.py:50
  23.3 28.7 %collective-permute-start.7 = (bf16[256,512]{1,0:T(8,128)(2,1)S(1)}, bf16[256,512]{1,0:T(8,128)(2,1)S(1)}, u32[]{:S(2)}, u32[]{:S(2)}) collective-permute-start(bf16[256,512]{1,0:T(8,128)(2,1)S(1)} %shard_map.61.refs_0_.points), channel_id=1, source_target_pairs={{16,0},{12,4},{24,8},{4,12},{0,16},{28,20},{8,24},{20,28},{17,1},{... | collective-permute-start | bytes 786440 | tf_op jit(solution)/shard_map/ppermute | solution.py:50
  28.9 24.6 %collective-permute-start.8 = (bf16[256,512]{1,0:T(8,128)(2,1)S(1)}, bf16[256,512]{1,0:T(8,128)(2,1)S(1)}, u32[]{:S(2)}, u32[]{:S(2)}) collective-permute-start(bf16[256,512]{1,0:T(8,128)(2,1)S(1)} %collective-permute-done.6.refs_1_), channel_id=1, source_target_pairs={{16,0},{12,4},{24,8},{4,12},{0,16},{28,20},{8,24},{20,28},{17,1},{... | collective-permute-start | bytes 786440 | tf_op jit(solution)/shard_map/ppermute | solution.py:50
  34.5 21.6 %collective-permute-start.3 = (bf16[256,512]{1,0:T(8,128)(2,1)S(1)}, bf16[256,512]{1,0:T(8,128)(2,1)S(1)}, u32[]{:S(2)}, u32[]{:S(2)}) collective-permute-start(bf16[256,512]{1,0:T(8,128)(2,1)S(1)} %collective-permute-done.1.refs_1_), channel_id=1, source_target_pairs={{16,0},{12,4},{24,8},{4,12},{0,16},{28,20},{8,24},{20,28},{17,1},{... | collective-permute-start | bytes 786440 | tf_op jit(solution)/shard_map/ppermute | solution.py:50
  36.1 6.2 %collective-permute-start.11 = (f32[3,512]{1,0:T(4,128)S(1)}, f32[3,512]{1,0:T(4,128)S(1)}, u32[]{:S(2)}, u32[]{:S(2)}) collective-permute-start(f32[3,512]{1,0:T(4,128)S(1)} %pad_maximum_fusion.1.refs_0_), channel_id=1, source_target_pairs={{3,0},{2,1},{1,2},{0,3},{7,4},{6,5},{5,6},{4,7},{11,8},{10,9},{9,1... | collective-permute-start | bytes 18440 | tf_op jit(solution)/shard_map/ppermute | solution.py:50
  42.3 4.5 %collective-permute-start.10 = (f32[3,512]{1,0:T(4,128)S(1)}, f32[3,512]{1,0:T(4,128)S(1)}, u32[]{:S(2)}, u32[]{:S(2)}) collective-permute-start(f32[3,512]{1,0:T(4,128)S(1)} %pad_maximum_fusion.1.refs_0_), channel_id=1, source_target_pairs={{2,0},{3,1},{0,2},{1,3},{6,4},{7,5},{4,6},{5,7},{10,8},{11,9},{8,1... | collective-permute-start | bytes 18440 | tf_op jit(solution)/shard_map/ppermute | solution.py:50
  46.8 3.7 %collective-permute-start.9 = (f32[3,512]{1,0:T(4,128)S(1)}, f32[3,512]{1,0:T(4,128)S(1)}, u32[]{:S(2)}, u32[]{:S(2)}) collective-permute-start(f32[3,512]{1,0:T(4,128)S(1)} %pad_maximum_fusion.1.refs_0_), channel_id=1, source_target_pairs={{1,0},{0,1},{3,2},{2,3},{5,4},{4,5},{7,6},{6,7},{9,8},{8,9},{11,10... | collective-permute-start | bytes 18440 | tf_op jit(solution)/shard_map/ppermute | solution.py:50
  50.5 8.0 %collective-permute-start.14 = (f32[2,512]{1,0:T(2,128)S(1)}, f32[2,512]{1,0:T(2,128)S(1)}, u32[]{:S(2)}, u32[]{:S(2)}) collective-permute-start(f32[2,512]{1,0:T(2,128)S(1)} %shard_map.64.refs_0_), channel_id=1, source_target_pairs={{24,0},{16,8},{8,16},{0,24},{25,1},{17,9},{9,17},{1,25},{26,2},{18... | collective-permute-start | bytes 12296 | tf_op jit(solution)/shard_map/ppermute | solution.py:50
  52.0 6.5 %collective-permute-start.13 = (f32[2,512]{1,0:T(2,128)S(1)}, f32[2,512]{1,0:T(2,128)S(1)}, u32[]{:S(2)}, u32[]{:S(2)}) collective-permute-start(f32[2,512]{1,0:T(2,128)S(1)} %shard_map.64.refs_0_), channel_id=1, source_target_pairs={{16,0},{24,8},{0,16},{8,24},{17,1},{25,9},{1,17},{9,25},{18,2},{26... | collective-permute-start | bytes 12296 | tf_op jit(solution)/shard_map/ppermute | solution.py:50
  53.5 5.0 %collective-permute-start.12 = (f32[2,512]{1,0:T(2,128)S(1)}, f32[2,512]{1,0:T(2,128)S(1)}, u32[]{:S(2)}, u32[]{:S(2)}) collective-permute-start(f32[2,512]{1,0:T(2,128)S(1)} %shard_map.64.refs_0_), channel_id=1, source_target_pairs={{8,0},{0,8},{24,16},{16,24},{9,1},{1,9},{25,17},{17,25},{10,2},{2,... | collective-permute-start | bytes 12296 | tf_op jit(solution)/shard_map/ppermute | solution.py:50
  60.5 2.6 %collective-permute-start.15 = (bf16[768,512]{1,0:T(8,128)(2,1)S(1)}, bf16[768,512]{1,0:T(8,128)(2,1)S(1)}, u32[]{:S(2)}, u32[]{:S(2)}) collective-permute-start(bf16[768,512]{1,0:T(8,128)(2,1)S(1)} %get-tuple-element.28), channel_id=1, source_target_pairs={{4,0},{0,4},{5,1},{1,5},{6,2},{2,6},{7,3},{3,7},{12,8},{8,12},{13,... | collective-permute-start | bytes 2359304 | tf_op jit(solution)/shard_map/ppermute | solution.py:50
  60.6 2.5 %collective-permute-start.16 = (f32[1,768]{1,0:T(1,128)S(1)}, f32[1,768]{1,0:T(1,128)S(1)}, u32[]{:S(2)}, u32[]{:S(2)}) collective-permute-start(f32[1,768]{1,0:T(1,128)S(1)} %get-tuple-element.29), channel_id=1, source_target_pairs={{4,0},{0,4},{5,1},{1,5},{6,2},{2,6},{7,3},{3,7},{12,8},{8,12},{13,... | collective-permute-start | bytes 9224 | tf_op jit(solution)/shard_map/ppermute | solution.py:50

commit v8 on v7

--- a/solution.py
+++ b/solution.py
@@ -54,18 +54,19 @@
     return [pl.BlockSpec(memory_space=pltpu.VMEM)] * n
 
 
-def join(above, below, after):
-    def kernel(above, below, after, out):
+def join(above, below, *after):
+    def kernel(above, below, *refs):
+        out = refs[-1]
         out[: above.shape[0], :] = above[...]
         out[above.shape[0] :, :] = below[...]
 
     return pl.pallas_call(
         kernel,
-        in_specs=in_vmem(3),
+        in_specs=in_vmem(2 + len(after)),
         out_specs=in_vmem(1)[0],
         out_shape=jax.ShapeDtypeStruct((above.shape[0] + below.shape[0], above.shape[1]), above.dtype),
         compiler_params=pltpu.CompilerParams(vmem_limit_bytes=VMEM_BYTES),
-    )(above, below, after)
+    )(above, below, *after)
 
 
 def scores(cells, points):
@@ -76,8 +77,9 @@
     return lax.axis_index("y") * 2 + lax.axis_index("x")
 
 
-def totals_kernel(rate, block, fetch, points, cells_from, inverse_from, *refs):
+def totals_kernel(rate, block, fetch, tokens, points, cells_from, inverse_from, *refs):
     every = points[...]
+    refs = refs[tokens:]
     if fetch:
         cells, inverse, stats, counters, arrived = refs
     else:
@@ -92,7 +94,7 @@
 
     if fetch:
         for at in (count, *range(count)):
-            copy(at).start()
+            copy(at).start(priority=at % 2)
         copy(count).wait()
     highest = total = novel = None
     for at in range(count):
@@ -123,7 +125,7 @@
     stats[...] = jnp.concatenate([highest, total, novel], axis=0)
 
 
-def totals_call(rate, block, points, cells, inverse=None, counters=None):
+def totals_call(rate, block, points, cells, inverse=None, counters=None, after=()):
     fetch = inverse is None
     n_points, width = points.shape
     n_cells = cells.shape[0]
@@ -137,8 +139,8 @@
         ] + out_shape
         scratch = [pltpu.VMEM(inverse.shape, inverse.dtype), pltpu.SemaphoreType.DMA((n_cells // block + 1,))]
     return pl.pallas_call(
-        functools.partial(totals_kernel, rate, block, fetch),
-        in_specs=in_vmem(1) + [pl.BlockSpec(memory_space=pltpu.HBM if fetch else pltpu.VMEM)] * 2,
+        functools.partial(totals_kernel, rate, block, fetch, len(after)),
+        in_specs=in_vmem(1) + [pl.BlockSpec(memory_space=pltpu.HBM if fetch else pltpu.VMEM)] * 2 + in_vmem(len(after)),
         out_specs=in_vmem(len(out_shape)),
         out_shape=out_shape,
         scratch_shapes=scratch,
@@ -148,11 +150,11 @@
             bytes_accessed=2 * n_cells * width,
             transcendentals=n_cells * n_points,
         ),
-    )(points, cells, inverse)
+    )(points, cells, inverse, *after)
 
 
 def goal_kernel(rate, *refs):
-    *stats, goal = refs
+    stats, goal = refs[:4], refs[-1]
     for at in range(4):
         here = [stat[:, (at ^ by) * 128 : ((at ^ by) + 1) * 128] for by, stat in enumerate(stats)]
         top = functools.reduce(jnp.maximum, [s[:1] for s in here])
@@ -173,16 +175,13 @@
 
 
 def factor_kernel(rate, *refs):
-    goals, tops, (factor, top, weight) = refs[:4], refs[4:6], refs[6:]
-    chip = chip_index()
-    for by, goal in enumerate(goals):
-        for at in range(4):
-            spot = pl.ds(pl.multiple_of((at % 2 * 4 + (chip ^ by)) * 128, 128), 128)
-            piece = goal[:, at * 128 : (at + 1) * 128]
-            top[at // 2, :, spot] = piece[:1]
-            weight[at // 2, :, spot] = piece[1:]
+    goals, tops, (factor,) = refs[:4], refs[4:6], refs[6:]
+    rows = goals[0].shape[1] // 2
     for group in range(2):
-        factor[group] = jnp.exp2((tops[group][...] - top[group]) * rate) * weight[group]
+        mine = slice(group * rows, (group + 1) * rows)
+        for at, goal in enumerate(goals):
+            here = slice(at * rows, (at + 1) * rows)
+            factor[group, :, here] = jnp.exp2((tops[group][:, here] - goal[:1, mine]) * rate) * goal[1:, mine]
 
 
 def factor_call(rate, goals, tops):
@@ -192,22 +191,19 @@
         in_specs=in_vmem(6),
         out_specs=in_vmem(1)[0],
         out_shape=jax.ShapeDtypeStruct((2, blocks, n_points), jnp.float32),
-        scratch_shapes=[pltpu.VMEM((2, 1, n_points), jnp.float32)] * 2,
         compiler_params=pltpu.CompilerParams(vmem_limit_bytes=VMEM_BYTES),
     )(*goals, *tops)
 
 
 def expo_kernel(rate, block, *refs):
     pieces, (cells, expo, tops, points) = refs[:4], refs[4:]
-    rows = pieces[0].shape[0] // 2
-    chip, lo = chip_index(), lax.axis_index("lo")
-    for away, piece in zip((0, 1 + lo, 2 - lo, 3), pieces):
-        for at in range(2):
-            spot = pl.ds(pl.multiple_of((at * 4 + (chip ^ away)) * rows, rows), rows)
-            points[spot, :] = piece[at * rows : (at + 1) * rows, :]
+    rows = pieces[0].shape[0]
+    for at, piece in enumerate(pieces):
+        points[at * rows : (at + 1) * rows, :] = piece[...]
     count = expo.shape[0] // block
+    chip = chip_index()
     for part in range(2):
-        some = slice(part * 4 * rows, (part + 1) * 4 * rows)
+        some = slice(part * 2 * rows, (part + 1) * 2 * rows)
         for at in range(count):
             mine = pl.ds(pl.multiple_of((chip * count + at) * block, block), block)
             logits = scores(cells[mine, :], points[some, :])
@@ -288,7 +284,7 @@
     for at in range(count):
         rows = slice(at * block, (at + 1) * block)
         out[rows, :] = here[rows, :] + there[rows, :].astype(jnp.float32)
-        copy(at).start()
+        copy(at).start(priority=at % 2)
     mass[...] = here_mass[...] + there_mass[...]
     for at in range(count):
         copy(at).wait()
@@ -325,21 +321,20 @@
     block = per_device // 3
 
     near_1, near_2, near_3 = (along_z(own, by) for by in (1, 2, 3))
-    near = jnp.concatenate([own, near_1])
-    cells, inverse, stat = totals_call(rate, 2 * block, near, centroids, counters=counters)
-    nears, stats = [near], [stat]
-    near = join(near_2, near_3, stat)
-    nears.append(near)
-    stats += totals_call(rate, 2 * block, near, cells, inverse)
-
-    stat = jnp.concatenate(stats, axis=1)
-    goal = goal_call(rate, stat, *(along_z(stat, by) for by in (1, 2, 3)))
-    goals = [goal] + [around(goal, by) for by in (1, 2, 3)]
+    cells, inverse, stat_0 = totals_call(rate, 2 * block, own, centroids, counters=counters)
+    (stat_1,) = totals_call(rate, 2 * block, near_1, cells, inverse)
+
+    nears = [join(own, near_1, stat_0), join(near_2, near_3, stat_1)]
+    firsts, seconds = [turn(near) for near in nears], [turn_back(near) for near in nears]
+    acrosses = [turn_back(first) for first in firsts]
+
+    (stat_2,) = totals_call(rate, 2 * block, nears[1], cells, inverse, after=(firsts[0], seconds[0]))
+    stat = jnp.concatenate([stat_0, stat_1, stat_2], axis=1)
+    goal = goal_call(rate, stat, *(along_z(stat, by) for by in (1, 2, 3)), acrosses[0])
+    goals = [goal, turn(goal), turn_back(goal), around(goal, 3)]
 
     expos, tops, points = [], [], []
-    for near in nears:
-        first, second = turn(near), turn_back(near)
-        pieces = (near, first, second, turn_back(first))
+    for pieces in zip(nears, firsts, seconds, acrosses):
         expo, top, chunks = expo_call(rate, block, 2 * per_device, pieces, cells)
         expos.append(expo), tops.append(top), points.append(chunks)
     factor = factor_call(rate, goals, tops)
@@ -347,7 +342,7 @@
     there = sums_call(block, 1, per_device, jnp.bfloat16, expos, points, factor)
     there = [exchange(a, ("lo",), lambda at: at ^ 1) for a in there]
     here = sums_call(block, 0, per_device, jnp.float32, expos, points, factor)
-    out, mass = add_call(block, *here, *there)
+    out, mass = add_call(block // 2, *here, *there)
     return (out[None], mass)
 
 

time: 65.3 us -> 58.3 us (0.89)
  waiting for transfers between devices: 16.8 us -> 10.4 us
  starting transfers between devices: 23.1 us -> 21 us
  Pallas kernels: 21.8 us -> 23.3 us
    ppermute x17, waiting for transfers between devices: 16.8 us -> 10.4 us  [exchange(): return lax.ppermute(a, axes, [(partner(at), at) for at in range(count)])]
    ppermute x17, starting transfers between devices: 23.1 us -> 21 us  [exchange(): return lax.ppermute(a, axes, [(partner(at), at) for at in range(count)])]
    pallas_call x3 -> x5, Pallas kernels: 11.6 us -> 13.1 us  [the longest x3 13.1 us: totals_call(): pl.pallas_call(functools.partial(totals_kernel, rate, block, fetch, len(a...]
  transfers between devices with their start and end apart: 17 -> 17, of which waited for: 7 -> 5; matrix products, arithmetic and copies ran while one was open for 0% -> 0% of each run, Pallas kernels for 28% -> 34%
where the time goes in v8:
time: 58.3 us; the launch traced here: 58.1 us
  Pallas kernels  23.3 us (40%)
  starting transfers between devices  21 us (36%)
  waiting for transfers between devices  10.4 us (18%)
  other arithmetic  1.7 us (3%)
  between operations  0.96 us (2%)
  local copies, waits for them, and re-layouts  0.74 us (1%)
    ppermute x17, starting transfers between devices, exchange(): return lax.ppermute(a, axes, [(partner(at), at) for at in range(count)])  21 us
    pallas_call x3, Pallas kernels, totals_call(): pl.pallas_call(functools.partial(totals_kernel, rate, block, fetch, len(a...  13.1 us
    ppermute x17, waiting for transfers between devices, exchange(): return lax.ppermute(a, axes, [(partner(at), at) for at in range(count)])  10.4 us
    pallas_call x2, Pallas kernels, expo_call(): pl.pallas_call(functools.partial(expo_kernel, rate, block), in_specs=in_v...  4.44 us
    pallas_call x2, Pallas kernels, sums_call(): pl.pallas_call(functools.partial(sums_kernel, n, block, side), in_specs=i...  3.96 us
    pallas_call x1, Pallas kernels, add_call(): pl.pallas_call(functools.partial(add_kernel, block), in_specs=in_vmem(4),...  1.79 us
  transfers between devices with their start and end apart: 17, of which 5 were waited for; matrix products, arithmetic and copies ran while one was open for 0% of the time, Pallas kernels for 34%

profile of v8, /device:TPU:0, one launch (start us, length us, event | category | flops | bytes accessed | tf_op | source)
XLA Modules:
  0.0 58.1 jit_solution(15246804318193163107)
XLA Ops:
  0.6 0.7 %convert_multiply_fusion = f32[128]{0:T(128)S(1)} fusion(s32[128]{0:T(128)} %param.5), kind=kLoop, calls=%fused_computation.2 | loop fusion | flops 512 | bytes 1024 | tf_op jit(solution)/shard_map/mul | solution.py:17
  1.3 1.0 %multiply_convert_fusion.points.above = bf16[128,512]{1,0:T(8,128)(2,1)S(1)} fusion(s32[128,512]{1,0:T(8,128)} %param.4, f32[128]{0:T(128)S(1)} %convert_multiply_fusion), kind=kLoop, calls=%fused_computation | loop fusion | flops 196608 | bytes 393728 | tf_op jit(solution)/shard_map/convert_element_type | solution.py:18
  2.3 3.1 %collective-permute-start = (bf16[128,512]{1,0:T(8,128)(2,1)S(1)}, bf16[128,512]{1,0:T(8,128)(2,1)S(1)}, u32[]{:S(2)}, u32[]{:S(2)}) collective-permute-start(bf16[128,512]{1,0:T(8,128)(2,1)S(1)} %multiply_convert_fusion.points.above), channel_id=1, source_target_pairs={{1,0},{0,1},{3,2},{2,3},{5,4},{4,5},{7,6},{6,7},{9,8},{8,9},{11,10... | collective-permute-start | bytes 393224 | tf_op jit(solution)/shard_map/ppermute | solution.py:50
  5.4 2.5 %collective-permute-start.5 = (bf16[128,512]{1,0:T(8,128)(2,1)S(1)}, bf16[128,512]{1,0:T(8,128)(2,1)S(1)}, u32[]{:S(2)}, u32[]{:S(2)}) collective-permute-start(bf16[128,512]{1,0:T(8,128)(2,1)S(1)} %multiply_convert_fusion.points.above), channel_id=1, source_target_pairs={{3,0},{2,1},{1,2},{0,3},{7,4},{6,5},{5,6},{4,7},{11,8},{10,9},{9,1... | collective-permute-start | bytes 393224 | tf_op jit(solution)/shard_map/ppermute | solution.py:50
  7.9 0.1 collective-permute-start.4
  8.0 0.0 copy-start
  8.0 0.7 %copy-done = s32[6144]{0:T(1024)S(1)} copy-done((s32[6144]{0:T(1024)S(1)}, s32[6144]{0:T(1024)}, u32[]{:S(2)}) %copy-start) | copy-done | bytes 24600
  8.8 7.9 %shard_map.59 = (bf16[6144,512]{1,0:T(8,128)(2,1)S(1)}, f32[6144,128]{1,0:T(8,128)S(1)}, f32[3,128]{1,0:T(4,128)S(1)}) custom-call(bf16[128,512]{1,0:T(8,128)(2,1)S(1)} %multiply_convert_fusion.points.above, bf16[6144,512]{1,0:T(8,128)(2,1)} %cells_from.1, s32[48,128]{1,0:T(8,128)S(1)} %bitcast.2), custom_call_target="tpu_custom_call" | custom-call | flops 805306368 | bytes 6291456 | tf_op jit(solution)/shard_map/pallas_call | solution.py:141
  16.6 0.0 collective-permute-done.below.points
  16.7 1.6 %collective-permute-start.1 = (bf16[256,512]{1,0:T(8,128)(2,1)S(1)}, bf16[256,512]{1,0:T(8,128)(2,1)S(1)}, u32[]{:S(2)}, u32[]{:S(2)}) collective-permute-start(bf16[256,512]{1,0:T(8,128)(2,1)S(1)} %shard_map.60.refs_0_), channel_id=1, source_target_pairs={{8,0},{20,4},{0,8},{28,12},{24,16},{4,20},{16,24},{12,28},{9,1},{2... | collective-permute-start | bytes 786440 | tf_op jit(solution)/shard_map/ppermute | solution.py:50
  18.2 2.2 %shard_map.62.refs_0_ = f32[3,128]{1,0:T(4,128)S(1)} custom-call(bf16[128,512]{1,0:T(8,128)(2,1)S(1)} %collective-permute-done.below.points, bf16[6144,512]{1,0:T(8,128)(2,1)S(1)} %get-tuple-element.18.refs_4_.cells_from, f32[6144,128]{1,0:T(8,128)S(1)} %get-tuple-element.20.inverse_from), custom_call_target="tpu_custom_call" | custom-call | flops 805306368 | bytes 6291456 | tf_op jit(solution)/shard_map/pallas_call | solution.py:141
  20.4 0.0 collective-permute-done.5.below
  20.4 0.0 collective-permute-done.4.above
  20.4 0.8 %collective-permute-start.6 = (bf16[256,512]{1,0:T(8,128)(2,1)S(1)}, bf16[256,512]{1,0:T(8,128)(2,1)S(1)}, u32[]{:S(2)}, u32[]{:S(2)}) collective-permute-start(bf16[256,512]{1,0:T(8,128)(2,1)S(1)} %shard_map.63.refs_0_.points), channel_id=1, source_target_pairs={{8,0},{20,4},{0,8},{28,12},{24,16},{4,20},{16,24},{12,28},{9,1},{2... | collective-permute-start | bytes 786440 | tf_op jit(solution)/shard_map/ppermute | solution.py:50
  21.2 1.5 %collective-permute-start.2 = (bf16[256,512]{1,0:T(8,128)(2,1)S(1)}, bf16[256,512]{1,0:T(8,128)(2,1)S(1)}, u32[]{:S(2)}, u32[]{:S(2)}) collective-permute-start(bf16[256,512]{1,0:T(8,128)(2,1)S(1)} %shard_map.60.refs_0_), channel_id=1, source_target_pairs={{16,0},{12,4},{24,8},{4,12},{0,16},{28,20},{8,24},{20,28},{17,1},{... | collective-permute-start | bytes 786440 | tf_op jit(solution)/shard_map/ppermute | solution.py:50
  22.7 0.5 collective-permute-start.7
  23.3 0.1 collective-permute-done.1.refs_1_.refs_0_
  23.3 1.9 %collective-permute-start.3 = (bf16[256,512]{1,0:T(8,128)(2,1)S(1)}, bf16[256,512]{1,0:T(8,128)(2,1)S(1)}, u32[]{:S(2)}, u32[]{:S(2)}) collective-permute-start(bf16[256,512]{1,0:T(8,128)(2,1)S(1)} %collective-permute-done.1.refs_1_.refs_0_), channel_id=1, source_target_pairs={{16,0},{12,4},{24,8},{4,12},{0,16},{28,20},{8,24},{20,28},{17,1},{... | collective-permute-start | bytes 786440 | tf_op jit(solution)/shard_map/ppermute | solution.py:50
  25.3 4.5 %collective-permute-done.6.refs_1_ = bf16[256,512]{1,0:T(8,128)(2,1)S(1)} collective-permute-done((bf16[256,512]{1,0:T(8,128)(2,1)S(1)}, bf16[256,512]{1,0:T(8,128)(2,1)S(1)}, u32[]{:S(2)}, u32[]{:S(2)}) %collective-permute-start.6) | collective-permute-done | bytes 262176 | tf_op jit(solution)/shard_map/ppermute | solution.py:50
  29.7 1.5 %collective-permute-start.8 = (bf16[256,512]{1,0:T(8,128)(2,1)S(1)}, bf16[256,512]{1,0:T(8,128)(2,1)S(1)}, u32[]{:S(2)}, u32[]{:S(2)}) collective-permute-start(bf16[256,512]{1,0:T(8,128)(2,1)S(1)} %collective-permute-done.6.refs_1_), channel_id=1, source_target_pairs={{16,0},{12,4},{24,8},{4,12},{0,16},{28,20},{8,24},{20,28},{17,1},{... | collective-permute-start | bytes 786440 | tf_op jit(solution)/shard_map/ppermute | solution.py:50
  31.3 0.0 collective-permute-done.2.refs_2_.refs_1_
  31.3 3.0 %shard_map.65 = f32[3,256]{1,0:T(4,128)S(1)} custom-call(bf16[256,512]{1,0:T(8,128)(2,1)S(1)} %shard_map.63.refs_0_.points, bf16[6144,512]{1,0:T(8,128)(2,1)S(1)} %get-tuple-element.18.refs_4_.cells_from, f32[6144,128]{1,0:T(8,128)S(1)} %get-tuple-element.20.inverse_from, bf16[256,512]{1,0:T(8,128)(2,1)S(1)} %collective-permute-done.1.refs_1_.refs_0_, ...), custom_call_target="tpu_custom_call" | custom-call | flops 1610612736 | bytes 6291456 | tf_op jit(solution)/shard_map/pallas_call | solution.py:141
  34.3 3.0 %collective-permute-start.11 = (f32[3,512]{1,0:T(4,128)S(1)}, f32[3,512]{1,0:T(4,128)S(1)}, u32[]{:S(2)}, u32[]{:S(2)}) collective-permute-start(f32[3,512]{1,0:T(4,128)S(1)} %pad_maximum_fusion.refs_0_), channel_id=1, source_target_pairs={{3,0},{2,1},{1,2},{0,3},{7,4},{6,5},{5,6},{4,7},{11,8},{10,9},{9,1... | collective-permute-start | bytes 18440 | tf_op jit(solution)/shard_map/ppermute | solution.py:50
  37.3 0.3 collective-permute-start.10
  37.6 2.2 %collective-permute-done.11.refs_3_ = f32[3,512]{1,0:T(4,128)S(1)} collective-permute-done((f32[3,512]{1,0:T(4,128)S(1)}, f32[3,512]{1,0:T(4,128)S(1)}, u32[]{:S(2)}, u32[]{:S(2)}) %collective-permute-start.11) | collective-permute-done | bytes 6176 | tf_op jit(solution)/shard_map/ppermute | solution.py:50
  39.8 0.0 collective-permute-start.9
  39.8 2.0 %collective-permute-done.10.refs_2_ = f32[3,512]{1,0:T(4,128)S(1)} collective-permute-done((f32[3,512]{1,0:T(4,128)S(1)}, f32[3,512]{1,0:T(4,128)S(1)}, u32[]{:S(2)}, u32[]{:S(2)}) %collective-permute-start.10) | collective-permute-done | bytes 6176 | tf_op jit(solution)/shard_map/ppermute | solution.py:50
  41.8 1.6 %collective-permute-done.9.refs_1_ = f32[3,512]{1,0:T(4,128)S(1)} collective-permute-done((f32[3,512]{1,0:T(4,128)S(1)}, f32[3,512]{1,0:T(4,128)S(1)}, u32[]{:S(2)}, u32[]{:S(2)}) %collective-permute-start.9) | collective-permute-done | bytes 6176 | tf_op jit(solution)/shard_map/ppermute | solution.py:50
  43.5 0.0 collective-permute-done.3.refs_3_.refs_4_
  43.5 0.7 %collective-permute-start.14 = (f32[2,512]{1,0:T(2,128)S(1)}, f32[2,512]{1,0:T(2,128)S(1)}, u32[]{:S(2)}, u32[]{:S(2)}) collective-permute-start(f32[2,512]{1,0:T(2,128)S(1)} %shard_map.66.refs_0_), channel_id=1, source_target_pairs={{24,0},{16,8},{8,16},{0,24},{25,1},{17,9},{9,17},{1,25},{26,2},{18... | collective-permute-start | bytes 12296 | tf_op jit(solution)/shard_map/ppermute | solution.py:50
  44.2 1.9 %collective-permute-start.13 = (f32[2,512]{1,0:T(2,128)S(1)}, f32[2,512]{1,0:T(2,128)S(1)}, u32[]{:S(2)}, u32[]{:S(2)}) collective-permute-start(f32[2,512]{1,0:T(2,128)S(1)} %shard_map.66.refs_0_), channel_id=1, source_target_pairs={{16,0},{12,4},{24,8},{4,12},{0,16},{28,20},{8,24},{20,28},{17,1},{... | collective-permute-start | bytes 12296 | tf_op jit(solution)/shard_map/ppermute | solution.py:50
  46.2 0.9 %collective-permute-start.12 = (f32[2,512]{1,0:T(2,128)S(1)}, f32[2,512]{1,0:T(2,128)S(1)}, u32[]{:S(2)}, u32[]{:S(2)}) collective-permute-start(f32[2,512]{1,0:T(2,128)S(1)} %shard_map.66.refs_0_), channel_id=1, source_target_pairs={{8,0},{20,4},{0,8},{28,12},{24,16},{4,20},{16,24},{12,28},{9,1},{2... | collective-permute-start | bytes 12296 | tf_op jit(solution)/shard_map/ppermute | solution.py:50
  47.1 2.1 %shard_map.61 = (bf16[1536,1024]{1,0:T(8,128)(2,1)S(1)}, f32[6,1024]{1,0:T(8,128)S(1)}, bf16[1024,512]{1,0:T(8,128)(2,1)S(1)}) custom-call(bf16[256,512]{1,0:T(8,128)(2,1)S(1)} %shard_map.60.refs_0_, bf16[256,512]{1,0:T(8,128)(2,1)S(1)} %collective-permute-done.1.refs_1_.refs_0_, bf16[256,512]{1,0:T(8,128)(2,1)S(1)} %collective-permute-done.2.refs_2_.refs_1_, ...), custom_call_target="tpu_custom_call" | custom-call | flops 1610612736 | bytes 5767168 | tf_op jit(solution)/shard_map/pallas_call | solution.py:218
  49.2 0.0 collective-permute-done.7.refs_2_
  49.2 0.0 collective-permute-done.8.refs_3_
  49.2 2.3 %shard_map.64 = (bf16[1536,1024]{1,0:T(8,128)(2,1)S(1)}, f32[6,1024]{1,0:T(8,128)S(1)}, bf16[1024,512]{1,0:T(8,128)(2,1)S(1)}) custom-call(bf16[256,512]{1,0:T(8,128)(2,1)S(1)} %shard_map.63.refs_0_.points, bf16[256,512]{1,0:T(8,128)(2,1)S(1)} %collective-permute-done.6.refs_1_, bf16[256,512]{1,0:T(8,128)(2,1)S(1)} %collective-permute-done.7.refs_2_, ...), custom_call_target="tpu_custom_call" | custom-call | flops 1610612736 | bytes 5767168 | tf_op jit(solution)/shard_map/pallas_call | solution.py:218
  51.5 0.0 collective-permute-done.14.refs_3_
  51.6 0.0 collective-permute-done.13.refs_2_
  51.6 0.0 collective-permute-done.12.refs_1_
  51.6 2.0 %shard_map.69 = (bf16[768,512]{1,0:T(8,128)(2,1)S(1)}, f32[1,768]{1,0:T(1,128)S(1)}) custom-call(bf16[1536,1024]{1,0:T(8,128)(2,1)S(1)} %get-tuple-element.19.refs_0_, bf16[1536,1024]{1,0:T(8,128)(2,1)S(1)} %get-tuple-element.21.refs_1_, bf16[1024,512]{1,0:T(8,128)(2,1)S(1)} %get-tuple-element.22.refs_2_, bf16[1024,512]{1,0:T(8,128)(2,1)S(1)} %get-tuple-element.23.refs_3_, ...), custom_call_target="tpu_custom_call" | custom-call | flops 1610612736 | bytes 6815744 | tf_op jit(solution)/shard_map/pallas_call | solution.py:264
  53.6 0.1 collective-permute-start.15
  53.7 0.5 collective-permute-start.16
  54.2 2.0 %shard_map.68 = (f32[768,512]{1,0:T(8,128)S(1)}, f32[1,768]{1,0:T(1,128)S(1)}) custom-call(bf16[1536,1024]{1,0:T(8,128)(2,1)S(1)} %get-tuple-element.19.refs_0_, bf16[1536,1024]{1,0:T(8,128)(2,1)S(1)} %get-tuple-element.21.refs_1_, bf16[1024,512]{1,0:T(8,128)(2,1)S(1)} %get-tuple-element.22.refs_2_, bf16[1024,512]{1,0:T(8,128)(2,1)S(1)} %get-tuple-element.23.refs_3_, ...), custom_call_target="tpu_custom_call" | custom-call | flops 1610612736 | bytes 6815744 | tf_op jit(solution)/shard_map/pallas_call | solution.py:264
  56.1 0.0 collective-permute-done.16.there_mass
  56.2 0.0 collective-permute-done.15.there
  56.2 1.8 %shard_map.70 = (f32[768,512]{1,0:T(8,128)}, f32[1,768]{1,0:T(1,128)}) custom-call(f32[768,512]{1,0:T(8,128)S(1)} %get-tuple-element.26.here, f32[1,768]{1,0:T(1,128)S(1)} %get-tuple-element.27.here_mass, bf16[768,512]{1,0:T(8,128)(2,1)S(1)} %collective-permute-done.15.there, f32[1,768]{1,0:T(1,128)S(1)} %collective-permute-done.16.there_mass), custom_call_target="tpu_custom_call" | custom-call | tf_op jit(solution)/shard_map/pallas_call | solution.py:294
  (5 shorter events, 0.1 us)
Async XLA Ops:
  2.3 14.3 %collective-permute-start = (bf16[128,512]{1,0:T(8,128)(2,1)S(1)}, bf16[128,512]{1,0:T(8,128)(2,1)S(1)}, u32[]{:S(2)}, u32[]{:S(2)}) collective-permute-start(bf16[128,512]{1,0:T(8,128)(2,1)S(1)} %multiply_convert_fusion.points.above), channel_id=1, source_target_pairs={{1,0},{0,1},{3,2},{2,3},{5,4},{4,5},{7,6},{6,7},{9,8},{8,9},{11,10... | collective-permute-start | bytes 393224 | tf_op jit(solution)/shard_map/ppermute | solution.py:50
  5.4 15.0 %collective-permute-start.5 = (bf16[128,512]{1,0:T(8,128)(2,1)S(1)}, bf16[128,512]{1,0:T(8,128)(2,1)S(1)}, u32[]{:S(2)}, u32[]{:S(2)}) collective-permute-start(bf16[128,512]{1,0:T(8,128)(2,1)S(1)} %multiply_convert_fusion.points.above), channel_id=1, source_target_pairs={{3,0},{2,1},{1,2},{0,3},{7,4},{6,5},{5,6},{4,7},{11,8},{10,9},{9,1... | collective-permute-start | bytes 393224 | tf_op jit(solution)/shard_map/ppermute | solution.py:50
  7.9 12.5 %collective-permute-start.4 = (bf16[128,512]{1,0:T(8,128)(2,1)S(1)}, bf16[128,512]{1,0:T(8,128)(2,1)S(1)}, u32[]{:S(2)}, u32[]{:S(2)}) collective-permute-start(bf16[128,512]{1,0:T(8,128)(2,1)S(1)} %multiply_convert_fusion.points.above), channel_id=1, source_target_pairs={{2,0},{3,1},{0,2},{1,3},{6,4},{7,5},{4,6},{5,7},{10,8},{11,9},{8,1... | collective-permute-start | bytes 393224 | tf_op jit(solution)/shard_map/ppermute | solution.py:50
  8.0 0.7 %copy-start = (s32[6144]{0:T(1024)S(1)}, s32[6144]{0:T(1024)}, u32[]{:S(2)}) copy-start(s32[6144]{0:T(1024)} %param.7) | copy-start | bytes 73732
  16.7 6.7 %collective-permute-start.1 = (bf16[256,512]{1,0:T(8,128)(2,1)S(1)}, bf16[256,512]{1,0:T(8,128)(2,1)S(1)}, u32[]{:S(2)}, u32[]{:S(2)}) collective-permute-start(bf16[256,512]{1,0:T(8,128)(2,1)S(1)} %shard_map.60.refs_0_), channel_id=1, source_target_pairs={{8,0},{20,4},{0,8},{28,12},{24,16},{4,20},{16,24},{12,28},{9,1},{2... | collective-permute-start | bytes 786440 | tf_op jit(solution)/shard_map/ppermute | solution.py:50
  20.4 9.3 %collective-permute-start.6 = (bf16[256,512]{1,0:T(8,128)(2,1)S(1)}, bf16[256,512]{1,0:T(8,128)(2,1)S(1)}, u32[]{:S(2)}, u32[]{:S(2)}) collective-permute-start(bf16[256,512]{1,0:T(8,128)(2,1)S(1)} %shard_map.63.refs_0_.points), channel_id=1, source_target_pairs={{8,0},{20,4},{0,8},{28,12},{24,16},{4,20},{16,24},{12,28},{9,1},{2... | collective-permute-start | bytes 786440 | tf_op jit(solution)/shard_map/ppermute | solution.py:50
  21.2 10.0 %collective-permute-start.2 = (bf16[256,512]{1,0:T(8,128)(2,1)S(1)}, bf16[256,512]{1,0:T(8,128)(2,1)S(1)}, u32[]{:S(2)}, u32[]{:S(2)}) collective-permute-start(bf16[256,512]{1,0:T(8,128)(2,1)S(1)} %shard_map.60.refs_0_), channel_id=1, source_target_pairs={{16,0},{12,4},{24,8},{4,12},{0,16},{28,20},{8,24},{20,28},{17,1},{... | collective-permute-start | bytes 786440 | tf_op jit(solution)/shard_map/ppermute | solution.py:50
  22.7 26.5 %collective-permute-start.7 = (bf16[256,512]{1,0:T(8,128)(2,1)S(1)}, bf16[256,512]{1,0:T(8,128)(2,1)S(1)}, u32[]{:S(2)}, u32[]{:S(2)}) collective-permute-start(bf16[256,512]{1,0:T(8,128)(2,1)S(1)} %shard_map.63.refs_0_.points), channel_id=1, source_target_pairs={{16,0},{12,4},{24,8},{4,12},{0,16},{28,20},{8,24},{20,28},{17,1},{... | collective-permute-start | bytes 786440 | tf_op jit(solution)/shard_map/ppermute | solution.py:50
  23.3 20.1 %collective-permute-start.3 = (bf16[256,512]{1,0:T(8,128)(2,1)S(1)}, bf16[256,512]{1,0:T(8,128)(2,1)S(1)}, u32[]{:S(2)}, u32[]{:S(2)}) collective-permute-start(bf16[256,512]{1,0:T(8,128)(2,1)S(1)} %collective-permute-done.1.refs_1_.refs_0_), channel_id=1, source_target_pairs={{16,0},{12,4},{24,8},{4,12},{0,16},{28,20},{8,24},{20,28},{17,1},{... | collective-permute-start | bytes 786440 | tf_op jit(solution)/shard_map/ppermute | solution.py:50
  29.7 19.5 %collective-permute-start.8 = (bf16[256,512]{1,0:T(8,128)(2,1)S(1)}, bf16[256,512]{1,0:T(8,128)(2,1)S(1)}, u32[]{:S(2)}, u32[]{:S(2)}) collective-permute-start(bf16[256,512]{1,0:T(8,128)(2,1)S(1)} %collective-permute-done.6.refs_1_), channel_id=1, source_target_pairs={{16,0},{12,4},{24,8},{4,12},{0,16},{28,20},{8,24},{20,28},{17,1},{... | collective-permute-start | bytes 786440 | tf_op jit(solution)/shard_map/ppermute | solution.py:50
  34.3 5.5 %collective-permute-start.11 = (f32[3,512]{1,0:T(4,128)S(1)}, f32[3,512]{1,0:T(4,128)S(1)}, u32[]{:S(2)}, u32[]{:S(2)}) collective-permute-start(f32[3,512]{1,0:T(4,128)S(1)} %pad_maximum_fusion.refs_0_), channel_id=1, source_target_pairs={{3,0},{2,1},{1,2},{0,3},{7,4},{6,5},{5,6},{4,7},{11,8},{10,9},{9,1... | collective-permute-start | bytes 18440 | tf_op jit(solution)/shard_map/ppermute | solution.py:50
  37.3 4.5 %collective-permute-start.10 = (f32[3,512]{1,0:T(4,128)S(1)}, f32[3,512]{1,0:T(4,128)S(1)}, u32[]{:S(2)}, u32[]{:S(2)}) collective-permute-start(f32[3,512]{1,0:T(4,128)S(1)} %pad_maximum_fusion.refs_0_), channel_id=1, source_target_pairs={{2,0},{3,1},{0,2},{1,3},{6,4},{7,5},{4,6},{5,7},{10,8},{11,9},{8,1... | collective-permute-start | bytes 18440 | tf_op jit(solution)/shard_map/ppermute | solution.py:50
  39.8 3.7 %collective-permute-start.9 = (f32[3,512]{1,0:T(4,128)S(1)}, f32[3,512]{1,0:T(4,128)S(1)}, u32[]{:S(2)}, u32[]{:S(2)}) collective-permute-start(f32[3,512]{1,0:T(4,128)S(1)} %pad_maximum_fusion.refs_0_), channel_id=1, source_target_pairs={{1,0},{0,1},{3,2},{2,3},{5,4},{4,5},{7,6},{6,7},{9,8},{8,9},{11,10... | collective-permute-start | bytes 18440 | tf_op jit(solution)/shard_map/ppermute | solution.py:50
  43.5 8.0 %collective-permute-start.14 = (f32[2,512]{1,0:T(2,128)S(1)}, f32[2,512]{1,0:T(2,128)S(1)}, u32[]{:S(2)}, u32[]{:S(2)}) collective-permute-start(f32[2,512]{1,0:T(2,128)S(1)} %shard_map.66.refs_0_), channel_id=1, source_target_pairs={{24,0},{16,8},{8,16},{0,24},{25,1},{17,9},{9,17},{1,25},{26,2},{18... | collective-permute-start | bytes 12296 | tf_op jit(solution)/shard_map/ppermute | solution.py:50
  44.2 7.3 %collective-permute-start.13 = (f32[2,512]{1,0:T(2,128)S(1)}, f32[2,512]{1,0:T(2,128)S(1)}, u32[]{:S(2)}, u32[]{:S(2)}) collective-permute-start(f32[2,512]{1,0:T(2,128)S(1)} %shard_map.66.refs_0_), channel_id=1, source_target_pairs={{16,0},{12,4},{24,8},{4,12},{0,16},{28,20},{8,24},{20,28},{17,1},{... | collective-permute-start | bytes 12296 | tf_op jit(solution)/shard_map/ppermute | solution.py:50
  46.2 5.4 %collective-permute-start.12 = (f32[2,512]{1,0:T(2,128)S(1)}, f32[2,512]{1,0:T(2,128)S(1)}, u32[]{:S(2)}, u32[]{:S(2)}) collective-permute-start(f32[2,512]{1,0:T(2,128)S(1)} %shard_map.66.refs_0_), channel_id=1, source_target_pairs={{8,0},{20,4},{0,8},{28,12},{24,16},{4,20},{16,24},{12,28},{9,1},{2... | collective-permute-start | bytes 12296 | tf_op jit(solution)/shard_map/ppermute | solution.py:50
  53.6 2.6 %collective-permute-start.15 = (bf16[768,512]{1,0:T(8,128)(2,1)S(1)}, bf16[768,512]{1,0:T(8,128)(2,1)S(1)}, u32[]{:S(2)}, u32[]{:S(2)}) collective-permute-start(bf16[768,512]{1,0:T(8,128)(2,1)S(1)} %get-tuple-element.28), channel_id=1, source_target_pairs={{4,0},{0,4},{5,1},{1,5},{6,2},{2,6},{7,3},{3,7},{12,8},{8,12},{13,... | collective-permute-start | bytes 2359304 | tf_op jit(solution)/shard_map/ppermute | solution.py:50
  53.7 2.5 %collective-permute-start.16 = (f32[1,768]{1,0:T(1,128)S(1)}, f32[1,768]{1,0:T(1,128)S(1)}, u32[]{:S(2)}, u32[]{:S(2)}) collective-permute-start(f32[1,768]{1,0:T(1,128)S(1)} %get-tuple-element.29), channel_id=1, source_target_pairs={{4,0},{0,4},{5,1},{1,5},{6,2},{2,6},{7,3},{3,7},{12,8},{8,12},{13,... | collective-permute-start | bytes 9224 | tf_op jit(solution)/shard_map/ppermute | solution.py:50

commit v9 on v8

v9 whole, which is shorter than its diff:
```python
import functools
import math

import jax
import jax.numpy as jnp
from jax import lax
from jax.experimental import pallas as pl
from jax.experimental.pallas import tpu as pltpu
from jax.sharding import Mesh, PartitionSpec as P

GATHER_BYTES = 8 << 20
VMEM_BYTES = 16 << 20


def to_points(codes, exponents):
    scale = lax.shift_left(jnp.ones_like(exponents), 16 - exponents).astype(jnp.float32) * 2.0**-16
    return (codes.astype(jnp.float32) * scale[:, None]).astype(jnp.bfloat16)


def split_points(codes, exponents, centroids, counters):
    local_rows = to_points(codes, exponents)
    points = lax.all_gather(local_rows, "cells", axis=0, tiled=True)
    beta = 4.0 / math.sqrt(points.shape[1])
    logits = (
        lax.dot_general(
            points, centroids, (((1,), (1,)), ((), ())), preferred_element_type=jnp.float32
        )
        * beta
    )
    inverse = lax.rsqrt(counters.astype(jnp.float32) + 1.0)
    top = lax.pmax(jnp.max(logits, axis=1), "cells")
    expo = jnp.exp(logits - top[:, None])
    total, novel = lax.psum(
        (jnp.sum(expo, axis=1), jnp.dot(expo, inverse, preferred_element_type=jnp.float32)), "cells"
    )
    weight = novel / total
    share = (expo * (weight / total)[:, None]).astype(jnp.bfloat16)
    mass_local = jnp.sum(share.astype(jnp.float32), axis=0)
    sums_local = lax.dot_general(
        share, points, (((0,), (0,)), ((), ())), preferred_element_type=jnp.float32
    )
    sums = lax.psum_scatter(sums_local, "pts", scatter_dimension=0, tiled=True)
    mass = lax.psum_scatter(mass_local, "pts", scatter_dimension=0, tiled=True)
    return (sums[None], mass[None])


def exchange(a, axes, partner):
    count = math.prod(lax.axis_size(axis) for axis in axes)
    return lax.ppermute(a, axes, [(partner(at), at) for at in range(count)])


def in_vmem(n):
    return [pl.BlockSpec(memory_space=pltpu.VMEM)] * n


def join(above, below, *after):
    def kernel(above, below, *refs):
        out = refs[-1]
        out[: above.shape[0], :] = above[...]
        out[above.shape[0] :, :] = below[...]

    return pl.pallas_call(
        kernel,
        in_specs=in_vmem(2 + len(after)),
        out_specs=in_vmem(1)[0],
        out_shape=jax.ShapeDtypeStruct((above.shape[0] + below.shape[0], above.shape[1]), above.dtype),
        compiler_params=pltpu.CompilerParams(vmem_limit_bytes=VMEM_BYTES),
    )(above, below, *after)


def hold(a, after):
    def kernel(a, after, out):
        out[...] = a[...]

    return pl.pallas_call(
        kernel,
        in_specs=in_vmem(2),
        out_specs=in_vmem(1)[0],
        out_shape=jax.ShapeDtypeStruct(a.shape, a.dtype),
        compiler_params=pltpu.CompilerParams(vmem_limit_bytes=VMEM_BYTES),
    )(a, after)


def scores(cells, points):
    return lax.dot_general(cells, points, (((1,), (1,)), ((), ())), preferred_element_type=jnp.float32)


def chip_index():
    return lax.axis_index("y") * 2 + lax.axis_index("x")


def inverse_kernel(counters, inverse):
    for line in range(counters.shape[0]):
        row = lax.rsqrt(counters[line : line + 1, :].astype(jnp.float32) + 1.0)
        inverse[line * 128 : (line + 1) * 128, :] = jnp.broadcast_to(row, (128, 128)).T


def inverse_call(counters):
    return pl.pallas_call(
        inverse_kernel,
        in_specs=in_vmem(1),
        out_specs=in_vmem(1)[0],
        out_shape=jax.ShapeDtypeStruct((counters.shape[0], 128), jnp.float32),
        compiler_params=pltpu.CompilerParams(vmem_limit_bytes=VMEM_BYTES),
    )(counters.reshape(-1, 128))


def totals_kernel(rate, block, points, low, high, inverse, *refs):
    stats = refs[-1]
    every = points[...]
    half, count = low.shape[0], inverse.shape[0]
    parts = []
    for at in range(0, count, block):
        here = slice(at, at + block)
        cells = low[here, :] if at < half else high[at - half : at - half + block, :]
        logits = scores(cells, every)
        top = jnp.max(logits, axis=0, keepdims=True)
        value = jnp.exp2((logits - top) * rate)
        scale = inverse[here, :]
        weighed = [
            jnp.sum(value[:, i : i + 128] * scale, axis=0, keepdims=True) for i in range(0, value.shape[1], 128)
        ]
        parts.append((top, jnp.sum(value, axis=0, keepdims=True), jnp.concatenate(weighed, axis=1)))
        while len(parts) > 1 and (at + block == count or len(parts) == 4):
            parts = [join_stats(rate, parts)]
    stats[...] = jnp.concatenate(parts[0], axis=0)


def join_stats(rate, parts):
    top = functools.reduce(jnp.maximum, [part[0] for part in parts])
    scales = [jnp.exp2((part[0] - top) * rate) for part in parts]
    return (top, *(sum(part[at] * scale for part, scale in zip(parts, scales)) for at in (1, 2)))


def totals_call(rate, block, points, halves, inverse, after=()):
    n_points, width = points.shape
    n_cells = inverse.shape[0]
    return pl.pallas_call(
        functools.partial(totals_kernel, rate, block),
        in_specs=in_vmem(4 + len(after)),
        out_specs=in_vmem(1)[0],
        out_shape=jax.ShapeDtypeStruct((3, n_points), jnp.float32),
        compiler_params=pltpu.CompilerParams(vmem_limit_bytes=VMEM_BYTES),
        cost_estimate=pl.CostEstimate(
            flops=2 * n_cells * n_points * width,
            bytes_accessed=2 * n_cells * width,
            transcendentals=n_cells * n_points,
        ),
    )(points, *halves, inverse, *after)


def goal_kernel(rate, *refs):
    stats, goal = refs[:4], refs[-1]
    for at in range(4):
        here = [stat[:, (at ^ by) * 128 : ((at ^ by) + 1) * 128] for by, stat in enumerate(stats)]
        top, total, novel = join_stats(rate, [(s[:1], s[1:2], s[2:]) for s in here])
        goal[:, at * 128 : (at + 1) * 128] = jnp.concatenate([top, novel / total / total], axis=0)


def goal_call(rate, *stats):
    return pl.pallas_call(
        functools.partial(goal_kernel, rate),
        in_specs=in_vmem(len(stats)),
        out_specs=in_vmem(1)[0],
        out_shape=jax.ShapeDtypeStruct((2, stats[0].shape[1]), jnp.float32),
        compiler_params=pltpu.CompilerParams(vmem_limit_bytes=VMEM_BYTES),
    )(*stats)


def factor_kernel(rate, *refs):
    goals, tops, factors = refs[:4], refs[4:6], refs[6:]
    rows = goals[0].shape[1] // 2
    for group in range(2):
        mine = slice(group * rows, (group + 1) * rows)
        for at, goal in enumerate(goals):
            here = slice(at * rows, (at + 1) * rows)
            factors[group][:, here] = jnp.exp2((tops[group][:, here] - goal[:1, mine]) * rate) * goal[1:, mine]


def factor_call(rate, goals, tops):
    return pl.pallas_call(
        functools.partial(factor_kernel, rate),
        in_specs=in_vmem(6),
        out_specs=in_vmem(2),
        out_shape=[jax.ShapeDtypeStruct(top.shape, jnp.float32) for top in tops],
        compiler_params=pltpu.CompilerParams(vmem_limit_bytes=VMEM_BYTES),
    )(*goals, *tops)


def expo_kernel(rate, block, *refs):
    pieces, (cells, expo, tops, points) = refs[:-4], refs[-4:]
    start = 0
    for piece in pieces:
        points[start : start + piece.shape[0], :] = piece[...]
        start += piece.shape[0]
    count = expo.shape[0] // block
    chip = chip_index()
    for at in range(count):
        mine = pl.ds(pl.multiple_of((chip * count + at) * block, block), block)
        for part in range(0, points.shape[0], 256):
            some = slice(part, part + 256)
            logits = scores(cells[mine, :], points[some, :])
            top = jnp.max(logits, axis=0, keepdims=True)
            expo[at * block : (at + 1) * block, some] = jnp.exp2((logits - top) * rate).astype(jnp.bfloat16)
            tops[at : at + 1, some] = top


def expo_call(rate, block, count, pieces, cells):
    width = cells.shape[1]
    n_points = sum(piece.shape[0] for piece in pieces)
    return pl.pallas_call(
        functools.partial(expo_kernel, rate, block),
        in_specs=in_vmem(len(pieces) + 1),
        out_specs=in_vmem(3),
        out_shape=[
            jax.ShapeDtypeStruct((count, n_points), jnp.bfloat16),
            jax.ShapeDtypeStruct((count // block, n_points), jnp.float32),
            jax.ShapeDtypeStruct((n_points, width), jnp.bfloat16),
        ],
        compiler_params=pltpu.CompilerParams(vmem_limit_bytes=VMEM_BYTES),
        cost_estimate=pl.CostEstimate(
            flops=2 * count * n_points * width,
            bytes_accessed=2 * (count * width + n_points * width + count * n_points),
            transcendentals=count * n_points,
        ),
    )(*pieces, cells)


def weighed_sums(start, count, expos, points, factors):
    total = weight = None
    for expo, chunk, factor in zip(expos, points, factors):
        block = expo.shape[0] // factor.shape[0]
        shares = []
        for at in range(0, count, block):
            here = pl.ds(pl.multiple_of(start + at, block), block)
            scale = factor[pl.ds((start + at) // block, 1), :]
            shares.append((expo[here, :].astype(jnp.float32) * scale).astype(jnp.bfloat16))
        share = jnp.concatenate(shares, axis=0)
        part = jnp.dot(share, chunk[...], preferred_element_type=jnp.float32)
        wide = share.astype(jnp.float32)
        lanes = sum(wide[:, i : i + 128] for i in range(0, wide.shape[1], 128))
        total = part if total is None else total + part
        weight = lanes if weight is None else weight + lanes
    return total, jnp.sum(weight.T, axis=0, keepdims=True)


def sums_kernel(n, block, side, *refs):
    expos, points, factors, (sums, mass) = refs[:n], refs[n : 2 * n], refs[2 * n : 3 * n], refs[3 * n :]
    rows = sums.shape[0]
    first = (lax.axis_index("lo") ^ side) * rows
    for at in range(0, rows, block):
        here = slice(at, at + block)
        total, weight = weighed_sums(first + at, block, expos, points, factors)
        sums[here, :] = total.astype(sums.dtype)
        mass[:, here] = weight


def sums_call(block, side, rows, dtype, expos, points, factors):
    n = len(expos)
    n_points, width = points[0].shape
    return pl.pallas_call(
        functools.partial(sums_kernel, n, block, side),
        in_specs=in_vmem(3 * n),
        out_specs=in_vmem(2),
        out_shape=[jax.ShapeDtypeStruct((rows, width), dtype), jax.ShapeDtypeStruct((1, rows), jnp.float32)],
        compiler_params=pltpu.CompilerParams(vmem_limit_bytes=VMEM_BYTES),
        cost_estimate=pl.CostEstimate(
            flops=2 * rows * n * n_points * width,
            bytes_accessed=2 * n * n_points * (rows + width) + 4 * rows * width,
            transcendentals=0,
        ),
    )(*expos, *points, *factors)


def add_kernel(block, here, here_mass, there, there_mass, sums, mass, out, left):
    def copy(at):
        rows = pl.ds(at * block, block)
        return pltpu.make_async_copy(out.at[rows, :], sums.at[rows, :], left.at[at])

    count = here.shape[0] // block
    for at in range(count):
        rows = slice(at * block, (at + 1) * block)
        out[rows, :] = here[rows, :] + there[rows, :].astype(jnp.float32)
        copy(at).start(priority=at % 2)
    mass[...] = here_mass[...] + there_mass[...]
    for at in range(count):
        copy(at).wait()


def add_call(block, here, here_mass, there, there_mass):
    return pl.pallas_call(
        functools.partial(add_kernel, block),
        in_specs=in_vmem(4),
        out_specs=[pl.BlockSpec(memory_space=pltpu.HBM)] + in_vmem(1),
        out_shape=[
            jax.ShapeDtypeStruct(here.shape, jnp.float32),
            jax.ShapeDtypeStruct(here_mass.shape, jnp.float32),
        ],
        scratch_shapes=[
            pltpu.VMEM(here.shape, jnp.float32),
            pltpu.SemaphoreType.DMA((here.shape[0] // block,)),
        ],
        compiler_params=pltpu.CompilerParams(vmem_limit_bytes=VMEM_BYTES),
    )(here, here_mass, there, there_mass)


def split_cells(codes, exponents, centroids, counters):
    own = to_points(codes, exponents)
    rate = 4.0 / math.sqrt(own.shape[1]) * math.log2(math.e)
    plane = ("y", "x", "lo")

    turn = lambda a: exchange(a, plane, lambda at: at ^ (4 if at % 2 else 2))
    turn_back = lambda a: exchange(a, plane, lambda at: at ^ (2 if at % 2 else 4))
    along_z = lambda a, by: exchange(a, ("cells",), lambda at: at ^ by)
    around = lambda a, by: exchange(a, ("y", "x"), lambda at: at ^ by)

    per_device = centroids.shape[0] // 8
    block = per_device // 3

    near_1, near_2, near_3 = (along_z(own, by) for by in (1, 2, 3))
    inverse = inverse_call(counters)
    halves = jnp.split(centroids, 2)
    near = join(own, near_1)
    stats = [totals_call(rate, 128, near, halves, inverse)]
    nears = [near, join(near_2, near_3, *stats)]
    firsts = [turn(near) for near in nears]
    stats.append(totals_call(rate, 256, nears[1], halves, inverse, after=firsts[:1]))
    seconds = [[turn_back(join(nears[0], firsts[0]))], [turn_back(nears[1]), turn_back(hold(firsts[1], stats[1]))]]

    stat = jnp.concatenate(stats, axis=1)
    goal = goal_call(rate, stat, *(along_z(stat, by) for by in (1, 2, 3)))
    goals = [goal, turn(goal), turn_back(goal), around(goal, 3)]

    expos, tops, points = [], [], []
    for cells, near, first, second in zip((128, 256), nears, firsts, seconds):
        expo, top, chunks = expo_call(rate, cells, 2 * per_device, (near, first, *second), centroids)
        expos.append(expo), tops.append(top), points.append(chunks)
    factors = factor_call(rate, goals, tops)

    there = sums_call(block, 1, per_device, jnp.bfloat16, expos, points, factors)
    there = [exchange(a, ("lo",), lambda at: at ^ 1) for a in there]
    here = sums_call(block, 0, per_device, jnp.float32, expos, points, factors)
    out, mass = add_call(block // 2, *here, *there)
    return (out[None], mass)


def solution(mesh):
    pts, cells = (mesh.shape[name] for name in ("pts", "cells"))
    square = (pts, cells) == (8, 4)
    shape, names = ((2, 2, 2, cells), ("y", "x", "lo", "cells")) if square else ((pts, cells), ("pts", "cells"))
    fine = Mesh(mesh.devices.reshape(shape), names)
    spread = names[:-1]
    in_specs = (P(names, None), P(names), P("cells", None), P("cells"))
    out_specs = (P("cells", spread, None), P("cells", spread))

    def run(codes, exponents, centroids, counters):
        small = codes.size * 2 <= GATHER_BYTES and codes.shape[0] == 128 * pts * cells
        body = split_cells if square and small else split_points
        mapped = jax.shard_map(body, mesh=fine, in_specs=in_specs, out_specs=out_specs, check_vma=False)
        return mapped(codes, exponents, centroids, counters)

    return run
```

time: 58.3 us -> 56.3 us (0.966)
  Pallas kernels: 23.3 us -> 20.4 us
  local copies, waits for them, and re-layouts: 0.74 us -> 3.27 us
  waiting for transfers between devices: 10.4 us -> 8.6 us
    pallas_call x3 -> x4, Pallas kernels: 13.1 us -> 8.13 us  [the longest x2 7.24 us: totals_call(): pl.pallas_call(functools.partial(totals_kernel, rate, block), in_specs=in...]
    split x0 -> x1, local copies, waits for them, and re-layouts: none -> 3.25 us  [split_cells(): halves = jnp.split(centroids, 2)]
    pallas_call x2, Pallas kernels: 4.44 us -> 6.43 us  [expo_call(): pl.pallas_call(functools.partial(expo_kernel, rate, block), in_specs=in_v...]
    ppermute x17 -> x16, waiting for transfers between devices: 10.4 us -> 8.6 us  [exchange(): return lax.ppermute(a, axes, [(partner(at), at) for at in range(count)])]
    unnamed x2 -> x6, local copies, waits for them, and re-layouts: 0.74 us -> 0.02 us
    ppermute x17 -> x16, starting transfers between devices: 21 us -> 21.2 us  [exchange(): return lax.ppermute(a, axes, [(partner(at), at) for at in range(count)])]
  transfers between devices with their start and end apart: 17 -> 16, of which waited for: 5 -> 4; matrix products, arithmetic and copies ran while one was open for 0% -> 6% of each run, Pallas kernels for 34% -> 30%
where the time goes in v9:
time: 56.3 us; the launch traced here: 56.2 us
  starting transfers between devices  21.2 us (38%)
  Pallas kernels  20.4 us (36%)
  waiting for transfers between devices  8.6 us (15%)
  local copies, waits for them, and re-layouts  3.27 us (6%)
  other arithmetic  1.7 us (3%)
  between operations  1 us (2%)
    ppermute x16, starting transfers between devices, exchange(): return lax.ppermute(a, axes, [(partner(at), at) for at in range(count)])  21.2 us
    ppermute x16, waiting for transfers between devices, exchange(): return lax.ppermute(a, axes, [(partner(at), at) for at in range(count)])  8.6 us
    pallas_call x2, Pallas kernels, totals_call(): pl.pallas_call(functools.partial(totals_kernel, rate, block), in_specs=in...  7.24 us
    pallas_call x2, Pallas kernels, expo_call(): pl.pallas_call(functools.partial(expo_kernel, rate, block), in_specs=in_v...  6.43 us
    pallas_call x2, Pallas kernels, sums_call(): pl.pallas_call(functools.partial(sums_kernel, n, block, side), in_specs=i...  3.95 us
    split x1, local copies, waits for them, and re-layouts, split_cells(): halves = jnp.split(centroids, 2)  3.25 us
    pallas_call x1, Pallas kernels, add_call(): pl.pallas_call(functools.partial(add_kernel, block), in_specs=in_vmem(4),...  1.79 us
  transfers between devices with their start and end apart: 16, of which 4 were waited for; matrix products, arithmetic and copies ran while one was open for 6% of the time, Pallas kernels for 30%

profile of v9, /device:TPU:0, one launch (start us, length us, event | category | flops | bytes accessed | tf_op | source)
XLA Modules:
  0.0 56.2 jit_solution(6992097465363204754)
XLA Ops:
  0.6 0.7 %convert_multiply_fusion = f32[128]{0:T(128)S(1)} fusion(s32[128]{0:T(128)} %param.5), kind=kLoop, calls=%fused_computation.2 | loop fusion | flops 512 | bytes 1024 | tf_op jit(solution)/shard_map/mul | solution.py:16
  1.3 1.0 %multiply_convert_fusion.above = bf16[128,512]{1,0:T(8,128)(2,1)S(1)} fusion(s32[128,512]{1,0:T(8,128)} %param.4, f32[128]{0:T(128)S(1)} %convert_multiply_fusion), kind=kLoop, calls=%fused_computation | loop fusion | flops 196608 | bytes 393728 | tf_op jit(solution)/shard_map/convert_element_type | solution.py:17
  2.3 0.0 copy-start
  2.3 3.1 %collective-permute-start = (bf16[128,512]{1,0:T(8,128)(2,1)S(1)}, bf16[128,512]{1,0:T(8,128)(2,1)S(1)}, u32[]{:S(2)}, u32[]{:S(2)}) collective-permute-start(bf16[128,512]{1,0:T(8,128)(2,1)S(1)} %multiply_convert_fusion.above), channel_id=1, source_target_pairs={{1,0},{0,1},{3,2},{2,3},{5,4},{4,5},{7,6},{6,7},{9,8},{8,9},{11,10... | collective-permute-start | bytes 393224 | tf_op jit(solution)/shard_map/ppermute | solution.py:49
  5.4 2.6 %collective-permute-start.3 = (bf16[128,512]{1,0:T(8,128)(2,1)S(1)}, bf16[128,512]{1,0:T(8,128)(2,1)S(1)}, u32[]{:S(2)}, u32[]{:S(2)}) collective-permute-start(bf16[128,512]{1,0:T(8,128)(2,1)S(1)} %multiply_convert_fusion.above), channel_id=1, source_target_pairs={{2,0},{3,1},{0,2},{1,3},{6,4},{7,5},{4,6},{5,7},{10,8},{11,9},{8,1... | collective-permute-start | bytes 393224 | tf_op jit(solution)/shard_map/ppermute | solution.py:49
  8.0 0.0 collective-permute-start.4
  8.0 3.3 %fusion = (bf16[3072,512]{1,0:T(8,128)(2,1)S(1)}, bf16[3072,512]{1,0:T(8,128)(2,1)S(1)}) fusion(bf16[6144,512]{1,0:T(8,128)(2,1)} %refs_4_.1), kind=kLoop, calls=%fused_computation.3 | loop fusion | bytes 12582912 | tf_op jit(solution)/shard_map/split | solution.py:322
  11.3 0.0 copy-done
  11.3 0.9 %shard_map.62.inverse = f32[6144,128]{1,0:T(8,128)S(1)} custom-call(s32[48,128]{1,0:T(8,128)S(1)} %bitcast.4), custom_call_target="tpu_custom_call" | custom-call | tf_op jit(solution)/shard_map/pallas_call | solution.py:99
  12.2 0.0 collective-permute-done.below
  12.2 1.8 %collective-permute-start.1 = (bf16[256,512]{1,0:T(8,128)(2,1)S(1)}, bf16[256,512]{1,0:T(8,128)(2,1)S(1)}, u32[]{:S(2)}, u32[]{:S(2)}) collective-permute-start(bf16[256,512]{1,0:T(8,128)(2,1)S(1)} %shard_map.59.above.refs_0_.points), channel_id=1, source_target_pairs={{8,0},{20,4},{0,8},{28,12},{24,16},{4,20},{16,24},{12,28},{9,1},{2... | collective-permute-start | bytes 786440 | tf_op jit(solution)/shard_map/ppermute | solution.py:49
  14.0 4.5 %shard_map.63.refs_0_ = f32[3,256]{1,0:T(4,128)S(1)} custom-call(bf16[256,512]{1,0:T(8,128)(2,1)S(1)} %shard_map.59.above.refs_0_.points, bf16[3072,512]{1,0:T(8,128)(2,1)S(1)} %get-tuple-element.31.low, bf16[3072,512]{1,0:T(8,128)(2,1)S(1)} %get-tuple-element.30.high, f32[6144,128]{1,0:T(8,128)S(1)} %shard_map.62.inverse), custom_call_target="tpu_custom_call" | custom-call | flops 1610612736 | bytes 6291456 | tf_op jit(solution)/shard_map/pallas_call | solution.py:138
  18.5 0.0 collective-permute-done.3.above
  18.5 0.0 collective-permute-done.4.below
  18.6 1.4 %collective-permute-start.5 = (bf16[256,512]{1,0:T(8,128)(2,1)S(1)}, bf16[256,512]{1,0:T(8,128)(2,1)S(1)}, u32[]{:S(2)}, u32[]{:S(2)}) collective-permute-start(bf16[256,512]{1,0:T(8,128)(2,1)S(1)} %shard_map.64.points.refs_0_), channel_id=1, source_target_pairs={{8,0},{20,4},{0,8},{28,12},{24,16},{4,20},{16,24},{12,28},{9,1},{2... | collective-permute-start | bytes 786440 | tf_op jit(solution)/shard_map/ppermute | solution.py:49
  19.9 1.5 %collective-permute-start.6 = (bf16[256,512]{1,0:T(8,128)(2,1)S(1)}, bf16[256,512]{1,0:T(8,128)(2,1)S(1)}, u32[]{:S(2)}, u32[]{:S(2)}) collective-permute-start(bf16[256,512]{1,0:T(8,128)(2,1)S(1)} %shard_map.64.points.refs_0_), channel_id=1, source_target_pairs={{16,0},{12,4},{24,8},{4,12},{0,16},{28,20},{8,24},{20,28},{17,1},{... | collective-permute-start | bytes 786440 | tf_op jit(solution)/shard_map/ppermute | solution.py:49
  21.5 0.0 collective-permute-done.1.below.refs_1_.refs_0_
  21.5 0.0 slice-start
  21.5 0.0 slice-start.1
  21.5 0.6 %collective-permute-start.2 = (bf16[512,512]{1,0:T(8,128)(2,1)S(1)}, bf16[512,512]{1,0:T(8,128)(2,1)S(1)}, u32[]{:S(2)}, u32[]{:S(2)}) collective-permute-start(bf16[512,512]{1,0:T(8,128)(2,1)S(1)} %shard_map.60), channel_id=1, source_target_pairs={{16,0},{12,4},{24,8},{4,12},{0,16},{28,20},{8,24},{20,28},{17,1},{... | collective-permute-start | bytes 1572872 | tf_op jit(solution)/shard_map/ppermute | solution.py:49
  22.1 2.7 %shard_map.65.after = f32[3,256]{1,0:T(4,128)S(1)} custom-call(bf16[256,512]{1,0:T(8,128)(2,1)S(1)} %shard_map.64.points.refs_0_, bf16[3072,512]{1,0:T(8,128)(2,1)S(1)} %get-tuple-element.31.low, bf16[3072,512]{1,0:T(8,128)(2,1)S(1)} %get-tuple-element.30.high, f32[6144,128]{1,0:T(8,128)S(1)} %shard_map.62.inverse, ...), custom_call_target="tpu_custom_call" | custom-call | flops 1610612736 | bytes 6291456 | tf_op jit(solution)/shard_map/pallas_call | solution.py:138
  24.8 3.1 %collective-permute-done.5.a.refs_1_ = bf16[256,512]{1,0:T(8,128)(2,1)S(1)} collective-permute-done((bf16[256,512]{1,0:T(8,128)(2,1)S(1)}, bf16[256,512]{1,0:T(8,128)(2,1)S(1)}, u32[]{:S(2)}, u32[]{:S(2)}) %collective-permute-start.5) | collective-permute-done | bytes 262176 | tf_op jit(solution)/shard_map/ppermute | solution.py:49
  27.9 1.6 %collective-permute-start.7 = (bf16[256,512]{1,0:T(8,128)(2,1)S(1)}, bf16[256,512]{1,0:T(8,128)(2,1)S(1)}, u32[]{:S(2)}, u32[]{:S(2)}) collective-permute-start(bf16[256,512]{1,0:T(8,128)(2,1)S(1)} %shard_map.66), channel_id=1, source_target_pairs={{16,0},{12,4},{24,8},{4,12},{0,16},{28,20},{8,24},{20,28},{17,1},{... | collective-permute-start | bytes 786440 | tf_op jit(solution)/shard_map/ppermute | solution.py:49
  29.5 3.6 %collective-permute-start.10 = (f32[3,512]{1,0:T(4,128)S(1)}, f32[3,512]{1,0:T(4,128)S(1)}, u32[]{:S(2)}, u32[]{:S(2)}) collective-permute-start(f32[3,512]{1,0:T(4,128)S(1)} %pad_maximum_fusion.refs_0_), channel_id=1, source_target_pairs={{3,0},{2,1},{1,2},{0,3},{7,4},{6,5},{5,6},{4,7},{11,8},{10,9},{9,1... | collective-permute-start | bytes 18440 | tf_op jit(solution)/shard_map/ppermute | solution.py:49
  33.1 0.0 collective-permute-start.8
  33.1 1.9 %collective-permute-done.10.refs_3_ = f32[3,512]{1,0:T(4,128)S(1)} collective-permute-done((f32[3,512]{1,0:T(4,128)S(1)}, f32[3,512]{1,0:T(4,128)S(1)}, u32[]{:S(2)}, u32[]{:S(2)}) %collective-permute-start.10) | collective-permute-done | bytes 6176 | tf_op jit(solution)/shard_map/ppermute | solution.py:49
  35.0 1.0 %collective-permute-start.9 = (f32[3,512]{1,0:T(4,128)S(1)}, f32[3,512]{1,0:T(4,128)S(1)}, u32[]{:S(2)}, u32[]{:S(2)}) collective-permute-start(f32[3,512]{1,0:T(4,128)S(1)} %pad_maximum_fusion.refs_0_), channel_id=1, source_target_pairs={{2,0},{3,1},{0,2},{1,3},{6,4},{7,5},{4,6},{5,7},{10,8},{11,9},{8,1... | collective-permute-start | bytes 18440 | tf_op jit(solution)/shard_map/ppermute | solution.py:49
  35.9 0.8 %collective-permute-done.8.refs_1_ = f32[3,512]{1,0:T(4,128)S(1)} collective-permute-done((f32[3,512]{1,0:T(4,128)S(1)}, f32[3,512]{1,0:T(4,128)S(1)}, u32[]{:S(2)}, u32[]{:S(2)}) %collective-permute-start.8) | collective-permute-done | bytes 6176 | tf_op jit(solution)/shard_map/ppermute | solution.py:49
  36.8 2.8 %collective-permute-done.9.refs_2_ = f32[3,512]{1,0:T(4,128)S(1)} collective-permute-done((f32[3,512]{1,0:T(4,128)S(1)}, f32[3,512]{1,0:T(4,128)S(1)}, u32[]{:S(2)}, u32[]{:S(2)}) %collective-permute-start.9) | collective-permute-done | bytes 6176 | tf_op jit(solution)/shard_map/ppermute | solution.py:49
  39.6 1.3 %collective-permute-start.11 = (f32[2,512]{1,0:T(2,128)S(1)}, f32[2,512]{1,0:T(2,128)S(1)}, u32[]{:S(2)}, u32[]{:S(2)}) collective-permute-start(f32[2,512]{1,0:T(2,128)S(1)} %shard_map.68.refs_0_), channel_id=1, source_target_pairs={{8,0},{20,4},{0,8},{28,12},{24,16},{4,20},{16,24},{12,28},{9,1},{2... | collective-permute-start | bytes 12296 | tf_op jit(solution)/shard_map/ppermute | solution.py:49
  40.9 0.5 collective-permute-start.12
  41.4 0.0 collective-permute-done.6.refs_2_
  41.4 1.7 %collective-permute-start.13 = (f32[2,512]{1,0:T(2,128)S(1)}, f32[2,512]{1,0:T(2,128)S(1)}, u32[]{:S(2)}, u32[]{:S(2)}) collective-permute-start(f32[2,512]{1,0:T(2,128)S(1)} %shard_map.68.refs_0_), channel_id=1, source_target_pairs={{24,0},{16,8},{8,16},{0,24},{25,1},{17,9},{9,17},{1,25},{26,2},{18... | collective-permute-start | bytes 12296 | tf_op jit(solution)/shard_map/ppermute | solution.py:49
  43.1 0.0 collective-permute-done.7.refs_3_
  43.1 0.0 slice-done
  43.1 0.0 slice-done.1
  43.1 2.0 %shard_map.67 = (bf16[1536,1024]{1,0:T(8,128)(2,1)S(1)}, f32[6,1024]{1,0:T(8,128)S(1)}, bf16[1024,512]{1,0:T(8,128)(2,1)S(1)}) custom-call(bf16[256,512]{1,0:T(8,128)(2,1)S(1)} %shard_map.64.points.refs_0_, bf16[256,512]{1,0:T(8,128)(2,1)S(1)} %collective-permute-done.5.a.refs_1_, bf16[256,512]{1,0:T(8,128)(2,1)S(1)} %collective-permute-done.6.refs_2_, ...), custom_call_target="tpu_custom_call" | custom-call | flops 1610612736 | bytes 5767168 | tf_op jit(solution)/shard_map/pallas_call | solution.py:211
  45.2 0.0 collective-permute-done.2.refs_2_
  45.2 4.4 %shard_map.61 = (bf16[1536,1024]{1,0:T(8,128)(2,1)S(1)}, f32[12,1024]{1,0:T(8,128)S(1)}, bf16[1024,512]{1,0:T(8,128)(2,1)S(1)}) custom-call(bf16[256,512]{1,0:T(8,128)(2,1)S(1)} %shard_map.59.above.refs_0_.points, bf16[256,512]{1,0:T(8,128)(2,1)S(1)} %collective-permute-done.1.below.refs_1_.refs_0_, bf16[512,512]{1,0:T(8,128)(2,1)S(1)} %collective-permute-done.2.refs_2_, ...), custom_call_target="tpu_custom_call" | custom-call | flops 1610612736 | bytes 5767168 | tf_op jit(solution)/shard_map/pallas_call | solution.py:211
  49.6 0.0 collective-permute-done.11.refs_1_
  49.6 0.0 collective-permute-done.12.refs_2_
  49.6 0.0 collective-permute-done.13.refs_3_
  49.7 2.0 %shard_map.71 = (bf16[768,512]{1,0:T(8,128)(2,1)S(1)}, f32[1,768]{1,0:T(1,128)S(1)}) custom-call(bf16[1536,1024]{1,0:T(8,128)(2,1)S(1)} %get-tuple-element.16.refs_0_, bf16[1536,1024]{1,0:T(8,128)(2,1)S(1)} %get-tuple-element.17.refs_1_, bf16[1024,512]{1,0:T(8,128)(2,1)S(1)} %get-tuple-element.18.refs_2_, bf16[1024,512]{1,0:T(8,128)(2,1)S(1)} %get-tuple-element.19.refs_3_, ...), custom_call_target="tpu_custom_call" | custom-call | flops 1610612736 | bytes 6815744 | tf_op jit(solution)/shard_map/pallas_call | solution.py:261
  51.6 0.1 collective-permute-start.14
  51.7 0.5 collective-permute-start.15
  52.2 2.0 %shard_map.70 = (f32[768,512]{1,0:T(8,128)S(1)}, f32[1,768]{1,0:T(1,128)S(1)}) custom-call(bf16[1536,1024]{1,0:T(8,128)(2,1)S(1)} %get-tuple-element.16.refs_0_, bf16[1536,1024]{1,0:T(8,128)(2,1)S(1)} %get-tuple-element.17.refs_1_, bf16[1024,512]{1,0:T(8,128)(2,1)S(1)} %get-tuple-element.18.refs_2_, bf16[1024,512]{1,0:T(8,128)(2,1)S(1)} %get-tuple-element.19.refs_3_, ...), custom_call_target="tpu_custom_call" | custom-call | flops 1610612736 | bytes 6815744 | tf_op jit(solution)/shard_map/pallas_call | solution.py:261
  54.2 0.0 collective-permute-done.15.there_mass
  54.2 0.0 collective-permute-done.14.there
  54.2 1.8 %shard_map.72 = (f32[768,512]{1,0:T(8,128)}, f32[1,768]{1,0:T(1,128)}) custom-call(f32[768,512]{1,0:T(8,128)S(1)} %get-tuple-element.24.here, f32[1,768]{1,0:T(1,128)S(1)} %get-tuple-element.25.here_mass, bf16[768,512]{1,0:T(8,128)(2,1)S(1)} %collective-permute-done.14.there, f32[1,768]{1,0:T(1,128)S(1)} %collective-permute-done.15.there_mass), custom_call_target="tpu_custom_call" | custom-call | tf_op jit(solution)/shard_map/pallas_call | solution.py:291
  (8 shorter events, 0.2 us)
Async XLA Ops:
  2.3 8.9 %copy-start = (s32[6144]{0:T(1024)S(1)}, s32[6144]{0:T(1024)}, u32[]{:S(2)}) copy-start(s32[6144]{0:T(1024)} %param.7) | copy-start | bytes 73732
  2.3 9.8 %collective-permute-start = (bf16[128,512]{1,0:T(8,128)(2,1)S(1)}, bf16[128,512]{1,0:T(8,128)(2,1)S(1)}, u32[]{:S(2)}, u32[]{:S(2)}) collective-permute-start(bf16[128,512]{1,0:T(8,128)(2,1)S(1)} %multiply_convert_fusion.above), channel_id=1, source_target_pairs={{1,0},{0,1},{3,2},{2,3},{5,4},{4,5},{7,6},{6,7},{9,8},{8,9},{11,10... | collective-permute-start | bytes 393224 | tf_op jit(solution)/shard_map/ppermute | solution.py:49
  5.4 13.1 %collective-permute-start.3 = (bf16[128,512]{1,0:T(8,128)(2,1)S(1)}, bf16[128,512]{1,0:T(8,128)(2,1)S(1)}, u32[]{:S(2)}, u32[]{:S(2)}) collective-permute-start(bf16[128,512]{1,0:T(8,128)(2,1)S(1)} %multiply_convert_fusion.above), channel_id=1, source_target_pairs={{2,0},{3,1},{0,2},{1,3},{6,4},{7,5},{4,6},{5,7},{10,8},{11,9},{8,1... | collective-permute-start | bytes 393224 | tf_op jit(solution)/shard_map/ppermute | solution.py:49
  8.0 10.5 %collective-permute-start.4 = (bf16[128,512]{1,0:T(8,128)(2,1)S(1)}, bf16[128,512]{1,0:T(8,128)(2,1)S(1)}, u32[]{:S(2)}, u32[]{:S(2)}) collective-permute-start(bf16[128,512]{1,0:T(8,128)(2,1)S(1)} %multiply_convert_fusion.above), channel_id=1, source_target_pairs={{3,0},{2,1},{1,2},{0,3},{7,4},{6,5},{5,6},{4,7},{11,8},{10,9},{9,1... | collective-permute-start | bytes 393224 | tf_op jit(solution)/shard_map/ppermute | solution.py:49
  12.2 9.2 %collective-permute-start.1 = (bf16[256,512]{1,0:T(8,128)(2,1)S(1)}, bf16[256,512]{1,0:T(8,128)(2,1)S(1)}, u32[]{:S(2)}, u32[]{:S(2)}) collective-permute-start(bf16[256,512]{1,0:T(8,128)(2,1)S(1)} %shard_map.59.above.refs_0_.points), channel_id=1, source_target_pairs={{8,0},{20,4},{0,8},{28,12},{24,16},{4,20},{16,24},{12,28},{9,1},{2... | collective-permute-start | bytes 786440 | tf_op jit(solution)/shard_map/ppermute | solution.py:49
  18.6 9.3 %collective-permute-start.5 = (bf16[256,512]{1,0:T(8,128)(2,1)S(1)}, bf16[256,512]{1,0:T(8,128)(2,1)S(1)}, u32[]{:S(2)}, u32[]{:S(2)}) collective-permute-start(bf16[256,512]{1,0:T(8,128)(2,1)S(1)} %shard_map.64.points.refs_0_), channel_id=1, source_target_pairs={{8,0},{20,4},{0,8},{28,12},{24,16},{4,20},{16,24},{12,28},{9,1},{2... | collective-permute-start | bytes 786440 | tf_op jit(solution)/shard_map/ppermute | solution.py:49
  19.9 21.5 %collective-permute-start.6 = (bf16[256,512]{1,0:T(8,128)(2,1)S(1)}, bf16[256,512]{1,0:T(8,128)(2,1)S(1)}, u32[]{:S(2)}, u32[]{:S(2)}) collective-permute-start(bf16[256,512]{1,0:T(8,128)(2,1)S(1)} %shard_map.64.points.refs_0_), channel_id=1, source_target_pairs={{16,0},{12,4},{24,8},{4,12},{0,16},{28,20},{8,24},{20,28},{17,1},{... | collective-permute-start | bytes 786440 | tf_op jit(solution)/shard_map/ppermute | solution.py:49
  21.5 21.7 %slice-start = ((s8[6291456]{0:T(1024)(128)(4,1)}), s8[4194304]{0:T(1024)(128)(4,1)S(1)}, s32[]{:S(2)}) async-start(s8[6291456]{0:T(1024)(128)(4,1)} %bitcast.2), calls=%async_computation | async-start | bytes 8388608
  21.5 21.6 %slice-start.1 = ((s8[6291456]{0:T(1024)(128)(4,1)}), s8[2097152]{0:T(1024)(128)(4,1)S(1)}, s32[]{:S(2)}) async-start(s8[6291456]{0:T(1024)(128)(4,1)} %bitcast.2), calls=%async_computation.1 | async-start | bytes 4194304
  21.5 23.7 %collective-permute-start.2 = (bf16[512,512]{1,0:T(8,128)(2,1)S(1)}, bf16[512,512]{1,0:T(8,128)(2,1)S(1)}, u32[]{:S(2)}, u32[]{:S(2)}) collective-permute-start(bf16[512,512]{1,0:T(8,128)(2,1)S(1)} %shard_map.60), channel_id=1, source_target_pairs={{16,0},{12,4},{24,8},{4,12},{0,16},{28,20},{8,24},{20,28},{17,1},{... | collective-permute-start | bytes 1572872 | tf_op jit(solution)/shard_map/ppermute | solution.py:49
  27.9 15.2 %collective-permute-start.7 = (bf16[256,512]{1,0:T(8,128)(2,1)S(1)}, bf16[256,512]{1,0:T(8,128)(2,1)S(1)}, u32[]{:S(2)}, u32[]{:S(2)}) collective-permute-start(bf16[256,512]{1,0:T(8,128)(2,1)S(1)} %shard_map.66), channel_id=1, source_target_pairs={{16,0},{12,4},{24,8},{4,12},{0,16},{28,20},{8,24},{20,28},{17,1},{... | collective-permute-start | bytes 786440 | tf_op jit(solution)/shard_map/ppermute | solution.py:49
  29.5 5.4 %collective-permute-start.10 = (f32[3,512]{1,0:T(4,128)S(1)}, f32[3,512]{1,0:T(4,128)S(1)}, u32[]{:S(2)}, u32[]{:S(2)}) collective-permute-start(f32[3,512]{1,0:T(4,128)S(1)} %pad_maximum_fusion.refs_0_), channel_id=1, source_target_pairs={{3,0},{2,1},{1,2},{0,3},{7,4},{6,5},{5,6},{4,7},{11,8},{10,9},{9,1... | collective-permute-start | bytes 18440 | tf_op jit(solution)/shard_map/ppermute | solution.py:49
  33.1 3.7 %collective-permute-start.8 = (f32[3,512]{1,0:T(4,128)S(1)}, f32[3,512]{1,0:T(4,128)S(1)}, u32[]{:S(2)}, u32[]{:S(2)}) collective-permute-start(f32[3,512]{1,0:T(4,128)S(1)} %pad_maximum_fusion.refs_0_), channel_id=1, source_target_pairs={{1,0},{0,1},{3,2},{2,3},{5,4},{4,5},{7,6},{6,7},{9,8},{8,9},{11,10... | collective-permute-start | bytes 18440 | tf_op jit(solution)/shard_map/ppermute | solution.py:49
  35.0 4.5 %collective-permute-start.9 = (f32[3,512]{1,0:T(4,128)S(1)}, f32[3,512]{1,0:T(4,128)S(1)}, u32[]{:S(2)}, u32[]{:S(2)}) collective-permute-start(f32[3,512]{1,0:T(4,128)S(1)} %pad_maximum_fusion.refs_0_), channel_id=1, source_target_pairs={{2,0},{3,1},{0,2},{1,3},{6,4},{7,5},{4,6},{5,7},{10,8},{11,9},{8,1... | collective-permute-start | bytes 18440 | tf_op jit(solution)/shard_map/ppermute | solution.py:49
  39.6 10.0 %collective-permute-start.11 = (f32[2,512]{1,0:T(2,128)S(1)}, f32[2,512]{1,0:T(2,128)S(1)}, u32[]{:S(2)}, u32[]{:S(2)}) collective-permute-start(f32[2,512]{1,0:T(2,128)S(1)} %shard_map.68.refs_0_), channel_id=1, source_target_pairs={{8,0},{20,4},{0,8},{28,12},{24,16},{4,20},{16,24},{12,28},{9,1},{2... | collective-permute-start | bytes 12296 | tf_op jit(solution)/shard_map/ppermute | solution.py:49
  40.9 8.7 %collective-permute-start.12 = (f32[2,512]{1,0:T(2,128)S(1)}, f32[2,512]{1,0:T(2,128)S(1)}, u32[]{:S(2)}, u32[]{:S(2)}) collective-permute-start(f32[2,512]{1,0:T(2,128)S(1)} %shard_map.68.refs_0_), channel_id=1, source_target_pairs={{16,0},{12,4},{24,8},{4,12},{0,16},{28,20},{8,24},{20,28},{17,1},{... | collective-permute-start | bytes 12296 | tf_op jit(solution)/shard_map/ppermute | solution.py:49
  41.4 8.2 %collective-permute-start.13 = (f32[2,512]{1,0:T(2,128)S(1)}, f32[2,512]{1,0:T(2,128)S(1)}, u32[]{:S(2)}, u32[]{:S(2)}) collective-permute-start(f32[2,512]{1,0:T(2,128)S(1)} %shard_map.68.refs_0_), channel_id=1, source_target_pairs={{24,0},{16,8},{8,16},{0,24},{25,1},{17,9},{9,17},{1,25},{26,2},{18... | collective-permute-start | bytes 12296 | tf_op jit(solution)/shard_map/ppermute | solution.py:49
  51.6 2.6 %collective-permute-start.14 = (bf16[768,512]{1,0:T(8,128)(2,1)S(1)}, bf16[768,512]{1,0:T(8,128)(2,1)S(1)}, u32[]{:S(2)}, u32[]{:S(2)}) collective-permute-start(bf16[768,512]{1,0:T(8,128)(2,1)S(1)} %get-tuple-element.26), channel_id=1, source_target_pairs={{4,0},{0,4},{5,1},{1,5},{6,2},{2,6},{7,3},{3,7},{12,8},{8,12},{13,... | collective-permute-start | bytes 2359304 | tf_op jit(solution)/shard_map/ppermute | solution.py:49
  51.7 2.5 %collective-permute-start.15 = (f32[1,768]{1,0:T(1,128)S(1)}, f32[1,768]{1,0:T(1,128)S(1)}, u32[]{:S(2)}, u32[]{:S(2)}) collective-permute-start(f32[1,768]{1,0:T(1,128)S(1)} %get-tuple-element.27), channel_id=1, source_target_pairs={{4,0},{0,4},{5,1},{1,5},{6,2},{2,6},{7,3},{3,7},{12,8},{8,12},{13,... | collective-permute-start | bytes 9224 | tf_op jit(solution)/shard_map/ppermute | solution.py:49

commit v10 on v9

--- a/solution.py
+++ b/solution.py
@@ -68,17 +68,17 @@
     )(above, below, *after)
 
 
-def hold(a, after):
-    def kernel(a, after, out):
-        out[...] = a[...]
+def hold(a, *after):
+    def kernel(a, *refs):
+        refs[-1][...] = a[...]
 
     return pl.pallas_call(
         kernel,
-        in_specs=in_vmem(2),
+        in_specs=in_vmem(1 + len(after)),
         out_specs=in_vmem(1)[0],
         out_shape=jax.ShapeDtypeStruct(a.shape, a.dtype),
         compiler_params=pltpu.CompilerParams(vmem_limit_bytes=VMEM_BYTES),
-    )(a, after)
+    )(a, *after)
 
 
 def scores(cells, points):
@@ -105,9 +105,9 @@
     )(counters.reshape(-1, 128))
 
 
-def totals_kernel(rate, block, points, low, high, inverse, *refs):
-    stats = refs[-1]
-    every = points[...]
+def totals_kernel(rate, block, n, *refs):
+    pieces, (low, high, inverse), stats = refs[:n], refs[n : n + 3], refs[-1]
+    every = jnp.concatenate([piece[...] for piece in pieces], axis=0)
     half, count = low.shape[0], inverse.shape[0]
     parts = []
     for at in range(0, count, block):
@@ -132,12 +132,13 @@
     return (top, *(sum(part[at] * scale for part, scale in zip(parts, scales)) for at in (1, 2)))
 
 
-def totals_call(rate, block, points, halves, inverse, after=()):
-    n_points, width = points.shape
+def totals_call(rate, block, pieces, halves, inverse, after=()):
+    n_points, width = sum(piece.shape[0] for piece in pieces), pieces[0].shape[1]
     n_cells = inverse.shape[0]
-    return pl.pallas_call(
-        functools.partial(totals_kernel, rate, block),
-        in_specs=in_vmem(4 + len(after)),
+    args = (*pieces, *halves, inverse, *after)
+    return pl.pallas_call(
+        functools.partial(totals_kernel, rate, block, len(pieces)),
+        in_specs=in_vmem(len(args)),
         out_specs=in_vmem(1)[0],
         out_shape=jax.ShapeDtypeStruct((3, n_points), jnp.float32),
         compiler_params=pltpu.CompilerParams(vmem_limit_bytes=VMEM_BYTES),
@@ -146,7 +147,7 @@
             bytes_accessed=2 * n_cells * width,
             transcendentals=n_cells * n_points,
         ),
-    )(points, *halves, inverse, *after)
+    )(*args)
 
 
 def goal_kernel(rate, *refs):
@@ -320,21 +321,23 @@
     near_1, near_2, near_3 = (along_z(own, by) for by in (1, 2, 3))
     inverse = inverse_call(counters)
     halves = jnp.split(centroids, 2)
-    near = join(own, near_1)
-    stats = [totals_call(rate, 128, near, halves, inverse)]
-    nears = [near, join(near_2, near_3, *stats)]
-    firsts = [turn(near) for near in nears]
-    stats.append(totals_call(rate, 256, nears[1], halves, inverse, after=firsts[:1]))
-    seconds = [[turn_back(join(nears[0], firsts[0]))], [turn_back(nears[1]), turn_back(hold(firsts[1], stats[1]))]]
-
+    expand = lambda near: (near, turn(near), turn_back(near))
+    own, first_0, second_0 = expand(own)
+    near_1, first_1, second_1 = expand(near_1)
+    across_0, across_1 = turn_back(first_0), turn_back(first_1)
+    stats = [totals_call(rate, block, (own, near_1), halves, inverse, after=(first_0, second_0))]
+    near_23, first_23, second_23 = expand(join(near_2, near_3, *stats))
+    stats.append(totals_call(rate, block, (near_23,), halves, inverse, after=(first_1, second_1, across_0)))
+    across_23 = turn_back(hold(first_23, stats[1], across_1))
+
+    groups = [
+        (own, near_1, first_0, first_1, second_0, second_1, across_0, across_1),
+        (near_23, first_23, second_23, across_23),
+    ]
+    expos, tops, points = zip(*(expo_call(rate, block, 2 * per_device, group, centroids) for group in groups))
     stat = jnp.concatenate(stats, axis=1)
-    goal = goal_call(rate, stat, *(along_z(stat, by) for by in (1, 2, 3)))
+    goal = goal_call(rate, stat, *(along_z(stat, by) for by in (1, 2, 3)), tops[0])
     goals = [goal, turn(goal), turn_back(goal), around(goal, 3)]
-
-    expos, tops, points = [], [], []
-    for cells, near, first, second in zip((128, 256), nears, firsts, seconds):
-        expo, top, chunks = expo_call(rate, cells, 2 * per_device, (near, first, *second), centroids)
-        expos.append(expo), tops.append(top), points.append(chunks)
     factors = factor_call(rate, goals, tops)
 
     there = sums_call(block, 1, per_device, jnp.bfloat16, expos, points, factors)

time: 56.3 us -> 54.1 us (0.961)
  Pallas kernels: 20.4 us -> 16.3 us
  starting transfers between devices: 21.2 us -> 24.2 us
  waiting for transfers between devices: 8.6 us -> 7.5 us
    ppermute x16 -> x20, starting transfers between devices: 21.2 us -> 24.2 us  [exchange(): return lax.ppermute(a, axes, [(partner(at), at) for at in range(count)])]
    pallas_call x2, Pallas kernels: 6.43 us -> 4.05 us  [expo_call(): pl.pallas_call(functools.partial(expo_kernel, rate, block), in_specs=in_v...]
    pallas_call x3, Pallas kernels: 7.25 us -> 5.4 us  [the longest x2 5.38 us: totals_call(): pl.pallas_call(functools.partial(totals_kernel, rate, block, len(pieces))...]
    ppermute x16 -> x20, waiting for transfers between devices: 8.6 us -> 7.5 us  [exchange(): return lax.ppermute(a, axes, [(partner(at), at) for at in range(count)])]
  transfers between devices with their start and end apart: 16 -> 20, of which waited for: 4 -> 3; matrix products, arithmetic and copies ran while one was open for 6% -> 6% of each run, Pallas kernels for 30% -> 23%
where the time goes in v10:
time: 54.1 us; the launch traced here: 54 us
  starting transfers between devices  24.2 us (45%)
  Pallas kernels  16.3 us (30%)
  waiting for transfers between devices  7.5 us (14%)
  local copies, waits for them, and re-layouts  3.27 us (6%)
  other arithmetic  1.7 us (3%)
  between operations  0.97 us (2%)
    ppermute x20, starting transfers between devices, exchange(): return lax.ppermute(a, axes, [(partner(at), at) for at in range(count)])  24.2 us
    ppermute x20, waiting for transfers between devices, exchange(): return lax.ppermute(a, axes, [(partner(at), at) for at in range(count)])  7.5 us
    pallas_call x2, Pallas kernels, totals_call(): pl.pallas_call(functools.partial(totals_kernel, rate, block, len(pieces))...  5.38 us
    pallas_call x2, Pallas kernels, sums_call(): pl.pallas_call(functools.partial(sums_kernel, n, block, side), in_specs=i...  4.15 us
    pallas_call x2, Pallas kernels, expo_call(): pl.pallas_call(functools.partial(expo_kernel, rate, block), in_specs=in_v...  4.05 us
    split x1, local copies, waits for them, and re-layouts, split_cells(): halves = jnp.split(centroids, 2)  3.25 us
    pallas_call x1, Pallas kernels, add_call(): pl.pallas_call(functools.partial(add_kernel, block), in_specs=in_vmem(4),...  1.79 us
  transfers between devices with their start and end apart: 20, of which 3 were waited for; matrix products, arithmetic and copies ran while one was open for 6% of the time, Pallas kernels for 23%

profile of v10, /device:TPU:0, one launch (start us, length us, event | category | flops | bytes accessed | tf_op | source)
XLA Modules:
  0.0 54.0 jit_solution(9776880842134042176)
XLA Ops:
  0.6 0.7 %convert_multiply_fusion = f32[128]{0:T(128)S(1)} fusion(s32[128]{0:T(128)} %param.5), kind=kLoop, calls=%fused_computation.2 | loop fusion | flops 512 | bytes 1024 | tf_op jit(solution)/shard_map/mul | solution.py:16
  1.3 1.0 %multiply_convert_fusion.refs_0_ = bf16[128,512]{1,0:T(8,128)(2,1)S(1)} fusion(s32[128,512]{1,0:T(8,128)} %param.4, f32[128]{0:T(128)S(1)} %convert_multiply_fusion), kind=kLoop, calls=%fused_computation | loop fusion | flops 196608 | bytes 393728 | tf_op jit(solution)/shard_map/convert_element_type | solution.py:17
  2.3 0.0 copy-start
  2.3 3.1 %collective-permute-start = (bf16[128,512]{1,0:T(8,128)(2,1)S(1)}, bf16[128,512]{1,0:T(8,128)(2,1)S(1)}, u32[]{:S(2)}, u32[]{:S(2)}) collective-permute-start(bf16[128,512]{1,0:T(8,128)(2,1)S(1)} %multiply_convert_fusion.refs_0_), channel_id=1, source_target_pairs={{1,0},{0,1},{3,2},{2,3},{5,4},{4,5},{7,6},{6,7},{9,8},{8,9},{11,10... | collective-permute-start | bytes 393224 | tf_op jit(solution)/shard_map/ppermute | solution.py:49
  5.4 1.5 %collective-permute-start.1 = (bf16[128,512]{1,0:T(8,128)(2,1)S(1)}, bf16[128,512]{1,0:T(8,128)(2,1)S(1)}, u32[]{:S(2)}, u32[]{:S(2)}) collective-permute-start(bf16[128,512]{1,0:T(8,128)(2,1)S(1)} %multiply_convert_fusion.refs_0_), channel_id=1, source_target_pairs={{8,0},{20,4},{0,8},{28,12},{24,16},{4,20},{16,24},{12,28},{9,1},{2... | collective-permute-start | bytes 393224 | tf_op jit(solution)/shard_map/ppermute | solution.py:49
  6.9 1.5 %collective-permute-start.3 = (bf16[128,512]{1,0:T(8,128)(2,1)S(1)}, bf16[128,512]{1,0:T(8,128)(2,1)S(1)}, u32[]{:S(2)}, u32[]{:S(2)}) collective-permute-start(bf16[128,512]{1,0:T(8,128)(2,1)S(1)} %multiply_convert_fusion.refs_0_), channel_id=1, source_target_pairs={{16,0},{12,4},{24,8},{4,12},{0,16},{28,20},{8,24},{20,28},{17,1},{... | collective-permute-start | bytes 393224 | tf_op jit(solution)/shard_map/ppermute | solution.py:49
  8.4 2.6 %collective-permute-start.7 = (bf16[128,512]{1,0:T(8,128)(2,1)S(1)}, bf16[128,512]{1,0:T(8,128)(2,1)S(1)}, u32[]{:S(2)}, u32[]{:S(2)}) collective-permute-start(bf16[128,512]{1,0:T(8,128)(2,1)S(1)} %multiply_convert_fusion.refs_0_), channel_id=1, source_target_pairs={{2,0},{3,1},{0,2},{1,3},{6,4},{7,5},{4,6},{5,7},{10,8},{11,9},{8,1... | collective-permute-start | bytes 393224 | tf_op jit(solution)/shard_map/ppermute | solution.py:49
  11.0 0.2 collective-permute-start.8
  11.3 3.2 %fusion = (bf16[3072,512]{1,0:T(8,128)(2,1)S(1)}, bf16[3072,512]{1,0:T(8,128)(2,1)S(1)}) fusion(bf16[6144,512]{1,0:T(8,128)(2,1)} %refs_4_.1), kind=kLoop, calls=%fused_computation.3 | loop fusion | bytes 12582912 | tf_op jit(solution)/shard_map/split | solution.py:323
  14.5 0.0 copy-done
  14.5 0.9 %shard_map.60.refs_4_.refs_3_ = f32[6144,128]{1,0:T(8,128)S(1)} custom-call(s32[48,128]{1,0:T(8,128)S(1)} %bitcast.4), custom_call_target="tpu_custom_call" | custom-call | tf_op jit(solution)/shard_map/pallas_call | solution.py:99
  15.4 0.0 collective-permute-done.refs_1_
  15.4 0.6 %collective-permute-start.2 = (bf16[128,512]{1,0:T(8,128)(2,1)S(1)}, bf16[128,512]{1,0:T(8,128)(2,1)S(1)}, u32[]{:S(2)}, u32[]{:S(2)}) collective-permute-start(bf16[128,512]{1,0:T(8,128)(2,1)S(1)} %collective-permute-done.refs_1_), channel_id=1, source_target_pairs={{8,0},{20,4},{0,8},{28,12},{24,16},{4,20},{16,24},{12,28},{9,1},{2... | collective-permute-start | bytes 393224 | tf_op jit(solution)/shard_map/ppermute | solution.py:49
  16.0 0.0 collective-permute-done.1.refs_2_.refs_5_
  16.0 0.3 collective-permute-start.4
  16.3 0.0 collective-permute-done.3.refs_4_.refs_6_
  16.3 1.7 %collective-permute-start.5 = (bf16[128,512]{1,0:T(8,128)(2,1)S(1)}, bf16[128,512]{1,0:T(8,128)(2,1)S(1)}, u32[]{:S(2)}, u32[]{:S(2)}) collective-permute-start(bf16[128,512]{1,0:T(8,128)(2,1)S(1)} %collective-permute-done.1.refs_2_.refs_5_), channel_id=1, source_target_pairs={{16,0},{12,4},{24,8},{4,12},{0,16},{28,20},{8,24},{20,28},{17,1},{... | collective-permute-start | bytes 393224 | tf_op jit(solution)/shard_map/ppermute | solution.py:49
  18.1 0.0 slice-start
  18.1 2.7 %shard_map.61.refs_0_ = f32[3,256]{1,0:T(4,128)S(1)} custom-call(bf16[128,512]{1,0:T(8,128)(2,1)S(1)} %multiply_convert_fusion.refs_0_, bf16[128,512]{1,0:T(8,128)(2,1)S(1)} %collective-permute-done.refs_1_, bf16[3072,512]{1,0:T(8,128)(2,1)S(1)} %get-tuple-element.31.refs_2_.refs_1_, bf16[3072,512]{1,0:T(8,128)(2,1)S(1)} %get-tuple-element.30.refs_3_.refs_2_, ...), custom_call_target="tpu_custom_call" | custom-call | flops 1610612736 | bytes 6291456 | tf_op jit(solution)/shard_map/pallas_call | solution.py:139
  20.7 0.0 collective-permute-done.7.above
  20.8 0.0 collective-permute-done.8.below
  20.8 0.0 slice-start.1
  20.8 1.6 %collective-permute-start.9 = (bf16[256,512]{1,0:T(8,128)(2,1)S(1)}, bf16[256,512]{1,0:T(8,128)(2,1)S(1)}, u32[]{:S(2)}, u32[]{:S(2)}) collective-permute-start(bf16[256,512]{1,0:T(8,128)(2,1)S(1)} %shard_map.62.refs_0_), channel_id=1, source_target_pairs={{8,0},{20,4},{0,8},{28,12},{24,16},{4,20},{16,24},{12,28},{9,1},{2... | collective-permute-start | bytes 786440 | tf_op jit(solution)/shard_map/ppermute | solution.py:49
  22.4 0.5 collective-permute-start.10
  22.9 0.0 collective-permute-done.2.refs_3_.refs_4_
  22.9 1.5 %collective-permute-start.6 = (bf16[128,512]{1,0:T(8,128)(2,1)S(1)}, bf16[128,512]{1,0:T(8,128)(2,1)S(1)}, u32[]{:S(2)}, u32[]{:S(2)}) collective-permute-start(bf16[128,512]{1,0:T(8,128)(2,1)S(1)} %collective-permute-done.2.refs_3_.refs_4_), channel_id=1, source_target_pairs={{16,0},{12,4},{24,8},{4,12},{0,16},{28,20},{8,24},{20,28},{17,1},{... | collective-permute-start | bytes 393224 | tf_op jit(solution)/shard_map/ppermute | solution.py:49
  24.4 0.0 collective-permute-done.4.refs_5_
  24.4 0.0 collective-permute-done.5.refs_6_
  24.4 2.7 %shard_map.63.refs_0_ = f32[3,256]{1,0:T(4,128)S(1)} custom-call(bf16[256,512]{1,0:T(8,128)(2,1)S(1)} %shard_map.62.refs_0_, bf16[3072,512]{1,0:T(8,128)(2,1)S(1)} %get-tuple-element.31.refs_2_.refs_1_, bf16[3072,512]{1,0:T(8,128)(2,1)S(1)} %get-tuple-element.30.refs_3_.refs_2_, f32[6144,128]{1,0:T(8,128)S(1)} %shard_map.60.refs_4_.refs_3_, ...), custom_call_target="tpu_custom_call" | custom-call | flops 1610612736 | bytes 6291456 | tf_op jit(solution)/shard_map/pallas_call | solution.py:139
  27.1 3.0 %collective-permute-done.6.refs_7_.refs_1_ = bf16[128,512]{1,0:T(8,128)(2,1)S(1)} collective-permute-done((bf16[128,512]{1,0:T(8,128)(2,1)S(1)}, bf16[128,512]{1,0:T(8,128)(2,1)S(1)}, u32[]{:S(2)}, u32[]{:S(2)}) %collective-permute-start.6) | collective-permute-done | bytes 131104 | tf_op jit(solution)/shard_map/ppermute | solution.py:49
  30.1 0.0 collective-permute-done.9.a.refs_1_
  30.2 0.6 %collective-permute-start.11 = (bf16[256,512]{1,0:T(8,128)(2,1)S(1)}, bf16[256,512]{1,0:T(8,128)(2,1)S(1)}, u32[]{:S(2)}, u32[]{:S(2)}) collective-permute-start(bf16[256,512]{1,0:T(8,128)(2,1)S(1)} %shard_map.64), channel_id=1, source_target_pairs={{16,0},{12,4},{24,8},{4,12},{0,16},{28,20},{8,24},{20,28},{17,1},{... | collective-permute-start | bytes 786440 | tf_op jit(solution)/shard_map/ppermute | solution.py:49
  30.7 1.9 %collective-permute-start.12 = (f32[3,512]{1,0:T(4,128)S(1)}, f32[3,512]{1,0:T(4,128)S(1)}, u32[]{:S(2)}, u32[]{:S(2)}) collective-permute-start(f32[3,512]{1,0:T(4,128)S(1)} %pad_maximum_fusion.refs_0_), channel_id=1, source_target_pairs={{1,0},{0,1},{3,2},{2,3},{5,4},{4,5},{7,6},{6,7},{9,8},{8,9},{11,10... | collective-permute-start | bytes 18440 | tf_op jit(solution)/shard_map/ppermute | solution.py:49
  32.6 2.3 %collective-permute-start.13 = (f32[3,512]{1,0:T(4,128)S(1)}, f32[3,512]{1,0:T(4,128)S(1)}, u32[]{:S(2)}, u32[]{:S(2)}) collective-permute-start(f32[3,512]{1,0:T(4,128)S(1)} %pad_maximum_fusion.refs_0_), channel_id=1, source_target_pairs={{2,0},{3,1},{0,2},{1,3},{6,4},{7,5},{4,6},{5,7},{10,8},{11,9},{8,1... | collective-permute-start | bytes 18440 | tf_op jit(solution)/shard_map/ppermute | solution.py:49
  34.9 0.2 collective-permute-start.14
  35.1 0.0 slice-done
  35.1 0.0 slice-done.1
  35.1 2.0 %shard_map.59 = (bf16[1536,1024]{1,0:T(8,128)(2,1)S(1)}, f32[6,1024]{1,0:T(8,128)S(1)}, bf16[1024,512]{1,0:T(8,128)(2,1)S(1)}) custom-call(bf16[128,512]{1,0:T(8,128)(2,1)S(1)} %multiply_convert_fusion.refs_0_, bf16[128,512]{1,0:T(8,128)(2,1)S(1)} %collective-permute-done.refs_1_, bf16[128,512]{1,0:T(8,128)(2,1)S(1)} %collective-permute-done.1.refs_2_.refs_5_, ...), custom_call_target="tpu_custom_call" | custom-call | flops 1610612736 | bytes 5767168 | tf_op jit(solution)/shard_map/pallas_call | solution.py:212
  37.2 0.0 collective-permute-done.12.refs_1_
  37.2 0.0 collective-permute-done.13.refs_2_
  37.2 3.2 %collective-permute-done.14.refs_3_ = f32[3,512]{1,0:T(4,128)S(1)} collective-permute-done((f32[3,512]{1,0:T(4,128)S(1)}, f32[3,512]{1,0:T(4,128)S(1)}, u32[]{:S(2)}, u32[]{:S(2)}) %collective-permute-start.14) | collective-permute-done | bytes 6176 | tf_op jit(solution)/shard_map/ppermute | solution.py:49
  40.4 0.9 %collective-permute-start.15 = (f32[2,512]{1,0:T(2,128)S(1)}, f32[2,512]{1,0:T(2,128)S(1)}, u32[]{:S(2)}, u32[]{:S(2)}) collective-permute-start(f32[2,512]{1,0:T(2,128)S(1)} %shard_map.66.refs_0_), channel_id=1, source_target_pairs={{8,0},{20,4},{0,8},{28,12},{24,16},{4,20},{16,24},{12,28},{9,1},{2... | collective-permute-start | bytes 12296 | tf_op jit(solution)/shard_map/ppermute | solution.py:49
  41.3 1.4 %collective-permute-start.16 = (f32[2,512]{1,0:T(2,128)S(1)}, f32[2,512]{1,0:T(2,128)S(1)}, u32[]{:S(2)}, u32[]{:S(2)}) collective-permute-start(f32[2,512]{1,0:T(2,128)S(1)} %shard_map.66.refs_0_), channel_id=1, source_target_pairs={{16,0},{12,4},{24,8},{4,12},{0,16},{28,20},{8,24},{20,28},{17,1},{... | collective-permute-start | bytes 12296 | tf_op jit(solution)/shard_map/ppermute | solution.py:49
  42.8 1.2 %collective-permute-start.17 = (f32[2,512]{1,0:T(2,128)S(1)}, f32[2,512]{1,0:T(2,128)S(1)}, u32[]{:S(2)}, u32[]{:S(2)}) collective-permute-start(f32[2,512]{1,0:T(2,128)S(1)} %shard_map.66.refs_0_), channel_id=1, source_target_pairs={{24,0},{16,8},{8,16},{0,24},{25,1},{17,9},{9,17},{1,25},{26,2},{18... | collective-permute-start | bytes 12296 | tf_op jit(solution)/shard_map/ppermute | solution.py:49
  43.9 0.0 collective-permute-done.10.refs_2_
  44.0 0.0 collective-permute-done.11.refs_3_
  44.0 2.0 %shard_map.65 = (bf16[1536,1024]{1,0:T(8,128)(2,1)S(1)}, f32[6,1024]{1,0:T(8,128)S(1)}, bf16[1024,512]{1,0:T(8,128)(2,1)S(1)}) custom-call(bf16[256,512]{1,0:T(8,128)(2,1)S(1)} %shard_map.62.refs_0_, bf16[256,512]{1,0:T(8,128)(2,1)S(1)} %collective-permute-done.9.a.refs_1_, bf16[256,512]{1,0:T(8,128)(2,1)S(1)} %collective-permute-done.10.refs_2_, ...), custom_call_target="tpu_custom_call" | custom-call | flops 1610612736 | bytes 5767168 | tf_op jit(solution)/shard_map/pallas_call | solution.py:212
  46.0 0.0 collective-permute-done.15.refs_1_
  46.0 0.0 collective-permute-done.16.refs_2_
  46.0 1.3 %collective-permute-done.17.refs_3_ = f32[2,512]{1,0:T(2,128)S(1)} collective-permute-done((f32[2,512]{1,0:T(2,128)S(1)}, f32[2,512]{1,0:T(2,128)S(1)}, u32[]{:S(2)}, u32[]{:S(2)}) %collective-permute-start.17) | collective-permute-done | bytes 4128 | tf_op jit(solution)/shard_map/ppermute | solution.py:49
  47.3 2.2 %shard_map.69 = (bf16[768,512]{1,0:T(8,128)(2,1)S(1)}, f32[1,768]{1,0:T(1,128)S(1)}) custom-call(bf16[1536,1024]{1,0:T(8,128)(2,1)S(1)} %get-tuple-element.16.refs_0_, bf16[1536,1024]{1,0:T(8,128)(2,1)S(1)} %get-tuple-element.17.refs_1_, bf16[1024,512]{1,0:T(8,128)(2,1)S(1)} %get-tuple-element.18.refs_2_, bf16[1024,512]{1,0:T(8,128)(2,1)S(1)} %get-tuple-element.19.refs_3_, ...), custom_call_target="tpu_custom_call" | custom-call | flops 1610612736 | bytes 6815744 | tf_op jit(solution)/shard_map/pallas_call | solution.py:262
  49.5 0.1 collective-permute-start.18
  49.5 0.5 collective-permute-start.19
  50.0 2.0 %shard_map.68 = (f32[768,512]{1,0:T(8,128)S(1)}, f32[1,768]{1,0:T(1,128)S(1)}) custom-call(bf16[1536,1024]{1,0:T(8,128)(2,1)S(1)} %get-tuple-element.16.refs_0_, bf16[1536,1024]{1,0:T(8,128)(2,1)S(1)} %get-tuple-element.17.refs_1_, bf16[1024,512]{1,0:T(8,128)(2,1)S(1)} %get-tuple-element.18.refs_2_, bf16[1024,512]{1,0:T(8,128)(2,1)S(1)} %get-tuple-element.19.refs_3_, ...), custom_call_target="tpu_custom_call" | custom-call | flops 1610612736 | bytes 6815744 | tf_op jit(solution)/shard_map/pallas_call | solution.py:262
  52.0 0.0 collective-permute-done.19.there_mass
  52.0 0.0 collective-permute-done.18.there
  52.0 1.8 %shard_map.70 = (f32[768,512]{1,0:T(8,128)}, f32[1,768]{1,0:T(1,128)}) custom-call(f32[768,512]{1,0:T(8,128)S(1)} %get-tuple-element.24.here, f32[1,768]{1,0:T(1,128)S(1)} %get-tuple-element.25.here_mass, bf16[768,512]{1,0:T(8,128)(2,1)S(1)} %collective-permute-done.18.there, f32[1,768]{1,0:T(1,128)S(1)} %collective-permute-done.19.there_mass), custom_call_target="tpu_custom_call" | custom-call | tf_op jit(solution)/shard_map/pallas_call | solution.py:292
  (6 shorter events, 0.1 us)
Async XLA Ops:
  2.3 12.2 %copy-start = (s32[6144]{0:T(1024)S(1)}, s32[6144]{0:T(1024)}, u32[]{:S(2)}) copy-start(s32[6144]{0:T(1024)} %param.7) | copy-start | bytes 73732
  2.3 13.1 %collective-permute-start = (bf16[128,512]{1,0:T(8,128)(2,1)S(1)}, bf16[128,512]{1,0:T(8,128)(2,1)S(1)}, u32[]{:S(2)}, u32[]{:S(2)}) collective-permute-start(bf16[128,512]{1,0:T(8,128)(2,1)S(1)} %multiply_convert_fusion.refs_0_), channel_id=1, source_target_pairs={{1,0},{0,1},{3,2},{2,3},{5,4},{4,5},{7,6},{6,7},{9,8},{8,9},{11,10... | collective-permute-start | bytes 393224 | tf_op jit(solution)/shard_map/ppermute | solution.py:49
  5.4 10.6 %collective-permute-start.1 = (bf16[128,512]{1,0:T(8,128)(2,1)S(1)}, bf16[128,512]{1,0:T(8,128)(2,1)S(1)}, u32[]{:S(2)}, u32[]{:S(2)}) collective-permute-start(bf16[128,512]{1,0:T(8,128)(2,1)S(1)} %multiply_convert_fusion.refs_0_), channel_id=1, source_target_pairs={{8,0},{20,4},{0,8},{28,12},{24,16},{4,20},{16,24},{12,28},{9,1},{2... | collective-permute-start | bytes 393224 | tf_op jit(solution)/shard_map/ppermute | solution.py:49
  6.9 9.4 %collective-permute-start.3 = (bf16[128,512]{1,0:T(8,128)(2,1)S(1)}, bf16[128,512]{1,0:T(8,128)(2,1)S(1)}, u32[]{:S(2)}, u32[]{:S(2)}) collective-permute-start(bf16[128,512]{1,0:T(8,128)(2,1)S(1)} %multiply_convert_fusion.refs_0_), channel_id=1, source_target_pairs={{16,0},{12,4},{24,8},{4,12},{0,16},{28,20},{8,24},{20,28},{17,1},{... | collective-permute-start | bytes 393224 | tf_op jit(solution)/shard_map/ppermute | solution.py:49
  8.4 12.3 %collective-permute-start.7 = (bf16[128,512]{1,0:T(8,128)(2,1)S(1)}, bf16[128,512]{1,0:T(8,128)(2,1)S(1)}, u32[]{:S(2)}, u32[]{:S(2)}) collective-permute-start(bf16[128,512]{1,0:T(8,128)(2,1)S(1)} %multiply_convert_fusion.refs_0_), channel_id=1, source_target_pairs={{2,0},{3,1},{0,2},{1,3},{6,4},{7,5},{4,6},{5,7},{10,8},{11,9},{8,1... | collective-permute-start | bytes 393224 | tf_op jit(solution)/shard_map/ppermute | solution.py:49
  11.0 9.7 %collective-permute-start.8 = (bf16[128,512]{1,0:T(8,128)(2,1)S(1)}, bf16[128,512]{1,0:T(8,128)(2,1)S(1)}, u32[]{:S(2)}, u32[]{:S(2)}) collective-permute-start(bf16[128,512]{1,0:T(8,128)(2,1)S(1)} %multiply_convert_fusion.refs_0_), channel_id=1, source_target_pairs={{3,0},{2,1},{1,2},{0,3},{7,4},{6,5},{5,6},{4,7},{11,8},{10,9},{9,1... | collective-permute-start | bytes 393224 | tf_op jit(solution)/shard_map/ppermute | solution.py:49
  15.4 7.5 %collective-permute-start.2 = (bf16[128,512]{1,0:T(8,128)(2,1)S(1)}, bf16[128,512]{1,0:T(8,128)(2,1)S(1)}, u32[]{:S(2)}, u32[]{:S(2)}) collective-permute-start(bf16[128,512]{1,0:T(8,128)(2,1)S(1)} %collective-permute-done.refs_1_), channel_id=1, source_target_pairs={{8,0},{20,4},{0,8},{28,12},{24,16},{4,20},{16,24},{12,28},{9,1},{2... | collective-permute-start | bytes 393224 | tf_op jit(solution)/shard_map/ppermute | solution.py:49
  16.0 8.4 %collective-permute-start.4 = (bf16[128,512]{1,0:T(8,128)(2,1)S(1)}, bf16[128,512]{1,0:T(8,128)(2,1)S(1)}, u32[]{:S(2)}, u32[]{:S(2)}) collective-permute-start(bf16[128,512]{1,0:T(8,128)(2,1)S(1)} %collective-permute-done.refs_1_), channel_id=1, source_target_pairs={{16,0},{12,4},{24,8},{4,12},{0,16},{28,20},{8,24},{20,28},{17,1},{... | collective-permute-start | bytes 393224 | tf_op jit(solution)/shard_map/ppermute | solution.py:49
  16.3 8.1 %collective-permute-start.5 = (bf16[128,512]{1,0:T(8,128)(2,1)S(1)}, bf16[128,512]{1,0:T(8,128)(2,1)S(1)}, u32[]{:S(2)}, u32[]{:S(2)}) collective-permute-start(bf16[128,512]{1,0:T(8,128)(2,1)S(1)} %collective-permute-done.1.refs_2_.refs_5_), channel_id=1, source_target_pairs={{16,0},{12,4},{24,8},{4,12},{0,16},{28,20},{8,24},{20,28},{17,1},{... | collective-permute-start | bytes 393224 | tf_op jit(solution)/shard_map/ppermute | solution.py:49
  18.1 17.1 %slice-start = ((s8[6291456]{0:T(1024)(128)(4,1)}), s8[4194304]{0:T(1024)(128)(4,1)S(1)}, s32[]{:S(2)}) async-start(s8[6291456]{0:T(1024)(128)(4,1)} %bitcast.2), calls=%async_computation | async-start | bytes 8388608
  20.8 14.3 %slice-start.1 = ((s8[6291456]{0:T(1024)(128)(4,1)}), s8[2097152]{0:T(1024)(128)(4,1)S(1)}, s32[]{:S(2)}) async-start(s8[6291456]{0:T(1024)(128)(4,1)} %bitcast.2), calls=%async_computation.1 | async-start | bytes 4194304
  20.8 9.3 %collective-permute-start.9 = (bf16[256,512]{1,0:T(8,128)(2,1)S(1)}, bf16[256,512]{1,0:T(8,128)(2,1)S(1)}, u32[]{:S(2)}, u32[]{:S(2)}) collective-permute-start(bf16[256,512]{1,0:T(8,128)(2,1)S(1)} %shard_map.62.refs_0_), channel_id=1, source_target_pairs={{8,0},{20,4},{0,8},{28,12},{24,16},{4,20},{16,24},{12,28},{9,1},{2... | collective-permute-start | bytes 786440 | tf_op jit(solution)/shard_map/ppermute | solution.py:49
  22.4 21.6 %collective-permute-start.10 = (bf16[256,512]{1,0:T(8,128)(2,1)S(1)}, bf16[256,512]{1,0:T(8,128)(2,1)S(1)}, u32[]{:S(2)}, u32[]{:S(2)}) collective-permute-start(bf16[256,512]{1,0:T(8,128)(2,1)S(1)} %shard_map.62.refs_0_), channel_id=1, source_target_pairs={{16,0},{12,4},{24,8},{4,12},{0,16},{28,20},{8,24},{20,28},{17,1},{... | collective-permute-start | bytes 786440 | tf_op jit(solution)/shard_map/ppermute | solution.py:49
  22.9 7.3 %collective-permute-start.6 = (bf16[128,512]{1,0:T(8,128)(2,1)S(1)}, bf16[128,512]{1,0:T(8,128)(2,1)S(1)}, u32[]{:S(2)}, u32[]{:S(2)}) collective-permute-start(bf16[128,512]{1,0:T(8,128)(2,1)S(1)} %collective-permute-done.2.refs_3_.refs_4_), channel_id=1, source_target_pairs={{16,0},{12,4},{24,8},{4,12},{0,16},{28,20},{8,24},{20,28},{17,1},{... | collective-permute-start | bytes 393224 | tf_op jit(solution)/shard_map/ppermute | solution.py:49
  30.2 13.8 %collective-permute-start.11 = (bf16[256,512]{1,0:T(8,128)(2,1)S(1)}, bf16[256,512]{1,0:T(8,128)(2,1)S(1)}, u32[]{:S(2)}, u32[]{:S(2)}) collective-permute-start(bf16[256,512]{1,0:T(8,128)(2,1)S(1)} %shard_map.64), channel_id=1, source_target_pairs={{16,0},{12,4},{24,8},{4,12},{0,16},{28,20},{8,24},{20,28},{17,1},{... | collective-permute-start | bytes 786440 | tf_op jit(solution)/shard_map/ppermute | solution.py:49
  30.7 6.4 %collective-permute-start.12 = (f32[3,512]{1,0:T(4,128)S(1)}, f32[3,512]{1,0:T(4,128)S(1)}, u32[]{:S(2)}, u32[]{:S(2)}) collective-permute-start(f32[3,512]{1,0:T(4,128)S(1)} %pad_maximum_fusion.refs_0_), channel_id=1, source_target_pairs={{1,0},{0,1},{3,2},{2,3},{5,4},{4,5},{7,6},{6,7},{9,8},{8,9},{11,10... | collective-permute-start | bytes 18440 | tf_op jit(solution)/shard_map/ppermute | solution.py:49
  32.6 4.6 %collective-permute-start.13 = (f32[3,512]{1,0:T(4,128)S(1)}, f32[3,512]{1,0:T(4,128)S(1)}, u32[]{:S(2)}, u32[]{:S(2)}) collective-permute-start(f32[3,512]{1,0:T(4,128)S(1)} %pad_maximum_fusion.refs_0_), channel_id=1, source_target_pairs={{2,0},{3,1},{0,2},{1,3},{6,4},{7,5},{4,6},{5,7},{10,8},{11,9},{8,1... | collective-permute-start | bytes 18440 | tf_op jit(solution)/shard_map/ppermute | solution.py:49
  34.9 5.4 %collective-permute-start.14 = (f32[3,512]{1,0:T(4,128)S(1)}, f32[3,512]{1,0:T(4,128)S(1)}, u32[]{:S(2)}, u32[]{:S(2)}) collective-permute-start(f32[3,512]{1,0:T(4,128)S(1)} %pad_maximum_fusion.refs_0_), channel_id=1, source_target_pairs={{3,0},{2,1},{1,2},{0,3},{7,4},{6,5},{5,6},{4,7},{11,8},{10,9},{9,1... | collective-permute-start | bytes 18440 | tf_op jit(solution)/shard_map/ppermute | solution.py:49
  40.4 5.6 %collective-permute-start.15 = (f32[2,512]{1,0:T(2,128)S(1)}, f32[2,512]{1,0:T(2,128)S(1)}, u32[]{:S(2)}, u32[]{:S(2)}) collective-permute-start(f32[2,512]{1,0:T(2,128)S(1)} %shard_map.66.refs_0_), channel_id=1, source_target_pairs={{8,0},{20,4},{0,8},{28,12},{24,16},{4,20},{16,24},{12,28},{9,1},{2... | collective-permute-start | bytes 12296 | tf_op jit(solution)/shard_map/ppermute | solution.py:49
  41.3 4.7 %collective-permute-start.16 = (f32[2,512]{1,0:T(2,128)S(1)}, f32[2,512]{1,0:T(2,128)S(1)}, u32[]{:S(2)}, u32[]{:S(2)}) collective-permute-start(f32[2,512]{1,0:T(2,128)S(1)} %shard_map.66.refs_0_), channel_id=1, source_target_pairs={{16,0},{12,4},{24,8},{4,12},{0,16},{28,20},{8,24},{20,28},{17,1},{... | collective-permute-start | bytes 12296 | tf_op jit(solution)/shard_map/ppermute | solution.py:49
  42.8 4.5 %collective-permute-start.17 = (f32[2,512]{1,0:T(2,128)S(1)}, f32[2,512]{1,0:T(2,128)S(1)}, u32[]{:S(2)}, u32[]{:S(2)}) collective-permute-start(f32[2,512]{1,0:T(2,128)S(1)} %shard_map.66.refs_0_), channel_id=1, source_target_pairs={{24,0},{16,8},{8,16},{0,24},{25,1},{17,9},{9,17},{1,25},{26,2},{18... | collective-permute-start | bytes 12296 | tf_op jit(solution)/shard_map/ppermute | solution.py:49
  49.5 2.6 %collective-permute-start.18 = (bf16[768,512]{1,0:T(8,128)(2,1)S(1)}, bf16[768,512]{1,0:T(8,128)(2,1)S(1)}, u32[]{:S(2)}, u32[]{:S(2)}) collective-permute-start(bf16[768,512]{1,0:T(8,128)(2,1)S(1)} %get-tuple-element.26), channel_id=1, source_target_pairs={{4,0},{0,4},{5,1},{1,5},{6,2},{2,6},{7,3},{3,7},{12,8},{8,12},{13,... | collective-permute-start | bytes 2359304 | tf_op jit(solution)/shard_map/ppermute | solution.py:49
  49.5 2.5 %collective-permute-start.19 = (f32[1,768]{1,0:T(1,128)S(1)}, f32[1,768]{1,0:T(1,128)S(1)}, u32[]{:S(2)}, u32[]{:S(2)}) collective-permute-start(f32[1,768]{1,0:T(1,128)S(1)} %get-tuple-element.27), channel_id=1, source_target_pairs={{4,0},{0,4},{5,1},{1,5},{6,2},{2,6},{7,3},{3,7},{12,8},{8,12},{13,... | collective-permute-start | bytes 9224 | tf_op jit(solution)/shard_map/ppermute | solution.py:49

commit v11 on v10

--- a/solution.py
+++ b/solution.py
@@ -68,6 +68,19 @@
     )(above, below, *after)
 
 
+def beside(left, right, *after):
+    def kernel(left, right, *refs):
+        refs[-1][...] = jnp.concatenate([left[...], right[...]], axis=1)
+
+    return pl.pallas_call(
+        kernel,
+        in_specs=in_vmem(2 + len(after)),
+        out_specs=in_vmem(1)[0],
+        out_shape=jax.ShapeDtypeStruct((left.shape[0], left.shape[1] + right.shape[1]), left.dtype),
+        compiler_params=pltpu.CompilerParams(vmem_limit_bytes=VMEM_BYTES),
+    )(left, right, *after)
+
+
 def hold(a, *after):
     def kernel(a, *refs):
         refs[-1][...] = a[...]
@@ -89,31 +102,32 @@
     return lax.axis_index("y") * 2 + lax.axis_index("x")
 
 
-def inverse_kernel(counters, inverse):
+def inverse_kernel(counters, *refs):
+    inverse = refs[-1]
     for line in range(counters.shape[0]):
         row = lax.rsqrt(counters[line : line + 1, :].astype(jnp.float32) + 1.0)
         inverse[line * 128 : (line + 1) * 128, :] = jnp.broadcast_to(row, (128, 128)).T
 
 
-def inverse_call(counters):
+def inverse_call(counters, *after):
     return pl.pallas_call(
         inverse_kernel,
-        in_specs=in_vmem(1),
+        in_specs=in_vmem(1 + len(after)),
         out_specs=in_vmem(1)[0],
         out_shape=jax.ShapeDtypeStruct((counters.shape[0], 128), jnp.float32),
         compiler_params=pltpu.CompilerParams(vmem_limit_bytes=VMEM_BYTES),
-    )(counters.reshape(-1, 128))
+        cost_estimate=pl.CostEstimate(flops=4 * 10**9, bytes_accessed=0, transcendentals=0),
+    )(counters.reshape(-1, 128), *after)
 
 
 def totals_kernel(rate, block, n, *refs):
-    pieces, (low, high, inverse), stats = refs[:n], refs[n : n + 3], refs[-1]
+    pieces, (cells, inverse), stats = refs[:n], refs[n : n + 2], refs[-1]
     every = jnp.concatenate([piece[...] for piece in pieces], axis=0)
-    half, count = low.shape[0], inverse.shape[0]
+    count = cells.shape[0]
     parts = []
     for at in range(0, count, block):
         here = slice(at, at + block)
-        cells = low[here, :] if at < half else high[at - half : at - half + block, :]
-        logits = scores(cells, every)
+        logits = scores(cells[here, :], every)
         top = jnp.max(logits, axis=0, keepdims=True)
         value = jnp.exp2((logits - top) * rate)
         scale = inverse[here, :]
@@ -132,10 +146,10 @@
     return (top, *(sum(part[at] * scale for part, scale in zip(parts, scales)) for at in (1, 2)))
 
 
-def totals_call(rate, block, pieces, halves, inverse, after=()):
+def totals_call(rate, block, pieces, cells, inverse, after=()):
     n_points, width = sum(piece.shape[0] for piece in pieces), pieces[0].shape[1]
     n_cells = inverse.shape[0]
-    args = (*pieces, *halves, inverse, *after)
+    args = (*pieces, cells, inverse, *after)
     return pl.pallas_call(
         functools.partial(totals_kernel, rate, block, len(pieces)),
         in_specs=in_vmem(len(args)),
@@ -188,8 +202,8 @@
     )(*goals, *tops)
 
 
-def expo_kernel(rate, block, *refs):
-    pieces, (cells, expo, tops, points) = refs[:-4], refs[-4:]
+def expo_kernel(rate, block, n, *refs):
+    pieces, cells, (expo, tops, points) = refs[:n], refs[n], refs[-3:]
     start = 0
     for piece in pieces:
         points[start : start + piece.shape[0], :] = piece[...]
@@ -206,12 +220,12 @@
             tops[at : at + 1, some] = top
 
 
-def expo_call(rate, block, count, pieces, cells):
+def expo_call(rate, block, count, pieces, cells, *after):
     width = cells.shape[1]
     n_points = sum(piece.shape[0] for piece in pieces)
     return pl.pallas_call(
-        functools.partial(expo_kernel, rate, block),
-        in_specs=in_vmem(len(pieces) + 1),
+        functools.partial(expo_kernel, rate, block, len(pieces)),
+        in_specs=in_vmem(len(pieces) + 1 + len(after)),
         out_specs=in_vmem(3),
         out_shape=[
             jax.ShapeDtypeStruct((count, n_points), jnp.bfloat16),
@@ -224,7 +238,7 @@
             bytes_accessed=2 * (count * width + n_points * width + count * n_points),
             transcendentals=count * n_points,
         ),
-    )(*pieces, cells)
+    )(*pieces, cells, *after)
 
 
 def weighed_sums(start, count, expos, points, factors):
@@ -319,24 +333,24 @@
     block = per_device // 3
 
     near_1, near_2, near_3 = (along_z(own, by) for by in (1, 2, 3))
-    inverse = inverse_call(counters)
-    halves = jnp.split(centroids, 2)
     expand = lambda near: (near, turn(near), turn_back(near))
     own, first_0, second_0 = expand(own)
     near_1, first_1, second_1 = expand(near_1)
     across_0, across_1 = turn_back(first_0), turn_back(first_1)
-    stats = [totals_call(rate, block, (own, near_1), halves, inverse, after=(first_0, second_0))]
+    inverse = inverse_call(counters, first_0, near_1)
+    stats = [totals_call(rate, block, (own, near_1), centroids, inverse, after=(second_0,))]
     near_23, first_23, second_23 = expand(join(near_2, near_3, *stats))
-    stats.append(totals_call(rate, block, (near_23,), halves, inverse, after=(first_1, second_1, across_0)))
-    across_23 = turn_back(hold(first_23, stats[1], across_1))
-
-    groups = [
-        (own, near_1, first_0, first_1, second_0, second_1, across_0, across_1),
-        (near_23, first_23, second_23, across_23),
-    ]
-    expos, tops, points = zip(*(expo_call(rate, block, 2 * per_device, group, centroids) for group in groups))
-    stat = jnp.concatenate(stats, axis=1)
-    goal = goal_call(rate, stat, *(along_z(stat, by) for by in (1, 2, 3)), tops[0])
+    stats.append(totals_call(rate, block, (near_23,), centroids, inverse, after=(first_1, second_1, across_0)))
+
+    expand = functools.partial(expo_call, rate, block, 2 * per_device)
+    groups = [expand((own, near_1, first_0, first_1, second_0, second_1, across_0, across_1), centroids, stats[1])]
+    tops = groups[0][1]
+    stat = beside(*stats, across_1)
+    theirs = [along_z(stat, by) for by in (1, 2, 3)]
+    goal = goal_call(rate, stat, *theirs, tops, second_23)
+    across_23 = turn_back(hold(first_23, goal))
+    groups.append(expand((near_23, first_23, second_23, across_23), centroids))
+    expos, tops, points = zip(*groups)
     goals = [goal, turn(goal), turn_back(goal), around(goal, 3)]
     factors = factor_call(rate, goals, tops)
 

time: 54.1 us -> 54 us (level)
  local copies, waits for them, and re-layouts: 3.27 us -> 1.48 us
  starting transfers between devices: 24.2 us -> 25.1 us
  Pallas kernels: 16.3 us -> 17.1 us
    split x1 -> x0, local copies, waits for them, and re-layouts: 3.25 us -> none  [split_cells(): halves = jnp.split(centroids, 2)]
    unnamed x6, local copies, waits for them, and re-layouts: 0.02 us -> 1.48 us
    ppermute x20, starting transfers between devices: 24.2 us -> 25.1 us  [exchange(): return lax.ppermute(a, axes, [(partner(at), at) for at in range(count)])]
    pallas_call x3 -> x4, Pallas kernels: 4.93 us -> 5.12 us  [the longest x2 4.24 us: expo_call(): pl.pallas_call(functools.partial(expo_kernel, rate, block, len(pieces)),...]
  transfers between devices with their start and end apart: 20 -> 20, of which waited for: 3 -> 4; matrix products, arithmetic and copies ran while one was open for 6% -> 0% of each run, Pallas kernels for 23% -> 24%
where the time goes in v11:
time: 54 us; the launch traced here: 53.8 us
  starting transfers between devices  25.1 us (46%)
  Pallas kernels  17.1 us (32%)
  waiting for transfers between devices  7.46 us (14%)
  other arithmetic  1.69 us (3%)
  local copies, waits for them, and re-layouts  1.48 us (3%)
  between operations  0.96 us (2%)
    ppermute x20, starting transfers between devices, exchange(): return lax.ppermute(a, axes, [(partner(at), at) for at in range(count)])  25.1 us
    ppermute x20, waiting for transfers between devices, exchange(): return lax.ppermute(a, axes, [(partner(at), at) for at in range(count)])  7.46 us
    pallas_call x2, Pallas kernels, totals_call(): pl.pallas_call(functools.partial(totals_kernel, rate, block, len(pieces))...  5.81 us
    pallas_call x2, Pallas kernels, sums_call(): pl.pallas_call(functools.partial(sums_kernel, n, block, side), in_specs=i...  4.29 us
    pallas_call x2, Pallas kernels, expo_call(): pl.pallas_call(functools.partial(expo_kernel, rate, block, len(pieces)),...  4.24 us
    pallas_call x1, Pallas kernels, add_call(): pl.pallas_call(functools.partial(add_kernel, block), in_specs=in_vmem(4),...  1.79 us
    unnamed x6, local copies, waits for them, and re-layouts  1.48 us
  transfers between devices with their start and end apart: 20, of which 4 were waited for; matrix products, arithmetic and copies ran while one was open for 0% of the time, Pallas kernels for 24%

profile of v11, /device:TPU:0, one launch (start us, length us, event | category | flops | bytes accessed | tf_op | source)
XLA Modules:
  0.0 53.8 jit_solution(8193901625115896610)
XLA Ops:
  0.6 0.7 %convert_multiply_fusion = f32[128]{0:T(128)S(1)} fusion(s32[128]{0:T(128)} %param.5), kind=kLoop, calls=%fused_computation.1 | loop fusion | flops 512 | bytes 1024 | tf_op jit(solution)/shard_map/mul | solution.py:16
  1.3 1.0 %multiply_convert_fusion.refs_0_ = bf16[128,512]{1,0:T(8,128)(2,1)S(1)} fusion(s32[128,512]{1,0:T(8,128)} %param.4, f32[128]{0:T(128)S(1)} %convert_multiply_fusion), kind=kLoop, calls=%fused_computation | loop fusion | flops 196608 | bytes 393728 | tf_op jit(solution)/shard_map/convert_element_type | solution.py:17
  2.3 3.1 %collective-permute-start = (bf16[128,512]{1,0:T(8,128)(2,1)S(1)}, bf16[128,512]{1,0:T(8,128)(2,1)S(1)}, u32[]{:S(2)}, u32[]{:S(2)}) collective-permute-start(bf16[128,512]{1,0:T(8,128)(2,1)S(1)} %multiply_convert_fusion.refs_0_), channel_id=1, source_target_pairs={{1,0},{0,1},{3,2},{2,3},{5,4},{4,5},{7,6},{6,7},{9,8},{8,9},{11,10... | collective-permute-start | bytes 393224 | tf_op jit(solution)/shard_map/ppermute | solution.py:49
  5.4 1.5 %collective-permute-start.1 = (bf16[128,512]{1,0:T(8,128)(2,1)S(1)}, bf16[128,512]{1,0:T(8,128)(2,1)S(1)}, u32[]{:S(2)}, u32[]{:S(2)}) collective-permute-start(bf16[128,512]{1,0:T(8,128)(2,1)S(1)} %multiply_convert_fusion.refs_0_), channel_id=1, source_target_pairs={{8,0},{20,4},{0,8},{28,12},{24,16},{4,20},{16,24},{12,28},{9,1},{2... | collective-permute-start | bytes 393224 | tf_op jit(solution)/shard_map/ppermute | solution.py:49
  6.9 1.5 %collective-permute-start.3 = (bf16[128,512]{1,0:T(8,128)(2,1)S(1)}, bf16[128,512]{1,0:T(8,128)(2,1)S(1)}, u32[]{:S(2)}, u32[]{:S(2)}) collective-permute-start(bf16[128,512]{1,0:T(8,128)(2,1)S(1)} %multiply_convert_fusion.refs_0_), channel_id=1, source_target_pairs={{16,0},{12,4},{24,8},{4,12},{0,16},{28,20},{8,24},{20,28},{17,1},{... | collective-permute-start | bytes 393224 | tf_op jit(solution)/shard_map/ppermute | solution.py:49
  8.4 2.6 %collective-permute-start.7 = (bf16[128,512]{1,0:T(8,128)(2,1)S(1)}, bf16[128,512]{1,0:T(8,128)(2,1)S(1)}, u32[]{:S(2)}, u32[]{:S(2)}) collective-permute-start(bf16[128,512]{1,0:T(8,128)(2,1)S(1)} %multiply_convert_fusion.refs_0_), channel_id=1, source_target_pairs={{2,0},{3,1},{0,2},{1,3},{6,4},{7,5},{4,6},{5,7},{10,8},{11,9},{8,1... | collective-permute-start | bytes 393224 | tf_op jit(solution)/shard_map/ppermute | solution.py:49
  11.0 0.2 collective-permute-start.8
  11.2 0.0 collective-permute-done.refs_1_
  11.2 0.5 collective-permute-start.2
  11.8 0.0 collective-permute-done.1.refs_0_.refs_2_
  11.8 1.4 %collective-permute-start.4 = (bf16[128,512]{1,0:T(8,128)(2,1)S(1)}, bf16[128,512]{1,0:T(8,128)(2,1)S(1)}, u32[]{:S(2)}, u32[]{:S(2)}) collective-permute-start(bf16[128,512]{1,0:T(8,128)(2,1)S(1)} %collective-permute-done.refs_1_), channel_id=1, source_target_pairs={{16,0},{12,4},{24,8},{4,12},{0,16},{28,20},{8,24},{20,28},{17,1},{... | collective-permute-start | bytes 393224 | tf_op jit(solution)/shard_map/ppermute | solution.py:49
  13.2 0.0 slice-start
  13.2 0.0 copy-start
  13.2 0.9 %copy-done = s32[6144]{0:T(1024)S(1)} copy-done((s32[6144]{0:T(1024)S(1)}, s32[6144]{0:T(1024)}, u32[]{:S(2)}) %copy-start) | copy-done | bytes 24600
  14.1 0.0 slice-start.1
  14.1 0.9 %shard_map.59.refs_3_.refs_2_ = f32[6144,128]{1,0:T(8,128)S(1)} custom-call(s32[48,128]{1,0:T(8,128)S(1)} %bitcast.4, bf16[128,512]{1,0:T(8,128)(2,1)S(1)} %collective-permute-done.1.refs_0_.refs_2_, bf16[128,512]{1,0:T(8,128)(2,1)S(1)} %collective-permute-done.refs_1_), custom_call_target="tpu_custom_call" | custom-call | flops 4000000000 | tf_op jit(solution)/shard_map/pallas_call | solution.py:113
  14.9 0.0 collective-permute-done.3.refs_4_
  14.9 0.7 %collective-permute-start.5 = (bf16[128,512]{1,0:T(8,128)(2,1)S(1)}, bf16[128,512]{1,0:T(8,128)(2,1)S(1)}, u32[]{:S(2)}, u32[]{:S(2)}) collective-permute-start(bf16[128,512]{1,0:T(8,128)(2,1)S(1)} %collective-permute-done.1.refs_0_.refs_2_), channel_id=1, source_target_pairs={{16,0},{12,4},{24,8},{4,12},{0,16},{28,20},{8,24},{20,28},{17,1},{... | collective-permute-start | bytes 393224 | tf_op jit(solution)/shard_map/ppermute | solution.py:49
  15.7 0.0 slice-done
  15.7 0.6 %slice-done.1 = s8[2097152]{0:T(1024)(128)(4,1)S(1)} async-done(((s8[6291456]{0:T(1024)(128)(4,1)}), s8[2097152]{0:T(1024)(128)(4,1)S(1)}, s32[]{:S(2)}) %slice-start.1) | async-done | bytes 2097176
  16.3 2.9 %shard_map.60.refs_0_.left = f32[3,256]{1,0:T(4,128)S(1)} custom-call(bf16[128,512]{1,0:T(8,128)(2,1)S(1)} %multiply_convert_fusion.refs_0_, bf16[128,512]{1,0:T(8,128)(2,1)S(1)} %collective-permute-done.refs_1_, bf16[6144,512]{1,0:T(8,128)(2,1)S(1)} %bitcast.3, f32[6144,128]{1,0:T(8,128)S(1)} %shard_map.59.refs_3_.refs_2_, ...), custom_call_target="tpu_custom_call" | custom-call | flops 1610612736 | bytes 6291456 | tf_op jit(solution)/shard_map/pallas_call | solution.py:153
  19.2 0.7 %collective-permute-done.7.above = bf16[128,512]{1,0:T(8,128)(2,1)S(1)} collective-permute-done((bf16[128,512]{1,0:T(8,128)(2,1)S(1)}, bf16[128,512]{1,0:T(8,128)(2,1)S(1)}, u32[]{:S(2)}, u32[]{:S(2)}) %collective-permute-start.7) | collective-permute-done | bytes 131104 | tf_op jit(solution)/shard_map/ppermute | solution.py:49
  19.9 0.0 collective-permute-done.8.below
  19.9 1.1 %collective-permute-start.10 = (bf16[256,512]{1,0:T(8,128)(2,1)S(1)}, bf16[256,512]{1,0:T(8,128)(2,1)S(1)}, u32[]{:S(2)}, u32[]{:S(2)}) collective-permute-start(bf16[256,512]{1,0:T(8,128)(2,1)S(1)} %shard_map.61.refs_0_), channel_id=1, source_target_pairs={{16,0},{12,4},{24,8},{4,12},{0,16},{28,20},{8,24},{20,28},{17,1},{... | collective-permute-start | bytes 786440 | tf_op jit(solution)/shard_map/ppermute | solution.py:49
  21.0 0.9 %collective-permute-start.9 = (bf16[256,512]{1,0:T(8,128)(2,1)S(1)}, bf16[256,512]{1,0:T(8,128)(2,1)S(1)}, u32[]{:S(2)}, u32[]{:S(2)}) collective-permute-start(bf16[256,512]{1,0:T(8,128)(2,1)S(1)} %shard_map.61.refs_0_), channel_id=1, source_target_pairs={{8,0},{20,4},{0,8},{28,12},{24,16},{4,20},{16,24},{12,28},{9,1},{2... | collective-permute-start | bytes 786440 | tf_op jit(solution)/shard_map/ppermute | solution.py:49
  21.9 0.0 collective-permute-done.2.refs_3_
  21.9 1.1 %collective-permute-start.6 = (bf16[128,512]{1,0:T(8,128)(2,1)S(1)}, bf16[128,512]{1,0:T(8,128)(2,1)S(1)}, u32[]{:S(2)}, u32[]{:S(2)}) collective-permute-start(bf16[128,512]{1,0:T(8,128)(2,1)S(1)} %collective-permute-done.2.refs_3_), channel_id=1, source_target_pairs={{16,0},{12,4},{24,8},{4,12},{0,16},{28,20},{8,24},{20,28},{17,1},{... | collective-permute-start | bytes 393224 | tf_op jit(solution)/shard_map/ppermute | solution.py:49
  23.0 0.0 collective-permute-done.4.refs_4_.refs_5_
  23.1 0.0 collective-permute-done.5.refs_5_.refs_6_
  23.1 2.9 %shard_map.62.refs_9_.right = f32[3,256]{1,0:T(4,128)S(1)} custom-call(bf16[256,512]{1,0:T(8,128)(2,1)S(1)} %shard_map.61.refs_0_, bf16[6144,512]{1,0:T(8,128)(2,1)S(1)} %bitcast.3, f32[6144,128]{1,0:T(8,128)S(1)} %shard_map.59.refs_3_.refs_2_, bf16[128,512]{1,0:T(8,128)(2,1)S(1)} %collective-permute-done.2.refs_3_, ...), custom_call_target="tpu_custom_call" | custom-call | flops 1610612736 | bytes 6291456 | tf_op jit(solution)/shard_map/pallas_call | solution.py:153
  26.0 2.7 %collective-permute-done.6.refs_7_.refs_0_ = bf16[128,512]{1,0:T(8,128)(2,1)S(1)} collective-permute-done((bf16[128,512]{1,0:T(8,128)(2,1)S(1)}, bf16[128,512]{1,0:T(8,128)(2,1)S(1)}, u32[]{:S(2)}, u32[]{:S(2)}) %collective-permute-start.6) | collective-permute-done | bytes 131104 | tf_op jit(solution)/shard_map/ppermute | solution.py:49
  28.7 3.4 %collective-permute-start.11 = (f32[3,512]{1,0:T(4,128)S(1)}, f32[3,512]{1,0:T(4,128)S(1)}, u32[]{:S(2)}, u32[]{:S(2)}) collective-permute-start(f32[3,512]{1,0:T(4,128)S(1)} %shard_map.64.refs_0_), channel_id=1, source_target_pairs={{1,0},{0,1},{3,2},{2,3},{5,4},{4,5},{7,6},{6,7},{9,8},{8,9},{11,10... | collective-permute-start | bytes 18440 | tf_op jit(solution)/shard_map/ppermute | solution.py:49
  32.0 0.8 %collective-permute-start.12 = (f32[3,512]{1,0:T(4,128)S(1)}, f32[3,512]{1,0:T(4,128)S(1)}, u32[]{:S(2)}, u32[]{:S(2)}) collective-permute-start(f32[3,512]{1,0:T(4,128)S(1)} %shard_map.64.refs_0_), channel_id=1, source_target_pairs={{2,0},{3,1},{0,2},{1,3},{6,4},{7,5},{4,6},{5,7},{10,8},{11,9},{8,1... | collective-permute-start | bytes 18440 | tf_op jit(solution)/shard_map/ppermute | solution.py:49
  32.8 1.7 %collective-permute-start.13 = (f32[3,512]{1,0:T(4,128)S(1)}, f32[3,512]{1,0:T(4,128)S(1)}, u32[]{:S(2)}, u32[]{:S(2)}) collective-permute-start(f32[3,512]{1,0:T(4,128)S(1)} %shard_map.64.refs_0_), channel_id=1, source_target_pairs={{3,0},{2,1},{1,2},{0,3},{7,4},{6,5},{5,6},{4,7},{11,8},{10,9},{9,1... | collective-permute-start | bytes 18440 | tf_op jit(solution)/shard_map/ppermute | solution.py:49
  34.5 2.1 %shard_map.63 = (bf16[1536,1024]{1,0:T(8,128)(2,1)S(1)}, f32[6,1024]{1,0:T(8,128)S(1)}, bf16[1024,512]{1,0:T(8,128)(2,1)S(1)}) custom-call(bf16[128,512]{1,0:T(8,128)(2,1)S(1)} %multiply_convert_fusion.refs_0_, bf16[128,512]{1,0:T(8,128)(2,1)S(1)} %collective-permute-done.refs_1_, bf16[128,512]{1,0:T(8,128)(2,1)S(1)} %collective-permute-done.1.refs_0_.refs_2_, ...), custom_call_target="tpu_custom_call" | custom-call | flops 1610612736 | bytes 5767168 | tf_op jit(solution)/shard_map/pallas_call | solution.py:226
  36.6 0.0 collective-permute-done.10.refs_5_.refs_2_
  36.6 0.0 collective-permute-done.11.refs_1_
  36.6 0.0 collective-permute-done.12.refs_2_
  36.6 1.6 %collective-permute-done.13.refs_3_ = f32[3,512]{1,0:T(4,128)S(1)} collective-permute-done((f32[3,512]{1,0:T(4,128)S(1)}, f32[3,512]{1,0:T(4,128)S(1)}, u32[]{:S(2)}, u32[]{:S(2)}) %collective-permute-start.13) | collective-permute-done | bytes 6176 | tf_op jit(solution)/shard_map/ppermute | solution.py:49
  38.3 0.0 collective-permute-done.9.a.refs_1_
  38.3 0.6 %collective-permute-start.14 = (bf16[256,512]{1,0:T(8,128)(2,1)S(1)}, bf16[256,512]{1,0:T(8,128)(2,1)S(1)}, u32[]{:S(2)}, u32[]{:S(2)}) collective-permute-start(bf16[256,512]{1,0:T(8,128)(2,1)S(1)} %shard_map.66), channel_id=1, source_target_pairs={{16,0},{12,4},{24,8},{4,12},{0,16},{28,20},{8,24},{20,28},{17,1},{... | collective-permute-start | bytes 786440 | tf_op jit(solution)/shard_map/ppermute | solution.py:49
  38.9 1.5 %collective-permute-start.15 = (f32[2,512]{1,0:T(2,128)S(1)}, f32[2,512]{1,0:T(2,128)S(1)}, u32[]{:S(2)}, u32[]{:S(2)}) collective-permute-start(f32[2,512]{1,0:T(2,128)S(1)} %shard_map.65.refs_0_), channel_id=1, source_target_pairs={{8,0},{20,4},{0,8},{28,12},{24,16},{4,20},{16,24},{12,28},{9,1},{2... | collective-permute-start | bytes 12296 | tf_op jit(solution)/shard_map/ppermute | solution.py:49
  40.4 1.4 %collective-permute-start.16 = (f32[2,512]{1,0:T(2,128)S(1)}, f32[2,512]{1,0:T(2,128)S(1)}, u32[]{:S(2)}, u32[]{:S(2)}) collective-permute-start(f32[2,512]{1,0:T(2,128)S(1)} %shard_map.65.refs_0_), channel_id=1, source_target_pairs={{16,0},{12,4},{24,8},{4,12},{0,16},{28,20},{8,24},{20,28},{17,1},{... | collective-permute-start | bytes 12296 | tf_op jit(solution)/shard_map/ppermute | solution.py:49
  41.8 0.5 %collective-permute-start.17 = (f32[2,512]{1,0:T(2,128)S(1)}, f32[2,512]{1,0:T(2,128)S(1)}, u32[]{:S(2)}, u32[]{:S(2)}) collective-permute-start(f32[2,512]{1,0:T(2,128)S(1)} %shard_map.65.refs_0_), channel_id=1, source_target_pairs={{24,0},{16,8},{8,16},{0,24},{25,1},{17,9},{9,17},{1,25},{26,2},{18... | collective-permute-start | bytes 12296 | tf_op jit(solution)/shard_map/ppermute | solution.py:49
  42.4 2.4 %collective-permute-done.14.refs_3_ = bf16[256,512]{1,0:T(8,128)(2,1)S(1)} collective-permute-done((bf16[256,512]{1,0:T(8,128)(2,1)S(1)}, bf16[256,512]{1,0:T(8,128)(2,1)S(1)}, u32[]{:S(2)}, u32[]{:S(2)}) %collective-permute-start.14) | collective-permute-done | bytes 262176 | tf_op jit(solution)/shard_map/ppermute | solution.py:49
  44.8 2.1 %shard_map.67 = (bf16[1536,1024]{1,0:T(8,128)(2,1)S(1)}, f32[6,1024]{1,0:T(8,128)S(1)}, bf16[1024,512]{1,0:T(8,128)(2,1)S(1)}) custom-call(bf16[256,512]{1,0:T(8,128)(2,1)S(1)} %shard_map.61.refs_0_, bf16[256,512]{1,0:T(8,128)(2,1)S(1)} %collective-permute-done.9.a.refs_1_, bf16[256,512]{1,0:T(8,128)(2,1)S(1)} %collective-permute-done.10.refs_5_.refs_2_, ...), custom_call_target="tpu_custom_call" | custom-call | flops 1610612736 | bytes 5767168 | tf_op jit(solution)/shard_map/pallas_call | solution.py:226
  46.9 0.0 collective-permute-done.15.refs_1_
  46.9 0.0 collective-permute-done.16.refs_2_
  46.9 0.0 collective-permute-done.17.refs_3_
  46.9 2.2 %shard_map.70 = (bf16[768,512]{1,0:T(8,128)(2,1)S(1)}, f32[1,768]{1,0:T(1,128)S(1)}) custom-call(bf16[1536,1024]{1,0:T(8,128)(2,1)S(1)} %get-tuple-element.16.refs_0_, bf16[1536,1024]{1,0:T(8,128)(2,1)S(1)} %get-tuple-element.18.refs_1_, bf16[1024,512]{1,0:T(8,128)(2,1)S(1)} %get-tuple-element.19.refs_2_, bf16[1024,512]{1,0:T(8,128)(2,1)S(1)} %get-tuple-element.20.refs_3_, ...), custom_call_target="tpu_custom_call" | custom-call | flops 1610612736 | bytes 6815744 | tf_op jit(solution)/shard_map/pallas_call | solution.py:276
  49.2 0.1 collective-permute-start.18
  49.3 0.5 collective-permute-start.19
  49.8 2.1 %shard_map.69 = (f32[768,512]{1,0:T(8,128)S(1)}, f32[1,768]{1,0:T(1,128)S(1)}) custom-call(bf16[1536,1024]{1,0:T(8,128)(2,1)S(1)} %get-tuple-element.16.refs_0_, bf16[1536,1024]{1,0:T(8,128)(2,1)S(1)} %get-tuple-element.18.refs_1_, bf16[1024,512]{1,0:T(8,128)(2,1)S(1)} %get-tuple-element.19.refs_2_, bf16[1024,512]{1,0:T(8,128)(2,1)S(1)} %get-tuple-element.20.refs_3_, ...), custom_call_target="tpu_custom_call" | custom-call | flops 1610612736 | bytes 6815744 | tf_op jit(solution)/shard_map/pallas_call | solution.py:276
  51.8 0.0 collective-permute-done.19.there_mass
  51.8 0.0 collective-permute-done.18.there
  51.8 1.8 %shard_map.71 = (f32[768,512]{1,0:T(8,128)}, f32[1,768]{1,0:T(1,128)}) custom-call(f32[768,512]{1,0:T(8,128)S(1)} %get-tuple-element.24.here, f32[1,768]{1,0:T(1,128)S(1)} %get-tuple-element.25.here_mass, bf16[768,512]{1,0:T(8,128)(2,1)S(1)} %collective-permute-done.18.there, f32[1,768]{1,0:T(1,128)S(1)} %collective-permute-done.19.there_mass), custom_call_target="tpu_custom_call" | custom-call | tf_op jit(solution)/shard_map/pallas_call | solution.py:306
  (6 shorter events, 0.1 us)
Async XLA Ops:
  2.3 8.9 %collective-permute-start = (bf16[128,512]{1,0:T(8,128)(2,1)S(1)}, bf16[128,512]{1,0:T(8,128)(2,1)S(1)}, u32[]{:S(2)}, u32[]{:S(2)}) collective-permute-start(bf16[128,512]{1,0:T(8,128)(2,1)S(1)} %multiply_convert_fusion.refs_0_), channel_id=1, source_target_pairs={{1,0},{0,1},{3,2},{2,3},{5,4},{4,5},{7,6},{6,7},{9,8},{8,9},{11,10... | collective-permute-start | bytes 393224 | tf_op jit(solution)/shard_map/ppermute | solution.py:49
  5.4 6.4 %collective-permute-start.1 = (bf16[128,512]{1,0:T(8,128)(2,1)S(1)}, bf16[128,512]{1,0:T(8,128)(2,1)S(1)}, u32[]{:S(2)}, u32[]{:S(2)}) collective-permute-start(bf16[128,512]{1,0:T(8,128)(2,1)S(1)} %multiply_convert_fusion.refs_0_), channel_id=1, source_target_pairs={{8,0},{20,4},{0,8},{28,12},{24,16},{4,20},{16,24},{12,28},{9,1},{2... | collective-permute-start | bytes 393224 | tf_op jit(solution)/shard_map/ppermute | solution.py:49
  6.9 8.0 %collective-permute-start.3 = (bf16[128,512]{1,0:T(8,128)(2,1)S(1)}, bf16[128,512]{1,0:T(8,128)(2,1)S(1)}, u32[]{:S(2)}, u32[]{:S(2)}) collective-permute-start(bf16[128,512]{1,0:T(8,128)(2,1)S(1)} %multiply_convert_fusion.refs_0_), channel_id=1, source_target_pairs={{16,0},{12,4},{24,8},{4,12},{0,16},{28,20},{8,24},{20,28},{17,1},{... | collective-permute-start | bytes 393224 | tf_op jit(solution)/shard_map/ppermute | solution.py:49
  8.4 11.4 %collective-permute-start.7 = (bf16[128,512]{1,0:T(8,128)(2,1)S(1)}, bf16[128,512]{1,0:T(8,128)(2,1)S(1)}, u32[]{:S(2)}, u32[]{:S(2)}) collective-permute-start(bf16[128,512]{1,0:T(8,128)(2,1)S(1)} %multiply_convert_fusion.refs_0_), channel_id=1, source_target_pairs={{2,0},{3,1},{0,2},{1,3},{6,4},{7,5},{4,6},{5,7},{10,8},{11,9},{8,1... | collective-permute-start | bytes 393224 | tf_op jit(solution)/shard_map/ppermute | solution.py:49
  11.0 8.8 %collective-permute-start.8 = (bf16[128,512]{1,0:T(8,128)(2,1)S(1)}, bf16[128,512]{1,0:T(8,128)(2,1)S(1)}, u32[]{:S(2)}, u32[]{:S(2)}) collective-permute-start(bf16[128,512]{1,0:T(8,128)(2,1)S(1)} %multiply_convert_fusion.refs_0_), channel_id=1, source_target_pairs={{3,0},{2,1},{1,2},{0,3},{7,4},{6,5},{5,6},{4,7},{11,8},{10,9},{9,1... | collective-permute-start | bytes 393224 | tf_op jit(solution)/shard_map/ppermute | solution.py:49
  11.2 10.7 %collective-permute-start.2 = (bf16[128,512]{1,0:T(8,128)(2,1)S(1)}, bf16[128,512]{1,0:T(8,128)(2,1)S(1)}, u32[]{:S(2)}, u32[]{:S(2)}) collective-permute-start(bf16[128,512]{1,0:T(8,128)(2,1)S(1)} %collective-permute-done.refs_1_), channel_id=1, source_target_pairs={{8,0},{20,4},{0,8},{28,12},{24,16},{4,20},{16,24},{12,28},{9,1},{2... | collective-permute-start | bytes 393224 | tf_op jit(solution)/shard_map/ppermute | solution.py:49
  11.8 11.3 %collective-permute-start.4 = (bf16[128,512]{1,0:T(8,128)(2,1)S(1)}, bf16[128,512]{1,0:T(8,128)(2,1)S(1)}, u32[]{:S(2)}, u32[]{:S(2)}) collective-permute-start(bf16[128,512]{1,0:T(8,128)(2,1)S(1)} %collective-permute-done.refs_1_), channel_id=1, source_target_pairs={{16,0},{12,4},{24,8},{4,12},{0,16},{28,20},{8,24},{20,28},{17,1},{... | collective-permute-start | bytes 393224 | tf_op jit(solution)/shard_map/ppermute | solution.py:49
  13.2 2.5 %slice-start = ((s8[6291456]{0:T(1024)(128)(4,1)}), s8[4194304]{0:T(1024)(128)(4,1)S(1)}, s32[]{:S(2)}) async-start(s8[6291456]{0:T(1024)(128)(4,1)} %bitcast.2), calls=%async_computation | async-start | bytes 8388608
  13.2 0.9 %copy-start = (s32[6144]{0:T(1024)S(1)}, s32[6144]{0:T(1024)}, u32[]{:S(2)}) copy-start(s32[6144]{0:T(1024)} %param.7) | copy-start | bytes 73732
  14.1 2.2 %slice-start.1 = ((s8[6291456]{0:T(1024)(128)(4,1)}), s8[2097152]{0:T(1024)(128)(4,1)S(1)}, s32[]{:S(2)}) async-start(s8[6291456]{0:T(1024)(128)(4,1)} %bitcast.2), calls=%async_computation.1 | async-start | bytes 4194304
  14.9 8.1 %collective-permute-start.5 = (bf16[128,512]{1,0:T(8,128)(2,1)S(1)}, bf16[128,512]{1,0:T(8,128)(2,1)S(1)}, u32[]{:S(2)}, u32[]{:S(2)}) collective-permute-start(bf16[128,512]{1,0:T(8,128)(2,1)S(1)} %collective-permute-done.1.refs_0_.refs_2_), channel_id=1, source_target_pairs={{16,0},{12,4},{24,8},{4,12},{0,16},{28,20},{8,24},{20,28},{17,1},{... | collective-permute-start | bytes 393224 | tf_op jit(solution)/shard_map/ppermute | solution.py:49
  19.9 16.7 %collective-permute-start.10 = (bf16[256,512]{1,0:T(8,128)(2,1)S(1)}, bf16[256,512]{1,0:T(8,128)(2,1)S(1)}, u32[]{:S(2)}, u32[]{:S(2)}) collective-permute-start(bf16[256,512]{1,0:T(8,128)(2,1)S(1)} %shard_map.61.refs_0_), channel_id=1, source_target_pairs={{16,0},{12,4},{24,8},{4,12},{0,16},{28,20},{8,24},{20,28},{17,1},{... | collective-permute-start | bytes 786440 | tf_op jit(solution)/shard_map/ppermute | solution.py:49
  21.0 17.3 %collective-permute-start.9 = (bf16[256,512]{1,0:T(8,128)(2,1)S(1)}, bf16[256,512]{1,0:T(8,128)(2,1)S(1)}, u32[]{:S(2)}, u32[]{:S(2)}) collective-permute-start(bf16[256,512]{1,0:T(8,128)(2,1)S(1)} %shard_map.61.refs_0_), channel_id=1, source_target_pairs={{8,0},{20,4},{0,8},{28,12},{24,16},{4,20},{16,24},{12,28},{9,1},{2... | collective-permute-start | bytes 786440 | tf_op jit(solution)/shard_map/ppermute | solution.py:49
  21.9 6.7 %collective-permute-start.6 = (bf16[128,512]{1,0:T(8,128)(2,1)S(1)}, bf16[128,512]{1,0:T(8,128)(2,1)S(1)}, u32[]{:S(2)}, u32[]{:S(2)}) collective-permute-start(bf16[128,512]{1,0:T(8,128)(2,1)S(1)} %collective-permute-done.2.refs_3_), channel_id=1, source_target_pairs={{16,0},{12,4},{24,8},{4,12},{0,16},{28,20},{8,24},{20,28},{17,1},{... | collective-permute-start | bytes 393224 | tf_op jit(solution)/shard_map/ppermute | solution.py:49
  28.7 7.9 %collective-permute-start.11 = (f32[3,512]{1,0:T(4,128)S(1)}, f32[3,512]{1,0:T(4,128)S(1)}, u32[]{:S(2)}, u32[]{:S(2)}) collective-permute-start(f32[3,512]{1,0:T(4,128)S(1)} %shard_map.64.refs_0_), channel_id=1, source_target_pairs={{1,0},{0,1},{3,2},{2,3},{5,4},{4,5},{7,6},{6,7},{9,8},{8,9},{11,10... | collective-permute-start | bytes 18440 | tf_op jit(solution)/shard_map/ppermute | solution.py:49
  32.0 4.6 %collective-permute-start.12 = (f32[3,512]{1,0:T(4,128)S(1)}, f32[3,512]{1,0:T(4,128)S(1)}, u32[]{:S(2)}, u32[]{:S(2)}) collective-permute-start(f32[3,512]{1,0:T(4,128)S(1)} %shard_map.64.refs_0_), channel_id=1, source_target_pairs={{2,0},{3,1},{0,2},{1,3},{6,4},{7,5},{4,6},{5,7},{10,8},{11,9},{8,1... | collective-permute-start | bytes 18440 | tf_op jit(solution)/shard_map/ppermute | solution.py:49
  32.8 5.4 %collective-permute-start.13 = (f32[3,512]{1,0:T(4,128)S(1)}, f32[3,512]{1,0:T(4,128)S(1)}, u32[]{:S(2)}, u32[]{:S(2)}) collective-permute-start(f32[3,512]{1,0:T(4,128)S(1)} %shard_map.64.refs_0_), channel_id=1, source_target_pairs={{3,0},{2,1},{1,2},{0,3},{7,4},{6,5},{5,6},{4,7},{11,8},{10,9},{9,1... | collective-permute-start | bytes 18440 | tf_op jit(solution)/shard_map/ppermute | solution.py:49
  38.3 6.4 %collective-permute-start.14 = (bf16[256,512]{1,0:T(8,128)(2,1)S(1)}, bf16[256,512]{1,0:T(8,128)(2,1)S(1)}, u32[]{:S(2)}, u32[]{:S(2)}) collective-permute-start(bf16[256,512]{1,0:T(8,128)(2,1)S(1)} %shard_map.66), channel_id=1, source_target_pairs={{16,0},{12,4},{24,8},{4,12},{0,16},{28,20},{8,24},{20,28},{17,1},{... | collective-permute-start | bytes 786440 | tf_op jit(solution)/shard_map/ppermute | solution.py:49
  38.9 8.0 %collective-permute-start.15 = (f32[2,512]{1,0:T(2,128)S(1)}, f32[2,512]{1,0:T(2,128)S(1)}, u32[]{:S(2)}, u32[]{:S(2)}) collective-permute-start(f32[2,512]{1,0:T(2,128)S(1)} %shard_map.65.refs_0_), channel_id=1, source_target_pairs={{8,0},{20,4},{0,8},{28,12},{24,16},{4,20},{16,24},{12,28},{9,1},{2... | collective-permute-start | bytes 12296 | tf_op jit(solution)/shard_map/ppermute | solution.py:49
  40.4 6.5 %collective-permute-start.16 = (f32[2,512]{1,0:T(2,128)S(1)}, f32[2,512]{1,0:T(2,128)S(1)}, u32[]{:S(2)}, u32[]{:S(2)}) collective-permute-start(f32[2,512]{1,0:T(2,128)S(1)} %shard_map.65.refs_0_), channel_id=1, source_target_pairs={{16,0},{12,4},{24,8},{4,12},{0,16},{28,20},{8,24},{20,28},{17,1},{... | collective-permute-start | bytes 12296 | tf_op jit(solution)/shard_map/ppermute | solution.py:49
  41.8 5.1 %collective-permute-start.17 = (f32[2,512]{1,0:T(2,128)S(1)}, f32[2,512]{1,0:T(2,128)S(1)}, u32[]{:S(2)}, u32[]{:S(2)}) collective-permute-start(f32[2,512]{1,0:T(2,128)S(1)} %shard_map.65.refs_0_), channel_id=1, source_target_pairs={{24,0},{16,8},{8,16},{0,24},{25,1},{17,9},{9,17},{1,25},{26,2},{18... | collective-permute-start | bytes 12296 | tf_op jit(solution)/shard_map/ppermute | solution.py:49
  49.2 2.6 %collective-permute-start.18 = (bf16[768,512]{1,0:T(8,128)(2,1)S(1)}, bf16[768,512]{1,0:T(8,128)(2,1)S(1)}, u32[]{:S(2)}, u32[]{:S(2)}) collective-permute-start(bf16[768,512]{1,0:T(8,128)(2,1)S(1)} %get-tuple-element.26), channel_id=1, source_target_pairs={{4,0},{0,4},{5,1},{1,5},{6,2},{2,6},{7,3},{3,7},{12,8},{8,12},{13,... | collective-permute-start | bytes 2359304 | tf_op jit(solution)/shard_map/ppermute | solution.py:49
  49.3 2.6 %collective-permute-start.19 = (f32[1,768]{1,0:T(1,128)S(1)}, f32[1,768]{1,0:T(1,128)S(1)}, u32[]{:S(2)}, u32[]{:S(2)}) collective-permute-start(f32[1,768]{1,0:T(1,128)S(1)} %get-tuple-element.27), channel_id=1, source_target_pairs={{4,0},{0,4},{5,1},{1,5},{6,2},{2,6},{7,3},{3,7},{12,8},{8,12},{13,... | collective-permute-start | bytes 9224 | tf_op jit(solution)/shard_map/ppermute | solution.py:49

commit v12 on v11

--- a/solution.py
+++ b/solution.py
@@ -339,16 +339,18 @@
     across_0, across_1 = turn_back(first_0), turn_back(first_1)
     inverse = inverse_call(counters, first_0, near_1)
     stats = [totals_call(rate, block, (own, near_1), centroids, inverse, after=(second_0,))]
-    near_23, first_23, second_23 = expand(join(near_2, near_3, *stats))
-    stats.append(totals_call(rate, block, (near_23,), centroids, inverse, after=(first_1, second_1, across_0)))
+    near_23 = join(near_2, near_3, *stats)
+    first_23 = turn(near_23)
+    after = (first_1, second_1, across_0, across_1)
+    stats.append(totals_call(rate, block, (near_23,), centroids, inverse, after=after))
+    second_23, across_23 = turn_back(hold(near_23, stats[1])), turn_back(hold(first_23, stats[1]))
 
     expand = functools.partial(expo_call, rate, block, 2 * per_device)
     groups = [expand((own, near_1, first_0, first_1, second_0, second_1, across_0, across_1), centroids, stats[1])]
     tops = groups[0][1]
-    stat = beside(*stats, across_1)
+    stat = beside(*stats)
     theirs = [along_z(stat, by) for by in (1, 2, 3)]
     goal = goal_call(rate, stat, *theirs, tops, second_23)
-    across_23 = turn_back(hold(first_23, goal))
     groups.append(expand((near_23, first_23, second_23, across_23), centroids))
     expos, tops, points = zip(*groups)
     goals = [goal, turn(goal), turn_back(goal), around(goal, 3)]

time: 54 us -> 54 us (level)
  waiting for transfers between devices: 7.46 us -> 9.46 us
  starting transfers between devices: 25.1 us -> 23.6 us
  local copies, waits for them, and re-layouts: 1.48 us -> 0.89 us
    ppermute x20, waiting for transfers between devices: 7.46 us -> 9.46 us  [exchange(): return lax.ppermute(a, axes, [(partner(at), at) for at in range(count)])]
    ppermute x20, starting transfers between devices: 25.1 us -> 23.6 us  [exchange(): return lax.ppermute(a, axes, [(partner(at), at) for at in range(count)])]
    unnamed x6, local copies, waits for them, and re-layouts: 1.48 us -> 0.89 us
  transfers between devices with their start and end apart: 20 -> 20, of which waited for: 4 -> 5; matrix products, arithmetic and copies ran while one was open for 0% -> 0% of each run, Pallas kernels for 24% -> 24%
where the time goes in v12:
time: 54 us; the launch traced here: 53.8 us
  starting transfers between devices  23.6 us (44%)
  Pallas kernels  17.2 us (32%)
  waiting for transfers between devices  9.46 us (18%)
  other arithmetic  1.69 us (3%)
  between operations  0.96 us (2%)
  local copies, waits for them, and re-layouts  0.89 us (2%)
    ppermute x20, starting transfers between devices, exchange(): return lax.ppermute(a, axes, [(partner(at), at) for at in range(count)])  23.6 us
    ppermute x20, waiting for transfers between devices, exchange(): return lax.ppermute(a, axes, [(partner(at), at) for at in range(count)])  9.46 us
    pallas_call x2, Pallas kernels, totals_call(): pl.pallas_call(functools.partial(totals_kernel, rate, block, len(pieces))...  5.82 us
    pallas_call x2, Pallas kernels, sums_call(): pl.pallas_call(functools.partial(sums_kernel, n, block, side), in_specs=i...  4.32 us
    pallas_call x2, Pallas kernels, expo_call(): pl.pallas_call(functools.partial(expo_kernel, rate, block, len(pieces)),...  4.23 us
    pallas_call x1, Pallas kernels, add_call(): pl.pallas_call(functools.partial(add_kernel, block), in_specs=in_vmem(4),...  1.79 us
  transfers between devices with their start and end apart: 20, of which 5 were waited for; matrix products, arithmetic and copies ran while one was open for 0% of the time, Pallas kernels for 24%

profile of v12, /device:TPU:0, one launch (start us, length us, event | category | flops | bytes accessed | tf_op | source)
XLA Modules:
  0.0 53.8 jit_solution(8639701866422154437)
XLA Ops:
  0.6 0.7 %convert_multiply_fusion = f32[128]{0:T(128)S(1)} fusion(s32[128]{0:T(128)} %param.5), kind=kLoop, calls=%fused_computation.1 | loop fusion | flops 512 | bytes 1024 | tf_op jit(solution)/shard_map/mul | solution.py:16
  1.3 1.0 %multiply_convert_fusion.refs_0_ = bf16[128,512]{1,0:T(8,128)(2,1)S(1)} fusion(s32[128,512]{1,0:T(8,128)} %param.4, f32[128]{0:T(128)S(1)} %convert_multiply_fusion), kind=kLoop, calls=%fused_computation | loop fusion | flops 196608 | bytes 393728 | tf_op jit(solution)/shard_map/convert_element_type | solution.py:17
  2.3 3.1 %collective-permute-start = (bf16[128,512]{1,0:T(8,128)(2,1)S(1)}, bf16[128,512]{1,0:T(8,128)(2,1)S(1)}, u32[]{:S(2)}, u32[]{:S(2)}) collective-permute-start(bf16[128,512]{1,0:T(8,128)(2,1)S(1)} %multiply_convert_fusion.refs_0_), channel_id=1, source_target_pairs={{1,0},{0,1},{3,2},{2,3},{5,4},{4,5},{7,6},{6,7},{9,8},{8,9},{11,10... | collective-permute-start | bytes 393224 | tf_op jit(solution)/shard_map/ppermute | solution.py:49
  5.4 1.5 %collective-permute-start.1 = (bf16[128,512]{1,0:T(8,128)(2,1)S(1)}, bf16[128,512]{1,0:T(8,128)(2,1)S(1)}, u32[]{:S(2)}, u32[]{:S(2)}) collective-permute-start(bf16[128,512]{1,0:T(8,128)(2,1)S(1)} %multiply_convert_fusion.refs_0_), channel_id=1, source_target_pairs={{8,0},{20,4},{0,8},{28,12},{24,16},{4,20},{16,24},{12,28},{9,1},{2... | collective-permute-start | bytes 393224 | tf_op jit(solution)/shard_map/ppermute | solution.py:49
  6.9 1.5 %collective-permute-start.3 = (bf16[128,512]{1,0:T(8,128)(2,1)S(1)}, bf16[128,512]{1,0:T(8,128)(2,1)S(1)}, u32[]{:S(2)}, u32[]{:S(2)}) collective-permute-start(bf16[128,512]{1,0:T(8,128)(2,1)S(1)} %multiply_convert_fusion.refs_0_), channel_id=1, source_target_pairs={{16,0},{12,4},{24,8},{4,12},{0,16},{28,20},{8,24},{20,28},{17,1},{... | collective-permute-start | bytes 393224 | tf_op jit(solution)/shard_map/ppermute | solution.py:49
  8.4 2.6 %collective-permute-start.7 = (bf16[128,512]{1,0:T(8,128)(2,1)S(1)}, bf16[128,512]{1,0:T(8,128)(2,1)S(1)}, u32[]{:S(2)}, u32[]{:S(2)}) collective-permute-start(bf16[128,512]{1,0:T(8,128)(2,1)S(1)} %multiply_convert_fusion.refs_0_), channel_id=1, source_target_pairs={{2,0},{3,1},{0,2},{1,3},{6,4},{7,5},{4,6},{5,7},{10,8},{11,9},{8,1... | collective-permute-start | bytes 393224 | tf_op jit(solution)/shard_map/ppermute | solution.py:49
  11.0 0.2 collective-permute-start.8
  11.2 0.0 collective-permute-done.refs_1_
  11.2 0.5 collective-permute-start.2
  11.8 0.0 collective-permute-done.1.refs_0_.refs_2_
  11.8 1.4 %collective-permute-start.4 = (bf16[128,512]{1,0:T(8,128)(2,1)S(1)}, bf16[128,512]{1,0:T(8,128)(2,1)S(1)}, u32[]{:S(2)}, u32[]{:S(2)}) collective-permute-start(bf16[128,512]{1,0:T(8,128)(2,1)S(1)} %collective-permute-done.refs_1_), channel_id=1, source_target_pairs={{16,0},{12,4},{24,8},{4,12},{0,16},{28,20},{8,24},{20,28},{17,1},{... | collective-permute-start | bytes 393224 | tf_op jit(solution)/shard_map/ppermute | solution.py:49
  13.2 0.0 slice-start
  13.2 0.0 copy-start
  13.2 0.9 %copy-done = s32[6144]{0:T(1024)S(1)} copy-done((s32[6144]{0:T(1024)S(1)}, s32[6144]{0:T(1024)}, u32[]{:S(2)}) %copy-start) | copy-done | bytes 24600
  14.1 0.0 slice-start.1
  14.1 0.9 %shard_map.59.refs_3_.refs_2_ = f32[6144,128]{1,0:T(8,128)S(1)} custom-call(s32[48,128]{1,0:T(8,128)S(1)} %bitcast.4, bf16[128,512]{1,0:T(8,128)(2,1)S(1)} %collective-permute-done.1.refs_0_.refs_2_, bf16[128,512]{1,0:T(8,128)(2,1)S(1)} %collective-permute-done.refs_1_), custom_call_target="tpu_custom_call" | custom-call | flops 4000000000 | tf_op jit(solution)/shard_map/pallas_call | solution.py:113
  14.9 0.0 collective-permute-done.3.refs_4_
  14.9 0.7 %collective-permute-start.5 = (bf16[128,512]{1,0:T(8,128)(2,1)S(1)}, bf16[128,512]{1,0:T(8,128)(2,1)S(1)}, u32[]{:S(2)}, u32[]{:S(2)}) collective-permute-start(bf16[128,512]{1,0:T(8,128)(2,1)S(1)} %collective-permute-done.1.refs_0_.refs_2_), channel_id=1, source_target_pairs={{16,0},{12,4},{24,8},{4,12},{0,16},{28,20},{8,24},{20,28},{17,1},{... | collective-permute-start | bytes 393224 | tf_op jit(solution)/shard_map/ppermute | solution.py:49
  15.7 1.8 %collective-permute-done.2.refs_3_ = bf16[128,512]{1,0:T(8,128)(2,1)S(1)} collective-permute-done((bf16[128,512]{1,0:T(8,128)(2,1)S(1)}, bf16[128,512]{1,0:T(8,128)(2,1)S(1)}, u32[]{:S(2)}, u32[]{:S(2)}) %collective-permute-start.2) | collective-permute-done | bytes 131104 | tf_op jit(solution)/shard_map/ppermute | solution.py:49
  17.5 0.0 collective-permute-start.6
  17.5 0.0 slice-done
  17.5 0.0 slice-done.1
  17.5 2.9 %shard_map.60.refs_0_.left = f32[3,256]{1,0:T(4,128)S(1)} custom-call(bf16[128,512]{1,0:T(8,128)(2,1)S(1)} %multiply_convert_fusion.refs_0_, bf16[128,512]{1,0:T(8,128)(2,1)S(1)} %collective-permute-done.refs_1_, bf16[6144,512]{1,0:T(8,128)(2,1)S(1)} %bitcast.3, f32[6144,128]{1,0:T(8,128)S(1)} %shard_map.59.refs_3_.refs_2_, ...), custom_call_target="tpu_custom_call" | custom-call | flops 1610612736 | bytes 6291456 | tf_op jit(solution)/shard_map/pallas_call | solution.py:153
  20.4 0.0 collective-permute-done.7.above
  20.5 0.0 collective-permute-done.8.below
  20.5 1.1 %collective-permute-start.9 = (bf16[256,512]{1,0:T(8,128)(2,1)S(1)}, bf16[256,512]{1,0:T(8,128)(2,1)S(1)}, u32[]{:S(2)}, u32[]{:S(2)}) collective-permute-start(bf16[256,512]{1,0:T(8,128)(2,1)S(1)} %shard_map.61.refs_0_.a), channel_id=1, source_target_pairs={{8,0},{20,4},{0,8},{28,12},{24,16},{4,20},{16,24},{12,28},{9,1},{2... | collective-permute-start | bytes 786440 | tf_op jit(solution)/shard_map/ppermute | solution.py:49
  21.6 0.0 collective-permute-done.4.refs_4_.refs_5_
  21.6 0.0 collective-permute-done.5.refs_5_.refs_6_
  21.6 1.8 %collective-permute-done.6.refs_6_.refs_7_ = bf16[128,512]{1,0:T(8,128)(2,1)S(1)} collective-permute-done((bf16[128,512]{1,0:T(8,128)(2,1)S(1)}, bf16[128,512]{1,0:T(8,128)(2,1)S(1)}, u32[]{:S(2)}, u32[]{:S(2)}) %collective-permute-start.6) | collective-permute-done | bytes 131104 | tf_op jit(solution)/shard_map/ppermute | solution.py:49
  23.4 2.9 %shard_map.62.refs_9_.refs_0_.right = f32[3,256]{1,0:T(4,128)S(1)} custom-call(bf16[256,512]{1,0:T(8,128)(2,1)S(1)} %shard_map.61.refs_0_.a, bf16[6144,512]{1,0:T(8,128)(2,1)S(1)} %bitcast.3, f32[6144,128]{1,0:T(8,128)S(1)} %shard_map.59.refs_3_.refs_2_, bf16[128,512]{1,0:T(8,128)(2,1)S(1)} %collective-permute-done.2.refs_3_, ...), custom_call_target="tpu_custom_call" | custom-call | flops 1610612736 | bytes 6291456 | tf_op jit(solution)/shard_map/pallas_call | solution.py:153
  26.4 0.1 collective-permute-start.10
  26.4 2.7 %collective-permute-done.9.a.refs_1_ = bf16[256,512]{1,0:T(8,128)(2,1)S(1)} collective-permute-done((bf16[256,512]{1,0:T(8,128)(2,1)S(1)}, bf16[256,512]{1,0:T(8,128)(2,1)S(1)}, u32[]{:S(2)}, u32[]{:S(2)}) %collective-permute-start.9) | collective-permute-done | bytes 262176 | tf_op jit(solution)/shard_map/ppermute | solution.py:49
  29.2 2.4 %collective-permute-start.11 = (bf16[256,512]{1,0:T(8,128)(2,1)S(1)}, bf16[256,512]{1,0:T(8,128)(2,1)S(1)}, u32[]{:S(2)}, u32[]{:S(2)}) collective-permute-start(bf16[256,512]{1,0:T(8,128)(2,1)S(1)} %shard_map.65), channel_id=1, source_target_pairs={{16,0},{12,4},{24,8},{4,12},{0,16},{28,20},{8,24},{20,28},{17,1},{... | collective-permute-start | bytes 786440 | tf_op jit(solution)/shard_map/ppermute | solution.py:49
  31.6 0.0 collective-permute-start.12
  31.6 3.1 %collective-permute-start.13 = (f32[3,512]{1,0:T(4,128)S(1)}, f32[3,512]{1,0:T(4,128)S(1)}, u32[]{:S(2)}, u32[]{:S(2)}) collective-permute-start(f32[3,512]{1,0:T(4,128)S(1)} %shard_map.67.refs_0_), channel_id=1, source_target_pairs={{2,0},{3,1},{0,2},{1,3},{6,4},{7,5},{4,6},{5,7},{10,8},{11,9},{8,1... | collective-permute-start | bytes 18440 | tf_op jit(solution)/shard_map/ppermute | solution.py:49
  34.7 1.3 %collective-permute-start.14 = (f32[3,512]{1,0:T(4,128)S(1)}, f32[3,512]{1,0:T(4,128)S(1)}, u32[]{:S(2)}, u32[]{:S(2)}) collective-permute-start(f32[3,512]{1,0:T(4,128)S(1)} %shard_map.67.refs_0_), channel_id=1, source_target_pairs={{3,0},{2,1},{1,2},{0,3},{7,4},{6,5},{5,6},{4,7},{11,8},{10,9},{9,1... | collective-permute-start | bytes 18440 | tf_op jit(solution)/shard_map/ppermute | solution.py:49
  36.0 2.1 %shard_map.63 = (bf16[1536,1024]{1,0:T(8,128)(2,1)S(1)}, f32[6,1024]{1,0:T(8,128)S(1)}, bf16[1024,512]{1,0:T(8,128)(2,1)S(1)}) custom-call(bf16[128,512]{1,0:T(8,128)(2,1)S(1)} %multiply_convert_fusion.refs_0_, bf16[128,512]{1,0:T(8,128)(2,1)S(1)} %collective-permute-done.refs_1_, bf16[128,512]{1,0:T(8,128)(2,1)S(1)} %collective-permute-done.1.refs_0_.refs_2_, ...), custom_call_target="tpu_custom_call" | custom-call | flops 1610612736 | bytes 5767168 | tf_op jit(solution)/shard_map/pallas_call | solution.py:226
  38.1 0.0 collective-permute-done.12.refs_1_
  38.1 0.0 collective-permute-done.13.refs_2_
  38.1 2.0 %collective-permute-done.14.refs_3_ = f32[3,512]{1,0:T(4,128)S(1)} collective-permute-done((f32[3,512]{1,0:T(4,128)S(1)}, f32[3,512]{1,0:T(4,128)S(1)}, u32[]{:S(2)}, u32[]{:S(2)}) %collective-permute-start.14) | collective-permute-done | bytes 6176 | tf_op jit(solution)/shard_map/ppermute | solution.py:49
  40.2 0.0 collective-permute-done.10.refs_2_.refs_5_
  40.2 2.0 %collective-permute-start.15 = (f32[2,512]{1,0:T(2,128)S(1)}, f32[2,512]{1,0:T(2,128)S(1)}, u32[]{:S(2)}, u32[]{:S(2)}) collective-permute-start(f32[2,512]{1,0:T(2,128)S(1)} %shard_map.68.refs_0_), channel_id=1, source_target_pairs={{8,0},{20,4},{0,8},{28,12},{24,16},{4,20},{16,24},{12,28},{9,1},{2... | collective-permute-start | bytes 12296 | tf_op jit(solution)/shard_map/ppermute | solution.py:49
  42.2 0.2 collective-permute-start.16
  42.4 1.4 %collective-permute-start.17 = (f32[2,512]{1,0:T(2,128)S(1)}, f32[2,512]{1,0:T(2,128)S(1)}, u32[]{:S(2)}, u32[]{:S(2)}) collective-permute-start(f32[2,512]{1,0:T(2,128)S(1)} %shard_map.68.refs_0_), channel_id=1, source_target_pairs={{24,0},{16,8},{8,16},{0,24},{25,1},{17,9},{9,17},{1,25},{26,2},{18... | collective-permute-start | bytes 12296 | tf_op jit(solution)/shard_map/ppermute | solution.py:49
  43.8 0.0 collective-permute-done.11.refs_3_
  43.8 2.1 %shard_map.66 = (bf16[1536,1024]{1,0:T(8,128)(2,1)S(1)}, f32[6,1024]{1,0:T(8,128)S(1)}, bf16[1024,512]{1,0:T(8,128)(2,1)S(1)}) custom-call(bf16[256,512]{1,0:T(8,128)(2,1)S(1)} %shard_map.61.refs_0_.a, bf16[256,512]{1,0:T(8,128)(2,1)S(1)} %collective-permute-done.9.a.refs_1_, bf16[256,512]{1,0:T(8,128)(2,1)S(1)} %collective-permute-done.10.refs_2_.refs_5_, ...), custom_call_target="tpu_custom_call" | custom-call | flops 1610612736 | bytes 5767168 | tf_op jit(solution)/shard_map/pallas_call | solution.py:226
  45.9 0.0 collective-permute-done.15.refs_1_
  45.9 0.0 collective-permute-done.16.refs_2_
  45.9 1.0 %collective-permute-done.17.refs_3_ = f32[2,512]{1,0:T(2,128)S(1)} collective-permute-done((f32[2,512]{1,0:T(2,128)S(1)}, f32[2,512]{1,0:T(2,128)S(1)}, u32[]{:S(2)}, u32[]{:S(2)}) %collective-permute-start.17) | collective-permute-done | bytes 4128 | tf_op jit(solution)/shard_map/ppermute | solution.py:49
  46.9 2.3 %shard_map.71 = (bf16[768,512]{1,0:T(8,128)(2,1)S(1)}, f32[1,768]{1,0:T(1,128)S(1)}) custom-call(bf16[1536,1024]{1,0:T(8,128)(2,1)S(1)} %get-tuple-element.16.refs_0_, bf16[1536,1024]{1,0:T(8,128)(2,1)S(1)} %get-tuple-element.17.refs_1_, bf16[1024,512]{1,0:T(8,128)(2,1)S(1)} %get-tuple-element.18.refs_2_, bf16[1024,512]{1,0:T(8,128)(2,1)S(1)} %get-tuple-element.19.refs_3_, ...), custom_call_target="tpu_custom_call" | custom-call | flops 1610612736 | bytes 6815744 | tf_op jit(solution)/shard_map/pallas_call | solution.py:276
  49.2 0.1 collective-permute-start.18
  49.3 0.5 collective-permute-start.19
  49.8 2.1 %shard_map.70 = (f32[768,512]{1,0:T(8,128)S(1)}, f32[1,768]{1,0:T(1,128)S(1)}) custom-call(bf16[1536,1024]{1,0:T(8,128)(2,1)S(1)} %get-tuple-element.16.refs_0_, bf16[1536,1024]{1,0:T(8,128)(2,1)S(1)} %get-tuple-element.17.refs_1_, bf16[1024,512]{1,0:T(8,128)(2,1)S(1)} %get-tuple-element.18.refs_2_, bf16[1024,512]{1,0:T(8,128)(2,1)S(1)} %get-tuple-element.19.refs_3_, ...), custom_call_target="tpu_custom_call" | custom-call | flops 1610612736 | bytes 6815744 | tf_op jit(solution)/shard_map/pallas_call | solution.py:276
  51.8 0.0 collective-permute-done.19.there_mass
  51.9 0.0 collective-permute-done.18.there
  51.9 1.8 %shard_map.72 = (f32[768,512]{1,0:T(8,128)}, f32[1,768]{1,0:T(1,128)}) custom-call(f32[768,512]{1,0:T(8,128)S(1)} %get-tuple-element.24.here, f32[1,768]{1,0:T(1,128)S(1)} %get-tuple-element.25.here_mass, bf16[768,512]{1,0:T(8,128)(2,1)S(1)} %collective-permute-done.18.there, f32[1,768]{1,0:T(1,128)S(1)} %collective-permute-done.19.there_mass), custom_call_target="tpu_custom_call" | custom-call | tf_op jit(solution)/shard_map/pallas_call | solution.py:306
  (7 shorter events, 0.1 us)
Async XLA Ops:
  2.3 8.9 %collective-permute-start = (bf16[128,512]{1,0:T(8,128)(2,1)S(1)}, bf16[128,512]{1,0:T(8,128)(2,1)S(1)}, u32[]{:S(2)}, u32[]{:S(2)}) collective-permute-start(bf16[128,512]{1,0:T(8,128)(2,1)S(1)} %multiply_convert_fusion.refs_0_), channel_id=1, source_target_pairs={{1,0},{0,1},{3,2},{2,3},{5,4},{4,5},{7,6},{6,7},{9,8},{8,9},{11,10... | collective-permute-start | bytes 393224 | tf_op jit(solution)/shard_map/ppermute | solution.py:49
  5.4 6.4 %collective-permute-start.1 = (bf16[128,512]{1,0:T(8,128)(2,1)S(1)}, bf16[128,512]{1,0:T(8,128)(2,1)S(1)}, u32[]{:S(2)}, u32[]{:S(2)}) collective-permute-start(bf16[128,512]{1,0:T(8,128)(2,1)S(1)} %multiply_convert_fusion.refs_0_), channel_id=1, source_target_pairs={{8,0},{20,4},{0,8},{28,12},{24,16},{4,20},{16,24},{12,28},{9,1},{2... | collective-permute-start | bytes 393224 | tf_op jit(solution)/shard_map/ppermute | solution.py:49
  6.9 8.0 %collective-permute-start.3 = (bf16[128,512]{1,0:T(8,128)(2,1)S(1)}, bf16[128,512]{1,0:T(8,128)(2,1)S(1)}, u32[]{:S(2)}, u32[]{:S(2)}) collective-permute-start(bf16[128,512]{1,0:T(8,128)(2,1)S(1)} %multiply_convert_fusion.refs_0_), channel_id=1, source_target_pairs={{16,0},{12,4},{24,8},{4,12},{0,16},{28,20},{8,24},{20,28},{17,1},{... | collective-permute-start | bytes 393224 | tf_op jit(solution)/shard_map/ppermute | solution.py:49
  8.4 12.0 %collective-permute-start.7 = (bf16[128,512]{1,0:T(8,128)(2,1)S(1)}, bf16[128,512]{1,0:T(8,128)(2,1)S(1)}, u32[]{:S(2)}, u32[]{:S(2)}) collective-permute-start(bf16[128,512]{1,0:T(8,128)(2,1)S(1)} %multiply_convert_fusion.refs_0_), channel_id=1, source_target_pairs={{2,0},{3,1},{0,2},{1,3},{6,4},{7,5},{4,6},{5,7},{10,8},{11,9},{8,1... | collective-permute-start | bytes 393224 | tf_op jit(solution)/shard_map/ppermute | solution.py:49
  11.0 9.4 %collective-permute-start.8 = (bf16[128,512]{1,0:T(8,128)(2,1)S(1)}, bf16[128,512]{1,0:T(8,128)(2,1)S(1)}, u32[]{:S(2)}, u32[]{:S(2)}) collective-permute-start(bf16[128,512]{1,0:T(8,128)(2,1)S(1)} %multiply_convert_fusion.refs_0_), channel_id=1, source_target_pairs={{3,0},{2,1},{1,2},{0,3},{7,4},{6,5},{5,6},{4,7},{11,8},{10,9},{9,1... | collective-permute-start | bytes 393224 | tf_op jit(solution)/shard_map/ppermute | solution.py:49
  11.2 6.2 %collective-permute-start.2 = (bf16[128,512]{1,0:T(8,128)(2,1)S(1)}, bf16[128,512]{1,0:T(8,128)(2,1)S(1)}, u32[]{:S(2)}, u32[]{:S(2)}) collective-permute-start(bf16[128,512]{1,0:T(8,128)(2,1)S(1)} %collective-permute-done.refs_1_), channel_id=1, source_target_pairs={{8,0},{20,4},{0,8},{28,12},{24,16},{4,20},{16,24},{12,28},{9,1},{2... | collective-permute-start | bytes 393224 | tf_op jit(solution)/shard_map/ppermute | solution.py:49
  11.8 9.8 %collective-permute-start.4 = (bf16[128,512]{1,0:T(8,128)(2,1)S(1)}, bf16[128,512]{1,0:T(8,128)(2,1)S(1)}, u32[]{:S(2)}, u32[]{:S(2)}) collective-permute-start(bf16[128,512]{1,0:T(8,128)(2,1)S(1)} %collective-permute-done.refs_1_), channel_id=1, source_target_pairs={{16,0},{12,4},{24,8},{4,12},{0,16},{28,20},{8,24},{20,28},{17,1},{... | collective-permute-start | bytes 393224 | tf_op jit(solution)/shard_map/ppermute | solution.py:49
  13.2 4.4 %slice-start = ((s8[6291456]{0:T(1024)(128)(4,1)}), s8[4194304]{0:T(1024)(128)(4,1)S(1)}, s32[]{:S(2)}) async-start(s8[6291456]{0:T(1024)(128)(4,1)} %bitcast.2), calls=%async_computation | async-start | bytes 8388608
  13.2 0.9 %copy-start = (s32[6144]{0:T(1024)S(1)}, s32[6144]{0:T(1024)}, u32[]{:S(2)}) copy-start(s32[6144]{0:T(1024)} %param.7) | copy-start | bytes 73732
  14.1 3.5 %slice-start.1 = ((s8[6291456]{0:T(1024)(128)(4,1)}), s8[2097152]{0:T(1024)(128)(4,1)S(1)}, s32[]{:S(2)}) async-start(s8[6291456]{0:T(1024)(128)(4,1)} %bitcast.2), calls=%async_computation.1 | async-start | bytes 4194304
  14.9 6.6 %collective-permute-start.5 = (bf16[128,512]{1,0:T(8,128)(2,1)S(1)}, bf16[128,512]{1,0:T(8,128)(2,1)S(1)}, u32[]{:S(2)}, u32[]{:S(2)}) collective-permute-start(bf16[128,512]{1,0:T(8,128)(2,1)S(1)} %collective-permute-done.1.refs_0_.refs_2_), channel_id=1, source_target_pairs={{16,0},{12,4},{24,8},{4,12},{0,16},{28,20},{8,24},{20,28},{17,1},{... | collective-permute-start | bytes 393224 | tf_op jit(solution)/shard_map/ppermute | solution.py:49
  17.5 5.9 %collective-permute-start.6 = (bf16[128,512]{1,0:T(8,128)(2,1)S(1)}, bf16[128,512]{1,0:T(8,128)(2,1)S(1)}, u32[]{:S(2)}, u32[]{:S(2)}) collective-permute-start(bf16[128,512]{1,0:T(8,128)(2,1)S(1)} %collective-permute-done.2.refs_3_), channel_id=1, source_target_pairs={{16,0},{12,4},{24,8},{4,12},{0,16},{28,20},{8,24},{20,28},{17,1},{... | collective-permute-start | bytes 393224 | tf_op jit(solution)/shard_map/ppermute | solution.py:49
  20.5 8.7 %collective-permute-start.9 = (bf16[256,512]{1,0:T(8,128)(2,1)S(1)}, bf16[256,512]{1,0:T(8,128)(2,1)S(1)}, u32[]{:S(2)}, u32[]{:S(2)}) collective-permute-start(bf16[256,512]{1,0:T(8,128)(2,1)S(1)} %shard_map.61.refs_0_.a), channel_id=1, source_target_pairs={{8,0},{20,4},{0,8},{28,12},{24,16},{4,20},{16,24},{12,28},{9,1},{2... | collective-permute-start | bytes 786440 | tf_op jit(solution)/shard_map/ppermute | solution.py:49
  26.4 13.8 %collective-permute-start.10 = (bf16[256,512]{1,0:T(8,128)(2,1)S(1)}, bf16[256,512]{1,0:T(8,128)(2,1)S(1)}, u32[]{:S(2)}, u32[]{:S(2)}) collective-permute-start(bf16[256,512]{1,0:T(8,128)(2,1)S(1)} %shard_map.64), channel_id=1, source_target_pairs={{16,0},{12,4},{24,8},{4,12},{0,16},{28,20},{8,24},{20,28},{17,1},{... | collective-permute-start | bytes 786440 | tf_op jit(solution)/shard_map/ppermute | solution.py:49
  29.2 14.6 %collective-permute-start.11 = (bf16[256,512]{1,0:T(8,128)(2,1)S(1)}, bf16[256,512]{1,0:T(8,128)(2,1)S(1)}, u32[]{:S(2)}, u32[]{:S(2)}) collective-permute-start(bf16[256,512]{1,0:T(8,128)(2,1)S(1)} %shard_map.65), channel_id=1, source_target_pairs={{16,0},{12,4},{24,8},{4,12},{0,16},{28,20},{8,24},{20,28},{17,1},{... | collective-permute-start | bytes 786440 | tf_op jit(solution)/shard_map/ppermute | solution.py:49
  31.6 6.5 %collective-permute-start.12 = (f32[3,512]{1,0:T(4,128)S(1)}, f32[3,512]{1,0:T(4,128)S(1)}, u32[]{:S(2)}, u32[]{:S(2)}) collective-permute-start(f32[3,512]{1,0:T(4,128)S(1)} %shard_map.67.refs_0_), channel_id=1, source_target_pairs={{1,0},{0,1},{3,2},{2,3},{5,4},{4,5},{7,6},{6,7},{9,8},{8,9},{11,10... | collective-permute-start | bytes 18440 | tf_op jit(solution)/shard_map/ppermute | solution.py:49
  31.6 6.5 %collective-permute-start.13 = (f32[3,512]{1,0:T(4,128)S(1)}, f32[3,512]{1,0:T(4,128)S(1)}, u32[]{:S(2)}, u32[]{:S(2)}) collective-permute-start(f32[3,512]{1,0:T(4,128)S(1)} %shard_map.67.refs_0_), channel_id=1, source_target_pairs={{2,0},{3,1},{0,2},{1,3},{6,4},{7,5},{4,6},{5,7},{10,8},{11,9},{8,1... | collective-permute-start | bytes 18440 | tf_op jit(solution)/shard_map/ppermute | solution.py:49
  34.7 5.4 %collective-permute-start.14 = (f32[3,512]{1,0:T(4,128)S(1)}, f32[3,512]{1,0:T(4,128)S(1)}, u32[]{:S(2)}, u32[]{:S(2)}) collective-permute-start(f32[3,512]{1,0:T(4,128)S(1)} %shard_map.67.refs_0_), channel_id=1, source_target_pairs={{3,0},{2,1},{1,2},{0,3},{7,4},{6,5},{5,6},{4,7},{11,8},{10,9},{9,1... | collective-permute-start | bytes 18440 | tf_op jit(solution)/shard_map/ppermute | solution.py:49
  40.2 5.7 %collective-permute-start.15 = (f32[2,512]{1,0:T(2,128)S(1)}, f32[2,512]{1,0:T(2,128)S(1)}, u32[]{:S(2)}, u32[]{:S(2)}) collective-permute-start(f32[2,512]{1,0:T(2,128)S(1)} %shard_map.68.refs_0_), channel_id=1, source_target_pairs={{8,0},{20,4},{0,8},{28,12},{24,16},{4,20},{16,24},{12,28},{9,1},{2... | collective-permute-start | bytes 12296 | tf_op jit(solution)/shard_map/ppermute | solution.py:49
  42.2 3.7 %collective-permute-start.16 = (f32[2,512]{1,0:T(2,128)S(1)}, f32[2,512]{1,0:T(2,128)S(1)}, u32[]{:S(2)}, u32[]{:S(2)}) collective-permute-start(f32[2,512]{1,0:T(2,128)S(1)} %shard_map.68.refs_0_), channel_id=1, source_target_pairs={{16,0},{12,4},{24,8},{4,12},{0,16},{28,20},{8,24},{20,28},{17,1},{... | collective-permute-start | bytes 12296 | tf_op jit(solution)/shard_map/ppermute | solution.py:49
  42.4 4.5 %collective-permute-start.17 = (f32[2,512]{1,0:T(2,128)S(1)}, f32[2,512]{1,0:T(2,128)S(1)}, u32[]{:S(2)}, u32[]{:S(2)}) collective-permute-start(f32[2,512]{1,0:T(2,128)S(1)} %shard_map.68.refs_0_), channel_id=1, source_target_pairs={{24,0},{16,8},{8,16},{0,24},{25,1},{17,9},{9,17},{1,25},{26,2},{18... | collective-permute-start | bytes 12296 | tf_op jit(solution)/shard_map/ppermute | solution.py:49
  49.2 2.6 %collective-permute-start.18 = (bf16[768,512]{1,0:T(8,128)(2,1)S(1)}, bf16[768,512]{1,0:T(8,128)(2,1)S(1)}, u32[]{:S(2)}, u32[]{:S(2)}) collective-permute-start(bf16[768,512]{1,0:T(8,128)(2,1)S(1)} %get-tuple-element.26), channel_id=1, source_target_pairs={{4,0},{0,4},{5,1},{1,5},{6,2},{2,6},{7,3},{3,7},{12,8},{8,12},{13,... | collective-permute-start | bytes 2359304 | tf_op jit(solution)/shard_map/ppermute | solution.py:49
  49.3 2.6 %collective-permute-start.19 = (f32[1,768]{1,0:T(1,128)S(1)}, f32[1,768]{1,0:T(1,128)S(1)}, u32[]{:S(2)}, u32[]{:S(2)}) collective-permute-start(f32[1,768]{1,0:T(1,128)S(1)} %get-tuple-element.27), channel_id=1, source_target_pairs={{4,0},{0,4},{5,1},{1,5},{6,2},{2,6},{7,3},{3,7},{12,8},{8,12},{13,... | collective-permute-start | bytes 9224 | tf_op jit(solution)/shard_map/ppermute | solution.py:49

commit v13 on v12

--- a/solution.py
+++ b/solution.py
@@ -146,7 +146,7 @@
     return (top, *(sum(part[at] * scale for part, scale in zip(parts, scales)) for at in (1, 2)))
 
 
-def totals_call(rate, block, pieces, cells, inverse, after=()):
+def totals_call(rate, block, pieces, cells, inverse, after=(), declared=1.0):
     n_points, width = sum(piece.shape[0] for piece in pieces), pieces[0].shape[1]
     n_cells = inverse.shape[0]
     args = (*pieces, cells, inverse, *after)
@@ -157,46 +157,49 @@
         out_shape=jax.ShapeDtypeStruct((3, n_points), jnp.float32),
         compiler_params=pltpu.CompilerParams(vmem_limit_bytes=VMEM_BYTES),
         cost_estimate=pl.CostEstimate(
-            flops=2 * n_cells * n_points * width,
-            bytes_accessed=2 * n_cells * width,
-            transcendentals=n_cells * n_points,
+            flops=int(declared * 2 * n_cells * n_points * width),
+            bytes_accessed=int(declared * 2 * n_cells * width),
+            transcendentals=int(declared * n_cells * n_points),
         ),
     )(*args)
 
 
-def goal_kernel(rate, *refs):
-    stats, goal = refs[:4], refs[-1]
+def merge_kernel(rate, by, goal, mine, theirs, *refs):
     for at in range(4):
-        here = [stat[:, (at ^ by) * 128 : ((at ^ by) + 1) * 128] for by, stat in enumerate(stats)]
-        top, total, novel = join_stats(rate, [(s[:1], s[1:2], s[2:]) for s in here])
-        goal[:, at * 128 : (at + 1) * 128] = jnp.concatenate([top, novel / total / total], axis=0)
-
-
-def goal_call(rate, *stats):
-    return pl.pallas_call(
-        functools.partial(goal_kernel, rate),
-        in_specs=in_vmem(len(stats)),
-        out_specs=in_vmem(1)[0],
-        out_shape=jax.ShapeDtypeStruct((2, stats[0].shape[1]), jnp.float32),
-        compiler_params=pltpu.CompilerParams(vmem_limit_bytes=VMEM_BYTES),
-    )(*stats)
-
-
-def factor_kernel(rate, *refs):
-    goals, tops, factors = refs[:4], refs[4:6], refs[6:]
+        ours = mine[:, at * 128 : (at + 1) * 128]
+        other = theirs[:, (at ^ by) * 128 : ((at ^ by) + 1) * 128]
+        top, total, novel = join_stats(rate, [(s[:1], s[1:2], s[2:]) for s in (ours, other)])
+        rows = (top, novel / total / total) if goal else (top, total, novel)
+        refs[-1][:, at * 128 : (at + 1) * 128] = jnp.concatenate(rows, axis=0)
+
+
+def merge_call(rate, by, goal, mine, theirs, *after):
+    return pl.pallas_call(
+        functools.partial(merge_kernel, rate, by, goal),
+        in_specs=in_vmem(2 + len(after)),
+        out_specs=in_vmem(1)[0],
+        out_shape=jax.ShapeDtypeStruct((2 if goal else 3, mine.shape[1]), jnp.float32),
+        compiler_params=pltpu.CompilerParams(vmem_limit_bytes=VMEM_BYTES),
+    )(mine, theirs, *after)
+
+
+def factor_kernel(rate, n, *refs):
+    goals, tops, factors = refs[:4], refs[4 : 4 + n], refs[4 + n :]
     rows = goals[0].shape[1] // 2
-    for group in range(2):
-        mine = slice(group * rows, (group + 1) * rows)
-        for at, goal in enumerate(goals):
-            here = slice(at * rows, (at + 1) * rows)
-            factors[group][:, here] = jnp.exp2((tops[group][:, here] - goal[:1, mine]) * rate) * goal[1:, mine]
+    spots = [(0, 0, 0), (0, 1, rows), (0, 2, 2 * rows), (0, 3, 3 * rows)]
+    spots += [(1, 0, 0), (1, 1, rows), (1, 2, 2 * rows), (2, 3, 0)]
+    for at, (bundle, goal, start) in enumerate(spots):
+        group = at // 4
+        mine, here = slice(group * rows, (group + 1) * rows), slice(start, start + rows)
+        scale = jnp.exp2((tops[bundle][:, here] - goals[goal][:1, mine]) * rate)
+        factors[bundle][:, here] = scale * goals[goal][1:, mine]
 
 
 def factor_call(rate, goals, tops):
     return pl.pallas_call(
-        functools.partial(factor_kernel, rate),
-        in_specs=in_vmem(6),
-        out_specs=in_vmem(2),
+        functools.partial(factor_kernel, rate, len(tops)),
+        in_specs=in_vmem(4 + len(tops)),
+        out_specs=in_vmem(len(tops)),
         out_shape=[jax.ShapeDtypeStruct(top.shape, jnp.float32) for top in tops],
         compiler_params=pltpu.CompilerParams(vmem_limit_bytes=VMEM_BYTES),
     )(*goals, *tops)
@@ -333,26 +336,25 @@
     block = per_device // 3
 
     near_1, near_2, near_3 = (along_z(own, by) for by in (1, 2, 3))
-    expand = lambda near: (near, turn(near), turn_back(near))
-    own, first_0, second_0 = expand(own)
-    near_1, first_1, second_1 = expand(near_1)
-    across_0, across_1 = turn_back(first_0), turn_back(first_1)
-    inverse = inverse_call(counters, first_0, near_1)
-    stats = [totals_call(rate, block, (own, near_1), centroids, inverse, after=(second_0,))]
+    inverse = inverse_call(counters)
+    near_01 = join(own, near_1)
+    first_01, second_01 = turn(near_01), turn_back(near_01)
+    stats = [totals_call(rate, block, (near_01,), centroids, inverse)]
     near_23 = join(near_2, near_3, *stats)
+    across_01 = turn_back(hold(first_01, near_23))
     first_23 = turn(near_23)
-    after = (first_1, second_1, across_0, across_1)
-    stats.append(totals_call(rate, block, (near_23,), centroids, inverse, after=after))
-    second_23, across_23 = turn_back(hold(near_23, stats[1])), turn_back(hold(first_23, stats[1]))
+    stats.append(totals_call(rate, block, (near_23,), centroids, inverse, after=(first_01, second_01)))
+    second_23 = turn_back(hold(near_23, stats[1]))
 
     expand = functools.partial(expo_call, rate, block, 2 * per_device)
-    groups = [expand((own, near_1, first_0, first_1, second_0, second_1, across_0, across_1), centroids, stats[1])]
-    tops = groups[0][1]
     stat = beside(*stats)
-    theirs = [along_z(stat, by) for by in (1, 2, 3)]
-    goal = goal_call(rate, stat, *theirs, tops, second_23)
-    groups.append(expand((near_23, first_23, second_23, across_23), centroids))
-    expos, tops, points = zip(*groups)
+    bundles = [expand((near_01, first_01, second_01, across_01), centroids, stat)]
+    stat = merge_call(rate, 1, False, stat, along_z(stat, 1), bundles[0][1])
+    across_23 = turn_back(hold(first_23, stat))
+    bundles.append(expand((near_23, first_23, second_23), centroids, stat))
+    goal = merge_call(rate, 2, True, stat, along_z(stat, 2), bundles[1][1])
+    bundles.append(expand((across_23,), centroids))
+    expos, tops, points = zip(*bundles)
     goals = [goal, turn(goal), turn_back(goal), around(goal, 3)]
     factors = factor_call(rate, goals, tops)
 

time: 54 us -> 48.9 us (0.906); the launches traced: 53.8 us -> 48 us
  waiting for transfers between devices: 9.46 us -> 5.09 us
  starting transfers between devices: 23.6 us -> 22.8 us
    ppermute x20 -> x16, waiting for transfers between devices: 9.46 us -> 5.09 us  [exchange(): return lax.ppermute(a, axes, [(partner(at), at) for at in range(count)])]
    ppermute x20 -> x16, starting transfers between devices: 23.6 us -> 22.8 us  [exchange(): return lax.ppermute(a, axes, [(partner(at), at) for at in range(count)])]
    pallas_call x2 -> x3, Pallas kernels: 4.23 us -> 4.27 us  [expo_call(): pl.pallas_call(functools.partial(expo_kernel, rate, block, len(pieces)),...]
  transfers between devices with their start and end apart: 20 -> 16, of which waited for: 5 -> 6; matrix products, arithmetic and copies ran while one was open for 0% -> 0% of each run, Pallas kernels for 24% -> 26%
where the time goes in v13:
time: 48.9 us; the launch traced here: 48 us
  starting transfers between devices  22.8 us (47%)
  Pallas kernels  16.7 us (34%)
  waiting for transfers between devices  5.09 us (10%)
  other arithmetic  1.69 us (3%)
  between operations  0.95 us (2%)
  local copies, waits for them, and re-layouts  0.74 us (2%)
    ppermute x16, starting transfers between devices, exchange(): return lax.ppermute(a, axes, [(partner(at), at) for at in range(count)])  22.8 us
    pallas_call x2, Pallas kernels, totals_call(): pl.pallas_call(functools.partial(totals_kernel, rate, block, len(pieces))...  5.4 us
    ppermute x16, waiting for transfers between devices, exchange(): return lax.ppermute(a, axes, [(partner(at), at) for at in range(count)])  5.09 us
    pallas_call x3, Pallas kernels, expo_call(): pl.pallas_call(functools.partial(expo_kernel, rate, block, len(pieces)),...  4.27 us
    pallas_call x2, Pallas kernels, sums_call(): pl.pallas_call(functools.partial(sums_kernel, n, block, side), in_specs=i...  4.19 us
    pallas_call x1, Pallas kernels, add_call(): pl.pallas_call(functools.partial(add_kernel, block), in_specs=in_vmem(4),...  1.79 us
    convert_element_type x1, other arithmetic, to_points(): return (codes.astype(jnp.float32) * scale[:, None]).astype(jnp.bfloat16)  1.03 us
  transfers between devices with their start and end apart: 16, of which 6 were waited for; matrix products, arithmetic and copies ran while one was open for 0% of the time, Pallas kernels for 26%

profile of v13, /device:TPU:0, one launch (start us, length us, event | category | flops | bytes accessed | tf_op | source)
XLA Modules:
  0.0 48.0 jit_solution(17017708208051058043)
XLA Ops:
  0.6 0.7 %convert_multiply_fusion = f32[128]{0:T(128)S(1)} fusion(s32[128]{0:T(128)} %param.5), kind=kLoop, calls=%fused_computation.1 | loop fusion | flops 512 | bytes 1024 | tf_op jit(solution)/shard_map/mul | solution.py:16
  1.3 1.0 %multiply_convert_fusion.above = bf16[128,512]{1,0:T(8,128)(2,1)S(1)} fusion(s32[128,512]{1,0:T(8,128)} %param.4, f32[128]{0:T(128)S(1)} %convert_multiply_fusion), kind=kLoop, calls=%fused_computation | loop fusion | flops 196608 | bytes 393728 | tf_op jit(solution)/shard_map/convert_element_type | solution.py:17
  2.3 3.1 %collective-permute-start = (bf16[128,512]{1,0:T(8,128)(2,1)S(1)}, bf16[128,512]{1,0:T(8,128)(2,1)S(1)}, u32[]{:S(2)}, u32[]{:S(2)}) collective-permute-start(bf16[128,512]{1,0:T(8,128)(2,1)S(1)} %multiply_convert_fusion.above), channel_id=1, source_target_pairs={{1,0},{0,1},{3,2},{2,3},{5,4},{4,5},{7,6},{6,7},{9,8},{8,9},{11,10... | collective-permute-start | bytes 393224 | tf_op jit(solution)/shard_map/ppermute | solution.py:49
  5.4 2.6 %collective-permute-start.3 = (bf16[128,512]{1,0:T(8,128)(2,1)S(1)}, bf16[128,512]{1,0:T(8,128)(2,1)S(1)}, u32[]{:S(2)}, u32[]{:S(2)}) collective-permute-start(bf16[128,512]{1,0:T(8,128)(2,1)S(1)} %multiply_convert_fusion.above), channel_id=1, source_target_pairs={{2,0},{3,1},{0,2},{1,3},{6,4},{7,5},{4,6},{5,7},{10,8},{11,9},{8,1... | collective-permute-start | bytes 393224 | tf_op jit(solution)/shard_map/ppermute | solution.py:49
  8.0 0.0 collective-permute-start.4
  8.0 2.4 %collective-permute-done.below = bf16[128,512]{1,0:T(8,128)(2,1)S(1)} collective-permute-done((bf16[128,512]{1,0:T(8,128)(2,1)S(1)}, bf16[128,512]{1,0:T(8,128)(2,1)S(1)}, u32[]{:S(2)}, u32[]{:S(2)}) %collective-permute-start) | collective-permute-done | bytes 131104 | tf_op jit(solution)/shard_map/ppermute | solution.py:49
  10.5 0.0 slice-start
  10.5 1.8 %collective-permute-start.1 = (bf16[256,512]{1,0:T(8,128)(2,1)S(1)}, bf16[256,512]{1,0:T(8,128)(2,1)S(1)}, u32[]{:S(2)}, u32[]{:S(2)}) collective-permute-start(bf16[256,512]{1,0:T(8,128)(2,1)S(1)} %shard_map.59.refs_0_), channel_id=1, source_target_pairs={{8,0},{20,4},{0,8},{28,12},{24,16},{4,20},{16,24},{12,28},{9,1},{2... | collective-permute-start | bytes 786440 | tf_op jit(solution)/shard_map/ppermute | solution.py:49
  12.3 0.0 copy-start
  12.3 0.7 %copy-done = s32[6144]{0:T(1024)S(1)} copy-done((s32[6144]{0:T(1024)S(1)}, s32[6144]{0:T(1024)}, u32[]{:S(2)}) %copy-start) | copy-done | bytes 24600
  13.0 0.0 slice-start.1
  13.0 0.9 %shard_map.60.refs_2_ = f32[6144,128]{1,0:T(8,128)S(1)} custom-call(s32[48,128]{1,0:T(8,128)S(1)} %bitcast.4), custom_call_target="tpu_custom_call" | custom-call | flops 4000000000 | tf_op jit(solution)/shard_map/pallas_call | solution.py:113
  13.9 1.6 %collective-permute-start.2 = (bf16[256,512]{1,0:T(8,128)(2,1)S(1)}, bf16[256,512]{1,0:T(8,128)(2,1)S(1)}, u32[]{:S(2)}, u32[]{:S(2)}) collective-permute-start(bf16[256,512]{1,0:T(8,128)(2,1)S(1)} %shard_map.59.refs_0_), channel_id=1, source_target_pairs={{16,0},{12,4},{24,8},{4,12},{0,16},{28,20},{8,24},{20,28},{17,1},{... | collective-permute-start | bytes 786440 | tf_op jit(solution)/shard_map/ppermute | solution.py:49
  15.5 0.0 slice-done
  15.5 0.0 slice-done.1
  15.5 2.7 %shard_map.61.refs_0_.left = f32[3,256]{1,0:T(4,128)S(1)} custom-call(bf16[256,512]{1,0:T(8,128)(2,1)S(1)} %shard_map.59.refs_0_, bf16[6144,512]{1,0:T(8,128)(2,1)S(1)} %bitcast.3, f32[6144,128]{1,0:T(8,128)S(1)} %shard_map.60.refs_2_), custom_call_target="tpu_custom_call" | custom-call | flops 1610612736 | bytes 6291456 | tf_op jit(solution)/shard_map/pallas_call | solution.py:153
  18.2 0.2 collective-permute-done.3.above
  18.3 0.0 collective-permute-done.4.below
  18.4 1.3 %collective-permute-done.1.a.refs_3_.refs_1_ = bf16[256,512]{1,0:T(8,128)(2,1)S(1)} collective-permute-done((bf16[256,512]{1,0:T(8,128)(2,1)S(1)}, bf16[256,512]{1,0:T(8,128)(2,1)S(1)}, u32[]{:S(2)}, u32[]{:S(2)}) %collective-permute-start.1) | collective-permute-done | bytes 262176 | tf_op jit(solution)/shard_map/ppermute | solution.py:49
  19.6 0.7 %collective-permute-start.5 = (bf16[256,512]{1,0:T(8,128)(2,1)S(1)}, bf16[256,512]{1,0:T(8,128)(2,1)S(1)}, u32[]{:S(2)}, u32[]{:S(2)}) collective-permute-start(bf16[256,512]{1,0:T(8,128)(2,1)S(1)} %shard_map.63), channel_id=1, source_target_pairs={{16,0},{12,4},{24,8},{4,12},{0,16},{28,20},{8,24},{20,28},{17,1},{... | collective-permute-start | bytes 786440 | tf_op jit(solution)/shard_map/ppermute | solution.py:49
  20.4 1.2 %collective-permute-start.6 = (bf16[256,512]{1,0:T(8,128)(2,1)S(1)}, bf16[256,512]{1,0:T(8,128)(2,1)S(1)}, u32[]{:S(2)}, u32[]{:S(2)}) collective-permute-start(bf16[256,512]{1,0:T(8,128)(2,1)S(1)} %shard_map.62.refs_0_.a), channel_id=1, source_target_pairs={{8,0},{20,4},{0,8},{28,12},{24,16},{4,20},{16,24},{12,28},{9,1},{2... | collective-permute-start | bytes 786440 | tf_op jit(solution)/shard_map/ppermute | solution.py:49
  21.5 0.0 collective-permute-done.2.refs_4_.refs_2_
  21.6 2.7 %shard_map.64.right.refs_0_ = f32[3,256]{1,0:T(4,128)S(1)} custom-call(bf16[256,512]{1,0:T(8,128)(2,1)S(1)} %shard_map.62.refs_0_.a, bf16[6144,512]{1,0:T(8,128)(2,1)S(1)} %bitcast.3, f32[6144,128]{1,0:T(8,128)S(1)} %shard_map.60.refs_2_, bf16[256,512]{1,0:T(8,128)(2,1)S(1)} %collective-permute-done.1.a.refs_3_.refs_1_, ...), custom_call_target="tpu_custom_call" | custom-call | flops 1610612736 | bytes 6291456 | tf_op jit(solution)/shard_map/pallas_call | solution.py:153
  24.3 2.0 %collective-permute-start.8 = (f32[3,512]{1,0:T(4,128)S(1)}, f32[3,512]{1,0:T(4,128)S(1)}, u32[]{:S(2)}, u32[]{:S(2)}) collective-permute-start(f32[3,512]{1,0:T(4,128)S(1)} %shard_map.65.refs_5_.mine), channel_id=1, source_target_pairs={{1,0},{0,1},{3,2},{2,3},{5,4},{4,5},{7,6},{6,7},{9,8},{8,9},{11,10... | collective-permute-start | bytes 18440 | tf_op jit(solution)/shard_map/ppermute | solution.py:49
  26.3 0.5 %collective-permute-start.7 = (bf16[256,512]{1,0:T(8,128)(2,1)S(1)}, bf16[256,512]{1,0:T(8,128)(2,1)S(1)}, u32[]{:S(2)}, u32[]{:S(2)}) collective-permute-start(bf16[256,512]{1,0:T(8,128)(2,1)S(1)} %shard_map.67), channel_id=1, source_target_pairs={{16,0},{12,4},{24,8},{4,12},{0,16},{28,20},{8,24},{20,28},{17,1},{... | collective-permute-start | bytes 786440 | tf_op jit(solution)/shard_map/ppermute | solution.py:49
  26.8 0.0 collective-permute-done.5.refs_3_
  26.8 2.0 %shard_map.66 = (bf16[1536,1024]{1,0:T(8,128)(2,1)S(1)}, f32[6,1024]{1,0:T(8,128)S(1)}, bf16[1024,512]{1,0:T(8,128)(2,1)S(1)}) custom-call(bf16[256,512]{1,0:T(8,128)(2,1)S(1)} %shard_map.59.refs_0_, bf16[256,512]{1,0:T(8,128)(2,1)S(1)} %collective-permute-done.1.a.refs_3_.refs_1_, bf16[256,512]{1,0:T(8,128)(2,1)S(1)} %collective-permute-done.2.refs_4_.refs_2_, ...), custom_call_target="tpu_custom_call" | custom-call | flops 1610612736 | bytes 5767168 | tf_op jit(solution)/shard_map/pallas_call | solution.py:229
  28.8 0.0 collective-permute-done.8.theirs
  28.8 0.0 collective-permute-done.6.refs_1_.a
  28.9 1.6 %collective-permute-start.9 = (bf16[256,512]{1,0:T(8,128)(2,1)S(1)}, bf16[256,512]{1,0:T(8,128)(2,1)S(1)}, u32[]{:S(2)}, u32[]{:S(2)}) collective-permute-start(bf16[256,512]{1,0:T(8,128)(2,1)S(1)} %shard_map.70), channel_id=1, source_target_pairs={{16,0},{12,4},{24,8},{4,12},{0,16},{28,20},{8,24},{20,28},{17,1},{... | collective-permute-start | bytes 786440 | tf_op jit(solution)/shard_map/ppermute | solution.py:49
  30.5 3.6 %collective-permute-start.10 = (f32[3,512]{1,0:T(4,128)S(1)}, f32[3,512]{1,0:T(4,128)S(1)}, u32[]{:S(2)}, u32[]{:S(2)}) collective-permute-start(f32[3,512]{1,0:T(4,128)S(1)} %shard_map.68.refs_4_.refs_0_.mine), channel_id=1, source_target_pairs={{2,0},{3,1},{0,2},{1,3},{6,4},{7,5},{4,6},{5,7},{10,8},{11,9},{8,1... | collective-permute-start | bytes 18440 | tf_op jit(solution)/shard_map/ppermute | solution.py:49
  34.1 0.0 collective-permute-done.7.refs_2_
  34.1 1.6 %shard_map.69 = (bf16[1536,768]{1,0:T(8,128)(2,1)S(1)}, f32[6,768]{1,0:T(8,128)S(1)}, bf16[768,512]{1,0:T(8,128)(2,1)S(1)}) custom-call(bf16[256,512]{1,0:T(8,128)(2,1)S(1)} %shard_map.62.refs_0_.a, bf16[256,512]{1,0:T(8,128)(2,1)S(1)} %collective-permute-done.6.refs_1_.a, bf16[256,512]{1,0:T(8,128)(2,1)S(1)} %collective-permute-done.7.refs_2_, ...), custom_call_target="tpu_custom_call" | custom-call | flops 1207959552 | bytes 4718592 | tf_op jit(solution)/shard_map/pallas_call | solution.py:229
  35.7 0.1 collective-permute-done.10.theirs
  35.8 0.8 %collective-permute-start.11 = (f32[2,512]{1,0:T(2,128)S(1)}, f32[2,512]{1,0:T(2,128)S(1)}, u32[]{:S(2)}, u32[]{:S(2)}) collective-permute-start(f32[2,512]{1,0:T(2,128)S(1)} %shard_map.72.refs_0_), channel_id=1, source_target_pairs={{8,0},{20,4},{0,8},{28,12},{24,16},{4,20},{16,24},{12,28},{9,1},{2... | collective-permute-start | bytes 12296 | tf_op jit(solution)/shard_map/ppermute | solution.py:49
  36.6 0.1 collective-permute-start.12
  36.7 2.6 %collective-permute-start.13 = (f32[2,512]{1,0:T(2,128)S(1)}, f32[2,512]{1,0:T(2,128)S(1)}, u32[]{:S(2)}, u32[]{:S(2)}) collective-permute-start(f32[2,512]{1,0:T(2,128)S(1)} %shard_map.72.refs_0_), channel_id=1, source_target_pairs={{24,0},{16,8},{8,16},{0,24},{25,1},{17,9},{9,17},{1,25},{26,2},{18... | collective-permute-start | bytes 12296 | tf_op jit(solution)/shard_map/ppermute | solution.py:49
  39.3 0.0 collective-permute-done.9.refs_0_
  39.3 0.7 %shard_map.71 = (bf16[1536,256]{1,0:T(8,128)(2,1)S(1)}, f32[6,256]{1,0:T(8,128)S(1)}, bf16[256,512]{1,0:T(8,128)(2,1)S(1)}) custom-call(bf16[256,512]{1,0:T(8,128)(2,1)S(1)} %collective-permute-done.9.refs_0_, bf16[6144,512]{1,0:T(8,128)(2,1)S(1)} %bitcast.3), custom_call_target="tpu_custom_call" | custom-call | flops 402653184 | bytes 2621440 | tf_op jit(solution)/shard_map/pallas_call | solution.py:229
  40.0 0.0 collective-permute-done.11.refs_1_
  40.0 0.1 collective-permute-done.12.refs_2_
  40.2 1.0 %collective-permute-done.13.refs_3_ = f32[2,512]{1,0:T(2,128)S(1)} collective-permute-done((f32[2,512]{1,0:T(2,128)S(1)}, f32[2,512]{1,0:T(2,128)S(1)}, u32[]{:S(2)}, u32[]{:S(2)}) %collective-permute-start.13) | collective-permute-done | bytes 4128 | tf_op jit(solution)/shard_map/ppermute | solution.py:49
  41.2 2.2 %shard_map.75 = (bf16[768,512]{1,0:T(8,128)(2,1)S(1)}, f32[1,768]{1,0:T(1,128)S(1)}) custom-call(bf16[1536,1024]{1,0:T(8,128)(2,1)S(1)} %get-tuple-element.20.refs_0_, bf16[1536,768]{1,0:T(8,128)(2,1)S(1)} %get-tuple-element.22.refs_1_, bf16[1536,256]{1,0:T(8,128)(2,1)S(1)} %get-tuple-element.23.refs_2_, bf16[1024,512]{1,0:T(8,128)(2,1)S(1)} %get-tuple-element.24.refs_3_, ...), custom_call_target="tpu_custom_call" | custom-call | flops 2415919104 | bytes 9437184 | tf_op jit(solution)/shard_map/pallas_call | solution.py:279
  43.4 0.1 collective-permute-start.14
  43.5 0.5 %collective-permute-start.15 = (f32[1,768]{1,0:T(1,128)S(1)}, f32[1,768]{1,0:T(1,128)S(1)}, u32[]{:S(2)}, u32[]{:S(2)}) collective-permute-start(f32[1,768]{1,0:T(1,128)S(1)} %get-tuple-element.35), channel_id=1, source_target_pairs={{4,0},{0,4},{5,1},{1,5},{6,2},{2,6},{7,3},{3,7},{12,8},{8,12},{13,... | collective-permute-start | bytes 9224 | tf_op jit(solution)/shard_map/ppermute | solution.py:49
  44.0 2.0 %shard_map.74 = (f32[768,512]{1,0:T(8,128)S(1)}, f32[1,768]{1,0:T(1,128)S(1)}) custom-call(bf16[1536,1024]{1,0:T(8,128)(2,1)S(1)} %get-tuple-element.20.refs_0_, bf16[1536,768]{1,0:T(8,128)(2,1)S(1)} %get-tuple-element.22.refs_1_, bf16[1536,256]{1,0:T(8,128)(2,1)S(1)} %get-tuple-element.23.refs_2_, bf16[1024,512]{1,0:T(8,128)(2,1)S(1)} %get-tuple-element.24.refs_3_, ...), custom_call_target="tpu_custom_call" | custom-call | flops 2415919104 | bytes 9437184 | tf_op jit(solution)/shard_map/pallas_call | solution.py:279
  46.0 0.0 collective-permute-done.15.there_mass
  46.0 0.0 collective-permute-done.14.there
  46.0 1.8 %shard_map.76 = (f32[768,512]{1,0:T(8,128)}, f32[1,768]{1,0:T(1,128)}) custom-call(f32[768,512]{1,0:T(8,128)S(1)} %get-tuple-element.32.here, f32[1,768]{1,0:T(1,128)S(1)} %get-tuple-element.33.here_mass, bf16[768,512]{1,0:T(8,128)(2,1)S(1)} %collective-permute-done.14.there, f32[1,768]{1,0:T(1,128)S(1)} %collective-permute-done.15.there_mass), custom_call_target="tpu_custom_call" | custom-call | tf_op jit(solution)/shard_map/pallas_call | solution.py:309
  (10 shorter events, 0.2 us)
Async XLA Ops:
  2.3 8.1 %collective-permute-start = (bf16[128,512]{1,0:T(8,128)(2,1)S(1)}, bf16[128,512]{1,0:T(8,128)(2,1)S(1)}, u32[]{:S(2)}, u32[]{:S(2)}) collective-permute-start(bf16[128,512]{1,0:T(8,128)(2,1)S(1)} %multiply_convert_fusion.above), channel_id=1, source_target_pairs={{1,0},{0,1},{3,2},{2,3},{5,4},{4,5},{7,6},{6,7},{9,8},{8,9},{11,10... | collective-permute-start | bytes 393224 | tf_op jit(solution)/shard_map/ppermute | solution.py:49
  5.4 12.9 %collective-permute-start.3 = (bf16[128,512]{1,0:T(8,128)(2,1)S(1)}, bf16[128,512]{1,0:T(8,128)(2,1)S(1)}, u32[]{:S(2)}, u32[]{:S(2)}) collective-permute-start(bf16[128,512]{1,0:T(8,128)(2,1)S(1)} %multiply_convert_fusion.above), channel_id=1, source_target_pairs={{2,0},{3,1},{0,2},{1,3},{6,4},{7,5},{4,6},{5,7},{10,8},{11,9},{8,1... | collective-permute-start | bytes 393224 | tf_op jit(solution)/shard_map/ppermute | solution.py:49
  8.0 10.3 %collective-permute-start.4 = (bf16[128,512]{1,0:T(8,128)(2,1)S(1)}, bf16[128,512]{1,0:T(8,128)(2,1)S(1)}, u32[]{:S(2)}, u32[]{:S(2)}) collective-permute-start(bf16[128,512]{1,0:T(8,128)(2,1)S(1)} %multiply_convert_fusion.above), channel_id=1, source_target_pairs={{3,0},{2,1},{1,2},{0,3},{7,4},{6,5},{5,6},{4,7},{11,8},{10,9},{9,1... | collective-permute-start | bytes 393224 | tf_op jit(solution)/shard_map/ppermute | solution.py:49
  10.5 5.0 %slice-start = ((s8[6291456]{0:T(1024)(128)(4,1)}), s8[4194304]{0:T(1024)(128)(4,1)S(1)}, s32[]{:S(2)}) async-start(s8[6291456]{0:T(1024)(128)(4,1)} %bitcast.2), calls=%async_computation | async-start | bytes 8388608
  10.5 9.1 %collective-permute-start.1 = (bf16[256,512]{1,0:T(8,128)(2,1)S(1)}, bf16[256,512]{1,0:T(8,128)(2,1)S(1)}, u32[]{:S(2)}, u32[]{:S(2)}) collective-permute-start(bf16[256,512]{1,0:T(8,128)(2,1)S(1)} %shard_map.59.refs_0_), channel_id=1, source_target_pairs={{8,0},{20,4},{0,8},{28,12},{24,16},{4,20},{16,24},{12,28},{9,1},{2... | collective-permute-start | bytes 786440 | tf_op jit(solution)/shard_map/ppermute | solution.py:49
  12.3 0.7 %copy-start = (s32[6144]{0:T(1024)S(1)}, s32[6144]{0:T(1024)}, u32[]{:S(2)}) copy-start(s32[6144]{0:T(1024)} %param.7) | copy-start | bytes 73732
  13.0 2.5 %slice-start.1 = ((s8[6291456]{0:T(1024)(128)(4,1)}), s8[2097152]{0:T(1024)(128)(4,1)S(1)}, s32[]{:S(2)}) async-start(s8[6291456]{0:T(1024)(128)(4,1)} %bitcast.2), calls=%async_computation.1 | async-start | bytes 4194304
  13.9 7.7 %collective-permute-start.2 = (bf16[256,512]{1,0:T(8,128)(2,1)S(1)}, bf16[256,512]{1,0:T(8,128)(2,1)S(1)}, u32[]{:S(2)}, u32[]{:S(2)}) collective-permute-start(bf16[256,512]{1,0:T(8,128)(2,1)S(1)} %shard_map.59.refs_0_), channel_id=1, source_target_pairs={{16,0},{12,4},{24,8},{4,12},{0,16},{28,20},{8,24},{20,28},{17,1},{... | collective-permute-start | bytes 786440 | tf_op jit(solution)/shard_map/ppermute | solution.py:49
  19.6 7.1 %collective-permute-start.5 = (bf16[256,512]{1,0:T(8,128)(2,1)S(1)}, bf16[256,512]{1,0:T(8,128)(2,1)S(1)}, u32[]{:S(2)}, u32[]{:S(2)}) collective-permute-start(bf16[256,512]{1,0:T(8,128)(2,1)S(1)} %shard_map.63), channel_id=1, source_target_pairs={{16,0},{12,4},{24,8},{4,12},{0,16},{28,20},{8,24},{20,28},{17,1},{... | collective-permute-start | bytes 786440 | tf_op jit(solution)/shard_map/ppermute | solution.py:49
  20.4 8.5 %collective-permute-start.6 = (bf16[256,512]{1,0:T(8,128)(2,1)S(1)}, bf16[256,512]{1,0:T(8,128)(2,1)S(1)}, u32[]{:S(2)}, u32[]{:S(2)}) collective-permute-start(bf16[256,512]{1,0:T(8,128)(2,1)S(1)} %shard_map.62.refs_0_.a), channel_id=1, source_target_pairs={{8,0},{20,4},{0,8},{28,12},{24,16},{4,20},{16,24},{12,28},{9,1},{2... | collective-permute-start | bytes 786440 | tf_op jit(solution)/shard_map/ppermute | solution.py:49
  24.3 4.5 %collective-permute-start.8 = (f32[3,512]{1,0:T(4,128)S(1)}, f32[3,512]{1,0:T(4,128)S(1)}, u32[]{:S(2)}, u32[]{:S(2)}) collective-permute-start(f32[3,512]{1,0:T(4,128)S(1)} %shard_map.65.refs_5_.mine), channel_id=1, source_target_pairs={{1,0},{0,1},{3,2},{2,3},{5,4},{4,5},{7,6},{6,7},{9,8},{8,9},{11,10... | collective-permute-start | bytes 18440 | tf_op jit(solution)/shard_map/ppermute | solution.py:49
  26.3 7.8 %collective-permute-start.7 = (bf16[256,512]{1,0:T(8,128)(2,1)S(1)}, bf16[256,512]{1,0:T(8,128)(2,1)S(1)}, u32[]{:S(2)}, u32[]{:S(2)}) collective-permute-start(bf16[256,512]{1,0:T(8,128)(2,1)S(1)} %shard_map.67), channel_id=1, source_target_pairs={{16,0},{12,4},{24,8},{4,12},{0,16},{28,20},{8,24},{20,28},{17,1},{... | collective-permute-start | bytes 786440 | tf_op jit(solution)/shard_map/ppermute | solution.py:49
  28.9 10.5 %collective-permute-start.9 = (bf16[256,512]{1,0:T(8,128)(2,1)S(1)}, bf16[256,512]{1,0:T(8,128)(2,1)S(1)}, u32[]{:S(2)}, u32[]{:S(2)}) collective-permute-start(bf16[256,512]{1,0:T(8,128)(2,1)S(1)} %shard_map.70), channel_id=1, source_target_pairs={{16,0},{12,4},{24,8},{4,12},{0,16},{28,20},{8,24},{20,28},{17,1},{... | collective-permute-start | bytes 786440 | tf_op jit(solution)/shard_map/ppermute | solution.py:49
  30.5 5.3 %collective-permute-start.10 = (f32[3,512]{1,0:T(4,128)S(1)}, f32[3,512]{1,0:T(4,128)S(1)}, u32[]{:S(2)}, u32[]{:S(2)}) collective-permute-start(f32[3,512]{1,0:T(4,128)S(1)} %shard_map.68.refs_4_.refs_0_.mine), channel_id=1, source_target_pairs={{2,0},{3,1},{0,2},{1,3},{6,4},{7,5},{4,6},{5,7},{10,8},{11,9},{8,1... | collective-permute-start | bytes 18440 | tf_op jit(solution)/shard_map/ppermute | solution.py:49
  35.8 4.3 %collective-permute-start.11 = (f32[2,512]{1,0:T(2,128)S(1)}, f32[2,512]{1,0:T(2,128)S(1)}, u32[]{:S(2)}, u32[]{:S(2)}) collective-permute-start(f32[2,512]{1,0:T(2,128)S(1)} %shard_map.72.refs_0_), channel_id=1, source_target_pairs={{8,0},{20,4},{0,8},{28,12},{24,16},{4,20},{16,24},{12,28},{9,1},{2... | collective-permute-start | bytes 12296 | tf_op jit(solution)/shard_map/ppermute | solution.py:49
  36.6 3.6 %collective-permute-start.12 = (f32[2,512]{1,0:T(2,128)S(1)}, f32[2,512]{1,0:T(2,128)S(1)}, u32[]{:S(2)}, u32[]{:S(2)}) collective-permute-start(f32[2,512]{1,0:T(2,128)S(1)} %shard_map.72.refs_0_), channel_id=1, source_target_pairs={{16,0},{12,4},{24,8},{4,12},{0,16},{28,20},{8,24},{20,28},{17,1},{... | collective-permute-start | bytes 12296 | tf_op jit(solution)/shard_map/ppermute | solution.py:49
  36.7 4.5 %collective-permute-start.13 = (f32[2,512]{1,0:T(2,128)S(1)}, f32[2,512]{1,0:T(2,128)S(1)}, u32[]{:S(2)}, u32[]{:S(2)}) collective-permute-start(f32[2,512]{1,0:T(2,128)S(1)} %shard_map.72.refs_0_), channel_id=1, source_target_pairs={{24,0},{16,8},{8,16},{0,24},{25,1},{17,9},{9,17},{1,25},{26,2},{18... | collective-permute-start | bytes 12296 | tf_op jit(solution)/shard_map/ppermute | solution.py:49
  43.4 2.6 %collective-permute-start.14 = (bf16[768,512]{1,0:T(8,128)(2,1)S(1)}, bf16[768,512]{1,0:T(8,128)(2,1)S(1)}, u32[]{:S(2)}, u32[]{:S(2)}) collective-permute-start(bf16[768,512]{1,0:T(8,128)(2,1)S(1)} %get-tuple-element.34), channel_id=1, source_target_pairs={{4,0},{0,4},{5,1},{1,5},{6,2},{2,6},{7,3},{3,7},{12,8},{8,12},{13,... | collective-permute-start | bytes 2359304 | tf_op jit(solution)/shard_map/ppermute | solution.py:49
  43.5 2.5 %collective-permute-start.15 = (f32[1,768]{1,0:T(1,128)S(1)}, f32[1,768]{1,0:T(1,128)S(1)}, u32[]{:S(2)}, u32[]{:S(2)}) collective-permute-start(f32[1,768]{1,0:T(1,128)S(1)} %get-tuple-element.35), channel_id=1, source_target_pairs={{4,0},{0,4},{5,1},{1,5},{6,2},{2,6},{7,3},{3,7},{12,8},{8,12},{13,... | collective-permute-start | bytes 9224 | tf_op jit(solution)/shard_map/ppermute | solution.py:49

commit v14 on v13

--- a/solution.py
+++ b/solution.py
@@ -81,7 +81,7 @@
     )(left, right, *after)
 
 
-def hold(a, *after):
+def hold(a, *after, declared=0):
     def kernel(a, *refs):
         refs[-1][...] = a[...]
 
@@ -91,6 +91,7 @@
         out_specs=in_vmem(1)[0],
         out_shape=jax.ShapeDtypeStruct(a.shape, a.dtype),
         compiler_params=pltpu.CompilerParams(vmem_limit_bytes=VMEM_BYTES),
+        cost_estimate=pl.CostEstimate(flops=declared, bytes_accessed=0, transcendentals=0),
     )(a, *after)
 
 
@@ -116,7 +117,6 @@
         out_specs=in_vmem(1)[0],
         out_shape=jax.ShapeDtypeStruct((counters.shape[0], 128), jnp.float32),
         compiler_params=pltpu.CompilerParams(vmem_limit_bytes=VMEM_BYTES),
-        cost_estimate=pl.CostEstimate(flops=4 * 10**9, bytes_accessed=0, transcendentals=0),
     )(counters.reshape(-1, 128), *after)
 
 
@@ -223,7 +223,7 @@
             tops[at : at + 1, some] = top
 
 
-def expo_call(rate, block, count, pieces, cells, *after):
+def expo_call(rate, block, count, pieces, cells, *after, declared=1.0):
     width = cells.shape[1]
     n_points = sum(piece.shape[0] for piece in pieces)
     return pl.pallas_call(
@@ -237,9 +237,9 @@
         ],
         compiler_params=pltpu.CompilerParams(vmem_limit_bytes=VMEM_BYTES),
         cost_estimate=pl.CostEstimate(
-            flops=2 * count * n_points * width,
-            bytes_accessed=2 * (count * width + n_points * width + count * n_points),
-            transcendentals=count * n_points,
+            flops=int(declared * 2 * count * n_points * width),
+            bytes_accessed=int(declared * 2 * (count * width + n_points * width + count * n_points)),
+            transcendentals=int(declared * count * n_points),
         ),
     )(*pieces, cells, *after)
 
@@ -249,8 +249,9 @@
     for expo, chunk, factor in zip(expos, points, factors):
         block = expo.shape[0] // factor.shape[0]
         shares = []
-        for at in range(0, count, block):
-            here = pl.ds(pl.multiple_of(start + at, block), block)
+        step = min(block, count)
+        for at in range(0, count, step):
+            here = pl.ds(pl.multiple_of(start + at, step), step)
             scale = factor[pl.ds((start + at) // block, 1), :]
             shares.append((expo[here, :].astype(jnp.float32) * scale).astype(jnp.bfloat16))
         share = jnp.concatenate(shares, axis=0)
@@ -264,62 +265,61 @@
 
 def sums_kernel(n, block, side, *refs):
     expos, points, factors, (sums, mass) = refs[:n], refs[n : 2 * n], refs[2 * n : 3 * n], refs[3 * n :]
-    rows = sums.shape[0]
-    first = (lax.axis_index("lo") ^ side) * rows
-    for at in range(0, rows, block):
+    half = expos[0].shape[0] // 2
+    first = (lax.axis_index("lo") ^ side) * half
+    for at in range(0, sums.shape[0], block):
         here = slice(at, at + block)
         total, weight = weighed_sums(first + at, block, expos, points, factors)
         sums[here, :] = total.astype(sums.dtype)
         mass[:, here] = weight
 
 
-def sums_call(block, side, rows, dtype, expos, points, factors):
+def last_kernel(n, block, *refs):
+    expos, points, factors = refs[:n], refs[n : 2 * n], refs[2 * n : 3 * n]
+    early, early_mass, there, there_mass, sums, mass, out, left = refs[3 * n :]
+    done, half = early.shape[0], there.shape[0]
+    first = lax.axis_index("lo") * half
+    copies = []
+
+    def store(start, stop, total):
+        out[start:stop, :] = total + there[start:stop, :].astype(jnp.float32)
+        here = pl.ds(start, stop - start)
+        copies.append(pltpu.make_async_copy(out.at[here, :], sums.at[here, :], left.at[len(copies)]))
+        copies[-1].start()
+
+    store(0, done, early[...])
+    mass[:, :done] = early_mass[...] + there_mass[:, :done]
+    for at in range(done, half, block):
+        here = slice(at, at + block)
+        total, weight = weighed_sums(first + at, block, expos, points, factors)
+        store(at, at + block, total)
+        mass[:, here] = weight + there_mass[:, here]
+    for copy in copies:
+        copy.wait()
+
+
+def sums_call(block, side, rows, dtype, expos, points, factors, *last):
     n = len(expos)
-    n_points, width = points[0].shape
-    return pl.pallas_call(
-        functools.partial(sums_kernel, n, block, side),
-        in_specs=in_vmem(3 * n),
-        out_specs=in_vmem(2),
+    width = points[0].shape[1]
+    kernel = functools.partial(sums_kernel, n, block, side)
+    done, scratch = 0, []
+    if last:
+        kernel, done = functools.partial(last_kernel, n, block), last[0].shape[0]
+        scratch = [pltpu.VMEM((rows, width), dtype), pltpu.SemaphoreType.DMA((1 + (rows - done) // block,))]
+    n_points = sum(chunk.shape[0] for chunk in points)
+    return pl.pallas_call(
+        kernel,
+        in_specs=in_vmem(3 * n + len(last)),
+        out_specs=[pl.BlockSpec(memory_space=pltpu.HBM if last else pltpu.VMEM)] + in_vmem(1),
         out_shape=[jax.ShapeDtypeStruct((rows, width), dtype), jax.ShapeDtypeStruct((1, rows), jnp.float32)],
+        scratch_shapes=scratch,
         compiler_params=pltpu.CompilerParams(vmem_limit_bytes=VMEM_BYTES),
         cost_estimate=pl.CostEstimate(
-            flops=2 * rows * n * n_points * width,
-            bytes_accessed=2 * n * n_points * (rows + width) + 4 * rows * width,
+            flops=2 * (rows - done) * n_points * width,
+            bytes_accessed=2 * n_points * (rows + width) + 4 * rows * width,
             transcendentals=0,
         ),
-    )(*expos, *points, *factors)
-
-
-def add_kernel(block, here, here_mass, there, there_mass, sums, mass, out, left):
-    def copy(at):
-        rows = pl.ds(at * block, block)
-        return pltpu.make_async_copy(out.at[rows, :], sums.at[rows, :], left.at[at])
-
-    count = here.shape[0] // block
-    for at in range(count):
-        rows = slice(at * block, (at + 1) * block)
-        out[rows, :] = here[rows, :] + there[rows, :].astype(jnp.float32)
-        copy(at).start(priority=at % 2)
-    mass[...] = here_mass[...] + there_mass[...]
-    for at in range(count):
-        copy(at).wait()
-
-
-def add_call(block, here, here_mass, there, there_mass):
-    return pl.pallas_call(
-        functools.partial(add_kernel, block),
-        in_specs=in_vmem(4),
-        out_specs=[pl.BlockSpec(memory_space=pltpu.HBM)] + in_vmem(1),
-        out_shape=[
-            jax.ShapeDtypeStruct(here.shape, jnp.float32),
-            jax.ShapeDtypeStruct(here_mass.shape, jnp.float32),
-        ],
-        scratch_shapes=[
-            pltpu.VMEM(here.shape, jnp.float32),
-            pltpu.SemaphoreType.DMA((here.shape[0] // block,)),
-        ],
-        compiler_params=pltpu.CompilerParams(vmem_limit_bytes=VMEM_BYTES),
-    )(here, here_mass, there, there_mass)
+    )(*expos, *points, *factors, *last)
 
 
 def split_cells(codes, exponents, centroids, counters):
@@ -337,21 +337,21 @@
 
     near_1, near_2, near_3 = (along_z(own, by) for by in (1, 2, 3))
     inverse = inverse_call(counters)
-    near_01 = join(own, near_1)
+    near_01 = join(own, near_1, inverse)
+    held_01 = hold(near_01, declared=4 * 10**9)
     first_01, second_01 = turn(near_01), turn_back(near_01)
-    stats = [totals_call(rate, block, (near_01,), centroids, inverse)]
+    stats = [totals_call(rate, block, (held_01,), centroids, inverse)]
+    across_01 = turn_back(hold(first_01, stats[0]))
     near_23 = join(near_2, near_3, *stats)
-    across_01 = turn_back(hold(first_01, near_23))
-    first_23 = turn(near_23)
     stats.append(totals_call(rate, block, (near_23,), centroids, inverse, after=(first_01, second_01)))
-    second_23 = turn_back(hold(near_23, stats[1]))
+    first_23, second_23 = turn(near_23), turn_back(hold(near_23, stats[1]))
 
     expand = functools.partial(expo_call, rate, block, 2 * per_device)
     stat = beside(*stats)
-    bundles = [expand((near_01, first_01, second_01, across_01), centroids, stat)]
+    bundles = [expand((near_01, first_01, second_01, across_01), centroids, stat, declared=0.01)]
     stat = merge_call(rate, 1, False, stat, along_z(stat, 1), bundles[0][1])
     across_23 = turn_back(hold(first_23, stat))
-    bundles.append(expand((near_23, first_23, second_23), centroids, stat))
+    bundles.append(expand((near_23, first_23, second_23), centroids, stat, declared=0.01))
     goal = merge_call(rate, 2, True, stat, along_z(stat, 2), bundles[1][1])
     bundles.append(expand((across_23,), centroids))
     expos, tops, points = zip(*bundles)
@@ -360,8 +360,8 @@
 
     there = sums_call(block, 1, per_device, jnp.bfloat16, expos, points, factors)
     there = [exchange(a, ("lo",), lambda at: at ^ 1) for a in there]
-    here = sums_call(block, 0, per_device, jnp.float32, expos, points, factors)
-    out, mass = add_call(block // 2, *here, *there)
+    early = sums_call(block, 0, block, jnp.float32, expos, points, factors)
+    out, mass = sums_call(block // 2, 0, per_device, jnp.float32, expos, points, factors, *early, *there)
     return (out[None], mass)
 
 

time: 48.9 us -> 51.2 us (1.047)
  the two profiles are of different devices: /device:TPU:0 before, /device:TPU:25 now
where the time goes in v14:
time: 51.2 us; the launch traced here: 51 us
  starting transfers between devices  22.7 us (44%)
  Pallas kernels  16.5 us (32%)
  waiting for transfers between devices  8.11 us (16%)
  other arithmetic  1.69 us (3%)
  local copies, waits for them, and re-layouts  1.04 us (2%)
  between operations  0.95 us (2%)
    ppermute x16, starting transfers between devices, exchange(): return lax.ppermute(a, axes, [(partner(at), at) for at in range(count)])  22.7 us
    ppermute x16, waiting for transfers between devices, exchange(): return lax.ppermute(a, axes, [(partner(at), at) for at in range(count)])  8.11 us
    pallas_call x3, Pallas kernels, sums_call(): pl.pallas_call(kernel, in_specs=in_vmem(3 * n + len(last)), out_specs=[pl...  5.63 us
    pallas_call x2, Pallas kernels, totals_call(): pl.pallas_call(functools.partial(totals_kernel, rate, block, len(pieces))...  5.53 us
    pallas_call x3, Pallas kernels, expo_call(): pl.pallas_call(functools.partial(expo_kernel, rate, block, len(pieces)),...  4.28 us
    unnamed x6, local copies, waits for them, and re-layouts  1.04 us
    convert_element_type x1, other arithmetic, to_points(): return (codes.astype(jnp.float32) * scale[:, None]).astype(jnp.bfloat16)  1.03 us
  transfers between devices with their start and end apart: 16, of which 7 were waited for; matrix products, arithmetic and copies ran while one was open for 0% of the time, Pallas kernels for 23%

profile of v14, /device:TPU:25, one launch (start us, length us, event | category | flops | bytes accessed | tf_op | source)
XLA Modules:
  0.0 51.0 jit_solution(8890475123034728717)
XLA Ops:
  0.6 0.7 %convert_multiply_fusion = f32[128]{0:T(128)S(1)} fusion(s32[128]{0:T(128)} %param.5), kind=kLoop, calls=%fused_computation.1 | loop fusion | flops 512 | bytes 1024 | tf_op jit(solution)/shard_map/mul | solution.py:16
  1.3 1.0 %multiply_convert_fusion.above = bf16[128,512]{1,0:T(8,128)(2,1)S(1)} fusion(s32[128,512]{1,0:T(8,128)} %param.4, f32[128]{0:T(128)S(1)} %convert_multiply_fusion), kind=kLoop, calls=%fused_computation | loop fusion | flops 196608 | bytes 393728 | tf_op jit(solution)/shard_map/convert_element_type | solution.py:17
  2.3 0.2 collective-permute-start
  2.6 1.1 %collective-permute-start.5 = (bf16[128,512]{1,0:T(8,128)(2,1)S(1)}, bf16[128,512]{1,0:T(8,128)(2,1)S(1)}, u32[]{:S(2)}, u32[]{:S(2)}) collective-permute-start(bf16[128,512]{1,0:T(8,128)(2,1)S(1)} %multiply_convert_fusion.above), channel_id=1, source_target_pairs={{3,0},{2,1},{1,2},{0,3},{7,4},{6,5},{5,6},{4,7},{11,8},{10,9},{9,1... | collective-permute-start | bytes 393224 | tf_op jit(solution)/shard_map/ppermute | solution.py:49
  3.6 1.4 %collective-permute-start.4 = (bf16[128,512]{1,0:T(8,128)(2,1)S(1)}, bf16[128,512]{1,0:T(8,128)(2,1)S(1)}, u32[]{:S(2)}, u32[]{:S(2)}) collective-permute-start(bf16[128,512]{1,0:T(8,128)(2,1)S(1)} %multiply_convert_fusion.above), channel_id=1, source_target_pairs={{2,0},{3,1},{0,2},{1,3},{6,4},{7,5},{4,6},{5,7},{10,8},{11,9},{8,1... | collective-permute-start | bytes 393224 | tf_op jit(solution)/shard_map/ppermute | solution.py:49
  5.0 0.0 copy-start
  5.0 0.7 %copy-done = s32[6144]{0:T(1024)S(1)} copy-done((s32[6144]{0:T(1024)S(1)}, s32[6144]{0:T(1024)}, u32[]{:S(2)}) %copy-start) | copy-done | bytes 24600
  5.8 0.9 %shard_map.59.refs_0_.refs_2_ = f32[6144,128]{1,0:T(8,128)S(1)} custom-call(s32[48,128]{1,0:T(8,128)S(1)} %bitcast.4), custom_call_target="tpu_custom_call" | custom-call | tf_op jit(solution)/shard_map/pallas_call | solution.py:114
  6.7 0.1 collective-permute-done.below
  6.8 0.0 slice-start
  6.8 0.0 slice-start.1
  6.8 1.3 %collective-permute-start.2 = (bf16[256,512]{1,0:T(8,128)(2,1)S(1)}, bf16[256,512]{1,0:T(8,128)(2,1)S(1)}, u32[]{:S(2)}, u32[]{:S(2)}) collective-permute-start(bf16[256,512]{1,0:T(8,128)(2,1)S(1)} %shard_map.60.a.refs_0_), channel_id=1, source_target_pairs={{16,0},{12,4},{24,8},{4,12},{0,16},{28,20},{8,24},{20,28},{17,1},{... | collective-permute-start | bytes 786440 | tf_op jit(solution)/shard_map/ppermute | solution.py:49
  8.1 1.2 %collective-permute-start.1 = (bf16[256,512]{1,0:T(8,128)(2,1)S(1)}, bf16[256,512]{1,0:T(8,128)(2,1)S(1)}, u32[]{:S(2)}, u32[]{:S(2)}) collective-permute-start(bf16[256,512]{1,0:T(8,128)(2,1)S(1)} %shard_map.60.a.refs_0_), channel_id=1, source_target_pairs={{8,0},{20,4},{0,8},{28,12},{24,16},{4,20},{16,24},{12,28},{9,1},{2... | collective-permute-start | bytes 786440 | tf_op jit(solution)/shard_map/ppermute | solution.py:49
  9.3 0.0 slice-done
  9.3 0.3 slice-done.1
  9.6 2.7 %shard_map.62.refs_0_.left = f32[3,256]{1,0:T(4,128)S(1)} custom-call(bf16[256,512]{1,0:T(8,128)(2,1)S(1)} %shard_map.61.refs_0_, bf16[6144,512]{1,0:T(8,128)(2,1)S(1)} %bitcast.3, f32[6144,128]{1,0:T(8,128)S(1)} %shard_map.59.refs_0_.refs_2_), custom_call_target="tpu_custom_call" | custom-call | flops 1610612736 | bytes 6291456 | tf_op jit(solution)/shard_map/pallas_call | solution.py:153
  12.3 1.0 %collective-permute-done.1.a.refs_3_.refs_1_ = bf16[256,512]{1,0:T(8,128)(2,1)S(1)} collective-permute-done((bf16[256,512]{1,0:T(8,128)(2,1)S(1)}, bf16[256,512]{1,0:T(8,128)(2,1)S(1)}, u32[]{:S(2)}, u32[]{:S(2)}) %collective-permute-start.1) | collective-permute-done | bytes 262176 | tf_op jit(solution)/shard_map/ppermute | solution.py:49
  13.3 0.3 collective-permute-start.3
  13.6 0.0 collective-permute-done.5.below
  13.6 2.7 %collective-permute-done.4.above = bf16[128,512]{1,0:T(8,128)(2,1)S(1)} collective-permute-done((bf16[128,512]{1,0:T(8,128)(2,1)S(1)}, bf16[128,512]{1,0:T(8,128)(2,1)S(1)}, u32[]{:S(2)}, u32[]{:S(2)}) %collective-permute-start.4) | collective-permute-done | bytes 131104 | tf_op jit(solution)/shard_map/ppermute | solution.py:49
  16.4 1.3 %collective-permute-start.6 = (bf16[256,512]{1,0:T(8,128)(2,1)S(1)}, bf16[256,512]{1,0:T(8,128)(2,1)S(1)}, u32[]{:S(2)}, u32[]{:S(2)}) collective-permute-start(bf16[256,512]{1,0:T(8,128)(2,1)S(1)} %shard_map.64.refs_0_.a), channel_id=1, source_target_pairs={{8,0},{20,4},{0,8},{28,12},{24,16},{4,20},{16,24},{12,28},{9,1},{2... | collective-permute-start | bytes 786440 | tf_op jit(solution)/shard_map/ppermute | solution.py:49
  17.7 0.0 collective-permute-done.2.refs_4_.refs_2_
  17.7 2.8 %shard_map.65.right.refs_0_ = f32[3,256]{1,0:T(4,128)S(1)} custom-call(bf16[256,512]{1,0:T(8,128)(2,1)S(1)} %shard_map.64.refs_0_.a, bf16[6144,512]{1,0:T(8,128)(2,1)S(1)} %bitcast.3, f32[6144,128]{1,0:T(8,128)S(1)} %shard_map.59.refs_0_.refs_2_, bf16[256,512]{1,0:T(8,128)(2,1)S(1)} %collective-permute-done.1.a.refs_3_.refs_1_, ...), custom_call_target="tpu_custom_call" | custom-call | flops 1610612736 | bytes 6291456 | tf_op jit(solution)/shard_map/pallas_call | solution.py:153
  20.5 0.1 collective-permute-start.8
  20.7 1.5 %collective-permute-start.7 = (bf16[256,512]{1,0:T(8,128)(2,1)S(1)}, bf16[256,512]{1,0:T(8,128)(2,1)S(1)}, u32[]{:S(2)}, u32[]{:S(2)}) collective-permute-start(bf16[256,512]{1,0:T(8,128)(2,1)S(1)} %shard_map.68), channel_id=1, source_target_pairs={{16,0},{12,4},{24,8},{4,12},{0,16},{28,20},{8,24},{20,28},{17,1},{... | collective-permute-start | bytes 786440 | tf_op jit(solution)/shard_map/ppermute | solution.py:49
  22.2 0.0 collective-permute-done.3.refs_3_
  22.2 2.0 %shard_map.67 = (bf16[1536,1024]{1,0:T(8,128)(2,1)S(1)}, f32[6,1024]{1,0:T(8,128)S(1)}, bf16[1024,512]{1,0:T(8,128)(2,1)S(1)}) custom-call(bf16[256,512]{1,0:T(8,128)(2,1)S(1)} %shard_map.60.a.refs_0_, bf16[256,512]{1,0:T(8,128)(2,1)S(1)} %collective-permute-done.1.a.refs_3_.refs_1_, bf16[256,512]{1,0:T(8,128)(2,1)S(1)} %collective-permute-done.2.refs_4_.refs_2_, ...), custom_call_target="tpu_custom_call" | custom-call | flops 16106127 | bytes 57671 | tf_op jit(solution)/shard_map/pallas_call | solution.py:229
  24.2 0.0 collective-permute-done.8.theirs
  24.2 0.0 collective-permute-done.6.refs_1_.a
  24.3 0.2 collective-permute-start.9
  24.4 1.5 %collective-permute-start.10 = (f32[3,512]{1,0:T(4,128)S(1)}, f32[3,512]{1,0:T(4,128)S(1)}, u32[]{:S(2)}, u32[]{:S(2)}) collective-permute-start(f32[3,512]{1,0:T(4,128)S(1)} %shard_map.69.refs_4_.refs_0_.mine), channel_id=1, source_target_pairs={{2,0},{3,1},{0,2},{1,3},{6,4},{7,5},{4,6},{5,7},{10,8},{11,9},{8,1... | collective-permute-start | bytes 18440 | tf_op jit(solution)/shard_map/ppermute | solution.py:49
  25.9 2.6 %collective-permute-done.7.refs_2_ = bf16[256,512]{1,0:T(8,128)(2,1)S(1)} collective-permute-done((bf16[256,512]{1,0:T(8,128)(2,1)S(1)}, bf16[256,512]{1,0:T(8,128)(2,1)S(1)}, u32[]{:S(2)}, u32[]{:S(2)}) %collective-permute-start.7) | collective-permute-done | bytes 262176 | tf_op jit(solution)/shard_map/ppermute | solution.py:49
  28.5 1.6 %shard_map.70 = (bf16[1536,768]{1,0:T(8,128)(2,1)S(1)}, f32[6,768]{1,0:T(8,128)S(1)}, bf16[768,512]{1,0:T(8,128)(2,1)S(1)}) custom-call(bf16[256,512]{1,0:T(8,128)(2,1)S(1)} %shard_map.64.refs_0_.a, bf16[256,512]{1,0:T(8,128)(2,1)S(1)} %collective-permute-done.6.refs_1_.a, bf16[256,512]{1,0:T(8,128)(2,1)S(1)} %collective-permute-done.7.refs_2_, ...), custom_call_target="tpu_custom_call" | custom-call | flops 12079595 | bytes 47185 | tf_op jit(solution)/shard_map/pallas_call | solution.py:229
  30.1 0.0 collective-permute-done.10.theirs
  30.2 0.1 collective-permute-start.13
  30.2 1.2 %collective-permute-start.12 = (f32[2,512]{1,0:T(2,128)S(1)}, f32[2,512]{1,0:T(2,128)S(1)}, u32[]{:S(2)}, u32[]{:S(2)}) collective-permute-start(f32[2,512]{1,0:T(2,128)S(1)} %shard_map.73.refs_0_), channel_id=1, source_target_pairs={{16,0},{12,4},{24,8},{4,12},{0,16},{28,20},{8,24},{20,28},{17,1},{... | collective-permute-start | bytes 12296 | tf_op jit(solution)/shard_map/ppermute | solution.py:49
  31.4 1.5 %collective-permute-start.11 = (f32[2,512]{1,0:T(2,128)S(1)}, f32[2,512]{1,0:T(2,128)S(1)}, u32[]{:S(2)}, u32[]{:S(2)}) collective-permute-start(f32[2,512]{1,0:T(2,128)S(1)} %shard_map.73.refs_0_), channel_id=1, source_target_pairs={{8,0},{20,4},{0,8},{28,12},{24,16},{4,20},{16,24},{12,28},{9,1},{2... | collective-permute-start | bytes 12296 | tf_op jit(solution)/shard_map/ppermute | solution.py:49
  32.9 0.0 collective-permute-done.9.refs_0_
  32.9 0.7 %shard_map.72 = (bf16[1536,256]{1,0:T(8,128)(2,1)S(1)}, f32[6,256]{1,0:T(8,128)S(1)}, bf16[256,512]{1,0:T(8,128)(2,1)S(1)}) custom-call(bf16[256,512]{1,0:T(8,128)(2,1)S(1)} %collective-permute-done.9.refs_0_, bf16[6144,512]{1,0:T(8,128)(2,1)S(1)} %bitcast.3), custom_call_target="tpu_custom_call" | custom-call | flops 402653184 | bytes 2621440 | tf_op jit(solution)/shard_map/pallas_call | solution.py:229
  33.6 0.1 collective-permute-done.13.refs_3_
  33.7 0.0 collective-permute-done.12.refs_2_
  33.7 0.5 collective-permute-done.11.refs_1_
  34.2 2.2 %shard_map.76 = (bf16[768,512]{1,0:T(8,128)(2,1)S(1)}, f32[1,768]{1,0:T(1,128)S(1)}) custom-call(bf16[1536,1024]{1,0:T(8,128)(2,1)S(1)} %get-tuple-element.20.refs_0_, bf16[1536,768]{1,0:T(8,128)(2,1)S(1)} %get-tuple-element.22.refs_1_, bf16[1536,256]{1,0:T(8,128)(2,1)S(1)} %get-tuple-element.23.refs_2_, bf16[1024,512]{1,0:T(8,128)(2,1)S(1)} %get-tuple-element.24.refs_3_, ...), custom_call_target="tpu_custom_call" | custom-call | flops 1610612736 | bytes 6815744 | tf_op jit(solution)/shard_map/pallas_call | solution.py:310
  36.4 9.8 %collective-permute-start.14 = (bf16[768,512]{1,0:T(8,128)(2,1)S(1)}, bf16[768,512]{1,0:T(8,128)(2,1)S(1)}, u32[]{:S(2)}, u32[]{:S(2)}) collective-permute-start(bf16[768,512]{1,0:T(8,128)(2,1)S(1)} %get-tuple-element.34), channel_id=1, source_target_pairs={{4,0},{0,4},{5,1},{1,5},{6,2},{2,6},{7,3},{3,7},{12,8},{8,12},{13,... | collective-permute-start | bytes 2359304 | tf_op jit(solution)/shard_map/ppermute | solution.py:49
  46.2 0.1 collective-permute-start.15
  46.3 0.7 %shard_map.75 = (f32[256,512]{1,0:T(8,128)S(1)}, f32[1,256]{1,0:T(1,128)S(1)}) custom-call(bf16[1536,1024]{1,0:T(8,128)(2,1)S(1)} %get-tuple-element.20.refs_0_, bf16[1536,768]{1,0:T(8,128)(2,1)S(1)} %get-tuple-element.22.refs_1_, bf16[1536,256]{1,0:T(8,128)(2,1)S(1)} %get-tuple-element.23.refs_2_, bf16[1024,512]{1,0:T(8,128)(2,1)S(1)} %get-tuple-element.24.refs_3_, ...), custom_call_target="tpu_custom_call" | custom-call | flops 536870912 | bytes 3670016 | tf_op jit(solution)/shard_map/pallas_call | solution.py:310
  47.0 1.1 %collective-permute-done.15.refs_12_ = f32[1,768]{1,0:T(1,128)S(1)} collective-permute-done((f32[1,768]{1,0:T(1,128)S(1)}, f32[1,768]{1,0:T(1,128)S(1)}, u32[]{:S(2)}, u32[]{:S(2)}) %collective-permute-start.15) | collective-permute-done | bytes 3104 | tf_op jit(solution)/shard_map/ppermute | solution.py:49
  48.1 0.0 collective-permute-done.14.refs_11_
  48.1 2.7 %shard_map.77 = (f32[768,512]{1,0:T(8,128)}, f32[1,768]{1,0:T(1,128)}) custom-call(bf16[1536,1024]{1,0:T(8,128)(2,1)S(1)} %get-tuple-element.20.refs_0_, bf16[1536,768]{1,0:T(8,128)(2,1)S(1)} %get-tuple-element.22.refs_1_, bf16[1536,256]{1,0:T(8,128)(2,1)S(1)} %get-tuple-element.23.refs_2_, bf16[1024,512]{1,0:T(8,128)(2,1)S(1)} %get-tuple-element.24.refs_3_, ...), custom_call_target="tpu_custom_call" | custom-call | flops 1073741824 | bytes 6815744 | tf_op jit(solution)/shard_map/pallas_call | solution.py:310
  (11 shorter events, 0.2 us)
Async XLA Ops:
  2.3 4.4 %collective-permute-start = (bf16[128,512]{1,0:T(8,128)(2,1)S(1)}, bf16[128,512]{1,0:T(8,128)(2,1)S(1)}, u32[]{:S(2)}, u32[]{:S(2)}) collective-permute-start(bf16[128,512]{1,0:T(8,128)(2,1)S(1)} %multiply_convert_fusion.above), channel_id=1, source_target_pairs={{1,0},{0,1},{3,2},{2,3},{5,4},{4,5},{7,6},{6,7},{9,8},{8,9},{11,10... | collective-permute-start | bytes 393224 | tf_op jit(solution)/shard_map/ppermute | solution.py:49
  2.6 11.1 %collective-permute-start.5 = (bf16[128,512]{1,0:T(8,128)(2,1)S(1)}, bf16[128,512]{1,0:T(8,128)(2,1)S(1)}, u32[]{:S(2)}, u32[]{:S(2)}) collective-permute-start(bf16[128,512]{1,0:T(8,128)(2,1)S(1)} %multiply_convert_fusion.above), channel_id=1, source_target_pairs={{3,0},{2,1},{1,2},{0,3},{7,4},{6,5},{5,6},{4,7},{11,8},{10,9},{9,1... | collective-permute-start | bytes 393224 | tf_op jit(solution)/shard_map/ppermute | solution.py:49
  3.6 12.7 %collective-permute-start.4 = (bf16[128,512]{1,0:T(8,128)(2,1)S(1)}, bf16[128,512]{1,0:T(8,128)(2,1)S(1)}, u32[]{:S(2)}, u32[]{:S(2)}) collective-permute-start(bf16[128,512]{1,0:T(8,128)(2,1)S(1)} %multiply_convert_fusion.above), channel_id=1, source_target_pairs={{2,0},{3,1},{0,2},{1,3},{6,4},{7,5},{4,6},{5,7},{10,8},{11,9},{8,1... | collective-permute-start | bytes 393224 | tf_op jit(solution)/shard_map/ppermute | solution.py:49
  5.0 0.7 %copy-start = (s32[6144]{0:T(1024)S(1)}, s32[6144]{0:T(1024)}, u32[]{:S(2)}) copy-start(s32[6144]{0:T(1024)} %param.7) | copy-start | bytes 73732
  6.8 2.6 %slice-start = ((s8[6291456]{0:T(1024)(128)(4,1)}), s8[4194304]{0:T(1024)(128)(4,1)S(1)}, s32[]{:S(2)}) async-start(s8[6291456]{0:T(1024)(128)(4,1)} %bitcast.2), calls=%async_computation | async-start | bytes 8388608
  6.8 2.9 %slice-start.1 = ((s8[6291456]{0:T(1024)(128)(4,1)}), s8[2097152]{0:T(1024)(128)(4,1)S(1)}, s32[]{:S(2)}) async-start(s8[6291456]{0:T(1024)(128)(4,1)} %bitcast.2), calls=%async_computation.1 | async-start | bytes 4194304
  6.8 10.9 %collective-permute-start.2 = (bf16[256,512]{1,0:T(8,128)(2,1)S(1)}, bf16[256,512]{1,0:T(8,128)(2,1)S(1)}, u32[]{:S(2)}, u32[]{:S(2)}) collective-permute-start(bf16[256,512]{1,0:T(8,128)(2,1)S(1)} %shard_map.60.a.refs_0_), channel_id=1, source_target_pairs={{16,0},{12,4},{24,8},{4,12},{0,16},{28,20},{8,24},{20,28},{17,1},{... | collective-permute-start | bytes 786440 | tf_op jit(solution)/shard_map/ppermute | solution.py:49
  8.1 5.2 %collective-permute-start.1 = (bf16[256,512]{1,0:T(8,128)(2,1)S(1)}, bf16[256,512]{1,0:T(8,128)(2,1)S(1)}, u32[]{:S(2)}, u32[]{:S(2)}) collective-permute-start(bf16[256,512]{1,0:T(8,128)(2,1)S(1)} %shard_map.60.a.refs_0_), channel_id=1, source_target_pairs={{8,0},{20,4},{0,8},{28,12},{24,16},{4,20},{16,24},{12,28},{9,1},{2... | collective-permute-start | bytes 786440 | tf_op jit(solution)/shard_map/ppermute | solution.py:49
  13.3 8.8 %collective-permute-start.3 = (bf16[256,512]{1,0:T(8,128)(2,1)S(1)}, bf16[256,512]{1,0:T(8,128)(2,1)S(1)}, u32[]{:S(2)}, u32[]{:S(2)}) collective-permute-start(bf16[256,512]{1,0:T(8,128)(2,1)S(1)} %shard_map.63), channel_id=1, source_target_pairs={{16,0},{12,4},{24,8},{4,12},{0,16},{28,20},{8,24},{20,28},{17,1},{... | collective-permute-start | bytes 786440 | tf_op jit(solution)/shard_map/ppermute | solution.py:49
  16.4 7.9 %collective-permute-start.6 = (bf16[256,512]{1,0:T(8,128)(2,1)S(1)}, bf16[256,512]{1,0:T(8,128)(2,1)S(1)}, u32[]{:S(2)}, u32[]{:S(2)}) collective-permute-start(bf16[256,512]{1,0:T(8,128)(2,1)S(1)} %shard_map.64.refs_0_.a), channel_id=1, source_target_pairs={{8,0},{20,4},{0,8},{28,12},{24,16},{4,20},{16,24},{12,28},{9,1},{2... | collective-permute-start | bytes 786440 | tf_op jit(solution)/shard_map/ppermute | solution.py:49
  20.5 3.7 %collective-permute-start.8 = (f32[3,512]{1,0:T(4,128)S(1)}, f32[3,512]{1,0:T(4,128)S(1)}, u32[]{:S(2)}, u32[]{:S(2)}) collective-permute-start(f32[3,512]{1,0:T(4,128)S(1)} %shard_map.66.refs_5_.mine), channel_id=1, source_target_pairs={{1,0},{0,1},{3,2},{2,3},{5,4},{4,5},{7,6},{6,7},{9,8},{8,9},{11,10... | collective-permute-start | bytes 18440 | tf_op jit(solution)/shard_map/ppermute | solution.py:49
  20.7 7.9 %collective-permute-start.7 = (bf16[256,512]{1,0:T(8,128)(2,1)S(1)}, bf16[256,512]{1,0:T(8,128)(2,1)S(1)}, u32[]{:S(2)}, u32[]{:S(2)}) collective-permute-start(bf16[256,512]{1,0:T(8,128)(2,1)S(1)} %shard_map.68), channel_id=1, source_target_pairs={{16,0},{12,4},{24,8},{4,12},{0,16},{28,20},{8,24},{20,28},{17,1},{... | collective-permute-start | bytes 786440 | tf_op jit(solution)/shard_map/ppermute | solution.py:49
  24.3 8.6 %collective-permute-start.9 = (bf16[256,512]{1,0:T(8,128)(2,1)S(1)}, bf16[256,512]{1,0:T(8,128)(2,1)S(1)}, u32[]{:S(2)}, u32[]{:S(2)}) collective-permute-start(bf16[256,512]{1,0:T(8,128)(2,1)S(1)} %shard_map.71), channel_id=1, source_target_pairs={{16,0},{12,4},{24,8},{4,12},{0,16},{28,20},{8,24},{20,28},{17,1},{... | collective-permute-start | bytes 786440 | tf_op jit(solution)/shard_map/ppermute | solution.py:49
  24.4 5.7 %collective-permute-start.10 = (f32[3,512]{1,0:T(4,128)S(1)}, f32[3,512]{1,0:T(4,128)S(1)}, u32[]{:S(2)}, u32[]{:S(2)}) collective-permute-start(f32[3,512]{1,0:T(4,128)S(1)} %shard_map.69.refs_4_.refs_0_.mine), channel_id=1, source_target_pairs={{2,0},{3,1},{0,2},{1,3},{6,4},{7,5},{4,6},{5,7},{10,8},{11,9},{8,1... | collective-permute-start | bytes 18440 | tf_op jit(solution)/shard_map/ppermute | solution.py:49
  30.2 3.5 %collective-permute-start.13 = (f32[2,512]{1,0:T(2,128)S(1)}, f32[2,512]{1,0:T(2,128)S(1)}, u32[]{:S(2)}, u32[]{:S(2)}) collective-permute-start(f32[2,512]{1,0:T(2,128)S(1)} %shard_map.73.refs_0_), channel_id=1, source_target_pairs={{24,0},{16,8},{8,16},{0,24},{25,1},{17,9},{9,17},{1,25},{26,2},{18... | collective-permute-start | bytes 12296 | tf_op jit(solution)/shard_map/ppermute | solution.py:49
  30.2 3.4 %collective-permute-start.12 = (f32[2,512]{1,0:T(2,128)S(1)}, f32[2,512]{1,0:T(2,128)S(1)}, u32[]{:S(2)}, u32[]{:S(2)}) collective-permute-start(f32[2,512]{1,0:T(2,128)S(1)} %shard_map.73.refs_0_), channel_id=1, source_target_pairs={{16,0},{12,4},{24,8},{4,12},{0,16},{28,20},{8,24},{20,28},{17,1},{... | collective-permute-start | bytes 12296 | tf_op jit(solution)/shard_map/ppermute | solution.py:49
  31.4 2.8 %collective-permute-start.11 = (f32[2,512]{1,0:T(2,128)S(1)}, f32[2,512]{1,0:T(2,128)S(1)}, u32[]{:S(2)}, u32[]{:S(2)}) collective-permute-start(f32[2,512]{1,0:T(2,128)S(1)} %shard_map.73.refs_0_), channel_id=1, source_target_pairs={{8,0},{20,4},{0,8},{28,12},{24,16},{4,20},{16,24},{12,28},{9,1},{2... | collective-permute-start | bytes 12296 | tf_op jit(solution)/shard_map/ppermute | solution.py:49
  36.4 11.7 %collective-permute-start.14 = (bf16[768,512]{1,0:T(8,128)(2,1)S(1)}, bf16[768,512]{1,0:T(8,128)(2,1)S(1)}, u32[]{:S(2)}, u32[]{:S(2)}) collective-permute-start(bf16[768,512]{1,0:T(8,128)(2,1)S(1)} %get-tuple-element.34), channel_id=1, source_target_pairs={{4,0},{0,4},{5,1},{1,5},{6,2},{2,6},{7,3},{3,7},{12,8},{8,12},{13,... | collective-permute-start | bytes 2359304 | tf_op jit(solution)/shard_map/ppermute | solution.py:49
  46.2 1.9 %collective-permute-start.15 = (f32[1,768]{1,0:T(1,128)S(1)}, f32[1,768]{1,0:T(1,128)S(1)}, u32[]{:S(2)}, u32[]{:S(2)}) collective-permute-start(f32[1,768]{1,0:T(1,128)S(1)} %get-tuple-element.35), channel_id=1, source_target_pairs={{4,0},{0,4},{5,1},{1,5},{6,2},{2,6},{7,3},{3,7},{12,8},{8,12},{13,... | collective-permute-start | bytes 9224 | tf_op jit(solution)/shard_map/ppermute | solution.py:49

commit v15 on v13

--- a/solution.py
+++ b/solution.py
@@ -81,7 +81,7 @@
     )(left, right, *after)
 
 
-def hold(a, *after):
+def hold(a, *after, declared=0):
     def kernel(a, *refs):
         refs[-1][...] = a[...]
 
@@ -91,6 +91,7 @@
         out_specs=in_vmem(1)[0],
         out_shape=jax.ShapeDtypeStruct(a.shape, a.dtype),
         compiler_params=pltpu.CompilerParams(vmem_limit_bytes=VMEM_BYTES),
+        cost_estimate=pl.CostEstimate(flops=declared, bytes_accessed=0, transcendentals=0),
     )(a, *after)
 
 
@@ -116,7 +117,7 @@
         out_specs=in_vmem(1)[0],
         out_shape=jax.ShapeDtypeStruct((counters.shape[0], 128), jnp.float32),
         compiler_params=pltpu.CompilerParams(vmem_limit_bytes=VMEM_BYTES),
-        cost_estimate=pl.CostEstimate(flops=4 * 10**9, bytes_accessed=0, transcendentals=0),
+        cost_estimate=pl.CostEstimate(flops=2 * 10**9, bytes_accessed=0, transcendentals=0),
     )(counters.reshape(-1, 128), *after)
 
 
@@ -223,7 +224,7 @@
             tops[at : at + 1, some] = top
 
 
-def expo_call(rate, block, count, pieces, cells, *after):
+def expo_call(rate, block, count, pieces, cells, *after, declared=1.0):
     width = cells.shape[1]
     n_points = sum(piece.shape[0] for piece in pieces)
     return pl.pallas_call(
@@ -237,9 +238,9 @@
         ],
         compiler_params=pltpu.CompilerParams(vmem_limit_bytes=VMEM_BYTES),
         cost_estimate=pl.CostEstimate(
-            flops=2 * count * n_points * width,
-            bytes_accessed=2 * (count * width + n_points * width + count * n_points),
-            transcendentals=count * n_points,
+            flops=int(declared * 2 * count * n_points * width),
+            bytes_accessed=int(declared * 2 * (count * width + n_points * width + count * n_points)),
+            transcendentals=int(declared * count * n_points),
         ),
     )(*pieces, cells, *after)
 
@@ -249,8 +250,9 @@
     for expo, chunk, factor in zip(expos, points, factors):
         block = expo.shape[0] // factor.shape[0]
         shares = []
-        for at in range(0, count, block):
-            here = pl.ds(pl.multiple_of(start + at, block), block)
+        step = min(block, count)
+        for at in range(0, count, step):
+            here = pl.ds(pl.multiple_of(start + at, step), step)
             scale = factor[pl.ds((start + at) // block, 1), :]
             shares.append((expo[here, :].astype(jnp.float32) * scale).astype(jnp.bfloat16))
         share = jnp.concatenate(shares, axis=0)
@@ -337,21 +339,21 @@
 
     near_1, near_2, near_3 = (along_z(own, by) for by in (1, 2, 3))
     inverse = inverse_call(counters)
-    near_01 = join(own, near_1)
-    first_01, second_01 = turn(near_01), turn_back(near_01)
-    stats = [totals_call(rate, block, (near_01,), centroids, inverse)]
+    near_01 = join(own, near_1, inverse)
+    held_01 = hold(near_01, declared=2 * 10**9)
+    first_01 = turn(near_01)
+    stats = [totals_call(rate, block, (held_01,), centroids, inverse)]
+    second_01, across_01 = turn_back(hold(near_01, stats[0])), turn_back(hold(first_01, stats[0]))
     near_23 = join(near_2, near_3, *stats)
-    across_01 = turn_back(hold(first_01, near_23))
-    first_23 = turn(near_23)
-    stats.append(totals_call(rate, block, (near_23,), centroids, inverse, after=(first_01, second_01)))
-    second_23 = turn_back(hold(near_23, stats[1]))
+    stats.append(totals_call(rate, block, (near_23,), centroids, inverse, after=(first_01,)))
+    first_23, second_23 = turn(near_23), turn_back(hold(near_23, stats[1]))
 
     expand = functools.partial(expo_call, rate, block, 2 * per_device)
     stat = beside(*stats)
-    bundles = [expand((near_01, first_01, second_01, across_01), centroids, stat)]
+    bundles = [expand((near_01, first_01, second_01, across_01), centroids, stat, declared=0.01)]
     stat = merge_call(rate, 1, False, stat, along_z(stat, 1), bundles[0][1])
     across_23 = turn_back(hold(first_23, stat))
-    bundles.append(expand((near_23, first_23, second_23), centroids, stat))
+    bundles.append(expand((near_23, first_23, second_23), centroids, stat, declared=0.01))
     goal = merge_call(rate, 2, True, stat, along_z(stat, 2), bundles[1][1])
     bundles.append(expand((across_23,), centroids))
     expos, tops, points = zip(*bundles)

time: 48.9 us -> 48.7 us (level); the launches traced: 48 us -> 48.5 us
  starting transfers between devices: 22.8 us -> 23.3 us
    ppermute x16, starting transfers between devices: 22.8 us -> 23.3 us  [exchange(): return lax.ppermute(a, axes, [(partner(at), at) for at in range(count)])]
where the time goes in v15:
time: 48.7 us; the launch traced here: 48.5 us
  starting transfers between devices  23.3 us (48%)
  Pallas kernels  16.7 us (34%)
  waiting for transfers between devices  5.02 us (10%)
  other arithmetic  1.69 us (3%)
  between operations  0.99 us (2%)
  local copies, waits for them, and re-layouts  0.75 us (2%)
    ppermute x16, starting transfers between devices, exchange(): return lax.ppermute(a, axes, [(partner(at), at) for at in range(count)])  23.3 us
    pallas_call x2, Pallas kernels, totals_call(): pl.pallas_call(functools.partial(totals_kernel, rate, block, len(pieces))...  5.39 us
    ppermute x16, waiting for transfers between devices, exchange(): return lax.ppermute(a, axes, [(partner(at), at) for at in range(count)])  5.02 us
    pallas_call x3, Pallas kernels, expo_call(): pl.pallas_call(functools.partial(expo_kernel, rate, block, len(pieces)),...  4.28 us
    pallas_call x2, Pallas kernels, sums_call(): pl.pallas_call(functools.partial(sums_kernel, n, block, side), in_specs=i...  4.2 us
    pallas_call x1, Pallas kernels, add_call(): pl.pallas_call(functools.partial(add_kernel, block), in_specs=in_vmem(4),...  1.79 us
    convert_element_type x1, other arithmetic, to_points(): return (codes.astype(jnp.float32) * scale[:, None]).astype(jnp.bfloat16)  1.03 us
  transfers between devices with their start and end apart: 16, of which 6 were waited for; matrix products, arithmetic and copies ran while one was open for 0% of the time, Pallas kernels for 26%

profile of v15, /device:TPU:0, one launch (start us, length us, event | category | flops | bytes accessed | tf_op | source)
XLA Modules:
  0.0 48.5 jit_solution(5019372907062758786)
XLA Ops:
  0.6 0.7 %convert_multiply_fusion = f32[128]{0:T(128)S(1)} fusion(s32[128]{0:T(128)} %param.5), kind=kLoop, calls=%fused_computation.1 | loop fusion | flops 512 | bytes 1024 | tf_op jit(solution)/shard_map/mul | solution.py:16
  1.3 1.0 %multiply_convert_fusion.above = bf16[128,512]{1,0:T(8,128)(2,1)S(1)} fusion(s32[128,512]{1,0:T(8,128)} %param.4, f32[128]{0:T(128)S(1)} %convert_multiply_fusion), kind=kLoop, calls=%fused_computation | loop fusion | flops 196608 | bytes 393728 | tf_op jit(solution)/shard_map/convert_element_type | solution.py:17
  2.3 3.1 %collective-permute-start = (bf16[128,512]{1,0:T(8,128)(2,1)S(1)}, bf16[128,512]{1,0:T(8,128)(2,1)S(1)}, u32[]{:S(2)}, u32[]{:S(2)}) collective-permute-start(bf16[128,512]{1,0:T(8,128)(2,1)S(1)} %multiply_convert_fusion.above), channel_id=1, source_target_pairs={{1,0},{0,1},{3,2},{2,3},{5,4},{4,5},{7,6},{6,7},{9,8},{8,9},{11,10... | collective-permute-start | bytes 393224 | tf_op jit(solution)/shard_map/ppermute | solution.py:49
  5.4 2.6 %collective-permute-start.4 = (bf16[128,512]{1,0:T(8,128)(2,1)S(1)}, bf16[128,512]{1,0:T(8,128)(2,1)S(1)}, u32[]{:S(2)}, u32[]{:S(2)}) collective-permute-start(bf16[128,512]{1,0:T(8,128)(2,1)S(1)} %multiply_convert_fusion.above), channel_id=1, source_target_pairs={{2,0},{3,1},{0,2},{1,3},{6,4},{7,5},{4,6},{5,7},{10,8},{11,9},{8,1... | collective-permute-start | bytes 393224 | tf_op jit(solution)/shard_map/ppermute | solution.py:49
  8.0 0.0 collective-permute-start.5
  8.0 0.0 copy-start
  8.0 0.7 %copy-done = s32[6144]{0:T(1024)S(1)} copy-done((s32[6144]{0:T(1024)S(1)}, s32[6144]{0:T(1024)}, u32[]{:S(2)}) %copy-start) | copy-done | bytes 24600
  8.8 0.0 slice-start
  8.8 0.9 %shard_map.59.refs_0_.refs_2_ = f32[6144,128]{1,0:T(8,128)S(1)} custom-call(s32[48,128]{1,0:T(8,128)S(1)} %bitcast.4), custom_call_target="tpu_custom_call" | custom-call | flops 2000000000 | tf_op jit(solution)/shard_map/pallas_call | solution.py:114
  9.6 0.0 slice-start.1
  9.7 0.8 %collective-permute-done.below = bf16[128,512]{1,0:T(8,128)(2,1)S(1)} collective-permute-done((bf16[128,512]{1,0:T(8,128)(2,1)S(1)}, bf16[128,512]{1,0:T(8,128)(2,1)S(1)}, u32[]{:S(2)}, u32[]{:S(2)}) %collective-permute-start) | collective-permute-done | bytes 131104 | tf_op jit(solution)/shard_map/ppermute | solution.py:49
  10.5 1.8 %collective-permute-start.1 = (bf16[256,512]{1,0:T(8,128)(2,1)S(1)}, bf16[256,512]{1,0:T(8,128)(2,1)S(1)}, u32[]{:S(2)}, u32[]{:S(2)}) collective-permute-start(bf16[256,512]{1,0:T(8,128)(2,1)S(1)} %shard_map.60.a.refs_0_), channel_id=1, source_target_pairs={{8,0},{20,4},{0,8},{28,12},{24,16},{4,20},{16,24},{12,28},{9,1},{2... | collective-permute-start | bytes 786440 | tf_op jit(solution)/shard_map/ppermute | solution.py:49
  12.3 0.0 slice-done
  12.3 0.0 slice-done.1
  12.3 2.7 %shard_map.62.refs_0_.left = f32[3,256]{1,0:T(4,128)S(1)} custom-call(bf16[256,512]{1,0:T(8,128)(2,1)S(1)} %shard_map.61.refs_0_, bf16[6144,512]{1,0:T(8,128)(2,1)S(1)} %bitcast.3, f32[6144,128]{1,0:T(8,128)S(1)} %shard_map.59.refs_0_.refs_2_), custom_call_target="tpu_custom_call" | custom-call | flops 1610612736 | bytes 6291456 | tf_op jit(solution)/shard_map/pallas_call | solution.py:154
  15.0 1.6 %collective-permute-start.2 = (bf16[256,512]{1,0:T(8,128)(2,1)S(1)}, bf16[256,512]{1,0:T(8,128)(2,1)S(1)}, u32[]{:S(2)}, u32[]{:S(2)}) collective-permute-start(bf16[256,512]{1,0:T(8,128)(2,1)S(1)} %shard_map.63), channel_id=1, source_target_pairs={{16,0},{12,4},{24,8},{4,12},{0,16},{28,20},{8,24},{20,28},{17,1},{... | collective-permute-start | bytes 786440 | tf_op jit(solution)/shard_map/ppermute | solution.py:49
  16.6 0.6 %collective-permute-done.1.a.refs_3_.refs_1_ = bf16[256,512]{1,0:T(8,128)(2,1)S(1)} collective-permute-done((bf16[256,512]{1,0:T(8,128)(2,1)S(1)}, bf16[256,512]{1,0:T(8,128)(2,1)S(1)}, u32[]{:S(2)}, u32[]{:S(2)}) %collective-permute-start.1) | collective-permute-done | bytes 262176 | tf_op jit(solution)/shard_map/ppermute | solution.py:49
  17.3 2.0 %collective-permute-start.3 = (bf16[256,512]{1,0:T(8,128)(2,1)S(1)}, bf16[256,512]{1,0:T(8,128)(2,1)S(1)}, u32[]{:S(2)}, u32[]{:S(2)}) collective-permute-start(bf16[256,512]{1,0:T(8,128)(2,1)S(1)} %shard_map.64), channel_id=1, source_target_pairs={{16,0},{12,4},{24,8},{4,12},{0,16},{28,20},{8,24},{20,28},{17,1},{... | collective-permute-start | bytes 786440 | tf_op jit(solution)/shard_map/ppermute | solution.py:49
  19.3 0.0 collective-permute-done.4.above
  19.3 0.0 collective-permute-done.5.below
  19.3 1.6 %collective-permute-start.6 = (bf16[256,512]{1,0:T(8,128)(2,1)S(1)}, bf16[256,512]{1,0:T(8,128)(2,1)S(1)}, u32[]{:S(2)}, u32[]{:S(2)}) collective-permute-start(bf16[256,512]{1,0:T(8,128)(2,1)S(1)} %shard_map.65.refs_0_.a), channel_id=1, source_target_pairs={{8,0},{20,4},{0,8},{28,12},{24,16},{4,20},{16,24},{12,28},{9,1},{2... | collective-permute-start | bytes 786440 | tf_op jit(solution)/shard_map/ppermute | solution.py:49
  20.9 2.7 %shard_map.66.right.refs_0_ = f32[3,256]{1,0:T(4,128)S(1)} custom-call(bf16[256,512]{1,0:T(8,128)(2,1)S(1)} %shard_map.65.refs_0_.a, bf16[6144,512]{1,0:T(8,128)(2,1)S(1)} %bitcast.3, f32[6144,128]{1,0:T(8,128)S(1)} %shard_map.59.refs_0_.refs_2_, bf16[256,512]{1,0:T(8,128)(2,1)S(1)} %collective-permute-done.1.a.refs_3_.refs_1_), custom_call_target="tpu_custom_call" | custom-call | flops 1610612736 | bytes 6291456 | tf_op jit(solution)/shard_map/pallas_call | solution.py:154
  23.6 1.1 %collective-permute-start.8 = (f32[3,512]{1,0:T(4,128)S(1)}, f32[3,512]{1,0:T(4,128)S(1)}, u32[]{:S(2)}, u32[]{:S(2)}) collective-permute-start(f32[3,512]{1,0:T(4,128)S(1)} %shard_map.67.refs_5_.mine), channel_id=1, source_target_pairs={{1,0},{0,1},{3,2},{2,3},{5,4},{4,5},{7,6},{6,7},{9,8},{8,9},{11,10... | collective-permute-start | bytes 18440 | tf_op jit(solution)/shard_map/ppermute | solution.py:49
  24.7 1.6 %collective-permute-start.7 = (bf16[256,512]{1,0:T(8,128)(2,1)S(1)}, bf16[256,512]{1,0:T(8,128)(2,1)S(1)}, u32[]{:S(2)}, u32[]{:S(2)}) collective-permute-start(bf16[256,512]{1,0:T(8,128)(2,1)S(1)} %shard_map.69), channel_id=1, source_target_pairs={{16,0},{12,4},{24,8},{4,12},{0,16},{28,20},{8,24},{20,28},{17,1},{... | collective-permute-start | bytes 786440 | tf_op jit(solution)/shard_map/ppermute | solution.py:49
  26.3 0.0 collective-permute-done.2.refs_2_
  26.3 0.7 %collective-permute-done.3.refs_3_ = bf16[256,512]{1,0:T(8,128)(2,1)S(1)} collective-permute-done((bf16[256,512]{1,0:T(8,128)(2,1)S(1)}, bf16[256,512]{1,0:T(8,128)(2,1)S(1)}, u32[]{:S(2)}, u32[]{:S(2)}) %collective-permute-start.3) | collective-permute-done | bytes 262176 | tf_op jit(solution)/shard_map/ppermute | solution.py:49
  27.0 2.0 %shard_map.68 = (bf16[1536,1024]{1,0:T(8,128)(2,1)S(1)}, f32[6,1024]{1,0:T(8,128)S(1)}, bf16[1024,512]{1,0:T(8,128)(2,1)S(1)}) custom-call(bf16[256,512]{1,0:T(8,128)(2,1)S(1)} %shard_map.60.a.refs_0_, bf16[256,512]{1,0:T(8,128)(2,1)S(1)} %collective-permute-done.1.a.refs_3_.refs_1_, bf16[256,512]{1,0:T(8,128)(2,1)S(1)} %collective-permute-done.2.refs_2_, ...), custom_call_target="tpu_custom_call" | custom-call | flops 16106127 | bytes 57671 | tf_op jit(solution)/shard_map/pallas_call | solution.py:230
  29.0 0.0 collective-permute-done.8.theirs
  29.0 0.0 collective-permute-done.6.refs_1_.a
  29.1 1.6 %collective-permute-start.9 = (bf16[256,512]{1,0:T(8,128)(2,1)S(1)}, bf16[256,512]{1,0:T(8,128)(2,1)S(1)}, u32[]{:S(2)}, u32[]{:S(2)}) collective-permute-start(bf16[256,512]{1,0:T(8,128)(2,1)S(1)} %shard_map.72), channel_id=1, source_target_pairs={{16,0},{12,4},{24,8},{4,12},{0,16},{28,20},{8,24},{20,28},{17,1},{... | collective-permute-start | bytes 786440 | tf_op jit(solution)/shard_map/ppermute | solution.py:49
  30.7 2.3 %collective-permute-start.10 = (f32[3,512]{1,0:T(4,128)S(1)}, f32[3,512]{1,0:T(4,128)S(1)}, u32[]{:S(2)}, u32[]{:S(2)}) collective-permute-start(f32[3,512]{1,0:T(4,128)S(1)} %shard_map.70.refs_4_.refs_0_.mine), channel_id=1, source_target_pairs={{2,0},{3,1},{0,2},{1,3},{6,4},{7,5},{4,6},{5,7},{10,8},{11,9},{8,1... | collective-permute-start | bytes 18440 | tf_op jit(solution)/shard_map/ppermute | solution.py:49
  32.9 0.0 collective-permute-done.7.refs_2_
  32.9 1.6 %shard_map.71 = (bf16[1536,768]{1,0:T(8,128)(2,1)S(1)}, f32[6,768]{1,0:T(8,128)S(1)}, bf16[768,512]{1,0:T(8,128)(2,1)S(1)}) custom-call(bf16[256,512]{1,0:T(8,128)(2,1)S(1)} %shard_map.65.refs_0_.a, bf16[256,512]{1,0:T(8,128)(2,1)S(1)} %collective-permute-done.6.refs_1_.a, bf16[256,512]{1,0:T(8,128)(2,1)S(1)} %collective-permute-done.7.refs_2_, ...), custom_call_target="tpu_custom_call" | custom-call | flops 12079595 | bytes 47185 | tf_op jit(solution)/shard_map/pallas_call | solution.py:230
  34.5 0.7 %collective-permute-done.10.theirs = f32[3,512]{1,0:T(4,128)S(1)} collective-permute-done((f32[3,512]{1,0:T(4,128)S(1)}, f32[3,512]{1,0:T(4,128)S(1)}, u32[]{:S(2)}, u32[]{:S(2)}) %collective-permute-start.10) | collective-permute-done | bytes 6176 | tf_op jit(solution)/shard_map/ppermute | solution.py:49
  35.2 1.4 %collective-permute-start.11 = (f32[2,512]{1,0:T(2,128)S(1)}, f32[2,512]{1,0:T(2,128)S(1)}, u32[]{:S(2)}, u32[]{:S(2)}) collective-permute-start(f32[2,512]{1,0:T(2,128)S(1)} %shard_map.74.refs_0_), channel_id=1, source_target_pairs={{8,0},{20,4},{0,8},{28,12},{24,16},{4,20},{16,24},{12,28},{9,1},{2... | collective-permute-start | bytes 12296 | tf_op jit(solution)/shard_map/ppermute | solution.py:49
  36.7 0.5 %collective-permute-start.12 = (f32[2,512]{1,0:T(2,128)S(1)}, f32[2,512]{1,0:T(2,128)S(1)}, u32[]{:S(2)}, u32[]{:S(2)}) collective-permute-start(f32[2,512]{1,0:T(2,128)S(1)} %shard_map.74.refs_0_), channel_id=1, source_target_pairs={{16,0},{12,4},{24,8},{4,12},{0,16},{28,20},{8,24},{20,28},{17,1},{... | collective-permute-start | bytes 12296 | tf_op jit(solution)/shard_map/ppermute | solution.py:49
  37.2 1.6 %collective-permute-start.13 = (f32[2,512]{1,0:T(2,128)S(1)}, f32[2,512]{1,0:T(2,128)S(1)}, u32[]{:S(2)}, u32[]{:S(2)}) collective-permute-start(f32[2,512]{1,0:T(2,128)S(1)} %shard_map.74.refs_0_), channel_id=1, source_target_pairs={{24,0},{16,8},{8,16},{0,24},{25,1},{17,9},{9,17},{1,25},{26,2},{18... | collective-permute-start | bytes 12296 | tf_op jit(solution)/shard_map/ppermute | solution.py:49
  38.8 0.0 collective-permute-done.9.refs_0_
  38.8 0.7 %shard_map.73 = (bf16[1536,256]{1,0:T(8,128)(2,1)S(1)}, f32[6,256]{1,0:T(8,128)S(1)}, bf16[256,512]{1,0:T(8,128)(2,1)S(1)}) custom-call(bf16[256,512]{1,0:T(8,128)(2,1)S(1)} %collective-permute-done.9.refs_0_, bf16[6144,512]{1,0:T(8,128)(2,1)S(1)} %bitcast.3), custom_call_target="tpu_custom_call" | custom-call | flops 402653184 | bytes 2621440 | tf_op jit(solution)/shard_map/pallas_call | solution.py:230
  39.5 0.0 collective-permute-done.11.refs_1_
  39.5 0.8 %collective-permute-done.12.refs_2_ = f32[2,512]{1,0:T(2,128)S(1)} collective-permute-done((f32[2,512]{1,0:T(2,128)S(1)}, f32[2,512]{1,0:T(2,128)S(1)}, u32[]{:S(2)}, u32[]{:S(2)}) %collective-permute-start.12) | collective-permute-done | bytes 4128 | tf_op jit(solution)/shard_map/ppermute | solution.py:49
  40.3 1.4 %collective-permute-done.13.refs_3_ = f32[2,512]{1,0:T(2,128)S(1)} collective-permute-done((f32[2,512]{1,0:T(2,128)S(1)}, f32[2,512]{1,0:T(2,128)S(1)}, u32[]{:S(2)}, u32[]{:S(2)}) %collective-permute-start.13) | collective-permute-done | bytes 4128 | tf_op jit(solution)/shard_map/ppermute | solution.py:49
  41.7 2.2 %shard_map.77 = (bf16[768,512]{1,0:T(8,128)(2,1)S(1)}, f32[1,768]{1,0:T(1,128)S(1)}) custom-call(bf16[1536,1024]{1,0:T(8,128)(2,1)S(1)} %get-tuple-element.20.refs_0_, bf16[1536,768]{1,0:T(8,128)(2,1)S(1)} %get-tuple-element.22.refs_1_, bf16[1536,256]{1,0:T(8,128)(2,1)S(1)} %get-tuple-element.23.refs_2_, bf16[1024,512]{1,0:T(8,128)(2,1)S(1)} %get-tuple-element.24.refs_3_, ...), custom_call_target="tpu_custom_call" | custom-call | flops 2415919104 | bytes 9437184 | tf_op jit(solution)/shard_map/pallas_call | solution.py:281
  43.9 0.1 collective-permute-start.14
  44.0 0.5 %collective-permute-start.15 = (f32[1,768]{1,0:T(1,128)S(1)}, f32[1,768]{1,0:T(1,128)S(1)}, u32[]{:S(2)}, u32[]{:S(2)}) collective-permute-start(f32[1,768]{1,0:T(1,128)S(1)} %get-tuple-element.35), channel_id=1, source_target_pairs={{4,0},{0,4},{5,1},{1,5},{6,2},{2,6},{7,3},{3,7},{12,8},{8,12},{13,... | collective-permute-start | bytes 9224 | tf_op jit(solution)/shard_map/ppermute | solution.py:49
  44.5 2.0 %shard_map.76 = (f32[768,512]{1,0:T(8,128)S(1)}, f32[1,768]{1,0:T(1,128)S(1)}) custom-call(bf16[1536,1024]{1,0:T(8,128)(2,1)S(1)} %get-tuple-element.20.refs_0_, bf16[1536,768]{1,0:T(8,128)(2,1)S(1)} %get-tuple-element.22.refs_1_, bf16[1536,256]{1,0:T(8,128)(2,1)S(1)} %get-tuple-element.23.refs_2_, bf16[1024,512]{1,0:T(8,128)(2,1)S(1)} %get-tuple-element.24.refs_3_, ...), custom_call_target="tpu_custom_call" | custom-call | flops 2415919104 | bytes 9437184 | tf_op jit(solution)/shard_map/pallas_call | solution.py:281
  46.5 0.0 collective-permute-done.15.there_mass
  46.5 0.0 collective-permute-done.14.there
  46.5 1.8 %shard_map.78 = (f32[768,512]{1,0:T(8,128)}, f32[1,768]{1,0:T(1,128)}) custom-call(f32[768,512]{1,0:T(8,128)S(1)} %get-tuple-element.32.here, f32[1,768]{1,0:T(1,128)S(1)} %get-tuple-element.33.here_mass, bf16[768,512]{1,0:T(8,128)(2,1)S(1)} %collective-permute-done.14.there, f32[1,768]{1,0:T(1,128)S(1)} %collective-permute-done.15.there_mass), custom_call_target="tpu_custom_call" | custom-call | tf_op jit(solution)/shard_map/pallas_call | solution.py:311
  (12 shorter events, 0.2 us)
Async XLA Ops:
  2.3 8.1 %collective-permute-start = (bf16[128,512]{1,0:T(8,128)(2,1)S(1)}, bf16[128,512]{1,0:T(8,128)(2,1)S(1)}, u32[]{:S(2)}, u32[]{:S(2)}) collective-permute-start(bf16[128,512]{1,0:T(8,128)(2,1)S(1)} %multiply_convert_fusion.above), channel_id=1, source_target_pairs={{1,0},{0,1},{3,2},{2,3},{5,4},{4,5},{7,6},{6,7},{9,8},{8,9},{11,10... | collective-permute-start | bytes 393224 | tf_op jit(solution)/shard_map/ppermute | solution.py:49
  5.4 13.9 %collective-permute-start.4 = (bf16[128,512]{1,0:T(8,128)(2,1)S(1)}, bf16[128,512]{1,0:T(8,128)(2,1)S(1)}, u32[]{:S(2)}, u32[]{:S(2)}) collective-permute-start(bf16[128,512]{1,0:T(8,128)(2,1)S(1)} %multiply_convert_fusion.above), channel_id=1, source_target_pairs={{2,0},{3,1},{0,2},{1,3},{6,4},{7,5},{4,6},{5,7},{10,8},{11,9},{8,1... | collective-permute-start | bytes 393224 | tf_op jit(solution)/shard_map/ppermute | solution.py:49
  8.0 11.3 %collective-permute-start.5 = (bf16[128,512]{1,0:T(8,128)(2,1)S(1)}, bf16[128,512]{1,0:T(8,128)(2,1)S(1)}, u32[]{:S(2)}, u32[]{:S(2)}) collective-permute-start(bf16[128,512]{1,0:T(8,128)(2,1)S(1)} %multiply_convert_fusion.above), channel_id=1, source_target_pairs={{3,0},{2,1},{1,2},{0,3},{7,4},{6,5},{5,6},{4,7},{11,8},{10,9},{9,1... | collective-permute-start | bytes 393224 | tf_op jit(solution)/shard_map/ppermute | solution.py:49
  8.0 0.7 %copy-start = (s32[6144]{0:T(1024)S(1)}, s32[6144]{0:T(1024)}, u32[]{:S(2)}) copy-start(s32[6144]{0:T(1024)} %param.7) | copy-start | bytes 73732
  8.8 3.5 %slice-start = ((s8[6291456]{0:T(1024)(128)(4,1)}), s8[4194304]{0:T(1024)(128)(4,1)S(1)}, s32[]{:S(2)}) async-start(s8[6291456]{0:T(1024)(128)(4,1)} %bitcast.2), calls=%async_computation | async-start | bytes 8388608
  9.6 2.6 %slice-start.1 = ((s8[6291456]{0:T(1024)(128)(4,1)}), s8[2097152]{0:T(1024)(128)(4,1)S(1)}, s32[]{:S(2)}) async-start(s8[6291456]{0:T(1024)(128)(4,1)} %bitcast.2), calls=%async_computation.1 | async-start | bytes 4194304
  10.5 6.8 %collective-permute-start.1 = (bf16[256,512]{1,0:T(8,128)(2,1)S(1)}, bf16[256,512]{1,0:T(8,128)(2,1)S(1)}, u32[]{:S(2)}, u32[]{:S(2)}) collective-permute-start(bf16[256,512]{1,0:T(8,128)(2,1)S(1)} %shard_map.60.a.refs_0_), channel_id=1, source_target_pairs={{8,0},{20,4},{0,8},{28,12},{24,16},{4,20},{16,24},{12,28},{9,1},{2... | collective-permute-start | bytes 786440 | tf_op jit(solution)/shard_map/ppermute | solution.py:49
  15.0 11.2 %collective-permute-start.2 = (bf16[256,512]{1,0:T(8,128)(2,1)S(1)}, bf16[256,512]{1,0:T(8,128)(2,1)S(1)}, u32[]{:S(2)}, u32[]{:S(2)}) collective-permute-start(bf16[256,512]{1,0:T(8,128)(2,1)S(1)} %shard_map.63), channel_id=1, source_target_pairs={{16,0},{12,4},{24,8},{4,12},{0,16},{28,20},{8,24},{20,28},{17,1},{... | collective-permute-start | bytes 786440 | tf_op jit(solution)/shard_map/ppermute | solution.py:49
  17.3 9.7 %collective-permute-start.3 = (bf16[256,512]{1,0:T(8,128)(2,1)S(1)}, bf16[256,512]{1,0:T(8,128)(2,1)S(1)}, u32[]{:S(2)}, u32[]{:S(2)}) collective-permute-start(bf16[256,512]{1,0:T(8,128)(2,1)S(1)} %shard_map.64), channel_id=1, source_target_pairs={{16,0},{12,4},{24,8},{4,12},{0,16},{28,20},{8,24},{20,28},{17,1},{... | collective-permute-start | bytes 786440 | tf_op jit(solution)/shard_map/ppermute | solution.py:49
  19.3 9.7 %collective-permute-start.6 = (bf16[256,512]{1,0:T(8,128)(2,1)S(1)}, bf16[256,512]{1,0:T(8,128)(2,1)S(1)}, u32[]{:S(2)}, u32[]{:S(2)}) collective-permute-start(bf16[256,512]{1,0:T(8,128)(2,1)S(1)} %shard_map.65.refs_0_.a), channel_id=1, source_target_pairs={{8,0},{20,4},{0,8},{28,12},{24,16},{4,20},{16,24},{12,28},{9,1},{2... | collective-permute-start | bytes 786440 | tf_op jit(solution)/shard_map/ppermute | solution.py:49
  23.6 5.4 %collective-permute-start.8 = (f32[3,512]{1,0:T(4,128)S(1)}, f32[3,512]{1,0:T(4,128)S(1)}, u32[]{:S(2)}, u32[]{:S(2)}) collective-permute-start(f32[3,512]{1,0:T(4,128)S(1)} %shard_map.67.refs_5_.mine), channel_id=1, source_target_pairs={{1,0},{0,1},{3,2},{2,3},{5,4},{4,5},{7,6},{6,7},{9,8},{8,9},{11,10... | collective-permute-start | bytes 18440 | tf_op jit(solution)/shard_map/ppermute | solution.py:49
  24.7 8.2 %collective-permute-start.7 = (bf16[256,512]{1,0:T(8,128)(2,1)S(1)}, bf16[256,512]{1,0:T(8,128)(2,1)S(1)}, u32[]{:S(2)}, u32[]{:S(2)}) collective-permute-start(bf16[256,512]{1,0:T(8,128)(2,1)S(1)} %shard_map.69), channel_id=1, source_target_pairs={{16,0},{12,4},{24,8},{4,12},{0,16},{28,20},{8,24},{20,28},{17,1},{... | collective-permute-start | bytes 786440 | tf_op jit(solution)/shard_map/ppermute | solution.py:49
  29.1 9.7 %collective-permute-start.9 = (bf16[256,512]{1,0:T(8,128)(2,1)S(1)}, bf16[256,512]{1,0:T(8,128)(2,1)S(1)}, u32[]{:S(2)}, u32[]{:S(2)}) collective-permute-start(bf16[256,512]{1,0:T(8,128)(2,1)S(1)} %shard_map.72), channel_id=1, source_target_pairs={{16,0},{12,4},{24,8},{4,12},{0,16},{28,20},{8,24},{20,28},{17,1},{... | collective-permute-start | bytes 786440 | tf_op jit(solution)/shard_map/ppermute | solution.py:49
  30.7 4.5 %collective-permute-start.10 = (f32[3,512]{1,0:T(4,128)S(1)}, f32[3,512]{1,0:T(4,128)S(1)}, u32[]{:S(2)}, u32[]{:S(2)}) collective-permute-start(f32[3,512]{1,0:T(4,128)S(1)} %shard_map.70.refs_4_.refs_0_.mine), channel_id=1, source_target_pairs={{2,0},{3,1},{0,2},{1,3},{6,4},{7,5},{4,6},{5,7},{10,8},{11,9},{8,1... | collective-permute-start | bytes 18440 | tf_op jit(solution)/shard_map/ppermute | solution.py:49
  35.2 4.3 %collective-permute-start.11 = (f32[2,512]{1,0:T(2,128)S(1)}, f32[2,512]{1,0:T(2,128)S(1)}, u32[]{:S(2)}, u32[]{:S(2)}) collective-permute-start(f32[2,512]{1,0:T(2,128)S(1)} %shard_map.74.refs_0_), channel_id=1, source_target_pairs={{8,0},{20,4},{0,8},{28,12},{24,16},{4,20},{16,24},{12,28},{9,1},{2... | collective-permute-start | bytes 12296 | tf_op jit(solution)/shard_map/ppermute | solution.py:49
  36.7 3.6 %collective-permute-start.12 = (f32[2,512]{1,0:T(2,128)S(1)}, f32[2,512]{1,0:T(2,128)S(1)}, u32[]{:S(2)}, u32[]{:S(2)}) collective-permute-start(f32[2,512]{1,0:T(2,128)S(1)} %shard_map.74.refs_0_), channel_id=1, source_target_pairs={{16,0},{12,4},{24,8},{4,12},{0,16},{28,20},{8,24},{20,28},{17,1},{... | collective-permute-start | bytes 12296 | tf_op jit(solution)/shard_map/ppermute | solution.py:49
  37.2 4.5 %collective-permute-start.13 = (f32[2,512]{1,0:T(2,128)S(1)}, f32[2,512]{1,0:T(2,128)S(1)}, u32[]{:S(2)}, u32[]{:S(2)}) collective-permute-start(f32[2,512]{1,0:T(2,128)S(1)} %shard_map.74.refs_0_), channel_id=1, source_target_pairs={{24,0},{16,8},{8,16},{0,24},{25,1},{17,9},{9,17},{1,25},{26,2},{18... | collective-permute-start | bytes 12296 | tf_op jit(solution)/shard_map/ppermute | solution.py:49
  43.9 2.6 %collective-permute-start.14 = (bf16[768,512]{1,0:T(8,128)(2,1)S(1)}, bf16[768,512]{1,0:T(8,128)(2,1)S(1)}, u32[]{:S(2)}, u32[]{:S(2)}) collective-permute-start(bf16[768,512]{1,0:T(8,128)(2,1)S(1)} %get-tuple-element.34), channel_id=1, source_target_pairs={{4,0},{0,4},{5,1},{1,5},{6,2},{2,6},{7,3},{3,7},{12,8},{8,12},{13,... | collective-permute-start | bytes 2359304 | tf_op jit(solution)/shard_map/ppermute | solution.py:49
  44.0 2.5 %collective-permute-start.15 = (f32[1,768]{1,0:T(1,128)S(1)}, f32[1,768]{1,0:T(1,128)S(1)}, u32[]{:S(2)}, u32[]{:S(2)}) collective-permute-start(f32[1,768]{1,0:T(1,128)S(1)} %get-tuple-element.35), channel_id=1, source_target_pairs={{4,0},{0,4},{5,1},{1,5},{6,2},{2,6},{7,3},{3,7},{12,8},{8,12},{13,... | collective-permute-start | bytes 9224 | tf_op jit(solution)/shard_map/ppermute | solution.py:49

commit v16 on v15

--- a/solution.py
+++ b/solution.py
@@ -187,8 +187,8 @@
 def factor_kernel(rate, n, *refs):
     goals, tops, factors = refs[:4], refs[4 : 4 + n], refs[4 + n :]
     rows = goals[0].shape[1] // 2
-    spots = [(0, 0, 0), (0, 1, rows), (0, 2, 2 * rows), (0, 3, 3 * rows)]
-    spots += [(1, 0, 0), (1, 1, rows), (1, 2, 2 * rows), (2, 3, 0)]
+    spots = [(0, 0, 0), (0, 1, rows), (0, 2, 2 * rows), (1, 3, 0)]
+    spots += [(2, at, at * rows) for at in range(4)]
     for at, (bundle, goal, start) in enumerate(spots):
         group = at // 4
         mine, here = slice(group * rows, (group + 1) * rows), slice(start, start + rows)
@@ -343,19 +343,20 @@
     held_01 = hold(near_01, declared=2 * 10**9)
     first_01 = turn(near_01)
     stats = [totals_call(rate, block, (held_01,), centroids, inverse)]
-    second_01, across_01 = turn_back(hold(near_01, stats[0])), turn_back(hold(first_01, stats[0]))
+    second_01 = turn_back(hold(near_01, stats[0]))
     near_23 = join(near_2, near_3, *stats)
     stats.append(totals_call(rate, block, (near_23,), centroids, inverse, after=(first_01,)))
+    across_01 = turn_back(hold(first_01, stats[1]))
     first_23, second_23 = turn(near_23), turn_back(hold(near_23, stats[1]))
 
     expand = functools.partial(expo_call, rate, block, 2 * per_device)
     stat = beside(*stats)
-    bundles = [expand((near_01, first_01, second_01, across_01), centroids, stat, declared=0.01)]
+    bundles = [expand((near_01, first_01, second_01), centroids, stat, declared=0.01)]
     stat = merge_call(rate, 1, False, stat, along_z(stat, 1), bundles[0][1])
     across_23 = turn_back(hold(first_23, stat))
-    bundles.append(expand((near_23, first_23, second_23), centroids, stat, declared=0.01))
+    bundles.append(expand((across_01,), centroids, stat, declared=0.01))
     goal = merge_call(rate, 2, True, stat, along_z(stat, 2), bundles[1][1])
-    bundles.append(expand((across_23,), centroids))
+    bundles.append(expand((near_23, first_23, second_23, across_23), centroids, goal))
     expos, tops, points = zip(*bundles)
     goals = [goal, turn(goal), turn_back(goal), around(goal, 3)]
     factors = factor_call(rate, goals, tops)

time: 48.7 us -> 47.9 us (0.984)
  starting transfers between devices: 23.3 us -> 21.4 us
  Pallas kernels: 16.7 us -> 17.6 us
    ppermute x16, starting transfers between devices: 23.3 us -> 21.4 us  [exchange(): return lax.ppermute(a, axes, [(partner(at), at) for at in range(count)])]
  transfers between devices with their start and end apart: 16 -> 16, of which waited for: 6 -> 3; matrix products, arithmetic and copies ran while one was open for 0% -> 0% of each run, Pallas kernels for 26% -> 28%
where the time goes in v16:
time: 47.9 us; the launch traced here: 47.6 us
  starting transfers between devices  21.4 us (45%)
  Pallas kernels  17.6 us (37%)
  waiting for transfers between devices  5.17 us (11%)
  other arithmetic  1.69 us (4%)
  between operations  1.01 us (2%)
  local copies, waits for them, and re-layouts  0.75 us (2%)
    ppermute x16, starting transfers between devices, exchange(): return lax.ppermute(a, axes, [(partner(at), at) for at in range(count)])  21.4 us
    pallas_call x2, Pallas kernels, totals_call(): pl.pallas_call(functools.partial(totals_kernel, rate, block, len(pieces))...  5.74 us
    ppermute x16, waiting for transfers between devices, exchange(): return lax.ppermute(a, axes, [(partner(at), at) for at in range(count)])  5.17 us
    pallas_call x3, Pallas kernels, expo_call(): pl.pallas_call(functools.partial(expo_kernel, rate, block, len(pieces)),...  4.65 us
    pallas_call x2, Pallas kernels, sums_call(): pl.pallas_call(functools.partial(sums_kernel, n, block, side), in_specs=i...  4.31 us
    pallas_call x1, Pallas kernels, add_call(): pl.pallas_call(functools.partial(add_kernel, block), in_specs=in_vmem(4),...  1.8 us
    convert_element_type x1, other arithmetic, to_points(): return (codes.astype(jnp.float32) * scale[:, None]).astype(jnp.bfloat16)  1.03 us
  transfers between devices with their start and end apart: 16, of which 3 were waited for; matrix products, arithmetic and copies ran while one was open for 0% of the time, Pallas kernels for 28%

profile of v16, /device:TPU:0, one launch (start us, length us, event | category | flops | bytes accessed | tf_op | source)
XLA Modules:
  0.0 47.6 jit_solution(4587818465645960998)
XLA Ops:
  0.6 0.7 %convert_multiply_fusion = f32[128]{0:T(128)S(1)} fusion(s32[128]{0:T(128)} %param.5), kind=kLoop, calls=%fused_computation.1 | loop fusion | flops 512 | bytes 1024 | tf_op jit(solution)/shard_map/mul | solution.py:16
  1.3 1.0 %multiply_convert_fusion.above = bf16[128,512]{1,0:T(8,128)(2,1)S(1)} fusion(s32[128,512]{1,0:T(8,128)} %param.4, f32[128]{0:T(128)S(1)} %convert_multiply_fusion), kind=kLoop, calls=%fused_computation | loop fusion | flops 196608 | bytes 393728 | tf_op jit(solution)/shard_map/convert_element_type | solution.py:17
  2.3 3.1 %collective-permute-start = (bf16[128,512]{1,0:T(8,128)(2,1)S(1)}, bf16[128,512]{1,0:T(8,128)(2,1)S(1)}, u32[]{:S(2)}, u32[]{:S(2)}) collective-permute-start(bf16[128,512]{1,0:T(8,128)(2,1)S(1)} %multiply_convert_fusion.above), channel_id=1, source_target_pairs={{1,0},{0,1},{3,2},{2,3},{5,4},{4,5},{7,6},{6,7},{9,8},{8,9},{11,10... | collective-permute-start | bytes 393224 | tf_op jit(solution)/shard_map/ppermute | solution.py:49
  5.4 2.6 %collective-permute-start.3 = (bf16[128,512]{1,0:T(8,128)(2,1)S(1)}, bf16[128,512]{1,0:T(8,128)(2,1)S(1)}, u32[]{:S(2)}, u32[]{:S(2)}) collective-permute-start(bf16[128,512]{1,0:T(8,128)(2,1)S(1)} %multiply_convert_fusion.above), channel_id=1, source_target_pairs={{2,0},{3,1},{0,2},{1,3},{6,4},{7,5},{4,6},{5,7},{10,8},{11,9},{8,1... | collective-permute-start | bytes 393224 | tf_op jit(solution)/shard_map/ppermute | solution.py:49
  8.0 0.0 collective-permute-start.4
  8.0 0.0 copy-start
  8.0 0.7 %copy-done = s32[6144]{0:T(1024)S(1)} copy-done((s32[6144]{0:T(1024)S(1)}, s32[6144]{0:T(1024)}, u32[]{:S(2)}) %copy-start) | copy-done | bytes 24600
  8.8 0.0 slice-start
  8.8 0.9 %shard_map.59.refs_0_.refs_2_ = f32[6144,128]{1,0:T(8,128)S(1)} custom-call(s32[48,128]{1,0:T(8,128)S(1)} %bitcast.4), custom_call_target="tpu_custom_call" | custom-call | flops 2000000000 | tf_op jit(solution)/shard_map/pallas_call | solution.py:114
  9.6 0.0 slice-start.1
  9.7 0.8 %collective-permute-done.below = bf16[128,512]{1,0:T(8,128)(2,1)S(1)} collective-permute-done((bf16[128,512]{1,0:T(8,128)(2,1)S(1)}, bf16[128,512]{1,0:T(8,128)(2,1)S(1)}, u32[]{:S(2)}, u32[]{:S(2)}) %collective-permute-start) | collective-permute-done | bytes 131104 | tf_op jit(solution)/shard_map/ppermute | solution.py:49
  10.5 1.8 %collective-permute-start.1 = (bf16[256,512]{1,0:T(8,128)(2,1)S(1)}, bf16[256,512]{1,0:T(8,128)(2,1)S(1)}, u32[]{:S(2)}, u32[]{:S(2)}) collective-permute-start(bf16[256,512]{1,0:T(8,128)(2,1)S(1)} %shard_map.60.a.refs_0_), channel_id=1, source_target_pairs={{8,0},{20,4},{0,8},{28,12},{24,16},{4,20},{16,24},{12,28},{9,1},{2... | collective-permute-start | bytes 786440 | tf_op jit(solution)/shard_map/ppermute | solution.py:49
  12.3 0.0 slice-done
  12.3 0.0 slice-done.1
  12.3 2.9 %shard_map.62.refs_0_.left = f32[3,256]{1,0:T(4,128)S(1)} custom-call(bf16[256,512]{1,0:T(8,128)(2,1)S(1)} %shard_map.61.refs_0_, bf16[6144,512]{1,0:T(8,128)(2,1)S(1)} %bitcast.3, f32[6144,128]{1,0:T(8,128)S(1)} %shard_map.59.refs_0_.refs_2_), custom_call_target="tpu_custom_call" | custom-call | flops 1610612736 | bytes 6291456 | tf_op jit(solution)/shard_map/pallas_call | solution.py:154
  15.2 1.6 %collective-permute-start.2 = (bf16[256,512]{1,0:T(8,128)(2,1)S(1)}, bf16[256,512]{1,0:T(8,128)(2,1)S(1)}, u32[]{:S(2)}, u32[]{:S(2)}) collective-permute-start(bf16[256,512]{1,0:T(8,128)(2,1)S(1)} %shard_map.63), channel_id=1, source_target_pairs={{16,0},{12,4},{24,8},{4,12},{0,16},{28,20},{8,24},{20,28},{17,1},{... | collective-permute-start | bytes 786440 | tf_op jit(solution)/shard_map/ppermute | solution.py:49
  16.8 1.6 %collective-permute-done.3.above = bf16[128,512]{1,0:T(8,128)(2,1)S(1)} collective-permute-done((bf16[128,512]{1,0:T(8,128)(2,1)S(1)}, bf16[128,512]{1,0:T(8,128)(2,1)S(1)}, u32[]{:S(2)}, u32[]{:S(2)}) %collective-permute-start.3) | collective-permute-done | bytes 131104 | tf_op jit(solution)/shard_map/ppermute | solution.py:49
  18.3 0.0 collective-permute-done.4.below
  18.4 1.6 %collective-permute-start.7 = (bf16[256,512]{1,0:T(8,128)(2,1)S(1)}, bf16[256,512]{1,0:T(8,128)(2,1)S(1)}, u32[]{:S(2)}, u32[]{:S(2)}) collective-permute-start(bf16[256,512]{1,0:T(8,128)(2,1)S(1)} %shard_map.64.refs_0_.a), channel_id=1, source_target_pairs={{8,0},{20,4},{0,8},{28,12},{24,16},{4,20},{16,24},{12,28},{9,1},{2... | collective-permute-start | bytes 786440 | tf_op jit(solution)/shard_map/ppermute | solution.py:49
  19.9 0.0 collective-permute-done.1.refs_3_.refs_1_.a
  19.9 2.9 %shard_map.65.right.refs_0_ = f32[3,256]{1,0:T(4,128)S(1)} custom-call(bf16[256,512]{1,0:T(8,128)(2,1)S(1)} %shard_map.64.refs_0_.a, bf16[6144,512]{1,0:T(8,128)(2,1)S(1)} %bitcast.3, f32[6144,128]{1,0:T(8,128)S(1)} %shard_map.59.refs_0_.refs_2_, bf16[256,512]{1,0:T(8,128)(2,1)S(1)} %collective-permute-done.1.refs_3_.refs_1_.a), custom_call_target="tpu_custom_call" | custom-call | flops 1610612736 | bytes 6291456 | tf_op jit(solution)/shard_map/pallas_call | solution.py:154
  22.8 2.0 %collective-permute-start.6 = (f32[3,512]{1,0:T(4,128)S(1)}, f32[3,512]{1,0:T(4,128)S(1)}, u32[]{:S(2)}, u32[]{:S(2)}) collective-permute-start(f32[3,512]{1,0:T(4,128)S(1)} %shard_map.66.refs_4_.mine), channel_id=1, source_target_pairs={{1,0},{0,1},{3,2},{2,3},{5,4},{4,5},{7,6},{6,7},{9,8},{8,9},{11,10... | collective-permute-start | bytes 18440 | tf_op jit(solution)/shard_map/ppermute | solution.py:49
  24.9 1.6 %collective-permute-start.5 = (bf16[256,512]{1,0:T(8,128)(2,1)S(1)}, bf16[256,512]{1,0:T(8,128)(2,1)S(1)}, u32[]{:S(2)}, u32[]{:S(2)}) collective-permute-start(bf16[256,512]{1,0:T(8,128)(2,1)S(1)} %shard_map.68), channel_id=1, source_target_pairs={{16,0},{12,4},{24,8},{4,12},{0,16},{28,20},{8,24},{20,28},{17,1},{... | collective-permute-start | bytes 786440 | tf_op jit(solution)/shard_map/ppermute | solution.py:49
  26.5 0.5 %collective-permute-start.8 = (bf16[256,512]{1,0:T(8,128)(2,1)S(1)}, bf16[256,512]{1,0:T(8,128)(2,1)S(1)}, u32[]{:S(2)}, u32[]{:S(2)}) collective-permute-start(bf16[256,512]{1,0:T(8,128)(2,1)S(1)} %shard_map.71), channel_id=1, source_target_pairs={{16,0},{12,4},{24,8},{4,12},{0,16},{28,20},{8,24},{20,28},{17,1},{... | collective-permute-start | bytes 786440 | tf_op jit(solution)/shard_map/ppermute | solution.py:49
  27.0 0.0 collective-permute-done.2.refs_2_
  27.0 1.7 %shard_map.67 = (bf16[1536,768]{1,0:T(8,128)(2,1)S(1)}, f32[6,768]{1,0:T(8,128)S(1)}, bf16[768,512]{1,0:T(8,128)(2,1)S(1)}) custom-call(bf16[256,512]{1,0:T(8,128)(2,1)S(1)} %shard_map.60.a.refs_0_, bf16[256,512]{1,0:T(8,128)(2,1)S(1)} %collective-permute-done.1.refs_3_.refs_1_.a, bf16[256,512]{1,0:T(8,128)(2,1)S(1)} %collective-permute-done.2.refs_2_, ...), custom_call_target="tpu_custom_call" | custom-call | flops 12079595 | bytes 47185 | tf_op jit(solution)/shard_map/pallas_call | solution.py:230
  28.7 0.0 collective-permute-done.6.theirs
  28.7 0.0 collective-permute-done.7.a.refs_1_
  28.7 1.6 %collective-permute-start.9 = (bf16[256,512]{1,0:T(8,128)(2,1)S(1)}, bf16[256,512]{1,0:T(8,128)(2,1)S(1)}, u32[]{:S(2)}, u32[]{:S(2)}) collective-permute-start(bf16[256,512]{1,0:T(8,128)(2,1)S(1)} %shard_map.72), channel_id=1, source_target_pairs={{16,0},{12,4},{24,8},{4,12},{0,16},{28,20},{8,24},{20,28},{17,1},{... | collective-permute-start | bytes 786440 | tf_op jit(solution)/shard_map/ppermute | solution.py:49
  30.3 1.0 %collective-permute-start.10 = (f32[3,512]{1,0:T(4,128)S(1)}, f32[3,512]{1,0:T(4,128)S(1)}, u32[]{:S(2)}, u32[]{:S(2)}) collective-permute-start(f32[3,512]{1,0:T(4,128)S(1)} %shard_map.69.refs_2_.refs_0_.mine), channel_id=1, source_target_pairs={{2,0},{3,1},{0,2},{1,3},{6,4},{7,5},{4,6},{5,7},{10,8},{11,9},{8,1... | collective-permute-start | bytes 18440 | tf_op jit(solution)/shard_map/ppermute | solution.py:49
  31.4 0.0 collective-permute-done.5.refs_0_
  31.4 0.7 %shard_map.70 = (bf16[1536,256]{1,0:T(8,128)(2,1)S(1)}, f32[6,256]{1,0:T(8,128)S(1)}, bf16[256,512]{1,0:T(8,128)(2,1)S(1)}) custom-call(bf16[256,512]{1,0:T(8,128)(2,1)S(1)} %collective-permute-done.5.refs_0_, bf16[6144,512]{1,0:T(8,128)(2,1)S(1)} %bitcast.3, f32[3,512]{1,0:T(4,128)S(1)} %shard_map.69.refs_2_.refs_0_.mine), custom_call_target="tpu_custom_call" | custom-call | flops 4026531 | bytes 26214 | tf_op jit(solution)/shard_map/pallas_call | solution.py:230
  32.1 2.8 %collective-permute-done.10.theirs = f32[3,512]{1,0:T(4,128)S(1)} collective-permute-done((f32[3,512]{1,0:T(4,128)S(1)}, f32[3,512]{1,0:T(4,128)S(1)}, u32[]{:S(2)}, u32[]{:S(2)}) %collective-permute-start.10) | collective-permute-done | bytes 6176 | tf_op jit(solution)/shard_map/ppermute | solution.py:49
  34.9 0.6 %collective-permute-start.11 = (f32[2,512]{1,0:T(2,128)S(1)}, f32[2,512]{1,0:T(2,128)S(1)}, u32[]{:S(2)}, u32[]{:S(2)}) collective-permute-start(f32[2,512]{1,0:T(2,128)S(1)} %shard_map.73.refs_5_.refs_0_), channel_id=1, source_target_pairs={{8,0},{20,4},{0,8},{28,12},{24,16},{4,20},{16,24},{12,28},{9,1},{2... | collective-permute-start | bytes 12296 | tf_op jit(solution)/shard_map/ppermute | solution.py:49
  35.5 0.5 %collective-permute-start.12 = (f32[2,512]{1,0:T(2,128)S(1)}, f32[2,512]{1,0:T(2,128)S(1)}, u32[]{:S(2)}, u32[]{:S(2)}) collective-permute-start(f32[2,512]{1,0:T(2,128)S(1)} %shard_map.73.refs_5_.refs_0_), channel_id=1, source_target_pairs={{16,0},{12,4},{24,8},{4,12},{0,16},{28,20},{8,24},{20,28},{17,1},{... | collective-permute-start | bytes 12296 | tf_op jit(solution)/shard_map/ppermute | solution.py:49
  36.0 2.4 %collective-permute-start.13 = (f32[2,512]{1,0:T(2,128)S(1)}, f32[2,512]{1,0:T(2,128)S(1)}, u32[]{:S(2)}, u32[]{:S(2)}) collective-permute-start(f32[2,512]{1,0:T(2,128)S(1)} %shard_map.73.refs_5_.refs_0_), channel_id=1, source_target_pairs={{24,0},{16,8},{8,16},{0,24},{25,1},{17,9},{9,17},{1,25},{26,2},{18... | collective-permute-start | bytes 12296 | tf_op jit(solution)/shard_map/ppermute | solution.py:49
  38.5 0.0 collective-permute-done.8.refs_2_
  38.5 0.0 collective-permute-done.9.refs_3_
  38.5 2.2 %shard_map.74 = (bf16[1536,1024]{1,0:T(8,128)(2,1)S(1)}, f32[6,1024]{1,0:T(8,128)S(1)}, bf16[1024,512]{1,0:T(8,128)(2,1)S(1)}) custom-call(bf16[256,512]{1,0:T(8,128)(2,1)S(1)} %shard_map.64.refs_0_.a, bf16[256,512]{1,0:T(8,128)(2,1)S(1)} %collective-permute-done.7.a.refs_1_, bf16[256,512]{1,0:T(8,128)(2,1)S(1)} %collective-permute-done.8.refs_2_, ...), custom_call_target="tpu_custom_call" | custom-call | flops 1610612736 | bytes 5767168 | tf_op jit(solution)/shard_map/pallas_call | solution.py:230
  40.7 0.0 collective-permute-done.11.refs_1_
  40.7 0.0 collective-permute-done.12.refs_2_
  40.7 0.0 collective-permute-done.13.refs_3_
  40.8 2.3 %shard_map.77 = (bf16[768,512]{1,0:T(8,128)(2,1)S(1)}, f32[1,768]{1,0:T(1,128)S(1)}) custom-call(bf16[1536,768]{1,0:T(8,128)(2,1)S(1)} %get-tuple-element.20.refs_0_, bf16[1536,256]{1,0:T(8,128)(2,1)S(1)} %get-tuple-element.22.refs_1_, bf16[1536,1024]{1,0:T(8,128)(2,1)S(1)} %get-tuple-element.24.refs_2_, bf16[768,512]{1,0:T(8,128)(2,1)S(1)} %get-tuple-element.25.refs_3_, ...), custom_call_target="tpu_custom_call" | custom-call | flops 1811939328 | bytes 7471104 | tf_op jit(solution)/shard_map/pallas_call | solution.py:281
  43.0 0.1 collective-permute-start.14
  43.1 0.5 %collective-permute-start.15 = (f32[1,768]{1,0:T(1,128)S(1)}, f32[1,768]{1,0:T(1,128)S(1)}, u32[]{:S(2)}, u32[]{:S(2)}) collective-permute-start(f32[1,768]{1,0:T(1,128)S(1)} %get-tuple-element.35), channel_id=1, source_target_pairs={{4,0},{0,4},{5,1},{1,5},{6,2},{2,6},{7,3},{3,7},{12,8},{8,12},{13,... | collective-permute-start | bytes 9224 | tf_op jit(solution)/shard_map/ppermute | solution.py:49
  43.6 2.0 %shard_map.76 = (f32[768,512]{1,0:T(8,128)S(1)}, f32[1,768]{1,0:T(1,128)S(1)}) custom-call(bf16[1536,768]{1,0:T(8,128)(2,1)S(1)} %get-tuple-element.20.refs_0_, bf16[1536,256]{1,0:T(8,128)(2,1)S(1)} %get-tuple-element.22.refs_1_, bf16[1536,1024]{1,0:T(8,128)(2,1)S(1)} %get-tuple-element.24.refs_2_, bf16[768,512]{1,0:T(8,128)(2,1)S(1)} %get-tuple-element.25.refs_3_, ...), custom_call_target="tpu_custom_call" | custom-call | flops 1811939328 | bytes 7471104 | tf_op jit(solution)/shard_map/pallas_call | solution.py:281
  45.7 0.0 collective-permute-done.15.there_mass
  45.7 0.0 collective-permute-done.14.there
  45.7 1.8 %shard_map.78 = (f32[768,512]{1,0:T(8,128)}, f32[1,768]{1,0:T(1,128)}) custom-call(f32[768,512]{1,0:T(8,128)S(1)} %get-tuple-element.32.here, f32[1,768]{1,0:T(1,128)S(1)} %get-tuple-element.33.here_mass, bf16[768,512]{1,0:T(8,128)(2,1)S(1)} %collective-permute-done.14.there, f32[1,768]{1,0:T(1,128)S(1)} %collective-permute-done.15.there_mass), custom_call_target="tpu_custom_call" | custom-call | tf_op jit(solution)/shard_map/pallas_call | solution.py:311
  (12 shorter events, 0.2 us)
Async XLA Ops:
  2.3 8.1 %collective-permute-start = (bf16[128,512]{1,0:T(8,128)(2,1)S(1)}, bf16[128,512]{1,0:T(8,128)(2,1)S(1)}, u32[]{:S(2)}, u32[]{:S(2)}) collective-permute-start(bf16[128,512]{1,0:T(8,128)(2,1)S(1)} %multiply_convert_fusion.above), channel_id=1, source_target_pairs={{1,0},{0,1},{3,2},{2,3},{5,4},{4,5},{7,6},{6,7},{9,8},{8,9},{11,10... | collective-permute-start | bytes 393224 | tf_op jit(solution)/shard_map/ppermute | solution.py:49
  5.4 12.9 %collective-permute-start.3 = (bf16[128,512]{1,0:T(8,128)(2,1)S(1)}, bf16[128,512]{1,0:T(8,128)(2,1)S(1)}, u32[]{:S(2)}, u32[]{:S(2)}) collective-permute-start(bf16[128,512]{1,0:T(8,128)(2,1)S(1)} %multiply_convert_fusion.above), channel_id=1, source_target_pairs={{2,0},{3,1},{0,2},{1,3},{6,4},{7,5},{4,6},{5,7},{10,8},{11,9},{8,1... | collective-permute-start | bytes 393224 | tf_op jit(solution)/shard_map/ppermute | solution.py:49
  8.0 10.3 %collective-permute-start.4 = (bf16[128,512]{1,0:T(8,128)(2,1)S(1)}, bf16[128,512]{1,0:T(8,128)(2,1)S(1)}, u32[]{:S(2)}, u32[]{:S(2)}) collective-permute-start(bf16[128,512]{1,0:T(8,128)(2,1)S(1)} %multiply_convert_fusion.above), channel_id=1, source_target_pairs={{3,0},{2,1},{1,2},{0,3},{7,4},{6,5},{5,6},{4,7},{11,8},{10,9},{9,1... | collective-permute-start | bytes 393224 | tf_op jit(solution)/shard_map/ppermute | solution.py:49
  8.0 0.7 %copy-start = (s32[6144]{0:T(1024)S(1)}, s32[6144]{0:T(1024)}, u32[]{:S(2)}) copy-start(s32[6144]{0:T(1024)} %param.7) | copy-start | bytes 73732
  8.8 3.5 %slice-start = ((s8[6291456]{0:T(1024)(128)(4,1)}), s8[4194304]{0:T(1024)(128)(4,1)S(1)}, s32[]{:S(2)}) async-start(s8[6291456]{0:T(1024)(128)(4,1)} %bitcast.2), calls=%async_computation | async-start | bytes 8388608
  9.6 2.6 %slice-start.1 = ((s8[6291456]{0:T(1024)(128)(4,1)}), s8[2097152]{0:T(1024)(128)(4,1)S(1)}, s32[]{:S(2)}) async-start(s8[6291456]{0:T(1024)(128)(4,1)} %bitcast.2), calls=%async_computation.1 | async-start | bytes 4194304
  10.5 9.5 %collective-permute-start.1 = (bf16[256,512]{1,0:T(8,128)(2,1)S(1)}, bf16[256,512]{1,0:T(8,128)(2,1)S(1)}, u32[]{:S(2)}, u32[]{:S(2)}) collective-permute-start(bf16[256,512]{1,0:T(8,128)(2,1)S(1)} %shard_map.60.a.refs_0_), channel_id=1, source_target_pairs={{8,0},{20,4},{0,8},{28,12},{24,16},{4,20},{16,24},{12,28},{9,1},{2... | collective-permute-start | bytes 786440 | tf_op jit(solution)/shard_map/ppermute | solution.py:49
  15.2 11.8 %collective-permute-start.2 = (bf16[256,512]{1,0:T(8,128)(2,1)S(1)}, bf16[256,512]{1,0:T(8,128)(2,1)S(1)}, u32[]{:S(2)}, u32[]{:S(2)}) collective-permute-start(bf16[256,512]{1,0:T(8,128)(2,1)S(1)} %shard_map.63), channel_id=1, source_target_pairs={{16,0},{12,4},{24,8},{4,12},{0,16},{28,20},{8,24},{20,28},{17,1},{... | collective-permute-start | bytes 786440 | tf_op jit(solution)/shard_map/ppermute | solution.py:49
  18.4 10.3 %collective-permute-start.7 = (bf16[256,512]{1,0:T(8,128)(2,1)S(1)}, bf16[256,512]{1,0:T(8,128)(2,1)S(1)}, u32[]{:S(2)}, u32[]{:S(2)}) collective-permute-start(bf16[256,512]{1,0:T(8,128)(2,1)S(1)} %shard_map.64.refs_0_.a), channel_id=1, source_target_pairs={{8,0},{20,4},{0,8},{28,12},{24,16},{4,20},{16,24},{12,28},{9,1},{2... | collective-permute-start | bytes 786440 | tf_op jit(solution)/shard_map/ppermute | solution.py:49
  22.8 5.9 %collective-permute-start.6 = (f32[3,512]{1,0:T(4,128)S(1)}, f32[3,512]{1,0:T(4,128)S(1)}, u32[]{:S(2)}, u32[]{:S(2)}) collective-permute-start(f32[3,512]{1,0:T(4,128)S(1)} %shard_map.66.refs_4_.mine), channel_id=1, source_target_pairs={{1,0},{0,1},{3,2},{2,3},{5,4},{4,5},{7,6},{6,7},{9,8},{8,9},{11,10... | collective-permute-start | bytes 18440 | tf_op jit(solution)/shard_map/ppermute | solution.py:49
  24.9 6.5 %collective-permute-start.5 = (bf16[256,512]{1,0:T(8,128)(2,1)S(1)}, bf16[256,512]{1,0:T(8,128)(2,1)S(1)}, u32[]{:S(2)}, u32[]{:S(2)}) collective-permute-start(bf16[256,512]{1,0:T(8,128)(2,1)S(1)} %shard_map.68), channel_id=1, source_target_pairs={{16,0},{12,4},{24,8},{4,12},{0,16},{28,20},{8,24},{20,28},{17,1},{... | collective-permute-start | bytes 786440 | tf_op jit(solution)/shard_map/ppermute | solution.py:49
  26.5 12.0 %collective-permute-start.8 = (bf16[256,512]{1,0:T(8,128)(2,1)S(1)}, bf16[256,512]{1,0:T(8,128)(2,1)S(1)}, u32[]{:S(2)}, u32[]{:S(2)}) collective-permute-start(bf16[256,512]{1,0:T(8,128)(2,1)S(1)} %shard_map.71), channel_id=1, source_target_pairs={{16,0},{12,4},{24,8},{4,12},{0,16},{28,20},{8,24},{20,28},{17,1},{... | collective-permute-start | bytes 786440 | tf_op jit(solution)/shard_map/ppermute | solution.py:49
  28.7 9.7 %collective-permute-start.9 = (bf16[256,512]{1,0:T(8,128)(2,1)S(1)}, bf16[256,512]{1,0:T(8,128)(2,1)S(1)}, u32[]{:S(2)}, u32[]{:S(2)}) collective-permute-start(bf16[256,512]{1,0:T(8,128)(2,1)S(1)} %shard_map.72), channel_id=1, source_target_pairs={{16,0},{12,4},{24,8},{4,12},{0,16},{28,20},{8,24},{20,28},{17,1},{... | collective-permute-start | bytes 786440 | tf_op jit(solution)/shard_map/ppermute | solution.py:49
  30.3 4.5 %collective-permute-start.10 = (f32[3,512]{1,0:T(4,128)S(1)}, f32[3,512]{1,0:T(4,128)S(1)}, u32[]{:S(2)}, u32[]{:S(2)}) collective-permute-start(f32[3,512]{1,0:T(4,128)S(1)} %shard_map.69.refs_2_.refs_0_.mine), channel_id=1, source_target_pairs={{2,0},{3,1},{0,2},{1,3},{6,4},{7,5},{4,6},{5,7},{10,8},{11,9},{8,1... | collective-permute-start | bytes 18440 | tf_op jit(solution)/shard_map/ppermute | solution.py:49
  34.9 5.8 %collective-permute-start.11 = (f32[2,512]{1,0:T(2,128)S(1)}, f32[2,512]{1,0:T(2,128)S(1)}, u32[]{:S(2)}, u32[]{:S(2)}) collective-permute-start(f32[2,512]{1,0:T(2,128)S(1)} %shard_map.73.refs_5_.refs_0_), channel_id=1, source_target_pairs={{8,0},{20,4},{0,8},{28,12},{24,16},{4,20},{16,24},{12,28},{9,1},{2... | collective-permute-start | bytes 12296 | tf_op jit(solution)/shard_map/ppermute | solution.py:49
  35.5 5.2 %collective-permute-start.12 = (f32[2,512]{1,0:T(2,128)S(1)}, f32[2,512]{1,0:T(2,128)S(1)}, u32[]{:S(2)}, u32[]{:S(2)}) collective-permute-start(f32[2,512]{1,0:T(2,128)S(1)} %shard_map.73.refs_5_.refs_0_), channel_id=1, source_target_pairs={{16,0},{12,4},{24,8},{4,12},{0,16},{28,20},{8,24},{20,28},{17,1},{... | collective-permute-start | bytes 12296 | tf_op jit(solution)/shard_map/ppermute | solution.py:49
  36.0 4.7 %collective-permute-start.13 = (f32[2,512]{1,0:T(2,128)S(1)}, f32[2,512]{1,0:T(2,128)S(1)}, u32[]{:S(2)}, u32[]{:S(2)}) collective-permute-start(f32[2,512]{1,0:T(2,128)S(1)} %shard_map.73.refs_5_.refs_0_), channel_id=1, source_target_pairs={{24,0},{16,8},{8,16},{0,24},{25,1},{17,9},{9,17},{1,25},{26,2},{18... | collective-permute-start | bytes 12296 | tf_op jit(solution)/shard_map/ppermute | solution.py:49
  43.0 2.6 %collective-permute-start.14 = (bf16[768,512]{1,0:T(8,128)(2,1)S(1)}, bf16[768,512]{1,0:T(8,128)(2,1)S(1)}, u32[]{:S(2)}, u32[]{:S(2)}) collective-permute-start(bf16[768,512]{1,0:T(8,128)(2,1)S(1)} %get-tuple-element.34), channel_id=1, source_target_pairs={{4,0},{0,4},{5,1},{1,5},{6,2},{2,6},{7,3},{3,7},{12,8},{8,12},{13,... | collective-permute-start | bytes 2359304 | tf_op jit(solution)/shard_map/ppermute | solution.py:49
  43.1 2.5 %collective-permute-start.15 = (f32[1,768]{1,0:T(1,128)S(1)}, f32[1,768]{1,0:T(1,128)S(1)}, u32[]{:S(2)}, u32[]{:S(2)}) collective-permute-start(f32[1,768]{1,0:T(1,128)S(1)} %get-tuple-element.35), channel_id=1, source_target_pairs={{4,0},{0,4},{5,1},{1,5},{6,2},{2,6},{7,3},{3,7},{12,8},{8,12},{13,... | collective-permute-start | bytes 9224 | tf_op jit(solution)/shard_map/ppermute | solution.py:49

commit v17 on v16

--- a/solution.py
+++ b/solution.py
@@ -13,8 +13,8 @@
 
 
 def to_points(codes, exponents):
-    scale = lax.shift_left(jnp.ones_like(exponents), 16 - exponents).astype(jnp.float32) * 2.0**-16
-    return (codes.astype(jnp.float32) * scale[:, None]).astype(jnp.bfloat16)
+    scaled = lax.shift_right_arithmetic(codes << 16, jnp.broadcast_to(exponents[:, None], codes.shape))
+    return (scaled.astype(jnp.float32) * 2.0**-16).astype(jnp.bfloat16)
 
 
 def split_points(codes, exponents, centroids, counters):
@@ -350,12 +350,11 @@
     first_23, second_23 = turn(near_23), turn_back(hold(near_23, stats[1]))
 
     expand = functools.partial(expo_call, rate, block, 2 * per_device)
-    stat = beside(*stats)
-    bundles = [expand((near_01, first_01, second_01), centroids, stat, declared=0.01)]
-    stat = merge_call(rate, 1, False, stat, along_z(stat, 1), bundles[0][1])
+    stat = beside(*stats, second_01)
+    stat = merge_call(rate, 1, False, stat, along_z(stat, 1))
     across_23 = turn_back(hold(first_23, stat))
-    bundles.append(expand((across_01,), centroids, stat, declared=0.01))
-    goal = merge_call(rate, 2, True, stat, along_z(stat, 2), bundles[1][1])
+    bundles = [expand(pieces, centroids, stat, declared=0.01) for pieces in ((near_01, first_01, second_01), (across_01,))]
+    goal = merge_call(rate, 2, True, stat, along_z(stat, 2), *(tops for _, tops, _ in bundles))
     bundles.append(expand((near_23, first_23, second_23, across_23), centroids, goal))
     expos, tops, points = zip(*bundles)
     goals = [goal, turn(goal), turn_back(goal), around(goal, 3)]

time: 47.9 us -> 46.9 us (0.979)
  other arithmetic: 1.69 us -> 1.05 us
    mul x1 -> x0, other arithmetic: 0.66 us -> none  [to_points(): lax.shift_left(jnp.ones_like(exponents), 16 - exponents).astype(jnp.float32)]
  transfers between devices with their start and end apart: 16 -> 16, of which waited for: 3 -> 5; matrix products, arithmetic and copies ran while one was open for 0% -> 0% of each run, Pallas kernels for 28% -> 29%
where the time goes in v17:
time: 46.9 us; the launch traced here: 46.7 us
  starting transfers between devices  21.5 us (46%)
  Pallas kernels  17.5 us (37%)
  waiting for transfers between devices  4.94 us (11%)
  other arithmetic  1.05 us (2%)
  between operations  0.97 us (2%)
  local copies, waits for them, and re-layouts  0.75 us (2%)
    ppermute x16, starting transfers between devices, exchange(): return lax.ppermute(a, axes, [(partner(at), at) for at in range(count)])  21.5 us
    pallas_call x2, Pallas kernels, totals_call(): pl.pallas_call(functools.partial(totals_kernel, rate, block, len(pieces))...  5.73 us
    ppermute x16, waiting for transfers between devices, exchange(): return lax.ppermute(a, axes, [(partner(at), at) for at in range(count)])  4.94 us
    pallas_call x3, Pallas kernels, expo_call(): pl.pallas_call(functools.partial(expo_kernel, rate, block, len(pieces)),...  4.62 us
    pallas_call x2, Pallas kernels, sums_call(): pl.pallas_call(functools.partial(sums_kernel, n, block, side), in_specs=i...  4.29 us
    pallas_call x1, Pallas kernels, add_call(): pl.pallas_call(functools.partial(add_kernel, block), in_specs=in_vmem(4),...  1.8 us
    convert_element_type x1, other arithmetic, to_points(): return (scaled.astype(jnp.float32) * 2.0 ** (-16)).astype(jnp.bfloat16)  1.05 us
  transfers between devices with their start and end apart: 16, of which 5 were waited for; matrix products, arithmetic and copies ran while one was open for 0% of the time, Pallas kernels for 29%

profile of v17, /device:TPU:0, one launch (start us, length us, event | category | flops | bytes accessed | tf_op | source)
XLA Modules:
  0.0 46.7 jit_solution(9718003153248106660)
XLA Ops:
  0.6 1.1 %multiply_convert_fusion.above = bf16[128,512]{1,0:T(8,128)(2,1)S(1)} fusion(s32[128,512]{1,0:T(8,128)} %param.4, s32[128]{0:T(128)} %param.5), kind=kLoop, calls=%fused_computation | loop fusion | flops 327680 | bytes 393728 | tf_op jit(solution)/shard_map/convert_element_type | solution.py:17
  1.7 3.1 %collective-permute-start = (bf16[128,512]{1,0:T(8,128)(2,1)S(1)}, bf16[128,512]{1,0:T(8,128)(2,1)S(1)}, u32[]{:S(2)}, u32[]{:S(2)}) collective-permute-start(bf16[128,512]{1,0:T(8,128)(2,1)S(1)} %multiply_convert_fusion.above), channel_id=1, source_target_pairs={{1,0},{0,1},{3,2},{2,3},{5,4},{4,5},{7,6},{6,7},{9,8},{8,9},{11,10... | collective-permute-start | bytes 393224 | tf_op jit(solution)/shard_map/ppermute | solution.py:49
  4.8 2.6 %collective-permute-start.3 = (bf16[128,512]{1,0:T(8,128)(2,1)S(1)}, bf16[128,512]{1,0:T(8,128)(2,1)S(1)}, u32[]{:S(2)}, u32[]{:S(2)}) collective-permute-start(bf16[128,512]{1,0:T(8,128)(2,1)S(1)} %multiply_convert_fusion.above), channel_id=1, source_target_pairs={{2,0},{3,1},{0,2},{1,3},{6,4},{7,5},{4,6},{5,7},{10,8},{11,9},{8,1... | collective-permute-start | bytes 393224 | tf_op jit(solution)/shard_map/ppermute | solution.py:49
  7.4 0.0 collective-permute-start.4
  7.4 0.0 copy-start
  7.4 0.7 %copy-done = s32[6144]{0:T(1024)S(1)} copy-done((s32[6144]{0:T(1024)S(1)}, s32[6144]{0:T(1024)}, u32[]{:S(2)}) %copy-start) | copy-done | bytes 24600
  8.1 0.0 slice-start
  8.1 0.9 %shard_map.59.refs_0_.refs_2_ = f32[6144,128]{1,0:T(8,128)S(1)} custom-call(s32[48,128]{1,0:T(8,128)S(1)} %bitcast.4), custom_call_target="tpu_custom_call" | custom-call | flops 2000000000 | tf_op jit(solution)/shard_map/pallas_call | solution.py:114
  9.0 0.0 slice-start.1
  9.0 0.8 %collective-permute-done.below = bf16[128,512]{1,0:T(8,128)(2,1)S(1)} collective-permute-done((bf16[128,512]{1,0:T(8,128)(2,1)S(1)}, bf16[128,512]{1,0:T(8,128)(2,1)S(1)}, u32[]{:S(2)}, u32[]{:S(2)}) %collective-permute-start) | collective-permute-done | bytes 131104 | tf_op jit(solution)/shard_map/ppermute | solution.py:49
  9.9 1.8 %collective-permute-start.1 = (bf16[256,512]{1,0:T(8,128)(2,1)S(1)}, bf16[256,512]{1,0:T(8,128)(2,1)S(1)}, u32[]{:S(2)}, u32[]{:S(2)}) collective-permute-start(bf16[256,512]{1,0:T(8,128)(2,1)S(1)} %shard_map.60.a.refs_0_), channel_id=1, source_target_pairs={{8,0},{20,4},{0,8},{28,12},{24,16},{4,20},{16,24},{12,28},{9,1},{2... | collective-permute-start | bytes 786440 | tf_op jit(solution)/shard_map/ppermute | solution.py:49
  11.6 0.0 slice-done
  11.6 0.0 slice-done.1
  11.6 2.9 %shard_map.62.refs_0_.left = f32[3,256]{1,0:T(4,128)S(1)} custom-call(bf16[256,512]{1,0:T(8,128)(2,1)S(1)} %shard_map.61.refs_0_, bf16[6144,512]{1,0:T(8,128)(2,1)S(1)} %bitcast.3, f32[6144,128]{1,0:T(8,128)S(1)} %shard_map.59.refs_0_.refs_2_), custom_call_target="tpu_custom_call" | custom-call | flops 1610612736 | bytes 6291456 | tf_op jit(solution)/shard_map/pallas_call | solution.py:154
  14.5 1.6 %collective-permute-start.2 = (bf16[256,512]{1,0:T(8,128)(2,1)S(1)}, bf16[256,512]{1,0:T(8,128)(2,1)S(1)}, u32[]{:S(2)}, u32[]{:S(2)}) collective-permute-start(bf16[256,512]{1,0:T(8,128)(2,1)S(1)} %shard_map.63), channel_id=1, source_target_pairs={{16,0},{12,4},{24,8},{4,12},{0,16},{28,20},{8,24},{20,28},{17,1},{... | collective-permute-start | bytes 786440 | tf_op jit(solution)/shard_map/ppermute | solution.py:49
  16.1 1.6 %collective-permute-done.3.above = bf16[128,512]{1,0:T(8,128)(2,1)S(1)} collective-permute-done((bf16[128,512]{1,0:T(8,128)(2,1)S(1)}, bf16[128,512]{1,0:T(8,128)(2,1)S(1)}, u32[]{:S(2)}, u32[]{:S(2)}) %collective-permute-start.3) | collective-permute-done | bytes 131104 | tf_op jit(solution)/shard_map/ppermute | solution.py:49
  17.7 0.0 collective-permute-done.4.below
  17.7 1.6 %collective-permute-start.7 = (bf16[256,512]{1,0:T(8,128)(2,1)S(1)}, bf16[256,512]{1,0:T(8,128)(2,1)S(1)}, u32[]{:S(2)}, u32[]{:S(2)}) collective-permute-start(bf16[256,512]{1,0:T(8,128)(2,1)S(1)} %shard_map.64.refs_0_.a), channel_id=1, source_target_pairs={{8,0},{20,4},{0,8},{28,12},{24,16},{4,20},{16,24},{12,28},{9,1},{2... | collective-permute-start | bytes 786440 | tf_op jit(solution)/shard_map/ppermute | solution.py:49
  19.3 0.0 collective-permute-done.1.refs_3_.refs_1_.a
  19.3 2.9 %shard_map.65.right.refs_0_ = f32[3,256]{1,0:T(4,128)S(1)} custom-call(bf16[256,512]{1,0:T(8,128)(2,1)S(1)} %shard_map.64.refs_0_.a, bf16[6144,512]{1,0:T(8,128)(2,1)S(1)} %bitcast.3, f32[6144,128]{1,0:T(8,128)S(1)} %shard_map.59.refs_0_.refs_2_, bf16[256,512]{1,0:T(8,128)(2,1)S(1)} %collective-permute-done.1.refs_3_.refs_1_.a), custom_call_target="tpu_custom_call" | custom-call | flops 1610612736 | bytes 6291456 | tf_op jit(solution)/shard_map/pallas_call | solution.py:154
  22.2 1.2 %collective-permute-done.2.refs_0_.refs_2_ = bf16[256,512]{1,0:T(8,128)(2,1)S(1)} collective-permute-done((bf16[256,512]{1,0:T(8,128)(2,1)S(1)}, bf16[256,512]{1,0:T(8,128)(2,1)S(1)}, u32[]{:S(2)}, u32[]{:S(2)}) %collective-permute-start.2) | collective-permute-done | bytes 262176 | tf_op jit(solution)/shard_map/ppermute | solution.py:49
  23.4 0.8 %collective-permute-start.5 = (f32[3,512]{1,0:T(4,128)S(1)}, f32[3,512]{1,0:T(4,128)S(1)}, u32[]{:S(2)}, u32[]{:S(2)}) collective-permute-start(f32[3,512]{1,0:T(4,128)S(1)} %shard_map.66.mine), channel_id=1, source_target_pairs={{1,0},{0,1},{3,2},{2,3},{5,4},{4,5},{7,6},{6,7},{9,8},{8,9},{11,10... | collective-permute-start | bytes 18440 | tf_op jit(solution)/shard_map/ppermute | solution.py:49
  24.2 1.6 %collective-permute-start.6 = (bf16[256,512]{1,0:T(8,128)(2,1)S(1)}, bf16[256,512]{1,0:T(8,128)(2,1)S(1)}, u32[]{:S(2)}, u32[]{:S(2)}) collective-permute-start(bf16[256,512]{1,0:T(8,128)(2,1)S(1)} %shard_map.69), channel_id=1, source_target_pairs={{16,0},{12,4},{24,8},{4,12},{0,16},{28,20},{8,24},{20,28},{17,1},{... | collective-permute-start | bytes 786440 | tf_op jit(solution)/shard_map/ppermute | solution.py:49
  25.8 0.6 %collective-permute-start.8 = (bf16[256,512]{1,0:T(8,128)(2,1)S(1)}, bf16[256,512]{1,0:T(8,128)(2,1)S(1)}, u32[]{:S(2)}, u32[]{:S(2)}) collective-permute-start(bf16[256,512]{1,0:T(8,128)(2,1)S(1)} %shard_map.71), channel_id=1, source_target_pairs={{16,0},{12,4},{24,8},{4,12},{0,16},{28,20},{8,24},{20,28},{17,1},{... | collective-permute-start | bytes 786440 | tf_op jit(solution)/shard_map/ppermute | solution.py:49
  26.4 0.6 %collective-permute-done.5.theirs = f32[3,512]{1,0:T(4,128)S(1)} collective-permute-done((f32[3,512]{1,0:T(4,128)S(1)}, f32[3,512]{1,0:T(4,128)S(1)}, u32[]{:S(2)}, u32[]{:S(2)}) %collective-permute-start.5) | collective-permute-done | bytes 6176 | tf_op jit(solution)/shard_map/ppermute | solution.py:49
  27.1 0.0 collective-permute-done.7.a.refs_1_
  27.1 1.6 %collective-permute-start.9 = (bf16[256,512]{1,0:T(8,128)(2,1)S(1)}, bf16[256,512]{1,0:T(8,128)(2,1)S(1)}, u32[]{:S(2)}, u32[]{:S(2)}) collective-permute-start(bf16[256,512]{1,0:T(8,128)(2,1)S(1)} %shard_map.72), channel_id=1, source_target_pairs={{16,0},{12,4},{24,8},{4,12},{0,16},{28,20},{8,24},{20,28},{17,1},{... | collective-permute-start | bytes 786440 | tf_op jit(solution)/shard_map/ppermute | solution.py:49
  28.7 2.2 %collective-permute-start.10 = (f32[3,512]{1,0:T(4,128)S(1)}, f32[3,512]{1,0:T(4,128)S(1)}, u32[]{:S(2)}, u32[]{:S(2)}) collective-permute-start(f32[3,512]{1,0:T(4,128)S(1)} %shard_map.67.refs_4_.refs_2_.refs_0_.mine), channel_id=1, source_target_pairs={{2,0},{3,1},{0,2},{1,3},{6,4},{7,5},{4,6},{5,7},{10,8},{11,9},{8,1... | collective-permute-start | bytes 18440 | tf_op jit(solution)/shard_map/ppermute | solution.py:49
  30.9 1.7 %shard_map.68 = (bf16[1536,768]{1,0:T(8,128)(2,1)S(1)}, f32[6,768]{1,0:T(8,128)S(1)}, bf16[768,512]{1,0:T(8,128)(2,1)S(1)}) custom-call(bf16[256,512]{1,0:T(8,128)(2,1)S(1)} %shard_map.60.a.refs_0_, bf16[256,512]{1,0:T(8,128)(2,1)S(1)} %collective-permute-done.1.refs_3_.refs_1_.a, bf16[256,512]{1,0:T(8,128)(2,1)S(1)} %collective-permute-done.2.refs_0_.refs_2_, ...), custom_call_target="tpu_custom_call" | custom-call | flops 12079595 | bytes 47185 | tf_op jit(solution)/shard_map/pallas_call | solution.py:230
  32.6 0.0 collective-permute-done.6.refs_0_
  32.6 0.7 %shard_map.70 = (bf16[1536,256]{1,0:T(8,128)(2,1)S(1)}, f32[6,256]{1,0:T(8,128)S(1)}, bf16[256,512]{1,0:T(8,128)(2,1)S(1)}) custom-call(bf16[256,512]{1,0:T(8,128)(2,1)S(1)} %collective-permute-done.6.refs_0_, bf16[6144,512]{1,0:T(8,128)(2,1)S(1)} %bitcast.3, f32[3,512]{1,0:T(4,128)S(1)} %shard_map.67.refs_4_.refs_2_.refs_0_.mine), custom_call_target="tpu_custom_call" | custom-call | flops 4026531 | bytes 26214 | tf_op jit(solution)/shard_map/pallas_call | solution.py:230
  33.3 0.0 collective-permute-done.10.theirs
  33.4 1.5 %collective-permute-start.11 = (f32[2,512]{1,0:T(2,128)S(1)}, f32[2,512]{1,0:T(2,128)S(1)}, u32[]{:S(2)}, u32[]{:S(2)}) collective-permute-start(f32[2,512]{1,0:T(2,128)S(1)} %shard_map.73.refs_5_.refs_0_), channel_id=1, source_target_pairs={{8,0},{20,4},{0,8},{28,12},{24,16},{4,20},{16,24},{12,28},{9,1},{2... | collective-permute-start | bytes 12296 | tf_op jit(solution)/shard_map/ppermute | solution.py:49
  34.8 0.5 %collective-permute-start.12 = (f32[2,512]{1,0:T(2,128)S(1)}, f32[2,512]{1,0:T(2,128)S(1)}, u32[]{:S(2)}, u32[]{:S(2)}) collective-permute-start(f32[2,512]{1,0:T(2,128)S(1)} %shard_map.73.refs_5_.refs_0_), channel_id=1, source_target_pairs={{16,0},{12,4},{24,8},{4,12},{0,16},{28,20},{8,24},{20,28},{17,1},{... | collective-permute-start | bytes 12296 | tf_op jit(solution)/shard_map/ppermute | solution.py:49
  35.3 1.6 %collective-permute-start.13 = (f32[2,512]{1,0:T(2,128)S(1)}, f32[2,512]{1,0:T(2,128)S(1)}, u32[]{:S(2)}, u32[]{:S(2)}) collective-permute-start(f32[2,512]{1,0:T(2,128)S(1)} %shard_map.73.refs_5_.refs_0_), channel_id=1, source_target_pairs={{24,0},{16,8},{8,16},{0,24},{25,1},{17,9},{9,17},{1,25},{26,2},{18... | collective-permute-start | bytes 12296 | tf_op jit(solution)/shard_map/ppermute | solution.py:49
  36.9 0.0 collective-permute-done.8.refs_2_
  36.9 0.0 collective-permute-done.9.refs_3_
  36.9 2.2 %shard_map.74 = (bf16[1536,1024]{1,0:T(8,128)(2,1)S(1)}, f32[6,1024]{1,0:T(8,128)S(1)}, bf16[1024,512]{1,0:T(8,128)(2,1)S(1)}) custom-call(bf16[256,512]{1,0:T(8,128)(2,1)S(1)} %shard_map.64.refs_0_.a, bf16[256,512]{1,0:T(8,128)(2,1)S(1)} %collective-permute-done.7.a.refs_1_, bf16[256,512]{1,0:T(8,128)(2,1)S(1)} %collective-permute-done.8.refs_2_, ...), custom_call_target="tpu_custom_call" | custom-call | flops 1610612736 | bytes 5767168 | tf_op jit(solution)/shard_map/pallas_call | solution.py:230
  39.2 0.0 collective-permute-done.11.refs_1_
  39.2 0.0 collective-permute-done.12.refs_2_
  39.2 0.7 %collective-permute-done.13.refs_3_ = f32[2,512]{1,0:T(2,128)S(1)} collective-permute-done((f32[2,512]{1,0:T(2,128)S(1)}, f32[2,512]{1,0:T(2,128)S(1)}, u32[]{:S(2)}, u32[]{:S(2)}) %collective-permute-start.13) | collective-permute-done | bytes 4128 | tf_op jit(solution)/shard_map/ppermute | solution.py:49
  39.9 2.3 %shard_map.77 = (bf16[768,512]{1,0:T(8,128)(2,1)S(1)}, f32[1,768]{1,0:T(1,128)S(1)}) custom-call(bf16[1536,768]{1,0:T(8,128)(2,1)S(1)} %get-tuple-element.20.refs_0_, bf16[1536,256]{1,0:T(8,128)(2,1)S(1)} %get-tuple-element.21.refs_1_, bf16[1536,1024]{1,0:T(8,128)(2,1)S(1)} %get-tuple-element.24.refs_2_, bf16[768,512]{1,0:T(8,128)(2,1)S(1)} %get-tuple-element.25.refs_3_, ...), custom_call_target="tpu_custom_call" | custom-call | flops 1811939328 | bytes 7471104 | tf_op jit(solution)/shard_map/pallas_call | solution.py:281
  42.1 0.1 collective-permute-start.14
  42.2 0.5 %collective-permute-start.15 = (f32[1,768]{1,0:T(1,128)S(1)}, f32[1,768]{1,0:T(1,128)S(1)}, u32[]{:S(2)}, u32[]{:S(2)}) collective-permute-start(f32[1,768]{1,0:T(1,128)S(1)} %get-tuple-element.35), channel_id=1, source_target_pairs={{4,0},{0,4},{5,1},{1,5},{6,2},{2,6},{7,3},{3,7},{12,8},{8,12},{13,... | collective-permute-start | bytes 9224 | tf_op jit(solution)/shard_map/ppermute | solution.py:49
  42.7 2.0 %shard_map.76 = (f32[768,512]{1,0:T(8,128)S(1)}, f32[1,768]{1,0:T(1,128)S(1)}) custom-call(bf16[1536,768]{1,0:T(8,128)(2,1)S(1)} %get-tuple-element.20.refs_0_, bf16[1536,256]{1,0:T(8,128)(2,1)S(1)} %get-tuple-element.21.refs_1_, bf16[1536,1024]{1,0:T(8,128)(2,1)S(1)} %get-tuple-element.24.refs_2_, bf16[768,512]{1,0:T(8,128)(2,1)S(1)} %get-tuple-element.25.refs_3_, ...), custom_call_target="tpu_custom_call" | custom-call | flops 1811939328 | bytes 7471104 | tf_op jit(solution)/shard_map/pallas_call | solution.py:281
  44.7 0.0 collective-permute-done.15.there_mass
  44.7 0.0 collective-permute-done.14.there
  44.8 1.8 %shard_map.78 = (f32[768,512]{1,0:T(8,128)}, f32[1,768]{1,0:T(1,128)}) custom-call(f32[768,512]{1,0:T(8,128)S(1)} %get-tuple-element.32.here, f32[1,768]{1,0:T(1,128)S(1)} %get-tuple-element.33.here_mass, bf16[768,512]{1,0:T(8,128)(2,1)S(1)} %collective-permute-done.14.there, f32[1,768]{1,0:T(1,128)S(1)} %collective-permute-done.15.there_mass), custom_call_target="tpu_custom_call" | custom-call | tf_op jit(solution)/shard_map/pallas_call | solution.py:311
  (12 shorter events, 0.2 us)
Async XLA Ops:
  1.7 8.1 %collective-permute-start = (bf16[128,512]{1,0:T(8,128)(2,1)S(1)}, bf16[128,512]{1,0:T(8,128)(2,1)S(1)}, u32[]{:S(2)}, u32[]{:S(2)}) collective-permute-start(bf16[128,512]{1,0:T(8,128)(2,1)S(1)} %multiply_convert_fusion.above), channel_id=1, source_target_pairs={{1,0},{0,1},{3,2},{2,3},{5,4},{4,5},{7,6},{6,7},{9,8},{8,9},{11,10... | collective-permute-start | bytes 393224 | tf_op jit(solution)/shard_map/ppermute | solution.py:49
  4.8 12.9 %collective-permute-start.3 = (bf16[128,512]{1,0:T(8,128)(2,1)S(1)}, bf16[128,512]{1,0:T(8,128)(2,1)S(1)}, u32[]{:S(2)}, u32[]{:S(2)}) collective-permute-start(bf16[128,512]{1,0:T(8,128)(2,1)S(1)} %multiply_convert_fusion.above), channel_id=1, source_target_pairs={{2,0},{3,1},{0,2},{1,3},{6,4},{7,5},{4,6},{5,7},{10,8},{11,9},{8,1... | collective-permute-start | bytes 393224 | tf_op jit(solution)/shard_map/ppermute | solution.py:49
  7.4 10.3 %collective-permute-start.4 = (bf16[128,512]{1,0:T(8,128)(2,1)S(1)}, bf16[128,512]{1,0:T(8,128)(2,1)S(1)}, u32[]{:S(2)}, u32[]{:S(2)}) collective-permute-start(bf16[128,512]{1,0:T(8,128)(2,1)S(1)} %multiply_convert_fusion.above), channel_id=1, source_target_pairs={{3,0},{2,1},{1,2},{0,3},{7,4},{6,5},{5,6},{4,7},{11,8},{10,9},{9,1... | collective-permute-start | bytes 393224 | tf_op jit(solution)/shard_map/ppermute | solution.py:49
  7.4 0.7 %copy-start = (s32[6144]{0:T(1024)S(1)}, s32[6144]{0:T(1024)}, u32[]{:S(2)}) copy-start(s32[6144]{0:T(1024)} %param.7) | copy-start | bytes 73732
  8.1 3.5 %slice-start = ((s8[6291456]{0:T(1024)(128)(4,1)}), s8[4194304]{0:T(1024)(128)(4,1)S(1)}, s32[]{:S(2)}) async-start(s8[6291456]{0:T(1024)(128)(4,1)} %bitcast.2), calls=%async_computation | async-start | bytes 8388608
  9.0 2.6 %slice-start.1 = ((s8[6291456]{0:T(1024)(128)(4,1)}), s8[2097152]{0:T(1024)(128)(4,1)S(1)}, s32[]{:S(2)}) async-start(s8[6291456]{0:T(1024)(128)(4,1)} %bitcast.2), calls=%async_computation.1 | async-start | bytes 4194304
  9.9 9.4 %collective-permute-start.1 = (bf16[256,512]{1,0:T(8,128)(2,1)S(1)}, bf16[256,512]{1,0:T(8,128)(2,1)S(1)}, u32[]{:S(2)}, u32[]{:S(2)}) collective-permute-start(bf16[256,512]{1,0:T(8,128)(2,1)S(1)} %shard_map.60.a.refs_0_), channel_id=1, source_target_pairs={{8,0},{20,4},{0,8},{28,12},{24,16},{4,20},{16,24},{12,28},{9,1},{2... | collective-permute-start | bytes 786440 | tf_op jit(solution)/shard_map/ppermute | solution.py:49
  14.5 8.9 %collective-permute-start.2 = (bf16[256,512]{1,0:T(8,128)(2,1)S(1)}, bf16[256,512]{1,0:T(8,128)(2,1)S(1)}, u32[]{:S(2)}, u32[]{:S(2)}) collective-permute-start(bf16[256,512]{1,0:T(8,128)(2,1)S(1)} %shard_map.63), channel_id=1, source_target_pairs={{16,0},{12,4},{24,8},{4,12},{0,16},{28,20},{8,24},{20,28},{17,1},{... | collective-permute-start | bytes 786440 | tf_op jit(solution)/shard_map/ppermute | solution.py:49
  17.7 9.3 %collective-permute-start.7 = (bf16[256,512]{1,0:T(8,128)(2,1)S(1)}, bf16[256,512]{1,0:T(8,128)(2,1)S(1)}, u32[]{:S(2)}, u32[]{:S(2)}) collective-permute-start(bf16[256,512]{1,0:T(8,128)(2,1)S(1)} %shard_map.64.refs_0_.a), channel_id=1, source_target_pairs={{8,0},{20,4},{0,8},{28,12},{24,16},{4,20},{16,24},{12,28},{9,1},{2... | collective-permute-start | bytes 786440 | tf_op jit(solution)/shard_map/ppermute | solution.py:49
  23.4 3.7 %collective-permute-start.5 = (f32[3,512]{1,0:T(4,128)S(1)}, f32[3,512]{1,0:T(4,128)S(1)}, u32[]{:S(2)}, u32[]{:S(2)}) collective-permute-start(f32[3,512]{1,0:T(4,128)S(1)} %shard_map.66.mine), channel_id=1, source_target_pairs={{1,0},{0,1},{3,2},{2,3},{5,4},{4,5},{7,6},{6,7},{9,8},{8,9},{11,10... | collective-permute-start | bytes 18440 | tf_op jit(solution)/shard_map/ppermute | solution.py:49
  24.2 8.4 %collective-permute-start.6 = (bf16[256,512]{1,0:T(8,128)(2,1)S(1)}, bf16[256,512]{1,0:T(8,128)(2,1)S(1)}, u32[]{:S(2)}, u32[]{:S(2)}) collective-permute-start(bf16[256,512]{1,0:T(8,128)(2,1)S(1)} %shard_map.69), channel_id=1, source_target_pairs={{16,0},{12,4},{24,8},{4,12},{0,16},{28,20},{8,24},{20,28},{17,1},{... | collective-permute-start | bytes 786440 | tf_op jit(solution)/shard_map/ppermute | solution.py:49
  25.8 11.1 %collective-permute-start.8 = (bf16[256,512]{1,0:T(8,128)(2,1)S(1)}, bf16[256,512]{1,0:T(8,128)(2,1)S(1)}, u32[]{:S(2)}, u32[]{:S(2)}) collective-permute-start(bf16[256,512]{1,0:T(8,128)(2,1)S(1)} %shard_map.71), channel_id=1, source_target_pairs={{16,0},{12,4},{24,8},{4,12},{0,16},{28,20},{8,24},{20,28},{17,1},{... | collective-permute-start | bytes 786440 | tf_op jit(solution)/shard_map/ppermute | solution.py:49
  27.1 9.8 %collective-permute-start.9 = (bf16[256,512]{1,0:T(8,128)(2,1)S(1)}, bf16[256,512]{1,0:T(8,128)(2,1)S(1)}, u32[]{:S(2)}, u32[]{:S(2)}) collective-permute-start(bf16[256,512]{1,0:T(8,128)(2,1)S(1)} %shard_map.72), channel_id=1, source_target_pairs={{16,0},{12,4},{24,8},{4,12},{0,16},{28,20},{8,24},{20,28},{17,1},{... | collective-permute-start | bytes 786440 | tf_op jit(solution)/shard_map/ppermute | solution.py:49
  28.7 4.6 %collective-permute-start.10 = (f32[3,512]{1,0:T(4,128)S(1)}, f32[3,512]{1,0:T(4,128)S(1)}, u32[]{:S(2)}, u32[]{:S(2)}) collective-permute-start(f32[3,512]{1,0:T(4,128)S(1)} %shard_map.67.refs_4_.refs_2_.refs_0_.mine), channel_id=1, source_target_pairs={{2,0},{3,1},{0,2},{1,3},{6,4},{7,5},{4,6},{5,7},{10,8},{11,9},{8,1... | collective-permute-start | bytes 18440 | tf_op jit(solution)/shard_map/ppermute | solution.py:49
  33.4 5.8 %collective-permute-start.11 = (f32[2,512]{1,0:T(2,128)S(1)}, f32[2,512]{1,0:T(2,128)S(1)}, u32[]{:S(2)}, u32[]{:S(2)}) collective-permute-start(f32[2,512]{1,0:T(2,128)S(1)} %shard_map.73.refs_5_.refs_0_), channel_id=1, source_target_pairs={{8,0},{20,4},{0,8},{28,12},{24,16},{4,20},{16,24},{12,28},{9,1},{2... | collective-permute-start | bytes 12296 | tf_op jit(solution)/shard_map/ppermute | solution.py:49
  34.8 4.4 %collective-permute-start.12 = (f32[2,512]{1,0:T(2,128)S(1)}, f32[2,512]{1,0:T(2,128)S(1)}, u32[]{:S(2)}, u32[]{:S(2)}) collective-permute-start(f32[2,512]{1,0:T(2,128)S(1)} %shard_map.73.refs_5_.refs_0_), channel_id=1, source_target_pairs={{16,0},{12,4},{24,8},{4,12},{0,16},{28,20},{8,24},{20,28},{17,1},{... | collective-permute-start | bytes 12296 | tf_op jit(solution)/shard_map/ppermute | solution.py:49
  35.3 4.5 %collective-permute-start.13 = (f32[2,512]{1,0:T(2,128)S(1)}, f32[2,512]{1,0:T(2,128)S(1)}, u32[]{:S(2)}, u32[]{:S(2)}) collective-permute-start(f32[2,512]{1,0:T(2,128)S(1)} %shard_map.73.refs_5_.refs_0_), channel_id=1, source_target_pairs={{24,0},{16,8},{8,16},{0,24},{25,1},{17,9},{9,17},{1,25},{26,2},{18... | collective-permute-start | bytes 12296 | tf_op jit(solution)/shard_map/ppermute | solution.py:49
  42.1 2.6 %collective-permute-start.14 = (bf16[768,512]{1,0:T(8,128)(2,1)S(1)}, bf16[768,512]{1,0:T(8,128)(2,1)S(1)}, u32[]{:S(2)}, u32[]{:S(2)}) collective-permute-start(bf16[768,512]{1,0:T(8,128)(2,1)S(1)} %get-tuple-element.34), channel_id=1, source_target_pairs={{4,0},{0,4},{5,1},{1,5},{6,2},{2,6},{7,3},{3,7},{12,8},{8,12},{13,... | collective-permute-start | bytes 2359304 | tf_op jit(solution)/shard_map/ppermute | solution.py:49
  42.2 2.5 %collective-permute-start.15 = (f32[1,768]{1,0:T(1,128)S(1)}, f32[1,768]{1,0:T(1,128)S(1)}, u32[]{:S(2)}, u32[]{:S(2)}) collective-permute-start(f32[1,768]{1,0:T(1,128)S(1)} %get-tuple-element.35), channel_id=1, source_target_pairs={{4,0},{0,4},{5,1},{1,5},{6,2},{2,6},{7,3},{3,7},{12,8},{8,12},{13,... | collective-permute-start | bytes 9224 | tf_op jit(solution)/shard_map/ppermute | solution.py:49

commit v18 on v17

--- a/solution.py
+++ b/solution.py
@@ -165,32 +165,30 @@
     )(*args)
 
 
-def merge_kernel(rate, by, goal, mine, theirs, *refs):
+def goal_kernel(rate, *refs):
+    stats, goal = refs[:4], refs[-1]
     for at in range(4):
-        ours = mine[:, at * 128 : (at + 1) * 128]
-        other = theirs[:, (at ^ by) * 128 : ((at ^ by) + 1) * 128]
-        top, total, novel = join_stats(rate, [(s[:1], s[1:2], s[2:]) for s in (ours, other)])
-        rows = (top, novel / total / total) if goal else (top, total, novel)
-        refs[-1][:, at * 128 : (at + 1) * 128] = jnp.concatenate(rows, axis=0)
-
-
-def merge_call(rate, by, goal, mine, theirs, *after):
-    return pl.pallas_call(
-        functools.partial(merge_kernel, rate, by, goal),
-        in_specs=in_vmem(2 + len(after)),
-        out_specs=in_vmem(1)[0],
-        out_shape=jax.ShapeDtypeStruct((2 if goal else 3, mine.shape[1]), jnp.float32),
-        compiler_params=pltpu.CompilerParams(vmem_limit_bytes=VMEM_BYTES),
-    )(mine, theirs, *after)
+        here = [stat[:, (at ^ by) * 128 : ((at ^ by) + 1) * 128] for by, stat in enumerate(stats)]
+        top, total, novel = join_stats(rate, [(s[:1], s[1:2], s[2:]) for s in here])
+        goal[:, at * 128 : (at + 1) * 128] = jnp.concatenate([top, novel / total / total], axis=0)
+
+
+def goal_call(rate, *stats):
+    return pl.pallas_call(
+        functools.partial(goal_kernel, rate),
+        in_specs=in_vmem(len(stats)),
+        out_specs=in_vmem(1)[0],
+        out_shape=jax.ShapeDtypeStruct((2, stats[0].shape[1]), jnp.float32),
+        compiler_params=pltpu.CompilerParams(vmem_limit_bytes=VMEM_BYTES),
+    )(*stats)
 
 
 def factor_kernel(rate, n, *refs):
     goals, tops, factors = refs[:4], refs[4 : 4 + n], refs[4 + n :]
     rows = goals[0].shape[1] // 2
-    spots = [(0, 0, 0), (0, 1, rows), (0, 2, 2 * rows), (1, 3, 0)]
-    spots += [(2, at, at * rows) for at in range(4)]
-    for at, (bundle, goal, start) in enumerate(spots):
-        group = at // 4
+    spots = [(0, 0, 0), (0, 0, 1), (0, 0, 2), (1, 0, 3), (1, 1, 0), (1, 1, 1), (1, 1, 2), (2, 1, 3)]
+    for at, (bundle, group, goal) in enumerate(spots):
+        start = (at - (0, 3, 7)[bundle]) * rows
         mine, here = slice(group * rows, (group + 1) * rows), slice(start, start + rows)
         scale = jnp.exp2((tops[bundle][:, here] - goals[goal][:1, mine]) * rate)
         factors[bundle][:, here] = scale * goals[goal][1:, mine]
@@ -206,12 +204,12 @@
     )(*goals, *tops)
 
 
-def expo_kernel(rate, block, n, *refs):
-    pieces, cells, (expo, tops, points) = refs[:n], refs[n], refs[-3:]
+def expo_kernel(rate, block, spots, *refs):
+    pieces, cells, (expo, tops, points) = refs[: len(spots)], refs[len(spots)], refs[-3:]
     start = 0
-    for piece in pieces:
-        points[start : start + piece.shape[0], :] = piece[...]
-        start += piece.shape[0]
+    for piece, (first, rows) in zip(pieces, spots):
+        points[start : start + rows, :] = piece[first : first + rows, :]
+        start += rows
     count = expo.shape[0] // block
     chip = chip_index()
     for at in range(count):
@@ -226,9 +224,10 @@
 
 def expo_call(rate, block, count, pieces, cells, *after, declared=1.0):
     width = cells.shape[1]
-    n_points = sum(piece.shape[0] for piece in pieces)
-    return pl.pallas_call(
-        functools.partial(expo_kernel, rate, block, len(pieces)),
+    pieces, spots = zip(*((piece[0], piece[1:]) if isinstance(piece, tuple) else (piece, (0, len(piece))) for piece in pieces))
+    n_points = sum(rows for _, rows in spots)
+    return pl.pallas_call(
+        functools.partial(expo_kernel, rate, block, spots),
         in_specs=in_vmem(len(pieces) + 1 + len(after)),
         out_specs=in_vmem(3),
         out_shape=[
@@ -346,16 +345,18 @@
     second_01 = turn_back(hold(near_01, stats[0]))
     near_23 = join(near_2, near_3, *stats)
     stats.append(totals_call(rate, block, (near_23,), centroids, inverse, after=(first_01,)))
-    across_01 = turn_back(hold(first_01, stats[1]))
-    first_23, second_23 = turn(near_23), turn_back(hold(near_23, stats[1]))
-
+    first_23 = turn(near_23)
+    rows = near_01.shape[0]
+    both = turn_back(join(first_01, near_23, stats[1]))
+    across_01, second_23 = (both, 0, rows), (both, rows, rows)
+    stat = beside(*stats)
     expand = functools.partial(expo_call, rate, block, 2 * per_device)
-    stat = beside(*stats, second_01)
-    stat = merge_call(rate, 1, False, stat, along_z(stat, 1))
-    across_23 = turn_back(hold(first_23, stat))
-    bundles = [expand(pieces, centroids, stat, declared=0.01) for pieces in ((near_01, first_01, second_01), (across_01,))]
-    goal = merge_call(rate, 2, True, stat, along_z(stat, 2), *(tops for _, tops, _ in bundles))
-    bundles.append(expand((near_23, first_23, second_23, across_23), centroids, goal))
+    bundles = [expand((near_01, first_01, second_01), centroids, stat, declared=0.01)]
+    goal = goal_call(rate, stat, *(along_z(stat, by) for by in (1, 2, 3)), bundles[0][1])
+    across_23 = turn_back(hold(first_23, goal))
+
+    bundles.append(expand((across_01, near_23, first_23, second_23), centroids, goal))
+    bundles.append(expand((across_23,), centroids, bundles[1][1]))
     expos, tops, points = zip(*bundles)
     goals = [goal, turn(goal), turn_back(goal), around(goal, 3)]
     factors = factor_call(rate, goals, tops)

time: 46.9 us -> 54.2 us (1.16)
  waiting for transfers between devices: 4.94 us -> 10.8 us
  starting transfers between devices: 21.5 us -> 22.8 us
    ppermute x16, waiting for transfers between devices: 4.94 us -> 10.8 us  [exchange(): return lax.ppermute(a, axes, [(partner(at), at) for at in range(count)])]
    ppermute x16, starting transfers between devices: 21.5 us -> 22.8 us  [exchange(): return lax.ppermute(a, axes, [(partner(at), at) for at in range(count)])]
    pallas_call x5 -> x4, Pallas kernels: 4.67 us -> 4.66 us  [the longest x3 4.62 us: expo_call(): pl.pallas_call(functools.partial(expo_kernel, rate, block, spots), in_spe...]
  transfers between devices with their start and end apart: 16 -> 16, of which waited for: 5 -> 4; matrix products, arithmetic and copies ran while one was open for 0% -> 0% of each run, Pallas kernels for 29% -> 20%
where the time goes in v18:
time: 54.2 us; the launch traced here: 54 us
  starting transfers between devices  22.8 us (42%)
  Pallas kernels  17.5 us (32%)
  waiting for transfers between devices  10.8 us (20%)
  other arithmetic  1.05 us (2%)
  between operations  1 us (2%)
  local copies, waits for them, and re-layouts  0.75 us (1%)
    ppermute x16, starting transfers between devices, exchange(): return lax.ppermute(a, axes, [(partner(at), at) for at in range(count)])  22.8 us
    ppermute x16, waiting for transfers between devices, exchange(): return lax.ppermute(a, axes, [(partner(at), at) for at in range(count)])  10.8 us
    pallas_call x2, Pallas kernels, totals_call(): pl.pallas_call(functools.partial(totals_kernel, rate, block, len(pieces))...  5.81 us
    pallas_call x3, Pallas kernels, expo_call(): pl.pallas_call(functools.partial(expo_kernel, rate, block, spots), in_spe...  4.62 us
    pallas_call x2, Pallas kernels, sums_call(): pl.pallas_call(functools.partial(sums_kernel, n, block, side), in_specs=i...  4.25 us
    pallas_call x1, Pallas kernels, add_call(): pl.pallas_call(functools.partial(add_kernel, block), in_specs=in_vmem(4),...  1.79 us
  transfers between devices with their start and end apart: 16, of which 4 were waited for; matrix products, arithmetic and copies ran while one was open for 0% of the time, Pallas kernels for 20%

profile of v18, /device:TPU:0, one launch (start us, length us, event | category | flops | bytes accessed | tf_op | source)
XLA Modules:
  0.0 54.0 jit_solution(5188069570985189953)
XLA Ops:
  0.6 1.1 %multiply_convert_fusion.above = bf16[128,512]{1,0:T(8,128)(2,1)S(1)} fusion(s32[128,512]{1,0:T(8,128)} %param.4, s32[128]{0:T(128)} %param.5), kind=kLoop, calls=%fused_computation | loop fusion | flops 327680 | bytes 393728 | tf_op jit(solution)/shard_map/convert_element_type | solution.py:17
  1.7 3.1 %collective-permute-start = (bf16[128,512]{1,0:T(8,128)(2,1)S(1)}, bf16[128,512]{1,0:T(8,128)(2,1)S(1)}, u32[]{:S(2)}, u32[]{:S(2)}) collective-permute-start(bf16[128,512]{1,0:T(8,128)(2,1)S(1)} %multiply_convert_fusion.above), channel_id=1, source_target_pairs={{1,0},{0,1},{3,2},{2,3},{5,4},{4,5},{7,6},{6,7},{9,8},{8,9},{11,10... | collective-permute-start | bytes 393224 | tf_op jit(solution)/shard_map/ppermute | solution.py:49
  4.8 2.6 %collective-permute-start.3 = (bf16[128,512]{1,0:T(8,128)(2,1)S(1)}, bf16[128,512]{1,0:T(8,128)(2,1)S(1)}, u32[]{:S(2)}, u32[]{:S(2)}) collective-permute-start(bf16[128,512]{1,0:T(8,128)(2,1)S(1)} %multiply_convert_fusion.above), channel_id=1, source_target_pairs={{2,0},{3,1},{0,2},{1,3},{6,4},{7,5},{4,6},{5,7},{10,8},{11,9},{8,1... | collective-permute-start | bytes 393224 | tf_op jit(solution)/shard_map/ppermute | solution.py:49
  7.4 0.0 collective-permute-start.4
  7.4 0.0 copy-start
  7.4 0.7 %copy-done = s32[6144]{0:T(1024)S(1)} copy-done((s32[6144]{0:T(1024)S(1)}, s32[6144]{0:T(1024)}, u32[]{:S(2)}) %copy-start) | copy-done | bytes 24600
  8.1 0.0 slice-start
  8.1 0.9 %shard_map.59.refs_0_.refs_2_ = f32[6144,128]{1,0:T(8,128)S(1)} custom-call(s32[48,128]{1,0:T(8,128)S(1)} %bitcast.4), custom_call_target="tpu_custom_call" | custom-call | flops 2000000000 | tf_op jit(solution)/shard_map/pallas_call | solution.py:114
  9.0 0.0 slice-start.1
  9.0 0.8 %collective-permute-done.below = bf16[128,512]{1,0:T(8,128)(2,1)S(1)} collective-permute-done((bf16[128,512]{1,0:T(8,128)(2,1)S(1)}, bf16[128,512]{1,0:T(8,128)(2,1)S(1)}, u32[]{:S(2)}, u32[]{:S(2)}) %collective-permute-start) | collective-permute-done | bytes 131104 | tf_op jit(solution)/shard_map/ppermute | solution.py:49
  9.8 1.8 %collective-permute-start.1 = (bf16[256,512]{1,0:T(8,128)(2,1)S(1)}, bf16[256,512]{1,0:T(8,128)(2,1)S(1)}, u32[]{:S(2)}, u32[]{:S(2)}) collective-permute-start(bf16[256,512]{1,0:T(8,128)(2,1)S(1)} %shard_map.60.a.refs_0_), channel_id=1, source_target_pairs={{8,0},{20,4},{0,8},{28,12},{24,16},{4,20},{16,24},{12,28},{9,1},{2... | collective-permute-start | bytes 786440 | tf_op jit(solution)/shard_map/ppermute | solution.py:49
  11.6 0.0 slice-done
  11.6 0.0 slice-done.1
  11.7 2.9 %shard_map.62.refs_0_.left = f32[3,256]{1,0:T(4,128)S(1)} custom-call(bf16[256,512]{1,0:T(8,128)(2,1)S(1)} %shard_map.61.refs_0_, bf16[6144,512]{1,0:T(8,128)(2,1)S(1)} %bitcast.3, f32[6144,128]{1,0:T(8,128)S(1)} %shard_map.59.refs_0_.refs_2_), custom_call_target="tpu_custom_call" | custom-call | flops 1610612736 | bytes 6291456 | tf_op jit(solution)/shard_map/pallas_call | solution.py:154
  14.6 3.1 %collective-permute-done.3.above = bf16[128,512]{1,0:T(8,128)(2,1)S(1)} collective-permute-done((bf16[128,512]{1,0:T(8,128)(2,1)S(1)}, bf16[128,512]{1,0:T(8,128)(2,1)S(1)}, u32[]{:S(2)}, u32[]{:S(2)}) %collective-permute-start.3) | collective-permute-done | bytes 131104 | tf_op jit(solution)/shard_map/ppermute | solution.py:49
  17.7 0.0 collective-permute-done.4.below
  17.7 0.0 collective-permute-done.1.refs_3_.refs_1_.above
  17.7 2.9 %shard_map.65.right.refs_0_ = f32[3,256]{1,0:T(4,128)S(1)} custom-call(bf16[256,512]{1,0:T(8,128)(2,1)S(1)} %shard_map.64.refs_0_.below.refs_1_, bf16[6144,512]{1,0:T(8,128)(2,1)S(1)} %bitcast.3, f32[6144,128]{1,0:T(8,128)S(1)} %shard_map.59.refs_0_.refs_2_, bf16[256,512]{1,0:T(8,128)(2,1)S(1)} %collective-permute-done.1.refs_3_.refs_1_.above), custom_call_target="tpu_custom_call" | custom-call | flops 1610612736 | bytes 6291456 | tf_op jit(solution)/shard_map/pallas_call | solution.py:154
  20.7 1.6 %collective-permute-start.5 = (bf16[512,512]{1,0:T(8,128)(2,1)S(1)}, bf16[512,512]{1,0:T(8,128)(2,1)S(1)}, u32[]{:S(2)}, u32[]{:S(2)}) collective-permute-start(bf16[512,512]{1,0:T(8,128)(2,1)S(1)} %shard_map.68), channel_id=1, source_target_pairs={{16,0},{12,4},{24,8},{4,12},{0,16},{28,20},{8,24},{20,28},{17,1},{... | collective-permute-start | bytes 1572872 | tf_op jit(solution)/shard_map/ppermute | solution.py:49
  22.3 0.6 %collective-permute-start.2 = (bf16[256,512]{1,0:T(8,128)(2,1)S(1)}, bf16[256,512]{1,0:T(8,128)(2,1)S(1)}, u32[]{:S(2)}, u32[]{:S(2)}) collective-permute-start(bf16[256,512]{1,0:T(8,128)(2,1)S(1)} %shard_map.63), channel_id=1, source_target_pairs={{16,0},{12,4},{24,8},{4,12},{0,16},{28,20},{8,24},{20,28},{17,1},{... | collective-permute-start | bytes 786440 | tf_op jit(solution)/shard_map/ppermute | solution.py:49
  22.9 1.5 %collective-permute-start.6 = (bf16[256,512]{1,0:T(8,128)(2,1)S(1)}, bf16[256,512]{1,0:T(8,128)(2,1)S(1)}, u32[]{:S(2)}, u32[]{:S(2)}) collective-permute-start(bf16[256,512]{1,0:T(8,128)(2,1)S(1)} %shard_map.64.refs_0_.below.refs_1_), channel_id=1, source_target_pairs={{8,0},{20,4},{0,8},{28,12},{24,16},{4,20},{16,24},{12,28},{9,1},{2... | collective-permute-start | bytes 786440 | tf_op jit(solution)/shard_map/ppermute | solution.py:49
  24.4 2.0 %collective-permute-start.7 = (f32[3,512]{1,0:T(4,128)S(1)}, f32[3,512]{1,0:T(4,128)S(1)}, u32[]{:S(2)}, u32[]{:S(2)}) collective-permute-start(f32[3,512]{1,0:T(4,128)S(1)} %shard_map.66.refs_4_.refs_0_), channel_id=1, source_target_pairs={{1,0},{0,1},{3,2},{2,3},{5,4},{4,5},{7,6},{6,7},{9,8},{8,9},{11,10... | collective-permute-start | bytes 18440 | tf_op jit(solution)/shard_map/ppermute | solution.py:49
  26.3 1.1 %collective-permute-start.8 = (f32[3,512]{1,0:T(4,128)S(1)}, f32[3,512]{1,0:T(4,128)S(1)}, u32[]{:S(2)}, u32[]{:S(2)}) collective-permute-start(f32[3,512]{1,0:T(4,128)S(1)} %shard_map.66.refs_4_.refs_0_), channel_id=1, source_target_pairs={{2,0},{3,1},{0,2},{1,3},{6,4},{7,5},{4,6},{5,7},{10,8},{11,9},{8,1... | collective-permute-start | bytes 18440 | tf_op jit(solution)/shard_map/ppermute | solution.py:49
  27.4 6.1 %collective-permute-done.2.refs_2_ = bf16[256,512]{1,0:T(8,128)(2,1)S(1)} collective-permute-done((bf16[256,512]{1,0:T(8,128)(2,1)S(1)}, bf16[256,512]{1,0:T(8,128)(2,1)S(1)}, u32[]{:S(2)}, u32[]{:S(2)}) %collective-permute-start.2) | collective-permute-done | bytes 262176 | tf_op jit(solution)/shard_map/ppermute | solution.py:49
  33.5 3.1 %collective-permute-start.9 = (f32[3,512]{1,0:T(4,128)S(1)}, f32[3,512]{1,0:T(4,128)S(1)}, u32[]{:S(2)}, u32[]{:S(2)}) collective-permute-start(f32[3,512]{1,0:T(4,128)S(1)} %shard_map.66.refs_4_.refs_0_), channel_id=1, source_target_pairs={{3,0},{2,1},{1,2},{0,3},{7,4},{6,5},{5,6},{4,7},{11,8},{10,9},{9,1... | collective-permute-start | bytes 18440 | tf_op jit(solution)/shard_map/ppermute | solution.py:49
  36.6 1.7 %shard_map.67 = (bf16[1536,768]{1,0:T(8,128)(2,1)S(1)}, f32[6,768]{1,0:T(8,128)S(1)}, bf16[768,512]{1,0:T(8,128)(2,1)S(1)}) custom-call(bf16[256,512]{1,0:T(8,128)(2,1)S(1)} %shard_map.60.a.refs_0_, bf16[256,512]{1,0:T(8,128)(2,1)S(1)} %collective-permute-done.1.refs_3_.refs_1_.above, bf16[256,512]{1,0:T(8,128)(2,1)S(1)} %collective-permute-done.2.refs_2_, ...), custom_call_target="tpu_custom_call" | custom-call | flops 12079595 | bytes 47185 | tf_op jit(solution)/shard_map/pallas_call | solution.py:229
  38.3 0.0 collective-permute-done.7.refs_1_
  38.3 0.0 collective-permute-done.8.refs_2_
  38.3 0.7 %collective-permute-done.9.refs_3_ = f32[3,512]{1,0:T(4,128)S(1)} collective-permute-done((f32[3,512]{1,0:T(4,128)S(1)}, f32[3,512]{1,0:T(4,128)S(1)}, u32[]{:S(2)}, u32[]{:S(2)}) %collective-permute-start.9) | collective-permute-done | bytes 6176 | tf_op jit(solution)/shard_map/ppermute | solution.py:49
  39.0 0.0 collective-permute-done.6.refs_2_.a
  39.0 1.6 %collective-permute-start.10 = (bf16[256,512]{1,0:T(8,128)(2,1)S(1)}, bf16[256,512]{1,0:T(8,128)(2,1)S(1)}, u32[]{:S(2)}, u32[]{:S(2)}) collective-permute-start(bf16[256,512]{1,0:T(8,128)(2,1)S(1)} %shard_map.71), channel_id=1, source_target_pairs={{16,0},{12,4},{24,8},{4,12},{0,16},{28,20},{8,24},{20,28},{17,1},{... | collective-permute-start | bytes 786440 | tf_op jit(solution)/shard_map/ppermute | solution.py:49
  40.6 1.5 %collective-permute-start.11 = (f32[2,512]{1,0:T(2,128)S(1)}, f32[2,512]{1,0:T(2,128)S(1)}, u32[]{:S(2)}, u32[]{:S(2)}) collective-permute-start(f32[2,512]{1,0:T(2,128)S(1)} %shard_map.69.refs_5_.refs_0_), channel_id=1, source_target_pairs={{8,0},{20,4},{0,8},{28,12},{24,16},{4,20},{16,24},{12,28},{9,1},{2... | collective-permute-start | bytes 12296 | tf_op jit(solution)/shard_map/ppermute | solution.py:49
  42.1 0.5 collective-permute-start.12
  42.6 1.5 %collective-permute-start.13 = (f32[2,512]{1,0:T(2,128)S(1)}, f32[2,512]{1,0:T(2,128)S(1)}, u32[]{:S(2)}, u32[]{:S(2)}) collective-permute-start(f32[2,512]{1,0:T(2,128)S(1)} %shard_map.69.refs_5_.refs_0_), channel_id=1, source_target_pairs={{24,0},{16,8},{8,16},{0,24},{25,1},{17,9},{9,17},{1,25},{26,2},{18... | collective-permute-start | bytes 12296 | tf_op jit(solution)/shard_map/ppermute | solution.py:49
  44.1 0.0 collective-permute-done.5.refs_0_.refs_3_
  44.1 2.2 %shard_map.70 = (bf16[1536,1024]{1,0:T(8,128)(2,1)S(1)}, f32[6,1024]{1,0:T(8,128)S(1)}, bf16[1024,512]{1,0:T(8,128)(2,1)S(1)}) custom-call(bf16[512,512]{1,0:T(8,128)(2,1)S(1)} %collective-permute-done.5.refs_0_.refs_3_, bf16[256,512]{1,0:T(8,128)(2,1)S(1)} %shard_map.64.refs_0_.below.refs_1_, bf16[256,512]{1,0:T(8,128)(2,1)S(1)} %collective-permute-done.6.refs_2_.a, ...), custom_call_target="tpu_custom_call" | custom-call | flops 1610612736 | bytes 5767168 | tf_op jit(solution)/shard_map/pallas_call | solution.py:229
  46.4 0.0 collective-permute-done.10.refs_0_
  46.4 0.7 %shard_map.72 = (bf16[1536,256]{1,0:T(8,128)(2,1)S(1)}, f32[6,256]{1,0:T(8,128)S(1)}, bf16[256,512]{1,0:T(8,128)(2,1)S(1)}) custom-call(bf16[256,512]{1,0:T(8,128)(2,1)S(1)} %collective-permute-done.10.refs_0_, bf16[6144,512]{1,0:T(8,128)(2,1)S(1)} %bitcast.3, f32[6,1024]{1,0:T(8,128)S(1)} %get-tuple-element.23.refs_2_.refs_5_), custom_call_target="tpu_custom_call" | custom-call | flops 402653184 | bytes 2621440 | tf_op jit(solution)/shard_map/pallas_call | solution.py:229
  47.1 0.0 collective-permute-done.11.refs_1_
  47.1 0.0 collective-permute-done.12.refs_2_
  47.1 0.0 collective-permute-done.13.refs_3_
  47.2 2.2 %shard_map.75 = (bf16[768,512]{1,0:T(8,128)(2,1)S(1)}, f32[1,768]{1,0:T(1,128)S(1)}) custom-call(bf16[1536,768]{1,0:T(8,128)(2,1)S(1)} %get-tuple-element.20.refs_0_, bf16[1536,1024]{1,0:T(8,128)(2,1)S(1)} %get-tuple-element.22.refs_1_, bf16[1536,256]{1,0:T(8,128)(2,1)S(1)} %get-tuple-element.24.refs_2_, bf16[768,512]{1,0:T(8,128)(2,1)S(1)} %get-tuple-element.25.refs_3_, ...), custom_call_target="tpu_custom_call" | custom-call | flops 1811939328 | bytes 7471104 | tf_op jit(solution)/shard_map/pallas_call | solution.py:280
  49.4 0.1 collective-permute-start.14
  49.5 0.5 collective-permute-start.15
  50.0 2.0 %shard_map.74 = (f32[768,512]{1,0:T(8,128)S(1)}, f32[1,768]{1,0:T(1,128)S(1)}) custom-call(bf16[1536,768]{1,0:T(8,128)(2,1)S(1)} %get-tuple-element.20.refs_0_, bf16[1536,1024]{1,0:T(8,128)(2,1)S(1)} %get-tuple-element.22.refs_1_, bf16[1536,256]{1,0:T(8,128)(2,1)S(1)} %get-tuple-element.24.refs_2_, bf16[768,512]{1,0:T(8,128)(2,1)S(1)} %get-tuple-element.25.refs_3_, ...), custom_call_target="tpu_custom_call" | custom-call | flops 1811939328 | bytes 7471104 | tf_op jit(solution)/shard_map/pallas_call | solution.py:280
  52.0 0.0 collective-permute-done.15.there_mass
  52.0 0.0 collective-permute-done.14.there
  52.0 1.8 %shard_map.76 = (f32[768,512]{1,0:T(8,128)}, f32[1,768]{1,0:T(1,128)}) custom-call(f32[768,512]{1,0:T(8,128)S(1)} %get-tuple-element.32.here, f32[1,768]{1,0:T(1,128)S(1)} %get-tuple-element.33.here_mass, bf16[768,512]{1,0:T(8,128)(2,1)S(1)} %collective-permute-done.14.there, f32[1,768]{1,0:T(1,128)S(1)} %collective-permute-done.15.there_mass), custom_call_target="tpu_custom_call" | custom-call | tf_op jit(solution)/shard_map/pallas_call | solution.py:310
  (10 shorter events, 0.2 us)
Async XLA Ops:
  1.7 8.1 %collective-permute-start = (bf16[128,512]{1,0:T(8,128)(2,1)S(1)}, bf16[128,512]{1,0:T(8,128)(2,1)S(1)}, u32[]{:S(2)}, u32[]{:S(2)}) collective-permute-start(bf16[128,512]{1,0:T(8,128)(2,1)S(1)} %multiply_convert_fusion.above), channel_id=1, source_target_pairs={{1,0},{0,1},{3,2},{2,3},{5,4},{4,5},{7,6},{6,7},{9,8},{8,9},{11,10... | collective-permute-start | bytes 393224 | tf_op jit(solution)/shard_map/ppermute | solution.py:49
  4.8 12.9 %collective-permute-start.3 = (bf16[128,512]{1,0:T(8,128)(2,1)S(1)}, bf16[128,512]{1,0:T(8,128)(2,1)S(1)}, u32[]{:S(2)}, u32[]{:S(2)}) collective-permute-start(bf16[128,512]{1,0:T(8,128)(2,1)S(1)} %multiply_convert_fusion.above), channel_id=1, source_target_pairs={{2,0},{3,1},{0,2},{1,3},{6,4},{7,5},{4,6},{5,7},{10,8},{11,9},{8,1... | collective-permute-start | bytes 393224 | tf_op jit(solution)/shard_map/ppermute | solution.py:49
  7.4 10.3 %collective-permute-start.4 = (bf16[128,512]{1,0:T(8,128)(2,1)S(1)}, bf16[128,512]{1,0:T(8,128)(2,1)S(1)}, u32[]{:S(2)}, u32[]{:S(2)}) collective-permute-start(bf16[128,512]{1,0:T(8,128)(2,1)S(1)} %multiply_convert_fusion.above), channel_id=1, source_target_pairs={{3,0},{2,1},{1,2},{0,3},{7,4},{6,5},{5,6},{4,7},{11,8},{10,9},{9,1... | collective-permute-start | bytes 393224 | tf_op jit(solution)/shard_map/ppermute | solution.py:49
  7.4 0.7 %copy-start = (s32[6144]{0:T(1024)S(1)}, s32[6144]{0:T(1024)}, u32[]{:S(2)}) copy-start(s32[6144]{0:T(1024)} %param.7) | copy-start | bytes 73732
  8.1 3.5 %slice-start = ((s8[6291456]{0:T(1024)(128)(4,1)}), s8[4194304]{0:T(1024)(128)(4,1)S(1)}, s32[]{:S(2)}) async-start(s8[6291456]{0:T(1024)(128)(4,1)} %bitcast.2), calls=%async_computation | async-start | bytes 8388608
  9.0 2.6 %slice-start.1 = ((s8[6291456]{0:T(1024)(128)(4,1)}), s8[2097152]{0:T(1024)(128)(4,1)S(1)}, s32[]{:S(2)}) async-start(s8[6291456]{0:T(1024)(128)(4,1)} %bitcast.2), calls=%async_computation.1 | async-start | bytes 4194304
  9.8 7.9 %collective-permute-start.1 = (bf16[256,512]{1,0:T(8,128)(2,1)S(1)}, bf16[256,512]{1,0:T(8,128)(2,1)S(1)}, u32[]{:S(2)}, u32[]{:S(2)}) collective-permute-start(bf16[256,512]{1,0:T(8,128)(2,1)S(1)} %shard_map.60.a.refs_0_), channel_id=1, source_target_pairs={{8,0},{20,4},{0,8},{28,12},{24,16},{4,20},{16,24},{12,28},{9,1},{2... | collective-permute-start | bytes 786440 | tf_op jit(solution)/shard_map/ppermute | solution.py:49
  20.7 23.4 %collective-permute-start.5 = (bf16[512,512]{1,0:T(8,128)(2,1)S(1)}, bf16[512,512]{1,0:T(8,128)(2,1)S(1)}, u32[]{:S(2)}, u32[]{:S(2)}) collective-permute-start(bf16[512,512]{1,0:T(8,128)(2,1)S(1)} %shard_map.68), channel_id=1, source_target_pairs={{16,0},{12,4},{24,8},{4,12},{0,16},{28,20},{8,24},{20,28},{17,1},{... | collective-permute-start | bytes 1572872 | tf_op jit(solution)/shard_map/ppermute | solution.py:49
  22.3 11.2 %collective-permute-start.2 = (bf16[256,512]{1,0:T(8,128)(2,1)S(1)}, bf16[256,512]{1,0:T(8,128)(2,1)S(1)}, u32[]{:S(2)}, u32[]{:S(2)}) collective-permute-start(bf16[256,512]{1,0:T(8,128)(2,1)S(1)} %shard_map.63), channel_id=1, source_target_pairs={{16,0},{12,4},{24,8},{4,12},{0,16},{28,20},{8,24},{20,28},{17,1},{... | collective-permute-start | bytes 786440 | tf_op jit(solution)/shard_map/ppermute | solution.py:49
  22.9 16.1 %collective-permute-start.6 = (bf16[256,512]{1,0:T(8,128)(2,1)S(1)}, bf16[256,512]{1,0:T(8,128)(2,1)S(1)}, u32[]{:S(2)}, u32[]{:S(2)}) collective-permute-start(bf16[256,512]{1,0:T(8,128)(2,1)S(1)} %shard_map.64.refs_0_.below.refs_1_), channel_id=1, source_target_pairs={{8,0},{20,4},{0,8},{28,12},{24,16},{4,20},{16,24},{12,28},{9,1},{2... | collective-permute-start | bytes 786440 | tf_op jit(solution)/shard_map/ppermute | solution.py:49
  24.4 13.9 %collective-permute-start.7 = (f32[3,512]{1,0:T(4,128)S(1)}, f32[3,512]{1,0:T(4,128)S(1)}, u32[]{:S(2)}, u32[]{:S(2)}) collective-permute-start(f32[3,512]{1,0:T(4,128)S(1)} %shard_map.66.refs_4_.refs_0_), channel_id=1, source_target_pairs={{1,0},{0,1},{3,2},{2,3},{5,4},{4,5},{7,6},{6,7},{9,8},{8,9},{11,10... | collective-permute-start | bytes 18440 | tf_op jit(solution)/shard_map/ppermute | solution.py:49
  26.3 12.0 %collective-permute-start.8 = (f32[3,512]{1,0:T(4,128)S(1)}, f32[3,512]{1,0:T(4,128)S(1)}, u32[]{:S(2)}, u32[]{:S(2)}) collective-permute-start(f32[3,512]{1,0:T(4,128)S(1)} %shard_map.66.refs_4_.refs_0_), channel_id=1, source_target_pairs={{2,0},{3,1},{0,2},{1,3},{6,4},{7,5},{4,6},{5,7},{10,8},{11,9},{8,1... | collective-permute-start | bytes 18440 | tf_op jit(solution)/shard_map/ppermute | solution.py:49
  33.5 5.4 %collective-permute-start.9 = (f32[3,512]{1,0:T(4,128)S(1)}, f32[3,512]{1,0:T(4,128)S(1)}, u32[]{:S(2)}, u32[]{:S(2)}) collective-permute-start(f32[3,512]{1,0:T(4,128)S(1)} %shard_map.66.refs_4_.refs_0_), channel_id=1, source_target_pairs={{3,0},{2,1},{1,2},{0,3},{7,4},{6,5},{5,6},{4,7},{11,8},{10,9},{9,1... | collective-permute-start | bytes 18440 | tf_op jit(solution)/shard_map/ppermute | solution.py:49
  39.0 7.3 %collective-permute-start.10 = (bf16[256,512]{1,0:T(8,128)(2,1)S(1)}, bf16[256,512]{1,0:T(8,128)(2,1)S(1)}, u32[]{:S(2)}, u32[]{:S(2)}) collective-permute-start(bf16[256,512]{1,0:T(8,128)(2,1)S(1)} %shard_map.71), channel_id=1, source_target_pairs={{16,0},{12,4},{24,8},{4,12},{0,16},{28,20},{8,24},{20,28},{17,1},{... | collective-permute-start | bytes 786440 | tf_op jit(solution)/shard_map/ppermute | solution.py:49
  40.6 6.5 %collective-permute-start.11 = (f32[2,512]{1,0:T(2,128)S(1)}, f32[2,512]{1,0:T(2,128)S(1)}, u32[]{:S(2)}, u32[]{:S(2)}) collective-permute-start(f32[2,512]{1,0:T(2,128)S(1)} %shard_map.69.refs_5_.refs_0_), channel_id=1, source_target_pairs={{8,0},{20,4},{0,8},{28,12},{24,16},{4,20},{16,24},{12,28},{9,1},{2... | collective-permute-start | bytes 12296 | tf_op jit(solution)/shard_map/ppermute | solution.py:49
  42.1 5.0 %collective-permute-start.12 = (f32[2,512]{1,0:T(2,128)S(1)}, f32[2,512]{1,0:T(2,128)S(1)}, u32[]{:S(2)}, u32[]{:S(2)}) collective-permute-start(f32[2,512]{1,0:T(2,128)S(1)} %shard_map.69.refs_5_.refs_0_), channel_id=1, source_target_pairs={{16,0},{12,4},{24,8},{4,12},{0,16},{28,20},{8,24},{20,28},{17,1},{... | collective-permute-start | bytes 12296 | tf_op jit(solution)/shard_map/ppermute | solution.py:49
  42.6 4.5 %collective-permute-start.13 = (f32[2,512]{1,0:T(2,128)S(1)}, f32[2,512]{1,0:T(2,128)S(1)}, u32[]{:S(2)}, u32[]{:S(2)}) collective-permute-start(f32[2,512]{1,0:T(2,128)S(1)} %shard_map.69.refs_5_.refs_0_), channel_id=1, source_target_pairs={{24,0},{16,8},{8,16},{0,24},{25,1},{17,9},{9,17},{1,25},{26,2},{18... | collective-permute-start | bytes 12296 | tf_op jit(solution)/shard_map/ppermute | solution.py:49
  49.4 2.6 %collective-permute-start.14 = (bf16[768,512]{1,0:T(8,128)(2,1)S(1)}, bf16[768,512]{1,0:T(8,128)(2,1)S(1)}, u32[]{:S(2)}, u32[]{:S(2)}) collective-permute-start(bf16[768,512]{1,0:T(8,128)(2,1)S(1)} %get-tuple-element.34), channel_id=1, source_target_pairs={{4,0},{0,4},{5,1},{1,5},{6,2},{2,6},{7,3},{3,7},{12,8},{8,12},{13,... | collective-permute-start | bytes 2359304 | tf_op jit(solution)/shard_map/ppermute | solution.py:49
  49.5 2.5 %collective-permute-start.15 = (f32[1,768]{1,0:T(1,128)S(1)}, f32[1,768]{1,0:T(1,128)S(1)}, u32[]{:S(2)}, u32[]{:S(2)}) collective-permute-start(f32[1,768]{1,0:T(1,128)S(1)} %get-tuple-element.35), channel_id=1, source_target_pairs={{4,0},{0,4},{5,1},{1,5},{6,2},{2,6},{7,3},{3,7},{12,8},{8,12},{13,... | collective-permute-start | bytes 9224 | tf_op jit(solution)/shard_map/ppermute | solution.py:49

commit v19 on v18

--- a/solution.py
+++ b/solution.py
@@ -355,7 +355,7 @@
     goal = goal_call(rate, stat, *(along_z(stat, by) for by in (1, 2, 3)), bundles[0][1])
     across_23 = turn_back(hold(first_23, goal))
 
-    bundles.append(expand((across_01, near_23, first_23, second_23), centroids, goal))
+    bundles.append(expand((across_01, near_23, first_23, second_23), centroids, goal, declared=0.01))
     bundles.append(expand((across_23,), centroids, bundles[1][1]))
     expos, tops, points = zip(*bundles)
     goals = [goal, turn(goal), turn_back(goal), around(goal, 3)]

time: 54.2 us -> 46.8 us (0.86)
  waiting for transfers between devices: 10.8 us -> 5.08 us
  starting transfers between devices: 22.8 us -> 21.2 us
    ppermute x16, waiting for transfers between devices: 10.8 us -> 5.08 us  [exchange(): return lax.ppermute(a, axes, [(partner(at), at) for at in range(count)])]
    ppermute x16, starting transfers between devices: 22.8 us -> 21.2 us  [exchange(): return lax.ppermute(a, axes, [(partner(at), at) for at in range(count)])]
  transfers between devices with their start and end apart: 16 -> 16, of which waited for: 4 -> 5; matrix products, arithmetic and copies ran while one was open for 0% -> 0% of each run, Pallas kernels for 20% -> 29%
where the time goes in v19:
time: 46.8 us; the launch traced here: 46.6 us
  starting transfers between devices  21.2 us (45%)
  Pallas kernels  17.5 us (37%)
  waiting for transfers between devices  5.08 us (11%)
  other arithmetic  1.05 us (2%)
  between operations  1 us (2%)
  local copies, waits for them, and re-layouts  0.75 us (2%)
    ppermute x16, starting transfers between devices, exchange(): return lax.ppermute(a, axes, [(partner(at), at) for at in range(count)])  21.2 us
    pallas_call x2, Pallas kernels, totals_call(): pl.pallas_call(functools.partial(totals_kernel, rate, block, len(pieces))...  5.81 us
    ppermute x16, waiting for transfers between devices, exchange(): return lax.ppermute(a, axes, [(partner(at), at) for at in range(count)])  5.08 us
    pallas_call x3, Pallas kernels, expo_call(): pl.pallas_call(functools.partial(expo_kernel, rate, block, spots), in_spe...  4.62 us
    pallas_call x2, Pallas kernels, sums_call(): pl.pallas_call(functools.partial(sums_kernel, n, block, side), in_specs=i...  4.25 us
    pallas_call x1, Pallas kernels, add_call(): pl.pallas_call(functools.partial(add_kernel, block), in_specs=in_vmem(4),...  1.79 us
    convert_element_type x1, other arithmetic, to_points(): return (scaled.astype(jnp.float32) * 2.0 ** (-16)).astype(jnp.bfloat16)  1.05 us
  transfers between devices with their start and end apart: 16, of which 5 were waited for; matrix products, arithmetic and copies ran while one was open for 0% of the time, Pallas kernels for 29%

profile of v19, /device:TPU:0, one launch (start us, length us, event | category | flops | bytes accessed | tf_op | source)
XLA Modules:
  0.0 46.6 jit_solution(18446359827589119035)
XLA Ops:
  0.6 1.1 %multiply_convert_fusion.above = bf16[128,512]{1,0:T(8,128)(2,1)S(1)} fusion(s32[128,512]{1,0:T(8,128)} %param.4, s32[128]{0:T(128)} %param.5), kind=kLoop, calls=%fused_computation | loop fusion | flops 327680 | bytes 393728 | tf_op jit(solution)/shard_map/convert_element_type | solution.py:17
  1.7 3.1 %collective-permute-start = (bf16[128,512]{1,0:T(8,128)(2,1)S(1)}, bf16[128,512]{1,0:T(8,128)(2,1)S(1)}, u32[]{:S(2)}, u32[]{:S(2)}) collective-permute-start(bf16[128,512]{1,0:T(8,128)(2,1)S(1)} %multiply_convert_fusion.above), channel_id=1, source_target_pairs={{1,0},{0,1},{3,2},{2,3},{5,4},{4,5},{7,6},{6,7},{9,8},{8,9},{11,10... | collective-permute-start | bytes 393224 | tf_op jit(solution)/shard_map/ppermute | solution.py:49
  4.8 2.6 %collective-permute-start.3 = (bf16[128,512]{1,0:T(8,128)(2,1)S(1)}, bf16[128,512]{1,0:T(8,128)(2,1)S(1)}, u32[]{:S(2)}, u32[]{:S(2)}) collective-permute-start(bf16[128,512]{1,0:T(8,128)(2,1)S(1)} %multiply_convert_fusion.above), channel_id=1, source_target_pairs={{2,0},{3,1},{0,2},{1,3},{6,4},{7,5},{4,6},{5,7},{10,8},{11,9},{8,1... | collective-permute-start | bytes 393224 | tf_op jit(solution)/shard_map/ppermute | solution.py:49
  7.4 0.0 collective-permute-start.4
  7.4 0.0 copy-start
  7.4 0.7 %copy-done = s32[6144]{0:T(1024)S(1)} copy-done((s32[6144]{0:T(1024)S(1)}, s32[6144]{0:T(1024)}, u32[]{:S(2)}) %copy-start) | copy-done | bytes 24600
  8.1 0.0 slice-start
  8.1 0.9 %shard_map.59.refs_0_.refs_2_ = f32[6144,128]{1,0:T(8,128)S(1)} custom-call(s32[48,128]{1,0:T(8,128)S(1)} %bitcast.4), custom_call_target="tpu_custom_call" | custom-call | flops 2000000000 | tf_op jit(solution)/shard_map/pallas_call | solution.py:114
  9.0 0.0 slice-start.1
  9.0 0.8 %collective-permute-done.below = bf16[128,512]{1,0:T(8,128)(2,1)S(1)} collective-permute-done((bf16[128,512]{1,0:T(8,128)(2,1)S(1)}, bf16[128,512]{1,0:T(8,128)(2,1)S(1)}, u32[]{:S(2)}, u32[]{:S(2)}) %collective-permute-start) | collective-permute-done | bytes 131104 | tf_op jit(solution)/shard_map/ppermute | solution.py:49
  9.8 1.8 %collective-permute-start.1 = (bf16[256,512]{1,0:T(8,128)(2,1)S(1)}, bf16[256,512]{1,0:T(8,128)(2,1)S(1)}, u32[]{:S(2)}, u32[]{:S(2)}) collective-permute-start(bf16[256,512]{1,0:T(8,128)(2,1)S(1)} %shard_map.60.a.refs_0_), channel_id=1, source_target_pairs={{8,0},{20,4},{0,8},{28,12},{24,16},{4,20},{16,24},{12,28},{9,1},{2... | collective-permute-start | bytes 786440 | tf_op jit(solution)/shard_map/ppermute | solution.py:49
  11.6 0.0 slice-done
  11.6 0.0 slice-done.1
  11.7 2.9 %shard_map.62.refs_0_.left = f32[3,256]{1,0:T(4,128)S(1)} custom-call(bf16[256,512]{1,0:T(8,128)(2,1)S(1)} %shard_map.61.refs_0_, bf16[6144,512]{1,0:T(8,128)(2,1)S(1)} %bitcast.3, f32[6144,128]{1,0:T(8,128)S(1)} %shard_map.59.refs_0_.refs_2_), custom_call_target="tpu_custom_call" | custom-call | flops 1610612736 | bytes 6291456 | tf_op jit(solution)/shard_map/pallas_call | solution.py:154
  14.6 1.6 %collective-permute-start.2 = (bf16[256,512]{1,0:T(8,128)(2,1)S(1)}, bf16[256,512]{1,0:T(8,128)(2,1)S(1)}, u32[]{:S(2)}, u32[]{:S(2)}) collective-permute-start(bf16[256,512]{1,0:T(8,128)(2,1)S(1)} %shard_map.63), channel_id=1, source_target_pairs={{16,0},{12,4},{24,8},{4,12},{0,16},{28,20},{8,24},{20,28},{17,1},{... | collective-permute-start | bytes 786440 | tf_op jit(solution)/shard_map/ppermute | solution.py:49
  16.2 1.5 %collective-permute-done.3.above = bf16[128,512]{1,0:T(8,128)(2,1)S(1)} collective-permute-done((bf16[128,512]{1,0:T(8,128)(2,1)S(1)}, bf16[128,512]{1,0:T(8,128)(2,1)S(1)}, u32[]{:S(2)}, u32[]{:S(2)}) %collective-permute-start.3) | collective-permute-done | bytes 131104 | tf_op jit(solution)/shard_map/ppermute | solution.py:49
  17.7 0.0 collective-permute-done.4.below
  17.7 0.0 collective-permute-done.1.refs_3_.refs_1_.above
  17.7 2.9 %shard_map.65.right.refs_0_ = f32[3,256]{1,0:T(4,128)S(1)} custom-call(bf16[256,512]{1,0:T(8,128)(2,1)S(1)} %shard_map.64.refs_0_.below.refs_1_, bf16[6144,512]{1,0:T(8,128)(2,1)S(1)} %bitcast.3, f32[6144,128]{1,0:T(8,128)S(1)} %shard_map.59.refs_0_.refs_2_, bf16[256,512]{1,0:T(8,128)(2,1)S(1)} %collective-permute-done.1.refs_3_.refs_1_.above), custom_call_target="tpu_custom_call" | custom-call | flops 1610612736 | bytes 6291456 | tf_op jit(solution)/shard_map/pallas_call | solution.py:154
  20.7 1.6 %collective-permute-start.5 = (bf16[512,512]{1,0:T(8,128)(2,1)S(1)}, bf16[512,512]{1,0:T(8,128)(2,1)S(1)}, u32[]{:S(2)}, u32[]{:S(2)}) collective-permute-start(bf16[512,512]{1,0:T(8,128)(2,1)S(1)} %shard_map.68), channel_id=1, source_target_pairs={{16,0},{12,4},{24,8},{4,12},{0,16},{28,20},{8,24},{20,28},{17,1},{... | collective-permute-start | bytes 1572872 | tf_op jit(solution)/shard_map/ppermute | solution.py:49
  22.3 1.5 %collective-permute-start.6 = (bf16[256,512]{1,0:T(8,128)(2,1)S(1)}, bf16[256,512]{1,0:T(8,128)(2,1)S(1)}, u32[]{:S(2)}, u32[]{:S(2)}) collective-permute-start(bf16[256,512]{1,0:T(8,128)(2,1)S(1)} %shard_map.64.refs_0_.below.refs_1_), channel_id=1, source_target_pairs={{8,0},{20,4},{0,8},{28,12},{24,16},{4,20},{16,24},{12,28},{9,1},{2... | collective-permute-start | bytes 786440 | tf_op jit(solution)/shard_map/ppermute | solution.py:49
  23.8 2.0 %collective-permute-start.7 = (f32[3,512]{1,0:T(4,128)S(1)}, f32[3,512]{1,0:T(4,128)S(1)}, u32[]{:S(2)}, u32[]{:S(2)}) collective-permute-start(f32[3,512]{1,0:T(4,128)S(1)} %shard_map.66.refs_4_.refs_0_), channel_id=1, source_target_pairs={{1,0},{0,1},{3,2},{2,3},{5,4},{4,5},{7,6},{6,7},{9,8},{8,9},{11,10... | collective-permute-start | bytes 18440 | tf_op jit(solution)/shard_map/ppermute | solution.py:49
  25.7 1.3 %collective-permute-start.8 = (f32[3,512]{1,0:T(4,128)S(1)}, f32[3,512]{1,0:T(4,128)S(1)}, u32[]{:S(2)}, u32[]{:S(2)}) collective-permute-start(f32[3,512]{1,0:T(4,128)S(1)} %shard_map.66.refs_4_.refs_0_), channel_id=1, source_target_pairs={{2,0},{3,1},{0,2},{1,3},{6,4},{7,5},{4,6},{5,7},{10,8},{11,9},{8,1... | collective-permute-start | bytes 18440 | tf_op jit(solution)/shard_map/ppermute | solution.py:49
  27.1 0.0 collective-permute-done.2.refs_2_
  27.1 1.2 %collective-permute-start.9 = (f32[3,512]{1,0:T(4,128)S(1)}, f32[3,512]{1,0:T(4,128)S(1)}, u32[]{:S(2)}, u32[]{:S(2)}) collective-permute-start(f32[3,512]{1,0:T(4,128)S(1)} %shard_map.66.refs_4_.refs_0_), channel_id=1, source_target_pairs={{3,0},{2,1},{1,2},{0,3},{7,4},{6,5},{5,6},{4,7},{11,8},{10,9},{9,1... | collective-permute-start | bytes 18440 | tf_op jit(solution)/shard_map/ppermute | solution.py:49
  28.2 1.7 %shard_map.67 = (bf16[1536,768]{1,0:T(8,128)(2,1)S(1)}, f32[6,768]{1,0:T(8,128)S(1)}, bf16[768,512]{1,0:T(8,128)(2,1)S(1)}) custom-call(bf16[256,512]{1,0:T(8,128)(2,1)S(1)} %shard_map.60.a.refs_0_, bf16[256,512]{1,0:T(8,128)(2,1)S(1)} %collective-permute-done.1.refs_3_.refs_1_.above, bf16[256,512]{1,0:T(8,128)(2,1)S(1)} %collective-permute-done.2.refs_2_, ...), custom_call_target="tpu_custom_call" | custom-call | flops 12079595 | bytes 47185 | tf_op jit(solution)/shard_map/pallas_call | solution.py:229
  29.9 0.0 collective-permute-done.7.refs_1_
  29.9 0.4 collective-permute-done.8.refs_2_
  30.3 2.2 %collective-permute-done.9.refs_3_ = f32[3,512]{1,0:T(4,128)S(1)} collective-permute-done((f32[3,512]{1,0:T(4,128)S(1)}, f32[3,512]{1,0:T(4,128)S(1)}, u32[]{:S(2)}, u32[]{:S(2)}) %collective-permute-start.9) | collective-permute-done | bytes 6176 | tf_op jit(solution)/shard_map/ppermute | solution.py:49
  32.5 0.0 collective-permute-done.6.refs_2_.a
  32.6 0.6 %collective-permute-start.10 = (bf16[256,512]{1,0:T(8,128)(2,1)S(1)}, bf16[256,512]{1,0:T(8,128)(2,1)S(1)}, u32[]{:S(2)}, u32[]{:S(2)}) collective-permute-start(bf16[256,512]{1,0:T(8,128)(2,1)S(1)} %shard_map.71), channel_id=1, source_target_pairs={{16,0},{12,4},{24,8},{4,12},{0,16},{28,20},{8,24},{20,28},{17,1},{... | collective-permute-start | bytes 786440 | tf_op jit(solution)/shard_map/ppermute | solution.py:49
  33.2 0.5 %collective-permute-start.11 = (f32[2,512]{1,0:T(2,128)S(1)}, f32[2,512]{1,0:T(2,128)S(1)}, u32[]{:S(2)}, u32[]{:S(2)}) collective-permute-start(f32[2,512]{1,0:T(2,128)S(1)} %shard_map.69.refs_5_.refs_0_), channel_id=1, source_target_pairs={{8,0},{20,4},{0,8},{28,12},{24,16},{4,20},{16,24},{12,28},{9,1},{2... | collective-permute-start | bytes 12296 | tf_op jit(solution)/shard_map/ppermute | solution.py:49
  33.7 1.5 %collective-permute-start.12 = (f32[2,512]{1,0:T(2,128)S(1)}, f32[2,512]{1,0:T(2,128)S(1)}, u32[]{:S(2)}, u32[]{:S(2)}) collective-permute-start(f32[2,512]{1,0:T(2,128)S(1)} %shard_map.69.refs_5_.refs_0_), channel_id=1, source_target_pairs={{16,0},{12,4},{24,8},{4,12},{0,16},{28,20},{8,24},{20,28},{17,1},{... | collective-permute-start | bytes 12296 | tf_op jit(solution)/shard_map/ppermute | solution.py:49
  35.2 1.4 %collective-permute-start.13 = (f32[2,512]{1,0:T(2,128)S(1)}, f32[2,512]{1,0:T(2,128)S(1)}, u32[]{:S(2)}, u32[]{:S(2)}) collective-permute-start(f32[2,512]{1,0:T(2,128)S(1)} %shard_map.69.refs_5_.refs_0_), channel_id=1, source_target_pairs={{24,0},{16,8},{8,16},{0,24},{25,1},{17,9},{9,17},{1,25},{26,2},{18... | collective-permute-start | bytes 12296 | tf_op jit(solution)/shard_map/ppermute | solution.py:49
  36.7 0.0 collective-permute-done.5.refs_0_.refs_3_
  36.7 2.2 %shard_map.70 = (bf16[1536,1024]{1,0:T(8,128)(2,1)S(1)}, f32[6,1024]{1,0:T(8,128)S(1)}, bf16[1024,512]{1,0:T(8,128)(2,1)S(1)}) custom-call(bf16[512,512]{1,0:T(8,128)(2,1)S(1)} %collective-permute-done.5.refs_0_.refs_3_, bf16[256,512]{1,0:T(8,128)(2,1)S(1)} %shard_map.64.refs_0_.below.refs_1_, bf16[256,512]{1,0:T(8,128)(2,1)S(1)} %collective-permute-done.6.refs_2_.a, ...), custom_call_target="tpu_custom_call" | custom-call | flops 16106127 | bytes 57671 | tf_op jit(solution)/shard_map/pallas_call | solution.py:229
  38.9 0.1 collective-permute-done.10.refs_0_
  39.0 0.7 %shard_map.72 = (bf16[1536,256]{1,0:T(8,128)(2,1)S(1)}, f32[6,256]{1,0:T(8,128)S(1)}, bf16[256,512]{1,0:T(8,128)(2,1)S(1)}) custom-call(bf16[256,512]{1,0:T(8,128)(2,1)S(1)} %collective-permute-done.10.refs_0_, bf16[6144,512]{1,0:T(8,128)(2,1)S(1)} %bitcast.3, f32[6,1024]{1,0:T(8,128)S(1)} %get-tuple-element.23.refs_2_.refs_5_), custom_call_target="tpu_custom_call" | custom-call | flops 402653184 | bytes 2621440 | tf_op jit(solution)/shard_map/pallas_call | solution.py:229
  39.7 0.0 collective-permute-done.11.refs_1_
  39.8 0.0 collective-permute-done.12.refs_2_
  39.8 0.0 collective-permute-done.13.refs_3_
  39.8 2.2 %shard_map.75 = (bf16[768,512]{1,0:T(8,128)(2,1)S(1)}, f32[1,768]{1,0:T(1,128)S(1)}) custom-call(bf16[1536,768]{1,0:T(8,128)(2,1)S(1)} %get-tuple-element.20.refs_0_, bf16[1536,1024]{1,0:T(8,128)(2,1)S(1)} %get-tuple-element.22.refs_1_, bf16[1536,256]{1,0:T(8,128)(2,1)S(1)} %get-tuple-element.24.refs_2_, bf16[768,512]{1,0:T(8,128)(2,1)S(1)} %get-tuple-element.25.refs_3_, ...), custom_call_target="tpu_custom_call" | custom-call | flops 1811939328 | bytes 7471104 | tf_op jit(solution)/shard_map/pallas_call | solution.py:280
  42.1 0.1 collective-permute-start.14
  42.1 0.5 %collective-permute-start.15 = (f32[1,768]{1,0:T(1,128)S(1)}, f32[1,768]{1,0:T(1,128)S(1)}, u32[]{:S(2)}, u32[]{:S(2)}) collective-permute-start(f32[1,768]{1,0:T(1,128)S(1)} %get-tuple-element.35), channel_id=1, source_target_pairs={{4,0},{0,4},{5,1},{1,5},{6,2},{2,6},{7,3},{3,7},{12,8},{8,12},{13,... | collective-permute-start | bytes 9224 | tf_op jit(solution)/shard_map/ppermute | solution.py:49
  42.6 2.0 %shard_map.74 = (f32[768,512]{1,0:T(8,128)S(1)}, f32[1,768]{1,0:T(1,128)S(1)}) custom-call(bf16[1536,768]{1,0:T(8,128)(2,1)S(1)} %get-tuple-element.20.refs_0_, bf16[1536,1024]{1,0:T(8,128)(2,1)S(1)} %get-tuple-element.22.refs_1_, bf16[1536,256]{1,0:T(8,128)(2,1)S(1)} %get-tuple-element.24.refs_2_, bf16[768,512]{1,0:T(8,128)(2,1)S(1)} %get-tuple-element.25.refs_3_, ...), custom_call_target="tpu_custom_call" | custom-call | flops 1811939328 | bytes 7471104 | tf_op jit(solution)/shard_map/pallas_call | solution.py:280
  44.6 0.0 collective-permute-done.15.there_mass
  44.7 0.0 collective-permute-done.14.there
  44.7 1.8 %shard_map.76 = (f32[768,512]{1,0:T(8,128)}, f32[1,768]{1,0:T(1,128)}) custom-call(f32[768,512]{1,0:T(8,128)S(1)} %get-tuple-element.32.here, f32[1,768]{1,0:T(1,128)S(1)} %get-tuple-element.33.here_mass, bf16[768,512]{1,0:T(8,128)(2,1)S(1)} %collective-permute-done.14.there, f32[1,768]{1,0:T(1,128)S(1)} %collective-permute-done.15.there_mass), custom_call_target="tpu_custom_call" | custom-call | tf_op jit(solution)/shard_map/pallas_call | solution.py:310
  (10 shorter events, 0.2 us)
Async XLA Ops:
  1.7 8.1 %collective-permute-start = (bf16[128,512]{1,0:T(8,128)(2,1)S(1)}, bf16[128,512]{1,0:T(8,128)(2,1)S(1)}, u32[]{:S(2)}, u32[]{:S(2)}) collective-permute-start(bf16[128,512]{1,0:T(8,128)(2,1)S(1)} %multiply_convert_fusion.above), channel_id=1, source_target_pairs={{1,0},{0,1},{3,2},{2,3},{5,4},{4,5},{7,6},{6,7},{9,8},{8,9},{11,10... | collective-permute-start | bytes 393224 | tf_op jit(solution)/shard_map/ppermute | solution.py:49
  4.8 12.9 %collective-permute-start.3 = (bf16[128,512]{1,0:T(8,128)(2,1)S(1)}, bf16[128,512]{1,0:T(8,128)(2,1)S(1)}, u32[]{:S(2)}, u32[]{:S(2)}) collective-permute-start(bf16[128,512]{1,0:T(8,128)(2,1)S(1)} %multiply_convert_fusion.above), channel_id=1, source_target_pairs={{2,0},{3,1},{0,2},{1,3},{6,4},{7,5},{4,6},{5,7},{10,8},{11,9},{8,1... | collective-permute-start | bytes 393224 | tf_op jit(solution)/shard_map/ppermute | solution.py:49
  7.4 10.3 %collective-permute-start.4 = (bf16[128,512]{1,0:T(8,128)(2,1)S(1)}, bf16[128,512]{1,0:T(8,128)(2,1)S(1)}, u32[]{:S(2)}, u32[]{:S(2)}) collective-permute-start(bf16[128,512]{1,0:T(8,128)(2,1)S(1)} %multiply_convert_fusion.above), channel_id=1, source_target_pairs={{3,0},{2,1},{1,2},{0,3},{7,4},{6,5},{5,6},{4,7},{11,8},{10,9},{9,1... | collective-permute-start | bytes 393224 | tf_op jit(solution)/shard_map/ppermute | solution.py:49
  7.4 0.7 %copy-start = (s32[6144]{0:T(1024)S(1)}, s32[6144]{0:T(1024)}, u32[]{:S(2)}) copy-start(s32[6144]{0:T(1024)} %param.7) | copy-start | bytes 73732
  8.1 3.5 %slice-start = ((s8[6291456]{0:T(1024)(128)(4,1)}), s8[4194304]{0:T(1024)(128)(4,1)S(1)}, s32[]{:S(2)}) async-start(s8[6291456]{0:T(1024)(128)(4,1)} %bitcast.2), calls=%async_computation | async-start | bytes 8388608
  9.0 2.6 %slice-start.1 = ((s8[6291456]{0:T(1024)(128)(4,1)}), s8[2097152]{0:T(1024)(128)(4,1)S(1)}, s32[]{:S(2)}) async-start(s8[6291456]{0:T(1024)(128)(4,1)} %bitcast.2), calls=%async_computation.1 | async-start | bytes 4194304
  9.8 7.9 %collective-permute-start.1 = (bf16[256,512]{1,0:T(8,128)(2,1)S(1)}, bf16[256,512]{1,0:T(8,128)(2,1)S(1)}, u32[]{:S(2)}, u32[]{:S(2)}) collective-permute-start(bf16[256,512]{1,0:T(8,128)(2,1)S(1)} %shard_map.60.a.refs_0_), channel_id=1, source_target_pairs={{8,0},{20,4},{0,8},{28,12},{24,16},{4,20},{16,24},{12,28},{9,1},{2... | collective-permute-start | bytes 786440 | tf_op jit(solution)/shard_map/ppermute | solution.py:49
  14.6 12.5 %collective-permute-start.2 = (bf16[256,512]{1,0:T(8,128)(2,1)S(1)}, bf16[256,512]{1,0:T(8,128)(2,1)S(1)}, u32[]{:S(2)}, u32[]{:S(2)}) collective-permute-start(bf16[256,512]{1,0:T(8,128)(2,1)S(1)} %shard_map.63), channel_id=1, source_target_pairs={{16,0},{12,4},{24,8},{4,12},{0,16},{28,20},{8,24},{20,28},{17,1},{... | collective-permute-start | bytes 786440 | tf_op jit(solution)/shard_map/ppermute | solution.py:49
  20.7 16.0 %collective-permute-start.5 = (bf16[512,512]{1,0:T(8,128)(2,1)S(1)}, bf16[512,512]{1,0:T(8,128)(2,1)S(1)}, u32[]{:S(2)}, u32[]{:S(2)}) collective-permute-start(bf16[512,512]{1,0:T(8,128)(2,1)S(1)} %shard_map.68), channel_id=1, source_target_pairs={{16,0},{12,4},{24,8},{4,12},{0,16},{28,20},{8,24},{20,28},{17,1},{... | collective-permute-start | bytes 1572872 | tf_op jit(solution)/shard_map/ppermute | solution.py:49
  22.3 10.3 %collective-permute-start.6 = (bf16[256,512]{1,0:T(8,128)(2,1)S(1)}, bf16[256,512]{1,0:T(8,128)(2,1)S(1)}, u32[]{:S(2)}, u32[]{:S(2)}) collective-permute-start(bf16[256,512]{1,0:T(8,128)(2,1)S(1)} %shard_map.64.refs_0_.below.refs_1_), channel_id=1, source_target_pairs={{8,0},{20,4},{0,8},{28,12},{24,16},{4,20},{16,24},{12,28},{9,1},{2... | collective-permute-start | bytes 786440 | tf_op jit(solution)/shard_map/ppermute | solution.py:49
  23.8 6.1 %collective-permute-start.7 = (f32[3,512]{1,0:T(4,128)S(1)}, f32[3,512]{1,0:T(4,128)S(1)}, u32[]{:S(2)}, u32[]{:S(2)}) collective-permute-start(f32[3,512]{1,0:T(4,128)S(1)} %shard_map.66.refs_4_.refs_0_), channel_id=1, source_target_pairs={{1,0},{0,1},{3,2},{2,3},{5,4},{4,5},{7,6},{6,7},{9,8},{8,9},{11,10... | collective-permute-start | bytes 18440 | tf_op jit(solution)/shard_map/ppermute | solution.py:49
  25.7 4.5 %collective-permute-start.8 = (f32[3,512]{1,0:T(4,128)S(1)}, f32[3,512]{1,0:T(4,128)S(1)}, u32[]{:S(2)}, u32[]{:S(2)}) collective-permute-start(f32[3,512]{1,0:T(4,128)S(1)} %shard_map.66.refs_4_.refs_0_), channel_id=1, source_target_pairs={{2,0},{3,1},{0,2},{1,3},{6,4},{7,5},{4,6},{5,7},{10,8},{11,9},{8,1... | collective-permute-start | bytes 18440 | tf_op jit(solution)/shard_map/ppermute | solution.py:49
  27.1 5.4 %collective-permute-start.9 = (f32[3,512]{1,0:T(4,128)S(1)}, f32[3,512]{1,0:T(4,128)S(1)}, u32[]{:S(2)}, u32[]{:S(2)}) collective-permute-start(f32[3,512]{1,0:T(4,128)S(1)} %shard_map.66.refs_4_.refs_0_), channel_id=1, source_target_pairs={{3,0},{2,1},{1,2},{0,3},{7,4},{6,5},{5,6},{4,7},{11,8},{10,9},{9,1... | collective-permute-start | bytes 18440 | tf_op jit(solution)/shard_map/ppermute | solution.py:49
  32.6 6.4 %collective-permute-start.10 = (bf16[256,512]{1,0:T(8,128)(2,1)S(1)}, bf16[256,512]{1,0:T(8,128)(2,1)S(1)}, u32[]{:S(2)}, u32[]{:S(2)}) collective-permute-start(bf16[256,512]{1,0:T(8,128)(2,1)S(1)} %shard_map.71), channel_id=1, source_target_pairs={{16,0},{12,4},{24,8},{4,12},{0,16},{28,20},{8,24},{20,28},{17,1},{... | collective-permute-start | bytes 786440 | tf_op jit(solution)/shard_map/ppermute | solution.py:49
  33.2 6.6 %collective-permute-start.11 = (f32[2,512]{1,0:T(2,128)S(1)}, f32[2,512]{1,0:T(2,128)S(1)}, u32[]{:S(2)}, u32[]{:S(2)}) collective-permute-start(f32[2,512]{1,0:T(2,128)S(1)} %shard_map.69.refs_5_.refs_0_), channel_id=1, source_target_pairs={{8,0},{20,4},{0,8},{28,12},{24,16},{4,20},{16,24},{12,28},{9,1},{2... | collective-permute-start | bytes 12296 | tf_op jit(solution)/shard_map/ppermute | solution.py:49
  33.7 6.1 %collective-permute-start.12 = (f32[2,512]{1,0:T(2,128)S(1)}, f32[2,512]{1,0:T(2,128)S(1)}, u32[]{:S(2)}, u32[]{:S(2)}) collective-permute-start(f32[2,512]{1,0:T(2,128)S(1)} %shard_map.69.refs_5_.refs_0_), channel_id=1, source_target_pairs={{16,0},{12,4},{24,8},{4,12},{0,16},{28,20},{8,24},{20,28},{17,1},{... | collective-permute-start | bytes 12296 | tf_op jit(solution)/shard_map/ppermute | solution.py:49
  35.2 4.5 %collective-permute-start.13 = (f32[2,512]{1,0:T(2,128)S(1)}, f32[2,512]{1,0:T(2,128)S(1)}, u32[]{:S(2)}, u32[]{:S(2)}) collective-permute-start(f32[2,512]{1,0:T(2,128)S(1)} %shard_map.69.refs_5_.refs_0_), channel_id=1, source_target_pairs={{24,0},{16,8},{8,16},{0,24},{25,1},{17,9},{9,17},{1,25},{26,2},{18... | collective-permute-start | bytes 12296 | tf_op jit(solution)/shard_map/ppermute | solution.py:49
  42.1 2.6 %collective-permute-start.14 = (bf16[768,512]{1,0:T(8,128)(2,1)S(1)}, bf16[768,512]{1,0:T(8,128)(2,1)S(1)}, u32[]{:S(2)}, u32[]{:S(2)}) collective-permute-start(bf16[768,512]{1,0:T(8,128)(2,1)S(1)} %get-tuple-element.34), channel_id=1, source_target_pairs={{4,0},{0,4},{5,1},{1,5},{6,2},{2,6},{7,3},{3,7},{12,8},{8,12},{13,... | collective-permute-start | bytes 2359304 | tf_op jit(solution)/shard_map/ppermute | solution.py:49
  42.1 2.5 %collective-permute-start.15 = (f32[1,768]{1,0:T(1,128)S(1)}, f32[1,768]{1,0:T(1,128)S(1)}, u32[]{:S(2)}, u32[]{:S(2)}) collective-permute-start(f32[1,768]{1,0:T(1,128)S(1)} %get-tuple-element.35), channel_id=1, source_target_pairs={{4,0},{0,4},{5,1},{1,5},{6,2},{2,6},{7,3},{3,7},{12,8},{8,12},{13,... | collective-permute-start | bytes 9224 | tf_op jit(solution)/shard_map/ppermute | solution.py:49

commit v20 on v19

--- a/solution.py
+++ b/solution.py
@@ -186,9 +186,9 @@
 def factor_kernel(rate, n, *refs):
     goals, tops, factors = refs[:4], refs[4 : 4 + n], refs[4 + n :]
     rows = goals[0].shape[1] // 2
-    spots = [(0, 0, 0), (0, 0, 1), (0, 0, 2), (1, 0, 3), (1, 1, 0), (1, 1, 1), (1, 1, 2), (2, 1, 3)]
+    spots = [(0, 0, 0), (0, 0, 1), (0, 0, 2), (0, 1, 0), (1, 0, 3), (1, 1, 1), (1, 1, 2), (2, 1, 3)]
     for at, (bundle, group, goal) in enumerate(spots):
-        start = (at - (0, 3, 7)[bundle]) * rows
+        start = (at - (0, 4, 7)[bundle]) * rows
         mine, here = slice(group * rows, (group + 1) * rows), slice(start, start + rows)
         scale = jnp.exp2((tops[bundle][:, here] - goals[goal][:1, mine]) * rate)
         factors[bundle][:, here] = scale * goals[goal][1:, mine]
@@ -248,16 +248,14 @@
     total = weight = None
     for expo, chunk, factor in zip(expos, points, factors):
         block = expo.shape[0] // factor.shape[0]
-        shares = []
-        step = min(block, count)
-        for at in range(0, count, step):
-            here = pl.ds(pl.multiple_of(start + at, step), step)
-            scale = factor[pl.ds((start + at) // block, 1), :]
-            shares.append((expo[here, :].astype(jnp.float32) * scale).astype(jnp.bfloat16))
-        share = jnp.concatenate(shares, axis=0)
+        shares, lanes = [], []
+        for at in range(0, count, block):
+            here = pl.ds(pl.multiple_of(start + at, block), block)
+            share = expo[here, :].astype(jnp.float32) * factor[pl.ds((start + at) // block, 1), :]
+            shares.append(share.astype(jnp.bfloat16))
+            lanes.append(sum(share[:, i : i + 128] for i in range(0, share.shape[1], 128)))
+        share, lanes = jnp.concatenate(shares, axis=0), jnp.concatenate(lanes, axis=0)
         part = jnp.dot(share, chunk[...], preferred_element_type=jnp.float32)
-        wide = share.astype(jnp.float32)
-        lanes = sum(wide[:, i : i + 128] for i in range(0, wide.shape[1], 128))
         total = part if total is None else total + part
         weight = lanes if weight is None else weight + lanes
     return total, jnp.sum(weight.T, axis=0, keepdims=True)
@@ -351,19 +349,19 @@
     across_01, second_23 = (both, 0, rows), (both, rows, rows)
     stat = beside(*stats)
     expand = functools.partial(expo_call, rate, block, 2 * per_device)
-    bundles = [expand((near_01, first_01, second_01), centroids, stat, declared=0.01)]
+    bundles = [expand((near_01, first_01, second_01, near_23), centroids, stat, declared=0.01)]
     goal = goal_call(rate, stat, *(along_z(stat, by) for by in (1, 2, 3)), bundles[0][1])
     across_23 = turn_back(hold(first_23, goal))
 
-    bundles.append(expand((across_01, near_23, first_23, second_23), centroids, goal, declared=0.01))
+    bundles.append(expand((across_01, first_23, second_23), centroids, goal, declared=0.01))
     bundles.append(expand((across_23,), centroids, bundles[1][1]))
     expos, tops, points = zip(*bundles)
     goals = [goal, turn(goal), turn_back(goal), around(goal, 3)]
     factors = factor_call(rate, goals, tops)
 
-    there = sums_call(block, 1, per_device, jnp.bfloat16, expos, points, factors)
+    there = sums_call(per_device, 1, per_device, jnp.bfloat16, expos, points, factors)
     there = [exchange(a, ("lo",), lambda at: at ^ 1) for a in there]
-    here = sums_call(block, 0, per_device, jnp.float32, expos, points, factors)
+    here = sums_call(per_device, 0, per_device, jnp.float32, expos, points, factors)
     out, mass = add_call(block // 2, *here, *there)
     return (out[None], mass)
 

time: 46.8 us -> 46.6 us (level)
  Pallas kernels: 17.5 us -> 16.6 us
  waiting for transfers between devices: 5.08 us -> 5.84 us
    ppermute x16, waiting for transfers between devices: 5.08 us -> 5.84 us  [exchange(): return lax.ppermute(a, axes, [(partner(at), at) for at in range(count)])]
  transfers between devices with their start and end apart: 16 -> 16, of which waited for: 5 -> 4; matrix products, arithmetic and copies ran while one was open for 0% -> 0% of each run, Pallas kernels for 29% -> 27%
where the time goes in v20:
time: 46.6 us; the launch traced here: 46.4 us
  starting transfers between devices  21.2 us (45%)
  Pallas kernels  16.6 us (36%)
  waiting for transfers between devices  5.84 us (13%)
  other arithmetic  1.05 us (2%)
  between operations  1 us (2%)
  local copies, waits for them, and re-layouts  0.75 us (2%)
    ppermute x16, starting transfers between devices, exchange(): return lax.ppermute(a, axes, [(partner(at), at) for at in range(count)])  21.2 us
    ppermute x16, waiting for transfers between devices, exchange(): return lax.ppermute(a, axes, [(partner(at), at) for at in range(count)])  5.84 us
    pallas_call x2, Pallas kernels, totals_call(): pl.pallas_call(functools.partial(totals_kernel, rate, block, len(pieces))...  5.53 us
    pallas_call x3, Pallas kernels, expo_call(): pl.pallas_call(functools.partial(expo_kernel, rate, block, spots), in_spe...  4.29 us
    pallas_call x2, Pallas kernels, sums_call(): pl.pallas_call(functools.partial(sums_kernel, n, block, side), in_specs=i...  3.88 us
    pallas_call x1, Pallas kernels, add_call(): pl.pallas_call(functools.partial(add_kernel, block), in_specs=in_vmem(4),...  1.79 us
    convert_element_type x1, other arithmetic, to_points(): return (scaled.astype(jnp.float32) * 2.0 ** (-16)).astype(jnp.bfloat16)  1.05 us
  transfers between devices with their start and end apart: 16, of which 4 were waited for; matrix products, arithmetic and copies ran while one was open for 0% of the time, Pallas kernels for 27%

profile of v20, /device:TPU:0, one launch (start us, length us, event | category | flops | bytes accessed | tf_op | source)
XLA Modules:
  0.0 46.4 jit_solution(8543405667463296137)
XLA Ops:
  0.6 1.1 %multiply_convert_fusion.above = bf16[128,512]{1,0:T(8,128)(2,1)S(1)} fusion(s32[128,512]{1,0:T(8,128)} %param.4, s32[128]{0:T(128)} %param.5), kind=kLoop, calls=%fused_computation | loop fusion | flops 327680 | bytes 393728 | tf_op jit(solution)/shard_map/convert_element_type | solution.py:17
  1.7 3.1 %collective-permute-start = (bf16[128,512]{1,0:T(8,128)(2,1)S(1)}, bf16[128,512]{1,0:T(8,128)(2,1)S(1)}, u32[]{:S(2)}, u32[]{:S(2)}) collective-permute-start(bf16[128,512]{1,0:T(8,128)(2,1)S(1)} %multiply_convert_fusion.above), channel_id=1, source_target_pairs={{1,0},{0,1},{3,2},{2,3},{5,4},{4,5},{7,6},{6,7},{9,8},{8,9},{11,10... | collective-permute-start | bytes 393224 | tf_op jit(solution)/shard_map/ppermute | solution.py:49
  4.8 2.6 %collective-permute-start.3 = (bf16[128,512]{1,0:T(8,128)(2,1)S(1)}, bf16[128,512]{1,0:T(8,128)(2,1)S(1)}, u32[]{:S(2)}, u32[]{:S(2)}) collective-permute-start(bf16[128,512]{1,0:T(8,128)(2,1)S(1)} %multiply_convert_fusion.above), channel_id=1, source_target_pairs={{2,0},{3,1},{0,2},{1,3},{6,4},{7,5},{4,6},{5,7},{10,8},{11,9},{8,1... | collective-permute-start | bytes 393224 | tf_op jit(solution)/shard_map/ppermute | solution.py:49
  7.4 0.0 collective-permute-start.4
  7.4 0.0 copy-start
  7.4 0.7 %copy-done = s32[6144]{0:T(1024)S(1)} copy-done((s32[6144]{0:T(1024)S(1)}, s32[6144]{0:T(1024)}, u32[]{:S(2)}) %copy-start) | copy-done | bytes 24600
  8.1 0.0 slice-start
  8.1 0.9 %shard_map.59.refs_0_.refs_2_ = f32[6144,128]{1,0:T(8,128)S(1)} custom-call(s32[48,128]{1,0:T(8,128)S(1)} %bitcast.4), custom_call_target="tpu_custom_call" | custom-call | flops 2000000000 | tf_op jit(solution)/shard_map/pallas_call | solution.py:114
  9.0 0.0 slice-start.1
  9.0 0.8 %collective-permute-done.below = bf16[128,512]{1,0:T(8,128)(2,1)S(1)} collective-permute-done((bf16[128,512]{1,0:T(8,128)(2,1)S(1)}, bf16[128,512]{1,0:T(8,128)(2,1)S(1)}, u32[]{:S(2)}, u32[]{:S(2)}) %collective-permute-start) | collective-permute-done | bytes 131104 | tf_op jit(solution)/shard_map/ppermute | solution.py:49
  9.8 1.8 %collective-permute-start.1 = (bf16[256,512]{1,0:T(8,128)(2,1)S(1)}, bf16[256,512]{1,0:T(8,128)(2,1)S(1)}, u32[]{:S(2)}, u32[]{:S(2)}) collective-permute-start(bf16[256,512]{1,0:T(8,128)(2,1)S(1)} %shard_map.60.a.refs_0_), channel_id=1, source_target_pairs={{8,0},{20,4},{0,8},{28,12},{24,16},{4,20},{16,24},{12,28},{9,1},{2... | collective-permute-start | bytes 786440 | tf_op jit(solution)/shard_map/ppermute | solution.py:49
  11.6 0.0 slice-done
  11.6 0.0 slice-done.1
  11.7 2.7 %shard_map.62.refs_0_.left = f32[3,256]{1,0:T(4,128)S(1)} custom-call(bf16[256,512]{1,0:T(8,128)(2,1)S(1)} %shard_map.61.refs_0_, bf16[6144,512]{1,0:T(8,128)(2,1)S(1)} %bitcast.3, f32[6144,128]{1,0:T(8,128)S(1)} %shard_map.59.refs_0_.refs_2_), custom_call_target="tpu_custom_call" | custom-call | flops 1610612736 | bytes 6291456 | tf_op jit(solution)/shard_map/pallas_call | solution.py:154
  14.4 1.6 %collective-permute-start.2 = (bf16[256,512]{1,0:T(8,128)(2,1)S(1)}, bf16[256,512]{1,0:T(8,128)(2,1)S(1)}, u32[]{:S(2)}, u32[]{:S(2)}) collective-permute-start(bf16[256,512]{1,0:T(8,128)(2,1)S(1)} %shard_map.63), channel_id=1, source_target_pairs={{16,0},{12,4},{24,8},{4,12},{0,16},{28,20},{8,24},{20,28},{17,1},{... | collective-permute-start | bytes 786440 | tf_op jit(solution)/shard_map/ppermute | solution.py:49
  16.0 1.7 %collective-permute-done.3.above = bf16[128,512]{1,0:T(8,128)(2,1)S(1)} collective-permute-done((bf16[128,512]{1,0:T(8,128)(2,1)S(1)}, bf16[128,512]{1,0:T(8,128)(2,1)S(1)}, u32[]{:S(2)}, u32[]{:S(2)}) %collective-permute-start.3) | collective-permute-done | bytes 131104 | tf_op jit(solution)/shard_map/ppermute | solution.py:49
  17.7 0.0 collective-permute-done.4.below
  17.7 0.0 collective-permute-done.1.refs_3_.refs_1_.above
  17.7 2.8 %shard_map.65.right.refs_0_ = f32[3,256]{1,0:T(4,128)S(1)} custom-call(bf16[256,512]{1,0:T(8,128)(2,1)S(1)} %shard_map.64.refs_0_.refs_3_.below, bf16[6144,512]{1,0:T(8,128)(2,1)S(1)} %bitcast.3, f32[6144,128]{1,0:T(8,128)S(1)} %shard_map.59.refs_0_.refs_2_, bf16[256,512]{1,0:T(8,128)(2,1)S(1)} %collective-permute-done.1.refs_3_.refs_1_.above), custom_call_target="tpu_custom_call" | custom-call | flops 1610612736 | bytes 6291456 | tf_op jit(solution)/shard_map/pallas_call | solution.py:154
  20.6 1.6 %collective-permute-start.5 = (bf16[512,512]{1,0:T(8,128)(2,1)S(1)}, bf16[512,512]{1,0:T(8,128)(2,1)S(1)}, u32[]{:S(2)}, u32[]{:S(2)}) collective-permute-start(bf16[512,512]{1,0:T(8,128)(2,1)S(1)} %shard_map.68), channel_id=1, source_target_pairs={{16,0},{12,4},{24,8},{4,12},{0,16},{28,20},{8,24},{20,28},{17,1},{... | collective-permute-start | bytes 1572872 | tf_op jit(solution)/shard_map/ppermute | solution.py:49
  22.2 1.5 %collective-permute-start.6 = (bf16[256,512]{1,0:T(8,128)(2,1)S(1)}, bf16[256,512]{1,0:T(8,128)(2,1)S(1)}, u32[]{:S(2)}, u32[]{:S(2)}) collective-permute-start(bf16[256,512]{1,0:T(8,128)(2,1)S(1)} %shard_map.64.refs_0_.refs_3_.below), channel_id=1, source_target_pairs={{8,0},{20,4},{0,8},{28,12},{24,16},{4,20},{16,24},{12,28},{9,1},{2... | collective-permute-start | bytes 786440 | tf_op jit(solution)/shard_map/ppermute | solution.py:49
  23.7 2.0 %collective-permute-start.7 = (f32[3,512]{1,0:T(4,128)S(1)}, f32[3,512]{1,0:T(4,128)S(1)}, u32[]{:S(2)}, u32[]{:S(2)}) collective-permute-start(f32[3,512]{1,0:T(4,128)S(1)} %shard_map.66.refs_5_.refs_0_), channel_id=1, source_target_pairs={{1,0},{0,1},{3,2},{2,3},{5,4},{4,5},{7,6},{6,7},{9,8},{8,9},{11,10... | collective-permute-start | bytes 18440 | tf_op jit(solution)/shard_map/ppermute | solution.py:49
  25.7 1.5 %collective-permute-start.8 = (f32[3,512]{1,0:T(4,128)S(1)}, f32[3,512]{1,0:T(4,128)S(1)}, u32[]{:S(2)}, u32[]{:S(2)}) collective-permute-start(f32[3,512]{1,0:T(4,128)S(1)} %shard_map.66.refs_5_.refs_0_), channel_id=1, source_target_pairs={{2,0},{3,1},{0,2},{1,3},{6,4},{7,5},{4,6},{5,7},{10,8},{11,9},{8,1... | collective-permute-start | bytes 18440 | tf_op jit(solution)/shard_map/ppermute | solution.py:49
  27.2 0.0 collective-permute-done.2.refs_2_
  27.2 0.9 %collective-permute-start.9 = (f32[3,512]{1,0:T(4,128)S(1)}, f32[3,512]{1,0:T(4,128)S(1)}, u32[]{:S(2)}, u32[]{:S(2)}) collective-permute-start(f32[3,512]{1,0:T(4,128)S(1)} %shard_map.66.refs_5_.refs_0_), channel_id=1, source_target_pairs={{3,0},{2,1},{1,2},{0,3},{7,4},{6,5},{5,6},{4,7},{11,8},{10,9},{9,1... | collective-permute-start | bytes 18440 | tf_op jit(solution)/shard_map/ppermute | solution.py:49
  28.1 2.0 %shard_map.67 = (bf16[1536,1024]{1,0:T(8,128)(2,1)S(1)}, f32[6,1024]{1,0:T(8,128)S(1)}, bf16[1024,512]{1,0:T(8,128)(2,1)S(1)}) custom-call(bf16[256,512]{1,0:T(8,128)(2,1)S(1)} %shard_map.60.a.refs_0_, bf16[256,512]{1,0:T(8,128)(2,1)S(1)} %collective-permute-done.1.refs_3_.refs_1_.above, bf16[256,512]{1,0:T(8,128)(2,1)S(1)} %collective-permute-done.2.refs_2_, ...), custom_call_target="tpu_custom_call" | custom-call | flops 16106127 | bytes 57671 | tf_op jit(solution)/shard_map/pallas_call | solution.py:229
  30.2 0.0 collective-permute-done.7.refs_1_
  30.2 0.0 collective-permute-done.8.refs_2_
  30.2 2.4 %collective-permute-done.9.refs_3_ = f32[3,512]{1,0:T(4,128)S(1)} collective-permute-done((f32[3,512]{1,0:T(4,128)S(1)}, f32[3,512]{1,0:T(4,128)S(1)}, u32[]{:S(2)}, u32[]{:S(2)}) %collective-permute-start.9) | collective-permute-done | bytes 6176 | tf_op jit(solution)/shard_map/ppermute | solution.py:49
  32.7 0.0 collective-permute-done.6.refs_1_.a
  32.7 0.6 %collective-permute-start.10 = (bf16[256,512]{1,0:T(8,128)(2,1)S(1)}, bf16[256,512]{1,0:T(8,128)(2,1)S(1)}, u32[]{:S(2)}, u32[]{:S(2)}) collective-permute-start(bf16[256,512]{1,0:T(8,128)(2,1)S(1)} %shard_map.71), channel_id=1, source_target_pairs={{16,0},{12,4},{24,8},{4,12},{0,16},{28,20},{8,24},{20,28},{17,1},{... | collective-permute-start | bytes 786440 | tf_op jit(solution)/shard_map/ppermute | solution.py:49
  33.3 0.5 %collective-permute-start.11 = (f32[2,512]{1,0:T(2,128)S(1)}, f32[2,512]{1,0:T(2,128)S(1)}, u32[]{:S(2)}, u32[]{:S(2)}) collective-permute-start(f32[2,512]{1,0:T(2,128)S(1)} %shard_map.69.refs_4_.refs_0_), channel_id=1, source_target_pairs={{8,0},{20,4},{0,8},{28,12},{24,16},{4,20},{16,24},{12,28},{9,1},{2... | collective-permute-start | bytes 12296 | tf_op jit(solution)/shard_map/ppermute | solution.py:49
  33.8 1.5 %collective-permute-start.12 = (f32[2,512]{1,0:T(2,128)S(1)}, f32[2,512]{1,0:T(2,128)S(1)}, u32[]{:S(2)}, u32[]{:S(2)}) collective-permute-start(f32[2,512]{1,0:T(2,128)S(1)} %shard_map.69.refs_4_.refs_0_), channel_id=1, source_target_pairs={{16,0},{12,4},{24,8},{4,12},{0,16},{28,20},{8,24},{20,28},{17,1},{... | collective-permute-start | bytes 12296 | tf_op jit(solution)/shard_map/ppermute | solution.py:49
  35.3 1.4 %collective-permute-start.13 = (f32[2,512]{1,0:T(2,128)S(1)}, f32[2,512]{1,0:T(2,128)S(1)}, u32[]{:S(2)}, u32[]{:S(2)}) collective-permute-start(f32[2,512]{1,0:T(2,128)S(1)} %shard_map.69.refs_4_.refs_0_), channel_id=1, source_target_pairs={{24,0},{16,8},{8,16},{0,24},{25,1},{17,9},{9,17},{1,25},{26,2},{18... | collective-permute-start | bytes 12296 | tf_op jit(solution)/shard_map/ppermute | solution.py:49
  36.8 0.0 collective-permute-done.5.refs_0_.refs_2_
  36.8 1.6 %shard_map.70 = (bf16[1536,768]{1,0:T(8,128)(2,1)S(1)}, f32[6,768]{1,0:T(8,128)S(1)}, bf16[768,512]{1,0:T(8,128)(2,1)S(1)}) custom-call(bf16[512,512]{1,0:T(8,128)(2,1)S(1)} %collective-permute-done.5.refs_0_.refs_2_, bf16[256,512]{1,0:T(8,128)(2,1)S(1)} %collective-permute-done.6.refs_1_.a, bf16[512,512]{1,0:T(8,128)(2,1)S(1)} %collective-permute-done.5.refs_0_.refs_2_, ...), custom_call_target="tpu_custom_call" | custom-call | flops 12079595 | bytes 47185 | tf_op jit(solution)/shard_map/pallas_call | solution.py:229
  38.3 0.8 %collective-permute-done.10.refs_0_ = bf16[256,512]{1,0:T(8,128)(2,1)S(1)} collective-permute-done((bf16[256,512]{1,0:T(8,128)(2,1)S(1)}, bf16[256,512]{1,0:T(8,128)(2,1)S(1)}, u32[]{:S(2)}, u32[]{:S(2)}) %collective-permute-start.10) | collective-permute-done | bytes 262176 | tf_op jit(solution)/shard_map/ppermute | solution.py:49
  39.2 0.7 %shard_map.72 = (bf16[1536,256]{1,0:T(8,128)(2,1)S(1)}, f32[6,256]{1,0:T(8,128)S(1)}, bf16[256,512]{1,0:T(8,128)(2,1)S(1)}) custom-call(bf16[256,512]{1,0:T(8,128)(2,1)S(1)} %collective-permute-done.10.refs_0_, bf16[6144,512]{1,0:T(8,128)(2,1)S(1)} %bitcast.3, f32[6,768]{1,0:T(8,128)S(1)} %get-tuple-element.23.refs_2_.refs_5_), custom_call_target="tpu_custom_call" | custom-call | flops 402653184 | bytes 2621440 | tf_op jit(solution)/shard_map/pallas_call | solution.py:229
  39.9 0.0 collective-permute-done.11.refs_1_
  39.9 0.0 collective-permute-done.12.refs_2_
  39.9 0.0 collective-permute-done.13.refs_3_
  39.9 2.0 %shard_map.75 = (bf16[768,512]{1,0:T(8,128)(2,1)S(1)}, f32[1,768]{1,0:T(1,128)S(1)}) custom-call(bf16[1536,1024]{1,0:T(8,128)(2,1)S(1)} %get-tuple-element.20.refs_0_, bf16[1536,768]{1,0:T(8,128)(2,1)S(1)} %get-tuple-element.22.refs_1_, bf16[1536,256]{1,0:T(8,128)(2,1)S(1)} %get-tuple-element.24.refs_2_, bf16[1024,512]{1,0:T(8,128)(2,1)S(1)} %get-tuple-element.25.refs_3_, ...), custom_call_target="tpu_custom_call" | custom-call | flops 2415919104 | bytes 9437184 | tf_op jit(solution)/shard_map/pallas_call | solution.py:278
  42.0 0.1 collective-permute-start.14
  42.1 0.5 %collective-permute-start.15 = (f32[1,768]{1,0:T(1,128)S(1)}, f32[1,768]{1,0:T(1,128)S(1)}, u32[]{:S(2)}, u32[]{:S(2)}) collective-permute-start(f32[1,768]{1,0:T(1,128)S(1)} %get-tuple-element.35), channel_id=1, source_target_pairs={{4,0},{0,4},{5,1},{1,5},{6,2},{2,6},{7,3},{3,7},{12,8},{8,12},{13,... | collective-permute-start | bytes 9224 | tf_op jit(solution)/shard_map/ppermute | solution.py:49
  42.6 1.8 %shard_map.74 = (f32[768,512]{1,0:T(8,128)S(1)}, f32[1,768]{1,0:T(1,128)S(1)}) custom-call(bf16[1536,1024]{1,0:T(8,128)(2,1)S(1)} %get-tuple-element.20.refs_0_, bf16[1536,768]{1,0:T(8,128)(2,1)S(1)} %get-tuple-element.22.refs_1_, bf16[1536,256]{1,0:T(8,128)(2,1)S(1)} %get-tuple-element.24.refs_2_, bf16[1024,512]{1,0:T(8,128)(2,1)S(1)} %get-tuple-element.25.refs_3_, ...), custom_call_target="tpu_custom_call" | custom-call | flops 2415919104 | bytes 9437184 | tf_op jit(solution)/shard_map/pallas_call | solution.py:278
  44.4 0.0 collective-permute-done.15.there_mass
  44.4 0.0 collective-permute-done.14.there
  44.4 1.8 %shard_map.76 = (f32[768,512]{1,0:T(8,128)}, f32[1,768]{1,0:T(1,128)}) custom-call(f32[768,512]{1,0:T(8,128)S(1)} %get-tuple-element.32.here, f32[1,768]{1,0:T(1,128)S(1)} %get-tuple-element.33.here_mass, bf16[768,512]{1,0:T(8,128)(2,1)S(1)} %collective-permute-done.14.there, f32[1,768]{1,0:T(1,128)S(1)} %collective-permute-done.15.there_mass), custom_call_target="tpu_custom_call" | custom-call | tf_op jit(solution)/shard_map/pallas_call | solution.py:308
  (10 shorter events, 0.2 us)
Async XLA Ops:
  1.7 8.1 %collective-permute-start = (bf16[128,512]{1,0:T(8,128)(2,1)S(1)}, bf16[128,512]{1,0:T(8,128)(2,1)S(1)}, u32[]{:S(2)}, u32[]{:S(2)}) collective-permute-start(bf16[128,512]{1,0:T(8,128)(2,1)S(1)} %multiply_convert_fusion.above), channel_id=1, source_target_pairs={{1,0},{0,1},{3,2},{2,3},{5,4},{4,5},{7,6},{6,7},{9,8},{8,9},{11,10... | collective-permute-start | bytes 393224 | tf_op jit(solution)/shard_map/ppermute | solution.py:49
  4.8 12.9 %collective-permute-start.3 = (bf16[128,512]{1,0:T(8,128)(2,1)S(1)}, bf16[128,512]{1,0:T(8,128)(2,1)S(1)}, u32[]{:S(2)}, u32[]{:S(2)}) collective-permute-start(bf16[128,512]{1,0:T(8,128)(2,1)S(1)} %multiply_convert_fusion.above), channel_id=1, source_target_pairs={{2,0},{3,1},{0,2},{1,3},{6,4},{7,5},{4,6},{5,7},{10,8},{11,9},{8,1... | collective-permute-start | bytes 393224 | tf_op jit(solution)/shard_map/ppermute | solution.py:49
  7.4 10.3 %collective-permute-start.4 = (bf16[128,512]{1,0:T(8,128)(2,1)S(1)}, bf16[128,512]{1,0:T(8,128)(2,1)S(1)}, u32[]{:S(2)}, u32[]{:S(2)}) collective-permute-start(bf16[128,512]{1,0:T(8,128)(2,1)S(1)} %multiply_convert_fusion.above), channel_id=1, source_target_pairs={{3,0},{2,1},{1,2},{0,3},{7,4},{6,5},{5,6},{4,7},{11,8},{10,9},{9,1... | collective-permute-start | bytes 393224 | tf_op jit(solution)/shard_map/ppermute | solution.py:49
  7.4 0.7 %copy-start = (s32[6144]{0:T(1024)S(1)}, s32[6144]{0:T(1024)}, u32[]{:S(2)}) copy-start(s32[6144]{0:T(1024)} %param.7) | copy-start | bytes 73732
  8.1 3.5 %slice-start = ((s8[6291456]{0:T(1024)(128)(4,1)}), s8[4194304]{0:T(1024)(128)(4,1)S(1)}, s32[]{:S(2)}) async-start(s8[6291456]{0:T(1024)(128)(4,1)} %bitcast.2), calls=%async_computation | async-start | bytes 8388608
  9.0 2.6 %slice-start.1 = ((s8[6291456]{0:T(1024)(128)(4,1)}), s8[2097152]{0:T(1024)(128)(4,1)S(1)}, s32[]{:S(2)}) async-start(s8[6291456]{0:T(1024)(128)(4,1)} %bitcast.2), calls=%async_computation.1 | async-start | bytes 4194304
  9.8 7.9 %collective-permute-start.1 = (bf16[256,512]{1,0:T(8,128)(2,1)S(1)}, bf16[256,512]{1,0:T(8,128)(2,1)S(1)}, u32[]{:S(2)}, u32[]{:S(2)}) collective-permute-start(bf16[256,512]{1,0:T(8,128)(2,1)S(1)} %shard_map.60.a.refs_0_), channel_id=1, source_target_pairs={{8,0},{20,4},{0,8},{28,12},{24,16},{4,20},{16,24},{12,28},{9,1},{2... | collective-permute-start | bytes 786440 | tf_op jit(solution)/shard_map/ppermute | solution.py:49
  14.4 12.8 %collective-permute-start.2 = (bf16[256,512]{1,0:T(8,128)(2,1)S(1)}, bf16[256,512]{1,0:T(8,128)(2,1)S(1)}, u32[]{:S(2)}, u32[]{:S(2)}) collective-permute-start(bf16[256,512]{1,0:T(8,128)(2,1)S(1)} %shard_map.63), channel_id=1, source_target_pairs={{16,0},{12,4},{24,8},{4,12},{0,16},{28,20},{8,24},{20,28},{17,1},{... | collective-permute-start | bytes 786440 | tf_op jit(solution)/shard_map/ppermute | solution.py:49
  20.6 16.2 %collective-permute-start.5 = (bf16[512,512]{1,0:T(8,128)(2,1)S(1)}, bf16[512,512]{1,0:T(8,128)(2,1)S(1)}, u32[]{:S(2)}, u32[]{:S(2)}) collective-permute-start(bf16[512,512]{1,0:T(8,128)(2,1)S(1)} %shard_map.68), channel_id=1, source_target_pairs={{16,0},{12,4},{24,8},{4,12},{0,16},{28,20},{8,24},{20,28},{17,1},{... | collective-permute-start | bytes 1572872 | tf_op jit(solution)/shard_map/ppermute | solution.py:49
  22.2 10.5 %collective-permute-start.6 = (bf16[256,512]{1,0:T(8,128)(2,1)S(1)}, bf16[256,512]{1,0:T(8,128)(2,1)S(1)}, u32[]{:S(2)}, u32[]{:S(2)}) collective-permute-start(bf16[256,512]{1,0:T(8,128)(2,1)S(1)} %shard_map.64.refs_0_.refs_3_.below), channel_id=1, source_target_pairs={{8,0},{20,4},{0,8},{28,12},{24,16},{4,20},{16,24},{12,28},{9,1},{2... | collective-permute-start | bytes 786440 | tf_op jit(solution)/shard_map/ppermute | solution.py:49
  23.7 6.5 %collective-permute-start.7 = (f32[3,512]{1,0:T(4,128)S(1)}, f32[3,512]{1,0:T(4,128)S(1)}, u32[]{:S(2)}, u32[]{:S(2)}) collective-permute-start(f32[3,512]{1,0:T(4,128)S(1)} %shard_map.66.refs_5_.refs_0_), channel_id=1, source_target_pairs={{1,0},{0,1},{3,2},{2,3},{5,4},{4,5},{7,6},{6,7},{9,8},{8,9},{11,10... | collective-permute-start | bytes 18440 | tf_op jit(solution)/shard_map/ppermute | solution.py:49
  25.7 4.5 %collective-permute-start.8 = (f32[3,512]{1,0:T(4,128)S(1)}, f32[3,512]{1,0:T(4,128)S(1)}, u32[]{:S(2)}, u32[]{:S(2)}) collective-permute-start(f32[3,512]{1,0:T(4,128)S(1)} %shard_map.66.refs_5_.refs_0_), channel_id=1, source_target_pairs={{2,0},{3,1},{0,2},{1,3},{6,4},{7,5},{4,6},{5,7},{10,8},{11,9},{8,1... | collective-permute-start | bytes 18440 | tf_op jit(solution)/shard_map/ppermute | solution.py:49
  27.2 5.4 %collective-permute-start.9 = (f32[3,512]{1,0:T(4,128)S(1)}, f32[3,512]{1,0:T(4,128)S(1)}, u32[]{:S(2)}, u32[]{:S(2)}) collective-permute-start(f32[3,512]{1,0:T(4,128)S(1)} %shard_map.66.refs_5_.refs_0_), channel_id=1, source_target_pairs={{3,0},{2,1},{1,2},{0,3},{7,4},{6,5},{5,6},{4,7},{11,8},{10,9},{9,1... | collective-permute-start | bytes 18440 | tf_op jit(solution)/shard_map/ppermute | solution.py:49
  32.7 6.4 %collective-permute-start.10 = (bf16[256,512]{1,0:T(8,128)(2,1)S(1)}, bf16[256,512]{1,0:T(8,128)(2,1)S(1)}, u32[]{:S(2)}, u32[]{:S(2)}) collective-permute-start(bf16[256,512]{1,0:T(8,128)(2,1)S(1)} %shard_map.71), channel_id=1, source_target_pairs={{16,0},{12,4},{24,8},{4,12},{0,16},{28,20},{8,24},{20,28},{17,1},{... | collective-permute-start | bytes 786440 | tf_op jit(solution)/shard_map/ppermute | solution.py:49
  33.3 6.6 %collective-permute-start.11 = (f32[2,512]{1,0:T(2,128)S(1)}, f32[2,512]{1,0:T(2,128)S(1)}, u32[]{:S(2)}, u32[]{:S(2)}) collective-permute-start(f32[2,512]{1,0:T(2,128)S(1)} %shard_map.69.refs_4_.refs_0_), channel_id=1, source_target_pairs={{8,0},{20,4},{0,8},{28,12},{24,16},{4,20},{16,24},{12,28},{9,1},{2... | collective-permute-start | bytes 12296 | tf_op jit(solution)/shard_map/ppermute | solution.py:49
  33.8 6.1 %collective-permute-start.12 = (f32[2,512]{1,0:T(2,128)S(1)}, f32[2,512]{1,0:T(2,128)S(1)}, u32[]{:S(2)}, u32[]{:S(2)}) collective-permute-start(f32[2,512]{1,0:T(2,128)S(1)} %shard_map.69.refs_4_.refs_0_), channel_id=1, source_target_pairs={{16,0},{12,4},{24,8},{4,12},{0,16},{28,20},{8,24},{20,28},{17,1},{... | collective-permute-start | bytes 12296 | tf_op jit(solution)/shard_map/ppermute | solution.py:49
  35.3 4.5 %collective-permute-start.13 = (f32[2,512]{1,0:T(2,128)S(1)}, f32[2,512]{1,0:T(2,128)S(1)}, u32[]{:S(2)}, u32[]{:S(2)}) collective-permute-start(f32[2,512]{1,0:T(2,128)S(1)} %shard_map.69.refs_4_.refs_0_), channel_id=1, source_target_pairs={{24,0},{16,8},{8,16},{0,24},{25,1},{17,9},{9,17},{1,25},{26,2},{18... | collective-permute-start | bytes 12296 | tf_op jit(solution)/shard_map/ppermute | solution.py:49
  42.0 2.4 %collective-permute-start.14 = (bf16[768,512]{1,0:T(8,128)(2,1)S(1)}, bf16[768,512]{1,0:T(8,128)(2,1)S(1)}, u32[]{:S(2)}, u32[]{:S(2)}) collective-permute-start(bf16[768,512]{1,0:T(8,128)(2,1)S(1)} %get-tuple-element.34), channel_id=1, source_target_pairs={{4,0},{0,4},{5,1},{1,5},{6,2},{2,6},{7,3},{3,7},{12,8},{8,12},{13,... | collective-permute-start | bytes 2359304 | tf_op jit(solution)/shard_map/ppermute | solution.py:49
  42.1 2.3 %collective-permute-start.15 = (f32[1,768]{1,0:T(1,128)S(1)}, f32[1,768]{1,0:T(1,128)S(1)}, u32[]{:S(2)}, u32[]{:S(2)}) collective-permute-start(f32[1,768]{1,0:T(1,128)S(1)} %get-tuple-element.35), channel_id=1, source_target_pairs={{4,0},{0,4},{5,1},{1,5},{6,2},{2,6},{7,3},{3,7},{12,8},{8,12},{13,... | collective-permute-start | bytes 9224 | tf_op jit(solution)/shard_map/ppermute | solution.py:49

commit v21 on v20

--- a/solution.py
+++ b/solution.py
@@ -340,19 +340,17 @@
     held_01 = hold(near_01, declared=2 * 10**9)
     first_01 = turn(near_01)
     stats = [totals_call(rate, block, (held_01,), centroids, inverse)]
-    second_01 = turn_back(hold(near_01, stats[0]))
+    second_01, across_01 = turn_back(hold(near_01, stats[0])), turn_back(hold(first_01, stats[0]))
     near_23 = join(near_2, near_3, *stats)
     stats.append(totals_call(rate, block, (near_23,), centroids, inverse, after=(first_01,)))
     first_23 = turn(near_23)
-    rows = near_01.shape[0]
-    both = turn_back(join(first_01, near_23, stats[1]))
-    across_01, second_23 = (both, 0, rows), (both, rows, rows)
     stat = beside(*stats)
     expand = functools.partial(expo_call, rate, block, 2 * per_device)
     bundles = [expand((near_01, first_01, second_01, near_23), centroids, stat, declared=0.01)]
-    goal = goal_call(rate, stat, *(along_z(stat, by) for by in (1, 2, 3)), bundles[0][1])
+    goal = goal_call(rate, stat, *(along_z(stat, by) for by in (1, 2, 3)), bundles[0][1], across_01)
     across_23 = turn_back(hold(first_23, goal))
 
+    second_23 = turn_back(hold(near_23, bundles[0][1]))
     bundles.append(expand((across_01, first_23, second_23), centroids, goal, declared=0.01))
     bundles.append(expand((across_23,), centroids, bundles[1][1]))
     expos, tops, points = zip(*bundles)

time: 46.6 us -> 46.2 us (level)
  waiting for transfers between devices: 5.84 us -> 4.47 us
  starting transfers between devices: 21.2 us -> 22.3 us
    ppermute x16 -> x17, waiting for transfers between devices: 5.84 us -> 4.47 us  [exchange(): return lax.ppermute(a, axes, [(partner(at), at) for at in range(count)])]
    ppermute x16 -> x17, starting transfers between devices: 21.2 us -> 22.3 us  [exchange(): return lax.ppermute(a, axes, [(partner(at), at) for at in range(count)])]
  transfers between devices with their start and end apart: 16 -> 17, of which waited for: 4 -> 6; matrix products, arithmetic and copies ran while one was open for 0% -> 0% of each run, Pallas kernels for 27% -> 27%
where the time goes in v21:
time: 46.2 us; the launch traced here: 46 us
  starting transfers between devices  22.3 us (48%)
  Pallas kernels  16.4 us (35%)
  waiting for transfers between devices  4.47 us (10%)
  other arithmetic  1.05 us (2%)
  between operations  1.01 us (2%)
  local copies, waits for them, and re-layouts  0.75 us (2%)
    ppermute x17, starting transfers between devices, exchange(): return lax.ppermute(a, axes, [(partner(at), at) for at in range(count)])  22.3 us
    pallas_call x2, Pallas kernels, totals_call(): pl.pallas_call(functools.partial(totals_kernel, rate, block, len(pieces))...  5.41 us
    ppermute x17, waiting for transfers between devices, exchange(): return lax.ppermute(a, axes, [(partner(at), at) for at in range(count)])  4.47 us
    pallas_call x3, Pallas kernels, expo_call(): pl.pallas_call(functools.partial(expo_kernel, rate, block, spots), in_spe...  4.27 us
    pallas_call x2, Pallas kernels, sums_call(): pl.pallas_call(functools.partial(sums_kernel, n, block, side), in_specs=i...  3.89 us
    pallas_call x1, Pallas kernels, add_call(): pl.pallas_call(functools.partial(add_kernel, block), in_specs=in_vmem(4),...  1.79 us
    convert_element_type x1, other arithmetic, to_points(): return (scaled.astype(jnp.float32) * 2.0 ** (-16)).astype(jnp.bfloat16)  1.05 us
  transfers between devices with their start and end apart: 17, of which 6 were waited for; matrix products, arithmetic and copies ran while one was open for 0% of the time, Pallas kernels for 27%

profile of v21, /device:TPU:0, one launch (start us, length us, event | category | flops | bytes accessed | tf_op | source)
XLA Modules:
  0.0 46.0 jit_solution(4700672471796803318)
XLA Ops:
  0.6 1.1 %multiply_convert_fusion.above = bf16[128,512]{1,0:T(8,128)(2,1)S(1)} fusion(s32[128,512]{1,0:T(8,128)} %param.4, s32[128]{0:T(128)} %param.5), kind=kLoop, calls=%fused_computation | loop fusion | flops 327680 | bytes 393728 | tf_op jit(solution)/shard_map/convert_element_type | solution.py:17
  1.7 3.1 %collective-permute-start = (bf16[128,512]{1,0:T(8,128)(2,1)S(1)}, bf16[128,512]{1,0:T(8,128)(2,1)S(1)}, u32[]{:S(2)}, u32[]{:S(2)}) collective-permute-start(bf16[128,512]{1,0:T(8,128)(2,1)S(1)} %multiply_convert_fusion.above), channel_id=1, source_target_pairs={{1,0},{0,1},{3,2},{2,3},{5,4},{4,5},{7,6},{6,7},{9,8},{8,9},{11,10... | collective-permute-start | bytes 393224 | tf_op jit(solution)/shard_map/ppermute | solution.py:49
  4.8 2.6 %collective-permute-start.3 = (bf16[128,512]{1,0:T(8,128)(2,1)S(1)}, bf16[128,512]{1,0:T(8,128)(2,1)S(1)}, u32[]{:S(2)}, u32[]{:S(2)}) collective-permute-start(bf16[128,512]{1,0:T(8,128)(2,1)S(1)} %multiply_convert_fusion.above), channel_id=1, source_target_pairs={{2,0},{3,1},{0,2},{1,3},{6,4},{7,5},{4,6},{5,7},{10,8},{11,9},{8,1... | collective-permute-start | bytes 393224 | tf_op jit(solution)/shard_map/ppermute | solution.py:49
  7.4 0.0 collective-permute-start.4
  7.4 0.0 copy-start
  7.4 0.7 %copy-done = s32[6144]{0:T(1024)S(1)} copy-done((s32[6144]{0:T(1024)S(1)}, s32[6144]{0:T(1024)}, u32[]{:S(2)}) %copy-start) | copy-done | bytes 24600
  8.1 0.0 slice-start
  8.1 0.9 %shard_map.59.refs_0_.refs_2_ = f32[6144,128]{1,0:T(8,128)S(1)} custom-call(s32[48,128]{1,0:T(8,128)S(1)} %bitcast.4), custom_call_target="tpu_custom_call" | custom-call | flops 2000000000 | tf_op jit(solution)/shard_map/pallas_call | solution.py:114
  9.0 0.0 slice-start.1
  9.0 0.8 %collective-permute-done.below = bf16[128,512]{1,0:T(8,128)(2,1)S(1)} collective-permute-done((bf16[128,512]{1,0:T(8,128)(2,1)S(1)}, bf16[128,512]{1,0:T(8,128)(2,1)S(1)}, u32[]{:S(2)}, u32[]{:S(2)}) %collective-permute-start) | collective-permute-done | bytes 131104 | tf_op jit(solution)/shard_map/ppermute | solution.py:49
  9.8 1.8 %collective-permute-start.1 = (bf16[256,512]{1,0:T(8,128)(2,1)S(1)}, bf16[256,512]{1,0:T(8,128)(2,1)S(1)}, u32[]{:S(2)}, u32[]{:S(2)}) collective-permute-start(bf16[256,512]{1,0:T(8,128)(2,1)S(1)} %shard_map.60.a.refs_0_), channel_id=1, source_target_pairs={{8,0},{20,4},{0,8},{28,12},{24,16},{4,20},{16,24},{12,28},{9,1},{2... | collective-permute-start | bytes 786440 | tf_op jit(solution)/shard_map/ppermute | solution.py:49
  11.6 0.0 slice-done
  11.6 0.0 slice-done.1
  11.7 2.7 %shard_map.62.refs_0_.left = f32[3,256]{1,0:T(4,128)S(1)} custom-call(bf16[256,512]{1,0:T(8,128)(2,1)S(1)} %shard_map.61.refs_0_, bf16[6144,512]{1,0:T(8,128)(2,1)S(1)} %bitcast.3, f32[6144,128]{1,0:T(8,128)S(1)} %shard_map.59.refs_0_.refs_2_), custom_call_target="tpu_custom_call" | custom-call | flops 1610612736 | bytes 6291456 | tf_op jit(solution)/shard_map/pallas_call | solution.py:154
  14.4 1.6 %collective-permute-start.2 = (bf16[256,512]{1,0:T(8,128)(2,1)S(1)}, bf16[256,512]{1,0:T(8,128)(2,1)S(1)}, u32[]{:S(2)}, u32[]{:S(2)}) collective-permute-start(bf16[256,512]{1,0:T(8,128)(2,1)S(1)} %shard_map.63), channel_id=1, source_target_pairs={{16,0},{12,4},{24,8},{4,12},{0,16},{28,20},{8,24},{20,28},{17,1},{... | collective-permute-start | bytes 786440 | tf_op jit(solution)/shard_map/ppermute | solution.py:49
  16.0 0.6 %collective-permute-done.1.refs_3_.refs_1_.a = bf16[256,512]{1,0:T(8,128)(2,1)S(1)} collective-permute-done((bf16[256,512]{1,0:T(8,128)(2,1)S(1)}, bf16[256,512]{1,0:T(8,128)(2,1)S(1)}, u32[]{:S(2)}, u32[]{:S(2)}) %collective-permute-start.1) | collective-permute-done | bytes 262176 | tf_op jit(solution)/shard_map/ppermute | solution.py:49
  16.6 2.0 %collective-permute-start.5 = (bf16[256,512]{1,0:T(8,128)(2,1)S(1)}, bf16[256,512]{1,0:T(8,128)(2,1)S(1)}, u32[]{:S(2)}, u32[]{:S(2)}) collective-permute-start(bf16[256,512]{1,0:T(8,128)(2,1)S(1)} %shard_map.68), channel_id=1, source_target_pairs={{16,0},{12,4},{24,8},{4,12},{0,16},{28,20},{8,24},{20,28},{17,1},{... | collective-permute-start | bytes 786440 | tf_op jit(solution)/shard_map/ppermute | solution.py:49
  18.7 0.0 collective-permute-done.3.above
  18.7 0.0 collective-permute-done.4.below
  18.7 1.6 %collective-permute-start.6 = (bf16[256,512]{1,0:T(8,128)(2,1)S(1)}, bf16[256,512]{1,0:T(8,128)(2,1)S(1)}, u32[]{:S(2)}, u32[]{:S(2)}) collective-permute-start(bf16[256,512]{1,0:T(8,128)(2,1)S(1)} %shard_map.64.refs_0_.refs_3_.a), channel_id=1, source_target_pairs={{8,0},{20,4},{0,8},{28,12},{24,16},{4,20},{16,24},{12,28},{9,1},{2... | collective-permute-start | bytes 786440 | tf_op jit(solution)/shard_map/ppermute | solution.py:49
  20.2 2.7 %shard_map.65.right = f32[3,256]{1,0:T(4,128)S(1)} custom-call(bf16[256,512]{1,0:T(8,128)(2,1)S(1)} %shard_map.64.refs_0_.refs_3_.a, bf16[6144,512]{1,0:T(8,128)(2,1)S(1)} %bitcast.3, f32[6144,128]{1,0:T(8,128)S(1)} %shard_map.59.refs_0_.refs_2_, bf16[256,512]{1,0:T(8,128)(2,1)S(1)} %collective-permute-done.1.refs_3_.refs_1_.a), custom_call_target="tpu_custom_call" | custom-call | flops 1610612736 | bytes 6291456 | tf_op jit(solution)/shard_map/pallas_call | solution.py:154
  23.0 3.7 %collective-permute-start.10 = (f32[3,512]{1,0:T(4,128)S(1)}, f32[3,512]{1,0:T(4,128)S(1)}, u32[]{:S(2)}, u32[]{:S(2)}) collective-permute-start(f32[3,512]{1,0:T(4,128)S(1)} %shard_map.66.refs_5_.refs_0_), channel_id=1, source_target_pairs={{3,0},{2,1},{1,2},{0,3},{7,4},{6,5},{5,6},{4,7},{11,8},{10,9},{9,1... | collective-permute-start | bytes 18440 | tf_op jit(solution)/shard_map/ppermute | solution.py:49
  26.6 0.0 collective-permute-start.8
  26.6 0.0 collective-permute-done.2.refs_2_
  26.6 0.8 %collective-permute-start.9 = (f32[3,512]{1,0:T(4,128)S(1)}, f32[3,512]{1,0:T(4,128)S(1)}, u32[]{:S(2)}, u32[]{:S(2)}) collective-permute-start(f32[3,512]{1,0:T(4,128)S(1)} %shard_map.66.refs_5_.refs_0_), channel_id=1, source_target_pairs={{2,0},{3,1},{0,2},{1,3},{6,4},{7,5},{4,6},{5,7},{10,8},{11,9},{8,1... | collective-permute-start | bytes 18440 | tf_op jit(solution)/shard_map/ppermute | solution.py:49
  27.4 2.0 %shard_map.67 = (bf16[1536,1024]{1,0:T(8,128)(2,1)S(1)}, f32[6,1024]{1,0:T(8,128)S(1)}, bf16[1024,512]{1,0:T(8,128)(2,1)S(1)}) custom-call(bf16[256,512]{1,0:T(8,128)(2,1)S(1)} %shard_map.60.a.refs_0_, bf16[256,512]{1,0:T(8,128)(2,1)S(1)} %collective-permute-done.1.refs_3_.refs_1_.a, bf16[256,512]{1,0:T(8,128)(2,1)S(1)} %collective-permute-done.2.refs_2_, ...), custom_call_target="tpu_custom_call" | custom-call | flops 16106127 | bytes 57671 | tf_op jit(solution)/shard_map/pallas_call | solution.py:229
  29.5 0.0 collective-permute-done.10.refs_3_
  29.5 0.6 %collective-permute-start.7 = (bf16[256,512]{1,0:T(8,128)(2,1)S(1)}, bf16[256,512]{1,0:T(8,128)(2,1)S(1)}, u32[]{:S(2)}, u32[]{:S(2)}) collective-permute-start(bf16[256,512]{1,0:T(8,128)(2,1)S(1)} %shard_map.69), channel_id=1, source_target_pairs={{16,0},{12,4},{24,8},{4,12},{0,16},{28,20},{8,24},{20,28},{17,1},{... | collective-permute-start | bytes 786440 | tf_op jit(solution)/shard_map/ppermute | solution.py:49
  30.1 0.2 collective-permute-done.8.refs_1_
  30.3 0.9 %collective-permute-done.9.refs_2_ = f32[3,512]{1,0:T(4,128)S(1)} collective-permute-done((f32[3,512]{1,0:T(4,128)S(1)}, f32[3,512]{1,0:T(4,128)S(1)}, u32[]{:S(2)}, u32[]{:S(2)}) %collective-permute-start.9) | collective-permute-done | bytes 6176 | tf_op jit(solution)/shard_map/ppermute | solution.py:49
  31.2 0.0 collective-permute-done.5.refs_5_.refs_0_
  31.2 0.0 collective-permute-done.6.refs_1_.a
  31.3 0.6 %collective-permute-start.11 = (bf16[256,512]{1,0:T(8,128)(2,1)S(1)}, bf16[256,512]{1,0:T(8,128)(2,1)S(1)}, u32[]{:S(2)}, u32[]{:S(2)}) collective-permute-start(bf16[256,512]{1,0:T(8,128)(2,1)S(1)} %shard_map.72), channel_id=1, source_target_pairs={{16,0},{12,4},{24,8},{4,12},{0,16},{28,20},{8,24},{20,28},{17,1},{... | collective-permute-start | bytes 786440 | tf_op jit(solution)/shard_map/ppermute | solution.py:49
  31.8 0.6 %collective-permute-start.12 = (f32[2,512]{1,0:T(2,128)S(1)}, f32[2,512]{1,0:T(2,128)S(1)}, u32[]{:S(2)}, u32[]{:S(2)}) collective-permute-start(f32[2,512]{1,0:T(2,128)S(1)} %shard_map.70.refs_4_.refs_0_), channel_id=1, source_target_pairs={{8,0},{20,4},{0,8},{28,12},{24,16},{4,20},{16,24},{12,28},{9,1},{2... | collective-permute-start | bytes 12296 | tf_op jit(solution)/shard_map/ppermute | solution.py:49
  32.4 1.5 %collective-permute-start.13 = (f32[2,512]{1,0:T(2,128)S(1)}, f32[2,512]{1,0:T(2,128)S(1)}, u32[]{:S(2)}, u32[]{:S(2)}) collective-permute-start(f32[2,512]{1,0:T(2,128)S(1)} %shard_map.70.refs_4_.refs_0_), channel_id=1, source_target_pairs={{16,0},{12,4},{24,8},{4,12},{0,16},{28,20},{8,24},{20,28},{17,1},{... | collective-permute-start | bytes 12296 | tf_op jit(solution)/shard_map/ppermute | solution.py:49
  33.9 1.4 %collective-permute-start.14 = (f32[2,512]{1,0:T(2,128)S(1)}, f32[2,512]{1,0:T(2,128)S(1)}, u32[]{:S(2)}, u32[]{:S(2)}) collective-permute-start(f32[2,512]{1,0:T(2,128)S(1)} %shard_map.70.refs_4_.refs_0_), channel_id=1, source_target_pairs={{24,0},{16,8},{8,16},{0,24},{25,1},{17,9},{9,17},{1,25},{26,2},{18... | collective-permute-start | bytes 12296 | tf_op jit(solution)/shard_map/ppermute | solution.py:49
  35.3 0.6 %collective-permute-done.7.refs_2_ = bf16[256,512]{1,0:T(8,128)(2,1)S(1)} collective-permute-done((bf16[256,512]{1,0:T(8,128)(2,1)S(1)}, bf16[256,512]{1,0:T(8,128)(2,1)S(1)}, u32[]{:S(2)}, u32[]{:S(2)}) %collective-permute-start.7) | collective-permute-done | bytes 262176 | tf_op jit(solution)/shard_map/ppermute | solution.py:49
  36.0 1.6 %shard_map.71 = (bf16[1536,768]{1,0:T(8,128)(2,1)S(1)}, f32[6,768]{1,0:T(8,128)S(1)}, bf16[768,512]{1,0:T(8,128)(2,1)S(1)}) custom-call(bf16[256,512]{1,0:T(8,128)(2,1)S(1)} %collective-permute-done.5.refs_5_.refs_0_, bf16[256,512]{1,0:T(8,128)(2,1)S(1)} %collective-permute-done.6.refs_1_.a, bf16[256,512]{1,0:T(8,128)(2,1)S(1)} %collective-permute-done.7.refs_2_, ...), custom_call_target="tpu_custom_call" | custom-call | flops 12079595 | bytes 47185 | tf_op jit(solution)/shard_map/pallas_call | solution.py:229
  37.5 1.3 %collective-permute-done.11.refs_0_ = bf16[256,512]{1,0:T(8,128)(2,1)S(1)} collective-permute-done((bf16[256,512]{1,0:T(8,128)(2,1)S(1)}, bf16[256,512]{1,0:T(8,128)(2,1)S(1)}, u32[]{:S(2)}, u32[]{:S(2)}) %collective-permute-start.11) | collective-permute-done | bytes 262176 | tf_op jit(solution)/shard_map/ppermute | solution.py:49
  38.8 0.7 %shard_map.73 = (bf16[1536,256]{1,0:T(8,128)(2,1)S(1)}, f32[6,256]{1,0:T(8,128)S(1)}, bf16[256,512]{1,0:T(8,128)(2,1)S(1)}) custom-call(bf16[256,512]{1,0:T(8,128)(2,1)S(1)} %collective-permute-done.11.refs_0_, bf16[6144,512]{1,0:T(8,128)(2,1)S(1)} %bitcast.3, f32[6,768]{1,0:T(8,128)S(1)} %get-tuple-element.23.refs_2_.refs_5_), custom_call_target="tpu_custom_call" | custom-call | flops 402653184 | bytes 2621440 | tf_op jit(solution)/shard_map/pallas_call | solution.py:229
  39.5 0.0 collective-permute-done.12.refs_1_
  39.5 0.0 collective-permute-done.13.refs_2_
  39.6 0.0 collective-permute-done.14.refs_3_
  39.6 2.1 %shard_map.76 = (bf16[768,512]{1,0:T(8,128)(2,1)S(1)}, f32[1,768]{1,0:T(1,128)S(1)}) custom-call(bf16[1536,1024]{1,0:T(8,128)(2,1)S(1)} %get-tuple-element.20.refs_0_, bf16[1536,768]{1,0:T(8,128)(2,1)S(1)} %get-tuple-element.22.refs_1_, bf16[1536,256]{1,0:T(8,128)(2,1)S(1)} %get-tuple-element.24.refs_2_, bf16[1024,512]{1,0:T(8,128)(2,1)S(1)} %get-tuple-element.25.refs_3_, ...), custom_call_target="tpu_custom_call" | custom-call | flops 2415919104 | bytes 9437184 | tf_op jit(solution)/shard_map/pallas_call | solution.py:278
  41.7 0.1 collective-permute-start.15
  41.7 0.5 %collective-permute-start.16 = (f32[1,768]{1,0:T(1,128)S(1)}, f32[1,768]{1,0:T(1,128)S(1)}, u32[]{:S(2)}, u32[]{:S(2)}) collective-permute-start(f32[1,768]{1,0:T(1,128)S(1)} %get-tuple-element.35), channel_id=1, source_target_pairs={{4,0},{0,4},{5,1},{1,5},{6,2},{2,6},{7,3},{3,7},{12,8},{8,12},{13,... | collective-permute-start | bytes 9224 | tf_op jit(solution)/shard_map/ppermute | solution.py:49
  42.2 1.8 %shard_map.75 = (f32[768,512]{1,0:T(8,128)S(1)}, f32[1,768]{1,0:T(1,128)S(1)}) custom-call(bf16[1536,1024]{1,0:T(8,128)(2,1)S(1)} %get-tuple-element.20.refs_0_, bf16[1536,768]{1,0:T(8,128)(2,1)S(1)} %get-tuple-element.22.refs_1_, bf16[1536,256]{1,0:T(8,128)(2,1)S(1)} %get-tuple-element.24.refs_2_, bf16[1024,512]{1,0:T(8,128)(2,1)S(1)} %get-tuple-element.25.refs_3_, ...), custom_call_target="tpu_custom_call" | custom-call | flops 2415919104 | bytes 9437184 | tf_op jit(solution)/shard_map/pallas_call | solution.py:278
  44.1 0.0 collective-permute-done.16.there_mass
  44.1 0.0 collective-permute-done.15.there
  44.1 1.8 %shard_map.77 = (f32[768,512]{1,0:T(8,128)}, f32[1,768]{1,0:T(1,128)}) custom-call(f32[768,512]{1,0:T(8,128)S(1)} %get-tuple-element.32.here, f32[1,768]{1,0:T(1,128)S(1)} %get-tuple-element.33.here_mass, bf16[768,512]{1,0:T(8,128)(2,1)S(1)} %collective-permute-done.15.there, f32[1,768]{1,0:T(1,128)S(1)} %collective-permute-done.16.there_mass), custom_call_target="tpu_custom_call" | custom-call | tf_op jit(solution)/shard_map/pallas_call | solution.py:308
  (11 shorter events, 0.2 us)
Async XLA Ops:
  1.7 8.1 %collective-permute-start = (bf16[128,512]{1,0:T(8,128)(2,1)S(1)}, bf16[128,512]{1,0:T(8,128)(2,1)S(1)}, u32[]{:S(2)}, u32[]{:S(2)}) collective-permute-start(bf16[128,512]{1,0:T(8,128)(2,1)S(1)} %multiply_convert_fusion.above), channel_id=1, source_target_pairs={{1,0},{0,1},{3,2},{2,3},{5,4},{4,5},{7,6},{6,7},{9,8},{8,9},{11,10... | collective-permute-start | bytes 393224 | tf_op jit(solution)/shard_map/ppermute | solution.py:49
  4.8 13.9 %collective-permute-start.3 = (bf16[128,512]{1,0:T(8,128)(2,1)S(1)}, bf16[128,512]{1,0:T(8,128)(2,1)S(1)}, u32[]{:S(2)}, u32[]{:S(2)}) collective-permute-start(bf16[128,512]{1,0:T(8,128)(2,1)S(1)} %multiply_convert_fusion.above), channel_id=1, source_target_pairs={{2,0},{3,1},{0,2},{1,3},{6,4},{7,5},{4,6},{5,7},{10,8},{11,9},{8,1... | collective-permute-start | bytes 393224 | tf_op jit(solution)/shard_map/ppermute | solution.py:49
  7.4 11.3 %collective-permute-start.4 = (bf16[128,512]{1,0:T(8,128)(2,1)S(1)}, bf16[128,512]{1,0:T(8,128)(2,1)S(1)}, u32[]{:S(2)}, u32[]{:S(2)}) collective-permute-start(bf16[128,512]{1,0:T(8,128)(2,1)S(1)} %multiply_convert_fusion.above), channel_id=1, source_target_pairs={{3,0},{2,1},{1,2},{0,3},{7,4},{6,5},{5,6},{4,7},{11,8},{10,9},{9,1... | collective-permute-start | bytes 393224 | tf_op jit(solution)/shard_map/ppermute | solution.py:49
  7.4 0.7 %copy-start = (s32[6144]{0:T(1024)S(1)}, s32[6144]{0:T(1024)}, u32[]{:S(2)}) copy-start(s32[6144]{0:T(1024)} %param.7) | copy-start | bytes 73732
  8.1 3.5 %slice-start = ((s8[6291456]{0:T(1024)(128)(4,1)}), s8[4194304]{0:T(1024)(128)(4,1)S(1)}, s32[]{:S(2)}) async-start(s8[6291456]{0:T(1024)(128)(4,1)} %bitcast.2), calls=%async_computation | async-start | bytes 8388608
  9.0 2.6 %slice-start.1 = ((s8[6291456]{0:T(1024)(128)(4,1)}), s8[2097152]{0:T(1024)(128)(4,1)S(1)}, s32[]{:S(2)}) async-start(s8[6291456]{0:T(1024)(128)(4,1)} %bitcast.2), calls=%async_computation.1 | async-start | bytes 4194304
  9.8 6.8 %collective-permute-start.1 = (bf16[256,512]{1,0:T(8,128)(2,1)S(1)}, bf16[256,512]{1,0:T(8,128)(2,1)S(1)}, u32[]{:S(2)}, u32[]{:S(2)}) collective-permute-start(bf16[256,512]{1,0:T(8,128)(2,1)S(1)} %shard_map.60.a.refs_0_), channel_id=1, source_target_pairs={{8,0},{20,4},{0,8},{28,12},{24,16},{4,20},{16,24},{12,28},{9,1},{2... | collective-permute-start | bytes 786440 | tf_op jit(solution)/shard_map/ppermute | solution.py:49
  14.4 12.3 %collective-permute-start.2 = (bf16[256,512]{1,0:T(8,128)(2,1)S(1)}, bf16[256,512]{1,0:T(8,128)(2,1)S(1)}, u32[]{:S(2)}, u32[]{:S(2)}) collective-permute-start(bf16[256,512]{1,0:T(8,128)(2,1)S(1)} %shard_map.63), channel_id=1, source_target_pairs={{16,0},{12,4},{24,8},{4,12},{0,16},{28,20},{8,24},{20,28},{17,1},{... | collective-permute-start | bytes 786440 | tf_op jit(solution)/shard_map/ppermute | solution.py:49
  16.6 14.6 %collective-permute-start.5 = (bf16[256,512]{1,0:T(8,128)(2,1)S(1)}, bf16[256,512]{1,0:T(8,128)(2,1)S(1)}, u32[]{:S(2)}, u32[]{:S(2)}) collective-permute-start(bf16[256,512]{1,0:T(8,128)(2,1)S(1)} %shard_map.68), channel_id=1, source_target_pairs={{16,0},{12,4},{24,8},{4,12},{0,16},{28,20},{8,24},{20,28},{17,1},{... | collective-permute-start | bytes 786440 | tf_op jit(solution)/shard_map/ppermute | solution.py:49
  18.7 12.6 %collective-permute-start.6 = (bf16[256,512]{1,0:T(8,128)(2,1)S(1)}, bf16[256,512]{1,0:T(8,128)(2,1)S(1)}, u32[]{:S(2)}, u32[]{:S(2)}) collective-permute-start(bf16[256,512]{1,0:T(8,128)(2,1)S(1)} %shard_map.64.refs_0_.refs_3_.a), channel_id=1, source_target_pairs={{8,0},{20,4},{0,8},{28,12},{24,16},{4,20},{16,24},{12,28},{9,1},{2... | collective-permute-start | bytes 786440 | tf_op jit(solution)/shard_map/ppermute | solution.py:49
  23.0 6.5 %collective-permute-start.10 = (f32[3,512]{1,0:T(4,128)S(1)}, f32[3,512]{1,0:T(4,128)S(1)}, u32[]{:S(2)}, u32[]{:S(2)}) collective-permute-start(f32[3,512]{1,0:T(4,128)S(1)} %shard_map.66.refs_5_.refs_0_), channel_id=1, source_target_pairs={{3,0},{2,1},{1,2},{0,3},{7,4},{6,5},{5,6},{4,7},{11,8},{10,9},{9,1... | collective-permute-start | bytes 18440 | tf_op jit(solution)/shard_map/ppermute | solution.py:49
  26.6 3.7 %collective-permute-start.8 = (f32[3,512]{1,0:T(4,128)S(1)}, f32[3,512]{1,0:T(4,128)S(1)}, u32[]{:S(2)}, u32[]{:S(2)}) collective-permute-start(f32[3,512]{1,0:T(4,128)S(1)} %shard_map.66.refs_5_.refs_0_), channel_id=1, source_target_pairs={{1,0},{0,1},{3,2},{2,3},{5,4},{4,5},{7,6},{6,7},{9,8},{8,9},{11,10... | collective-permute-start | bytes 18440 | tf_op jit(solution)/shard_map/ppermute | solution.py:49
  26.6 4.6 %collective-permute-start.9 = (f32[3,512]{1,0:T(4,128)S(1)}, f32[3,512]{1,0:T(4,128)S(1)}, u32[]{:S(2)}, u32[]{:S(2)}) collective-permute-start(f32[3,512]{1,0:T(4,128)S(1)} %shard_map.66.refs_5_.refs_0_), channel_id=1, source_target_pairs={{2,0},{3,1},{0,2},{1,3},{6,4},{7,5},{4,6},{5,7},{10,8},{11,9},{8,1... | collective-permute-start | bytes 18440 | tf_op jit(solution)/shard_map/ppermute | solution.py:49
  29.5 6.5 %collective-permute-start.7 = (bf16[256,512]{1,0:T(8,128)(2,1)S(1)}, bf16[256,512]{1,0:T(8,128)(2,1)S(1)}, u32[]{:S(2)}, u32[]{:S(2)}) collective-permute-start(bf16[256,512]{1,0:T(8,128)(2,1)S(1)} %shard_map.69), channel_id=1, source_target_pairs={{16,0},{12,4},{24,8},{4,12},{0,16},{28,20},{8,24},{20,28},{17,1},{... | collective-permute-start | bytes 786440 | tf_op jit(solution)/shard_map/ppermute | solution.py:49
  31.3 7.6 %collective-permute-start.11 = (bf16[256,512]{1,0:T(8,128)(2,1)S(1)}, bf16[256,512]{1,0:T(8,128)(2,1)S(1)}, u32[]{:S(2)}, u32[]{:S(2)}) collective-permute-start(bf16[256,512]{1,0:T(8,128)(2,1)S(1)} %shard_map.72), channel_id=1, source_target_pairs={{16,0},{12,4},{24,8},{4,12},{0,16},{28,20},{8,24},{20,28},{17,1},{... | collective-permute-start | bytes 786440 | tf_op jit(solution)/shard_map/ppermute | solution.py:49
  31.8 7.7 %collective-permute-start.12 = (f32[2,512]{1,0:T(2,128)S(1)}, f32[2,512]{1,0:T(2,128)S(1)}, u32[]{:S(2)}, u32[]{:S(2)}) collective-permute-start(f32[2,512]{1,0:T(2,128)S(1)} %shard_map.70.refs_4_.refs_0_), channel_id=1, source_target_pairs={{8,0},{20,4},{0,8},{28,12},{24,16},{4,20},{16,24},{12,28},{9,1},{2... | collective-permute-start | bytes 12296 | tf_op jit(solution)/shard_map/ppermute | solution.py:49
  32.4 7.1 %collective-permute-start.13 = (f32[2,512]{1,0:T(2,128)S(1)}, f32[2,512]{1,0:T(2,128)S(1)}, u32[]{:S(2)}, u32[]{:S(2)}) collective-permute-start(f32[2,512]{1,0:T(2,128)S(1)} %shard_map.70.refs_4_.refs_0_), channel_id=1, source_target_pairs={{16,0},{12,4},{24,8},{4,12},{0,16},{28,20},{8,24},{20,28},{17,1},{... | collective-permute-start | bytes 12296 | tf_op jit(solution)/shard_map/ppermute | solution.py:49
  33.9 5.6 %collective-permute-start.14 = (f32[2,512]{1,0:T(2,128)S(1)}, f32[2,512]{1,0:T(2,128)S(1)}, u32[]{:S(2)}, u32[]{:S(2)}) collective-permute-start(f32[2,512]{1,0:T(2,128)S(1)} %shard_map.70.refs_4_.refs_0_), channel_id=1, source_target_pairs={{24,0},{16,8},{8,16},{0,24},{25,1},{17,9},{9,17},{1,25},{26,2},{18... | collective-permute-start | bytes 12296 | tf_op jit(solution)/shard_map/ppermute | solution.py:49
  41.7 2.4 %collective-permute-start.15 = (bf16[768,512]{1,0:T(8,128)(2,1)S(1)}, bf16[768,512]{1,0:T(8,128)(2,1)S(1)}, u32[]{:S(2)}, u32[]{:S(2)}) collective-permute-start(bf16[768,512]{1,0:T(8,128)(2,1)S(1)} %get-tuple-element.34), channel_id=1, source_target_pairs={{4,0},{0,4},{5,1},{1,5},{6,2},{2,6},{7,3},{3,7},{12,8},{8,12},{13,... | collective-permute-start | bytes 2359304 | tf_op jit(solution)/shard_map/ppermute | solution.py:49
  41.7 2.3 %collective-permute-start.16 = (f32[1,768]{1,0:T(1,128)S(1)}, f32[1,768]{1,0:T(1,128)S(1)}, u32[]{:S(2)}, u32[]{:S(2)}) collective-permute-start(f32[1,768]{1,0:T(1,128)S(1)} %get-tuple-element.35), channel_id=1, source_target_pairs={{4,0},{0,4},{5,1},{1,5},{6,2},{2,6},{7,3},{3,7},{12,8},{8,12},{13,... | collective-permute-start | bytes 9224 | tf_op jit(solution)/shard_map/ppermute | solution.py:49

commit v22 on v21

--- a/solution.py
+++ b/solution.py
@@ -186,7 +186,7 @@
 def factor_kernel(rate, n, *refs):
     goals, tops, factors = refs[:4], refs[4 : 4 + n], refs[4 + n :]
     rows = goals[0].shape[1] // 2
-    spots = [(0, 0, 0), (0, 0, 1), (0, 0, 2), (0, 1, 0), (1, 0, 3), (1, 1, 1), (1, 1, 2), (2, 1, 3)]
+    spots = [(0, 0, 0), (0, 0, 1), (0, 0, 2), (0, 1, 0), (1, 0, 3), (1, 1, 1), (1, 1, 3), (2, 1, 2)]
     for at, (bundle, group, goal) in enumerate(spots):
         start = (at - (0, 4, 7)[bundle]) * rows
         mine, here = slice(group * rows, (group + 1) * rows), slice(start, start + rows)
@@ -348,11 +348,9 @@
     expand = functools.partial(expo_call, rate, block, 2 * per_device)
     bundles = [expand((near_01, first_01, second_01, near_23), centroids, stat, declared=0.01)]
     goal = goal_call(rate, stat, *(along_z(stat, by) for by in (1, 2, 3)), bundles[0][1], across_01)
-    across_23 = turn_back(hold(first_23, goal))
-
-    second_23 = turn_back(hold(near_23, bundles[0][1]))
-    bundles.append(expand((across_01, first_23, second_23), centroids, goal, declared=0.01))
-    bundles.append(expand((across_23,), centroids, bundles[1][1]))
+    across_23, second_23 = turn_back(hold(first_23, bundles[0][1])), turn_back(hold(near_23, goal))
+    bundles.append(expand((across_01, first_23, across_23), centroids, goal, declared=0.01))
+    bundles.append(expand((second_23,), centroids, bundles[1][1]))
     expos, tops, points = zip(*bundles)
     goals = [goal, turn(goal), turn_back(goal), around(goal, 3)]
     factors = factor_call(rate, goals, tops)

time: 46.2 us -> 46.9 us (1.015)
  waiting for transfers between devices: 4.47 us -> 5.62 us
  starting transfers between devices: 22.3 us -> 21.8 us
    ppermute x17, waiting for transfers between devices: 4.47 us -> 5.62 us  [exchange(): return lax.ppermute(a, axes, [(partner(at), at) for at in range(count)])]
    ppermute x17, starting transfers between devices: 22.3 us -> 21.8 us  [exchange(): return lax.ppermute(a, axes, [(partner(at), at) for at in range(count)])]
  transfers between devices with their start and end apart: 17 -> 17, of which waited for: 6 -> 5; matrix products, arithmetic and copies ran while one was open for 0% -> 0% of each run, Pallas kernels for 27% -> 27%
where the time goes in v22:
time: 46.9 us; the launch traced here: 46.7 us
  starting transfers between devices  21.8 us (46%)
  Pallas kernels  16.4 us (35%)
  waiting for transfers between devices  5.62 us (12%)
  other arithmetic  1.05 us (2%)
  between operations  1 us (2%)
  local copies, waits for them, and re-layouts  0.75 us (2%)
    ppermute x17, starting transfers between devices, exchange(): return lax.ppermute(a, axes, [(partner(at), at) for at in range(count)])  21.8 us
    ppermute x17, waiting for transfers between devices, exchange(): return lax.ppermute(a, axes, [(partner(at), at) for at in range(count)])  5.62 us
    pallas_call x2, Pallas kernels, totals_call(): pl.pallas_call(functools.partial(totals_kernel, rate, block, len(pieces))...  5.4 us
    pallas_call x3, Pallas kernels, expo_call(): pl.pallas_call(functools.partial(expo_kernel, rate, block, spots), in_spe...  4.27 us
    pallas_call x2, Pallas kernels, sums_call(): pl.pallas_call(functools.partial(sums_kernel, n, block, side), in_specs=i...  3.9 us
    pallas_call x1, Pallas kernels, add_call(): pl.pallas_call(functools.partial(add_kernel, block), in_specs=in_vmem(4),...  1.79 us
    convert_element_type x1, other arithmetic, to_points(): return (scaled.astype(jnp.float32) * 2.0 ** (-16)).astype(jnp.bfloat16)  1.05 us
  transfers between devices with their start and end apart: 17, of which 5 were waited for; matrix products, arithmetic and copies ran while one was open for 0% of the time, Pallas kernels for 27%

profile of v22, /device:TPU:0, one launch (start us, length us, event | category | flops | bytes accessed | tf_op | source)
XLA Modules:
  0.0 46.7 jit_solution(13020493159778306496)
XLA Ops:
  0.6 1.1 %multiply_convert_fusion.above = bf16[128,512]{1,0:T(8,128)(2,1)S(1)} fusion(s32[128,512]{1,0:T(8,128)} %param.4, s32[128]{0:T(128)} %param.5), kind=kLoop, calls=%fused_computation | loop fusion | flops 327680 | bytes 393728 | tf_op jit(solution)/shard_map/convert_element_type | solution.py:17
  1.7 3.1 %collective-permute-start = (bf16[128,512]{1,0:T(8,128)(2,1)S(1)}, bf16[128,512]{1,0:T(8,128)(2,1)S(1)}, u32[]{:S(2)}, u32[]{:S(2)}) collective-permute-start(bf16[128,512]{1,0:T(8,128)(2,1)S(1)} %multiply_convert_fusion.above), channel_id=1, source_target_pairs={{1,0},{0,1},{3,2},{2,3},{5,4},{4,5},{7,6},{6,7},{9,8},{8,9},{11,10... | collective-permute-start | bytes 393224 | tf_op jit(solution)/shard_map/ppermute | solution.py:49
  4.8 2.6 %collective-permute-start.3 = (bf16[128,512]{1,0:T(8,128)(2,1)S(1)}, bf16[128,512]{1,0:T(8,128)(2,1)S(1)}, u32[]{:S(2)}, u32[]{:S(2)}) collective-permute-start(bf16[128,512]{1,0:T(8,128)(2,1)S(1)} %multiply_convert_fusion.above), channel_id=1, source_target_pairs={{2,0},{3,1},{0,2},{1,3},{6,4},{7,5},{4,6},{5,7},{10,8},{11,9},{8,1... | collective-permute-start | bytes 393224 | tf_op jit(solution)/shard_map/ppermute | solution.py:49
  7.4 0.0 collective-permute-start.4
  7.4 0.0 copy-start
  7.4 0.7 %copy-done = s32[6144]{0:T(1024)S(1)} copy-done((s32[6144]{0:T(1024)S(1)}, s32[6144]{0:T(1024)}, u32[]{:S(2)}) %copy-start) | copy-done | bytes 24600
  8.1 0.0 slice-start
  8.1 0.9 %shard_map.59.refs_0_.refs_2_ = f32[6144,128]{1,0:T(8,128)S(1)} custom-call(s32[48,128]{1,0:T(8,128)S(1)} %bitcast.4), custom_call_target="tpu_custom_call" | custom-call | flops 2000000000 | tf_op jit(solution)/shard_map/pallas_call | solution.py:114
  9.0 0.0 slice-start.1
  9.0 0.8 %collective-permute-done.below = bf16[128,512]{1,0:T(8,128)(2,1)S(1)} collective-permute-done((bf16[128,512]{1,0:T(8,128)(2,1)S(1)}, bf16[128,512]{1,0:T(8,128)(2,1)S(1)}, u32[]{:S(2)}, u32[]{:S(2)}) %collective-permute-start) | collective-permute-done | bytes 131104 | tf_op jit(solution)/shard_map/ppermute | solution.py:49
  9.8 1.8 %collective-permute-start.1 = (bf16[256,512]{1,0:T(8,128)(2,1)S(1)}, bf16[256,512]{1,0:T(8,128)(2,1)S(1)}, u32[]{:S(2)}, u32[]{:S(2)}) collective-permute-start(bf16[256,512]{1,0:T(8,128)(2,1)S(1)} %shard_map.60.a.refs_0_), channel_id=1, source_target_pairs={{8,0},{20,4},{0,8},{28,12},{24,16},{4,20},{16,24},{12,28},{9,1},{2... | collective-permute-start | bytes 786440 | tf_op jit(solution)/shard_map/ppermute | solution.py:49
  11.6 0.0 slice-done
  11.6 0.0 slice-done.1
  11.7 2.7 %shard_map.62.refs_0_.left = f32[3,256]{1,0:T(4,128)S(1)} custom-call(bf16[256,512]{1,0:T(8,128)(2,1)S(1)} %shard_map.61.refs_0_, bf16[6144,512]{1,0:T(8,128)(2,1)S(1)} %bitcast.3, f32[6144,128]{1,0:T(8,128)S(1)} %shard_map.59.refs_0_.refs_2_), custom_call_target="tpu_custom_call" | custom-call | flops 1610612736 | bytes 6291456 | tf_op jit(solution)/shard_map/pallas_call | solution.py:154
  14.4 1.6 %collective-permute-start.2 = (bf16[256,512]{1,0:T(8,128)(2,1)S(1)}, bf16[256,512]{1,0:T(8,128)(2,1)S(1)}, u32[]{:S(2)}, u32[]{:S(2)}) collective-permute-start(bf16[256,512]{1,0:T(8,128)(2,1)S(1)} %shard_map.63), channel_id=1, source_target_pairs={{16,0},{12,4},{24,8},{4,12},{0,16},{28,20},{8,24},{20,28},{17,1},{... | collective-permute-start | bytes 786440 | tf_op jit(solution)/shard_map/ppermute | solution.py:49
  16.0 1.7 %collective-permute-done.3.above = bf16[128,512]{1,0:T(8,128)(2,1)S(1)} collective-permute-done((bf16[128,512]{1,0:T(8,128)(2,1)S(1)}, bf16[128,512]{1,0:T(8,128)(2,1)S(1)}, u32[]{:S(2)}, u32[]{:S(2)}) %collective-permute-start.3) | collective-permute-done | bytes 131104 | tf_op jit(solution)/shard_map/ppermute | solution.py:49
  17.7 0.0 collective-permute-done.4.below
  17.7 1.6 %collective-permute-start.6 = (bf16[256,512]{1,0:T(8,128)(2,1)S(1)}, bf16[256,512]{1,0:T(8,128)(2,1)S(1)}, u32[]{:S(2)}, u32[]{:S(2)}) collective-permute-start(bf16[256,512]{1,0:T(8,128)(2,1)S(1)} %shard_map.64.refs_0_.refs_3_.a), channel_id=1, source_target_pairs={{8,0},{20,4},{0,8},{28,12},{24,16},{4,20},{16,24},{12,28},{9,1},{2... | collective-permute-start | bytes 786440 | tf_op jit(solution)/shard_map/ppermute | solution.py:49
  19.3 0.0 collective-permute-done.1.refs_3_.refs_1_.a
  19.3 1.6 %collective-permute-start.5 = (bf16[256,512]{1,0:T(8,128)(2,1)S(1)}, bf16[256,512]{1,0:T(8,128)(2,1)S(1)}, u32[]{:S(2)}, u32[]{:S(2)}) collective-permute-start(bf16[256,512]{1,0:T(8,128)(2,1)S(1)} %shard_map.68), channel_id=1, source_target_pairs={{16,0},{12,4},{24,8},{4,12},{0,16},{28,20},{8,24},{20,28},{17,1},{... | collective-permute-start | bytes 786440 | tf_op jit(solution)/shard_map/ppermute | solution.py:49
  20.9 2.7 %shard_map.65.right = f32[3,256]{1,0:T(4,128)S(1)} custom-call(bf16[256,512]{1,0:T(8,128)(2,1)S(1)} %shard_map.64.refs_0_.refs_3_.a, bf16[6144,512]{1,0:T(8,128)(2,1)S(1)} %bitcast.3, f32[6144,128]{1,0:T(8,128)S(1)} %shard_map.59.refs_0_.refs_2_, bf16[256,512]{1,0:T(8,128)(2,1)S(1)} %collective-permute-done.1.refs_3_.refs_1_.a), custom_call_target="tpu_custom_call" | custom-call | flops 1610612736 | bytes 6291456 | tf_op jit(solution)/shard_map/pallas_call | solution.py:154
  23.6 2.4 %collective-permute-start.10 = (f32[3,512]{1,0:T(4,128)S(1)}, f32[3,512]{1,0:T(4,128)S(1)}, u32[]{:S(2)}, u32[]{:S(2)}) collective-permute-start(f32[3,512]{1,0:T(4,128)S(1)} %shard_map.66.refs_5_.refs_0_), channel_id=1, source_target_pairs={{3,0},{2,1},{1,2},{0,3},{7,4},{6,5},{5,6},{4,7},{11,8},{10,9},{9,1... | collective-permute-start | bytes 18440 | tf_op jit(solution)/shard_map/ppermute | solution.py:49
  26.0 1.2 %collective-permute-start.8 = (f32[3,512]{1,0:T(4,128)S(1)}, f32[3,512]{1,0:T(4,128)S(1)}, u32[]{:S(2)}, u32[]{:S(2)}) collective-permute-start(f32[3,512]{1,0:T(4,128)S(1)} %shard_map.66.refs_5_.refs_0_), channel_id=1, source_target_pairs={{1,0},{0,1},{3,2},{2,3},{5,4},{4,5},{7,6},{6,7},{9,8},{8,9},{11,10... | collective-permute-start | bytes 18440 | tf_op jit(solution)/shard_map/ppermute | solution.py:49
  27.2 0.0 collective-permute-done.2.refs_2_
  27.2 0.9 %collective-permute-start.9 = (f32[3,512]{1,0:T(4,128)S(1)}, f32[3,512]{1,0:T(4,128)S(1)}, u32[]{:S(2)}, u32[]{:S(2)}) collective-permute-start(f32[3,512]{1,0:T(4,128)S(1)} %shard_map.66.refs_5_.refs_0_), channel_id=1, source_target_pairs={{2,0},{3,1},{0,2},{1,3},{6,4},{7,5},{4,6},{5,7},{10,8},{11,9},{8,1... | collective-permute-start | bytes 18440 | tf_op jit(solution)/shard_map/ppermute | solution.py:49
  28.1 2.0 %shard_map.67 = (bf16[1536,1024]{1,0:T(8,128)(2,1)S(1)}, f32[6,1024]{1,0:T(8,128)S(1)}, bf16[1024,512]{1,0:T(8,128)(2,1)S(1)}) custom-call(bf16[256,512]{1,0:T(8,128)(2,1)S(1)} %shard_map.60.a.refs_0_, bf16[256,512]{1,0:T(8,128)(2,1)S(1)} %collective-permute-done.1.refs_3_.refs_1_.a, bf16[256,512]{1,0:T(8,128)(2,1)S(1)} %collective-permute-done.2.refs_2_, ...), custom_call_target="tpu_custom_call" | custom-call | flops 16106127 | bytes 57671 | tf_op jit(solution)/shard_map/pallas_call | solution.py:229
  30.1 0.0 collective-permute-done.6.a.refs_1_
  30.1 0.6 %collective-permute-start.7 = (bf16[256,512]{1,0:T(8,128)(2,1)S(1)}, bf16[256,512]{1,0:T(8,128)(2,1)S(1)}, u32[]{:S(2)}, u32[]{:S(2)}) collective-permute-start(bf16[256,512]{1,0:T(8,128)(2,1)S(1)} %shard_map.69), channel_id=1, source_target_pairs={{16,0},{12,4},{24,8},{4,12},{0,16},{28,20},{8,24},{20,28},{17,1},{... | collective-permute-start | bytes 786440 | tf_op jit(solution)/shard_map/ppermute | solution.py:49
  30.7 0.0 collective-permute-done.10.refs_3_
  30.7 0.0 collective-permute-done.8.refs_1_
  30.7 1.1 %collective-permute-done.9.refs_2_ = f32[3,512]{1,0:T(4,128)S(1)} collective-permute-done((f32[3,512]{1,0:T(4,128)S(1)}, f32[3,512]{1,0:T(4,128)S(1)}, u32[]{:S(2)}, u32[]{:S(2)}) %collective-permute-start.9) | collective-permute-done | bytes 6176 | tf_op jit(solution)/shard_map/ppermute | solution.py:49
  31.8 0.0 collective-permute-done.5.refs_5_.refs_0_
  31.8 0.6 %collective-permute-start.11 = (bf16[256,512]{1,0:T(8,128)(2,1)S(1)}, bf16[256,512]{1,0:T(8,128)(2,1)S(1)}, u32[]{:S(2)}, u32[]{:S(2)}) collective-permute-start(bf16[256,512]{1,0:T(8,128)(2,1)S(1)} %shard_map.72), channel_id=1, source_target_pairs={{16,0},{12,4},{24,8},{4,12},{0,16},{28,20},{8,24},{20,28},{17,1},{... | collective-permute-start | bytes 786440 | tf_op jit(solution)/shard_map/ppermute | solution.py:49
  32.4 0.5 %collective-permute-start.12 = (f32[2,512]{1,0:T(2,128)S(1)}, f32[2,512]{1,0:T(2,128)S(1)}, u32[]{:S(2)}, u32[]{:S(2)}) collective-permute-start(f32[2,512]{1,0:T(2,128)S(1)} %shard_map.70.refs_4_.refs_0_), channel_id=1, source_target_pairs={{8,0},{20,4},{0,8},{28,12},{24,16},{4,20},{16,24},{12,28},{9,1},{2... | collective-permute-start | bytes 12296 | tf_op jit(solution)/shard_map/ppermute | solution.py:49
  32.9 1.5 %collective-permute-start.13 = (f32[2,512]{1,0:T(2,128)S(1)}, f32[2,512]{1,0:T(2,128)S(1)}, u32[]{:S(2)}, u32[]{:S(2)}) collective-permute-start(f32[2,512]{1,0:T(2,128)S(1)} %shard_map.70.refs_4_.refs_0_), channel_id=1, source_target_pairs={{16,0},{12,4},{24,8},{4,12},{0,16},{28,20},{8,24},{20,28},{17,1},{... | collective-permute-start | bytes 12296 | tf_op jit(solution)/shard_map/ppermute | solution.py:49
  34.5 1.4 %collective-permute-start.14 = (f32[2,512]{1,0:T(2,128)S(1)}, f32[2,512]{1,0:T(2,128)S(1)}, u32[]{:S(2)}, u32[]{:S(2)}) collective-permute-start(f32[2,512]{1,0:T(2,128)S(1)} %shard_map.70.refs_4_.refs_0_), channel_id=1, source_target_pairs={{24,0},{16,8},{8,16},{0,24},{25,1},{17,9},{9,17},{1,25},{26,2},{18... | collective-permute-start | bytes 12296 | tf_op jit(solution)/shard_map/ppermute | solution.py:49
  35.9 0.7 %collective-permute-done.7.refs_2_ = bf16[256,512]{1,0:T(8,128)(2,1)S(1)} collective-permute-done((bf16[256,512]{1,0:T(8,128)(2,1)S(1)}, bf16[256,512]{1,0:T(8,128)(2,1)S(1)}, u32[]{:S(2)}, u32[]{:S(2)}) %collective-permute-start.7) | collective-permute-done | bytes 262176 | tf_op jit(solution)/shard_map/ppermute | solution.py:49
  36.6 1.6 %shard_map.71 = (bf16[1536,768]{1,0:T(8,128)(2,1)S(1)}, f32[6,768]{1,0:T(8,128)S(1)}, bf16[768,512]{1,0:T(8,128)(2,1)S(1)}) custom-call(bf16[256,512]{1,0:T(8,128)(2,1)S(1)} %collective-permute-done.5.refs_5_.refs_0_, bf16[256,512]{1,0:T(8,128)(2,1)S(1)} %collective-permute-done.6.a.refs_1_, bf16[256,512]{1,0:T(8,128)(2,1)S(1)} %collective-permute-done.7.refs_2_, ...), custom_call_target="tpu_custom_call" | custom-call | flops 12079595 | bytes 47185 | tf_op jit(solution)/shard_map/pallas_call | solution.py:229
  38.2 1.3 %collective-permute-done.11.refs_0_ = bf16[256,512]{1,0:T(8,128)(2,1)S(1)} collective-permute-done((bf16[256,512]{1,0:T(8,128)(2,1)S(1)}, bf16[256,512]{1,0:T(8,128)(2,1)S(1)}, u32[]{:S(2)}, u32[]{:S(2)}) %collective-permute-start.11) | collective-permute-done | bytes 262176 | tf_op jit(solution)/shard_map/ppermute | solution.py:49
  39.5 0.7 %shard_map.73 = (bf16[1536,256]{1,0:T(8,128)(2,1)S(1)}, f32[6,256]{1,0:T(8,128)S(1)}, bf16[256,512]{1,0:T(8,128)(2,1)S(1)}) custom-call(bf16[256,512]{1,0:T(8,128)(2,1)S(1)} %collective-permute-done.11.refs_0_, bf16[6144,512]{1,0:T(8,128)(2,1)S(1)} %bitcast.3, f32[6,768]{1,0:T(8,128)S(1)} %get-tuple-element.23.refs_2_.refs_5_), custom_call_target="tpu_custom_call" | custom-call | flops 402653184 | bytes 2621440 | tf_op jit(solution)/shard_map/pallas_call | solution.py:229
  40.2 0.0 collective-permute-done.12.refs_1_
  40.2 0.0 collective-permute-done.13.refs_2_
  40.2 0.0 collective-permute-done.14.refs_3_
  40.2 2.1 %shard_map.76 = (bf16[768,512]{1,0:T(8,128)(2,1)S(1)}, f32[1,768]{1,0:T(1,128)S(1)}) custom-call(bf16[1536,1024]{1,0:T(8,128)(2,1)S(1)} %get-tuple-element.20.refs_0_, bf16[1536,768]{1,0:T(8,128)(2,1)S(1)} %get-tuple-element.22.refs_1_, bf16[1536,256]{1,0:T(8,128)(2,1)S(1)} %get-tuple-element.24.refs_2_, bf16[1024,512]{1,0:T(8,128)(2,1)S(1)} %get-tuple-element.25.refs_3_, ...), custom_call_target="tpu_custom_call" | custom-call | flops 2415919104 | bytes 9437184 | tf_op jit(solution)/shard_map/pallas_call | solution.py:278
  42.3 0.1 collective-permute-start.15
  42.4 0.5 %collective-permute-start.16 = (f32[1,768]{1,0:T(1,128)S(1)}, f32[1,768]{1,0:T(1,128)S(1)}, u32[]{:S(2)}, u32[]{:S(2)}) collective-permute-start(f32[1,768]{1,0:T(1,128)S(1)} %get-tuple-element.35), channel_id=1, source_target_pairs={{4,0},{0,4},{5,1},{1,5},{6,2},{2,6},{7,3},{3,7},{12,8},{8,12},{13,... | collective-permute-start | bytes 9224 | tf_op jit(solution)/shard_map/ppermute | solution.py:49
  42.9 1.8 %shard_map.75 = (f32[768,512]{1,0:T(8,128)S(1)}, f32[1,768]{1,0:T(1,128)S(1)}) custom-call(bf16[1536,1024]{1,0:T(8,128)(2,1)S(1)} %get-tuple-element.20.refs_0_, bf16[1536,768]{1,0:T(8,128)(2,1)S(1)} %get-tuple-element.22.refs_1_, bf16[1536,256]{1,0:T(8,128)(2,1)S(1)} %get-tuple-element.24.refs_2_, bf16[1024,512]{1,0:T(8,128)(2,1)S(1)} %get-tuple-element.25.refs_3_, ...), custom_call_target="tpu_custom_call" | custom-call | flops 2415919104 | bytes 9437184 | tf_op jit(solution)/shard_map/pallas_call | solution.py:278
  44.7 0.0 collective-permute-done.16.there_mass
  44.7 0.0 collective-permute-done.15.there
  44.7 1.8 %shard_map.77 = (f32[768,512]{1,0:T(8,128)}, f32[1,768]{1,0:T(1,128)}) custom-call(f32[768,512]{1,0:T(8,128)S(1)} %get-tuple-element.32.here, f32[1,768]{1,0:T(1,128)S(1)} %get-tuple-element.33.here_mass, bf16[768,512]{1,0:T(8,128)(2,1)S(1)} %collective-permute-done.15.there, f32[1,768]{1,0:T(1,128)S(1)} %collective-permute-done.16.there_mass), custom_call_target="tpu_custom_call" | custom-call | tf_op jit(solution)/shard_map/pallas_call | solution.py:308
  (11 shorter events, 0.2 us)
Async XLA Ops:
  1.7 8.1 %collective-permute-start = (bf16[128,512]{1,0:T(8,128)(2,1)S(1)}, bf16[128,512]{1,0:T(8,128)(2,1)S(1)}, u32[]{:S(2)}, u32[]{:S(2)}) collective-permute-start(bf16[128,512]{1,0:T(8,128)(2,1)S(1)} %multiply_convert_fusion.above), channel_id=1, source_target_pairs={{1,0},{0,1},{3,2},{2,3},{5,4},{4,5},{7,6},{6,7},{9,8},{8,9},{11,10... | collective-permute-start | bytes 393224 | tf_op jit(solution)/shard_map/ppermute | solution.py:49
  4.8 12.9 %collective-permute-start.3 = (bf16[128,512]{1,0:T(8,128)(2,1)S(1)}, bf16[128,512]{1,0:T(8,128)(2,1)S(1)}, u32[]{:S(2)}, u32[]{:S(2)}) collective-permute-start(bf16[128,512]{1,0:T(8,128)(2,1)S(1)} %multiply_convert_fusion.above), channel_id=1, source_target_pairs={{2,0},{3,1},{0,2},{1,3},{6,4},{7,5},{4,6},{5,7},{10,8},{11,9},{8,1... | collective-permute-start | bytes 393224 | tf_op jit(solution)/shard_map/ppermute | solution.py:49
  7.4 10.3 %collective-permute-start.4 = (bf16[128,512]{1,0:T(8,128)(2,1)S(1)}, bf16[128,512]{1,0:T(8,128)(2,1)S(1)}, u32[]{:S(2)}, u32[]{:S(2)}) collective-permute-start(bf16[128,512]{1,0:T(8,128)(2,1)S(1)} %multiply_convert_fusion.above), channel_id=1, source_target_pairs={{3,0},{2,1},{1,2},{0,3},{7,4},{6,5},{5,6},{4,7},{11,8},{10,9},{9,1... | collective-permute-start | bytes 393224 | tf_op jit(solution)/shard_map/ppermute | solution.py:49
  7.4 0.7 %copy-start = (s32[6144]{0:T(1024)S(1)}, s32[6144]{0:T(1024)}, u32[]{:S(2)}) copy-start(s32[6144]{0:T(1024)} %param.7) | copy-start | bytes 73732
  8.1 3.5 %slice-start = ((s8[6291456]{0:T(1024)(128)(4,1)}), s8[4194304]{0:T(1024)(128)(4,1)S(1)}, s32[]{:S(2)}) async-start(s8[6291456]{0:T(1024)(128)(4,1)} %bitcast.2), calls=%async_computation | async-start | bytes 8388608
  9.0 2.6 %slice-start.1 = ((s8[6291456]{0:T(1024)(128)(4,1)}), s8[2097152]{0:T(1024)(128)(4,1)S(1)}, s32[]{:S(2)}) async-start(s8[6291456]{0:T(1024)(128)(4,1)} %bitcast.2), calls=%async_computation.1 | async-start | bytes 4194304
  9.8 9.5 %collective-permute-start.1 = (bf16[256,512]{1,0:T(8,128)(2,1)S(1)}, bf16[256,512]{1,0:T(8,128)(2,1)S(1)}, u32[]{:S(2)}, u32[]{:S(2)}) collective-permute-start(bf16[256,512]{1,0:T(8,128)(2,1)S(1)} %shard_map.60.a.refs_0_), channel_id=1, source_target_pairs={{8,0},{20,4},{0,8},{28,12},{24,16},{4,20},{16,24},{12,28},{9,1},{2... | collective-permute-start | bytes 786440 | tf_op jit(solution)/shard_map/ppermute | solution.py:49
  14.4 12.8 %collective-permute-start.2 = (bf16[256,512]{1,0:T(8,128)(2,1)S(1)}, bf16[256,512]{1,0:T(8,128)(2,1)S(1)}, u32[]{:S(2)}, u32[]{:S(2)}) collective-permute-start(bf16[256,512]{1,0:T(8,128)(2,1)S(1)} %shard_map.63), channel_id=1, source_target_pairs={{16,0},{12,4},{24,8},{4,12},{0,16},{28,20},{8,24},{20,28},{17,1},{... | collective-permute-start | bytes 786440 | tf_op jit(solution)/shard_map/ppermute | solution.py:49
  17.7 12.4 %collective-permute-start.6 = (bf16[256,512]{1,0:T(8,128)(2,1)S(1)}, bf16[256,512]{1,0:T(8,128)(2,1)S(1)}, u32[]{:S(2)}, u32[]{:S(2)}) collective-permute-start(bf16[256,512]{1,0:T(8,128)(2,1)S(1)} %shard_map.64.refs_0_.refs_3_.a), channel_id=1, source_target_pairs={{8,0},{20,4},{0,8},{28,12},{24,16},{4,20},{16,24},{12,28},{9,1},{2... | collective-permute-start | bytes 786440 | tf_op jit(solution)/shard_map/ppermute | solution.py:49
  19.3 12.4 %collective-permute-start.5 = (bf16[256,512]{1,0:T(8,128)(2,1)S(1)}, bf16[256,512]{1,0:T(8,128)(2,1)S(1)}, u32[]{:S(2)}, u32[]{:S(2)}) collective-permute-start(bf16[256,512]{1,0:T(8,128)(2,1)S(1)} %shard_map.68), channel_id=1, source_target_pairs={{16,0},{12,4},{24,8},{4,12},{0,16},{28,20},{8,24},{20,28},{17,1},{... | collective-permute-start | bytes 786440 | tf_op jit(solution)/shard_map/ppermute | solution.py:49
  23.6 7.1 %collective-permute-start.10 = (f32[3,512]{1,0:T(4,128)S(1)}, f32[3,512]{1,0:T(4,128)S(1)}, u32[]{:S(2)}, u32[]{:S(2)}) collective-permute-start(f32[3,512]{1,0:T(4,128)S(1)} %shard_map.66.refs_5_.refs_0_), channel_id=1, source_target_pairs={{3,0},{2,1},{1,2},{0,3},{7,4},{6,5},{5,6},{4,7},{11,8},{10,9},{9,1... | collective-permute-start | bytes 18440 | tf_op jit(solution)/shard_map/ppermute | solution.py:49
  26.0 4.7 %collective-permute-start.8 = (f32[3,512]{1,0:T(4,128)S(1)}, f32[3,512]{1,0:T(4,128)S(1)}, u32[]{:S(2)}, u32[]{:S(2)}) collective-permute-start(f32[3,512]{1,0:T(4,128)S(1)} %shard_map.66.refs_5_.refs_0_), channel_id=1, source_target_pairs={{1,0},{0,1},{3,2},{2,3},{5,4},{4,5},{7,6},{6,7},{9,8},{8,9},{11,10... | collective-permute-start | bytes 18440 | tf_op jit(solution)/shard_map/ppermute | solution.py:49
  27.2 4.6 %collective-permute-start.9 = (f32[3,512]{1,0:T(4,128)S(1)}, f32[3,512]{1,0:T(4,128)S(1)}, u32[]{:S(2)}, u32[]{:S(2)}) collective-permute-start(f32[3,512]{1,0:T(4,128)S(1)} %shard_map.66.refs_5_.refs_0_), channel_id=1, source_target_pairs={{2,0},{3,1},{0,2},{1,3},{6,4},{7,5},{4,6},{5,7},{10,8},{11,9},{8,1... | collective-permute-start | bytes 18440 | tf_op jit(solution)/shard_map/ppermute | solution.py:49
  30.1 6.5 %collective-permute-start.7 = (bf16[256,512]{1,0:T(8,128)(2,1)S(1)}, bf16[256,512]{1,0:T(8,128)(2,1)S(1)}, u32[]{:S(2)}, u32[]{:S(2)}) collective-permute-start(bf16[256,512]{1,0:T(8,128)(2,1)S(1)} %shard_map.69), channel_id=1, source_target_pairs={{16,0},{12,4},{24,8},{4,12},{0,16},{28,20},{8,24},{20,28},{17,1},{... | collective-permute-start | bytes 786440 | tf_op jit(solution)/shard_map/ppermute | solution.py:49
  31.8 7.6 %collective-permute-start.11 = (bf16[256,512]{1,0:T(8,128)(2,1)S(1)}, bf16[256,512]{1,0:T(8,128)(2,1)S(1)}, u32[]{:S(2)}, u32[]{:S(2)}) collective-permute-start(bf16[256,512]{1,0:T(8,128)(2,1)S(1)} %shard_map.72), channel_id=1, source_target_pairs={{16,0},{12,4},{24,8},{4,12},{0,16},{28,20},{8,24},{20,28},{17,1},{... | collective-permute-start | bytes 786440 | tf_op jit(solution)/shard_map/ppermute | solution.py:49
  32.4 7.8 %collective-permute-start.12 = (f32[2,512]{1,0:T(2,128)S(1)}, f32[2,512]{1,0:T(2,128)S(1)}, u32[]{:S(2)}, u32[]{:S(2)}) collective-permute-start(f32[2,512]{1,0:T(2,128)S(1)} %shard_map.70.refs_4_.refs_0_), channel_id=1, source_target_pairs={{8,0},{20,4},{0,8},{28,12},{24,16},{4,20},{16,24},{12,28},{9,1},{2... | collective-permute-start | bytes 12296 | tf_op jit(solution)/shard_map/ppermute | solution.py:49
  32.9 7.2 %collective-permute-start.13 = (f32[2,512]{1,0:T(2,128)S(1)}, f32[2,512]{1,0:T(2,128)S(1)}, u32[]{:S(2)}, u32[]{:S(2)}) collective-permute-start(f32[2,512]{1,0:T(2,128)S(1)} %shard_map.70.refs_4_.refs_0_), channel_id=1, source_target_pairs={{16,0},{12,4},{24,8},{4,12},{0,16},{28,20},{8,24},{20,28},{17,1},{... | collective-permute-start | bytes 12296 | tf_op jit(solution)/shard_map/ppermute | solution.py:49
  34.5 5.7 %collective-permute-start.14 = (f32[2,512]{1,0:T(2,128)S(1)}, f32[2,512]{1,0:T(2,128)S(1)}, u32[]{:S(2)}, u32[]{:S(2)}) collective-permute-start(f32[2,512]{1,0:T(2,128)S(1)} %shard_map.70.refs_4_.refs_0_), channel_id=1, source_target_pairs={{24,0},{16,8},{8,16},{0,24},{25,1},{17,9},{9,17},{1,25},{26,2},{18... | collective-permute-start | bytes 12296 | tf_op jit(solution)/shard_map/ppermute | solution.py:49
  42.3 2.4 %collective-permute-start.15 = (bf16[768,512]{1,0:T(8,128)(2,1)S(1)}, bf16[768,512]{1,0:T(8,128)(2,1)S(1)}, u32[]{:S(2)}, u32[]{:S(2)}) collective-permute-start(bf16[768,512]{1,0:T(8,128)(2,1)S(1)} %get-tuple-element.34), channel_id=1, source_target_pairs={{4,0},{0,4},{5,1},{1,5},{6,2},{2,6},{7,3},{3,7},{12,8},{8,12},{13,... | collective-permute-start | bytes 2359304 | tf_op jit(solution)/shard_map/ppermute | solution.py:49
  42.4 2.3 %collective-permute-start.16 = (f32[1,768]{1,0:T(1,128)S(1)}, f32[1,768]{1,0:T(1,128)S(1)}, u32[]{:S(2)}, u32[]{:S(2)}) collective-permute-start(f32[1,768]{1,0:T(1,128)S(1)} %get-tuple-element.35), channel_id=1, source_target_pairs={{4,0},{0,4},{5,1},{1,5},{6,2},{2,6},{7,3},{3,7},{12,8},{8,12},{13,... | collective-permute-start | bytes 9224 | tf_op jit(solution)/shard_map/ppermute | solution.py:49

commit v23 on v21

--- a/solution.py
+++ b/solution.py
@@ -261,53 +261,69 @@
     return total, jnp.sum(weight.T, axis=0, keepdims=True)
 
 
-def sums_kernel(n, block, side, *refs):
-    expos, points, factors, (sums, mass) = refs[:n], refs[n : 2 * n], refs[2 * n : 3 * n], refs[3 * n :]
-    rows = sums.shape[0]
+def sums_kernel(n, side, *refs):
+    expos, points, factors, outs = refs[:n], refs[n : 2 * n], refs[2 * n : 3 * n], refs[3 * n :]
+    rows, width = expos[0].shape[0] // 2, points[0].shape[1]
     first = (lax.axis_index("lo") ^ side) * rows
-    for at in range(0, rows, block):
-        here = slice(at, at + block)
-        total, weight = weighed_sums(first + at, block, expos, points, factors)
-        sums[here, :] = total.astype(sums.dtype)
-        mass[:, here] = weight
-
-
-def sums_call(block, side, rows, dtype, expos, points, factors):
+    total, weight = weighed_sums(first, rows, expos, points, factors)
+    outs[0][:rows, :] = total.astype(outs[0].dtype)
+    if side:
+        high = weight.astype(jnp.bfloat16).astype(jnp.float32)
+        empty = jnp.zeros((1, -rows % width), jnp.float32)
+        lines = [
+            half[:, at : at + width]
+            for half in (jnp.concatenate([part, empty], axis=1) for part in (high, weight - high))
+            for at in range(0, half.shape[1], width)
+        ]
+        lines.append(jnp.zeros((16 - len(lines), width), jnp.float32))
+        outs[0][rows:, :] = jnp.concatenate(lines, axis=0).astype(jnp.bfloat16)
+    else:
+        outs[1][...] = weight
+
+
+def sums_call(side, rows, expos, points, factors):
     n = len(expos)
-    n_points, width = points[0].shape
-    return pl.pallas_call(
-        functools.partial(sums_kernel, n, block, side),
+    width = points[0].shape[1]
+    n_points = sum(chunk.shape[0] for chunk in points)
+    out_shape = [jax.ShapeDtypeStruct((rows + 16, width), jnp.bfloat16)]
+    if not side:
+        out_shape = [jax.ShapeDtypeStruct((rows, width), jnp.float32), jax.ShapeDtypeStruct((1, rows), jnp.float32)]
+    return pl.pallas_call(
+        functools.partial(sums_kernel, n, side),
         in_specs=in_vmem(3 * n),
-        out_specs=in_vmem(2),
-        out_shape=[jax.ShapeDtypeStruct((rows, width), dtype), jax.ShapeDtypeStruct((1, rows), jnp.float32)],
+        out_specs=in_vmem(len(out_shape)),
+        out_shape=out_shape,
         compiler_params=pltpu.CompilerParams(vmem_limit_bytes=VMEM_BYTES),
         cost_estimate=pl.CostEstimate(
-            flops=2 * rows * n * n_points * width,
-            bytes_accessed=2 * n * n_points * (rows + width) + 4 * rows * width,
+            flops=2 * rows * n_points * width,
+            bytes_accessed=2 * n_points * (rows + width) + 4 * rows * width,
             transcendentals=0,
         ),
     )(*expos, *points, *factors)
 
 
-def add_kernel(block, here, here_mass, there, there_mass, sums, mass, out, left):
+def add_kernel(block, here, here_mass, there, sums, mass, out, left):
     def copy(at):
         rows = pl.ds(at * block, block)
         return pltpu.make_async_copy(out.at[rows, :], sums.at[rows, :], left.at[at])
 
-    count = here.shape[0] // block
+    count, width = here.shape[0] // block, here.shape[1]
     for at in range(count):
         rows = slice(at * block, (at + 1) * block)
         out[rows, :] = here[rows, :] + there[rows, :].astype(jnp.float32)
         copy(at).start(priority=at % 2)
-    mass[...] = here_mass[...] + there_mass[...]
+    lines = there[here.shape[0] :, :].astype(jnp.float32)
+    n = -(-here.shape[0] // width)
+    parts = [jnp.concatenate([lines[at : at + 1, :] for at in range(i * n, i * n + n)], axis=1) for i in range(2)]
+    mass[...] = here_mass[...] + (parts[0] + parts[1])[:, : here.shape[0]]
     for at in range(count):
         copy(at).wait()
 
 
-def add_call(block, here, here_mass, there, there_mass):
+def add_call(block, here, here_mass, there):
     return pl.pallas_call(
         functools.partial(add_kernel, block),
-        in_specs=in_vmem(4),
+        in_specs=in_vmem(3),
         out_specs=[pl.BlockSpec(memory_space=pltpu.HBM)] + in_vmem(1),
         out_shape=[
             jax.ShapeDtypeStruct(here.shape, jnp.float32),
@@ -318,7 +334,7 @@
             pltpu.SemaphoreType.DMA((here.shape[0] // block,)),
         ],
         compiler_params=pltpu.CompilerParams(vmem_limit_bytes=VMEM_BYTES),
-    )(here, here_mass, there, there_mass)
+    )(here, here_mass, there)
 
 
 def split_cells(codes, exponents, centroids, counters):
@@ -357,10 +373,10 @@
     goals = [goal, turn(goal), turn_back(goal), around(goal, 3)]
     factors = factor_call(rate, goals, tops)
 
-    there = sums_call(per_device, 1, per_device, jnp.bfloat16, expos, points, factors)
-    there = [exchange(a, ("lo",), lambda at: at ^ 1) for a in there]
-    here = sums_call(per_device, 0, per_device, jnp.float32, expos, points, factors)
-    out, mass = add_call(block // 2, *here, *there)
+    (there,) = sums_call(1, per_device, expos, points, factors)
+    there = exchange(there, ("lo",), lambda at: at ^ 1)
+    here = sums_call(0, per_device, expos, points, factors)
+    out, mass = add_call(block // 2, *here, there)
     return (out[None], mass)
 
 

time: 46.2 us -> 46.5 us (level)
    ppermute x17 -> x16, waiting for transfers between devices: 4.47 us -> 4.53 us  [exchange(): return lax.ppermute(a, axes, [(partner(at), at) for at in range(count)])]
    ppermute x17 -> x16, starting transfers between devices: 22.3 us -> 22.3 us  [exchange(): return lax.ppermute(a, axes, [(partner(at), at) for at in range(count)])]
  transfers between devices with their start and end apart: 17 -> 16, of which waited for: 6 -> 5; matrix products, arithmetic and copies ran while one was open for 0% -> 0% of each run, Pallas kernels for 27% -> 28%
where the time goes in v23:
time: 46.5 us; the launch traced here: 46.3 us
  starting transfers between devices  22.3 us (48%)
  Pallas kernels  16.7 us (36%)
  waiting for transfers between devices  4.53 us (10%)
  other arithmetic  1.05 us (2%)
  between operations  0.99 us (2%)
  local copies, waits for them, and re-layouts  0.75 us (2%)
    ppermute x16, starting transfers between devices, exchange(): return lax.ppermute(a, axes, [(partner(at), at) for at in range(count)])  22.3 us
    pallas_call x2, Pallas kernels, totals_call(): pl.pallas_call(functools.partial(totals_kernel, rate, block, len(pieces))...  5.65 us
    ppermute x16, waiting for transfers between devices, exchange(): return lax.ppermute(a, axes, [(partner(at), at) for at in range(count)])  4.53 us
    pallas_call x3, Pallas kernels, expo_call(): pl.pallas_call(functools.partial(expo_kernel, rate, block, spots), in_spe...  4.31 us
    pallas_call x2, Pallas kernels, sums_call(): pl.pallas_call(functools.partial(sums_kernel, n, side), in_specs=in_vmem(...  3.88 us
    pallas_call x1, Pallas kernels, add_call(): pl.pallas_call(functools.partial(add_kernel, block), in_specs=in_vmem(3),...  1.78 us
    convert_element_type x1, other arithmetic, to_points(): return (scaled.astype(jnp.float32) * 2.0 ** (-16)).astype(jnp.bfloat16)  1.05 us
  transfers between devices with their start and end apart: 16, of which 5 were waited for; matrix products, arithmetic and copies ran while one was open for 0% of the time, Pallas kernels for 28%

profile of v23, /device:TPU:0, one launch (start us, length us, event | category | flops | bytes accessed | tf_op | source)
XLA Modules:
  0.0 46.3 jit_solution(8698698006111049947)
XLA Ops:
  0.6 1.1 %multiply_convert_fusion.above = bf16[128,512]{1,0:T(8,128)(2,1)S(1)} fusion(s32[128,512]{1,0:T(8,128)} %param.4, s32[128]{0:T(128)} %param.5), kind=kLoop, calls=%fused_computation | loop fusion | flops 327680 | bytes 393728 | tf_op jit(solution)/shard_map/convert_element_type | solution.py:17
  1.7 3.1 %collective-permute-start = (bf16[128,512]{1,0:T(8,128)(2,1)S(1)}, bf16[128,512]{1,0:T(8,128)(2,1)S(1)}, u32[]{:S(2)}, u32[]{:S(2)}) collective-permute-start(bf16[128,512]{1,0:T(8,128)(2,1)S(1)} %multiply_convert_fusion.above), channel_id=1, source_target_pairs={{1,0},{0,1},{3,2},{2,3},{5,4},{4,5},{7,6},{6,7},{9,8},{8,9},{11,10... | collective-permute-start | bytes 393224 | tf_op jit(solution)/shard_map/ppermute | solution.py:49
  4.8 2.6 %collective-permute-start.3 = (bf16[128,512]{1,0:T(8,128)(2,1)S(1)}, bf16[128,512]{1,0:T(8,128)(2,1)S(1)}, u32[]{:S(2)}, u32[]{:S(2)}) collective-permute-start(bf16[128,512]{1,0:T(8,128)(2,1)S(1)} %multiply_convert_fusion.above), channel_id=1, source_target_pairs={{2,0},{3,1},{0,2},{1,3},{6,4},{7,5},{4,6},{5,7},{10,8},{11,9},{8,1... | collective-permute-start | bytes 393224 | tf_op jit(solution)/shard_map/ppermute | solution.py:49
  7.4 0.0 collective-permute-start.4
  7.4 0.0 copy-start
  7.4 0.7 %copy-done = s32[6144]{0:T(1024)S(1)} copy-done((s32[6144]{0:T(1024)S(1)}, s32[6144]{0:T(1024)}, u32[]{:S(2)}) %copy-start) | copy-done | bytes 24600
  8.1 0.0 slice-start
  8.1 0.9 %shard_map.59.refs_0_.refs_2_ = f32[6144,128]{1,0:T(8,128)S(1)} custom-call(s32[48,128]{1,0:T(8,128)S(1)} %bitcast.4), custom_call_target="tpu_custom_call" | custom-call | flops 2000000000 | tf_op jit(solution)/shard_map/pallas_call | solution.py:114
  9.0 0.0 slice-start.1
  9.0 0.8 %collective-permute-done.below = bf16[128,512]{1,0:T(8,128)(2,1)S(1)} collective-permute-done((bf16[128,512]{1,0:T(8,128)(2,1)S(1)}, bf16[128,512]{1,0:T(8,128)(2,1)S(1)}, u32[]{:S(2)}, u32[]{:S(2)}) %collective-permute-start) | collective-permute-done | bytes 131104 | tf_op jit(solution)/shard_map/ppermute | solution.py:49
  9.8 1.8 %collective-permute-start.1 = (bf16[256,512]{1,0:T(8,128)(2,1)S(1)}, bf16[256,512]{1,0:T(8,128)(2,1)S(1)}, u32[]{:S(2)}, u32[]{:S(2)}) collective-permute-start(bf16[256,512]{1,0:T(8,128)(2,1)S(1)} %shard_map.60.a.refs_0_), channel_id=1, source_target_pairs={{8,0},{20,4},{0,8},{28,12},{24,16},{4,20},{16,24},{12,28},{9,1},{2... | collective-permute-start | bytes 786440 | tf_op jit(solution)/shard_map/ppermute | solution.py:49
  11.6 0.0 slice-done
  11.6 0.0 slice-done.1
  11.7 2.8 %shard_map.62.refs_0_.left = f32[3,256]{1,0:T(4,128)S(1)} custom-call(bf16[256,512]{1,0:T(8,128)(2,1)S(1)} %shard_map.61.refs_0_, bf16[6144,512]{1,0:T(8,128)(2,1)S(1)} %bitcast.3, f32[6144,128]{1,0:T(8,128)S(1)} %shard_map.59.refs_0_.refs_2_), custom_call_target="tpu_custom_call" | custom-call | flops 1610612736 | bytes 6291456 | tf_op jit(solution)/shard_map/pallas_call | solution.py:154
  14.5 1.6 %collective-permute-start.2 = (bf16[256,512]{1,0:T(8,128)(2,1)S(1)}, bf16[256,512]{1,0:T(8,128)(2,1)S(1)}, u32[]{:S(2)}, u32[]{:S(2)}) collective-permute-start(bf16[256,512]{1,0:T(8,128)(2,1)S(1)} %shard_map.63), channel_id=1, source_target_pairs={{16,0},{12,4},{24,8},{4,12},{0,16},{28,20},{8,24},{20,28},{17,1},{... | collective-permute-start | bytes 786440 | tf_op jit(solution)/shard_map/ppermute | solution.py:49
  16.1 0.4 collective-permute-done.1.refs_3_.refs_1_.a
  16.5 2.0 %collective-permute-start.5 = (bf16[256,512]{1,0:T(8,128)(2,1)S(1)}, bf16[256,512]{1,0:T(8,128)(2,1)S(1)}, u32[]{:S(2)}, u32[]{:S(2)}) collective-permute-start(bf16[256,512]{1,0:T(8,128)(2,1)S(1)} %shard_map.68), channel_id=1, source_target_pairs={{16,0},{12,4},{24,8},{4,12},{0,16},{28,20},{8,24},{20,28},{17,1},{... | collective-permute-start | bytes 786440 | tf_op jit(solution)/shard_map/ppermute | solution.py:49
  18.5 0.0 collective-permute-done.3.above
  18.5 0.0 collective-permute-done.4.below
  18.6 1.6 %collective-permute-start.6 = (bf16[256,512]{1,0:T(8,128)(2,1)S(1)}, bf16[256,512]{1,0:T(8,128)(2,1)S(1)}, u32[]{:S(2)}, u32[]{:S(2)}) collective-permute-start(bf16[256,512]{1,0:T(8,128)(2,1)S(1)} %shard_map.64.refs_0_.refs_3_.a), channel_id=1, source_target_pairs={{8,0},{20,4},{0,8},{28,12},{24,16},{4,20},{16,24},{12,28},{9,1},{2... | collective-permute-start | bytes 786440 | tf_op jit(solution)/shard_map/ppermute | solution.py:49
  20.1 2.8 %shard_map.65.right = f32[3,256]{1,0:T(4,128)S(1)} custom-call(bf16[256,512]{1,0:T(8,128)(2,1)S(1)} %shard_map.64.refs_0_.refs_3_.a, bf16[6144,512]{1,0:T(8,128)(2,1)S(1)} %bitcast.3, f32[6144,128]{1,0:T(8,128)S(1)} %shard_map.59.refs_0_.refs_2_, bf16[256,512]{1,0:T(8,128)(2,1)S(1)} %collective-permute-done.1.refs_3_.refs_1_.a), custom_call_target="tpu_custom_call" | custom-call | flops 1610612736 | bytes 6291456 | tf_op jit(solution)/shard_map/pallas_call | solution.py:154
  23.0 1.2 %collective-permute-start.8 = (f32[3,512]{1,0:T(4,128)S(1)}, f32[3,512]{1,0:T(4,128)S(1)}, u32[]{:S(2)}, u32[]{:S(2)}) collective-permute-start(f32[3,512]{1,0:T(4,128)S(1)} %shard_map.66.refs_5_.refs_0_), channel_id=1, source_target_pairs={{1,0},{0,1},{3,2},{2,3},{5,4},{4,5},{7,6},{6,7},{9,8},{8,9},{11,10... | collective-permute-start | bytes 18440 | tf_op jit(solution)/shard_map/ppermute | solution.py:49
  24.2 3.0 %collective-permute-start.9 = (f32[3,512]{1,0:T(4,128)S(1)}, f32[3,512]{1,0:T(4,128)S(1)}, u32[]{:S(2)}, u32[]{:S(2)}) collective-permute-start(f32[3,512]{1,0:T(4,128)S(1)} %shard_map.66.refs_5_.refs_0_), channel_id=1, source_target_pairs={{2,0},{3,1},{0,2},{1,3},{6,4},{7,5},{4,6},{5,7},{10,8},{11,9},{8,1... | collective-permute-start | bytes 18440 | tf_op jit(solution)/shard_map/ppermute | solution.py:49
  27.2 0.0 collective-permute-done.2.refs_2_
  27.2 0.2 collective-permute-start.10
  27.4 2.0 %shard_map.67 = (bf16[1536,1024]{1,0:T(8,128)(2,1)S(1)}, f32[6,1024]{1,0:T(8,128)S(1)}, bf16[1024,512]{1,0:T(8,128)(2,1)S(1)}) custom-call(bf16[256,512]{1,0:T(8,128)(2,1)S(1)} %shard_map.60.a.refs_0_, bf16[256,512]{1,0:T(8,128)(2,1)S(1)} %collective-permute-done.1.refs_3_.refs_1_.a, bf16[256,512]{1,0:T(8,128)(2,1)S(1)} %collective-permute-done.2.refs_2_, ...), custom_call_target="tpu_custom_call" | custom-call | flops 16106127 | bytes 57671 | tf_op jit(solution)/shard_map/pallas_call | solution.py:229
  29.5 0.0 collective-permute-done.8.refs_1_
  29.5 1.1 %collective-permute-start.7 = (bf16[256,512]{1,0:T(8,128)(2,1)S(1)}, bf16[256,512]{1,0:T(8,128)(2,1)S(1)}, u32[]{:S(2)}, u32[]{:S(2)}) collective-permute-start(bf16[256,512]{1,0:T(8,128)(2,1)S(1)} %shard_map.69), channel_id=1, source_target_pairs={{16,0},{12,4},{24,8},{4,12},{0,16},{28,20},{8,24},{20,28},{17,1},{... | collective-permute-start | bytes 786440 | tf_op jit(solution)/shard_map/ppermute | solution.py:49
  30.6 0.0 collective-permute-done.9.refs_2_
  30.6 2.1 %collective-permute-done.10.refs_3_ = f32[3,512]{1,0:T(4,128)S(1)} collective-permute-done((f32[3,512]{1,0:T(4,128)S(1)}, f32[3,512]{1,0:T(4,128)S(1)}, u32[]{:S(2)}, u32[]{:S(2)}) %collective-permute-start.10) | collective-permute-done | bytes 6176 | tf_op jit(solution)/shard_map/ppermute | solution.py:49
  32.7 0.0 collective-permute-done.5.refs_5_.refs_0_
  32.7 0.0 collective-permute-done.6.refs_1_.a
  32.7 0.6 %collective-permute-start.11 = (bf16[256,512]{1,0:T(8,128)(2,1)S(1)}, bf16[256,512]{1,0:T(8,128)(2,1)S(1)}, u32[]{:S(2)}, u32[]{:S(2)}) collective-permute-start(bf16[256,512]{1,0:T(8,128)(2,1)S(1)} %shard_map.72), channel_id=1, source_target_pairs={{16,0},{12,4},{24,8},{4,12},{0,16},{28,20},{8,24},{20,28},{17,1},{... | collective-permute-start | bytes 786440 | tf_op jit(solution)/shard_map/ppermute | solution.py:49
  33.3 0.5 %collective-permute-start.12 = (f32[2,512]{1,0:T(2,128)S(1)}, f32[2,512]{1,0:T(2,128)S(1)}, u32[]{:S(2)}, u32[]{:S(2)}) collective-permute-start(f32[2,512]{1,0:T(2,128)S(1)} %shard_map.70.refs_4_.refs_0_), channel_id=1, source_target_pairs={{8,0},{20,4},{0,8},{28,12},{24,16},{4,20},{16,24},{12,28},{9,1},{2... | collective-permute-start | bytes 12296 | tf_op jit(solution)/shard_map/ppermute | solution.py:49
  33.8 1.5 %collective-permute-start.13 = (f32[2,512]{1,0:T(2,128)S(1)}, f32[2,512]{1,0:T(2,128)S(1)}, u32[]{:S(2)}, u32[]{:S(2)}) collective-permute-start(f32[2,512]{1,0:T(2,128)S(1)} %shard_map.70.refs_4_.refs_0_), channel_id=1, source_target_pairs={{16,0},{12,4},{24,8},{4,12},{0,16},{28,20},{8,24},{20,28},{17,1},{... | collective-permute-start | bytes 12296 | tf_op jit(solution)/shard_map/ppermute | solution.py:49
  35.4 1.4 %collective-permute-start.14 = (f32[2,512]{1,0:T(2,128)S(1)}, f32[2,512]{1,0:T(2,128)S(1)}, u32[]{:S(2)}, u32[]{:S(2)}) collective-permute-start(f32[2,512]{1,0:T(2,128)S(1)} %shard_map.70.refs_4_.refs_0_), channel_id=1, source_target_pairs={{24,0},{16,8},{8,16},{0,24},{25,1},{17,9},{9,17},{1,25},{26,2},{18... | collective-permute-start | bytes 12296 | tf_op jit(solution)/shard_map/ppermute | solution.py:49
  36.8 0.0 collective-permute-done.7.refs_2_
  36.8 1.6 %shard_map.71 = (bf16[1536,768]{1,0:T(8,128)(2,1)S(1)}, f32[6,768]{1,0:T(8,128)S(1)}, bf16[768,512]{1,0:T(8,128)(2,1)S(1)}) custom-call(bf16[256,512]{1,0:T(8,128)(2,1)S(1)} %collective-permute-done.5.refs_5_.refs_0_, bf16[256,512]{1,0:T(8,128)(2,1)S(1)} %collective-permute-done.6.refs_1_.a, bf16[256,512]{1,0:T(8,128)(2,1)S(1)} %collective-permute-done.7.refs_2_, ...), custom_call_target="tpu_custom_call" | custom-call | flops 12079595 | bytes 47185 | tf_op jit(solution)/shard_map/pallas_call | solution.py:229
  38.4 0.8 %collective-permute-done.11.refs_0_ = bf16[256,512]{1,0:T(8,128)(2,1)S(1)} collective-permute-done((bf16[256,512]{1,0:T(8,128)(2,1)S(1)}, bf16[256,512]{1,0:T(8,128)(2,1)S(1)}, u32[]{:S(2)}, u32[]{:S(2)}) %collective-permute-start.11) | collective-permute-done | bytes 262176 | tf_op jit(solution)/shard_map/ppermute | solution.py:49
  39.2 0.7 %shard_map.73 = (bf16[1536,256]{1,0:T(8,128)(2,1)S(1)}, f32[6,256]{1,0:T(8,128)S(1)}, bf16[256,512]{1,0:T(8,128)(2,1)S(1)}) custom-call(bf16[256,512]{1,0:T(8,128)(2,1)S(1)} %collective-permute-done.11.refs_0_, bf16[6144,512]{1,0:T(8,128)(2,1)S(1)} %bitcast.3, f32[6,768]{1,0:T(8,128)S(1)} %get-tuple-element.21.refs_2_.refs_5_), custom_call_target="tpu_custom_call" | custom-call | flops 402653184 | bytes 2621440 | tf_op jit(solution)/shard_map/pallas_call | solution.py:229
  39.9 0.0 collective-permute-done.12.refs_1_
  39.9 0.0 collective-permute-done.13.refs_2_
  39.9 0.0 collective-permute-done.14.refs_3_
  40.0 2.0 %shard_map.76 = bf16[784,512]{1,0:T(8,128)(2,1)S(1)} custom-call(bf16[1536,1024]{1,0:T(8,128)(2,1)S(1)} %get-tuple-element.18.refs_0_, bf16[1536,768]{1,0:T(8,128)(2,1)S(1)} %get-tuple-element.20.refs_1_, bf16[1536,256]{1,0:T(8,128)(2,1)S(1)} %get-tuple-element.22.refs_2_, bf16[1024,512]{1,0:T(8,128)(2,1)S(1)} %get-tuple-element.23.refs_3_, ...), custom_call_target="tpu_custom_call" | custom-call | flops 1610612736 | bytes 6815744 | tf_op jit(solution)/shard_map/pallas_call | solution.py:291
  42.0 0.1 collective-permute-start.15
  42.1 1.8 %shard_map.75 = (f32[768,512]{1,0:T(8,128)S(1)}, f32[1,768]{1,0:T(1,128)S(1)}) custom-call(bf16[1536,1024]{1,0:T(8,128)(2,1)S(1)} %get-tuple-element.18.refs_0_, bf16[1536,768]{1,0:T(8,128)(2,1)S(1)} %get-tuple-element.20.refs_1_, bf16[1536,256]{1,0:T(8,128)(2,1)S(1)} %get-tuple-element.22.refs_2_, bf16[1024,512]{1,0:T(8,128)(2,1)S(1)} %get-tuple-element.23.refs_3_, ...), custom_call_target="tpu_custom_call" | custom-call | flops 1610612736 | bytes 6815744 | tf_op jit(solution)/shard_map/pallas_call | solution.py:291
  43.9 0.5 collective-permute-done.15.there
  44.4 1.8 %shard_map.77 = (f32[768,512]{1,0:T(8,128)}, f32[1,768]{1,0:T(1,128)}) custom-call(f32[768,512]{1,0:T(8,128)S(1)} %get-tuple-element.30.here, f32[1,768]{1,0:T(1,128)S(1)} %get-tuple-element.31.here_mass, bf16[784,512]{1,0:T(8,128)(2,1)S(1)} %collective-permute-done.15.there), custom_call_target="tpu_custom_call" | custom-call | tf_op jit(solution)/shard_map/pallas_call | solution.py:324
  (11 shorter events, 0.2 us)
Async XLA Ops:
  1.7 8.1 %collective-permute-start = (bf16[128,512]{1,0:T(8,128)(2,1)S(1)}, bf16[128,512]{1,0:T(8,128)(2,1)S(1)}, u32[]{:S(2)}, u32[]{:S(2)}) collective-permute-start(bf16[128,512]{1,0:T(8,128)(2,1)S(1)} %multiply_convert_fusion.above), channel_id=1, source_target_pairs={{1,0},{0,1},{3,2},{2,3},{5,4},{4,5},{7,6},{6,7},{9,8},{8,9},{11,10... | collective-permute-start | bytes 393224 | tf_op jit(solution)/shard_map/ppermute | solution.py:49
  4.8 13.8 %collective-permute-start.3 = (bf16[128,512]{1,0:T(8,128)(2,1)S(1)}, bf16[128,512]{1,0:T(8,128)(2,1)S(1)}, u32[]{:S(2)}, u32[]{:S(2)}) collective-permute-start(bf16[128,512]{1,0:T(8,128)(2,1)S(1)} %multiply_convert_fusion.above), channel_id=1, source_target_pairs={{2,0},{3,1},{0,2},{1,3},{6,4},{7,5},{4,6},{5,7},{10,8},{11,9},{8,1... | collective-permute-start | bytes 393224 | tf_op jit(solution)/shard_map/ppermute | solution.py:49
  7.4 11.2 %collective-permute-start.4 = (bf16[128,512]{1,0:T(8,128)(2,1)S(1)}, bf16[128,512]{1,0:T(8,128)(2,1)S(1)}, u32[]{:S(2)}, u32[]{:S(2)}) collective-permute-start(bf16[128,512]{1,0:T(8,128)(2,1)S(1)} %multiply_convert_fusion.above), channel_id=1, source_target_pairs={{3,0},{2,1},{1,2},{0,3},{7,4},{6,5},{5,6},{4,7},{11,8},{10,9},{9,1... | collective-permute-start | bytes 393224 | tf_op jit(solution)/shard_map/ppermute | solution.py:49
  7.4 0.7 %copy-start = (s32[6144]{0:T(1024)S(1)}, s32[6144]{0:T(1024)}, u32[]{:S(2)}) copy-start(s32[6144]{0:T(1024)} %param.7) | copy-start | bytes 73732
  8.1 3.5 %slice-start = ((s8[6291456]{0:T(1024)(128)(4,1)}), s8[4194304]{0:T(1024)(128)(4,1)S(1)}, s32[]{:S(2)}) async-start(s8[6291456]{0:T(1024)(128)(4,1)} %bitcast.2), calls=%async_computation | async-start | bytes 8388608
  9.0 2.6 %slice-start.1 = ((s8[6291456]{0:T(1024)(128)(4,1)}), s8[2097152]{0:T(1024)(128)(4,1)S(1)}, s32[]{:S(2)}) async-start(s8[6291456]{0:T(1024)(128)(4,1)} %bitcast.2), calls=%async_computation.1 | async-start | bytes 4194304
  9.8 6.7 %collective-permute-start.1 = (bf16[256,512]{1,0:T(8,128)(2,1)S(1)}, bf16[256,512]{1,0:T(8,128)(2,1)S(1)}, u32[]{:S(2)}, u32[]{:S(2)}) collective-permute-start(bf16[256,512]{1,0:T(8,128)(2,1)S(1)} %shard_map.60.a.refs_0_), channel_id=1, source_target_pairs={{8,0},{20,4},{0,8},{28,12},{24,16},{4,20},{16,24},{12,28},{9,1},{2... | collective-permute-start | bytes 786440 | tf_op jit(solution)/shard_map/ppermute | solution.py:49
  14.5 12.7 %collective-permute-start.2 = (bf16[256,512]{1,0:T(8,128)(2,1)S(1)}, bf16[256,512]{1,0:T(8,128)(2,1)S(1)}, u32[]{:S(2)}, u32[]{:S(2)}) collective-permute-start(bf16[256,512]{1,0:T(8,128)(2,1)S(1)} %shard_map.63), channel_id=1, source_target_pairs={{16,0},{12,4},{24,8},{4,12},{0,16},{28,20},{8,24},{20,28},{17,1},{... | collective-permute-start | bytes 786440 | tf_op jit(solution)/shard_map/ppermute | solution.py:49
  16.5 16.1 %collective-permute-start.5 = (bf16[256,512]{1,0:T(8,128)(2,1)S(1)}, bf16[256,512]{1,0:T(8,128)(2,1)S(1)}, u32[]{:S(2)}, u32[]{:S(2)}) collective-permute-start(bf16[256,512]{1,0:T(8,128)(2,1)S(1)} %shard_map.68), channel_id=1, source_target_pairs={{16,0},{12,4},{24,8},{4,12},{0,16},{28,20},{8,24},{20,28},{17,1},{... | collective-permute-start | bytes 786440 | tf_op jit(solution)/shard_map/ppermute | solution.py:49
  18.6 14.1 %collective-permute-start.6 = (bf16[256,512]{1,0:T(8,128)(2,1)S(1)}, bf16[256,512]{1,0:T(8,128)(2,1)S(1)}, u32[]{:S(2)}, u32[]{:S(2)}) collective-permute-start(bf16[256,512]{1,0:T(8,128)(2,1)S(1)} %shard_map.64.refs_0_.refs_3_.a), channel_id=1, source_target_pairs={{8,0},{20,4},{0,8},{28,12},{24,16},{4,20},{16,24},{12,28},{9,1},{2... | collective-permute-start | bytes 786440 | tf_op jit(solution)/shard_map/ppermute | solution.py:49
  23.0 6.5 %collective-permute-start.8 = (f32[3,512]{1,0:T(4,128)S(1)}, f32[3,512]{1,0:T(4,128)S(1)}, u32[]{:S(2)}, u32[]{:S(2)}) collective-permute-start(f32[3,512]{1,0:T(4,128)S(1)} %shard_map.66.refs_5_.refs_0_), channel_id=1, source_target_pairs={{1,0},{0,1},{3,2},{2,3},{5,4},{4,5},{7,6},{6,7},{9,8},{8,9},{11,10... | collective-permute-start | bytes 18440 | tf_op jit(solution)/shard_map/ppermute | solution.py:49
  24.2 6.4 %collective-permute-start.9 = (f32[3,512]{1,0:T(4,128)S(1)}, f32[3,512]{1,0:T(4,128)S(1)}, u32[]{:S(2)}, u32[]{:S(2)}) collective-permute-start(f32[3,512]{1,0:T(4,128)S(1)} %shard_map.66.refs_5_.refs_0_), channel_id=1, source_target_pairs={{2,0},{3,1},{0,2},{1,3},{6,4},{7,5},{4,6},{5,7},{10,8},{11,9},{8,1... | collective-permute-start | bytes 18440 | tf_op jit(solution)/shard_map/ppermute | solution.py:49
  27.2 5.4 %collective-permute-start.10 = (f32[3,512]{1,0:T(4,128)S(1)}, f32[3,512]{1,0:T(4,128)S(1)}, u32[]{:S(2)}, u32[]{:S(2)}) collective-permute-start(f32[3,512]{1,0:T(4,128)S(1)} %shard_map.66.refs_5_.refs_0_), channel_id=1, source_target_pairs={{3,0},{2,1},{1,2},{0,3},{7,4},{6,5},{5,6},{4,7},{11,8},{10,9},{9,1... | collective-permute-start | bytes 18440 | tf_op jit(solution)/shard_map/ppermute | solution.py:49
  29.5 7.3 %collective-permute-start.7 = (bf16[256,512]{1,0:T(8,128)(2,1)S(1)}, bf16[256,512]{1,0:T(8,128)(2,1)S(1)}, u32[]{:S(2)}, u32[]{:S(2)}) collective-permute-start(bf16[256,512]{1,0:T(8,128)(2,1)S(1)} %shard_map.69), channel_id=1, source_target_pairs={{16,0},{12,4},{24,8},{4,12},{0,16},{28,20},{8,24},{20,28},{17,1},{... | collective-permute-start | bytes 786440 | tf_op jit(solution)/shard_map/ppermute | solution.py:49
  32.7 6.4 %collective-permute-start.11 = (bf16[256,512]{1,0:T(8,128)(2,1)S(1)}, bf16[256,512]{1,0:T(8,128)(2,1)S(1)}, u32[]{:S(2)}, u32[]{:S(2)}) collective-permute-start(bf16[256,512]{1,0:T(8,128)(2,1)S(1)} %shard_map.72), channel_id=1, source_target_pairs={{16,0},{12,4},{24,8},{4,12},{0,16},{28,20},{8,24},{20,28},{17,1},{... | collective-permute-start | bytes 786440 | tf_op jit(solution)/shard_map/ppermute | solution.py:49
  33.3 6.6 %collective-permute-start.12 = (f32[2,512]{1,0:T(2,128)S(1)}, f32[2,512]{1,0:T(2,128)S(1)}, u32[]{:S(2)}, u32[]{:S(2)}) collective-permute-start(f32[2,512]{1,0:T(2,128)S(1)} %shard_map.70.refs_4_.refs_0_), channel_id=1, source_target_pairs={{8,0},{20,4},{0,8},{28,12},{24,16},{4,20},{16,24},{12,28},{9,1},{2... | collective-permute-start | bytes 12296 | tf_op jit(solution)/shard_map/ppermute | solution.py:49
  33.8 6.1 %collective-permute-start.13 = (f32[2,512]{1,0:T(2,128)S(1)}, f32[2,512]{1,0:T(2,128)S(1)}, u32[]{:S(2)}, u32[]{:S(2)}) collective-permute-start(f32[2,512]{1,0:T(2,128)S(1)} %shard_map.70.refs_4_.refs_0_), channel_id=1, source_target_pairs={{16,0},{12,4},{24,8},{4,12},{0,16},{28,20},{8,24},{20,28},{17,1},{... | collective-permute-start | bytes 12296 | tf_op jit(solution)/shard_map/ppermute | solution.py:49
  35.4 4.6 %collective-permute-start.14 = (f32[2,512]{1,0:T(2,128)S(1)}, f32[2,512]{1,0:T(2,128)S(1)}, u32[]{:S(2)}, u32[]{:S(2)}) collective-permute-start(f32[2,512]{1,0:T(2,128)S(1)} %shard_map.70.refs_4_.refs_0_), channel_id=1, source_target_pairs={{24,0},{16,8},{8,16},{0,24},{25,1},{17,9},{9,17},{1,25},{26,2},{18... | collective-permute-start | bytes 12296 | tf_op jit(solution)/shard_map/ppermute | solution.py:49
  42.0 2.4 %collective-permute-start.15 = (bf16[784,512]{1,0:T(8,128)(2,1)S(1)}, bf16[784,512]{1,0:T(8,128)(2,1)S(1)}, u32[]{:S(2)}, u32[]{:S(2)}) collective-permute-start(bf16[784,512]{1,0:T(8,128)(2,1)S(1)} %shard_map.76), channel_id=1, source_target_pairs={{4,0},{0,4},{5,1},{1,5},{6,2},{2,6},{7,3},{3,7},{12,8},{8,12},{13,... | collective-permute-start | bytes 2408456 | tf_op jit(solution)/shard_map/ppermute | solution.py:49

commit v24 on v20

--- a/solution.py
+++ b/solution.py
@@ -344,15 +344,12 @@
     near_23 = join(near_2, near_3, *stats)
     stats.append(totals_call(rate, block, (near_23,), centroids, inverse, after=(first_01,)))
     first_23 = turn(near_23)
-    rows = near_01.shape[0]
-    both = turn_back(join(first_01, near_23, stats[1]))
-    across_01, second_23 = (both, 0, rows), (both, rows, rows)
+    second_23 = turn_back(near_23)
     stat = beside(*stats)
     expand = functools.partial(expo_call, rate, block, 2 * per_device)
     bundles = [expand((near_01, first_01, second_01, near_23), centroids, stat, declared=0.01)]
     goal = goal_call(rate, stat, *(along_z(stat, by) for by in (1, 2, 3)), bundles[0][1])
-    across_23 = turn_back(hold(first_23, goal))
-
+    across_01, across_23 = turn(hold(second_01, bundles[0][1])), turn_back(hold(first_23, goal))
     bundles.append(expand((across_01, first_23, second_23), centroids, goal, declared=0.01))
     bundles.append(expand((across_23,), centroids, bundles[1][1]))
     expos, tops, points = zip(*bundles)

time: 46.6 us -> 46.5 us (level)
  starting transfers between devices: 21.2 us -> 21.8 us
  waiting for transfers between devices: 5.84 us -> 5.32 us
    ppermute x16 -> x17, starting transfers between devices: 21.2 us -> 21.8 us  [exchange(): return lax.ppermute(a, axes, [(partner(at), at) for at in range(count)])]
    ppermute x16 -> x17, waiting for transfers between devices: 5.84 us -> 5.32 us  [exchange(): return lax.ppermute(a, axes, [(partner(at), at) for at in range(count)])]
  transfers between devices with their start and end apart: 16 -> 17, of which waited for: 4 -> 6; matrix products, arithmetic and copies ran while one was open for 0% -> 0% of each run, Pallas kernels for 27% -> 27%
where the time goes in v24:
time: 46.5 us; the launch traced here: 46.3 us
  starting transfers between devices  21.8 us (47%)
  Pallas kernels  16.4 us (35%)
  waiting for transfers between devices  5.32 us (11%)
  other arithmetic  1.05 us (2%)
  between operations  0.99 us (2%)
  local copies, waits for them, and re-layouts  0.75 us (2%)
    ppermute x17, starting transfers between devices, exchange(): return lax.ppermute(a, axes, [(partner(at), at) for at in range(count)])  21.8 us
    pallas_call x2, Pallas kernels, totals_call(): pl.pallas_call(functools.partial(totals_kernel, rate, block, len(pieces))...  5.39 us
    ppermute x17, waiting for transfers between devices, exchange(): return lax.ppermute(a, axes, [(partner(at), at) for at in range(count)])  5.32 us
    pallas_call x3, Pallas kernels, expo_call(): pl.pallas_call(functools.partial(expo_kernel, rate, block, spots), in_spe...  4.28 us
    pallas_call x2, Pallas kernels, sums_call(): pl.pallas_call(functools.partial(sums_kernel, n, block, side), in_specs=i...  3.91 us
    pallas_call x1, Pallas kernels, add_call(): pl.pallas_call(functools.partial(add_kernel, block), in_specs=in_vmem(4),...  1.79 us
    convert_element_type x1, other arithmetic, to_points(): return (scaled.astype(jnp.float32) * 2.0 ** (-16)).astype(jnp.bfloat16)  1.05 us
  transfers between devices with their start and end apart: 17, of which 6 were waited for; matrix products, arithmetic and copies ran while one was open for 0% of the time, Pallas kernels for 27%

profile of v24, /device:TPU:0, one launch (start us, length us, event | category | flops | bytes accessed | tf_op | source)
XLA Modules:
  0.0 46.3 jit_solution(10756924225495373613)
XLA Ops:
  0.6 1.1 %multiply_convert_fusion.above = bf16[128,512]{1,0:T(8,128)(2,1)S(1)} fusion(s32[128,512]{1,0:T(8,128)} %param.4, s32[128]{0:T(128)} %param.5), kind=kLoop, calls=%fused_computation | loop fusion | flops 327680 | bytes 393728 | tf_op jit(solution)/shard_map/convert_element_type | solution.py:17
  1.7 3.1 %collective-permute-start = (bf16[128,512]{1,0:T(8,128)(2,1)S(1)}, bf16[128,512]{1,0:T(8,128)(2,1)S(1)}, u32[]{:S(2)}, u32[]{:S(2)}) collective-permute-start(bf16[128,512]{1,0:T(8,128)(2,1)S(1)} %multiply_convert_fusion.above), channel_id=1, source_target_pairs={{1,0},{0,1},{3,2},{2,3},{5,4},{4,5},{7,6},{6,7},{9,8},{8,9},{11,10... | collective-permute-start | bytes 393224 | tf_op jit(solution)/shard_map/ppermute | solution.py:49
  4.8 2.6 %collective-permute-start.3 = (bf16[128,512]{1,0:T(8,128)(2,1)S(1)}, bf16[128,512]{1,0:T(8,128)(2,1)S(1)}, u32[]{:S(2)}, u32[]{:S(2)}) collective-permute-start(bf16[128,512]{1,0:T(8,128)(2,1)S(1)} %multiply_convert_fusion.above), channel_id=1, source_target_pairs={{2,0},{3,1},{0,2},{1,3},{6,4},{7,5},{4,6},{5,7},{10,8},{11,9},{8,1... | collective-permute-start | bytes 393224 | tf_op jit(solution)/shard_map/ppermute | solution.py:49
  7.4 0.0 collective-permute-start.4
  7.4 0.0 copy-start
  7.4 0.7 %copy-done = s32[6144]{0:T(1024)S(1)} copy-done((s32[6144]{0:T(1024)S(1)}, s32[6144]{0:T(1024)}, u32[]{:S(2)}) %copy-start) | copy-done | bytes 24600
  8.1 0.0 slice-start
  8.1 0.9 %shard_map.59.refs_0_.refs_2_ = f32[6144,128]{1,0:T(8,128)S(1)} custom-call(s32[48,128]{1,0:T(8,128)S(1)} %bitcast.4), custom_call_target="tpu_custom_call" | custom-call | flops 2000000000 | tf_op jit(solution)/shard_map/pallas_call | solution.py:114
  9.0 0.0 slice-start.1
  9.0 0.8 %collective-permute-done.below = bf16[128,512]{1,0:T(8,128)(2,1)S(1)} collective-permute-done((bf16[128,512]{1,0:T(8,128)(2,1)S(1)}, bf16[128,512]{1,0:T(8,128)(2,1)S(1)}, u32[]{:S(2)}, u32[]{:S(2)}) %collective-permute-start) | collective-permute-done | bytes 131104 | tf_op jit(solution)/shard_map/ppermute | solution.py:49
  9.8 1.8 %collective-permute-start.1 = (bf16[256,512]{1,0:T(8,128)(2,1)S(1)}, bf16[256,512]{1,0:T(8,128)(2,1)S(1)}, u32[]{:S(2)}, u32[]{:S(2)}) collective-permute-start(bf16[256,512]{1,0:T(8,128)(2,1)S(1)} %shard_map.60.a.refs_0_), channel_id=1, source_target_pairs={{8,0},{20,4},{0,8},{28,12},{24,16},{4,20},{16,24},{12,28},{9,1},{2... | collective-permute-start | bytes 786440 | tf_op jit(solution)/shard_map/ppermute | solution.py:49
  11.6 0.0 slice-done
  11.6 0.0 slice-done.1
  11.7 2.7 %shard_map.62.refs_0_.left = f32[3,256]{1,0:T(4,128)S(1)} custom-call(bf16[256,512]{1,0:T(8,128)(2,1)S(1)} %shard_map.61.refs_0_, bf16[6144,512]{1,0:T(8,128)(2,1)S(1)} %bitcast.3, f32[6144,128]{1,0:T(8,128)S(1)} %shard_map.59.refs_0_.refs_2_), custom_call_target="tpu_custom_call" | custom-call | flops 1610612736 | bytes 6291456 | tf_op jit(solution)/shard_map/pallas_call | solution.py:154
  14.4 1.6 %collective-permute-start.2 = (bf16[256,512]{1,0:T(8,128)(2,1)S(1)}, bf16[256,512]{1,0:T(8,128)(2,1)S(1)}, u32[]{:S(2)}, u32[]{:S(2)}) collective-permute-start(bf16[256,512]{1,0:T(8,128)(2,1)S(1)} %shard_map.63), channel_id=1, source_target_pairs={{16,0},{12,4},{24,8},{4,12},{0,16},{28,20},{8,24},{20,28},{17,1},{... | collective-permute-start | bytes 786440 | tf_op jit(solution)/shard_map/ppermute | solution.py:49
  16.0 1.7 %collective-permute-done.3.above = bf16[128,512]{1,0:T(8,128)(2,1)S(1)} collective-permute-done((bf16[128,512]{1,0:T(8,128)(2,1)S(1)}, bf16[128,512]{1,0:T(8,128)(2,1)S(1)}, u32[]{:S(2)}, u32[]{:S(2)}) %collective-permute-start.3) | collective-permute-done | bytes 131104 | tf_op jit(solution)/shard_map/ppermute | solution.py:49
  17.7 0.0 collective-permute-done.4.below
  17.7 1.6 %collective-permute-start.6 = (bf16[256,512]{1,0:T(8,128)(2,1)S(1)}, bf16[256,512]{1,0:T(8,128)(2,1)S(1)}, u32[]{:S(2)}, u32[]{:S(2)}) collective-permute-start(bf16[256,512]{1,0:T(8,128)(2,1)S(1)} %shard_map.64.refs_0_.refs_3_), channel_id=1, source_target_pairs={{8,0},{20,4},{0,8},{28,12},{24,16},{4,20},{16,24},{12,28},{9,1},{2... | collective-permute-start | bytes 786440 | tf_op jit(solution)/shard_map/ppermute | solution.py:49
  19.3 0.0 collective-permute-done.1.refs_3_.refs_1_
  19.3 2.7 %shard_map.65.right = f32[3,256]{1,0:T(4,128)S(1)} custom-call(bf16[256,512]{1,0:T(8,128)(2,1)S(1)} %shard_map.64.refs_0_.refs_3_, bf16[6144,512]{1,0:T(8,128)(2,1)S(1)} %bitcast.3, f32[6144,128]{1,0:T(8,128)S(1)} %shard_map.59.refs_0_.refs_2_, bf16[256,512]{1,0:T(8,128)(2,1)S(1)} %collective-permute-done.1.refs_3_.refs_1_), custom_call_target="tpu_custom_call" | custom-call | flops 1610612736 | bytes 6291456 | tf_op jit(solution)/shard_map/pallas_call | solution.py:154
  22.0 2.4 %collective-permute-start.10 = (f32[3,512]{1,0:T(4,128)S(1)}, f32[3,512]{1,0:T(4,128)S(1)}, u32[]{:S(2)}, u32[]{:S(2)}) collective-permute-start(f32[3,512]{1,0:T(4,128)S(1)} %shard_map.66.refs_5_.refs_0_), channel_id=1, source_target_pairs={{3,0},{2,1},{1,2},{0,3},{7,4},{6,5},{5,6},{4,7},{11,8},{10,9},{9,1... | collective-permute-start | bytes 18440 | tf_op jit(solution)/shard_map/ppermute | solution.py:49
  24.4 1.3 %collective-permute-start.8 = (f32[3,512]{1,0:T(4,128)S(1)}, f32[3,512]{1,0:T(4,128)S(1)}, u32[]{:S(2)}, u32[]{:S(2)}) collective-permute-start(f32[3,512]{1,0:T(4,128)S(1)} %shard_map.66.refs_5_.refs_0_), channel_id=1, source_target_pairs={{1,0},{0,1},{3,2},{2,3},{5,4},{4,5},{7,6},{6,7},{9,8},{8,9},{11,10... | collective-permute-start | bytes 18440 | tf_op jit(solution)/shard_map/ppermute | solution.py:49
  25.6 0.8 %collective-permute-start.9 = (f32[3,512]{1,0:T(4,128)S(1)}, f32[3,512]{1,0:T(4,128)S(1)}, u32[]{:S(2)}, u32[]{:S(2)}) collective-permute-start(f32[3,512]{1,0:T(4,128)S(1)} %shard_map.66.refs_5_.refs_0_), channel_id=1, source_target_pairs={{2,0},{3,1},{0,2},{1,3},{6,4},{7,5},{4,6},{5,7},{10,8},{11,9},{8,1... | collective-permute-start | bytes 18440 | tf_op jit(solution)/shard_map/ppermute | solution.py:49
  26.4 0.0 collective-permute-done.2.refs_2_.a
  26.4 1.5 %collective-permute-start.7 = (bf16[256,512]{1,0:T(8,128)(2,1)S(1)}, bf16[256,512]{1,0:T(8,128)(2,1)S(1)}, u32[]{:S(2)}, u32[]{:S(2)}) collective-permute-start(bf16[256,512]{1,0:T(8,128)(2,1)S(1)} %shard_map.64.refs_0_.refs_3_), channel_id=1, source_target_pairs={{16,0},{12,4},{24,8},{4,12},{0,16},{28,20},{8,24},{20,28},{17,1},{... | collective-permute-start | bytes 786440 | tf_op jit(solution)/shard_map/ppermute | solution.py:49
  28.0 2.0 %shard_map.67 = (bf16[1536,1024]{1,0:T(8,128)(2,1)S(1)}, f32[6,1024]{1,0:T(8,128)S(1)}, bf16[1024,512]{1,0:T(8,128)(2,1)S(1)}) custom-call(bf16[256,512]{1,0:T(8,128)(2,1)S(1)} %shard_map.60.a.refs_0_, bf16[256,512]{1,0:T(8,128)(2,1)S(1)} %collective-permute-done.1.refs_3_.refs_1_, bf16[256,512]{1,0:T(8,128)(2,1)S(1)} %collective-permute-done.2.refs_2_.a, ...), custom_call_target="tpu_custom_call" | custom-call | flops 16106127 | bytes 57671 | tf_op jit(solution)/shard_map/pallas_call | solution.py:229
  30.0 0.0 collective-permute-done.10.refs_3_
  30.0 0.6 %collective-permute-start.5 = (bf16[256,512]{1,0:T(8,128)(2,1)S(1)}, bf16[256,512]{1,0:T(8,128)(2,1)S(1)}, u32[]{:S(2)}, u32[]{:S(2)}) collective-permute-start(bf16[256,512]{1,0:T(8,128)(2,1)S(1)} %shard_map.68), channel_id=1, source_target_pairs={{8,0},{20,4},{0,8},{28,12},{24,16},{4,20},{16,24},{12,28},{9,1},{2... | collective-permute-start | bytes 786440 | tf_op jit(solution)/shard_map/ppermute | solution.py:49
  30.6 0.0 collective-permute-done.8.refs_1_
  30.7 0.0 collective-permute-done.9.refs_2_
  30.7 0.0 collective-permute-done.6.refs_1_.a
  30.7 1.1 %collective-permute-start.11 = (bf16[256,512]{1,0:T(8,128)(2,1)S(1)}, bf16[256,512]{1,0:T(8,128)(2,1)S(1)}, u32[]{:S(2)}, u32[]{:S(2)}) collective-permute-start(bf16[256,512]{1,0:T(8,128)(2,1)S(1)} %shard_map.71), channel_id=1, source_target_pairs={{16,0},{12,4},{24,8},{4,12},{0,16},{28,20},{8,24},{20,28},{17,1},{... | collective-permute-start | bytes 786440 | tf_op jit(solution)/shard_map/ppermute | solution.py:49
  31.8 1.0 %collective-permute-start.12 = (f32[2,512]{1,0:T(2,128)S(1)}, f32[2,512]{1,0:T(2,128)S(1)}, u32[]{:S(2)}, u32[]{:S(2)}) collective-permute-start(f32[2,512]{1,0:T(2,128)S(1)} %shard_map.69.refs_4_.refs_0_), channel_id=1, source_target_pairs={{8,0},{20,4},{0,8},{28,12},{24,16},{4,20},{16,24},{12,28},{9,1},{2... | collective-permute-start | bytes 12296 | tf_op jit(solution)/shard_map/ppermute | solution.py:49
  32.8 1.5 %collective-permute-start.13 = (f32[2,512]{1,0:T(2,128)S(1)}, f32[2,512]{1,0:T(2,128)S(1)}, u32[]{:S(2)}, u32[]{:S(2)}) collective-permute-start(f32[2,512]{1,0:T(2,128)S(1)} %shard_map.69.refs_4_.refs_0_), channel_id=1, source_target_pairs={{16,0},{12,4},{24,8},{4,12},{0,16},{28,20},{8,24},{20,28},{17,1},{... | collective-permute-start | bytes 12296 | tf_op jit(solution)/shard_map/ppermute | solution.py:49
  34.3 1.0 %collective-permute-done.7.refs_2_ = bf16[256,512]{1,0:T(8,128)(2,1)S(1)} collective-permute-done((bf16[256,512]{1,0:T(8,128)(2,1)S(1)}, bf16[256,512]{1,0:T(8,128)(2,1)S(1)}, u32[]{:S(2)}, u32[]{:S(2)}) %collective-permute-start.7) | collective-permute-done | bytes 262176 | tf_op jit(solution)/shard_map/ppermute | solution.py:49
  35.3 0.5 %collective-permute-start.14 = (f32[2,512]{1,0:T(2,128)S(1)}, f32[2,512]{1,0:T(2,128)S(1)}, u32[]{:S(2)}, u32[]{:S(2)}) collective-permute-start(f32[2,512]{1,0:T(2,128)S(1)} %shard_map.69.refs_4_.refs_0_), channel_id=1, source_target_pairs={{24,0},{16,8},{8,16},{0,24},{25,1},{17,9},{9,17},{1,25},{26,2},{18... | collective-permute-start | bytes 12296 | tf_op jit(solution)/shard_map/ppermute | solution.py:49
  35.8 0.7 %collective-permute-done.5.refs_0_ = bf16[256,512]{1,0:T(8,128)(2,1)S(1)} collective-permute-done((bf16[256,512]{1,0:T(8,128)(2,1)S(1)}, bf16[256,512]{1,0:T(8,128)(2,1)S(1)}, u32[]{:S(2)}, u32[]{:S(2)}) %collective-permute-start.5) | collective-permute-done | bytes 262176 | tf_op jit(solution)/shard_map/ppermute | solution.py:49
  36.5 1.6 %shard_map.70 = (bf16[1536,768]{1,0:T(8,128)(2,1)S(1)}, f32[6,768]{1,0:T(8,128)S(1)}, bf16[768,512]{1,0:T(8,128)(2,1)S(1)}) custom-call(bf16[256,512]{1,0:T(8,128)(2,1)S(1)} %collective-permute-done.5.refs_0_, bf16[256,512]{1,0:T(8,128)(2,1)S(1)} %collective-permute-done.6.refs_1_.a, bf16[256,512]{1,0:T(8,128)(2,1)S(1)} %collective-permute-done.7.refs_2_, ...), custom_call_target="tpu_custom_call" | custom-call | flops 12079595 | bytes 47185 | tf_op jit(solution)/shard_map/pallas_call | solution.py:229
  38.0 0.1 collective-permute-done.11.refs_0_
  38.1 0.7 %shard_map.72 = (bf16[1536,256]{1,0:T(8,128)(2,1)S(1)}, f32[6,256]{1,0:T(8,128)S(1)}, bf16[256,512]{1,0:T(8,128)(2,1)S(1)}) custom-call(bf16[256,512]{1,0:T(8,128)(2,1)S(1)} %collective-permute-done.11.refs_0_, bf16[6144,512]{1,0:T(8,128)(2,1)S(1)} %bitcast.3, f32[6,768]{1,0:T(8,128)S(1)} %get-tuple-element.23.refs_2_.refs_5_), custom_call_target="tpu_custom_call" | custom-call | flops 402653184 | bytes 2621440 | tf_op jit(solution)/shard_map/pallas_call | solution.py:229
  38.8 0.0 collective-permute-done.12.refs_1_
  38.9 0.0 collective-permute-done.13.refs_2_
  38.9 1.0 %collective-permute-done.14.refs_3_ = f32[2,512]{1,0:T(2,128)S(1)} collective-permute-done((f32[2,512]{1,0:T(2,128)S(1)}, f32[2,512]{1,0:T(2,128)S(1)}, u32[]{:S(2)}, u32[]{:S(2)}) %collective-permute-start.14) | collective-permute-done | bytes 4128 | tf_op jit(solution)/shard_map/ppermute | solution.py:49
  39.9 2.1 %shard_map.75 = (bf16[768,512]{1,0:T(8,128)(2,1)S(1)}, f32[1,768]{1,0:T(1,128)S(1)}) custom-call(bf16[1536,1024]{1,0:T(8,128)(2,1)S(1)} %get-tuple-element.20.refs_0_, bf16[1536,768]{1,0:T(8,128)(2,1)S(1)} %get-tuple-element.22.refs_1_, bf16[1536,256]{1,0:T(8,128)(2,1)S(1)} %get-tuple-element.24.refs_2_, bf16[1024,512]{1,0:T(8,128)(2,1)S(1)} %get-tuple-element.25.refs_3_, ...), custom_call_target="tpu_custom_call" | custom-call | flops 2415919104 | bytes 9437184 | tf_op jit(solution)/shard_map/pallas_call | solution.py:278
  41.9 0.1 collective-permute-start.15
  42.0 0.5 %collective-permute-start.16 = (f32[1,768]{1,0:T(1,128)S(1)}, f32[1,768]{1,0:T(1,128)S(1)}, u32[]{:S(2)}, u32[]{:S(2)}) collective-permute-start(f32[1,768]{1,0:T(1,128)S(1)} %get-tuple-element.35), channel_id=1, source_target_pairs={{4,0},{0,4},{5,1},{1,5},{6,2},{2,6},{7,3},{3,7},{12,8},{8,12},{13,... | collective-permute-start | bytes 9224 | tf_op jit(solution)/shard_map/ppermute | solution.py:49
  42.5 1.9 %shard_map.74 = (f32[768,512]{1,0:T(8,128)S(1)}, f32[1,768]{1,0:T(1,128)S(1)}) custom-call(bf16[1536,1024]{1,0:T(8,128)(2,1)S(1)} %get-tuple-element.20.refs_0_, bf16[1536,768]{1,0:T(8,128)(2,1)S(1)} %get-tuple-element.22.refs_1_, bf16[1536,256]{1,0:T(8,128)(2,1)S(1)} %get-tuple-element.24.refs_2_, bf16[1024,512]{1,0:T(8,128)(2,1)S(1)} %get-tuple-element.25.refs_3_, ...), custom_call_target="tpu_custom_call" | custom-call | flops 2415919104 | bytes 9437184 | tf_op jit(solution)/shard_map/pallas_call | solution.py:278
  44.4 0.0 collective-permute-done.16.there_mass
  44.4 0.0 collective-permute-done.15.there
  44.4 1.8 %shard_map.76 = (f32[768,512]{1,0:T(8,128)}, f32[1,768]{1,0:T(1,128)}) custom-call(f32[768,512]{1,0:T(8,128)S(1)} %get-tuple-element.32.here, f32[1,768]{1,0:T(1,128)S(1)} %get-tuple-element.33.here_mass, bf16[768,512]{1,0:T(8,128)(2,1)S(1)} %collective-permute-done.15.there, f32[1,768]{1,0:T(1,128)S(1)} %collective-permute-done.16.there_mass), custom_call_target="tpu_custom_call" | custom-call | tf_op jit(solution)/shard_map/pallas_call | solution.py:308
  (10 shorter events, 0.2 us)
Async XLA Ops:
  1.7 8.1 %collective-permute-start = (bf16[128,512]{1,0:T(8,128)(2,1)S(1)}, bf16[128,512]{1,0:T(8,128)(2,1)S(1)}, u32[]{:S(2)}, u32[]{:S(2)}) collective-permute-start(bf16[128,512]{1,0:T(8,128)(2,1)S(1)} %multiply_convert_fusion.above), channel_id=1, source_target_pairs={{1,0},{0,1},{3,2},{2,3},{5,4},{4,5},{7,6},{6,7},{9,8},{8,9},{11,10... | collective-permute-start | bytes 393224 | tf_op jit(solution)/shard_map/ppermute | solution.py:49
  4.8 12.9 %collective-permute-start.3 = (bf16[128,512]{1,0:T(8,128)(2,1)S(1)}, bf16[128,512]{1,0:T(8,128)(2,1)S(1)}, u32[]{:S(2)}, u32[]{:S(2)}) collective-permute-start(bf16[128,512]{1,0:T(8,128)(2,1)S(1)} %multiply_convert_fusion.above), channel_id=1, source_target_pairs={{2,0},{3,1},{0,2},{1,3},{6,4},{7,5},{4,6},{5,7},{10,8},{11,9},{8,1... | collective-permute-start | bytes 393224 | tf_op jit(solution)/shard_map/ppermute | solution.py:49
  7.4 10.3 %collective-permute-start.4 = (bf16[128,512]{1,0:T(8,128)(2,1)S(1)}, bf16[128,512]{1,0:T(8,128)(2,1)S(1)}, u32[]{:S(2)}, u32[]{:S(2)}) collective-permute-start(bf16[128,512]{1,0:T(8,128)(2,1)S(1)} %multiply_convert_fusion.above), channel_id=1, source_target_pairs={{3,0},{2,1},{1,2},{0,3},{7,4},{6,5},{5,6},{4,7},{11,8},{10,9},{9,1... | collective-permute-start | bytes 393224 | tf_op jit(solution)/shard_map/ppermute | solution.py:49
  7.4 0.7 %copy-start = (s32[6144]{0:T(1024)S(1)}, s32[6144]{0:T(1024)}, u32[]{:S(2)}) copy-start(s32[6144]{0:T(1024)} %param.7) | copy-start | bytes 73732
  8.1 3.5 %slice-start = ((s8[6291456]{0:T(1024)(128)(4,1)}), s8[4194304]{0:T(1024)(128)(4,1)S(1)}, s32[]{:S(2)}) async-start(s8[6291456]{0:T(1024)(128)(4,1)} %bitcast.2), calls=%async_computation | async-start | bytes 8388608
  9.0 2.6 %slice-start.1 = ((s8[6291456]{0:T(1024)(128)(4,1)}), s8[2097152]{0:T(1024)(128)(4,1)S(1)}, s32[]{:S(2)}) async-start(s8[6291456]{0:T(1024)(128)(4,1)} %bitcast.2), calls=%async_computation.1 | async-start | bytes 4194304
  9.8 9.5 %collective-permute-start.1 = (bf16[256,512]{1,0:T(8,128)(2,1)S(1)}, bf16[256,512]{1,0:T(8,128)(2,1)S(1)}, u32[]{:S(2)}, u32[]{:S(2)}) collective-permute-start(bf16[256,512]{1,0:T(8,128)(2,1)S(1)} %shard_map.60.a.refs_0_), channel_id=1, source_target_pairs={{8,0},{20,4},{0,8},{28,12},{24,16},{4,20},{16,24},{12,28},{9,1},{2... | collective-permute-start | bytes 786440 | tf_op jit(solution)/shard_map/ppermute | solution.py:49
  14.4 12.1 %collective-permute-start.2 = (bf16[256,512]{1,0:T(8,128)(2,1)S(1)}, bf16[256,512]{1,0:T(8,128)(2,1)S(1)}, u32[]{:S(2)}, u32[]{:S(2)}) collective-permute-start(bf16[256,512]{1,0:T(8,128)(2,1)S(1)} %shard_map.63), channel_id=1, source_target_pairs={{16,0},{12,4},{24,8},{4,12},{0,16},{28,20},{8,24},{20,28},{17,1},{... | collective-permute-start | bytes 786440 | tf_op jit(solution)/shard_map/ppermute | solution.py:49
  17.7 13.0 %collective-permute-start.6 = (bf16[256,512]{1,0:T(8,128)(2,1)S(1)}, bf16[256,512]{1,0:T(8,128)(2,1)S(1)}, u32[]{:S(2)}, u32[]{:S(2)}) collective-permute-start(bf16[256,512]{1,0:T(8,128)(2,1)S(1)} %shard_map.64.refs_0_.refs_3_), channel_id=1, source_target_pairs={{8,0},{20,4},{0,8},{28,12},{24,16},{4,20},{16,24},{12,28},{9,1},{2... | collective-permute-start | bytes 786440 | tf_op jit(solution)/shard_map/ppermute | solution.py:49
  22.0 8.0 %collective-permute-start.10 = (f32[3,512]{1,0:T(4,128)S(1)}, f32[3,512]{1,0:T(4,128)S(1)}, u32[]{:S(2)}, u32[]{:S(2)}) collective-permute-start(f32[3,512]{1,0:T(4,128)S(1)} %shard_map.66.refs_5_.refs_0_), channel_id=1, source_target_pairs={{3,0},{2,1},{1,2},{0,3},{7,4},{6,5},{5,6},{4,7},{11,8},{10,9},{9,1... | collective-permute-start | bytes 18440 | tf_op jit(solution)/shard_map/ppermute | solution.py:49
  24.4 6.3 %collective-permute-start.8 = (f32[3,512]{1,0:T(4,128)S(1)}, f32[3,512]{1,0:T(4,128)S(1)}, u32[]{:S(2)}, u32[]{:S(2)}) collective-permute-start(f32[3,512]{1,0:T(4,128)S(1)} %shard_map.66.refs_5_.refs_0_), channel_id=1, source_target_pairs={{1,0},{0,1},{3,2},{2,3},{5,4},{4,5},{7,6},{6,7},{9,8},{8,9},{11,10... | collective-permute-start | bytes 18440 | tf_op jit(solution)/shard_map/ppermute | solution.py:49
  25.6 5.0 %collective-permute-start.9 = (f32[3,512]{1,0:T(4,128)S(1)}, f32[3,512]{1,0:T(4,128)S(1)}, u32[]{:S(2)}, u32[]{:S(2)}) collective-permute-start(f32[3,512]{1,0:T(4,128)S(1)} %shard_map.66.refs_5_.refs_0_), channel_id=1, source_target_pairs={{2,0},{3,1},{0,2},{1,3},{6,4},{7,5},{4,6},{5,7},{10,8},{11,9},{8,1... | collective-permute-start | bytes 18440 | tf_op jit(solution)/shard_map/ppermute | solution.py:49
  26.4 8.9 %collective-permute-start.7 = (bf16[256,512]{1,0:T(8,128)(2,1)S(1)}, bf16[256,512]{1,0:T(8,128)(2,1)S(1)}, u32[]{:S(2)}, u32[]{:S(2)}) collective-permute-start(bf16[256,512]{1,0:T(8,128)(2,1)S(1)} %shard_map.64.refs_0_.refs_3_), channel_id=1, source_target_pairs={{16,0},{12,4},{24,8},{4,12},{0,16},{28,20},{8,24},{20,28},{17,1},{... | collective-permute-start | bytes 786440 | tf_op jit(solution)/shard_map/ppermute | solution.py:49
  30.0 6.4 %collective-permute-start.5 = (bf16[256,512]{1,0:T(8,128)(2,1)S(1)}, bf16[256,512]{1,0:T(8,128)(2,1)S(1)}, u32[]{:S(2)}, u32[]{:S(2)}) collective-permute-start(bf16[256,512]{1,0:T(8,128)(2,1)S(1)} %shard_map.68), channel_id=1, source_target_pairs={{8,0},{20,4},{0,8},{28,12},{24,16},{4,20},{16,24},{12,28},{9,1},{2... | collective-permute-start | bytes 786440 | tf_op jit(solution)/shard_map/ppermute | solution.py:49
  30.7 7.4 %collective-permute-start.11 = (bf16[256,512]{1,0:T(8,128)(2,1)S(1)}, bf16[256,512]{1,0:T(8,128)(2,1)S(1)}, u32[]{:S(2)}, u32[]{:S(2)}) collective-permute-start(bf16[256,512]{1,0:T(8,128)(2,1)S(1)} %shard_map.71), channel_id=1, source_target_pairs={{16,0},{12,4},{24,8},{4,12},{0,16},{28,20},{8,24},{20,28},{17,1},{... | collective-permute-start | bytes 786440 | tf_op jit(solution)/shard_map/ppermute | solution.py:49
  31.8 7.0 %collective-permute-start.12 = (f32[2,512]{1,0:T(2,128)S(1)}, f32[2,512]{1,0:T(2,128)S(1)}, u32[]{:S(2)}, u32[]{:S(2)}) collective-permute-start(f32[2,512]{1,0:T(2,128)S(1)} %shard_map.69.refs_4_.refs_0_), channel_id=1, source_target_pairs={{8,0},{20,4},{0,8},{28,12},{24,16},{4,20},{16,24},{12,28},{9,1},{2... | collective-permute-start | bytes 12296 | tf_op jit(solution)/shard_map/ppermute | solution.py:49
  32.8 6.1 %collective-permute-start.13 = (f32[2,512]{1,0:T(2,128)S(1)}, f32[2,512]{1,0:T(2,128)S(1)}, u32[]{:S(2)}, u32[]{:S(2)}) collective-permute-start(f32[2,512]{1,0:T(2,128)S(1)} %shard_map.69.refs_4_.refs_0_), channel_id=1, source_target_pairs={{16,0},{12,4},{24,8},{4,12},{0,16},{28,20},{8,24},{20,28},{17,1},{... | collective-permute-start | bytes 12296 | tf_op jit(solution)/shard_map/ppermute | solution.py:49
  35.3 4.5 %collective-permute-start.14 = (f32[2,512]{1,0:T(2,128)S(1)}, f32[2,512]{1,0:T(2,128)S(1)}, u32[]{:S(2)}, u32[]{:S(2)}) collective-permute-start(f32[2,512]{1,0:T(2,128)S(1)} %shard_map.69.refs_4_.refs_0_), channel_id=1, source_target_pairs={{24,0},{16,8},{8,16},{0,24},{25,1},{17,9},{9,17},{1,25},{26,2},{18... | collective-permute-start | bytes 12296 | tf_op jit(solution)/shard_map/ppermute | solution.py:49
  41.9 2.4 %collective-permute-start.15 = (bf16[768,512]{1,0:T(8,128)(2,1)S(1)}, bf16[768,512]{1,0:T(8,128)(2,1)S(1)}, u32[]{:S(2)}, u32[]{:S(2)}) collective-permute-start(bf16[768,512]{1,0:T(8,128)(2,1)S(1)} %get-tuple-element.34), channel_id=1, source_target_pairs={{4,0},{0,4},{5,1},{1,5},{6,2},{2,6},{7,3},{3,7},{12,8},{8,12},{13,... | collective-permute-start | bytes 2359304 | tf_op jit(solution)/shard_map/ppermute | solution.py:49
  42.0 2.4 %collective-permute-start.16 = (f32[1,768]{1,0:T(1,128)S(1)}, f32[1,768]{1,0:T(1,128)S(1)}, u32[]{:S(2)}, u32[]{:S(2)}) collective-permute-start(f32[1,768]{1,0:T(1,128)S(1)} %get-tuple-element.35), channel_id=1, source_target_pairs={{4,0},{0,4},{5,1},{1,5},{6,2},{2,6},{7,3},{3,7},{12,8},{8,12},{13,... | collective-permute-start | bytes 9224 | tf_op jit(solution)/shard_map/ppermute | solution.py:49

commit v25 on v23

--- a/solution.py
+++ b/solution.py
@@ -249,8 +249,9 @@
     for expo, chunk, factor in zip(expos, points, factors):
         block = expo.shape[0] // factor.shape[0]
         shares, lanes = [], []
-        for at in range(0, count, block):
-            here = pl.ds(pl.multiple_of(start + at, block), block)
+        step = math.gcd(block, count)
+        for at in range(0, count, step):
+            here = pl.ds(pl.multiple_of(start + at, step), step)
             share = expo[here, :].astype(jnp.float32) * factor[pl.ds((start + at) // block, 1), :]
             shares.append(share.astype(jnp.bfloat16))
             lanes.append(sum(share[:, i : i + 128] for i in range(0, share.shape[1], 128)))
@@ -261,80 +262,104 @@
     return total, jnp.sum(weight.T, axis=0, keepdims=True)
 
 
-def sums_kernel(n, side, *refs):
+def sums_kernel(n, side, part, rows, *refs):
     expos, points, factors, outs = refs[:n], refs[n : 2 * n], refs[2 * n : 3 * n], refs[3 * n :]
-    rows, width = expos[0].shape[0] // 2, points[0].shape[1]
-    first = (lax.axis_index("lo") ^ side) * rows
+    width = points[0].shape[1]
+    first = (lax.axis_index("lo") ^ side) * (expos[0].shape[0] // 2) + part * rows
     total, weight = weighed_sums(first, rows, expos, points, factors)
     outs[0][:rows, :] = total.astype(outs[0].dtype)
     if side:
         high = weight.astype(jnp.bfloat16).astype(jnp.float32)
-        empty = jnp.zeros((1, -rows % width), jnp.float32)
-        lines = [
-            half[:, at : at + width]
-            for half in (jnp.concatenate([part, empty], axis=1) for part in (high, weight - high))
-            for at in range(0, half.shape[1], width)
-        ]
-        lines.append(jnp.zeros((16 - len(lines), width), jnp.float32))
+        empty = jnp.zeros((1, width - rows), jnp.float32)
+        lines = [jnp.concatenate([line, empty], axis=1) for line in (high, weight - high)]
+        lines.append(jnp.zeros((14, width), jnp.float32))
         outs[0][rows:, :] = jnp.concatenate(lines, axis=0).astype(jnp.bfloat16)
     else:
         outs[1][...] = weight
 
 
-def sums_call(side, rows, expos, points, factors):
+def sums_call(side, part, rows, expos, points, factors):
     n = len(expos)
     width = points[0].shape[1]
-    n_points = sum(chunk.shape[0] for chunk in points)
     out_shape = [jax.ShapeDtypeStruct((rows + 16, width), jnp.bfloat16)]
     if not side:
         out_shape = [jax.ShapeDtypeStruct((rows, width), jnp.float32), jax.ShapeDtypeStruct((1, rows), jnp.float32)]
     return pl.pallas_call(
-        functools.partial(sums_kernel, n, side),
+        functools.partial(sums_kernel, n, side, part, rows),
         in_specs=in_vmem(3 * n),
         out_specs=in_vmem(len(out_shape)),
         out_shape=out_shape,
         compiler_params=pltpu.CompilerParams(vmem_limit_bytes=VMEM_BYTES),
-        cost_estimate=pl.CostEstimate(
-            flops=2 * rows * n_points * width,
-            bytes_accessed=2 * n_points * (rows + width) + 4 * rows * width,
-            transcendentals=0,
-        ),
+        cost_estimate=pl.CostEstimate(flops=4 * 10**9, bytes_accessed=0, transcendentals=0),
     )(*expos, *points, *factors)
 
 
-def add_kernel(block, here, here_mass, there, sums, mass, out, left):
-    def copy(at):
-        rows = pl.ds(at * block, block)
-        return pltpu.make_async_copy(out.at[rows, :], sums.at[rows, :], left.at[at])
-
-    count, width = here.shape[0] // block, here.shape[1]
-    for at in range(count):
-        rows = slice(at * block, (at + 1) * block)
-        out[rows, :] = here[rows, :] + there[rows, :].astype(jnp.float32)
-        copy(at).start(priority=at % 2)
-    lines = there[here.shape[0] :, :].astype(jnp.float32)
-    n = -(-here.shape[0] // width)
-    parts = [jnp.concatenate([lines[at : at + 1, :] for at in range(i * n, i * n + n)], axis=1) for i in range(2)]
-    mass[...] = here_mass[...] + (parts[0] + parts[1])[:, : here.shape[0]]
-    for at in range(count):
-        copy(at).wait()
-
-
-def add_call(block, here, here_mass, there):
-    return pl.pallas_call(
-        functools.partial(add_kernel, block),
-        in_specs=in_vmem(3),
-        out_specs=[pl.BlockSpec(memory_space=pltpu.HBM)] + in_vmem(1),
+def masses(here_mass, there):
+    rows = here_mass.shape[1]
+    lines = there[rows:, :].astype(jnp.float32)
+    return here_mass[...] + (lines[:1, :rows] + lines[1:2, :rows])
+
+
+def half_kernel(n, *refs):
+    expos, points, factors = refs[:n], refs[n : 2 * n], refs[2 * n : 3 * n]
+    here, here_mass, there, sums, mass, later, later_mass, out, left = refs[3 * n :]
+    rows = here.shape[0]
+    out[...] = here[...] + there[:rows, :].astype(jnp.float32)
+    copy = pltpu.make_async_copy(out, sums.at[pl.ds(0, rows), :], left)
+    copy.start()
+    mass[...] = masses(here_mass, there)
+    first = lax.axis_index("lo") * (2 * rows) + rows
+    total, weight = weighed_sums(first, rows, expos, points, factors)
+    later[...] = total
+    later_mass[...] = weight
+    copy.wait()
+
+
+def half_call(expos, points, factors, here, here_mass, there):
+    n, (rows, width) = len(expos), here.shape
+    part = [jax.ShapeDtypeStruct((1, rows), jnp.float32), jax.ShapeDtypeStruct((rows, width), jnp.float32)]
+    return pl.pallas_call(
+        functools.partial(half_kernel, n),
+        in_specs=in_vmem(3 * n + 3),
+        out_specs=[pl.BlockSpec(memory_space=pltpu.HBM)] + in_vmem(3),
+        out_shape=[jax.ShapeDtypeStruct((2 * rows, width), jnp.float32), *part, part[0]],
+        scratch_shapes=[pltpu.VMEM((rows, width), jnp.float32), pltpu.SemaphoreType.DMA],
+        compiler_params=pltpu.CompilerParams(vmem_limit_bytes=VMEM_BYTES),
+    )(*expos, *points, *factors, here, here_mass, there)
+
+
+def end_kernel(so_far, mass_so_far, here, here_mass, there, sums, mass, out, left):
+    rows = here.shape[0]
+    half = rows // 2
+    copies = []
+    for at in (0, half):
+        here_rows = slice(at, at + half)
+        out[here_rows, :] = here[here_rows, :] + there[here_rows, :].astype(jnp.float32)
+        copies.append(
+            pltpu.make_async_copy(out.at[pl.ds(at, half), :], sums.at[pl.ds(rows + at, half), :], left.at[len(copies)])
+        )
+        copies[-1].start()
+    mass[:, :rows] = mass_so_far[...]
+    mass[:, rows:] = masses(here_mass, there)
+    for copy in copies:
+        copy.wait()
+
+
+def end_call(so_far, mass_so_far, here, here_mass, there):
+    rows, width = here.shape
+    hbm = [pl.BlockSpec(memory_space=pltpu.HBM)]
+    return pl.pallas_call(
+        end_kernel,
+        in_specs=hbm + in_vmem(4),
+        out_specs=hbm + in_vmem(1),
         out_shape=[
-            jax.ShapeDtypeStruct(here.shape, jnp.float32),
-            jax.ShapeDtypeStruct(here_mass.shape, jnp.float32),
+            jax.ShapeDtypeStruct(so_far.shape, jnp.float32),
+            jax.ShapeDtypeStruct((1, 2 * rows), jnp.float32),
         ],
-        scratch_shapes=[
-            pltpu.VMEM(here.shape, jnp.float32),
-            pltpu.SemaphoreType.DMA((here.shape[0] // block,)),
-        ],
-        compiler_params=pltpu.CompilerParams(vmem_limit_bytes=VMEM_BYTES),
-    )(here, here_mass, there)
+        input_output_aliases={0: 0},
+        scratch_shapes=[pltpu.VMEM((rows, width), jnp.float32), pltpu.SemaphoreType.DMA((2,))],
+        compiler_params=pltpu.CompilerParams(vmem_limit_bytes=VMEM_BYTES),
+    )(so_far, mass_so_far, here, here_mass, there)
 
 
 def split_cells(codes, exponents, centroids, counters):
@@ -373,10 +398,11 @@
     goals = [goal, turn(goal), turn_back(goal), around(goal, 3)]
     factors = factor_call(rate, goals, tops)
 
-    (there,) = sums_call(1, per_device, expos, points, factors)
-    there = exchange(there, ("lo",), lambda at: at ^ 1)
-    here = sums_call(0, per_device, expos, points, factors)
-    out, mass = add_call(block // 2, *here, there)
+    parts, rows = (expos, points, factors), per_device // 2
+    there = [exchange(*sums_call(1, part, rows, *parts), ("lo",), lambda at: at ^ 1) for part in range(2)]
+    here = sums_call(0, 0, rows, *parts)
+    so_far, mass_so_far, later, later_mass = half_call(*parts, *here, there[0])
+    out, mass = end_call(so_far, mass_so_far, later, later_mass, there[1])
     return (out[None], mass)
 
 

time: 46.5 us -> 47.5 us (1.022)
  Pallas kernels: 16.7 us -> 17.5 us
  starting transfers between devices: 22.3 us -> 23 us
  waiting for transfers between devices: 4.53 us -> 3.96 us
    pallas_call x3 -> x5, Pallas kernels: 5.66 us -> 6.65 us  [the longest x3 3.18 us: sums_call(): pl.pallas_call(functools.partial(sums_kernel, n, side, part, rows), in_sp...]
    ppermute x16 -> x17, starting transfers between devices: 22.3 us -> 23 us  [exchange(): return lax.ppermute(a, axes, [(partner(at), at) for at in range(count)])]
    ppermute x16 -> x17, waiting for transfers between devices: 4.53 us -> 3.96 us  [exchange(): return lax.ppermute(a, axes, [(partner(at), at) for at in range(count)])]
  transfers between devices with their start and end apart: 16 -> 17, of which waited for: 5 -> 4; matrix products, arithmetic and copies ran while one was open for 0% -> 0% of each run, Pallas kernels for 28% -> 32%
where the time goes in v25:
time: 47.5 us; the launch traced here: 47.3 us
  starting transfers between devices  23 us (48%)
  Pallas kernels  17.5 us (37%)
  waiting for transfers between devices  3.96 us (8%)
  other arithmetic  1.05 us (2%)
  between operations  1.02 us (2%)
  local copies, waits for them, and re-layouts  0.75 us (2%)
    ppermute x17, starting transfers between devices, exchange(): return lax.ppermute(a, axes, [(partner(at), at) for at in range(count)])  23 us
    pallas_call x2, Pallas kernels, totals_call(): pl.pallas_call(functools.partial(totals_kernel, rate, block, len(pieces))...  5.51 us
    pallas_call x3, Pallas kernels, expo_call(): pl.pallas_call(functools.partial(expo_kernel, rate, block, spots), in_spe...  4.28 us
    ppermute x17, waiting for transfers between devices, exchange(): return lax.ppermute(a, axes, [(partner(at), at) for at in range(count)])  3.96 us
    pallas_call x3, Pallas kernels, sums_call(): pl.pallas_call(functools.partial(sums_kernel, n, side, part, rows), in_sp...  3.18 us
    pallas_call x1, Pallas kernels, half_call(): pl.pallas_call(functools.partial(half_kernel, n), in_specs=in_vmem(3 * n...  1.94 us
    pallas_call x1, Pallas kernels, end_call(): pl.pallas_call(end_kernel, in_specs=hbm + in_vmem(4), out_specs=hbm + in_...  1.53 us
    convert_element_type x1, other arithmetic, to_points(): return (scaled.astype(jnp.float32) * 2.0 ** (-16)).astype(jnp.bfloat16)  1.05 us
  transfers between devices with their start and end apart: 17, of which 4 were waited for; matrix products, arithmetic and copies ran while one was open for 0% of the time, Pallas kernels for 32%

profile of v25, /device:TPU:0, one launch (start us, length us, event | category | flops | bytes accessed | tf_op | source)
XLA Modules:
  0.0 47.3 jit_solution(2778215879692000854)
XLA Ops:
  0.6 1.1 %multiply_convert_fusion.above = bf16[128,512]{1,0:T(8,128)(2,1)S(1)} fusion(s32[128,512]{1,0:T(8,128)} %param.4, s32[128]{0:T(128)} %param.5), kind=kLoop, calls=%fused_computation | loop fusion | flops 327680 | bytes 393728 | tf_op jit(solution)/shard_map/convert_element_type | solution.py:17
  1.7 3.1 %collective-permute-start = (bf16[128,512]{1,0:T(8,128)(2,1)S(1)}, bf16[128,512]{1,0:T(8,128)(2,1)S(1)}, u32[]{:S(2)}, u32[]{:S(2)}) collective-permute-start(bf16[128,512]{1,0:T(8,128)(2,1)S(1)} %multiply_convert_fusion.above), channel_id=1, source_target_pairs={{1,0},{0,1},{3,2},{2,3},{5,4},{4,5},{7,6},{6,7},{9,8},{8,9},{11,10... | collective-permute-start | bytes 393224 | tf_op jit(solution)/shard_map/ppermute | solution.py:49
  4.8 2.6 %collective-permute-start.3 = (bf16[128,512]{1,0:T(8,128)(2,1)S(1)}, bf16[128,512]{1,0:T(8,128)(2,1)S(1)}, u32[]{:S(2)}, u32[]{:S(2)}) collective-permute-start(bf16[128,512]{1,0:T(8,128)(2,1)S(1)} %multiply_convert_fusion.above), channel_id=1, source_target_pairs={{2,0},{3,1},{0,2},{1,3},{6,4},{7,5},{4,6},{5,7},{10,8},{11,9},{8,1... | collective-permute-start | bytes 393224 | tf_op jit(solution)/shard_map/ppermute | solution.py:49
  7.4 0.0 collective-permute-start.4
  7.4 0.0 copy-start
  7.4 0.7 %copy-done = s32[6144]{0:T(1024)S(1)} copy-done((s32[6144]{0:T(1024)S(1)}, s32[6144]{0:T(1024)}, u32[]{:S(2)}) %copy-start) | copy-done | bytes 24600
  8.1 0.0 slice-start
  8.1 0.9 %shard_map.59.refs_0_.refs_2_ = f32[6144,128]{1,0:T(8,128)S(1)} custom-call(s32[48,128]{1,0:T(8,128)S(1)} %bitcast.4), custom_call_target="tpu_custom_call" | custom-call | flops 2000000000 | tf_op jit(solution)/shard_map/pallas_call | solution.py:114
  9.0 0.0 slice-start.1
  9.0 0.8 %collective-permute-done.below = bf16[128,512]{1,0:T(8,128)(2,1)S(1)} collective-permute-done((bf16[128,512]{1,0:T(8,128)(2,1)S(1)}, bf16[128,512]{1,0:T(8,128)(2,1)S(1)}, u32[]{:S(2)}, u32[]{:S(2)}) %collective-permute-start) | collective-permute-done | bytes 131104 | tf_op jit(solution)/shard_map/ppermute | solution.py:49
  9.8 1.8 %collective-permute-start.1 = (bf16[256,512]{1,0:T(8,128)(2,1)S(1)}, bf16[256,512]{1,0:T(8,128)(2,1)S(1)}, u32[]{:S(2)}, u32[]{:S(2)}) collective-permute-start(bf16[256,512]{1,0:T(8,128)(2,1)S(1)} %shard_map.60.a.refs_0_), channel_id=1, source_target_pairs={{8,0},{20,4},{0,8},{28,12},{24,16},{4,20},{16,24},{12,28},{9,1},{2... | collective-permute-start | bytes 786440 | tf_op jit(solution)/shard_map/ppermute | solution.py:49
  11.6 0.0 slice-done
  11.6 0.0 slice-done.1
  11.7 2.8 %shard_map.62.refs_0_.left = f32[3,256]{1,0:T(4,128)S(1)} custom-call(bf16[256,512]{1,0:T(8,128)(2,1)S(1)} %shard_map.61.refs_0_, bf16[6144,512]{1,0:T(8,128)(2,1)S(1)} %bitcast.3, f32[6144,128]{1,0:T(8,128)S(1)} %shard_map.59.refs_0_.refs_2_), custom_call_target="tpu_custom_call" | custom-call | flops 1610612736 | bytes 6291456 | tf_op jit(solution)/shard_map/pallas_call | solution.py:154
  14.5 1.6 %collective-permute-start.2 = (bf16[256,512]{1,0:T(8,128)(2,1)S(1)}, bf16[256,512]{1,0:T(8,128)(2,1)S(1)}, u32[]{:S(2)}, u32[]{:S(2)}) collective-permute-start(bf16[256,512]{1,0:T(8,128)(2,1)S(1)} %shard_map.63), channel_id=1, source_target_pairs={{16,0},{12,4},{24,8},{4,12},{0,16},{28,20},{8,24},{20,28},{17,1},{... | collective-permute-start | bytes 786440 | tf_op jit(solution)/shard_map/ppermute | solution.py:49
  16.1 0.4 collective-permute-done.1.refs_3_.refs_1_.a
  16.5 2.0 %collective-permute-start.5 = (bf16[256,512]{1,0:T(8,128)(2,1)S(1)}, bf16[256,512]{1,0:T(8,128)(2,1)S(1)}, u32[]{:S(2)}, u32[]{:S(2)}) collective-permute-start(bf16[256,512]{1,0:T(8,128)(2,1)S(1)} %shard_map.68), channel_id=1, source_target_pairs={{16,0},{12,4},{24,8},{4,12},{0,16},{28,20},{8,24},{20,28},{17,1},{... | collective-permute-start | bytes 786440 | tf_op jit(solution)/shard_map/ppermute | solution.py:49
  18.5 0.0 collective-permute-done.3.above
  18.5 0.0 collective-permute-done.4.below
  18.6 1.6 %collective-permute-start.6 = (bf16[256,512]{1,0:T(8,128)(2,1)S(1)}, bf16[256,512]{1,0:T(8,128)(2,1)S(1)}, u32[]{:S(2)}, u32[]{:S(2)}) collective-permute-start(bf16[256,512]{1,0:T(8,128)(2,1)S(1)} %shard_map.64.refs_0_.refs_3_.a), channel_id=1, source_target_pairs={{8,0},{20,4},{0,8},{28,12},{24,16},{4,20},{16,24},{12,28},{9,1},{2... | collective-permute-start | bytes 786440 | tf_op jit(solution)/shard_map/ppermute | solution.py:49
  20.1 2.7 %shard_map.65.right = f32[3,256]{1,0:T(4,128)S(1)} custom-call(bf16[256,512]{1,0:T(8,128)(2,1)S(1)} %shard_map.64.refs_0_.refs_3_.a, bf16[6144,512]{1,0:T(8,128)(2,1)S(1)} %bitcast.3, f32[6144,128]{1,0:T(8,128)S(1)} %shard_map.59.refs_0_.refs_2_, bf16[256,512]{1,0:T(8,128)(2,1)S(1)} %collective-permute-done.1.refs_3_.refs_1_.a), custom_call_target="tpu_custom_call" | custom-call | flops 1610612736 | bytes 6291456 | tf_op jit(solution)/shard_map/pallas_call | solution.py:154
  22.8 1.2 %collective-permute-start.8 = (f32[3,512]{1,0:T(4,128)S(1)}, f32[3,512]{1,0:T(4,128)S(1)}, u32[]{:S(2)}, u32[]{:S(2)}) collective-permute-start(f32[3,512]{1,0:T(4,128)S(1)} %shard_map.66.refs_5_.refs_0_), channel_id=1, source_target_pairs={{1,0},{0,1},{3,2},{2,3},{5,4},{4,5},{7,6},{6,7},{9,8},{8,9},{11,10... | collective-permute-start | bytes 18440 | tf_op jit(solution)/shard_map/ppermute | solution.py:49
  24.0 3.0 %collective-permute-start.9 = (f32[3,512]{1,0:T(4,128)S(1)}, f32[3,512]{1,0:T(4,128)S(1)}, u32[]{:S(2)}, u32[]{:S(2)}) collective-permute-start(f32[3,512]{1,0:T(4,128)S(1)} %shard_map.66.refs_5_.refs_0_), channel_id=1, source_target_pairs={{2,0},{3,1},{0,2},{1,3},{6,4},{7,5},{4,6},{5,7},{10,8},{11,9},{8,1... | collective-permute-start | bytes 18440 | tf_op jit(solution)/shard_map/ppermute | solution.py:49
  27.1 0.0 collective-permute-done.2.refs_2_
  27.1 0.2 collective-permute-start.10
  27.3 2.0 %shard_map.67 = (bf16[1536,1024]{1,0:T(8,128)(2,1)S(1)}, f32[6,1024]{1,0:T(8,128)S(1)}, bf16[1024,512]{1,0:T(8,128)(2,1)S(1)}) custom-call(bf16[256,512]{1,0:T(8,128)(2,1)S(1)} %shard_map.60.a.refs_0_, bf16[256,512]{1,0:T(8,128)(2,1)S(1)} %collective-permute-done.1.refs_3_.refs_1_.a, bf16[256,512]{1,0:T(8,128)(2,1)S(1)} %collective-permute-done.2.refs_2_, ...), custom_call_target="tpu_custom_call" | custom-call | flops 16106127 | bytes 57671 | tf_op jit(solution)/shard_map/pallas_call | solution.py:229
  29.3 0.0 collective-permute-done.8.refs_1_
  29.3 1.3 %collective-permute-start.7 = (bf16[256,512]{1,0:T(8,128)(2,1)S(1)}, bf16[256,512]{1,0:T(8,128)(2,1)S(1)}, u32[]{:S(2)}, u32[]{:S(2)}) collective-permute-start(bf16[256,512]{1,0:T(8,128)(2,1)S(1)} %shard_map.69), channel_id=1, source_target_pairs={{16,0},{12,4},{24,8},{4,12},{0,16},{28,20},{8,24},{20,28},{17,1},{... | collective-permute-start | bytes 786440 | tf_op jit(solution)/shard_map/ppermute | solution.py:49
  30.6 0.0 collective-permute-done.9.refs_2_
  30.6 1.9 %collective-permute-done.10.refs_3_ = f32[3,512]{1,0:T(4,128)S(1)} collective-permute-done((f32[3,512]{1,0:T(4,128)S(1)}, f32[3,512]{1,0:T(4,128)S(1)}, u32[]{:S(2)}, u32[]{:S(2)}) %collective-permute-start.10) | collective-permute-done | bytes 6176 | tf_op jit(solution)/shard_map/ppermute | solution.py:49
  32.5 0.0 collective-permute-done.5.refs_5_.refs_0_
  32.6 0.0 collective-permute-done.6.refs_1_.a
  32.6 0.6 %collective-permute-start.11 = (bf16[256,512]{1,0:T(8,128)(2,1)S(1)}, bf16[256,512]{1,0:T(8,128)(2,1)S(1)}, u32[]{:S(2)}, u32[]{:S(2)}) collective-permute-start(bf16[256,512]{1,0:T(8,128)(2,1)S(1)} %shard_map.72), channel_id=1, source_target_pairs={{16,0},{12,4},{24,8},{4,12},{0,16},{28,20},{8,24},{20,28},{17,1},{... | collective-permute-start | bytes 786440 | tf_op jit(solution)/shard_map/ppermute | solution.py:49
  33.2 0.5 %collective-permute-start.12 = (f32[2,512]{1,0:T(2,128)S(1)}, f32[2,512]{1,0:T(2,128)S(1)}, u32[]{:S(2)}, u32[]{:S(2)}) collective-permute-start(f32[2,512]{1,0:T(2,128)S(1)} %shard_map.70.refs_4_.refs_0_), channel_id=1, source_target_pairs={{8,0},{20,4},{0,8},{28,12},{24,16},{4,20},{16,24},{12,28},{9,1},{2... | collective-permute-start | bytes 12296 | tf_op jit(solution)/shard_map/ppermute | solution.py:49
  33.7 1.5 %collective-permute-start.13 = (f32[2,512]{1,0:T(2,128)S(1)}, f32[2,512]{1,0:T(2,128)S(1)}, u32[]{:S(2)}, u32[]{:S(2)}) collective-permute-start(f32[2,512]{1,0:T(2,128)S(1)} %shard_map.70.refs_4_.refs_0_), channel_id=1, source_target_pairs={{16,0},{12,4},{24,8},{4,12},{0,16},{28,20},{8,24},{20,28},{17,1},{... | collective-permute-start | bytes 12296 | tf_op jit(solution)/shard_map/ppermute | solution.py:49
  35.2 1.4 %collective-permute-start.14 = (f32[2,512]{1,0:T(2,128)S(1)}, f32[2,512]{1,0:T(2,128)S(1)}, u32[]{:S(2)}, u32[]{:S(2)}) collective-permute-start(f32[2,512]{1,0:T(2,128)S(1)} %shard_map.70.refs_4_.refs_0_), channel_id=1, source_target_pairs={{24,0},{16,8},{8,16},{0,24},{25,1},{17,9},{9,17},{1,25},{26,2},{18... | collective-permute-start | bytes 12296 | tf_op jit(solution)/shard_map/ppermute | solution.py:49
  36.7 0.0 collective-permute-done.7.refs_2_
  36.7 1.6 %shard_map.71 = (bf16[1536,768]{1,0:T(8,128)(2,1)S(1)}, f32[6,768]{1,0:T(8,128)S(1)}, bf16[768,512]{1,0:T(8,128)(2,1)S(1)}) custom-call(bf16[256,512]{1,0:T(8,128)(2,1)S(1)} %collective-permute-done.5.refs_5_.refs_0_, bf16[256,512]{1,0:T(8,128)(2,1)S(1)} %collective-permute-done.6.refs_1_.a, bf16[256,512]{1,0:T(8,128)(2,1)S(1)} %collective-permute-done.7.refs_2_, ...), custom_call_target="tpu_custom_call" | custom-call | flops 12079595 | bytes 47185 | tf_op jit(solution)/shard_map/pallas_call | solution.py:229
  38.2 0.8 %collective-permute-done.11.refs_0_ = bf16[256,512]{1,0:T(8,128)(2,1)S(1)} collective-permute-done((bf16[256,512]{1,0:T(8,128)(2,1)S(1)}, bf16[256,512]{1,0:T(8,128)(2,1)S(1)}, u32[]{:S(2)}, u32[]{:S(2)}) %collective-permute-start.11) | collective-permute-done | bytes 262176 | tf_op jit(solution)/shard_map/ppermute | solution.py:49
  39.0 0.7 %shard_map.73 = (bf16[1536,256]{1,0:T(8,128)(2,1)S(1)}, f32[6,256]{1,0:T(8,128)S(1)}, bf16[256,512]{1,0:T(8,128)(2,1)S(1)}) custom-call(bf16[256,512]{1,0:T(8,128)(2,1)S(1)} %collective-permute-done.11.refs_0_, bf16[6144,512]{1,0:T(8,128)(2,1)S(1)} %bitcast.3, f32[6,768]{1,0:T(8,128)S(1)} %get-tuple-element.25.refs_2_.refs_5_), custom_call_target="tpu_custom_call" | custom-call | flops 402653184 | bytes 2621440 | tf_op jit(solution)/shard_map/pallas_call | solution.py:229
  39.8 0.0 collective-permute-done.12.refs_1_
  39.8 0.0 collective-permute-done.13.refs_2_
  39.8 0.0 collective-permute-done.14.refs_3_
  39.8 1.0 %shard_map.76 = bf16[400,512]{1,0:T(8,128)(2,1)S(1)} custom-call(bf16[1536,1024]{1,0:T(8,128)(2,1)S(1)} %get-tuple-element.22.refs_0_, bf16[1536,768]{1,0:T(8,128)(2,1)S(1)} %get-tuple-element.24.refs_1_, bf16[1536,256]{1,0:T(8,128)(2,1)S(1)} %get-tuple-element.26.refs_2_, bf16[1024,512]{1,0:T(8,128)(2,1)S(1)} %get-tuple-element.27.refs_3_, ...), custom_call_target="tpu_custom_call" | custom-call | flops 4000000000 | tf_op jit(solution)/shard_map/pallas_call | solution.py:287
  40.8 0.1 collective-permute-start.15
  40.9 1.2 %shard_map.78 = bf16[400,512]{1,0:T(8,128)(2,1)S(1)} custom-call(bf16[1536,1024]{1,0:T(8,128)(2,1)S(1)} %get-tuple-element.22.refs_0_, bf16[1536,768]{1,0:T(8,128)(2,1)S(1)} %get-tuple-element.24.refs_1_, bf16[1536,256]{1,0:T(8,128)(2,1)S(1)} %get-tuple-element.26.refs_2_, bf16[1024,512]{1,0:T(8,128)(2,1)S(1)} %get-tuple-element.27.refs_3_, ...), custom_call_target="tpu_custom_call" | custom-call | flops 4000000000 | tf_op jit(solution)/shard_map/pallas_call | solution.py:287
  42.1 0.6 %collective-permute-start.16 = (bf16[400,512]{1,0:T(8,128)(2,1)S(1)}, bf16[400,512]{1,0:T(8,128)(2,1)S(1)}, u32[]{:S(2)}, u32[]{:S(2)}) collective-permute-start(bf16[400,512]{1,0:T(8,128)(2,1)S(1)} %shard_map.78), channel_id=1, source_target_pairs={{4,0},{0,4},{5,1},{1,5},{6,2},{2,6},{7,3},{3,7},{12,8},{8,12},{13,... | collective-permute-start | bytes 1228808 | tf_op jit(solution)/shard_map/ppermute | solution.py:49
  42.6 1.0 %shard_map.75 = (f32[384,512]{1,0:T(8,128)S(1)}, f32[1,384]{1,0:T(1,128)S(1)}) custom-call(bf16[1536,1024]{1,0:T(8,128)(2,1)S(1)} %get-tuple-element.22.refs_0_, bf16[1536,768]{1,0:T(8,128)(2,1)S(1)} %get-tuple-element.24.refs_1_, bf16[1536,256]{1,0:T(8,128)(2,1)S(1)} %get-tuple-element.26.refs_2_, bf16[1024,512]{1,0:T(8,128)(2,1)S(1)} %get-tuple-element.27.refs_3_, ...), custom_call_target="tpu_custom_call" | custom-call | flops 4000000000 | tf_op jit(solution)/shard_map/pallas_call | solution.py:287
  43.7 0.0 collective-permute-done.15.refs_11_
  43.7 1.9 %shard_map.77 = (f32[768,512]{1,0:T(8,128)}, f32[1,384]{1,0:T(1,128)S(1)}, f32[384,512]{1,0:T(8,128)S(1)}, f32[1,384]{1,0:T(1,128)S(1)}) custom-call(bf16[1536,1024]{1,0:T(8,128)(2,1)S(1)} %get-tuple-element.22.refs_0_, bf16[1536,768]{1,0:T(8,128)(2,1)S(1)} %get-tuple-element.24.refs_1_, bf16[1536,256]{1,0:T(8,128)(2,1)S(1)} %get-tuple-element.26.refs_2_, ...), custom_call_target="tpu_custom_call" | custom-call | tf_op jit(solution)/shard_map/pallas_call | solution.py:321
  45.6 0.0 collective-permute-done.16.there
  45.6 1.5 %shard_map.79 = (f32[768,512]{1,0:T(8,128)}, f32[1,768]{1,0:T(1,128)}) custom-call(f32[768,512]{1,0:T(8,128)} %get-tuple-element.36.so_far, f32[1,384]{1,0:T(1,128)S(1)} %get-tuple-element.37.mass_so_far, f32[384,512]{1,0:T(8,128)S(1)} %get-tuple-element.38.here, f32[1,384]{1,0:T(1,128)S(1)} %get-tuple-element.39.here_mass, ...), custom_call_target="tpu_custom_call", output_to_operand_aliasing={{0}: (0, {})} | custom-call | tf_op jit(solution)/shard_map/pallas_call | solution.py:351
  (11 shorter events, 0.2 us)
Async XLA Ops:
  1.7 8.1 %collective-permute-start = (bf16[128,512]{1,0:T(8,128)(2,1)S(1)}, bf16[128,512]{1,0:T(8,128)(2,1)S(1)}, u32[]{:S(2)}, u32[]{:S(2)}) collective-permute-start(bf16[128,512]{1,0:T(8,128)(2,1)S(1)} %multiply_convert_fusion.above), channel_id=1, source_target_pairs={{1,0},{0,1},{3,2},{2,3},{5,4},{4,5},{7,6},{6,7},{9,8},{8,9},{11,10... | collective-permute-start | bytes 393224 | tf_op jit(solution)/shard_map/ppermute | solution.py:49
  4.8 13.8 %collective-permute-start.3 = (bf16[128,512]{1,0:T(8,128)(2,1)S(1)}, bf16[128,512]{1,0:T(8,128)(2,1)S(1)}, u32[]{:S(2)}, u32[]{:S(2)}) collective-permute-start(bf16[128,512]{1,0:T(8,128)(2,1)S(1)} %multiply_convert_fusion.above), channel_id=1, source_target_pairs={{2,0},{3,1},{0,2},{1,3},{6,4},{7,5},{4,6},{5,7},{10,8},{11,9},{8,1... | collective-permute-start | bytes 393224 | tf_op jit(solution)/shard_map/ppermute | solution.py:49
  7.4 11.2 %collective-permute-start.4 = (bf16[128,512]{1,0:T(8,128)(2,1)S(1)}, bf16[128,512]{1,0:T(8,128)(2,1)S(1)}, u32[]{:S(2)}, u32[]{:S(2)}) collective-permute-start(bf16[128,512]{1,0:T(8,128)(2,1)S(1)} %multiply_convert_fusion.above), channel_id=1, source_target_pairs={{3,0},{2,1},{1,2},{0,3},{7,4},{6,5},{5,6},{4,7},{11,8},{10,9},{9,1... | collective-permute-start | bytes 393224 | tf_op jit(solution)/shard_map/ppermute | solution.py:49
  7.4 0.7 %copy-start = (s32[6144]{0:T(1024)S(1)}, s32[6144]{0:T(1024)}, u32[]{:S(2)}) copy-start(s32[6144]{0:T(1024)} %param.7) | copy-start | bytes 73732
  8.1 3.5 %slice-start = ((s8[6291456]{0:T(1024)(128)(4,1)}), s8[4194304]{0:T(1024)(128)(4,1)S(1)}, s32[]{:S(2)}) async-start(s8[6291456]{0:T(1024)(128)(4,1)} %bitcast.2), calls=%async_computation | async-start | bytes 8388608
  9.0 2.6 %slice-start.1 = ((s8[6291456]{0:T(1024)(128)(4,1)}), s8[2097152]{0:T(1024)(128)(4,1)S(1)}, s32[]{:S(2)}) async-start(s8[6291456]{0:T(1024)(128)(4,1)} %bitcast.2), calls=%async_computation.1 | async-start | bytes 4194304
  9.8 6.7 %collective-permute-start.1 = (bf16[256,512]{1,0:T(8,128)(2,1)S(1)}, bf16[256,512]{1,0:T(8,128)(2,1)S(1)}, u32[]{:S(2)}, u32[]{:S(2)}) collective-permute-start(bf16[256,512]{1,0:T(8,128)(2,1)S(1)} %shard_map.60.a.refs_0_), channel_id=1, source_target_pairs={{8,0},{20,4},{0,8},{28,12},{24,16},{4,20},{16,24},{12,28},{9,1},{2... | collective-permute-start | bytes 786440 | tf_op jit(solution)/shard_map/ppermute | solution.py:49
  14.5 12.6 %collective-permute-start.2 = (bf16[256,512]{1,0:T(8,128)(2,1)S(1)}, bf16[256,512]{1,0:T(8,128)(2,1)S(1)}, u32[]{:S(2)}, u32[]{:S(2)}) collective-permute-start(bf16[256,512]{1,0:T(8,128)(2,1)S(1)} %shard_map.63), channel_id=1, source_target_pairs={{16,0},{12,4},{24,8},{4,12},{0,16},{28,20},{8,24},{20,28},{17,1},{... | collective-permute-start | bytes 786440 | tf_op jit(solution)/shard_map/ppermute | solution.py:49
  16.5 16.0 %collective-permute-start.5 = (bf16[256,512]{1,0:T(8,128)(2,1)S(1)}, bf16[256,512]{1,0:T(8,128)(2,1)S(1)}, u32[]{:S(2)}, u32[]{:S(2)}) collective-permute-start(bf16[256,512]{1,0:T(8,128)(2,1)S(1)} %shard_map.68), channel_id=1, source_target_pairs={{16,0},{12,4},{24,8},{4,12},{0,16},{28,20},{8,24},{20,28},{17,1},{... | collective-permute-start | bytes 786440 | tf_op jit(solution)/shard_map/ppermute | solution.py:49
  18.6 14.0 %collective-permute-start.6 = (bf16[256,512]{1,0:T(8,128)(2,1)S(1)}, bf16[256,512]{1,0:T(8,128)(2,1)S(1)}, u32[]{:S(2)}, u32[]{:S(2)}) collective-permute-start(bf16[256,512]{1,0:T(8,128)(2,1)S(1)} %shard_map.64.refs_0_.refs_3_.a), channel_id=1, source_target_pairs={{8,0},{20,4},{0,8},{28,12},{24,16},{4,20},{16,24},{12,28},{9,1},{2... | collective-permute-start | bytes 786440 | tf_op jit(solution)/shard_map/ppermute | solution.py:49
  22.8 6.5 %collective-permute-start.8 = (f32[3,512]{1,0:T(4,128)S(1)}, f32[3,512]{1,0:T(4,128)S(1)}, u32[]{:S(2)}, u32[]{:S(2)}) collective-permute-start(f32[3,512]{1,0:T(4,128)S(1)} %shard_map.66.refs_5_.refs_0_), channel_id=1, source_target_pairs={{1,0},{0,1},{3,2},{2,3},{5,4},{4,5},{7,6},{6,7},{9,8},{8,9},{11,10... | collective-permute-start | bytes 18440 | tf_op jit(solution)/shard_map/ppermute | solution.py:49
  24.0 6.6 %collective-permute-start.9 = (f32[3,512]{1,0:T(4,128)S(1)}, f32[3,512]{1,0:T(4,128)S(1)}, u32[]{:S(2)}, u32[]{:S(2)}) collective-permute-start(f32[3,512]{1,0:T(4,128)S(1)} %shard_map.66.refs_5_.refs_0_), channel_id=1, source_target_pairs={{2,0},{3,1},{0,2},{1,3},{6,4},{7,5},{4,6},{5,7},{10,8},{11,9},{8,1... | collective-permute-start | bytes 18440 | tf_op jit(solution)/shard_map/ppermute | solution.py:49
  27.1 5.4 %collective-permute-start.10 = (f32[3,512]{1,0:T(4,128)S(1)}, f32[3,512]{1,0:T(4,128)S(1)}, u32[]{:S(2)}, u32[]{:S(2)}) collective-permute-start(f32[3,512]{1,0:T(4,128)S(1)} %shard_map.66.refs_5_.refs_0_), channel_id=1, source_target_pairs={{3,0},{2,1},{1,2},{0,3},{7,4},{6,5},{5,6},{4,7},{11,8},{10,9},{9,1... | collective-permute-start | bytes 18440 | tf_op jit(solution)/shard_map/ppermute | solution.py:49
  29.3 7.3 %collective-permute-start.7 = (bf16[256,512]{1,0:T(8,128)(2,1)S(1)}, bf16[256,512]{1,0:T(8,128)(2,1)S(1)}, u32[]{:S(2)}, u32[]{:S(2)}) collective-permute-start(bf16[256,512]{1,0:T(8,128)(2,1)S(1)} %shard_map.69), channel_id=1, source_target_pairs={{16,0},{12,4},{24,8},{4,12},{0,16},{28,20},{8,24},{20,28},{17,1},{... | collective-permute-start | bytes 786440 | tf_op jit(solution)/shard_map/ppermute | solution.py:49
  32.6 6.4 %collective-permute-start.11 = (bf16[256,512]{1,0:T(8,128)(2,1)S(1)}, bf16[256,512]{1,0:T(8,128)(2,1)S(1)}, u32[]{:S(2)}, u32[]{:S(2)}) collective-permute-start(bf16[256,512]{1,0:T(8,128)(2,1)S(1)} %shard_map.72), channel_id=1, source_target_pairs={{16,0},{12,4},{24,8},{4,12},{0,16},{28,20},{8,24},{20,28},{17,1},{... | collective-permute-start | bytes 786440 | tf_op jit(solution)/shard_map/ppermute | solution.py:49
  33.2 6.6 %collective-permute-start.12 = (f32[2,512]{1,0:T(2,128)S(1)}, f32[2,512]{1,0:T(2,128)S(1)}, u32[]{:S(2)}, u32[]{:S(2)}) collective-permute-start(f32[2,512]{1,0:T(2,128)S(1)} %shard_map.70.refs_4_.refs_0_), channel_id=1, source_target_pairs={{8,0},{20,4},{0,8},{28,12},{24,16},{4,20},{16,24},{12,28},{9,1},{2... | collective-permute-start | bytes 12296 | tf_op jit(solution)/shard_map/ppermute | solution.py:49
  33.7 6.1 %collective-permute-start.13 = (f32[2,512]{1,0:T(2,128)S(1)}, f32[2,512]{1,0:T(2,128)S(1)}, u32[]{:S(2)}, u32[]{:S(2)}) collective-permute-start(f32[2,512]{1,0:T(2,128)S(1)} %shard_map.70.refs_4_.refs_0_), channel_id=1, source_target_pairs={{16,0},{12,4},{24,8},{4,12},{0,16},{28,20},{8,24},{20,28},{17,1},{... | collective-permute-start | bytes 12296 | tf_op jit(solution)/shard_map/ppermute | solution.py:49
  35.2 4.5 %collective-permute-start.14 = (f32[2,512]{1,0:T(2,128)S(1)}, f32[2,512]{1,0:T(2,128)S(1)}, u32[]{:S(2)}, u32[]{:S(2)}) collective-permute-start(f32[2,512]{1,0:T(2,128)S(1)} %shard_map.70.refs_4_.refs_0_), channel_id=1, source_target_pairs={{24,0},{16,8},{8,16},{0,24},{25,1},{17,9},{9,17},{1,25},{26,2},{18... | collective-permute-start | bytes 12296 | tf_op jit(solution)/shard_map/ppermute | solution.py:49
  40.8 2.8 %collective-permute-start.15 = (bf16[400,512]{1,0:T(8,128)(2,1)S(1)}, bf16[400,512]{1,0:T(8,128)(2,1)S(1)}, u32[]{:S(2)}, u32[]{:S(2)}) collective-permute-start(bf16[400,512]{1,0:T(8,128)(2,1)S(1)} %shard_map.76), channel_id=1, source_target_pairs={{4,0},{0,4},{5,1},{1,5},{6,2},{2,6},{7,3},{3,7},{12,8},{8,12},{13,... | collective-permute-start | bytes 1228808 | tf_op jit(solution)/shard_map/ppermute | solution.py:49
  42.1 3.5 %collective-permute-start.16 = (bf16[400,512]{1,0:T(8,128)(2,1)S(1)}, bf16[400,512]{1,0:T(8,128)(2,1)S(1)}, u32[]{:S(2)}, u32[]{:S(2)}) collective-permute-start(bf16[400,512]{1,0:T(8,128)(2,1)S(1)} %shard_map.78), channel_id=1, source_target_pairs={{4,0},{0,4},{5,1},{1,5},{6,2},{2,6},{7,3},{3,7},{12,8},{8,12},{13,... | collective-permute-start | bytes 1228808 | tf_op jit(solution)/shard_map/ppermute | solution.py:49

commit v26 on v21

--- a/solution.py
+++ b/solution.py
@@ -289,17 +289,20 @@
     )(*expos, *points, *factors)
 
 
-def add_kernel(block, here, here_mass, there, there_mass, sums, mass, out, left):
+def add_kernel(block, here, here_mass, there, there_mass, sums, mass, out, mass_out, left):
     def copy(at):
         rows = pl.ds(at * block, block)
         return pltpu.make_async_copy(out.at[rows, :], sums.at[rows, :], left.at[at])
 
     count = here.shape[0] // block
+    mass_out[...] = here_mass[...] + there_mass[...]
+    mass_copy = pltpu.make_async_copy(mass_out, mass, left.at[count])
+    mass_copy.start()
     for at in range(count):
         rows = slice(at * block, (at + 1) * block)
         out[rows, :] = here[rows, :] + there[rows, :].astype(jnp.float32)
         copy(at).start(priority=at % 2)
-    mass[...] = here_mass[...] + there_mass[...]
+    mass_copy.wait()
     for at in range(count):
         copy(at).wait()
 
@@ -308,14 +311,15 @@
     return pl.pallas_call(
         functools.partial(add_kernel, block),
         in_specs=in_vmem(4),
-        out_specs=[pl.BlockSpec(memory_space=pltpu.HBM)] + in_vmem(1),
+        out_specs=[pl.BlockSpec(memory_space=pltpu.HBM)] * 2,
         out_shape=[
             jax.ShapeDtypeStruct(here.shape, jnp.float32),
             jax.ShapeDtypeStruct(here_mass.shape, jnp.float32),
         ],
         scratch_shapes=[
             pltpu.VMEM(here.shape, jnp.float32),
-            pltpu.SemaphoreType.DMA((here.shape[0] // block,)),
+            pltpu.VMEM(here_mass.shape, jnp.float32),
+            pltpu.SemaphoreType.DMA((here.shape[0] // block + 1,)),
         ],
         compiler_params=pltpu.CompilerParams(vmem_limit_bytes=VMEM_BYTES),
     )(here, here_mass, there, there_mass)

time: 46.2 us -> 45.7 us (0.989)
  Pallas kernels: 16.4 us -> 15.9 us
    pallas_call x1, Pallas kernels: 1.79 us -> 1.23 us  [add_call(): pl.pallas_call(functools.partial(add_kernel, block), in_specs=in_vmem(4),...]
  transfers between devices with their start and end apart: 17 -> 17, of which waited for: 6 -> 6; matrix products, arithmetic and copies ran while one was open for 0% -> 0% of each run, Pallas kernels for 27% -> 28%
where the time goes in v26:
time: 45.7 us; the launch traced here: 45.5 us
  starting transfers between devices  22.3 us (49%)
  Pallas kernels  15.9 us (35%)
  waiting for transfers between devices  4.47 us (10%)
  other arithmetic  1.05 us (2%)
  between operations  1.01 us (2%)
  local copies, waits for them, and re-layouts  0.75 us (2%)
    ppermute x17, starting transfers between devices, exchange(): return lax.ppermute(a, axes, [(partner(at), at) for at in range(count)])  22.3 us
    pallas_call x2, Pallas kernels, totals_call(): pl.pallas_call(functools.partial(totals_kernel, rate, block, len(pieces))...  5.41 us
    ppermute x17, waiting for transfers between devices, exchange(): return lax.ppermute(a, axes, [(partner(at), at) for at in range(count)])  4.47 us
    pallas_call x3, Pallas kernels, expo_call(): pl.pallas_call(functools.partial(expo_kernel, rate, block, spots), in_spe...  4.27 us
    pallas_call x2, Pallas kernels, sums_call(): pl.pallas_call(functools.partial(sums_kernel, n, block, side), in_specs=i...  3.89 us
    pallas_call x1, Pallas kernels, add_call(): pl.pallas_call(functools.partial(add_kernel, block), in_specs=in_vmem(4),...  1.23 us
    convert_element_type x1, other arithmetic, to_points(): return (scaled.astype(jnp.float32) * 2.0 ** (-16)).astype(jnp.bfloat16)  1.05 us
  transfers between devices with their start and end apart: 17, of which 6 were waited for; matrix products, arithmetic and copies ran while one was open for 0% of the time, Pallas kernels for 28%

profile of v26, /device:TPU:0, one launch (start us, length us, event | category | flops | bytes accessed | tf_op | source)
XLA Modules:
  0.0 45.5 jit_solution(13452984679339689611)
XLA Ops:
  0.6 1.1 %multiply_convert_fusion.above = bf16[128,512]{1,0:T(8,128)(2,1)S(1)} fusion(s32[128,512]{1,0:T(8,128)} %param.4, s32[128]{0:T(128)} %param.5), kind=kLoop, calls=%fused_computation | loop fusion | flops 327680 | bytes 393728 | tf_op jit(solution)/shard_map/convert_element_type | solution.py:17
  1.7 3.1 %collective-permute-start = (bf16[128,512]{1,0:T(8,128)(2,1)S(1)}, bf16[128,512]{1,0:T(8,128)(2,1)S(1)}, u32[]{:S(2)}, u32[]{:S(2)}) collective-permute-start(bf16[128,512]{1,0:T(8,128)(2,1)S(1)} %multiply_convert_fusion.above), channel_id=1, source_target_pairs={{1,0},{0,1},{3,2},{2,3},{5,4},{4,5},{7,6},{6,7},{9,8},{8,9},{11,10... | collective-permute-start | bytes 393224 | tf_op jit(solution)/shard_map/ppermute | solution.py:49
  4.8 2.6 %collective-permute-start.3 = (bf16[128,512]{1,0:T(8,128)(2,1)S(1)}, bf16[128,512]{1,0:T(8,128)(2,1)S(1)}, u32[]{:S(2)}, u32[]{:S(2)}) collective-permute-start(bf16[128,512]{1,0:T(8,128)(2,1)S(1)} %multiply_convert_fusion.above), channel_id=1, source_target_pairs={{2,0},{3,1},{0,2},{1,3},{6,4},{7,5},{4,6},{5,7},{10,8},{11,9},{8,1... | collective-permute-start | bytes 393224 | tf_op jit(solution)/shard_map/ppermute | solution.py:49
  7.4 0.0 collective-permute-start.4
  7.4 0.0 copy-start
  7.4 0.7 %copy-done = s32[6144]{0:T(1024)S(1)} copy-done((s32[6144]{0:T(1024)S(1)}, s32[6144]{0:T(1024)}, u32[]{:S(2)}) %copy-start) | copy-done | bytes 24600
  8.1 0.0 slice-start
  8.1 0.9 %shard_map.59.refs_0_.refs_2_ = f32[6144,128]{1,0:T(8,128)S(1)} custom-call(s32[48,128]{1,0:T(8,128)S(1)} %bitcast.4), custom_call_target="tpu_custom_call" | custom-call | flops 2000000000 | tf_op jit(solution)/shard_map/pallas_call | solution.py:114
  9.0 0.0 slice-start.1
  9.0 0.8 %collective-permute-done.below = bf16[128,512]{1,0:T(8,128)(2,1)S(1)} collective-permute-done((bf16[128,512]{1,0:T(8,128)(2,1)S(1)}, bf16[128,512]{1,0:T(8,128)(2,1)S(1)}, u32[]{:S(2)}, u32[]{:S(2)}) %collective-permute-start) | collective-permute-done | bytes 131104 | tf_op jit(solution)/shard_map/ppermute | solution.py:49
  9.8 1.8 %collective-permute-start.1 = (bf16[256,512]{1,0:T(8,128)(2,1)S(1)}, bf16[256,512]{1,0:T(8,128)(2,1)S(1)}, u32[]{:S(2)}, u32[]{:S(2)}) collective-permute-start(bf16[256,512]{1,0:T(8,128)(2,1)S(1)} %shard_map.60.a.refs_0_), channel_id=1, source_target_pairs={{8,0},{20,4},{0,8},{28,12},{24,16},{4,20},{16,24},{12,28},{9,1},{2... | collective-permute-start | bytes 786440 | tf_op jit(solution)/shard_map/ppermute | solution.py:49
  11.6 0.0 slice-done
  11.6 0.0 slice-done.1
  11.7 2.7 %shard_map.62.refs_0_.left = f32[3,256]{1,0:T(4,128)S(1)} custom-call(bf16[256,512]{1,0:T(8,128)(2,1)S(1)} %shard_map.61.refs_0_, bf16[6144,512]{1,0:T(8,128)(2,1)S(1)} %bitcast.3, f32[6144,128]{1,0:T(8,128)S(1)} %shard_map.59.refs_0_.refs_2_), custom_call_target="tpu_custom_call" | custom-call | flops 1610612736 | bytes 6291456 | tf_op jit(solution)/shard_map/pallas_call | solution.py:154
  14.4 1.6 %collective-permute-start.2 = (bf16[256,512]{1,0:T(8,128)(2,1)S(1)}, bf16[256,512]{1,0:T(8,128)(2,1)S(1)}, u32[]{:S(2)}, u32[]{:S(2)}) collective-permute-start(bf16[256,512]{1,0:T(8,128)(2,1)S(1)} %shard_map.63), channel_id=1, source_target_pairs={{16,0},{12,4},{24,8},{4,12},{0,16},{28,20},{8,24},{20,28},{17,1},{... | collective-permute-start | bytes 786440 | tf_op jit(solution)/shard_map/ppermute | solution.py:49
  16.0 0.6 %collective-permute-done.1.refs_3_.refs_1_.a = bf16[256,512]{1,0:T(8,128)(2,1)S(1)} collective-permute-done((bf16[256,512]{1,0:T(8,128)(2,1)S(1)}, bf16[256,512]{1,0:T(8,128)(2,1)S(1)}, u32[]{:S(2)}, u32[]{:S(2)}) %collective-permute-start.1) | collective-permute-done | bytes 262176 | tf_op jit(solution)/shard_map/ppermute | solution.py:49
  16.6 2.0 %collective-permute-start.5 = (bf16[256,512]{1,0:T(8,128)(2,1)S(1)}, bf16[256,512]{1,0:T(8,128)(2,1)S(1)}, u32[]{:S(2)}, u32[]{:S(2)}) collective-permute-start(bf16[256,512]{1,0:T(8,128)(2,1)S(1)} %shard_map.68), channel_id=1, source_target_pairs={{16,0},{12,4},{24,8},{4,12},{0,16},{28,20},{8,24},{20,28},{17,1},{... | collective-permute-start | bytes 786440 | tf_op jit(solution)/shard_map/ppermute | solution.py:49
  18.7 0.0 collective-permute-done.3.above
  18.7 0.0 collective-permute-done.4.below
  18.7 1.6 %collective-permute-start.6 = (bf16[256,512]{1,0:T(8,128)(2,1)S(1)}, bf16[256,512]{1,0:T(8,128)(2,1)S(1)}, u32[]{:S(2)}, u32[]{:S(2)}) collective-permute-start(bf16[256,512]{1,0:T(8,128)(2,1)S(1)} %shard_map.64.refs_0_.refs_3_.a), channel_id=1, source_target_pairs={{8,0},{20,4},{0,8},{28,12},{24,16},{4,20},{16,24},{12,28},{9,1},{2... | collective-permute-start | bytes 786440 | tf_op jit(solution)/shard_map/ppermute | solution.py:49
  20.2 2.7 %shard_map.65.right = f32[3,256]{1,0:T(4,128)S(1)} custom-call(bf16[256,512]{1,0:T(8,128)(2,1)S(1)} %shard_map.64.refs_0_.refs_3_.a, bf16[6144,512]{1,0:T(8,128)(2,1)S(1)} %bitcast.3, f32[6144,128]{1,0:T(8,128)S(1)} %shard_map.59.refs_0_.refs_2_, bf16[256,512]{1,0:T(8,128)(2,1)S(1)} %collective-permute-done.1.refs_3_.refs_1_.a), custom_call_target="tpu_custom_call" | custom-call | flops 1610612736 | bytes 6291456 | tf_op jit(solution)/shard_map/pallas_call | solution.py:154
  23.0 3.7 %collective-permute-start.10 = (f32[3,512]{1,0:T(4,128)S(1)}, f32[3,512]{1,0:T(4,128)S(1)}, u32[]{:S(2)}, u32[]{:S(2)}) collective-permute-start(f32[3,512]{1,0:T(4,128)S(1)} %shard_map.66.refs_5_.refs_0_), channel_id=1, source_target_pairs={{3,0},{2,1},{1,2},{0,3},{7,4},{6,5},{5,6},{4,7},{11,8},{10,9},{9,1... | collective-permute-start | bytes 18440 | tf_op jit(solution)/shard_map/ppermute | solution.py:49
  26.6 0.0 collective-permute-start.8
  26.6 0.0 collective-permute-done.2.refs_2_
  26.6 0.8 %collective-permute-start.9 = (f32[3,512]{1,0:T(4,128)S(1)}, f32[3,512]{1,0:T(4,128)S(1)}, u32[]{:S(2)}, u32[]{:S(2)}) collective-permute-start(f32[3,512]{1,0:T(4,128)S(1)} %shard_map.66.refs_5_.refs_0_), channel_id=1, source_target_pairs={{2,0},{3,1},{0,2},{1,3},{6,4},{7,5},{4,6},{5,7},{10,8},{11,9},{8,1... | collective-permute-start | bytes 18440 | tf_op jit(solution)/shard_map/ppermute | solution.py:49
  27.4 2.0 %shard_map.67 = (bf16[1536,1024]{1,0:T(8,128)(2,1)S(1)}, f32[6,1024]{1,0:T(8,128)S(1)}, bf16[1024,512]{1,0:T(8,128)(2,1)S(1)}) custom-call(bf16[256,512]{1,0:T(8,128)(2,1)S(1)} %shard_map.60.a.refs_0_, bf16[256,512]{1,0:T(8,128)(2,1)S(1)} %collective-permute-done.1.refs_3_.refs_1_.a, bf16[256,512]{1,0:T(8,128)(2,1)S(1)} %collective-permute-done.2.refs_2_, ...), custom_call_target="tpu_custom_call" | custom-call | flops 16106127 | bytes 57671 | tf_op jit(solution)/shard_map/pallas_call | solution.py:229
  29.5 0.0 collective-permute-done.10.refs_3_
  29.5 0.6 %collective-permute-start.7 = (bf16[256,512]{1,0:T(8,128)(2,1)S(1)}, bf16[256,512]{1,0:T(8,128)(2,1)S(1)}, u32[]{:S(2)}, u32[]{:S(2)}) collective-permute-start(bf16[256,512]{1,0:T(8,128)(2,1)S(1)} %shard_map.69), channel_id=1, source_target_pairs={{16,0},{12,4},{24,8},{4,12},{0,16},{28,20},{8,24},{20,28},{17,1},{... | collective-permute-start | bytes 786440 | tf_op jit(solution)/shard_map/ppermute | solution.py:49
  30.1 0.2 collective-permute-done.8.refs_1_
  30.3 0.9 %collective-permute-done.9.refs_2_ = f32[3,512]{1,0:T(4,128)S(1)} collective-permute-done((f32[3,512]{1,0:T(4,128)S(1)}, f32[3,512]{1,0:T(4,128)S(1)}, u32[]{:S(2)}, u32[]{:S(2)}) %collective-permute-start.9) | collective-permute-done | bytes 6176 | tf_op jit(solution)/shard_map/ppermute | solution.py:49
  31.2 0.0 collective-permute-done.5.refs_5_.refs_0_
  31.2 0.0 collective-permute-done.6.refs_1_.a
  31.3 0.6 %collective-permute-start.11 = (bf16[256,512]{1,0:T(8,128)(2,1)S(1)}, bf16[256,512]{1,0:T(8,128)(2,1)S(1)}, u32[]{:S(2)}, u32[]{:S(2)}) collective-permute-start(bf16[256,512]{1,0:T(8,128)(2,1)S(1)} %shard_map.72), channel_id=1, source_target_pairs={{16,0},{12,4},{24,8},{4,12},{0,16},{28,20},{8,24},{20,28},{17,1},{... | collective-permute-start | bytes 786440 | tf_op jit(solution)/shard_map/ppermute | solution.py:49
  31.8 0.6 %collective-permute-start.12 = (f32[2,512]{1,0:T(2,128)S(1)}, f32[2,512]{1,0:T(2,128)S(1)}, u32[]{:S(2)}, u32[]{:S(2)}) collective-permute-start(f32[2,512]{1,0:T(2,128)S(1)} %shard_map.70.refs_4_.refs_0_), channel_id=1, source_target_pairs={{8,0},{20,4},{0,8},{28,12},{24,16},{4,20},{16,24},{12,28},{9,1},{2... | collective-permute-start | bytes 12296 | tf_op jit(solution)/shard_map/ppermute | solution.py:49
  32.4 1.5 %collective-permute-start.13 = (f32[2,512]{1,0:T(2,128)S(1)}, f32[2,512]{1,0:T(2,128)S(1)}, u32[]{:S(2)}, u32[]{:S(2)}) collective-permute-start(f32[2,512]{1,0:T(2,128)S(1)} %shard_map.70.refs_4_.refs_0_), channel_id=1, source_target_pairs={{16,0},{12,4},{24,8},{4,12},{0,16},{28,20},{8,24},{20,28},{17,1},{... | collective-permute-start | bytes 12296 | tf_op jit(solution)/shard_map/ppermute | solution.py:49
  33.9 1.4 %collective-permute-start.14 = (f32[2,512]{1,0:T(2,128)S(1)}, f32[2,512]{1,0:T(2,128)S(1)}, u32[]{:S(2)}, u32[]{:S(2)}) collective-permute-start(f32[2,512]{1,0:T(2,128)S(1)} %shard_map.70.refs_4_.refs_0_), channel_id=1, source_target_pairs={{24,0},{16,8},{8,16},{0,24},{25,1},{17,9},{9,17},{1,25},{26,2},{18... | collective-permute-start | bytes 12296 | tf_op jit(solution)/shard_map/ppermute | solution.py:49
  35.3 0.6 %collective-permute-done.7.refs_2_ = bf16[256,512]{1,0:T(8,128)(2,1)S(1)} collective-permute-done((bf16[256,512]{1,0:T(8,128)(2,1)S(1)}, bf16[256,512]{1,0:T(8,128)(2,1)S(1)}, u32[]{:S(2)}, u32[]{:S(2)}) %collective-permute-start.7) | collective-permute-done | bytes 262176 | tf_op jit(solution)/shard_map/ppermute | solution.py:49
  36.0 1.6 %shard_map.71 = (bf16[1536,768]{1,0:T(8,128)(2,1)S(1)}, f32[6,768]{1,0:T(8,128)S(1)}, bf16[768,512]{1,0:T(8,128)(2,1)S(1)}) custom-call(bf16[256,512]{1,0:T(8,128)(2,1)S(1)} %collective-permute-done.5.refs_5_.refs_0_, bf16[256,512]{1,0:T(8,128)(2,1)S(1)} %collective-permute-done.6.refs_1_.a, bf16[256,512]{1,0:T(8,128)(2,1)S(1)} %collective-permute-done.7.refs_2_, ...), custom_call_target="tpu_custom_call" | custom-call | flops 12079595 | bytes 47185 | tf_op jit(solution)/shard_map/pallas_call | solution.py:229
  37.5 1.3 %collective-permute-done.11.refs_0_ = bf16[256,512]{1,0:T(8,128)(2,1)S(1)} collective-permute-done((bf16[256,512]{1,0:T(8,128)(2,1)S(1)}, bf16[256,512]{1,0:T(8,128)(2,1)S(1)}, u32[]{:S(2)}, u32[]{:S(2)}) %collective-permute-start.11) | collective-permute-done | bytes 262176 | tf_op jit(solution)/shard_map/ppermute | solution.py:49
  38.8 0.7 %shard_map.73 = (bf16[1536,256]{1,0:T(8,128)(2,1)S(1)}, f32[6,256]{1,0:T(8,128)S(1)}, bf16[256,512]{1,0:T(8,128)(2,1)S(1)}) custom-call(bf16[256,512]{1,0:T(8,128)(2,1)S(1)} %collective-permute-done.11.refs_0_, bf16[6144,512]{1,0:T(8,128)(2,1)S(1)} %bitcast.3, f32[6,768]{1,0:T(8,128)S(1)} %get-tuple-element.23.refs_2_.refs_5_), custom_call_target="tpu_custom_call" | custom-call | flops 402653184 | bytes 2621440 | tf_op jit(solution)/shard_map/pallas_call | solution.py:229
  39.5 0.0 collective-permute-done.12.refs_1_
  39.5 0.0 collective-permute-done.13.refs_2_
  39.6 0.0 collective-permute-done.14.refs_3_
  39.6 2.1 %shard_map.76 = (bf16[768,512]{1,0:T(8,128)(2,1)S(1)}, f32[1,768]{1,0:T(1,128)S(1)}) custom-call(bf16[1536,1024]{1,0:T(8,128)(2,1)S(1)} %get-tuple-element.20.refs_0_, bf16[1536,768]{1,0:T(8,128)(2,1)S(1)} %get-tuple-element.22.refs_1_, bf16[1536,256]{1,0:T(8,128)(2,1)S(1)} %get-tuple-element.24.refs_2_, bf16[1024,512]{1,0:T(8,128)(2,1)S(1)} %get-tuple-element.25.refs_3_, ...), custom_call_target="tpu_custom_call" | custom-call | flops 2415919104 | bytes 9437184 | tf_op jit(solution)/shard_map/pallas_call | solution.py:278
  41.7 0.1 collective-permute-start.15
  41.7 0.5 %collective-permute-start.16 = (f32[1,768]{1,0:T(1,128)S(1)}, f32[1,768]{1,0:T(1,128)S(1)}, u32[]{:S(2)}, u32[]{:S(2)}) collective-permute-start(f32[1,768]{1,0:T(1,128)S(1)} %get-tuple-element.35), channel_id=1, source_target_pairs={{4,0},{0,4},{5,1},{1,5},{6,2},{2,6},{7,3},{3,7},{12,8},{8,12},{13,... | collective-permute-start | bytes 9224 | tf_op jit(solution)/shard_map/ppermute | solution.py:49
  42.2 1.8 %shard_map.75 = (f32[768,512]{1,0:T(8,128)S(1)}, f32[1,768]{1,0:T(1,128)S(1)}) custom-call(bf16[1536,1024]{1,0:T(8,128)(2,1)S(1)} %get-tuple-element.20.refs_0_, bf16[1536,768]{1,0:T(8,128)(2,1)S(1)} %get-tuple-element.22.refs_1_, bf16[1536,256]{1,0:T(8,128)(2,1)S(1)} %get-tuple-element.24.refs_2_, bf16[1024,512]{1,0:T(8,128)(2,1)S(1)} %get-tuple-element.25.refs_3_, ...), custom_call_target="tpu_custom_call" | custom-call | flops 2415919104 | bytes 9437184 | tf_op jit(solution)/shard_map/pallas_call | solution.py:278
  44.1 0.0 collective-permute-done.16.there_mass
  44.1 0.0 collective-permute-done.15.there
  44.1 1.2 %shard_map.77 = (f32[768,512]{1,0:T(8,128)}, f32[1,768]{1,0:T(1,128)}) custom-call(f32[768,512]{1,0:T(8,128)S(1)} %get-tuple-element.32.here, f32[1,768]{1,0:T(1,128)S(1)} %get-tuple-element.33.here_mass, bf16[768,512]{1,0:T(8,128)(2,1)S(1)} %collective-permute-done.15.there, f32[1,768]{1,0:T(1,128)S(1)} %collective-permute-done.16.there_mass), custom_call_target="tpu_custom_call" | custom-call | tf_op jit(solution)/shard_map/pallas_call | solution.py:311
  (11 shorter events, 0.2 us)
Async XLA Ops:
  1.7 8.1 %collective-permute-start = (bf16[128,512]{1,0:T(8,128)(2,1)S(1)}, bf16[128,512]{1,0:T(8,128)(2,1)S(1)}, u32[]{:S(2)}, u32[]{:S(2)}) collective-permute-start(bf16[128,512]{1,0:T(8,128)(2,1)S(1)} %multiply_convert_fusion.above), channel_id=1, source_target_pairs={{1,0},{0,1},{3,2},{2,3},{5,4},{4,5},{7,6},{6,7},{9,8},{8,9},{11,10... | collective-permute-start | bytes 393224 | tf_op jit(solution)/shard_map/ppermute | solution.py:49
  4.8 13.9 %collective-permute-start.3 = (bf16[128,512]{1,0:T(8,128)(2,1)S(1)}, bf16[128,512]{1,0:T(8,128)(2,1)S(1)}, u32[]{:S(2)}, u32[]{:S(2)}) collective-permute-start(bf16[128,512]{1,0:T(8,128)(2,1)S(1)} %multiply_convert_fusion.above), channel_id=1, source_target_pairs={{2,0},{3,1},{0,2},{1,3},{6,4},{7,5},{4,6},{5,7},{10,8},{11,9},{8,1... | collective-permute-start | bytes 393224 | tf_op jit(solution)/shard_map/ppermute | solution.py:49
  7.4 11.3 %collective-permute-start.4 = (bf16[128,512]{1,0:T(8,128)(2,1)S(1)}, bf16[128,512]{1,0:T(8,128)(2,1)S(1)}, u32[]{:S(2)}, u32[]{:S(2)}) collective-permute-start(bf16[128,512]{1,0:T(8,128)(2,1)S(1)} %multiply_convert_fusion.above), channel_id=1, source_target_pairs={{3,0},{2,1},{1,2},{0,3},{7,4},{6,5},{5,6},{4,7},{11,8},{10,9},{9,1... | collective-permute-start | bytes 393224 | tf_op jit(solution)/shard_map/ppermute | solution.py:49
  7.4 0.7 %copy-start = (s32[6144]{0:T(1024)S(1)}, s32[6144]{0:T(1024)}, u32[]{:S(2)}) copy-start(s32[6144]{0:T(1024)} %param.7) | copy-start | bytes 73732
  8.1 3.5 %slice-start = ((s8[6291456]{0:T(1024)(128)(4,1)}), s8[4194304]{0:T(1024)(128)(4,1)S(1)}, s32[]{:S(2)}) async-start(s8[6291456]{0:T(1024)(128)(4,1)} %bitcast.2), calls=%async_computation | async-start | bytes 8388608
  9.0 2.6 %slice-start.1 = ((s8[6291456]{0:T(1024)(128)(4,1)}), s8[2097152]{0:T(1024)(128)(4,1)S(1)}, s32[]{:S(2)}) async-start(s8[6291456]{0:T(1024)(128)(4,1)} %bitcast.2), calls=%async_computation.1 | async-start | bytes 4194304
  9.8 6.8 %collective-permute-start.1 = (bf16[256,512]{1,0:T(8,128)(2,1)S(1)}, bf16[256,512]{1,0:T(8,128)(2,1)S(1)}, u32[]{:S(2)}, u32[]{:S(2)}) collective-permute-start(bf16[256,512]{1,0:T(8,128)(2,1)S(1)} %shard_map.60.a.refs_0_), channel_id=1, source_target_pairs={{8,0},{20,4},{0,8},{28,12},{24,16},{4,20},{16,24},{12,28},{9,1},{2... | collective-permute-start | bytes 786440 | tf_op jit(solution)/shard_map/ppermute | solution.py:49
  14.4 12.3 %collective-permute-start.2 = (bf16[256,512]{1,0:T(8,128)(2,1)S(1)}, bf16[256,512]{1,0:T(8,128)(2,1)S(1)}, u32[]{:S(2)}, u32[]{:S(2)}) collective-permute-start(bf16[256,512]{1,0:T(8,128)(2,1)S(1)} %shard_map.63), channel_id=1, source_target_pairs={{16,0},{12,4},{24,8},{4,12},{0,16},{28,20},{8,24},{20,28},{17,1},{... | collective-permute-start | bytes 786440 | tf_op jit(solution)/shard_map/ppermute | solution.py:49
  16.6 14.6 %collective-permute-start.5 = (bf16[256,512]{1,0:T(8,128)(2,1)S(1)}, bf16[256,512]{1,0:T(8,128)(2,1)S(1)}, u32[]{:S(2)}, u32[]{:S(2)}) collective-permute-start(bf16[256,512]{1,0:T(8,128)(2,1)S(1)} %shard_map.68), channel_id=1, source_target_pairs={{16,0},{12,4},{24,8},{4,12},{0,16},{28,20},{8,24},{20,28},{17,1},{... | collective-permute-start | bytes 786440 | tf_op jit(solution)/shard_map/ppermute | solution.py:49
  18.7 12.6 %collective-permute-start.6 = (bf16[256,512]{1,0:T(8,128)(2,1)S(1)}, bf16[256,512]{1,0:T(8,128)(2,1)S(1)}, u32[]{:S(2)}, u32[]{:S(2)}) collective-permute-start(bf16[256,512]{1,0:T(8,128)(2,1)S(1)} %shard_map.64.refs_0_.refs_3_.a), channel_id=1, source_target_pairs={{8,0},{20,4},{0,8},{28,12},{24,16},{4,20},{16,24},{12,28},{9,1},{2... | collective-permute-start | bytes 786440 | tf_op jit(solution)/shard_map/ppermute | solution.py:49
  23.0 6.5 %collective-permute-start.10 = (f32[3,512]{1,0:T(4,128)S(1)}, f32[3,512]{1,0:T(4,128)S(1)}, u32[]{:S(2)}, u32[]{:S(2)}) collective-permute-start(f32[3,512]{1,0:T(4,128)S(1)} %shard_map.66.refs_5_.refs_0_), channel_id=1, source_target_pairs={{3,0},{2,1},{1,2},{0,3},{7,4},{6,5},{5,6},{4,7},{11,8},{10,9},{9,1... | collective-permute-start | bytes 18440 | tf_op jit(solution)/shard_map/ppermute | solution.py:49
  26.6 3.7 %collective-permute-start.8 = (f32[3,512]{1,0:T(4,128)S(1)}, f32[3,512]{1,0:T(4,128)S(1)}, u32[]{:S(2)}, u32[]{:S(2)}) collective-permute-start(f32[3,512]{1,0:T(4,128)S(1)} %shard_map.66.refs_5_.refs_0_), channel_id=1, source_target_pairs={{1,0},{0,1},{3,2},{2,3},{5,4},{4,5},{7,6},{6,7},{9,8},{8,9},{11,10... | collective-permute-start | bytes 18440 | tf_op jit(solution)/shard_map/ppermute | solution.py:49
  26.6 4.6 %collective-permute-start.9 = (f32[3,512]{1,0:T(4,128)S(1)}, f32[3,512]{1,0:T(4,128)S(1)}, u32[]{:S(2)}, u32[]{:S(2)}) collective-permute-start(f32[3,512]{1,0:T(4,128)S(1)} %shard_map.66.refs_5_.refs_0_), channel_id=1, source_target_pairs={{2,0},{3,1},{0,2},{1,3},{6,4},{7,5},{4,6},{5,7},{10,8},{11,9},{8,1... | collective-permute-start | bytes 18440 | tf_op jit(solution)/shard_map/ppermute | solution.py:49
  29.5 6.5 %collective-permute-start.7 = (bf16[256,512]{1,0:T(8,128)(2,1)S(1)}, bf16[256,512]{1,0:T(8,128)(2,1)S(1)}, u32[]{:S(2)}, u32[]{:S(2)}) collective-permute-start(bf16[256,512]{1,0:T(8,128)(2,1)S(1)} %shard_map.69), channel_id=1, source_target_pairs={{16,0},{12,4},{24,8},{4,12},{0,16},{28,20},{8,24},{20,28},{17,1},{... | collective-permute-start | bytes 786440 | tf_op jit(solution)/shard_map/ppermute | solution.py:49
  31.3 7.6 %collective-permute-start.11 = (bf16[256,512]{1,0:T(8,128)(2,1)S(1)}, bf16[256,512]{1,0:T(8,128)(2,1)S(1)}, u32[]{:S(2)}, u32[]{:S(2)}) collective-permute-start(bf16[256,512]{1,0:T(8,128)(2,1)S(1)} %shard_map.72), channel_id=1, source_target_pairs={{16,0},{12,4},{24,8},{4,12},{0,16},{28,20},{8,24},{20,28},{17,1},{... | collective-permute-start | bytes 786440 | tf_op jit(solution)/shard_map/ppermute | solution.py:49
  31.8 7.7 %collective-permute-start.12 = (f32[2,512]{1,0:T(2,128)S(1)}, f32[2,512]{1,0:T(2,128)S(1)}, u32[]{:S(2)}, u32[]{:S(2)}) collective-permute-start(f32[2,512]{1,0:T(2,128)S(1)} %shard_map.70.refs_4_.refs_0_), channel_id=1, source_target_pairs={{8,0},{20,4},{0,8},{28,12},{24,16},{4,20},{16,24},{12,28},{9,1},{2... | collective-permute-start | bytes 12296 | tf_op jit(solution)/shard_map/ppermute | solution.py:49
  32.4 7.1 %collective-permute-start.13 = (f32[2,512]{1,0:T(2,128)S(1)}, f32[2,512]{1,0:T(2,128)S(1)}, u32[]{:S(2)}, u32[]{:S(2)}) collective-permute-start(f32[2,512]{1,0:T(2,128)S(1)} %shard_map.70.refs_4_.refs_0_), channel_id=1, source_target_pairs={{16,0},{12,4},{24,8},{4,12},{0,16},{28,20},{8,24},{20,28},{17,1},{... | collective-permute-start | bytes 12296 | tf_op jit(solution)/shard_map/ppermute | solution.py:49
  33.9 5.6 %collective-permute-start.14 = (f32[2,512]{1,0:T(2,128)S(1)}, f32[2,512]{1,0:T(2,128)S(1)}, u32[]{:S(2)}, u32[]{:S(2)}) collective-permute-start(f32[2,512]{1,0:T(2,128)S(1)} %shard_map.70.refs_4_.refs_0_), channel_id=1, source_target_pairs={{24,0},{16,8},{8,16},{0,24},{25,1},{17,9},{9,17},{1,25},{26,2},{18... | collective-permute-start | bytes 12296 | tf_op jit(solution)/shard_map/ppermute | solution.py:49
  41.7 2.4 %collective-permute-start.15 = (bf16[768,512]{1,0:T(8,128)(2,1)S(1)}, bf16[768,512]{1,0:T(8,128)(2,1)S(1)}, u32[]{:S(2)}, u32[]{:S(2)}) collective-permute-start(bf16[768,512]{1,0:T(8,128)(2,1)S(1)} %get-tuple-element.34), channel_id=1, source_target_pairs={{4,0},{0,4},{5,1},{1,5},{6,2},{2,6},{7,3},{3,7},{12,8},{8,12},{13,... | collective-permute-start | bytes 2359304 | tf_op jit(solution)/shard_map/ppermute | solution.py:49
  41.7 2.3 %collective-permute-start.16 = (f32[1,768]{1,0:T(1,128)S(1)}, f32[1,768]{1,0:T(1,128)S(1)}, u32[]{:S(2)}, u32[]{:S(2)}) collective-permute-start(f32[1,768]{1,0:T(1,128)S(1)} %get-tuple-element.35), channel_id=1, source_target_pairs={{4,0},{0,4},{5,1},{1,5},{6,2},{2,6},{7,3},{3,7},{12,8},{8,12},{13,... | collective-permute-start | bytes 9224 | tf_op jit(solution)/shard_map/ppermute | solution.py:49

commit v27 on v26

--- a/solution.py
+++ b/solution.py
@@ -364,7 +364,7 @@
     there = sums_call(per_device, 1, per_device, jnp.bfloat16, expos, points, factors)
     there = [exchange(a, ("lo",), lambda at: at ^ 1) for a in there]
     here = sums_call(per_device, 0, per_device, jnp.float32, expos, points, factors)
-    out, mass = add_call(block // 2, *here, *there)
+    out, mass = add_call(block, *here, *there)
     return (out[None], mass)
 
 

time: 45.7 us -> 45.7 us (level)
  no operation moved by 1% of the time
where the time goes in v27:
time: 45.7 us; the launch traced here: 45.5 us
  starting transfers between devices  22.3 us (49%)
  Pallas kernels  15.9 us (35%)
  waiting for transfers between devices  4.47 us (10%)
  other arithmetic  1.05 us (2%)
  between operations  1.01 us (2%)
  local copies, waits for them, and re-layouts  0.75 us (2%)
    ppermute x17, starting transfers between devices, exchange(): return lax.ppermute(a, axes, [(partner(at), at) for at in range(count)])  22.3 us
    pallas_call x2, Pallas kernels, totals_call(): pl.pallas_call(functools.partial(totals_kernel, rate, block, len(pieces))...  5.41 us
    ppermute x17, waiting for transfers between devices, exchange(): return lax.ppermute(a, axes, [(partner(at), at) for at in range(count)])  4.47 us
    pallas_call x3, Pallas kernels, expo_call(): pl.pallas_call(functools.partial(expo_kernel, rate, block, spots), in_spe...  4.27 us
    pallas_call x2, Pallas kernels, sums_call(): pl.pallas_call(functools.partial(sums_kernel, n, block, side), in_specs=i...  3.89 us
    pallas_call x1, Pallas kernels, add_call(): pl.pallas_call(functools.partial(add_kernel, block), in_specs=in_vmem(4),...  1.24 us
    convert_element_type x1, other arithmetic, to_points(): return (scaled.astype(jnp.float32) * 2.0 ** (-16)).astype(jnp.bfloat16)  1.05 us
  transfers between devices with their start and end apart: 17, of which 6 were waited for; matrix products, arithmetic and copies ran while one was open for 0% of the time, Pallas kernels for 28%

profile of v27, /device:TPU:0, one launch (start us, length us, event | category | flops | bytes accessed | tf_op | source)
XLA Modules:
  0.0 45.5 jit_solution(6849656297052310713)
XLA Ops:
  0.6 1.1 %multiply_convert_fusion.above = bf16[128,512]{1,0:T(8,128)(2,1)S(1)} fusion(s32[128,512]{1,0:T(8,128)} %param.4, s32[128]{0:T(128)} %param.5), kind=kLoop, calls=%fused_computation | loop fusion | flops 327680 | bytes 393728 | tf_op jit(solution)/shard_map/convert_element_type | solution.py:17
  1.7 3.1 %collective-permute-start = (bf16[128,512]{1,0:T(8,128)(2,1)S(1)}, bf16[128,512]{1,0:T(8,128)(2,1)S(1)}, u32[]{:S(2)}, u32[]{:S(2)}) collective-permute-start(bf16[128,512]{1,0:T(8,128)(2,1)S(1)} %multiply_convert_fusion.above), channel_id=1, source_target_pairs={{1,0},{0,1},{3,2},{2,3},{5,4},{4,5},{7,6},{6,7},{9,8},{8,9},{11,10... | collective-permute-start | bytes 393224 | tf_op jit(solution)/shard_map/ppermute | solution.py:49
  4.8 2.6 %collective-permute-start.3 = (bf16[128,512]{1,0:T(8,128)(2,1)S(1)}, bf16[128,512]{1,0:T(8,128)(2,1)S(1)}, u32[]{:S(2)}, u32[]{:S(2)}) collective-permute-start(bf16[128,512]{1,0:T(8,128)(2,1)S(1)} %multiply_convert_fusion.above), channel_id=1, source_target_pairs={{2,0},{3,1},{0,2},{1,3},{6,4},{7,5},{4,6},{5,7},{10,8},{11,9},{8,1... | collective-permute-start | bytes 393224 | tf_op jit(solution)/shard_map/ppermute | solution.py:49
  7.4 0.0 collective-permute-start.4
  7.4 0.0 copy-start
  7.4 0.7 %copy-done = s32[6144]{0:T(1024)S(1)} copy-done((s32[6144]{0:T(1024)S(1)}, s32[6144]{0:T(1024)}, u32[]{:S(2)}) %copy-start) | copy-done | bytes 24600
  8.1 0.0 slice-start
  8.1 0.9 %shard_map.59.refs_0_.refs_2_ = f32[6144,128]{1,0:T(8,128)S(1)} custom-call(s32[48,128]{1,0:T(8,128)S(1)} %bitcast.4), custom_call_target="tpu_custom_call" | custom-call | flops 2000000000 | tf_op jit(solution)/shard_map/pallas_call | solution.py:114
  9.0 0.0 slice-start.1
  9.0 0.8 %collective-permute-done.below = bf16[128,512]{1,0:T(8,128)(2,1)S(1)} collective-permute-done((bf16[128,512]{1,0:T(8,128)(2,1)S(1)}, bf16[128,512]{1,0:T(8,128)(2,1)S(1)}, u32[]{:S(2)}, u32[]{:S(2)}) %collective-permute-start) | collective-permute-done | bytes 131104 | tf_op jit(solution)/shard_map/ppermute | solution.py:49
  9.8 1.8 %collective-permute-start.1 = (bf16[256,512]{1,0:T(8,128)(2,1)S(1)}, bf16[256,512]{1,0:T(8,128)(2,1)S(1)}, u32[]{:S(2)}, u32[]{:S(2)}) collective-permute-start(bf16[256,512]{1,0:T(8,128)(2,1)S(1)} %shard_map.60.a.refs_0_), channel_id=1, source_target_pairs={{8,0},{20,4},{0,8},{28,12},{24,16},{4,20},{16,24},{12,28},{9,1},{2... | collective-permute-start | bytes 786440 | tf_op jit(solution)/shard_map/ppermute | solution.py:49
  11.6 0.0 slice-done
  11.6 0.0 slice-done.1
  11.7 2.7 %shard_map.62.refs_0_.left = f32[3,256]{1,0:T(4,128)S(1)} custom-call(bf16[256,512]{1,0:T(8,128)(2,1)S(1)} %shard_map.61.refs_0_, bf16[6144,512]{1,0:T(8,128)(2,1)S(1)} %bitcast.3, f32[6144,128]{1,0:T(8,128)S(1)} %shard_map.59.refs_0_.refs_2_), custom_call_target="tpu_custom_call" | custom-call | flops 1610612736 | bytes 6291456 | tf_op jit(solution)/shard_map/pallas_call | solution.py:154
  14.4 1.6 %collective-permute-start.2 = (bf16[256,512]{1,0:T(8,128)(2,1)S(1)}, bf16[256,512]{1,0:T(8,128)(2,1)S(1)}, u32[]{:S(2)}, u32[]{:S(2)}) collective-permute-start(bf16[256,512]{1,0:T(8,128)(2,1)S(1)} %shard_map.63), channel_id=1, source_target_pairs={{16,0},{12,4},{24,8},{4,12},{0,16},{28,20},{8,24},{20,28},{17,1},{... | collective-permute-start | bytes 786440 | tf_op jit(solution)/shard_map/ppermute | solution.py:49
  16.0 0.6 %collective-permute-done.1.refs_3_.refs_1_.a = bf16[256,512]{1,0:T(8,128)(2,1)S(1)} collective-permute-done((bf16[256,512]{1,0:T(8,128)(2,1)S(1)}, bf16[256,512]{1,0:T(8,128)(2,1)S(1)}, u32[]{:S(2)}, u32[]{:S(2)}) %collective-permute-start.1) | collective-permute-done | bytes 262176 | tf_op jit(solution)/shard_map/ppermute | solution.py:49
  16.6 2.0 %collective-permute-start.5 = (bf16[256,512]{1,0:T(8,128)(2,1)S(1)}, bf16[256,512]{1,0:T(8,128)(2,1)S(1)}, u32[]{:S(2)}, u32[]{:S(2)}) collective-permute-start(bf16[256,512]{1,0:T(8,128)(2,1)S(1)} %shard_map.68), channel_id=1, source_target_pairs={{16,0},{12,4},{24,8},{4,12},{0,16},{28,20},{8,24},{20,28},{17,1},{... | collective-permute-start | bytes 786440 | tf_op jit(solution)/shard_map/ppermute | solution.py:49
  18.7 0.0 collective-permute-done.3.above
  18.7 0.0 collective-permute-done.4.below
  18.7 1.6 %collective-permute-start.6 = (bf16[256,512]{1,0:T(8,128)(2,1)S(1)}, bf16[256,512]{1,0:T(8,128)(2,1)S(1)}, u32[]{:S(2)}, u32[]{:S(2)}) collective-permute-start(bf16[256,512]{1,0:T(8,128)(2,1)S(1)} %shard_map.64.refs_0_.refs_3_.a), channel_id=1, source_target_pairs={{8,0},{20,4},{0,8},{28,12},{24,16},{4,20},{16,24},{12,28},{9,1},{2... | collective-permute-start | bytes 786440 | tf_op jit(solution)/shard_map/ppermute | solution.py:49
  20.2 2.7 %shard_map.65.right = f32[3,256]{1,0:T(4,128)S(1)} custom-call(bf16[256,512]{1,0:T(8,128)(2,1)S(1)} %shard_map.64.refs_0_.refs_3_.a, bf16[6144,512]{1,0:T(8,128)(2,1)S(1)} %bitcast.3, f32[6144,128]{1,0:T(8,128)S(1)} %shard_map.59.refs_0_.refs_2_, bf16[256,512]{1,0:T(8,128)(2,1)S(1)} %collective-permute-done.1.refs_3_.refs_1_.a), custom_call_target="tpu_custom_call" | custom-call | flops 1610612736 | bytes 6291456 | tf_op jit(solution)/shard_map/pallas_call | solution.py:154
  23.0 3.7 %collective-permute-start.10 = (f32[3,512]{1,0:T(4,128)S(1)}, f32[3,512]{1,0:T(4,128)S(1)}, u32[]{:S(2)}, u32[]{:S(2)}) collective-permute-start(f32[3,512]{1,0:T(4,128)S(1)} %shard_map.66.refs_5_.refs_0_), channel_id=1, source_target_pairs={{3,0},{2,1},{1,2},{0,3},{7,4},{6,5},{5,6},{4,7},{11,8},{10,9},{9,1... | collective-permute-start | bytes 18440 | tf_op jit(solution)/shard_map/ppermute | solution.py:49
  26.6 0.0 collective-permute-start.8
  26.6 0.0 collective-permute-done.2.refs_2_
  26.6 0.8 %collective-permute-start.9 = (f32[3,512]{1,0:T(4,128)S(1)}, f32[3,512]{1,0:T(4,128)S(1)}, u32[]{:S(2)}, u32[]{:S(2)}) collective-permute-start(f32[3,512]{1,0:T(4,128)S(1)} %shard_map.66.refs_5_.refs_0_), channel_id=1, source_target_pairs={{2,0},{3,1},{0,2},{1,3},{6,4},{7,5},{4,6},{5,7},{10,8},{11,9},{8,1... | collective-permute-start | bytes 18440 | tf_op jit(solution)/shard_map/ppermute | solution.py:49
  27.4 2.0 %shard_map.67 = (bf16[1536,1024]{1,0:T(8,128)(2,1)S(1)}, f32[6,1024]{1,0:T(8,128)S(1)}, bf16[1024,512]{1,0:T(8,128)(2,1)S(1)}) custom-call(bf16[256,512]{1,0:T(8,128)(2,1)S(1)} %shard_map.60.a.refs_0_, bf16[256,512]{1,0:T(8,128)(2,1)S(1)} %collective-permute-done.1.refs_3_.refs_1_.a, bf16[256,512]{1,0:T(8,128)(2,1)S(1)} %collective-permute-done.2.refs_2_, ...), custom_call_target="tpu_custom_call" | custom-call | flops 16106127 | bytes 57671 | tf_op jit(solution)/shard_map/pallas_call | solution.py:229
  29.5 0.0 collective-permute-done.10.refs_3_
  29.5 0.6 %collective-permute-start.7 = (bf16[256,512]{1,0:T(8,128)(2,1)S(1)}, bf16[256,512]{1,0:T(8,128)(2,1)S(1)}, u32[]{:S(2)}, u32[]{:S(2)}) collective-permute-start(bf16[256,512]{1,0:T(8,128)(2,1)S(1)} %shard_map.69), channel_id=1, source_target_pairs={{16,0},{12,4},{24,8},{4,12},{0,16},{28,20},{8,24},{20,28},{17,1},{... | collective-permute-start | bytes 786440 | tf_op jit(solution)/shard_map/ppermute | solution.py:49
  30.1 0.2 collective-permute-done.8.refs_1_
  30.3 0.9 %collective-permute-done.9.refs_2_ = f32[3,512]{1,0:T(4,128)S(1)} collective-permute-done((f32[3,512]{1,0:T(4,128)S(1)}, f32[3,512]{1,0:T(4,128)S(1)}, u32[]{:S(2)}, u32[]{:S(2)}) %collective-permute-start.9) | collective-permute-done | bytes 6176 | tf_op jit(solution)/shard_map/ppermute | solution.py:49
  31.2 0.0 collective-permute-done.5.refs_5_.refs_0_
  31.2 0.0 collective-permute-done.6.refs_1_.a
  31.3 0.6 %collective-permute-start.11 = (bf16[256,512]{1,0:T(8,128)(2,1)S(1)}, bf16[256,512]{1,0:T(8,128)(2,1)S(1)}, u32[]{:S(2)}, u32[]{:S(2)}) collective-permute-start(bf16[256,512]{1,0:T(8,128)(2,1)S(1)} %shard_map.72), channel_id=1, source_target_pairs={{16,0},{12,4},{24,8},{4,12},{0,16},{28,20},{8,24},{20,28},{17,1},{... | collective-permute-start | bytes 786440 | tf_op jit(solution)/shard_map/ppermute | solution.py:49
  31.8 0.6 %collective-permute-start.12 = (f32[2,512]{1,0:T(2,128)S(1)}, f32[2,512]{1,0:T(2,128)S(1)}, u32[]{:S(2)}, u32[]{:S(2)}) collective-permute-start(f32[2,512]{1,0:T(2,128)S(1)} %shard_map.70.refs_4_.refs_0_), channel_id=1, source_target_pairs={{8,0},{20,4},{0,8},{28,12},{24,16},{4,20},{16,24},{12,28},{9,1},{2... | collective-permute-start | bytes 12296 | tf_op jit(solution)/shard_map/ppermute | solution.py:49
  32.4 1.5 %collective-permute-start.13 = (f32[2,512]{1,0:T(2,128)S(1)}, f32[2,512]{1,0:T(2,128)S(1)}, u32[]{:S(2)}, u32[]{:S(2)}) collective-permute-start(f32[2,512]{1,0:T(2,128)S(1)} %shard_map.70.refs_4_.refs_0_), channel_id=1, source_target_pairs={{16,0},{12,4},{24,8},{4,12},{0,16},{28,20},{8,24},{20,28},{17,1},{... | collective-permute-start | bytes 12296 | tf_op jit(solution)/shard_map/ppermute | solution.py:49
  33.9 1.4 %collective-permute-start.14 = (f32[2,512]{1,0:T(2,128)S(1)}, f32[2,512]{1,0:T(2,128)S(1)}, u32[]{:S(2)}, u32[]{:S(2)}) collective-permute-start(f32[2,512]{1,0:T(2,128)S(1)} %shard_map.70.refs_4_.refs_0_), channel_id=1, source_target_pairs={{24,0},{16,8},{8,16},{0,24},{25,1},{17,9},{9,17},{1,25},{26,2},{18... | collective-permute-start | bytes 12296 | tf_op jit(solution)/shard_map/ppermute | solution.py:49
  35.3 0.6 %collective-permute-done.7.refs_2_ = bf16[256,512]{1,0:T(8,128)(2,1)S(1)} collective-permute-done((bf16[256,512]{1,0:T(8,128)(2,1)S(1)}, bf16[256,512]{1,0:T(8,128)(2,1)S(1)}, u32[]{:S(2)}, u32[]{:S(2)}) %collective-permute-start.7) | collective-permute-done | bytes 262176 | tf_op jit(solution)/shard_map/ppermute | solution.py:49
  36.0 1.6 %shard_map.71 = (bf16[1536,768]{1,0:T(8,128)(2,1)S(1)}, f32[6,768]{1,0:T(8,128)S(1)}, bf16[768,512]{1,0:T(8,128)(2,1)S(1)}) custom-call(bf16[256,512]{1,0:T(8,128)(2,1)S(1)} %collective-permute-done.5.refs_5_.refs_0_, bf16[256,512]{1,0:T(8,128)(2,1)S(1)} %collective-permute-done.6.refs_1_.a, bf16[256,512]{1,0:T(8,128)(2,1)S(1)} %collective-permute-done.7.refs_2_, ...), custom_call_target="tpu_custom_call" | custom-call | flops 12079595 | bytes 47185 | tf_op jit(solution)/shard_map/pallas_call | solution.py:229
  37.5 1.3 %collective-permute-done.11.refs_0_ = bf16[256,512]{1,0:T(8,128)(2,1)S(1)} collective-permute-done((bf16[256,512]{1,0:T(8,128)(2,1)S(1)}, bf16[256,512]{1,0:T(8,128)(2,1)S(1)}, u32[]{:S(2)}, u32[]{:S(2)}) %collective-permute-start.11) | collective-permute-done | bytes 262176 | tf_op jit(solution)/shard_map/ppermute | solution.py:49
  38.8 0.7 %shard_map.73 = (bf16[1536,256]{1,0:T(8,128)(2,1)S(1)}, f32[6,256]{1,0:T(8,128)S(1)}, bf16[256,512]{1,0:T(8,128)(2,1)S(1)}) custom-call(bf16[256,512]{1,0:T(8,128)(2,1)S(1)} %collective-permute-done.11.refs_0_, bf16[6144,512]{1,0:T(8,128)(2,1)S(1)} %bitcast.3, f32[6,768]{1,0:T(8,128)S(1)} %get-tuple-element.23.refs_2_.refs_5_), custom_call_target="tpu_custom_call" | custom-call | flops 402653184 | bytes 2621440 | tf_op jit(solution)/shard_map/pallas_call | solution.py:229
  39.5 0.0 collective-permute-done.12.refs_1_
  39.5 0.0 collective-permute-done.13.refs_2_
  39.6 0.0 collective-permute-done.14.refs_3_
  39.6 2.1 %shard_map.76 = (bf16[768,512]{1,0:T(8,128)(2,1)S(1)}, f32[1,768]{1,0:T(1,128)S(1)}) custom-call(bf16[1536,1024]{1,0:T(8,128)(2,1)S(1)} %get-tuple-element.20.refs_0_, bf16[1536,768]{1,0:T(8,128)(2,1)S(1)} %get-tuple-element.22.refs_1_, bf16[1536,256]{1,0:T(8,128)(2,1)S(1)} %get-tuple-element.24.refs_2_, bf16[1024,512]{1,0:T(8,128)(2,1)S(1)} %get-tuple-element.25.refs_3_, ...), custom_call_target="tpu_custom_call" | custom-call | flops 2415919104 | bytes 9437184 | tf_op jit(solution)/shard_map/pallas_call | solution.py:278
  41.7 0.1 collective-permute-start.15
  41.7 0.5 %collective-permute-start.16 = (f32[1,768]{1,0:T(1,128)S(1)}, f32[1,768]{1,0:T(1,128)S(1)}, u32[]{:S(2)}, u32[]{:S(2)}) collective-permute-start(f32[1,768]{1,0:T(1,128)S(1)} %get-tuple-element.35), channel_id=1, source_target_pairs={{4,0},{0,4},{5,1},{1,5},{6,2},{2,6},{7,3},{3,7},{12,8},{8,12},{13,... | collective-permute-start | bytes 9224 | tf_op jit(solution)/shard_map/ppermute | solution.py:49
  42.2 1.8 %shard_map.75 = (f32[768,512]{1,0:T(8,128)S(1)}, f32[1,768]{1,0:T(1,128)S(1)}) custom-call(bf16[1536,1024]{1,0:T(8,128)(2,1)S(1)} %get-tuple-element.20.refs_0_, bf16[1536,768]{1,0:T(8,128)(2,1)S(1)} %get-tuple-element.22.refs_1_, bf16[1536,256]{1,0:T(8,128)(2,1)S(1)} %get-tuple-element.24.refs_2_, bf16[1024,512]{1,0:T(8,128)(2,1)S(1)} %get-tuple-element.25.refs_3_, ...), custom_call_target="tpu_custom_call" | custom-call | flops 2415919104 | bytes 9437184 | tf_op jit(solution)/shard_map/pallas_call | solution.py:278
  44.1 0.0 collective-permute-done.16.there_mass
  44.1 0.0 collective-permute-done.15.there
  44.1 1.2 %shard_map.77 = (f32[768,512]{1,0:T(8,128)}, f32[1,768]{1,0:T(1,128)}) custom-call(f32[768,512]{1,0:T(8,128)S(1)} %get-tuple-element.32.here, f32[1,768]{1,0:T(1,128)S(1)} %get-tuple-element.33.here_mass, bf16[768,512]{1,0:T(8,128)(2,1)S(1)} %collective-permute-done.15.there, f32[1,768]{1,0:T(1,128)S(1)} %collective-permute-done.16.there_mass), custom_call_target="tpu_custom_call" | custom-call | tf_op jit(solution)/shard_map/pallas_call | solution.py:311
  (11 shorter events, 0.2 us)
Async XLA Ops:
  1.7 8.1 %collective-permute-start = (bf16[128,512]{1,0:T(8,128)(2,1)S(1)}, bf16[128,512]{1,0:T(8,128)(2,1)S(1)}, u32[]{:S(2)}, u32[]{:S(2)}) collective-permute-start(bf16[128,512]{1,0:T(8,128)(2,1)S(1)} %multiply_convert_fusion.above), channel_id=1, source_target_pairs={{1,0},{0,1},{3,2},{2,3},{5,4},{4,5},{7,6},{6,7},{9,8},{8,9},{11,10... | collective-permute-start | bytes 393224 | tf_op jit(solution)/shard_map/ppermute | solution.py:49
  4.8 13.9 %collective-permute-start.3 = (bf16[128,512]{1,0:T(8,128)(2,1)S(1)}, bf16[128,512]{1,0:T(8,128)(2,1)S(1)}, u32[]{:S(2)}, u32[]{:S(2)}) collective-permute-start(bf16[128,512]{1,0:T(8,128)(2,1)S(1)} %multiply_convert_fusion.above), channel_id=1, source_target_pairs={{2,0},{3,1},{0,2},{1,3},{6,4},{7,5},{4,6},{5,7},{10,8},{11,9},{8,1... | collective-permute-start | bytes 393224 | tf_op jit(solution)/shard_map/ppermute | solution.py:49
  7.4 11.3 %collective-permute-start.4 = (bf16[128,512]{1,0:T(8,128)(2,1)S(1)}, bf16[128,512]{1,0:T(8,128)(2,1)S(1)}, u32[]{:S(2)}, u32[]{:S(2)}) collective-permute-start(bf16[128,512]{1,0:T(8,128)(2,1)S(1)} %multiply_convert_fusion.above), channel_id=1, source_target_pairs={{3,0},{2,1},{1,2},{0,3},{7,4},{6,5},{5,6},{4,7},{11,8},{10,9},{9,1... | collective-permute-start | bytes 393224 | tf_op jit(solution)/shard_map/ppermute | solution.py:49
  7.4 0.7 %copy-start = (s32[6144]{0:T(1024)S(1)}, s32[6144]{0:T(1024)}, u32[]{:S(2)}) copy-start(s32[6144]{0:T(1024)} %param.7) | copy-start | bytes 73732
  8.1 3.5 %slice-start = ((s8[6291456]{0:T(1024)(128)(4,1)}), s8[4194304]{0:T(1024)(128)(4,1)S(1)}, s32[]{:S(2)}) async-start(s8[6291456]{0:T(1024)(128)(4,1)} %bitcast.2), calls=%async_computation | async-start | bytes 8388608
  9.0 2.6 %slice-start.1 = ((s8[6291456]{0:T(1024)(128)(4,1)}), s8[2097152]{0:T(1024)(128)(4,1)S(1)}, s32[]{:S(2)}) async-start(s8[6291456]{0:T(1024)(128)(4,1)} %bitcast.2), calls=%async_computation.1 | async-start | bytes 4194304
  9.8 6.8 %collective-permute-start.1 = (bf16[256,512]{1,0:T(8,128)(2,1)S(1)}, bf16[256,512]{1,0:T(8,128)(2,1)S(1)}, u32[]{:S(2)}, u32[]{:S(2)}) collective-permute-start(bf16[256,512]{1,0:T(8,128)(2,1)S(1)} %shard_map.60.a.refs_0_), channel_id=1, source_target_pairs={{8,0},{20,4},{0,8},{28,12},{24,16},{4,20},{16,24},{12,28},{9,1},{2... | collective-permute-start | bytes 786440 | tf_op jit(solution)/shard_map/ppermute | solution.py:49
  14.4 12.3 %collective-permute-start.2 = (bf16[256,512]{1,0:T(8,128)(2,1)S(1)}, bf16[256,512]{1,0:T(8,128)(2,1)S(1)}, u32[]{:S(2)}, u32[]{:S(2)}) collective-permute-start(bf16[256,512]{1,0:T(8,128)(2,1)S(1)} %shard_map.63), channel_id=1, source_target_pairs={{16,0},{12,4},{24,8},{4,12},{0,16},{28,20},{8,24},{20,28},{17,1},{... | collective-permute-start | bytes 786440 | tf_op jit(solution)/shard_map/ppermute | solution.py:49
  16.6 14.6 %collective-permute-start.5 = (bf16[256,512]{1,0:T(8,128)(2,1)S(1)}, bf16[256,512]{1,0:T(8,128)(2,1)S(1)}, u32[]{:S(2)}, u32[]{:S(2)}) collective-permute-start(bf16[256,512]{1,0:T(8,128)(2,1)S(1)} %shard_map.68), channel_id=1, source_target_pairs={{16,0},{12,4},{24,8},{4,12},{0,16},{28,20},{8,24},{20,28},{17,1},{... | collective-permute-start | bytes 786440 | tf_op jit(solution)/shard_map/ppermute | solution.py:49
  18.7 12.6 %collective-permute-start.6 = (bf16[256,512]{1,0:T(8,128)(2,1)S(1)}, bf16[256,512]{1,0:T(8,128)(2,1)S(1)}, u32[]{:S(2)}, u32[]{:S(2)}) collective-permute-start(bf16[256,512]{1,0:T(8,128)(2,1)S(1)} %shard_map.64.refs_0_.refs_3_.a), channel_id=1, source_target_pairs={{8,0},{20,4},{0,8},{28,12},{24,16},{4,20},{16,24},{12,28},{9,1},{2... | collective-permute-start | bytes 786440 | tf_op jit(solution)/shard_map/ppermute | solution.py:49
  23.0 6.5 %collective-permute-start.10 = (f32[3,512]{1,0:T(4,128)S(1)}, f32[3,512]{1,0:T(4,128)S(1)}, u32[]{:S(2)}, u32[]{:S(2)}) collective-permute-start(f32[3,512]{1,0:T(4,128)S(1)} %shard_map.66.refs_5_.refs_0_), channel_id=1, source_target_pairs={{3,0},{2,1},{1,2},{0,3},{7,4},{6,5},{5,6},{4,7},{11,8},{10,9},{9,1... | collective-permute-start | bytes 18440 | tf_op jit(solution)/shard_map/ppermute | solution.py:49
  26.6 3.7 %collective-permute-start.8 = (f32[3,512]{1,0:T(4,128)S(1)}, f32[3,512]{1,0:T(4,128)S(1)}, u32[]{:S(2)}, u32[]{:S(2)}) collective-permute-start(f32[3,512]{1,0:T(4,128)S(1)} %shard_map.66.refs_5_.refs_0_), channel_id=1, source_target_pairs={{1,0},{0,1},{3,2},{2,3},{5,4},{4,5},{7,6},{6,7},{9,8},{8,9},{11,10... | collective-permute-start | bytes 18440 | tf_op jit(solution)/shard_map/ppermute | solution.py:49
  26.6 4.6 %collective-permute-start.9 = (f32[3,512]{1,0:T(4,128)S(1)}, f32[3,512]{1,0:T(4,128)S(1)}, u32[]{:S(2)}, u32[]{:S(2)}) collective-permute-start(f32[3,512]{1,0:T(4,128)S(1)} %shard_map.66.refs_5_.refs_0_), channel_id=1, source_target_pairs={{2,0},{3,1},{0,2},{1,3},{6,4},{7,5},{4,6},{5,7},{10,8},{11,9},{8,1... | collective-permute-start | bytes 18440 | tf_op jit(solution)/shard_map/ppermute | solution.py:49
  29.5 6.5 %collective-permute-start.7 = (bf16[256,512]{1,0:T(8,128)(2,1)S(1)}, bf16[256,512]{1,0:T(8,128)(2,1)S(1)}, u32[]{:S(2)}, u32[]{:S(2)}) collective-permute-start(bf16[256,512]{1,0:T(8,128)(2,1)S(1)} %shard_map.69), channel_id=1, source_target_pairs={{16,0},{12,4},{24,8},{4,12},{0,16},{28,20},{8,24},{20,28},{17,1},{... | collective-permute-start | bytes 786440 | tf_op jit(solution)/shard_map/ppermute | solution.py:49
  31.3 7.6 %collective-permute-start.11 = (bf16[256,512]{1,0:T(8,128)(2,1)S(1)}, bf16[256,512]{1,0:T(8,128)(2,1)S(1)}, u32[]{:S(2)}, u32[]{:S(2)}) collective-permute-start(bf16[256,512]{1,0:T(8,128)(2,1)S(1)} %shard_map.72), channel_id=1, source_target_pairs={{16,0},{12,4},{24,8},{4,12},{0,16},{28,20},{8,24},{20,28},{17,1},{... | collective-permute-start | bytes 786440 | tf_op jit(solution)/shard_map/ppermute | solution.py:49
  31.8 7.7 %collective-permute-start.12 = (f32[2,512]{1,0:T(2,128)S(1)}, f32[2,512]{1,0:T(2,128)S(1)}, u32[]{:S(2)}, u32[]{:S(2)}) collective-permute-start(f32[2,512]{1,0:T(2,128)S(1)} %shard_map.70.refs_4_.refs_0_), channel_id=1, source_target_pairs={{8,0},{20,4},{0,8},{28,12},{24,16},{4,20},{16,24},{12,28},{9,1},{2... | collective-permute-start | bytes 12296 | tf_op jit(solution)/shard_map/ppermute | solution.py:49
  32.4 7.1 %collective-permute-start.13 = (f32[2,512]{1,0:T(2,128)S(1)}, f32[2,512]{1,0:T(2,128)S(1)}, u32[]{:S(2)}, u32[]{:S(2)}) collective-permute-start(f32[2,512]{1,0:T(2,128)S(1)} %shard_map.70.refs_4_.refs_0_), channel_id=1, source_target_pairs={{16,0},{12,4},{24,8},{4,12},{0,16},{28,20},{8,24},{20,28},{17,1},{... | collective-permute-start | bytes 12296 | tf_op jit(solution)/shard_map/ppermute | solution.py:49
  33.9 5.6 %collective-permute-start.14 = (f32[2,512]{1,0:T(2,128)S(1)}, f32[2,512]{1,0:T(2,128)S(1)}, u32[]{:S(2)}, u32[]{:S(2)}) collective-permute-start(f32[2,512]{1,0:T(2,128)S(1)} %shard_map.70.refs_4_.refs_0_), channel_id=1, source_target_pairs={{24,0},{16,8},{8,16},{0,24},{25,1},{17,9},{9,17},{1,25},{26,2},{18... | collective-permute-start | bytes 12296 | tf_op jit(solution)/shard_map/ppermute | solution.py:49
  41.7 2.4 %collective-permute-start.15 = (bf16[768,512]{1,0:T(8,128)(2,1)S(1)}, bf16[768,512]{1,0:T(8,128)(2,1)S(1)}, u32[]{:S(2)}, u32[]{:S(2)}) collective-permute-start(bf16[768,512]{1,0:T(8,128)(2,1)S(1)} %get-tuple-element.34), channel_id=1, source_target_pairs={{4,0},{0,4},{5,1},{1,5},{6,2},{2,6},{7,3},{3,7},{12,8},{8,12},{13,... | collective-permute-start | bytes 2359304 | tf_op jit(solution)/shard_map/ppermute | solution.py:49
  41.7 2.3 %collective-permute-start.16 = (f32[1,768]{1,0:T(1,128)S(1)}, f32[1,768]{1,0:T(1,128)S(1)}, u32[]{:S(2)}, u32[]{:S(2)}) collective-permute-start(f32[1,768]{1,0:T(1,128)S(1)} %get-tuple-element.35), channel_id=1, source_target_pairs={{4,0},{0,4},{5,1},{1,5},{6,2},{2,6},{7,3},{3,7},{12,8},{8,12},{13,... | collective-permute-start | bytes 9224 | tf_op jit(solution)/shard_map/ppermute | solution.py:49
